TPU v7x, 32 devices: a whole 2x2x4 slice. The times are simulated.
32 devices in a mesh: grp: 2 (over y), row: 4 (over z), col: 4 (over x, core).
Axes of the slice: x: 2, y: 2, z: 4, core: 2. Of those that a mesh axis runs over, the one named last changes fastest.
Arguments:
- inputs: bfloat16 [1024, 8192], P('row', 'col'), may hold values from -6 to 6
- w_gate: bfloat16 [8192, 14336], P('col', 'row'), may hold values from -0.0625 to 0.0625
- w_up: bfloat16 [8192, 14336], P('col', 'row'), may hold values from -0.0625 to 0.0625
- w_down: bfloat16 [14336, 8192], P('row', 'col'), may hold values from -0.046875 to 0.046875
- query: bfloat16 [16384, 14336], P(('grp', 'col'), 'row'), parts along dimension 0, may hold values from -0.0625 to 0.0625
- curvature: float32 [2048, 8192], P('grp', 'col'), parts along dimension 0, may hold values from 0.5 to 16
Outputs:
- gnvp: float32 [16384, 14336], P(('grp', 'col'), 'row'), parts along dimension 0
There are 2 independent parts, one for each index of `grp`. A program takes and returns all parts, laid end to end along the dimension named above; an argument that names none is the same for every part. Nothing has to cross between parts.
All inputs are finite; a program needn't handle non-finite values.
Results may differ from a plain program's by a relative error of at most 0.0043.
Values may be sent and summed in bfloat16 or wider, within the bound.
No kernel may reach another device: no remote copies, remote signals or barrier semaphores. Data moves between devices by JAX's collectives and lax.ppermute only.
A program may use at most 320 MiB of HBM per device.

v0:
```python
import jax
import jax.numpy as jnp
from jax import lax
from jax.sharding import PartitionSpec as P


def silu_slope(values):
    sigmas = jax.nn.sigmoid(values)
    return sigmas * (1.0 + values * (1.0 - sigmas))


def matmul(left, right):
    return jnp.dot(left, right, preferred_element_type=jnp.float32)


def times_down(left, w_down):
    return lax.dot_general(
        left, w_down, (((1,), (1,)), ((), ())), preferred_element_type=jnp.float32
    )


def per_device(inputs, w_gate, w_up, w_down, query, curvature):
    gathered = lax.all_gather(inputs, "row", axis=0, tiled=True)
    tokens_all = gathered.shape[0]
    hidden_width = w_gate.shape[1]
    row_block = gathered
    stacked = lax.psum_scatter(
        jnp.concatenate(
            [matmul(row_block, w_gate), matmul(row_block, w_up), matmul(row_block, query)], axis=1
        ),
        "col",
        scatter_dimension=0,
        tiled=True,
    )
    gate_out = stacked[:, :hidden_width]
    up_out = stacked[:, hidden_width : 2 * hidden_width]
    tangent = stacked[:, 2 * hidden_width :]
    slopes = silu_slope(gate_out)
    hidden_tangent = (slopes * tangent * up_out).astype(jnp.bfloat16)
    out_part = matmul(lax.all_gather(hidden_tangent, "col", axis=0, tiled=True), w_down)
    local_rows = tokens_all // lax.axis_size("row")
    out_rows = lax.psum_scatter(out_part, "row", scatter_dimension=0, tiled=True)
    curv_rows = lax.dynamic_slice_in_dim(
        curvature, lax.axis_index("row") * local_rows, local_rows, 0
    )
    scaled = (curv_rows * out_rows).astype(jnp.bfloat16)
    scaled_all = lax.all_gather(scaled, "row", axis=0, tiled=True)
    row_block = scaled_all
    back_sum = lax.psum_scatter(
        times_down(row_block, w_down), "col", scatter_dimension=0, tiled=True
    )
    gate_bar = (back_sum * up_out * slopes).astype(jnp.bfloat16)
    row_block = gathered
    result = lax.dot_general(
        row_block,
        lax.all_gather(gate_bar, "col", axis=0, tiled=True),
        (((0,), (0,)), ((), ())),
        preferred_element_type=jnp.float32,
    )
    return result / tokens_all


def solution(mesh):
    in_specs = (
        P("row", "col"),
        P("col", "row"),
        P("col", "row"),
        P("row", "col"),
        P(("grp", "col"), "row"),
        P("grp", "col"),
    )
    out_specs = P(("grp", "col"), "row")
    return jax.shard_map(
        per_device, mesh=mesh, in_specs=in_specs, out_specs=out_specs, check_vma=False
    )
```

profile of v0, /device:TPU:0, one launch (start us, length us, event | category | flops | bytes accessed | tf_op | source)
XLA Modules:
  0.0 1047.3 jit_solution(18293609047323782734)
XLA Ops:
  6.5 0.0 all-gather.5.cloned.1.call-start
  6.5 0.7 all-gather.5.cloned.1.call-update
  7.3 0.0 reduce-scatter.4.cloned.1.call-start
  7.3 85.1 %all-gather.5.cloned.1.call-done = bf16[1024,2048]{1,0:T(8,128)(2,1)} async-done(((bf16[256,2048]{1,0:T(8,128)(2,1)}), bf16[1024,2048]{1,0:T(8,128)(2,1)}) %all-gather.5.cloned.1.call-update) | async-done | bytes 4194320 | tf_op jit(solution)/shard_map/all_gather | solution.py:23
  92.4 0.0 copy-start
  92.4 0.0 slice-start
  92.4 0.0 slice-start.1
  92.4 22.9 %fusion.2 = f32[1024,3584]{1,0:T(8,128)} fusion(bf16[1024,2048]{1,0:T(8,128)(2,1)} %all-gather.5.cloned.1.call-done, bf16[2048,3584]{1,0:T(8,128)(2,1)} %param.7), kind=kOutput, calls=%fused_computation.8 | convolution fusion | flops 15032385536 | bytes 33554432 | tf_op jit(solution)/shard_map/dot_general | solution.py:13
  115.3 0.0 copy-done
  115.3 0.0 slice-start.2
  115.3 0.0 slice-start.3
  115.3 21.7 %fusion.3 = f32[1024,3584]{1,0:T(8,128)} fusion(bf16[1024,2048]{1,0:T(8,128)(2,1)S(1)} %copy-done, bf16[2048,3584]{1,0:T(8,128)(2,1)} %param.8), kind=kOutput, calls=%fused_computation.9 | convolution fusion | flops 15032385536 | bytes 33554432 | tf_op jit(solution)/shard_map/dot_general | solution.py:13
  137.1 0.0 slice-done
  137.1 0.0 slice-done.1
  137.1 0.0 slice-done.2
  137.1 0.0 slice-done.3
  137.1 18.8 %fusion.4 = f32[1024,3584]{1,0:T(8,128)} fusion(bf16[1024,2048]{1,0:T(8,128)(2,1)S(1)} %copy-done, bf16[2048,3584]{1,0:T(8,128)(2,1)S(1)} %bitcast.15), kind=kOutput, calls=%fused_computation.10 | convolution fusion | flops 15032385536 | bytes 33554432 | tf_op jit(solution)/shard_map/dot_general | solution.py:13
  155.9 29.6 %pad_maximum_fusion = f32[1024,10752]{1,0:T(8,128)} fusion(f32[1024,3584]{1,0:T(8,128)} %fusion.4, f32[1024,3584]{1,0:T(8,128)} %fusion.3, f32[1024,3584]{1,0:T(8,128)} %fusion.2), kind=kLoop, calls=%fused_computation | loop fusion | flops 22020096 | bytes 88080384 | tf_op jit(solution)/shard_map/concatenate | solution.py:28
  185.5 0.0 reduce-scatter.4.cloned.1.call-update
  185.5 0.0 all-gather.7.cloned.1.call-start
  185.5 301.0 %reduce-scatter.4.cloned.1.call-done = f32[256,10752]{1,0:T(8,128)} async-done(((f32[1024,10752]{1,0:T(8,128)}), f32[256,10752]{1,0:T(8,128)}) %reduce-scatter.4.cloned.1.call-update) | async-done | bytes 11010064 | tf_op jit(solution)/shard_map/reduce_scatter | solution.py:27
  486.5 5.8 fusion.1
  492.3 0.0 all-gather.7.cloned.1.call-update
  492.3 0.0 reduce-scatter.6.cloned.1.call-start
  492.3 52.4 %all-gather.7.cloned.1.call-done = bf16[1024,3584]{1,0:T(8,128)(2,1)} async-done(((bf16[256,3584]{1,0:T(8,128)(2,1)}), bf16[1024,3584]{1,0:T(8,128)(2,1)}) %all-gather.7.cloned.1.call-update) | async-done | bytes 7340048 | tf_op jit(solution)/shard_map/all_gather | solution.py:40
  544.8 21.3 %fusion.5 = f32[1024,2048]{1,0:T(8,128)} fusion(bf16[1024,3584]{1,0:T(8,128)(2,1)} %all-gather.7.cloned.1.call-done, bf16[3584,2048]{1,0:T(8,128)(2,1)} %param.9), kind=kOutput, calls=%fused_computation.11 | convolution fusion | flops 15032385536 | bytes 30408704 | tf_op jit(solution)/shard_map/dot_general | solution.py:13
  566.1 0.0 reduce-scatter.6.cloned.1.call-update
  566.1 0.0 all-gather.9.cloned.1.call-start
  566.2 144.6 %reduce-scatter.6.cloned.1.call-done = f32[256,2048]{1,0:T(8,128)} async-done(((f32[1024,2048]{1,0:T(8,128)}), f32[256,2048]{1,0:T(8,128)}) %reduce-scatter.6.cloned.1.call-update) | async-done | bytes 2097168 | tf_op jit(solution)/shard_map/reduce_scatter | solution.py:42
  710.8 3.5 multiply_convert_fusion.1
  714.2 0.0 all-gather.9.cloned.1.call-update
  714.2 0.0 reduce-scatter.8.cloned.1.call-start
  714.3 81.6 %all-gather.9.cloned.1.call-done = bf16[1024,2048]{1,0:T(8,128)(2,1)} async-done(((bf16[256,2048]{1,0:T(8,128)(2,1)}), bf16[1024,2048]{1,0:T(8,128)(2,1)}) %all-gather.9.cloned.1.call-update) | async-done | bytes 4194320 | tf_op jit(solution)/shard_map/all_gather | solution.py:47
  795.9 22.9 %fusion.6 = f32[1024,3584]{1,0:T(8,128)} fusion(bf16[1024,2048]{1,0:T(8,128)(2,1)} %all-gather.9.cloned.1.call-done, bf16[3584,2048]{1,0:T(8,128)(2,1)} %param.9), kind=kOutput, calls=%fused_computation.12 | convolution fusion | flops 15032385536 | bytes 33554432 | tf_op jit(solution)/shard_map/dot_general | solution.py:17
  818.8 0.0 reduce-scatter.8.cloned.1.call-update
  818.8 0.0 all-gather.11.cloned.1.call-start
  818.8 111.6 %reduce-scatter.8.cloned.1.call-done = f32[256,3584]{1,0:T(8,128)} async-done(((f32[1024,3584]{1,0:T(8,128)}), f32[256,3584]{1,0:T(8,128)}) %reduce-scatter.8.cloned.1.call-update) | async-done | bytes 3670032 | tf_op jit(solution)/shard_map/reduce_scatter | solution.py:49
  930.4 5.9 multiply_convert_fusion
  936.3 0.0 all-gather.11.cloned.1.call-update
  936.3 52.5 %all-gather.11.cloned.1.call-done = bf16[1024,3584]{1,0:T(8,128)(2,1)} async-done(((bf16[256,3584]{1,0:T(8,128)(2,1)}), bf16[1024,3584]{1,0:T(8,128)(2,1)}) %all-gather.11.cloned.1.call-update) | async-done | bytes 7340048 | tf_op jit(solution)/shard_map/all_gather | solution.py:56
  988.8 24.2 %multiply_bitcast_fusion = f32[2048,3584]{0,1:T(8,128)} fusion(bf16[1024,3584]{1,0:T(8,128)(2,1)} %all-gather.11.cloned.1.call-done, bf16[1024,2048]{1,0:T(8,128)(2,1)} %all-gather.5.cloned.1.call-done), kind=kOutput, calls=%fused_computation.1 | convolution fusion | flops 15039725568 | bytes 40894464 | tf_op jit(solution)/shard_map/dot_general | solution.py:54
  1012.9 27.6 %copy.7 = f32[2048,3584]{1,0:T(8,128)} copy(f32[2048,3584]{0,1:T(8,128)} %multiply_bitcast_fusion) | data formatting | bytes 58720256 | tf_op jit(solution)/shard_map/div | solution.py:60
  (1 shorter events, 0.0 us)
Async XLA Ops:
  6.5 85.9 %all-gather.5.cloned.1.call-start = ((), (), s32[]{:S(2)}) async-start(), calls=%async_computation.3 | async-start | bytes 5242880 | tf_op jit(solution)/shard_map/all_gather | solution.py:23
  7.3 479.2 %reduce-scatter.4.cloned.1.call-start = ((), (), s32[]{:S(2)}) async-start(), calls=%async_computation.4 | async-start | bytes 55050240 | tf_op jit(solution)/shard_map/reduce_scatter | solution.py:27
  92.4 22.9 %copy-start = (bf16[1024,2048]{1,0:T(8,128)(2,1)S(1)}, bf16[1024,2048]{1,0:T(8,128)(2,1)}, u32[]{:S(2)}) copy-start(bf16[1024,2048]{1,0:T(8,128)(2,1)} %all-gather.5.cloned.1.call-done) | copy-start | bytes 12582916
  92.4 44.7 %slice-start = ((s8[14680064]{0:T(1024)(128)(4,1)}), s8[4194304]{0:T(1024)(128)(4,1)S(1)}, s32[]{:S(2)}) async-start(s8[14680064]{0:T(1024)(128)(4,1)} %bitcast.14), calls=%async_computation.10 | async-start | bytes 8388608
  92.4 44.7 %slice-start.1 = ((s8[14680064]{0:T(1024)(128)(4,1)}), s8[4194304]{0:T(1024)(128)(4,1)S(1)}, s32[]{:S(2)}) async-start(s8[14680064]{0:T(1024)(128)(4,1)} %bitcast.14), calls=%async_computation.11 | async-start | bytes 8388608
  115.3 21.8 %slice-start.2 = ((s8[14680064]{0:T(1024)(128)(4,1)}), s8[4194304]{0:T(1024)(128)(4,1)S(1)}, s32[]{:S(2)}) async-start(s8[14680064]{0:T(1024)(128)(4,1)} %bitcast.14), calls=%async_computation.12 | async-start | bytes 8388608
  115.3 21.8 %slice-start.3 = ((s8[14680064]{0:T(1024)(128)(4,1)}), s8[2097152]{0:T(1024)(128)(4,1)S(1)}, s32[]{:S(2)}) async-start(s8[14680064]{0:T(1024)(128)(4,1)} %bitcast.14), calls=%async_computation.13 | async-start | bytes 4194304
  185.5 359.3 %all-gather.7.cloned.1.call-start = ((), (), s32[]{:S(2)}) async-start(), calls=%async_computation.5 | async-start | bytes 9175040 | tf_op jit(solution)/shard_map/all_gather | solution.py:40
  492.3 218.5 %reduce-scatter.6.cloned.1.call-start = ((), (), s32[]{:S(2)}) async-start(), calls=%async_computation.6 | async-start | bytes 10485760 | tf_op jit(solution)/shard_map/reduce_scatter | solution.py:42
  566.1 229.7 %all-gather.9.cloned.1.call-start = ((), (), s32[]{:S(2)}) async-start(), calls=%async_computation.7 | async-start | bytes 5242880 | tf_op jit(solution)/shard_map/all_gather | solution.py:47
  714.2 216.2 %reduce-scatter.8.cloned.1.call-start = ((), (), s32[]{:S(2)}) async-start(), calls=%async_computation.8 | async-start | bytes 18350080 | tf_op jit(solution)/shard_map/reduce_scatter | solution.py:49
  818.8 170.0 %all-gather.11.cloned.1.call-start = ((), (), s32[]{:S(2)}) async-start(), calls=%async_computation.9 | async-start | bytes 9175040 | tf_op jit(solution)/shard_map/all_gather | solution.py:56
Sparse Core Ops, SparseCore 0:
  8.9 83.4 all-gather.4
  185.6 300.8 reduce-scatter.3
  492.4 52.3 all-gather.6
  566.3 144.4 reduce-scatter.5
  714.4 81.4 all-gather.8
  818.9 111.4 reduce-scatter.7
  936.4 52.3 all-gather.10
where the time goes:
time: 1050 us
  waiting for transfers between devices  830 us (79%)
  matrix products  132 us (13%)
  other arithmetic  44.7 us (4%)
  local copies, waits for them, and re-layouts  27.6 us (3%)
  between operations  13.5 us (1%)
    reduce_scatter x1, waiting for transfers between devices, per_device(): lax.psum_scatter(jnp.concatenate([matmul(row_block, w_gate), matmul(row_b...  301 us
    reduce_scatter x1, waiting for transfers between devices, per_device(): lax.psum_scatter(out_part, 'row', scatter_dimension=0, tiled=True)  145 us
    reduce_scatter x1, waiting for transfers between devices, per_device(): lax.psum_scatter(times_down(row_block, w_down), 'col', scatter_dimension=...  112 us
    all_gather x1, waiting for transfers between devices, per_device(): gathered = lax.all_gather(inputs, 'row', axis=0, tiled=True)  85.1 us
    dot_general x4, matrix products, matmul(): return jnp.dot(left, right, preferred_element_type=jnp.float32)  84.7 us
    all_gather x1, waiting for transfers between devices, per_device(): scaled_all = lax.all_gather(scaled, 'row', axis=0, tiled=True)  81.6 us
    all_gather x1, waiting for transfers between devices, per_device(): lax.all_gather(gate_bar, 'col', axis=0, tiled=True)  52.5 us
    all_gather x1, waiting for transfers between devices, per_device(): lax.all_gather(hidden_tangent, 'col', axis=0, tiled=True)  52.4 us
  transfers between devices with their start and end apart: 7, of which 7 were waited for; matrix products, arithmetic and copies ran while one was open for 0% of the time, Pallas kernels for 0%

commit v1 on v0

v1 whole, which is shorter than its diff:
```python
import functools

import jax
import jax.numpy as jnp
from jax import lax
from jax.experimental import pallas as pl
from jax.experimental.pallas import tpu as pltpu
from jax.sharding import PartitionSpec as P

F16_TOP = 32768.0
LEAST_TOP = 1e-30
GROUPS = 2


def matmul(left, right):
    return jnp.dot(left, right, preferred_element_type=jnp.float32)


def times_down(left, w_down):
    return lax.dot_general(
        left, w_down, (((1,), (1,)), ((), ())), preferred_element_type=jnp.float32
    )


def slot_masks(count):
    bits = count.bit_length() - 1
    assert 1 << bits == count
    return [sum(((s >> b) & 1) << (bits - 1 - b) for b in range(bits)) for s in range(count)]


def swap(values, axis, mask):
    count = lax.axis_size(axis)
    return lax.ppermute(values, axis, [(i, i ^ mask) for i in range(count)])


def shift(values, axis):
    count = lax.axis_size(axis)
    return lax.ppermute(values, axis, [(i, (i + 1) % count) for i in range(count)])


def send_16(values, move):
    top = jnp.maximum(jnp.max(jnp.abs(values), axis=-1, keepdims=True), LEAST_TOP)
    coded = (values * (F16_TOP / top)).astype(jnp.float16)
    unit = (top * (1.0 / F16_TOP)).reshape(top.shape[:-1])
    coded, unit = move(coded), move(unit)
    return coded.astype(jnp.float32) * unit[..., None]


def sum_over_col(part):
    count = lax.axis_size("col")
    mask = 1
    while mask < count:
        half = part.shape[0] // 2
        keep, give = part[:half], part[half:]
        if mask == 1:
            part = keep + swap(give, "col", mask)
        else:
            part = keep + send_16(give, lambda v: swap(v, "col", mask))
        mask *= 2
    return part


def gather_over_col(rows):
    mask = lax.axis_size("col") // 2
    while mask >= 1:
        rows = jnp.concatenate([rows, swap(rows, "col", mask)], axis=0)
        mask //= 2
    return rows


def last_kernel(scale, parts, *refs):
    turned, bars, out_ref = refs[:parts], refs[parts : 2 * parts], refs[2 * parts]
    height = out_ref.shape[0]
    step = 512 if height % 512 == 0 else height

    @pl.loop(0, height // step)
    def _(at):
        rows = pl.ds(pl.multiple_of(at * step, step), step)
        total = jnp.dot(turned[0][rows, :], bars[0][...], preferred_element_type=jnp.float32)
        for left, right in zip(turned[1:], bars[1:]):
            total += jnp.dot(left[rows, :], right[...], preferred_element_type=jnp.float32)
        out_ref[rows, :] = total * scale


def last_product(turned, bars, tokens):
    features, hidden = turned[0].shape[0], bars[0].shape[1]
    tile = 512 if hidden % 512 == 0 else hidden
    depth = sum(t.shape[1] for t in turned)
    return pl.pallas_call(
        functools.partial(last_kernel, 1.0 / tokens, len(turned)),
        grid=(hidden // tile,),
        out_shape=jax.ShapeDtypeStruct((features, hidden), jnp.float32),
        in_specs=[pl.BlockSpec(t.shape, lambda j: (0, 0)) for t in turned]
        + [pl.BlockSpec((b.shape[0], tile), lambda j: (0, j)) for b in bars],
        out_specs=pl.BlockSpec((features, tile), lambda j: (0, j)),
        compiler_params=pltpu.CompilerParams(vmem_limit_bytes=40 * 1024 * 1024),
        cost_estimate=pl.CostEstimate(
            flops=2 * features * hidden * depth,
            bytes_accessed=features * hidden * 4 + depth * (features + hidden) * 2,
            transcendentals=0,
        ),
    )(*turned, *bars)


def per_device(inputs, w_gate, w_up, w_down, query, curvature):
    ring, count = lax.axis_size("row"), lax.axis_size("col")
    assert lax.axis_size("grp") == 2
    shard, width = inputs.shape
    tokens = shard * ring
    rows = shard // 2 // count
    per_group = ring // GROUPS
    masks = slot_masks(count)
    place, grp, me = lax.axis_index("col"), lax.axis_index("grp"), lax.axis_index("row")

    def own_rows(array, start, half):
        begin = start + half * (shard // 2)
        return jnp.stack(
            [
                lax.dynamic_slice_in_dim(array, begin + (place ^ mask) * rows, rows, 0)
                for mask in masks
            ]
        )

    def ring_pieces(first):
        pieces = [first]
        for _ in range(ring - 1):
            pieces.append(shift(pieces[-1], "row"))
        return pieces

    def grouped(pieces):
        return [
            jnp.concatenate(pieces[j * per_group : (j + 1) * per_group], axis=1).reshape(
                count * per_group * rows, width
            )
            for j in range(GROUPS)
        ]

    first = ring_pieces(own_rows(inputs, 0, grp))
    second = [own_rows(inputs, 0, 1 - grp)] + [swap(piece, "grp", 1) for piece in first[1:]]
    acts = [grouped(first), grouped(second)]
    curv = [own_rows(curvature, me * shard, grp), own_rows(curvature, me * shard, 1 - grp)]

    def out_pieces(half, gains):
        pieces = []
        for j in range(GROUPS):
            tangent = sum_over_col(matmul(acts[half][j], query))
            hidden_tangent = (gains[j] * tangent).astype(jnp.bfloat16)
            part = matmul(gather_over_col(hidden_tangent), w_down)
            part = part.reshape(count, per_group, rows, width)
            pieces += [part[:, k] for k in range(per_group)]
        return pieces

    def scaled_groups(half, pieces):
        total = pieces[1 % ring]
        for k in range(2, ring + 1):
            total = send_16(total, lambda v: shift(v, "row")) + pieces[k % ring]
        return grouped(ring_pieces((curv[half] * total).astype(jnp.bfloat16)))

    gains = []
    for j in range(GROUPS):
        gate_out = sum_over_col(matmul(acts[0][j], w_gate))
        up_out = sum_over_col(matmul(acts[0][j], w_up))
        sigmas = jax.nn.sigmoid(gate_out)
        gains.append(sigmas * (1.0 + gate_out * (1.0 - sigmas)) * up_out)
    gains = [gains, [swap(gain, "grp", 1) for gain in gains]]

    bars = []
    for half in range(2):
        groups = scaled_groups(half, out_pieces(half, gains[half]))
        for j in range(GROUPS):
            back = sum_over_col(times_down(groups[j], w_down))
            bars.append(gather_over_col((back * gains[half][j]).astype(jnp.bfloat16)))
    turned = [act.T for half in range(2) for act in acts[half]]
    return last_product(turned, bars, tokens)


def solution(mesh):
    in_specs = (
        P("row", "col"),
        P("col", "row"),
        P("col", "row"),
        P("row", "col"),
        P(("grp", "col"), "row"),
        P("grp", "col"),
    )
    out_specs = P(("grp", "col"), "row")
    return jax.shard_map(
        per_device, mesh=mesh, in_specs=in_specs, out_specs=out_specs, check_vma=False
    )
```

time: 1050 us -> 489 us (0.47)
  waiting for transfers between devices: 830 us -> 227 us
  starting transfers between devices: 0.25 us -> 52.4 us
  Pallas kernels: 0 us -> 22.5 us
  matrix products: 132 us -> 114 us
  between operations: 13.5 us -> 1.75 us
    reduce_scatter x3 -> x0, waiting for transfers between devices: 557 us -> none  [the longest x1 301 us: per_device(): lax.psum_scatter(jnp.concatenate([matmul(row_block, w_gate), matmul(row_b...]
    all_gather x4 -> x0, waiting for transfers between devices: 272 us -> none  [the longest x1 85.1 us: per_device(): gathered = lax.all_gather(inputs, 'row', axis=0, tiled=True)]
    ppermute x0 -> x78, waiting for transfers between devices: none -> 227 us  [the longest x57 122 us: swap(): return lax.ppermute(values, axis, [(i, i ^ mask) for i in range(count)])]
    ppermute x0 -> x78, starting transfers between devices: none -> 52.4 us  [the longest x57 44.1 us: swap(): return lax.ppermute(values, axis, [(i, i ^ mask) for i in range(count)])]
    div x1 -> x0, local copies, waits for them, and re-layouts: 27.6 us -> none  [per_device(): return result / tokens_all]
    dot_general x1 -> x0, matrix products: 24.2 us -> none  [per_device(): lax.dot_general(row_block, lax.all_gather(gate_bar, 'col', axis=0, tiled=...]
    pallas_call x0 -> x1, Pallas kernels: none -> 22.5 us  [last_product(): pl.pallas_call(functools.partial(last_kernel, 1.0 / tokens, len(turned)),...]
    concatenate x1 -> x20, other arithmetic: 29.6 us -> 8.26 us  [the longest x8 7.3 us: grouped(): jnp.concatenate(pieces[j * per_group:(j + 1) * per_group], axis=1)]
  transfers between devices with their start and end apart: 7 -> 78, of which waited for: 7 -> 31; matrix products, arithmetic and copies ran while one was open for 0% -> 35% of each run, Pallas kernels for 0% -> 0%
where the time goes in v1:
time: 489 us; the launch traced here: 483 us
  waiting for transfers between devices  227 us (46%)
  matrix products  114 us (23%)
  starting transfers between devices  52.4 us (11%)
  other arithmetic  40 us (8%)
  local copies, waits for them, and re-layouts  25.5 us (5%)
  Pallas kernels  22.5 us (5%)
    ppermute x57, waiting for transfers between devices, swap(): return lax.ppermute(values, axis, [(i, i ^ mask) for i in range(count)])  122 us
    ppermute x21, waiting for transfers between devices, shift(): lax.ppermute(values, axis, [(i, (i + 1) % count) for i in range(count)])  105 us
    dot_general x12, matrix products, matmul(): return jnp.dot(left, right, preferred_element_type=jnp.float32)  82.5 us
    ppermute x57, starting transfers between devices, swap(): return lax.ppermute(values, axis, [(i, i ^ mask) for i in range(count)])  44.1 us
    dot_general x4, matrix products, times_down(): lax.dot_general(left, w_down, (((1,), (1,)), ((), ())), preferred_element...  31.7 us
    pallas_call x1, Pallas kernels, last_product(): pl.pallas_call(functools.partial(last_kernel, 1.0 / tokens, len(turned)),...  22.5 us
    add x12, other arithmetic, sum_over_col(): part = keep + swap(give, 'col', mask)  16.6 us
    slice x12, local copies, waits for them, and re-layouts, sum_over_col(): keep, give = (part[:half], part[half:])  14.6 us
  transfers between devices with their start and end apart: 78, of which 31 were waited for; matrix products, arithmetic and copies ran while one was open for 35% of the time, Pallas kernels for 0%

profile of v1, /device:TPU:0, one launch (start us, length us, event | category | flops | bytes accessed | tf_op | source)
XLA Modules:
  0.0 483.1 jit_solution(14114586367263789443)
XLA Ops:
  1.4 3.1 collective-permute-start
  4.5 13.9 %collective-permute-done = bf16[4,32,2048]{2,1,0:T(8,128)(2,1)S(1)} collective-permute-done((bf16[4,32,2048]{2,1,0:T(8,128)(2,1)S(1)}, bf16[4,32,2048]{2,1,0:T(8,128)(2,1)S(1)}, u32[]{:S(2)}, u32[]{:S(2)}) %collective-permute-start) | collective-permute-done | bytes 524320 | tf_op jit(solution)/shard_map/ppermute | solution.py:38
  18.6 7.4 %fusion.60 = f32[256,3584]{1,0:T(8,128)S(1)} fusion(bf16[256,2048]{1,0:T(8,128)(2,1)S(1)} %bitcast.166, bf16[2048,3584]{1,0:T(8,128)(2,1)} %param.10), kind=kOutput, calls=%fused_computation.199 | convolution fusion | flops 3758096384 | bytes 19398656 | tf_op jit(solution)/shard_map/dot_general | solution.py:16
  27.9 3.9 fusion.59
  34.9 7.2 %fusion.58 = f32[256,3584]{1,0:T(8,128)S(1)} fusion(bf16[256,2048]{1,0:T(8,128)(2,1)S(1)} %bitcast.168, bf16[2048,3584]{1,0:T(8,128)(2,1)} %param.7), kind=kOutput, calls=%fused_computation.197 | convolution fusion | flops 3758096384 | bytes 19398656 | tf_op jit(solution)/shard_map/dot_general | solution.py:16
  43.8 7.0 %collective-permute-done.1 = bf16[4,32,2048]{2,1,0:T(8,128)(2,1)S(1)} collective-permute-done((bf16[4,32,2048]{2,1,0:T(8,128)(2,1)S(1)}, bf16[4,32,2048]{2,1,0:T(8,128)(2,1)S(1)}, u32[]{:S(2)}, u32[]{:S(2)}) %collective-permute-start.1) | collective-permute-done | bytes 524320 | tf_op jit(solution)/shard_map/ppermute | solution.py:38
  51.3 7.3 %fusion.66 = f32[256,3584]{1,0:T(8,128)S(1)} fusion(bf16[256,2048]{1,0:T(8,128)(2,1)S(1)} %bitcast.170, bf16[2048,3584]{1,0:T(8,128)(2,1)} %param.10), kind=kOutput, calls=%fused_computation.205 | convolution fusion | flops 3758096384 | bytes 19398656 | tf_op jit(solution)/shard_map/dot_general | solution.py:16
  60.5 5.8 %collective-permute-done.2 = bf16[4,32,2048]{2,1,0:T(8,128)(2,1)S(1)} collective-permute-done((bf16[4,32,2048]{2,1,0:T(8,128)(2,1)S(1)}, bf16[4,32,2048]{2,1,0:T(8,128)(2,1)S(1)}, u32[]{:S(2)}, u32[]{:S(2)}) %collective-permute-start.2) | collective-permute-done | bytes 524320 | tf_op jit(solution)/shard_map/ppermute | solution.py:38
  66.4 7.7 %fusion.63 = f32[256,3584]{1,0:T(8,128)S(1)} fusion(bf16[256,2048]{1,0:T(8,128)(2,1)S(1)} %bitcast.172, bf16[2048,3584]{1,0:T(8,128)(2,1)} %param.10), kind=kOutput, calls=%fused_computation.202 | convolution fusion | flops 3758096384 | bytes 19398656 | tf_op jit(solution)/shard_map/dot_general | solution.py:16
  74.1 7.3 %fusion.62 = f32[256,3584]{1,0:T(8,128)S(1)} fusion(bf16[256,2048]{1,0:T(8,128)(2,1)S(1)} %bitcast.173, bf16[2048,3584]{1,0:T(8,128)(2,1)} %param.8), kind=kOutput, calls=%fused_computation.201 | convolution fusion | flops 3758096384 | bytes 19398656 | tf_op jit(solution)/shard_map/dot_general | solution.py:16
  81.9 7.3 %fusion.61 = f32[256,3584]{1,0:T(8,128)S(1)} fusion(bf16[256,2048]{1,0:T(8,128)(2,1)S(1)} %bitcast.174, bf16[2048,3584]{1,0:T(8,128)(2,1)} %param.7), kind=kOutput, calls=%fused_computation.200 | convolution fusion | flops 3758096384 | bytes 19398656 | tf_op jit(solution)/shard_map/dot_general | solution.py:16
  106.3 5.1 %collective-permute-done.11 = f32[64]{0:T(128)S(1)} collective-permute-done((f32[64]{0:T(128)S(1)}, f32[64]{0:T(128)S(1)}, u32[]{:S(2)}, u32[]{:S(2)}) %collective-permute-start.11) | collective-permute-done | bytes 288 | tf_op jit(solution)/shard_map/ppermute | solution.py:33
  112.0 7.6 %fusion.67 = f32[256,3584]{1,0:T(8,128)S(1)} fusion(bf16[256,2048]{1,0:T(8,128)(2,1)S(1)} %bitcast.176, bf16[2048,3584]{1,0:T(8,128)(2,1)} %param.10), kind=kOutput, calls=%fused_computation.206 | convolution fusion | flops 3758096384 | bytes 19398656 | tf_op jit(solution)/shard_map/dot_general | solution.py:16
  121.9 8.0 %collective-permute-done.7 = f16[64,3584]{1,0:T(8,128)(2,1)S(1)} collective-permute-done((f16[64,3584]{1,0:T(8,128)(2,1)S(1)}, f16[64,3584]{1,0:T(8,128)(2,1)S(1)}, u32[]{:S(2)}, u32[]{:S(2)}) %collective-permute-start.7) | collective-permute-done | bytes 458784 | tf_op jit(solution)/shard_map/ppermute | solution.py:33
  134.8 7.3 %collective-permute-done.15 = bf16[64,3584]{1,0:T(8,128)(2,1)S(1)} collective-permute-done((bf16[64,3584]{1,0:T(8,128)(2,1)S(1)}, bf16[64,3584]{1,0:T(8,128)(2,1)S(1)}, u32[]{:S(2)}, u32[]{:S(2)}) %collective-permute-start.15) | collective-permute-done | bytes 458784 | tf_op jit(solution)/shard_map/ppermute | solution.py:33
  157.2 19.1 %collective-permute-done.21 = f32[64]{0:T(128)S(1)} collective-permute-done((f32[64]{0:T(128)S(1)}, f32[64]{0:T(128)S(1)}, u32[]{:S(2)}, u32[]{:S(2)}) %collective-permute-start.21) | collective-permute-done | bytes 288 | tf_op jit(solution)/shard_map/ppermute | solution.py:33
  177.8 8.2 %collective-permute-done.20 = f16[64,3584]{1,0:T(8,128)(2,1)S(1)} collective-permute-done((f16[64,3584]{1,0:T(8,128)(2,1)S(1)}, f16[64,3584]{1,0:T(8,128)(2,1)S(1)}, u32[]{:S(2)}, u32[]{:S(2)}) %collective-permute-start.20) | collective-permute-done | bytes 458784 | tf_op jit(solution)/shard_map/ppermute | solution.py:33
  192.8 7.2 %fusion = f32[256,2048]{1,0:T(8,128)S(1)} fusion(bf16[3584,2048]{1,0:T(8,128)(2,1)} %param.9, bf16[128,3584]{1,0:T(8,128)(2,1)S(1)} %collective-permute-done.16, bf16[64,3584]{1,0:T(8,128)(2,1)S(1)} %collective-permute-done.15, bf16[64,3584]{1,0:T(8,128)(2,1)S(1)} %get-tuple-element.7), kind=kOutput, calls=%fused_computation.12 | convolution fusion | flops 3763601408 | bytes 18612224 | tf_op jit(solution)/shard_map/dot_general | solution.py:16
  200.5 5.2 %collective-permute-done.28 = bf16[64,3584]{1,0:T(8,128)(2,1)S(1)} collective-permute-done((bf16[64,3584]{1,0:T(8,128)(2,1)S(1)}, bf16[64,3584]{1,0:T(8,128)(2,1)S(1)}, u32[]{:S(2)}, u32[]{:S(2)}) %collective-permute-start.28) | collective-permute-done | bytes 458784 | tf_op jit(solution)/shard_map/ppermute | solution.py:33
  205.9 7.4 %collective-permute-done.57 = f16[64,3584]{1,0:T(8,128)(2,1)S(1)} collective-permute-done((f16[64,3584]{1,0:T(8,128)(2,1)S(1)}, f16[64,3584]{1,0:T(8,128)(2,1)S(1)}, u32[]{:S(2)}, u32[]{:S(2)}) %collective-permute-start.57) | collective-permute-done | bytes 458784 | tf_op jit(solution)/shard_map/ppermute | solution.py:33
  214.2 7.4 %fusion.12 = f32[256,2048]{1,0:T(8,128)S(1)} fusion(bf16[3584,2048]{1,0:T(8,128)(2,1)} %param.9, bf16[128,3584]{1,0:T(8,128)(2,1)S(1)} %collective-permute-done.52, bf16[64,3584]{1,0:T(8,128)(2,1)S(1)} %collective-permute-done.51, bf16[64,3584]{1,0:T(8,128)(2,1)S(1)} %fusion.41), kind=kOutput, calls=%fused_computation.26 | convolution fusion | flops 3763601408 | bytes 18612224 | tf_op jit(solution)/shard_map/dot_general | solution.py:16
  221.9 7.9 %fusion.6 = f32[256,2048]{1,0:T(8,128)S(1)} fusion(bf16[3584,2048]{1,0:T(8,128)(2,1)} %param.9, bf16[128,3584]{1,0:T(8,128)(2,1)S(1)} %collective-permute-done.29, bf16[64,3584]{1,0:T(8,128)(2,1)S(1)} %collective-permute-done.28, bf16[64,3584]{1,0:T(8,128)(2,1)S(1)} %get-tuple-element.5), kind=kOutput, calls=%fused_computation.18 | convolution fusion | flops 3763601408 | bytes 18612224 | tf_op jit(solution)/shard_map/dot_general | solution.py:16
  231.5 3.9 collective-permute-start.53
  235.4 11.6 %collective-permute-done.31 = f32[4,32]{1,0:T(4,128)S(1)} collective-permute-done((f32[4,32]{1,0:T(4,128)S(1)}, f32[4,32]{1,0:T(4,128)S(1)}, u32[]{:S(2)}, u32[]{:S(2)}) %collective-permute-start.31) | collective-permute-done | bytes 544 | tf_op jit(solution)/shard_map/ppermute | solution.py:38
  247.9 4.2 fusion.18
  252.2 6.1 %collective-permute-done.53 = f16[4,32,2048]{2,1,0:T(8,128)(2,1)S(1)} collective-permute-done((f16[4,32,2048]{2,1,0:T(8,128)(2,1)S(1)}, f16[4,32,2048]{2,1,0:T(8,128)(2,1)S(1)}, u32[]{:S(2)}, u32[]{:S(2)}) %collective-permute-start.53) | collective-permute-done | bytes 524320 | tf_op jit(solution)/shard_map/ppermute | solution.py:38
  259.0 2.5 dynamic-slice_bitcast_fusion.3
  261.5 8.0 %collective-permute-done.32 = f16[4,32,2048]{2,1,0:T(8,128)(2,1)S(1)} collective-permute-done((f16[4,32,2048]{2,1,0:T(8,128)(2,1)S(1)}, f16[4,32,2048]{2,1,0:T(8,128)(2,1)S(1)}, u32[]{:S(2)}, u32[]{:S(2)}) %collective-permute-start.32) | collective-permute-done | bytes 524320 | tf_op jit(solution)/shard_map/ppermute | solution.py:38
  270.6 10.2 %collective-permute-done.62 = f32[4,32]{1,0:T(4,128)S(1)} collective-permute-done((f32[4,32]{1,0:T(4,128)S(1)}, f32[4,32]{1,0:T(4,128)S(1)}, u32[]{:S(2)}, u32[]{:S(2)}) %collective-permute-start.62) | collective-permute-done | bytes 544 | tf_op jit(solution)/shard_map/ppermute | solution.py:38
  284.9 2.3 copy.16
  287.2 5.0 %collective-permute-done.34 = bf16[4,32,2048]{2,1,0:T(8,128)(2,1)} collective-permute-done((bf16[4,32,2048]{2,1,0:T(8,128)(2,1)}, bf16[4,32,2048]{2,1,0:T(8,128)(2,1)}, u32[]{:S(2)}, u32[]{:S(2)}) %collective-permute-start.34) | collective-permute-done | bytes 524320 | tf_op jit(solution)/shard_map/ppermute | solution.py:38
  292.2 2.3 pad_maximum_fusion.8
  294.5 8.9 %collective-permute-done.64 = f32[4,32]{1,0:T(4,128)S(1)} collective-permute-done((f32[4,32]{1,0:T(4,128)S(1)}, f32[4,32]{1,0:T(4,128)S(1)}, u32[]{:S(2)}, u32[]{:S(2)}) %collective-permute-start.64) | collective-permute-done | bytes 544 | tf_op jit(solution)/shard_map/ppermute | solution.py:38
  305.1 7.6 %fusion.64 = f32[256,3584]{1,0:T(8,128)S(1)} fusion(bf16[256,2048]{1,0:T(8,128)(2,1)} %bitcast.178, bf16[3584,2048]{1,0:T(8,128)(2,1)} %param.9), kind=kOutput, calls=%fused_computation.203 | convolution fusion | flops 3758096384 | bytes 19398656 | tf_op jit(solution)/shard_map/dot_general | solution.py:20
  314.6 11.3 %collective-permute-done.65 = bf16[4,32,2048]{2,1,0:T(8,128)(2,1)} collective-permute-done((bf16[4,32,2048]{2,1,0:T(8,128)(2,1)S(1)}, bf16[4,32,2048]{2,1,0:T(8,128)(2,1)}, u32[]{:S(2)}, u32[]{:S(2)}) %collective-permute-start.65) | collective-permute-done | bytes 524320 | tf_op jit(solution)/shard_map/ppermute | solution.py:38
  328.1 7.6 %fusion.68 = f32[256,3584]{1,0:T(8,128)S(1)} fusion(bf16[256,2048]{1,0:T(8,128)(2,1)} %bitcast.181, bf16[3584,2048]{1,0:T(8,128)(2,1)} %param.9), kind=kOutput, calls=%fused_computation.207 | convolution fusion | flops 3758096384 | bytes 19398656 | tf_op jit(solution)/shard_map/dot_general | solution.py:20
  338.9 7.3 %fusion.65 = f32[256,3584]{1,0:T(8,128)S(1)} fusion(bf16[256,2048]{1,0:T(8,128)(2,1)S(1)} %bitcast.179, bf16[3584,2048]{1,0:T(8,128)(2,1)} %param.9), kind=kOutput, calls=%fused_computation.204 | convolution fusion | flops 3758096384 | bytes 19398656 | tf_op jit(solution)/shard_map/dot_general | solution.py:20
  348.0 5.9 %collective-permute-done.71 = bf16[4,32,2048]{2,1,0:T(8,128)(2,1)} collective-permute-done((bf16[4,32,2048]{2,1,0:T(8,128)(2,1)}, bf16[4,32,2048]{2,1,0:T(8,128)(2,1)}, u32[]{:S(2)}, u32[]{:S(2)}) %collective-permute-start.71) | collective-permute-done | bytes 524320 | tf_op jit(solution)/shard_map/ppermute | solution.py:38
  358.8 10.6 %collective-permute-done.72 = bf16[4,32,2048]{2,1,0:T(8,128)(2,1)S(1)} collective-permute-done((bf16[4,32,2048]{2,1,0:T(8,128)(2,1)}, bf16[4,32,2048]{2,1,0:T(8,128)(2,1)S(1)}, u32[]{:S(2)}, u32[]{:S(2)}) %collective-permute-start.72) | collective-permute-done | bytes 524320 | tf_op jit(solution)/shard_map/ppermute | solution.py:38
  370.6 9.1 %fusion.69 = f32[256,3584]{1,0:T(8,128)} fusion(bf16[256,2048]{1,0:T(8,128)(2,1)S(1)} %bitcast.180, bf16[3584,2048]{1,0:T(8,128)(2,1)} %param.9), kind=kOutput, calls=%fused_computation.208 | convolution fusion | flops 3758096384 | bytes 19398656 | tf_op jit(solution)/shard_map/dot_general | solution.py:20
  388.7 7.6 %collective-permute-done.38 = bf16[64,3584]{1,0:T(8,128)(2,1)S(1)} collective-permute-done((bf16[64,3584]{1,0:T(8,128)(2,1)S(1)}, bf16[64,3584]{1,0:T(8,128)(2,1)S(1)}, u32[]{:S(2)}, u32[]{:S(2)}) %collective-permute-start.38) | collective-permute-done | bytes 458784 | tf_op jit(solution)/shard_map/ppermute | solution.py:33
  400.7 5.4 %collective-permute-done.67 = f16[64,3584]{1,0:T(8,128)(2,1)S(1)} collective-permute-done((f16[64,3584]{1,0:T(8,128)(2,1)S(1)}, f16[64,3584]{1,0:T(8,128)(2,1)S(1)}, u32[]{:S(2)}, u32[]{:S(2)}) %collective-permute-start.67) | collective-permute-done | bytes 458784 | tf_op jit(solution)/shard_map/ppermute | solution.py:33
  408.0 8.0 %collective-permute-done.43 = f16[64,3584]{1,0:T(8,128)(2,1)S(1)} collective-permute-done((f16[64,3584]{1,0:T(8,128)(2,1)S(1)}, f16[64,3584]{1,0:T(8,128)(2,1)S(1)}, u32[]{:S(2)}, u32[]{:S(2)}) %collective-permute-start.43) | collective-permute-done | bytes 458784 | tf_op jit(solution)/shard_map/ppermute | solution.py:33
  421.0 4.8 %collective-permute-done.69 = bf16[64,3584]{1,0:T(8,128)(2,1)S(1)} collective-permute-done((bf16[64,3584]{1,0:T(8,128)(2,1)S(1)}, bf16[64,3584]{1,0:T(8,128)(2,1)S(1)}, u32[]{:S(2)}, u32[]{:S(2)}) %collective-permute-start.69) | collective-permute-done | bytes 458784 | tf_op jit(solution)/shard_map/ppermute | solution.py:33
  426.0 9.8 %collective-permute-done.75 = f32[64]{0:T(128)S(1)} collective-permute-done((f32[64]{0:T(128)S(1)}, f32[64]{0:T(128)S(1)}, u32[]{:S(2)}, u32[]{:S(2)}) %collective-permute-start.75) | collective-permute-done | bytes 288 | tf_op jit(solution)/shard_map/ppermute | solution.py:33
  435.7 9.3 %collective-permute-done.74 = f16[64,3584]{1,0:T(8,128)(2,1)S(1)} collective-permute-done((f16[64,3584]{1,0:T(8,128)(2,1)S(1)}, f16[64,3584]{1,0:T(8,128)(2,1)S(1)}, u32[]{:S(2)}, u32[]{:S(2)}) %collective-permute-start.74) | collective-permute-done | bytes 458784 | tf_op jit(solution)/shard_map/ppermute | solution.py:33
  447.0 10.5 %collective-permute-done.76 = bf16[64,3584]{1,0:T(8,128)(2,1)S(1)} collective-permute-done((bf16[64,3584]{1,0:T(8,128)(2,1)S(1)}, bf16[64,3584]{1,0:T(8,128)(2,1)S(1)}, u32[]{:S(2)}, u32[]{:S(2)}) %collective-permute-start.76) | collective-permute-done | bytes 458784 | tf_op jit(solution)/shard_map/ppermute | solution.py:33
  460.2 22.5 %shard_map.64 = f32[2048,3584]{1,0:T(8,128)} custom-call(bf16[2048,256]{1,0:T(8,128)(2,1)S(1)} %bitcast.148, bf16[2048,256]{1,0:T(8,128)(2,1)S(1)} %bitcast.150, bf16[2048,256]{1,0:T(8,128)(2,1)S(1)} %bitcast.149, bf16[2048,256]{1,0:T(8,128)(2,1)S(1)} %bitcast.151, bf16[256,3584]{1,0:T(8,128)(2,1)S(1)} %pad_maximum_fusion.refs_4_, ...), custom_call_target="tpu_custom_call" | custom-call | flops 15032385536 | bytes 40894464 | tf_op jit(solution)/shard_map/pallas_call | solution.py:89
  (310 shorter events, 110.5 us)
Async XLA Ops:
  26.1 67.7 %collective-permute-start.12 = (f32[128,3584]{1,0:T(8,128)S(1)}, f32[128,3584]{1,0:T(8,128)}, u32[]{:S(2)}, u32[]{:S(2)}) collective-permute-start(f32[128,3584]{1,0:T(8,128)S(1)} %slice.233), channel_id=1, source_target_pairs={{0,1},{1,0},{2,3},{3,2},{4,5},{5,4},{6,7},{7,6},{8,9},{9,8},{10,11... | collective-permute-start | bytes 5505032 | tf_op jit(solution)/shard_map/ppermute | solution.py:33
  33.4 65.1 %collective-permute-start.9 = (f32[128,3584]{1,0:T(8,128)}, f32[128,3584]{1,0:T(8,128)}, u32[]{:S(2)}, u32[]{:S(2)}) collective-permute-start(f32[128,3584]{1,0:T(8,128)} %slice.229), channel_id=1, source_target_pairs={{0,1},{1,0},{2,3},{3,2},{4,5},{5,4},{6,7},{7,6},{8,9},{9,8},{10,11... | collective-permute-start | bytes 5505032 | tf_op jit(solution)/shard_map/ppermute | solution.py:33
  33.4 17.8 %collective-permute-start.3 = (bf16[4,32,2048]{2,1,0:T(8,128)(2,1)S(1)}, bf16[4,32,2048]{2,1,0:T(8,128)(2,1)S(1)}, u32[]{:S(2)}, u32[]{:S(2)}) collective-permute-start(bf16[4,32,2048]{2,1,0:T(8,128)(2,1)S(1)} %collective-permute-done), channel_id=1, source_target_pairs={{0,16},{16,0},{1,17},{17,1},{2,18},{18,2},{3,19},{19,3},{4,20},{20... | collective-permute-start | bytes 1572872 | tf_op jit(solution)/shard_map/ppermute | solution.py:33
  43.5 58.6 %collective-permute-start.6 = (f32[128,3584]{1,0:T(8,128)}, f32[128,3584]{1,0:T(8,128)}, u32[]{:S(2)}, u32[]{:S(2)}) collective-permute-start(f32[128,3584]{1,0:T(8,128)} %slice.225), channel_id=1, source_target_pairs={{0,1},{1,0},{2,3},{3,2},{4,5},{5,4},{6,7},{7,6},{8,9},{9,8},{10,11... | collective-permute-start | bytes 5505032 | tf_op jit(solution)/shard_map/ppermute | solution.py:33
  59.9 33.4 %collective-permute-start.4 = (bf16[4,32,2048]{2,1,0:T(8,128)(2,1)S(1)}, bf16[4,32,2048]{2,1,0:T(8,128)(2,1)S(1)}, u32[]{:S(2)}, u32[]{:S(2)}) collective-permute-start(bf16[4,32,2048]{2,1,0:T(8,128)(2,1)S(1)} %collective-permute-done.1), channel_id=1, source_target_pairs={{0,16},{16,0},{1,17},{17,1},{2,18},{18,2},{3,19},{19,3},{4,20},{20... | collective-permute-start | bytes 1572872 | tf_op jit(solution)/shard_map/ppermute | solution.py:33
  93.3 37.9 %collective-permute-start.48 = (f32[128,3584]{1,0:T(8,128)}, f32[128,3584]{1,0:T(8,128)}, u32[]{:S(2)}, u32[]{:S(2)}) collective-permute-start(f32[128,3584]{1,0:T(8,128)} %slice.261), channel_id=1, source_target_pairs={{0,1},{1,0},{2,3},{3,2},{4,5},{5,4},{6,7},{7,6},{8,9},{9,8},{10,11... | collective-permute-start | bytes 5505032 | tf_op jit(solution)/shard_map/ppermute | solution.py:33
  97.9 23.4 %collective-permute-start.13 = (f16[64,3584]{1,0:T(8,128)(2,1)S(1)}, f16[64,3584]{1,0:T(8,128)(2,1)S(1)}, u32[]{:S(2)}, u32[]{:S(2)}) collective-permute-start(f16[64,3584]{1,0:T(8,128)(2,1)S(1)} %multiply_convert_fusion.15), channel_id=1, source_target_pairs={{0,2},{1,3},{2,0},{3,1},{4,6},{5,7},{6,4},{7,5},{8,10},{9,11},{10,... | collective-permute-start | bytes 1376264 | tf_op jit(solution)/shard_map/ppermute | solution.py:33
  102.1 19.7 %collective-permute-start.10 = (f16[64,3584]{1,0:T(8,128)(2,1)S(1)}, f16[64,3584]{1,0:T(8,128)(2,1)S(1)}, u32[]{:S(2)}, u32[]{:S(2)}) collective-permute-start(f16[64,3584]{1,0:T(8,128)(2,1)S(1)} %multiply_convert_fusion.16), channel_id=1, source_target_pairs={{0,2},{1,3},{2,0},{3,1},{4,6},{5,7},{6,4},{7,5},{8,10},{9,11},{10,... | collective-permute-start | bytes 1376264 | tf_op jit(solution)/shard_map/ppermute | solution.py:33
  111.4 18.5 %collective-permute-start.7 = (f16[64,3584]{1,0:T(8,128)(2,1)S(1)}, f16[64,3584]{1,0:T(8,128)(2,1)S(1)}, u32[]{:S(2)}, u32[]{:S(2)}) collective-permute-start(f16[64,3584]{1,0:T(8,128)(2,1)S(1)} %multiply_convert_fusion.17), channel_id=1, source_target_pairs={{0,2},{1,3},{2,0},{3,1},{4,6},{5,7},{6,4},{7,5},{8,10},{9,11},{10,... | collective-permute-start | bytes 1376264 | tf_op jit(solution)/shard_map/ppermute | solution.py:33
  121.3 21.4 %collective-permute-start.25 = (f32[128,3584]{1,0:T(8,128)S(1)}, f32[128,3584]{1,0:T(8,128)}, u32[]{:S(2)}, u32[]{:S(2)}) collective-permute-start(f32[128,3584]{1,0:T(8,128)S(1)} %copy-done.24), channel_id=1, source_target_pairs={{0,1},{1,0},{2,3},{3,2},{4,5},{5,4},{6,7},{7,6},{8,9},{9,8},{10,11... | collective-permute-start | bytes 5505032 | tf_op jit(solution)/shard_map/ppermute | solution.py:33
  121.3 24.8 %collective-permute-start.22 = (f32[128,3584]{1,0:T(8,128)S(1)}, f32[128,3584]{1,0:T(8,128)}, u32[]{:S(2)}, u32[]{:S(2)}) collective-permute-start(f32[128,3584]{1,0:T(8,128)S(1)} %copy-done.23), channel_id=1, source_target_pairs={{0,1},{1,0},{2,3},{3,2},{4,5},{5,4},{6,7},{7,6},{8,9},{9,8},{10,11... | collective-permute-start | bytes 5505032 | tf_op jit(solution)/shard_map/ppermute | solution.py:33
  121.8 27.1 %collective-permute-start.19 = (f32[128,3584]{1,0:T(8,128)S(1)}, f32[128,3584]{1,0:T(8,128)S(1)}, u32[]{:S(2)}, u32[]{:S(2)}) collective-permute-start(f32[128,3584]{1,0:T(8,128)S(1)} %copy-done.22), channel_id=1, source_target_pairs={{0,1},{1,0},{2,3},{3,2},{4,5},{5,4},{6,7},{7,6},{8,9},{9,8},{10,11... | collective-permute-start | bytes 5505032 | tf_op jit(solution)/shard_map/ppermute | solution.py:33
  131.2 25.3 %collective-permute-start.47 = (f32[64,3584]{1,0:T(8,128)S(1)}, f32[64,3584]{1,0:T(8,128)S(1)}, u32[]{:S(2)}, u32[]{:S(2)}) collective-permute-start(f32[64,3584]{1,0:T(8,128)S(1)} %get-tuple-element.8), channel_id=1, source_target_pairs={{0,16},{16,0},{1,17},{17,1},{2,18},{18,2},{3,19},{19,3},{4,20},{20... | collective-permute-start | bytes 2752520 | tf_op jit(solution)/shard_map/ppermute | solution.py:33
  151.1 39.0 %collective-permute-start.56 = (f32[128,3584]{1,0:T(8,128)S(1)}, f32[128,3584]{1,0:T(8,128)S(1)}, u32[]{:S(2)}, u32[]{:S(2)}) collective-permute-start(f32[128,3584]{1,0:T(8,128)S(1)} %slice.266), channel_id=1, source_target_pairs={{0,1},{1,0},{2,3},{3,2},{4,5},{5,4},{6,7},{7,6},{8,9},{9,8},{10,11... | collective-permute-start | bytes 5505032 | tf_op jit(solution)/shard_map/ppermute | solution.py:33
  152.9 23.4 %collective-permute-start.26 = (f16[64,3584]{1,0:T(8,128)(2,1)S(1)}, f16[64,3584]{1,0:T(8,128)(2,1)S(1)}, u32[]{:S(2)}, u32[]{:S(2)}) collective-permute-start(f16[64,3584]{1,0:T(8,128)(2,1)S(1)} %multiply_convert_fusion.12), channel_id=1, source_target_pairs={{0,2},{1,3},{2,0},{3,1},{4,6},{5,7},{6,4},{7,5},{8,10},{9,11},{10,... | collective-permute-start | bytes 1376264 | tf_op jit(solution)/shard_map/ppermute | solution.py:33
  154.4 23.4 %collective-permute-start.23 = (f16[64,3584]{1,0:T(8,128)(2,1)S(1)}, f16[64,3584]{1,0:T(8,128)(2,1)S(1)}, u32[]{:S(2)}, u32[]{:S(2)}) collective-permute-start(f16[64,3584]{1,0:T(8,128)(2,1)S(1)} %multiply_convert_fusion.13), channel_id=1, source_target_pairs={{0,2},{1,3},{2,0},{3,1},{4,6},{5,7},{6,4},{7,5},{8,10},{9,11},{10,... | collective-permute-start | bytes 1376264 | tf_op jit(solution)/shard_map/ppermute | solution.py:33
  154.9 21.3 %collective-permute-start.21 = (f32[64]{0:T(128)S(1)}, f32[64]{0:T(128)S(1)}, u32[]{:S(2)}, u32[]{:S(2)}) collective-permute-start(f32[64]{0:T(128)S(1)} %get-tuple-element.50), channel_id=1, source_target_pairs={{0,2},{1,3},{2,0},{3,1},{4,6},{5,7},{6,4},{7,5},{8,10},{9,11},{10,... | collective-permute-start | bytes 776 | tf_op jit(solution)/shard_map/ppermute | solution.py:33
  156.5 29.6 %collective-permute-start.20 = (f16[64,3584]{1,0:T(8,128)(2,1)S(1)}, f16[64,3584]{1,0:T(8,128)(2,1)S(1)}, u32[]{:S(2)}, u32[]{:S(2)}) collective-permute-start(f16[64,3584]{1,0:T(8,128)(2,1)S(1)} %multiply_convert_fusion.14), channel_id=1, source_target_pairs={{0,2},{1,3},{2,0},{3,1},{4,6},{5,7},{6,4},{7,5},{8,10},{9,11},{10,... | collective-permute-start | bytes 1376264 | tf_op jit(solution)/shard_map/ppermute | solution.py:33
  176.3 24.1 %collective-permute-start.51 = (bf16[64,3584]{1,0:T(8,128)(2,1)S(1)}, bf16[64,3584]{1,0:T(8,128)(2,1)S(1)}, u32[]{:S(2)}, u32[]{:S(2)}) collective-permute-start(bf16[64,3584]{1,0:T(8,128)(2,1)S(1)} %fusion.41), channel_id=1, source_target_pairs={{0,2},{1,3},{2,0},{3,1},{4,6},{5,7},{6,4},{7,5},{8,10},{9,11},{10,... | collective-permute-start | bytes 1376264 | tf_op jit(solution)/shard_map/ppermute | solution.py:33
  186.8 18.9 %collective-permute-start.28 = (bf16[64,3584]{1,0:T(8,128)(2,1)S(1)}, bf16[64,3584]{1,0:T(8,128)(2,1)S(1)}, u32[]{:S(2)}, u32[]{:S(2)}) collective-permute-start(bf16[64,3584]{1,0:T(8,128)(2,1)S(1)} %get-tuple-element.5), channel_id=1, source_target_pairs={{0,2},{1,3},{2,0},{3,1},{4,6},{5,7},{6,4},{7,5},{8,10},{9,11},{10,... | collective-permute-start | bytes 1376264 | tf_op jit(solution)/shard_map/ppermute | solution.py:33
  188.4 24.9 %collective-permute-start.55 = (f32[64,3584]{1,0:T(8,128)S(1)}, f32[64,3584]{1,0:T(8,128)S(1)}, u32[]{:S(2)}, u32[]{:S(2)}) collective-permute-start(f32[64,3584]{1,0:T(8,128)S(1)} %get-tuple-element.6), channel_id=1, source_target_pairs={{0,16},{16,0},{1,17},{17,1},{2,18},{18,2},{3,19},{19,3},{4,20},{20... | collective-permute-start | bytes 2752520 | tf_op jit(solution)/shard_map/ppermute | solution.py:33
  191.9 21.3 %collective-permute-start.57 = (f16[64,3584]{1,0:T(8,128)(2,1)S(1)}, f16[64,3584]{1,0:T(8,128)(2,1)S(1)}, u32[]{:S(2)}, u32[]{:S(2)}) collective-permute-start(f16[64,3584]{1,0:T(8,128)(2,1)S(1)} %multiply_convert_fusion.8), channel_id=1, source_target_pairs={{0,2},{1,3},{2,0},{3,1},{4,6},{5,7},{6,4},{7,5},{8,10},{9,11},{10,... | collective-permute-start | bytes 1376264 | tf_op jit(solution)/shard_map/ppermute | solution.py:33
  200.4 29.4 %collective-permute-start.18 = (f32[4,32]{1,0:T(4,128)S(1)}, f32[4,32]{1,0:T(4,128)S(1)}, u32[]{:S(2)}, u32[]{:S(2)}) collective-permute-start(f32[4,32]{1,0:T(4,128)S(1)} %get-tuple-element.35), channel_id=1, source_target_pairs={{0,4},{4,8},{8,12},{12,0},{1,5},{5,9},{9,13},{13,1},{2,6},{6,10},{... | collective-permute-start | bytes 1544 | tf_op jit(solution)/shard_map/ppermute | solution.py:38
  205.7 24.1 %collective-permute-start.17 = (f16[4,32,2048]{2,1,0:T(8,128)(2,1)S(1)}, f16[4,32,2048]{2,1,0:T(8,128)(2,1)S(1)}, u32[]{:S(2)}, u32[]{:S(2)}) collective-permute-start(f16[4,32,2048]{2,1,0:T(8,128)(2,1)S(1)} %multiply_convert_fusion.5), channel_id=1, source_target_pairs={{0,4},{4,8},{8,12},{12,0},{1,5},{5,9},{9,13},{13,1},{2,6},{6,10},{... | collective-permute-start | bytes 1572872 | tf_op jit(solution)/shard_map/ppermute | solution.py:38
  221.8 30.4 %collective-permute-start.54 = (f32[4,32]{1,0:T(4,128)S(1)}, f32[4,32]{1,0:T(4,128)S(1)}, u32[]{:S(2)}, u32[]{:S(2)}) collective-permute-start(f32[4,32]{1,0:T(4,128)S(1)} %get-tuple-element.29), channel_id=1, source_target_pairs={{0,4},{4,8},{8,12},{12,0},{1,5},{5,9},{9,13},{13,1},{2,6},{6,10},{... | collective-permute-start | bytes 1544 | tf_op jit(solution)/shard_map/ppermute | solution.py:38
  230.6 17.3 %collective-permute-start.60 = (bf16[128,3584]{1,0:T(8,128)(2,1)S(1)}, bf16[128,3584]{1,0:T(8,128)(2,1)S(1)}, u32[]{:S(2)}, u32[]{:S(2)}) collective-permute-start(bf16[128,3584]{1,0:T(8,128)(2,1)S(1)} %pad_maximum_fusion.17), channel_id=1, source_target_pairs={{0,1},{1,0},{2,3},{3,2},{4,5},{5,4},{6,7},{7,6},{8,9},{9,8},{10,11... | collective-permute-start | bytes 2752520 | tf_op jit(solution)/shard_map/ppermute | solution.py:33
  231.5 26.8 %collective-permute-start.53 = (f16[4,32,2048]{2,1,0:T(8,128)(2,1)S(1)}, f16[4,32,2048]{2,1,0:T(8,128)(2,1)S(1)}, u32[]{:S(2)}, u32[]{:S(2)}) collective-permute-start(f16[4,32,2048]{2,1,0:T(8,128)(2,1)S(1)} %multiply_convert_fusion.2), channel_id=1, source_target_pairs={{0,4},{4,8},{8,12},{12,0},{1,5},{5,9},{9,13},{13,1},{2,6},{6,10},{... | collective-permute-start | bytes 1572872 | tf_op jit(solution)/shard_map/ppermute | solution.py:38
  247.8 21.8 %collective-permute-start.32 = (f16[4,32,2048]{2,1,0:T(8,128)(2,1)S(1)}, f16[4,32,2048]{2,1,0:T(8,128)(2,1)S(1)}, u32[]{:S(2)}, u32[]{:S(2)}) collective-permute-start(f16[4,32,2048]{2,1,0:T(8,128)(2,1)S(1)} %multiply_convert_fusion.3), channel_id=1, source_target_pairs={{0,4},{4,8},{8,12},{12,0},{1,5},{5,9},{9,13},{13,1},{2,6},{6,10},{... | collective-permute-start | bytes 1572872 | tf_op jit(solution)/shard_map/ppermute | solution.py:38
  259.0 21.9 %collective-permute-start.61 = (f16[4,32,2048]{2,1,0:T(8,128)(2,1)S(1)}, f16[4,32,2048]{2,1,0:T(8,128)(2,1)S(1)}, u32[]{:S(2)}, u32[]{:S(2)}) collective-permute-start(f16[4,32,2048]{2,1,0:T(8,128)(2,1)S(1)} %multiply_convert_fusion.1), channel_id=1, source_target_pairs={{0,4},{4,8},{8,12},{12,0},{1,5},{5,9},{9,13},{13,1},{2,6},{6,10},{... | collective-permute-start | bytes 1572872 | tf_op jit(solution)/shard_map/ppermute | solution.py:38
  261.5 19.3 %collective-permute-start.62 = (f32[4,32]{1,0:T(4,128)S(1)}, f32[4,32]{1,0:T(4,128)S(1)}, u32[]{:S(2)}, u32[]{:S(2)}) collective-permute-start(f32[4,32]{1,0:T(4,128)S(1)} %get-tuple-element.27), channel_id=1, source_target_pairs={{0,4},{4,8},{8,12},{12,0},{1,5},{5,9},{9,13},{13,1},{2,6},{6,10},{... | collective-permute-start | bytes 1544 | tf_op jit(solution)/shard_map/ppermute | solution.py:38
  270.6 21.6 %collective-permute-start.34 = (bf16[4,32,2048]{2,1,0:T(8,128)(2,1)}, bf16[4,32,2048]{2,1,0:T(8,128)(2,1)}, u32[]{:S(2)}, u32[]{:S(2)}) collective-permute-start(bf16[4,32,2048]{2,1,0:T(8,128)(2,1)} %fusion.31), channel_id=1, source_target_pairs={{0,4},{4,8},{8,12},{12,0},{1,5},{5,9},{9,13},{13,1},{2,6},{6,10},{... | collective-permute-start | bytes 1572872 | tf_op jit(solution)/shard_map/ppermute | solution.py:38
  282.3 21.1 %collective-permute-start.63 = (f16[4,32,2048]{2,1,0:T(8,128)(2,1)}, f16[4,32,2048]{2,1,0:T(8,128)(2,1)}, u32[]{:S(2)}, u32[]{:S(2)}) collective-permute-start(f16[4,32,2048]{2,1,0:T(8,128)(2,1)} %multiply_convert_fusion), channel_id=1, source_target_pairs={{0,4},{4,8},{8,12},{12,0},{1,5},{5,9},{9,13},{13,1},{2,6},{6,10},{... | collective-permute-start | bytes 1572872 | tf_op jit(solution)/shard_map/ppermute | solution.py:38
  294.5 20.1 %collective-permute-start.40 = (bf16[4,32,2048]{2,1,0:T(8,128)(2,1)}, bf16[4,32,2048]{2,1,0:T(8,128)(2,1)S(1)}, u32[]{:S(2)}, u32[]{:S(2)}) collective-permute-start(bf16[4,32,2048]{2,1,0:T(8,128)(2,1)} %collective-permute-done.34), channel_id=1, source_target_pairs={{0,4},{4,8},{8,12},{12,0},{1,5},{5,9},{9,13},{13,1},{2,6},{6,10},{... | collective-permute-start | bytes 1572872 | tf_op jit(solution)/shard_map/ppermute | solution.py:38
  305.0 21.0 %collective-permute-start.65 = (bf16[4,32,2048]{2,1,0:T(8,128)(2,1)S(1)}, bf16[4,32,2048]{2,1,0:T(8,128)(2,1)}, u32[]{:S(2)}, u32[]{:S(2)}) collective-permute-start(bf16[4,32,2048]{2,1,0:T(8,128)(2,1)S(1)} %fusion.26), channel_id=1, source_target_pairs={{0,4},{4,8},{8,12},{12,0},{1,5},{5,9},{9,13},{13,1},{2,6},{6,10},{... | collective-permute-start | bytes 1572872 | tf_op jit(solution)/shard_map/ppermute | solution.py:38
  314.1 39.8 %collective-permute-start.35 = (f32[128,3584]{1,0:T(8,128)}, f32[128,3584]{1,0:T(8,128)}, u32[]{:S(2)}, u32[]{:S(2)}) collective-permute-start(f32[128,3584]{1,0:T(8,128)} %slice.253), channel_id=1, source_target_pairs={{0,1},{1,0},{2,3},{3,2},{4,5},{5,4},{6,7},{7,6},{8,9},{9,8},{10,11... | collective-permute-start | bytes 5505032 | tf_op jit(solution)/shard_map/ppermute | solution.py:33
  314.6 22.8 %collective-permute-start.41 = (bf16[4,32,2048]{2,1,0:T(8,128)(2,1)S(1)}, bf16[4,32,2048]{2,1,0:T(8,128)(2,1)}, u32[]{:S(2)}, u32[]{:S(2)}) collective-permute-start(bf16[4,32,2048]{2,1,0:T(8,128)(2,1)S(1)} %collective-permute-done.40), channel_id=1, source_target_pairs={{0,4},{4,8},{8,12},{12,0},{1,5},{5,9},{9,13},{13,1},{2,6},{6,10},{... | collective-permute-start | bytes 1572872 | tf_op jit(solution)/shard_map/ppermute | solution.py:38
  337.2 47.3 %collective-permute-start.66 = (f32[128,3584]{1,0:T(8,128)}, f32[128,3584]{1,0:T(8,128)}, u32[]{:S(2)}, u32[]{:S(2)}) collective-permute-start(f32[128,3584]{1,0:T(8,128)} %slice.273), channel_id=1, source_target_pairs={{0,1},{1,0},{2,3},{3,2},{4,5},{5,4},{6,7},{7,6},{8,9},{9,8},{10,11... | collective-permute-start | bytes 5505032 | tf_op jit(solution)/shard_map/ppermute | solution.py:33
  347.6 48.9 %collective-permute-start.42 = (f32[128,3584]{1,0:T(8,128)}, f32[128,3584]{1,0:T(8,128)}, u32[]{:S(2)}, u32[]{:S(2)}) collective-permute-start(f32[128,3584]{1,0:T(8,128)} %slice.257), channel_id=1, source_target_pairs={{0,1},{1,0},{2,3},{3,2},{4,5},{5,4},{6,7},{7,6},{8,9},{9,8},{10,11... | collective-permute-start | bytes 5505032 | tf_op jit(solution)/shard_map/ppermute | solution.py:33
  355.8 25.8 %collective-permute-start.37 = (f32[64]{0:T(128)S(1)}, f32[64]{0:T(128)S(1)}, u32[]{:S(2)}, u32[]{:S(2)}) collective-permute-start(f32[64]{0:T(128)S(1)} %get-tuple-element.47), channel_id=1, source_target_pairs={{0,2},{1,3},{2,0},{3,1},{4,6},{5,7},{6,4},{7,5},{8,10},{9,11},{10,... | collective-permute-start | bytes 776 | tf_op jit(solution)/shard_map/ppermute | solution.py:33
  358.3 23.3 %collective-permute-start.36 = (f16[64,3584]{1,0:T(8,128)(2,1)}, f16[64,3584]{1,0:T(8,128)(2,1)}, u32[]{:S(2)}, u32[]{:S(2)}) collective-permute-start(f16[64,3584]{1,0:T(8,128)(2,1)} %multiply_convert_fusion.11), channel_id=1, source_target_pairs={{0,2},{1,3},{2,0},{3,1},{4,6},{5,7},{6,4},{7,5},{8,10},{9,11},{10,... | collective-permute-start | bytes 1376264 | tf_op jit(solution)/shard_map/ppermute | solution.py:33
  381.5 36.4 %collective-permute-start.73 = (f32[128,3584]{1,0:T(8,128)S(1)}, f32[128,3584]{1,0:T(8,128)S(1)}, u32[]{:S(2)}, u32[]{:S(2)}) collective-permute-start(f32[128,3584]{1,0:T(8,128)S(1)} %slice.277), channel_id=1, source_target_pairs={{0,1},{1,0},{2,3},{3,2},{4,5},{5,4},{6,7},{7,6},{8,9},{9,8},{10,11... | collective-permute-start | bytes 5505032 | tf_op jit(solution)/shard_map/ppermute | solution.py:33
  387.2 19.0 %collective-permute-start.67 = (f16[64,3584]{1,0:T(8,128)(2,1)S(1)}, f16[64,3584]{1,0:T(8,128)(2,1)S(1)}, u32[]{:S(2)}, u32[]{:S(2)}) collective-permute-start(f16[64,3584]{1,0:T(8,128)(2,1)S(1)} %multiply_convert_fusion.7), channel_id=1, source_target_pairs={{0,2},{1,3},{2,0},{3,1},{4,6},{5,7},{6,4},{7,5},{8,10},{9,11},{10,... | collective-permute-start | bytes 1376264 | tf_op jit(solution)/shard_map/ppermute | solution.py:33
  396.4 21.4 %collective-permute-start.39 = (bf16[128,3584]{1,0:T(8,128)(2,1)S(1)}, bf16[128,3584]{1,0:T(8,128)(2,1)S(1)}, u32[]{:S(2)}, u32[]{:S(2)}) collective-permute-start(bf16[128,3584]{1,0:T(8,128)(2,1)S(1)} %pad_maximum_fusion.14), channel_id=1, source_target_pairs={{0,1},{1,0},{2,3},{3,2},{4,5},{5,4},{6,7},{7,6},{8,9},{9,8},{10,11... | collective-permute-start | bytes 2752520 | tf_op jit(solution)/shard_map/ppermute | solution.py:33
  406.4 19.4 %collective-permute-start.69 = (bf16[64,3584]{1,0:T(8,128)(2,1)S(1)}, bf16[64,3584]{1,0:T(8,128)(2,1)S(1)}, u32[]{:S(2)}, u32[]{:S(2)}) collective-permute-start(bf16[64,3584]{1,0:T(8,128)(2,1)S(1)} %fusion.37), channel_id=1, source_target_pairs={{0,2},{1,3},{2,0},{3,1},{4,6},{5,7},{6,4},{7,5},{8,10},{9,11},{10,... | collective-permute-start | bytes 1376264 | tf_op jit(solution)/shard_map/ppermute | solution.py:33
  416.3 30.6 %collective-permute-start.45 = (bf16[64,3584]{1,0:T(8,128)(2,1)S(1)}, bf16[64,3584]{1,0:T(8,128)(2,1)S(1)}, u32[]{:S(2)}, u32[]{:S(2)}) collective-permute-start(bf16[64,3584]{1,0:T(8,128)(2,1)S(1)} %fusion.43), channel_id=1, source_target_pairs={{0,2},{1,3},{2,0},{3,1},{4,6},{5,7},{6,4},{7,5},{8,10},{9,11},{10,... | collective-permute-start | bytes 1376264 | tf_op jit(solution)/shard_map/ppermute | solution.py:33
  418.7 17.0 %collective-permute-start.75 = (f32[64]{0:T(128)S(1)}, f32[64]{0:T(128)S(1)}, u32[]{:S(2)}, u32[]{:S(2)}) collective-permute-start(f32[64]{0:T(128)S(1)} %get-tuple-element.37), channel_id=1, source_target_pairs={{0,2},{1,3},{2,0},{3,1},{4,6},{5,7},{6,4},{7,5},{8,10},{9,11},{10,... | collective-permute-start | bytes 776 | tf_op jit(solution)/shard_map/ppermute | solution.py:33
  420.4 24.7 %collective-permute-start.74 = (f16[64,3584]{1,0:T(8,128)(2,1)S(1)}, f16[64,3584]{1,0:T(8,128)(2,1)S(1)}, u32[]{:S(2)}, u32[]{:S(2)}) collective-permute-start(f16[64,3584]{1,0:T(8,128)(2,1)S(1)} %multiply_convert_fusion.6), channel_id=1, source_target_pairs={{0,2},{1,3},{2,0},{3,1},{4,6},{5,7},{6,4},{7,5},{8,10},{9,11},{10,... | collective-permute-start | bytes 1376264 | tf_op jit(solution)/shard_map/ppermute | solution.py:33
  425.9 31.7 %collective-permute-start.70 = (bf16[128,3584]{1,0:T(8,128)(2,1)S(1)}, bf16[128,3584]{1,0:T(8,128)(2,1)S(1)}, u32[]{:S(2)}, u32[]{:S(2)}) collective-permute-start(bf16[128,3584]{1,0:T(8,128)(2,1)S(1)} %pad_maximum_fusion.18), channel_id=1, source_target_pairs={{0,1},{1,0},{2,3},{3,2},{4,5},{5,4},{6,7},{7,6},{8,9},{9,8},{10,11... | collective-permute-start | bytes 2752520 | tf_op jit(solution)/shard_map/ppermute | solution.py:33
  (64 other events, 788.1 us)

commit v2 on v1

v2 whole, which is shorter than its diff:
```python
import functools

import jax
import jax.numpy as jnp
from jax import lax
from jax.experimental import pallas as pl
from jax.experimental.pallas import tpu as pltpu
from jax.sharding import PartitionSpec as P

TOP_BITS = 14
LEAST_TOP = 1e-30
LANES = 128
MIB = 1024 * 1024


def slot_masks(count):
    bits = count.bit_length() - 1
    assert 1 << bits == count
    return [sum(((s >> b) & 1) << (bits - 1 - b) for b in range(bits)) for s in range(count)]


def swap(values, axis, mask):
    count = lax.axis_size(axis)
    return lax.ppermute(values, axis, [(i, i ^ mask) for i in range(count)])


def shift(values, axis):
    count = lax.axis_size(axis)
    return lax.ppermute(values, axis, [(i, (i + 1) % count) for i in range(count)])


def scaled_rows(values):
    top = jnp.max(jnp.abs(values), axis=-1, keepdims=True)
    power = jnp.ceil(jnp.log2(jnp.maximum(top, LEAST_TOP)))
    return values * jnp.exp2(TOP_BITS - power), power


def coded(values):
    body, power = scaled_rows(values)
    marks = jnp.broadcast_to(power, (*values.shape[:-1], LANES))
    return jnp.concatenate([body, marks], axis=-1)


def decoded(code):
    width = code.shape[-1] - LANES
    unit = jnp.exp2(code[..., width : width + 1].astype(jnp.float32) - TOP_BITS)
    return code[..., :width].astype(jnp.float32) * unit


def tile_of(size, tile):
    return tile if size % tile == 0 else size


def params(mib):
    return pltpu.CompilerParams(vmem_limit_bytes=mib * MIB)


def cost(rows, depth, width, moved):
    return pl.CostEstimate(
        flops=2 * rows * depth * width, bytes_accessed=moved, transcendentals=0
    )


ANYWHERE = pl.BlockSpec(memory_space=pl.ANY)


def split_kernel(count, turned, x_ref, *refs):
    keep_ref, give_ref = refs[-2:]
    half = keep_ref.shape[1]
    contract = (((1,), (1,)), ((), ())) if turned else (((1,), (0,)), ((), ()))
    for at in range(count):
        part = lax.dot_general(
            x_ref[...], refs[at][...], contract, preferred_element_type=jnp.float32
        )
        keep_ref[at] = part[:half]
        give_ref[at] = part[half:]


def split_products(x, weights, after=(), turned=False):
    rows, depth = x.shape
    width = weights[0].shape[0 if turned else 1]
    count = len(weights)
    tile = tile_of(width, 512 if count == 1 else 256)
    spec = (
        pl.BlockSpec((tile, depth), lambda j: (j, 0))
        if turned
        else pl.BlockSpec((depth, tile), lambda j: (0, j))
    )
    out = pl.BlockSpec((count, rows // 2, tile), lambda j: (0, 0, j))
    extra = list(after)
    return pl.pallas_call(
        functools.partial(split_kernel, count, turned),
        grid=(width // tile,),
        out_shape=[jax.ShapeDtypeStruct((count, rows // 2, width), jnp.float32)] * 2,
        in_specs=[pl.BlockSpec(x.shape, lambda j: (0, 0))]
        + [spec] * count
        + [ANYWHERE] * len(extra),
        out_specs=[out, out],
        compiler_params=params(32),
        cost_estimate=cost(
            rows, depth, width * count, count * width * (depth * 2 + rows * 4) + rows * depth * 2
        ),
    )(x, *weights, *extra)


def fold_kernel(keep_ref, got_ref, own_ref, code_ref):
    rows, width = own_ref.shape[1:]
    own_ref[0] = keep_ref[0, :rows] + got_ref[0, :rows]
    body, power = scaled_rows(keep_ref[0, rows:] + got_ref[0, rows:])
    code_ref[0, :, :width] = body
    code_ref[0, :, width:] = jnp.broadcast_to(power, (rows, LANES))


def fold(keep, got):
    count, both, width = keep.shape
    rows = both // 2
    if width % LANES or rows % 8:
        total = keep + got
        return total[:, :rows], coded(total[:, rows:])
    taken = pl.BlockSpec((1, both, width), lambda i: (i, 0, 0))
    return pl.pallas_call(
        fold_kernel,
        grid=(count,),
        out_shape=[
            jax.ShapeDtypeStruct((count, rows, width), jnp.float32),
            jax.ShapeDtypeStruct((count, rows, width + LANES), jnp.float32),
        ],
        in_specs=[taken, taken],
        out_specs=[
            pl.BlockSpec((1, rows, width), lambda i: (i, 0, 0)),
            pl.BlockSpec((1, rows, width + LANES), lambda i: (i, 0, 0)),
        ],
        compiler_params=params(20),
        cost_estimate=cost(1, count * both, width, count * both * width * 12),
    )(keep, got)


def whole_kernel(parts, *refs):
    weight_ref, out_ref, held = refs[parts], refs[-2], refs[-1]

    @pl.when(pl.program_id(0) == 0)
    def _():
        at = 0
        for part in refs[:parts]:
            held[at : at + part.shape[0]] = part[...]
            at += part.shape[0]

    out_ref[...] = jnp.dot(held[...], weight_ref[...], preferred_element_type=jnp.float32)


def whole_product(parts, weight):
    rows = sum(part.shape[0] for part in parts)
    depth, width = weight.shape
    tile = tile_of(width, 256)
    return pl.pallas_call(
        functools.partial(whole_kernel, len(parts)),
        grid=(width // tile,),
        out_shape=jax.ShapeDtypeStruct((rows, width), jnp.float32),
        in_specs=[pl.BlockSpec(part.shape, lambda j: (0, 0)) for part in parts]
        + [pl.BlockSpec((depth, tile), lambda j: (0, j))],
        out_specs=pl.BlockSpec((rows, tile), lambda j: (0, j)),
        scratch_shapes=[pltpu.VMEM((rows, depth), jnp.bfloat16)],
        compiler_params=params(24),
        cost_estimate=cost(rows, depth, width, (depth * width + rows * depth) * 2 + rows * width * 4),
    )(*parts, weight)


def last_kernel(scale, parts, *refs):
    turned, bars = refs[:parts], refs[parts:-3]
    out_ref, left, right = refs[-3:]
    height = out_ref.shape[0]
    step = tile_of(height, 512)

    @pl.when(pl.program_id(0) == 0)
    def _():
        at = 0
        for part in turned:
            left[:, at : at + part.shape[1]] = part[...]
            at += part.shape[1]

    at = 0
    for part in bars:
        right[at : at + part.shape[0]] = part[...]
        at += part.shape[0]

    @pl.loop(0, height // step)
    def _(at):
        rows = pl.ds(pl.multiple_of(at * step, step), step)
        total = jnp.dot(left[rows, :], right[...], preferred_element_type=jnp.float32)
        out_ref[rows, :] = total * scale


def last_product(turned, bars, tokens):
    features, hidden = turned[0].shape[0], bars[0].shape[1]
    tile = tile_of(hidden, 512)
    return pl.pallas_call(
        functools.partial(last_kernel, 1.0 / tokens, len(turned)),
        grid=(hidden // tile,),
        out_shape=jax.ShapeDtypeStruct((features, hidden), jnp.float32),
        in_specs=[pl.BlockSpec(t.shape, lambda j: (0, 0)) for t in turned]
        + [pl.BlockSpec((b.shape[0], tile), lambda j: (0, j)) for b in bars],
        out_specs=pl.BlockSpec((features, tile), lambda j: (0, j)),
        scratch_shapes=[
            pltpu.VMEM((features, tokens), jnp.bfloat16),
            pltpu.VMEM((tokens, tile), jnp.bfloat16),
        ],
        compiler_params=params(36),
        cost_estimate=cost(
            features, tokens, hidden, features * hidden * 4 + tokens * (features + hidden) * 2
        ),
    )(*turned, *bars)


def per_device(inputs, w_gate, w_up, w_down, query, curvature):
    ring, count = lax.axis_size("row"), lax.axis_size("col")
    assert lax.axis_size("grp") == 2 and ring % 4 == 0
    shard, width = inputs.shape
    tokens = shard * ring
    rows = shard // 2 // count
    masks = slot_masks(count)
    place, grp, me = lax.axis_index("col"), lax.axis_index("grp"), lax.axis_index("row")

    def own_rows(array, start, half):
        begin = start + half * (shard // 2)
        return jnp.stack(
            [
                lax.dynamic_slice_in_dim(array, begin + (place ^ mask) * rows, rows, 0)
                for mask in masks
            ]
        )

    def joined(pieces):
        return jnp.concatenate(pieces, axis=1).reshape(-1, pieces[0].shape[-1])

    def spans(*cuts):
        ends = [cut * ring // 4 for cut in cuts]
        return [list(range(a, b)) for a, b in zip(ends, ends[1:])]

    steps = [spans(0, 1, 2, 4), spans(0, 2, 4)]
    halves = (grp, 1 - grp)

    acts = [[own_rows(inputs, 0, half)] for half in halves]
    for k in range(1, ring):
        acts[0].append(shift(acts[0][-1], "row"))
        acts[1].append(swap(acts[0][-1], "grp", 1))

    def sum_over_col(x, weights, after, turned=False):
        keep, give = split_products(x, weights, after, turned)
        own, code = fold(keep, swap(give, "col", 1))
        mark, mask = code, 2
        while True:
            own = own + decoded(swap(code.astype(jnp.float16), "col", mask))
            mask *= 2
            if mask >= count:
                return own, mark
            upper = own.shape[1] // 2
            own, code = own[:, :upper], coded(own[:, upper:])

    def gather_over_col(values):
        parts, mask = [values], count // 2
        while mask >= 1:
            block = parts[0] if len(parts) == 1 else jnp.concatenate(parts, axis=0)
            parts.append(swap(block, "col", mask))
            mask //= 2
        return parts

    gains = [[None] * ring, [None] * ring]
    sums = [None, None]
    scaled = [None, None]

    def hidden(half, step, own):
        if half == 0:
            gate_out, up_out = own[0], own[1]
            sigmas = jax.nn.sigmoid(gate_out)
            gain = sigmas * (1.0 + gate_out * (1.0 - sigmas)) * up_out
            other = swap(gain, "grp", 1)
            for i, k in enumerate(step):
                gains[0][k] = gain[i * rows : (i + 1) * rows]
                gains[1][k] = other[i * rows : (i + 1) * rows]
        else:
            gain = jnp.concatenate([gains[1][k] for k in step], axis=0)
        return (gain * own[-1]).astype(jnp.bfloat16)

    def add_to_ring(half, step, out):
        out = out.reshape(count, len(step), rows, width)
        for i, k in enumerate(step):
            if k == 0:
                sums[half] = out[:, i]
            else:
                moved = shift(coded(sums[half]).astype(jnp.float16), "row")
                sums[half] = decoded(moved) + out[:, i]
        if step[-1] == ring - 1:
            owner = (me + 1) % ring
            curv = own_rows(curvature, owner * shard, halves[half])
            scaled[half] = (curv * sums[half]).astype(jnp.bfloat16)

    order = [(0, 0), (0, 1), (1, 0), (0, 2), (1, 1)]
    after = []
    for half, at in order:
        step = steps[half][at]
        x = joined([acts[half][k] for k in step])
        weights = [w_gate, w_up, query] if half == 0 else [query]
        own, mark = sum_over_col(x, weights, after)
        after = [mark]
        out = whole_product(gather_over_col(hidden(half, step, own)), w_down)
        add_to_ring(half, step, out)

    turned, bars = [], []
    for half in range(2):
        arrivals = [(ring - 1 + k) % ring for k in range(ring)]
        pieces = [scaled[half]]
        for _ in range(ring - 1):
            pieces.append(shift(pieces[-1], "row"))
        for span in spans(0, 2, 4):
            step = [arrivals[i] for i in span]
            turned.append(joined([acts[half][k] for k in step]).T)
            x = joined([pieces[i] for i in span])
            own, mark = sum_over_col(x, [w_down], after, True)
            after = [mark, turned[-1]]
            gain = jnp.concatenate([gains[half][k] for k in step], axis=0)
            bars += gather_over_col((own[0] * gain).astype(jnp.bfloat16))
    return last_product(turned, bars, tokens)


def solution(mesh):
    in_specs = (
        P("row", "col"),
        P("col", "row"),
        P("col", "row"),
        P("row", "col"),
        P(("grp", "col"), "row"),
        P("grp", "col"),
    )
    out_specs = P(("grp", "col"), "row")
    return jax.shard_map(
        per_device, mesh=mesh, in_specs=in_specs, out_specs=out_specs, check_vma=False
    )
```

time: 489 us -> 575 us (1.18)
  Pallas kernels: 22.5 us -> 167 us
  matrix products: 114 us -> 0 us
  local copies, waits for them, and re-layouts: 25.5 us -> 90.4 us
  starting transfers between devices: 52.4 us -> 35.1 us
  other arithmetic: 40 us -> 48.5 us
    pallas_call x0 -> x23, Pallas kernels: none -> 143 us  [the longest x9 95.9 us: split_products(): pl.pallas_call(functools.partial(split_kernel, count, turned), grid=(widt...]
    dot_general x16 -> x0, matrix products: 114 us -> none  [the longest x12 82.5 us: matmul(): return jnp.dot(left, right, preferred_element_type=jnp.float32)]
    unnamed x68 -> x174, local copies, waits for them, and re-layouts: 2.27 us -> 76.8 us
    ppermute x57 -> x42, starting transfers between devices: 44.1 us -> 26.9 us  [swap(): return lax.ppermute(values, axis, [(i, i ^ mask) for i in range(count)])]
    slice x12 -> x2, local copies, waits for them, and re-layouts: 14.6 us -> 1.28 us  [the longest x1 1.22 us: hidden(): gains[0][k] = gain[i * rows:(i + 1) * rows]]
    add x12 -> x3, other arithmetic: 16.6 us -> 4.86 us  [sum_over_col(): own = own + decoded(swap(code.astype(jnp.float16), 'col', mask))]
    concatenate x20 -> x21, other arithmetic: 8.26 us -> 18.5 us  [the longest x6 8.09 us: joined(): return jnp.concatenate(pieces, axis=1).reshape(-1, pieces[0].shape[-1])]
    exp2 x0 -> x21, other arithmetic: none -> 7 us  [the longest x15 6.91 us: decoded(): unit = jnp.exp2(code[..., width:width + 1].astype(jnp.float32) - TOP_BITS)]
  transfers between devices with their start and end apart: 78 -> 57, of which waited for: 31 -> 30; matrix products, arithmetic and copies ran while one was open for 35% -> 11% of each run, Pallas kernels for 0% -> 19%
where the time goes in v2:
time: 575 us; the launch traced here: 573 us
  waiting for transfers between devices  230 us (40%)
  Pallas kernels  167 us (29%)
  local copies, waits for them, and re-layouts  90.4 us (16%)
  other arithmetic  48.5 us (8%)
  starting transfers between devices  35.1 us (6%)
    ppermute x42, waiting for transfers between devices, swap(): return lax.ppermute(values, axis, [(i, i ^ mask) for i in range(count)])  126 us
    ppermute x15, waiting for transfers between devices, shift(): lax.ppermute(values, axis, [(i, (i + 1) % count) for i in range(count)])  104 us
    pallas_call x9, Pallas kernels, split_products(): pl.pallas_call(functools.partial(split_kernel, count, turned), grid=(widt...  95.9 us
    unnamed x174, local copies, waits for them, and re-layouts  76.8 us
    pallas_call x5, Pallas kernels, whole_product(): pl.pallas_call(functools.partial(whole_kernel, len(parts)), grid=(width /...  34.7 us
    ppermute x42, starting transfers between devices, swap(): return lax.ppermute(values, axis, [(i, i ^ mask) for i in range(count)])  26.9 us
    pallas_call x1, Pallas kernels, last_product(): pl.pallas_call(functools.partial(last_kernel, 1.0 / tokens, len(turned)),...  24.6 us
    pallas_call x9, Pallas kernels, fold(): pl.pallas_call(fold_kernel, grid=(count,), out_shape=[jax.ShapeDtypeStruc...  11.9 us
  transfers between devices with their start and end apart: 57, of which 30 were waited for; matrix products, arithmetic and copies ran while one was open for 11% of the time, Pallas kernels for 19%

profile of v2, /device:TPU:0, one launch (start us, length us, event | category | flops | bytes accessed | tf_op | source)
XLA Modules:
  0.0 572.7 jit_solution(3110750422303948605)
XLA Ops:
  2.8 5.2 copy-done.7
  8.0 17.2 %shard_map.64 = (f32[3,64,3584]{2,1,0:T(8,128)S(1)}, f32[3,64,3584]{2,1,0:T(8,128)S(1)}) custom-call(bf16[128,2048]{1,0:T(8,128)(2,1)S(1)} %bitcast.211, bf16[2048,3584]{1,0:T(8,128)(2,1)S(1)} %copy-done.7, bf16[2048,3584]{1,0:T(8,128)(2,1)} %refs_1_.5, bf16[2048,3584]{1,0:T(8,128)(2,1)} %refs_0_.13), custom_call_target="tpu_custom_call" | custom-call | flops 5637144576 | bytes 50069504 | tf_op jit(solution)/shard_map/pallas_call | solution.py:91
  28.4 14.5 %collective-permute-done = bf16[4,32,2048]{2,1,0:T(8,128)(2,1)S(1)} collective-permute-done((bf16[4,32,2048]{2,1,0:T(8,128)(2,1)S(1)}, bf16[4,32,2048]{2,1,0:T(8,128)(2,1)S(1)}, u32[]{:S(2)}, u32[]{:S(2)}) %collective-permute-start) | collective-permute-done | bytes 524320 | tf_op jit(solution)/shard_map/ppermute | solution.py:29
  46.1 12.4 %collective-permute-done.1 = bf16[4,32,2048]{2,1,0:T(8,128)(2,1)} collective-permute-done((bf16[4,32,2048]{2,1,0:T(8,128)(2,1)S(1)}, bf16[4,32,2048]{2,1,0:T(8,128)(2,1)}, u32[]{:S(2)}, u32[]{:S(2)}) %collective-permute-start.1) | collective-permute-done | bytes 524320 | tf_op jit(solution)/shard_map/ppermute | solution.py:29
  58.5 5.2 copy-done.8
  65.1 19.0 %shard_map.67 = (f32[3,64,3584]{2,1,0:T(8,128)S(1)}, f32[3,64,3584]{2,1,0:T(8,128)}) custom-call(bf16[128,2048]{1,0:T(8,128)(2,1)S(1)} %bitcast.210, bf16[2048,3584]{1,0:T(8,128)(2,1)S(1)} %copy-done.8, bf16[2048,3584]{1,0:T(8,128)(2,1)} %refs_1_.5, bf16[2048,3584]{1,0:T(8,128)(2,1)} %refs_0_.13, f32[3,32,3712]{2,1,0:T(8,128)S(1)} %copy-done.14), custom_call_target="tpu_custom_call" | custom-call | flops 5637144576 | bytes 50069504 | tf_op jit(solution)/shard_map/pallas_call | solution.py:91
  100.6 4.9 collective-permute-done.4
  105.5 11.2 %collective-permute-done.5 = bf16[4,32,2048]{2,1,0:T(8,128)(2,1)S(1)} collective-permute-done((bf16[4,32,2048]{2,1,0:T(8,128)(2,1)}, bf16[4,32,2048]{2,1,0:T(8,128)(2,1)S(1)}, u32[]{:S(2)}, u32[]{:S(2)}) %collective-permute-start.5) | collective-permute-done | bytes 524320 | tf_op jit(solution)/shard_map/ppermute | solution.py:24
  116.7 10.5 %collective-permute-done.3 = bf16[4,32,2048]{2,1,0:T(8,128)(2,1)S(1)} collective-permute-done((bf16[4,32,2048]{2,1,0:T(8,128)(2,1)S(1)}, bf16[4,32,2048]{2,1,0:T(8,128)(2,1)S(1)}, u32[]{:S(2)}, u32[]{:S(2)}) %collective-permute-start.3) | collective-permute-done | bytes 524320 | tf_op jit(solution)/shard_map/ppermute | solution.py:24
  130.9 5.7 shard_map.66
  144.0 5.2 copy-done.5
  149.2 6.1 %shard_map.70 = (f32[1,128,3584]{2,1,0:T(8,128)S(1)}, f32[1,128,3584]{2,1,0:T(8,128)S(1)}) custom-call(bf16[256,2048]{1,0:T(8,128)(2,1)S(1)} %bitcast.209, bf16[2048,3584]{1,0:T(8,128)(2,1)S(1)} %copy-done.5, f32[3,32,3712]{2,1,0:T(8,128)S(1)} %get-tuple-element.48.refs_1_), custom_call_target="tpu_custom_call" | custom-call | flops 3758096384 | bytes 19398656 | tf_op jit(solution)/shard_map/pallas_call | solution.py:91
  155.4 4.2 collective-permute-done.12
  162.7 24.0 %shard_map.72 = (f32[3,128,3584]{2,1,0:T(8,128)S(1)}, f32[3,128,3584]{2,1,0:T(8,128)}) custom-call(bf16[256,2048]{1,0:T(8,128)(2,1)S(1)} %bitcast.197, bf16[2048,3584]{1,0:T(8,128)(2,1)} %refs_0_.12, bf16[2048,3584]{1,0:T(8,128)(2,1)} %refs_1_.5, bf16[2048,3584]{1,0:T(8,128)(2,1)} %refs_0_.13, f32[1,64,3712]{2,1,0:T(8,128)S(1)} %get-tuple-element.51.refs_3_), custom_call_target="tpu_custom_call" | custom-call | flops 11274289152 | bytes 56098816 | tf_op jit(solution)/shard_map/pallas_call | solution.py:91
  191.2 11.3 %collective-permute-done.35 = f32[32,3584]{1,0:T(8,128)S(1)} collective-permute-done((f32[32,3584]{1,0:T(8,128)S(1)}, f32[32,3584]{1,0:T(8,128)S(1)}, u32[]{:S(2)}, u32[]{:S(2)}) %collective-permute-start.35) | collective-permute-done | bytes 458784 | tf_op jit(solution)/shard_map/ppermute | solution.py:24
  206.7 5.2 copy-done
  211.8 5.6 shard_map.69
  220.4 7.5 %shard_map.81 = f32[256,2048]{1,0:T(8,128)S(1)} custom-call(bf16[64,3584]{1,0:T(8,128)(2,1)S(1)} %fusion.14.refs_0_, bf16[64,3584]{1,0:T(8,128)(2,1)S(1)} %collective-permute-done.37.refs_1_, bf16[128,3584]{1,0:T(8,128)(2,1)S(1)} %collective-permute-done.38.refs_2_, bf16[3584,2048]{1,0:T(8,128)(2,1)S(1)} %copy-done), custom_call_target="tpu_custom_call" | custom-call | flops 3758096384 | bytes 18612224 | tf_op jit(solution)/shard_map/pallas_call | solution.py:155
  232.3 3.7 shard_map.73
  243.0 5.4 collective-permute-done.39
  250.7 5.2 copy-done.6
  257.7 6.7 %shard_map.75 = (f32[1,128,3584]{2,1,0:T(8,128)S(1)}, f32[1,128,3584]{2,1,0:T(8,128)}) custom-call(bf16[256,2048]{1,0:T(8,128)(2,1)S(1)} %bitcast.208, bf16[2048,3584]{1,0:T(8,128)(2,1)S(1)} %copy-done.6, f32[3,64,3712]{2,1,0:T(8,128)S(1)} %copy-done.10), custom_call_target="tpu_custom_call" | custom-call | flops 3758096384 | bytes 19398656 | tf_op jit(solution)/shard_map/pallas_call | solution.py:91
  265.7 5.7 collective-permute-done.18
  281.5 7.5 %collective-permute-done.19.refs_1_ = bf16[64,3584]{1,0:T(8,128)(2,1)S(1)} collective-permute-done((bf16[64,3584]{1,0:T(8,128)(2,1)S(1)}, bf16[64,3584]{1,0:T(8,128)(2,1)S(1)}, u32[]{:S(2)}, u32[]{:S(2)}) %collective-permute-start.19) | collective-permute-done | bytes 458784 | tf_op jit(solution)/shard_map/ppermute | solution.py:24
  289.1 8.1 %collective-permute-done.42 = f16[1,64,3712]{2,1,0:T(8,128)(2,1)S(1)} collective-permute-done((f16[1,64,3712]{2,1,0:T(8,128)(2,1)S(1)}, f16[1,64,3712]{2,1,0:T(8,128)(2,1)S(1)}, u32[]{:S(2)}, u32[]{:S(2)}) %collective-permute-start.42) | collective-permute-done | bytes 475168 | tf_op jit(solution)/shard_map/ppermute | solution.py:24
  300.4 7.5 %shard_map.74 = f32[256,2048]{1,0:T(8,128)S(1)} custom-call(bf16[64,3584]{1,0:T(8,128)(2,1)S(1)} %get-tuple-element.81.refs_0_, bf16[64,3584]{1,0:T(8,128)(2,1)S(1)} %collective-permute-done.19.refs_1_, bf16[128,3584]{1,0:T(8,128)(2,1)S(1)} %collective-permute-done.20.refs_2_, bf16[3584,2048]{1,0:T(8,128)(2,1)S(1)} %bitcast.184), custom_call_target="tpu_custom_call" | custom-call | flops 3758096384 | bytes 18612224 | tf_op jit(solution)/shard_map/pallas_call | solution.py:155
  317.1 8.9 %collective-permute-done.21 = f16[4,32,2176]{2,1,0:T(8,128)(2,1)} collective-permute-done((f16[4,32,2176]{2,1,0:T(8,128)(2,1)}, f16[4,32,2176]{2,1,0:T(8,128)(2,1)}, u32[]{:S(2)}, u32[]{:S(2)}) %collective-permute-start.21) | collective-permute-done | bytes 557088 | tf_op jit(solution)/shard_map/ppermute | solution.py:29
  330.1 5.2 copy-done.1
  335.3 8.4 %shard_map.82 = f32[256,2048]{1,0:T(8,128)S(1)} custom-call(bf16[64,3584]{1,0:T(8,128)(2,1)S(1)} %fusion.17.refs_0_, bf16[64,3584]{1,0:T(8,128)(2,1)S(1)} %copy-done.38, bf16[128,3584]{1,0:T(8,128)(2,1)} %collective-permute-done.44.refs_2_, bf16[3584,2048]{1,0:T(8,128)(2,1)S(1)} %copy-done.1), custom_call_target="tpu_custom_call" | custom-call | flops 3758096384 | bytes 18612224 | tf_op jit(solution)/shard_map/pallas_call | solution.py:155
  344.2 5.2 copy-done.2
  349.3 6.0 %shard_map.77 = (f32[1,128,3584]{2,1,0:T(8,128)S(1)}, f32[1,128,3584]{2,1,0:T(8,128)}) custom-call(bf16[256,2048]{1,0:T(8,128)(2,1)S(1)} %bitcast.207, bf16[3584,2048]{1,0:T(8,128)(2,1)S(1)} %copy-done.2, f32[1,64,3712]{2,1,0:T(8,128)S(1)} %get-tuple-element.58.refs_1_), custom_call_target="tpu_custom_call" | custom-call | flops 3758096384 | bytes 19398656 | tf_op jit(solution)/shard_map/pallas_call | solution.py:91
  359.0 13.3 %collective-permute-done.28 = bf16[4,32,2048]{2,1,0:T(8,128)(2,1)} collective-permute-done((bf16[4,32,2048]{2,1,0:T(8,128)(2,1)S(1)}, bf16[4,32,2048]{2,1,0:T(8,128)(2,1)}, u32[]{:S(2)}, u32[]{:S(2)}) %collective-permute-start.28) | collective-permute-done | bytes 524320 | tf_op jit(solution)/shard_map/ppermute | solution.py:29
  373.9 10.4 %collective-permute-done.45 = f16[4,32,2176]{2,1,0:T(8,128)(2,1)} collective-permute-done((f16[4,32,2176]{2,1,0:T(8,128)(2,1)}, f16[4,32,2176]{2,1,0:T(8,128)(2,1)}, u32[]{:S(2)}, u32[]{:S(2)}) %collective-permute-start.45) | collective-permute-done | bytes 557088 | tf_op jit(solution)/shard_map/ppermute | solution.py:29
  385.2 10.2 %collective-permute-done.29 = bf16[4,32,2048]{2,1,0:T(8,128)(2,1)} collective-permute-done((bf16[4,32,2048]{2,1,0:T(8,128)(2,1)}, bf16[4,32,2048]{2,1,0:T(8,128)(2,1)}, u32[]{:S(2)}, u32[]{:S(2)}) %collective-permute-start.29) | collective-permute-done | bytes 524320 | tf_op jit(solution)/shard_map/ppermute | solution.py:29
  399.5 5.5 copy-done.3
  405.0 6.0 %shard_map.79 = (f32[1,128,3584]{2,1,0:T(8,128)S(1)}, f32[1,128,3584]{2,1,0:T(8,128)}) custom-call(bf16[256,2048]{1,0:T(8,128)(2,1)S(1)} %bitcast.206, bf16[3584,2048]{1,0:T(8,128)(2,1)S(1)} %copy-done.3, f32[1,64,3712]{2,1,0:T(8,128)S(1)} %get-tuple-element.62.refs_1_, bf16[2048,256]{1,0:T(8,128)(2,1)S(1)} %bitcast.198), custom_call_target="tpu_custom_call" | custom-call | flops 3758096384 | bytes 19398656 | tf_op jit(solution)/shard_map/pallas_call | solution.py:91
  416.5 13.0 %collective-permute-done.46 = bf16[4,32,2048]{2,1,0:T(8,128)(2,1)} collective-permute-done((bf16[4,32,2048]{2,1,0:T(8,128)(2,1)}, bf16[4,32,2048]{2,1,0:T(8,128)(2,1)}, u32[]{:S(2)}, u32[]{:S(2)}) %collective-permute-start.46) | collective-permute-done | bytes 524320 | tf_op jit(solution)/shard_map/ppermute | solution.py:29
  432.3 12.4 %collective-permute-done.51 = bf16[4,32,2048]{2,1,0:T(8,128)(2,1)S(1)} collective-permute-done((bf16[4,32,2048]{2,1,0:T(8,128)(2,1)}, bf16[4,32,2048]{2,1,0:T(8,128)(2,1)S(1)}, u32[]{:S(2)}, u32[]{:S(2)}) %collective-permute-start.51) | collective-permute-done | bytes 524320 | tf_op jit(solution)/shard_map/ppermute | solution.py:29
  447.7 5.2 copy-done.4
  452.9 5.4 shard_map.83
  462.4 10.3 %collective-permute-done.31 = f16[1,64,3712]{2,1,0:T(8,128)(2,1)S(1)} collective-permute-done((f16[1,64,3712]{2,1,0:T(8,128)(2,1)S(1)}, f16[1,64,3712]{2,1,0:T(8,128)(2,1)S(1)}, u32[]{:S(2)}, u32[]{:S(2)}) %collective-permute-start.31) | collective-permute-done | bytes 475168 | tf_op jit(solution)/shard_map/ppermute | solution.py:24
  473.1 5.4 shard_map.85
  483.0 9.2 %collective-permute-done.32.refs_8_ = bf16[64,3584]{1,0:T(8,128)(2,1)S(1)} collective-permute-done((bf16[64,3584]{1,0:T(8,128)(2,1)S(1)}, bf16[64,3584]{1,0:T(8,128)(2,1)S(1)}, u32[]{:S(2)}, u32[]{:S(2)}) %collective-permute-start.32) | collective-permute-done | bytes 458784 | tf_op jit(solution)/shard_map/ppermute | solution.py:24
  493.3 8.7 %collective-permute-done.48 = f16[1,64,3712]{2,1,0:T(8,128)(2,1)S(1)} collective-permute-done((f16[1,64,3712]{2,1,0:T(8,128)(2,1)S(1)}, f16[1,64,3712]{2,1,0:T(8,128)(2,1)S(1)}, u32[]{:S(2)}, u32[]{:S(2)}) %collective-permute-start.48) | collective-permute-done | bytes 475168 | tf_op jit(solution)/shard_map/ppermute | solution.py:24
  504.9 11.5 %collective-permute-done.54 = f16[1,64,3712]{2,1,0:T(8,128)(2,1)S(1)} collective-permute-done((f16[1,64,3712]{2,1,0:T(8,128)(2,1)S(1)}, f16[1,64,3712]{2,1,0:T(8,128)(2,1)S(1)}, u32[]{:S(2)}, u32[]{:S(2)}) %collective-permute-start.54) | collective-permute-done | bytes 475168 | tf_op jit(solution)/shard_map/ppermute | solution.py:24
  517.9 8.3 %collective-permute-done.49.refs_11_ = bf16[64,3584]{1,0:T(8,128)(2,1)S(1)} collective-permute-done((bf16[64,3584]{1,0:T(8,128)(2,1)S(1)}, bf16[64,3584]{1,0:T(8,128)(2,1)S(1)}, u32[]{:S(2)}, u32[]{:S(2)}) %collective-permute-start.49) | collective-permute-done | bytes 458784 | tf_op jit(solution)/shard_map/ppermute | solution.py:24
  527.3 7.4 %collective-permute-done.55.refs_14_ = bf16[64,3584]{1,0:T(8,128)(2,1)S(1)} collective-permute-done((bf16[64,3584]{1,0:T(8,128)(2,1)S(1)}, bf16[64,3584]{1,0:T(8,128)(2,1)S(1)}, u32[]{:S(2)}, u32[]{:S(2)}) %collective-permute-start.55) | collective-permute-done | bytes 458784 | tf_op jit(solution)/shard_map/ppermute | solution.py:24
  548.1 24.6 %shard_map.87 = f32[2048,3584]{1,0:T(8,128)} custom-call(bf16[2048,256]{1,0:T(8,128)(2,1)S(1)} %bitcast.199, bf16[2048,256]{1,0:T(8,128)(2,1)S(1)} %bitcast.201, bf16[2048,256]{1,0:T(8,128)(2,1)S(1)} %bitcast.203, bf16[2048,256]{1,0:T(8,128)(2,1)S(1)} %bitcast.212, bf16[64,3584]{1,0:T(8,128)(2,1)S(1)} %copy-done.32, bf16[64,3584]{1,0:T(8,128)(2,1)S(1)} %copy-done.46, ...), custom_call_target="tpu_custom_call" | custom-call | flops 15032385536 | bytes 40894464 | tf_op jit(solution)/shard_map/pallas_call | solution.py:196
  (360 shorter events, 146.2 us)
Async XLA Ops:
  25.2 17.7 %collective-permute-start.6 = (f32[3,64,3584]{2,1,0:T(8,128)S(1)}, f32[3,64,3584]{2,1,0:T(8,128)S(1)}, u32[]{:S(2)}, u32[]{:S(2)}) collective-permute-start(f32[3,64,3584]{2,1,0:T(8,128)S(1)} %get-tuple-element.42), channel_id=1, source_target_pairs={{0,1},{1,0},{2,3},{3,2},{4,5},{5,4},{6,7},{7,6},{8,9},{9,8},{10,11... | collective-permute-start | bytes 8257544 | tf_op jit(solution)/shard_map/ppermute | solution.py:24
  25.7 17.2 %collective-permute-start = (bf16[4,32,2048]{2,1,0:T(8,128)(2,1)S(1)}, bf16[4,32,2048]{2,1,0:T(8,128)(2,1)S(1)}, u32[]{:S(2)}, u32[]{:S(2)}) collective-permute-start(bf16[4,32,2048]{2,1,0:T(8,128)(2,1)S(1)} %pad_maximum_fusion.22), channel_id=1, source_target_pairs={{0,4},{4,8},{8,12},{12,0},{1,5},{5,9},{9,13},{13,1},{2,6},{6,10},{... | collective-permute-start | bytes 1572872 | tf_op jit(solution)/shard_map/ppermute | solution.py:29
  42.9 15.6 %collective-permute-start.1 = (bf16[4,32,2048]{2,1,0:T(8,128)(2,1)S(1)}, bf16[4,32,2048]{2,1,0:T(8,128)(2,1)}, u32[]{:S(2)}, u32[]{:S(2)}) collective-permute-start(bf16[4,32,2048]{2,1,0:T(8,128)(2,1)S(1)} %collective-permute-done), channel_id=1, source_target_pairs={{0,4},{4,8},{8,12},{12,0},{1,5},{5,9},{9,13},{13,1},{2,6},{6,10},{... | collective-permute-start | bytes 1572872 | tf_op jit(solution)/shard_map/ppermute | solution.py:29
  44.6 41.0 %collective-permute-start.7 = (f16[3,32,3712]{2,1,0:T(8,128)(2,1)}, f16[3,32,3712]{2,1,0:T(8,128)(2,1)}, u32[]{:S(2)}, u32[]{:S(2)}) collective-permute-start(f16[3,32,3712]{2,1,0:T(8,128)(2,1)} %convert_element_type.156), channel_id=1, source_target_pairs={{0,2},{1,3},{2,0},{3,1},{4,6},{5,7},{6,4},{7,5},{8,10},{9,11},{10,... | collective-permute-start | bytes 2138120 | tf_op jit(solution)/shard_map/ppermute | solution.py:24
  58.5 34.2 %collective-permute-start.2 = (bf16[4,32,2048]{2,1,0:T(8,128)(2,1)}, bf16[4,32,2048]{2,1,0:T(8,128)(2,1)S(1)}, u32[]{:S(2)}, u32[]{:S(2)}) collective-permute-start(bf16[4,32,2048]{2,1,0:T(8,128)(2,1)} %collective-permute-done.1), channel_id=1, source_target_pairs={{0,4},{4,8},{8,12},{12,0},{1,5},{5,9},{9,13},{13,1},{2,6},{6,10},{... | collective-permute-start | bytes 1572872 | tf_op jit(solution)/shard_map/ppermute | solution.py:29
  85.6 52.3 %collective-permute-start.11 = (f32[3,64,3584]{2,1,0:T(8,128)}, f32[3,64,3584]{2,1,0:T(8,128)}, u32[]{:S(2)}, u32[]{:S(2)}) collective-permute-start(f32[3,64,3584]{2,1,0:T(8,128)} %get-tuple-element.46), channel_id=1, source_target_pairs={{0,1},{1,0},{2,3},{3,2},{4,5},{5,4},{6,7},{7,6},{8,9},{9,8},{10,11... | collective-permute-start | bytes 8257544 | tf_op jit(solution)/shard_map/ppermute | solution.py:24
  90.7 14.8 %collective-permute-start.4 = (bf16[4,32,2048]{2,1,0:T(8,128)(2,1)S(1)}, bf16[4,32,2048]{2,1,0:T(8,128)(2,1)S(1)}, u32[]{:S(2)}, u32[]{:S(2)}) collective-permute-start(bf16[4,32,2048]{2,1,0:T(8,128)(2,1)S(1)} %collective-permute-done), channel_id=1, source_target_pairs={{0,16},{16,0},{1,17},{17,1},{2,18},{18,2},{3,19},{19,3},{4,20},{20... | collective-permute-start | bytes 1572872 | tf_op jit(solution)/shard_map/ppermute | solution.py:24
  92.2 24.5 %collective-permute-start.5 = (bf16[4,32,2048]{2,1,0:T(8,128)(2,1)}, bf16[4,32,2048]{2,1,0:T(8,128)(2,1)S(1)}, u32[]{:S(2)}, u32[]{:S(2)}) collective-permute-start(bf16[4,32,2048]{2,1,0:T(8,128)(2,1)} %collective-permute-done.1), channel_id=1, source_target_pairs={{0,16},{16,0},{1,17},{17,1},{2,18},{18,2},{3,19},{19,3},{4,20},{20... | collective-permute-start | bytes 1572872 | tf_op jit(solution)/shard_map/ppermute | solution.py:24
  92.7 34.5 %collective-permute-start.3 = (bf16[4,32,2048]{2,1,0:T(8,128)(2,1)S(1)}, bf16[4,32,2048]{2,1,0:T(8,128)(2,1)S(1)}, u32[]{:S(2)}, u32[]{:S(2)}) collective-permute-start(bf16[4,32,2048]{2,1,0:T(8,128)(2,1)S(1)} %collective-permute-done.2), channel_id=1, source_target_pairs={{0,16},{16,0},{1,17},{17,1},{2,18},{18,2},{3,19},{19,3},{4,20},{20... | collective-permute-start | bytes 1572872 | tf_op jit(solution)/shard_map/ppermute | solution.py:24
  97.4 33.4 %collective-permute-start.9 = (bf16[64,3584]{1,0:T(8,128)(2,1)S(1)}, bf16[64,3584]{1,0:T(8,128)(2,1)S(1)}, u32[]{:S(2)}, u32[]{:S(2)}) collective-permute-start(bf16[64,3584]{1,0:T(8,128)(2,1)S(1)} %pad_maximum_fusion.23), channel_id=1, source_target_pairs={{0,1},{1,0},{2,3},{3,2},{4,5},{5,4},{6,7},{7,6},{8,9},{9,8},{10,11... | collective-permute-start | bytes 1376264 | tf_op jit(solution)/shard_map/ppermute | solution.py:24
  129.3 61.8 %collective-permute-start.34 = (f32[32,3584]{1,0:T(8,128)}, f32[32,3584]{1,0:T(8,128)S(1)}, u32[]{:S(2)}, u32[]{:S(2)}) collective-permute-start(f32[32,3584]{1,0:T(8,128)} %get-tuple-element.78), channel_id=1, source_target_pairs={{0,16},{16,0},{1,17},{17,1},{2,18},{18,2},{3,19},{19,3},{4,20},{20... | collective-permute-start | bytes 1376264 | tf_op jit(solution)/shard_map/ppermute | solution.py:24
  142.6 17.1 %collective-permute-start.12 = (f16[3,32,3712]{2,1,0:T(8,128)(2,1)S(1)}, f16[3,32,3712]{2,1,0:T(8,128)(2,1)S(1)}, u32[]{:S(2)}, u32[]{:S(2)}) collective-permute-start(f16[3,32,3712]{2,1,0:T(8,128)(2,1)S(1)} %convert_element_type.162), channel_id=1, source_target_pairs={{0,2},{1,3},{2,0},{3,1},{4,6},{5,7},{6,4},{7,5},{8,10},{9,11},{10,... | collective-permute-start | bytes 2138120 | tf_op jit(solution)/shard_map/ppermute | solution.py:24
  160.2 29.2 %collective-permute-start.13 = (bf16[32,3584]{1,0:T(8,128)(2,1)S(1)}, bf16[32,3584]{1,0:T(8,128)(2,1)S(1)}, u32[]{:S(2)}, u32[]{:S(2)}) collective-permute-start(bf16[32,3584]{1,0:T(8,128)(2,1)S(1)} %get-tuple-element.79.refs_0_), channel_id=1, source_target_pairs={{0,2},{1,3},{2,0},{3,1},{4,6},{5,7},{6,4},{7,5},{8,10},{9,11},{10,... | collective-permute-start | bytes 688136 | tf_op jit(solution)/shard_map/ppermute | solution.py:24
  161.2 29.6 %collective-permute-start.36 = (f16[1,64,3712]{2,1,0:T(8,128)(2,1)S(1)}, f16[1,64,3712]{2,1,0:T(8,128)(2,1)S(1)}, u32[]{:S(2)}, u32[]{:S(2)}) collective-permute-start(f16[1,64,3712]{2,1,0:T(8,128)(2,1)S(1)} %convert_element_type.183), channel_id=1, source_target_pairs={{0,2},{1,3},{2,0},{3,1},{4,6},{5,7},{6,4},{7,5},{8,10},{9,11},{10,... | collective-permute-start | bytes 1425416 | tf_op jit(solution)/shard_map/ppermute | solution.py:24
  189.1 40.6 %collective-permute-start.17 = (f32[3,128,3584]{2,1,0:T(8,128)}, f32[3,128,3584]{2,1,0:T(8,128)}, u32[]{:S(2)}, u32[]{:S(2)}) collective-permute-start(f32[3,128,3584]{2,1,0:T(8,128)} %get-tuple-element.53), channel_id=1, source_target_pairs={{0,1},{1,0},{2,3},{3,2},{4,5},{5,4},{6,7},{7,6},{8,9},{9,8},{10,11... | collective-permute-start | bytes 16515080 | tf_op jit(solution)/shard_map/ppermute | solution.py:24
  189.4 17.2 %collective-permute-start.10 = (f16[4,32,2176]{2,1,0:T(8,128)(2,1)S(1)}, f16[4,32,2176]{2,1,0:T(8,128)(2,1)S(1)}, u32[]{:S(2)}, u32[]{:S(2)}) collective-permute-start(f16[4,32,2176]{2,1,0:T(8,128)(2,1)S(1)} %pad_maximum_fusion.16), channel_id=1, source_target_pairs={{0,4},{4,8},{8,12},{12,0},{1,5},{5,9},{9,13},{13,1},{2,6},{6,10},{... | collective-permute-start | bytes 1671176 | tf_op jit(solution)/shard_map/ppermute | solution.py:29
  190.8 15.8 %collective-permute-start.14 = (bf16[64,3584]{1,0:T(8,128)(2,1)}, bf16[64,3584]{1,0:T(8,128)(2,1)S(1)}, u32[]{:S(2)}, u32[]{:S(2)}) collective-permute-start(bf16[64,3584]{1,0:T(8,128)(2,1)} %pad_maximum_fusion.24), channel_id=1, source_target_pairs={{0,1},{1,0},{2,3},{3,2},{4,5},{5,4},{6,7},{7,6},{8,9},{9,8},{10,11... | collective-permute-start | bytes 1376264 | tf_op jit(solution)/shard_map/ppermute | solution.py:24
  202.7 15.2 %collective-permute-start.37 = (bf16[64,3584]{1,0:T(8,128)(2,1)S(1)}, bf16[64,3584]{1,0:T(8,128)(2,1)S(1)}, u32[]{:S(2)}, u32[]{:S(2)}) collective-permute-start(bf16[64,3584]{1,0:T(8,128)(2,1)S(1)} %fusion.14.refs_0_), channel_id=1, source_target_pairs={{0,2},{1,3},{2,0},{3,1},{4,6},{5,7},{6,4},{7,5},{8,10},{9,11},{10,... | collective-permute-start | bytes 1376264 | tf_op jit(solution)/shard_map/ppermute | solution.py:24
  219.3 22.8 %collective-permute-start.15 = (f16[4,32,2176]{2,1,0:T(8,128)(2,1)}, f16[4,32,2176]{2,1,0:T(8,128)(2,1)}, u32[]{:S(2)}, u32[]{:S(2)}) collective-permute-start(f16[4,32,2176]{2,1,0:T(8,128)(2,1)} %pad_maximum_fusion.17), channel_id=1, source_target_pairs={{0,4},{4,8},{8,12},{12,0},{1,5},{5,9},{9,13},{13,1},{2,6},{6,10},{... | collective-permute-start | bytes 1671176 | tf_op jit(solution)/shard_map/ppermute | solution.py:29
  229.3 19.1 %collective-permute-start.39 = (f16[4,32,2176]{2,1,0:T(8,128)(2,1)}, f16[4,32,2176]{2,1,0:T(8,128)(2,1)}, u32[]{:S(2)}, u32[]{:S(2)}) collective-permute-start(f16[4,32,2176]{2,1,0:T(8,128)(2,1)} %pad_maximum_fusion.19), channel_id=1, source_target_pairs={{0,4},{4,8},{8,12},{12,0},{1,5},{5,9},{9,13},{13,1},{2,6},{6,10},{... | collective-permute-start | bytes 1671176 | tf_op jit(solution)/shard_map/ppermute | solution.py:29
  238.0 33.4 %collective-permute-start.18 = (f16[3,64,3712]{2,1,0:T(8,128)(2,1)}, f16[3,64,3712]{2,1,0:T(8,128)(2,1)}, u32[]{:S(2)}, u32[]{:S(2)}) collective-permute-start(f16[3,64,3712]{2,1,0:T(8,128)(2,1)} %convert_element_type.168), channel_id=1, source_target_pairs={{0,2},{1,3},{2,0},{3,1},{4,6},{5,7},{6,4},{7,5},{8,10},{9,11},{10,... | collective-permute-start | bytes 4276232 | tf_op jit(solution)/shard_map/ppermute | solution.py:24
  275.5 13.5 %collective-permute-start.19 = (bf16[64,3584]{1,0:T(8,128)(2,1)S(1)}, bf16[64,3584]{1,0:T(8,128)(2,1)S(1)}, u32[]{:S(2)}, u32[]{:S(2)}) collective-permute-start(bf16[64,3584]{1,0:T(8,128)(2,1)S(1)} %get-tuple-element.81.refs_0_), channel_id=1, source_target_pairs={{0,2},{1,3},{2,0},{3,1},{4,6},{5,7},{6,4},{7,5},{8,10},{9,11},{10,... | collective-permute-start | bytes 1376264 | tf_op jit(solution)/shard_map/ppermute | solution.py:24
  278.1 21.1 %collective-permute-start.41 = (f32[64,3584]{1,0:T(8,128)S(1)}, f32[64,3584]{1,0:T(8,128)S(1)}, u32[]{:S(2)}, u32[]{:S(2)}) collective-permute-start(f32[64,3584]{1,0:T(8,128)S(1)} %get-tuple-element.82), channel_id=1, source_target_pairs={{0,16},{16,0},{1,17},{17,1},{2,18},{18,2},{3,19},{19,3},{4,20},{20... | collective-permute-start | bytes 2752520 | tf_op jit(solution)/shard_map/ppermute | solution.py:24
  279.1 18.2 %collective-permute-start.42 = (f16[1,64,3712]{2,1,0:T(8,128)(2,1)S(1)}, f16[1,64,3712]{2,1,0:T(8,128)(2,1)S(1)}, u32[]{:S(2)}, u32[]{:S(2)}) collective-permute-start(f16[1,64,3712]{2,1,0:T(8,128)(2,1)S(1)} %convert_element_type.191), channel_id=1, source_target_pairs={{0,2},{1,3},{2,0},{3,1},{4,6},{5,7},{6,4},{7,5},{8,10},{9,11},{10,... | collective-permute-start | bytes 1425416 | tf_op jit(solution)/shard_map/ppermute | solution.py:24
  280.2 34.5 %collective-permute-start.40 = (f16[4,32,2176]{2,1,0:T(8,128)(2,1)S(1)}, f16[4,32,2176]{2,1,0:T(8,128)(2,1)S(1)}, u32[]{:S(2)}, u32[]{:S(2)}) collective-permute-start(f16[4,32,2176]{2,1,0:T(8,128)(2,1)S(1)} %pad_maximum_fusion.20), channel_id=1, source_target_pairs={{0,4},{4,8},{8,12},{12,0},{1,5},{5,9},{9,13},{13,1},{2,6},{6,10},{... | collective-permute-start | bytes 1671176 | tf_op jit(solution)/shard_map/ppermute | solution.py:29
  299.5 13.5 %collective-permute-start.43 = (bf16[64,3584]{1,0:T(8,128)(2,1)S(1)}, bf16[64,3584]{1,0:T(8,128)(2,1)S(1)}, u32[]{:S(2)}, u32[]{:S(2)}) collective-permute-start(bf16[64,3584]{1,0:T(8,128)(2,1)S(1)} %fusion.17.refs_0_), channel_id=1, source_target_pairs={{0,2},{1,3},{2,0},{3,1},{4,6},{5,7},{6,4},{7,5},{8,10},{9,11},{10,... | collective-permute-start | bytes 1376264 | tf_op jit(solution)/shard_map/ppermute | solution.py:24
  311.6 14.4 %collective-permute-start.21 = (f16[4,32,2176]{2,1,0:T(8,128)(2,1)}, f16[4,32,2176]{2,1,0:T(8,128)(2,1)}, u32[]{:S(2)}, u32[]{:S(2)}) collective-permute-start(f16[4,32,2176]{2,1,0:T(8,128)(2,1)} %pad_maximum_fusion.18), channel_id=1, source_target_pairs={{0,4},{4,8},{8,12},{12,0},{1,5},{5,9},{9,13},{13,1},{2,6},{6,10},{... | collective-permute-start | bytes 1671176 | tf_op jit(solution)/shard_map/ppermute | solution.py:29
  314.7 15.4 %collective-permute-start.44 = (bf16[128,3584]{1,0:T(8,128)(2,1)}, bf16[128,3584]{1,0:T(8,128)(2,1)}, u32[]{:S(2)}, u32[]{:S(2)}) collective-permute-start(bf16[128,3584]{1,0:T(8,128)(2,1)} %pad_maximum_fusion.13), channel_id=1, source_target_pairs={{0,1},{1,0},{2,3},{3,2},{4,5},{5,4},{6,7},{7,6},{8,9},{9,8},{10,11... | collective-permute-start | bytes 2752520 | tf_op jit(solution)/shard_map/ppermute | solution.py:24
  330.0 14.0 %collective-permute-start.22 = (bf16[4,32,2048]{2,1,0:T(8,128)(2,1)S(1)}, bf16[4,32,2048]{2,1,0:T(8,128)(2,1)S(1)}, u32[]{:S(2)}, u32[]{:S(2)}) collective-permute-start(bf16[4,32,2048]{2,1,0:T(8,128)(2,1)S(1)} %fusion.7), channel_id=1, source_target_pairs={{0,4},{4,8},{8,12},{12,0},{1,5},{5,9},{9,13},{13,1},{2,6},{6,10},{... | collective-permute-start | bytes 1572872 | tf_op jit(solution)/shard_map/ppermute | solution.py:29
  355.3 41.3 %collective-permute-start.24 = (f32[1,128,3584]{2,1,0:T(8,128)}, f32[1,128,3584]{2,1,0:T(8,128)}, u32[]{:S(2)}, u32[]{:S(2)}) collective-permute-start(f32[1,128,3584]{2,1,0:T(8,128)} %get-tuple-element.60), channel_id=1, source_target_pairs={{0,1},{1,0},{2,3},{3,2},{4,5},{5,4},{6,7},{7,6},{8,9},{9,8},{10,11... | collective-permute-start | bytes 5505032 | tf_op jit(solution)/shard_map/ppermute | solution.py:24
  355.6 16.8 %collective-permute-start.28 = (bf16[4,32,2048]{2,1,0:T(8,128)(2,1)S(1)}, bf16[4,32,2048]{2,1,0:T(8,128)(2,1)}, u32[]{:S(2)}, u32[]{:S(2)}) collective-permute-start(bf16[4,32,2048]{2,1,0:T(8,128)(2,1)S(1)} %collective-permute-done.22), channel_id=1, source_target_pairs={{0,4},{4,8},{8,12},{12,0},{1,5},{5,9},{9,13},{13,1},{2,6},{6,10},{... | collective-permute-start | bytes 1572872 | tf_op jit(solution)/shard_map/ppermute | solution.py:29
  358.2 26.1 %collective-permute-start.45 = (f16[4,32,2176]{2,1,0:T(8,128)(2,1)}, f16[4,32,2176]{2,1,0:T(8,128)(2,1)}, u32[]{:S(2)}, u32[]{:S(2)}) collective-permute-start(f16[4,32,2176]{2,1,0:T(8,128)(2,1)} %pad_maximum_fusion.21), channel_id=1, source_target_pairs={{0,4},{4,8},{8,12},{12,0},{1,5},{5,9},{9,13},{13,1},{2,6},{6,10},{... | collective-permute-start | bytes 1671176 | tf_op jit(solution)/shard_map/ppermute | solution.py:29
  372.4 23.0 %collective-permute-start.29 = (bf16[4,32,2048]{2,1,0:T(8,128)(2,1)}, bf16[4,32,2048]{2,1,0:T(8,128)(2,1)}, u32[]{:S(2)}, u32[]{:S(2)}) collective-permute-start(bf16[4,32,2048]{2,1,0:T(8,128)(2,1)} %collective-permute-done.28), channel_id=1, source_target_pairs={{0,4},{4,8},{8,12},{12,0},{1,5},{5,9},{9,13},{13,1},{2,6},{6,10},{... | collective-permute-start | bytes 1572872 | tf_op jit(solution)/shard_map/ppermute | solution.py:29
  411.1 34.8 %collective-permute-start.30 = (f32[1,128,3584]{2,1,0:T(8,128)}, f32[1,128,3584]{2,1,0:T(8,128)}, u32[]{:S(2)}, u32[]{:S(2)}) collective-permute-start(f32[1,128,3584]{2,1,0:T(8,128)} %get-tuple-element.64), channel_id=1, source_target_pairs={{0,1},{1,0},{2,3},{3,2},{4,5},{5,4},{6,7},{7,6},{8,9},{9,8},{10,11... | collective-permute-start | bytes 5505032 | tf_op jit(solution)/shard_map/ppermute | solution.py:24
  413.6 16.0 %collective-permute-start.46 = (bf16[4,32,2048]{2,1,0:T(8,128)(2,1)}, bf16[4,32,2048]{2,1,0:T(8,128)(2,1)}, u32[]{:S(2)}, u32[]{:S(2)}) collective-permute-start(bf16[4,32,2048]{2,1,0:T(8,128)(2,1)} %fusion.2), channel_id=1, source_target_pairs={{0,4},{4,8},{8,12},{12,0},{1,5},{5,9},{9,13},{13,1},{2,6},{6,10},{... | collective-permute-start | bytes 1572872 | tf_op jit(solution)/shard_map/ppermute | solution.py:29
  429.6 15.1 %collective-permute-start.51 = (bf16[4,32,2048]{2,1,0:T(8,128)(2,1)}, bf16[4,32,2048]{2,1,0:T(8,128)(2,1)S(1)}, u32[]{:S(2)}, u32[]{:S(2)}) collective-permute-start(bf16[4,32,2048]{2,1,0:T(8,128)(2,1)} %collective-permute-done.46), channel_id=1, source_target_pairs={{0,4},{4,8},{8,12},{12,0},{1,5},{5,9},{9,13},{13,1},{2,6},{6,10},{... | collective-permute-start | bytes 1572872 | tf_op jit(solution)/shard_map/ppermute | solution.py:29
  444.7 14.0 %collective-permute-start.52 = (bf16[4,32,2048]{2,1,0:T(8,128)(2,1)S(1)}, bf16[4,32,2048]{2,1,0:T(8,128)(2,1)S(1)}, u32[]{:S(2)}, u32[]{:S(2)}) collective-permute-start(bf16[4,32,2048]{2,1,0:T(8,128)(2,1)S(1)} %collective-permute-done.51), channel_id=1, source_target_pairs={{0,4},{4,8},{8,12},{12,0},{1,5},{5,9},{9,13},{13,1},{2,6},{6,10},{... | collective-permute-start | bytes 1572872 | tf_op jit(solution)/shard_map/ppermute | solution.py:29
  444.7 14.0 %collective-permute-start.25 = (f16[1,64,3712]{2,1,0:T(8,128)(2,1)S(1)}, f16[1,64,3712]{2,1,0:T(8,128)(2,1)S(1)}, u32[]{:S(2)}, u32[]{:S(2)}) collective-permute-start(f16[1,64,3712]{2,1,0:T(8,128)(2,1)S(1)} %convert_element_type.175), channel_id=1, source_target_pairs={{0,2},{1,3},{2,0},{3,1},{4,6},{5,7},{6,4},{7,5},{8,10},{9,11},{10,... | collective-permute-start | bytes 1425416 | tf_op jit(solution)/shard_map/ppermute | solution.py:24
  458.3 14.5 %collective-permute-start.47 = (f32[1,128,3584]{2,1,0:T(8,128)S(1)}, f32[1,128,3584]{2,1,0:T(8,128)S(1)}, u32[]{:S(2)}, u32[]{:S(2)}) collective-permute-start(f32[1,128,3584]{2,1,0:T(8,128)S(1)} %get-tuple-element.70), channel_id=1, source_target_pairs={{0,1},{1,0},{2,3},{3,2},{4,5},{5,4},{6,7},{7,6},{8,9},{9,8},{10,11... | collective-permute-start | bytes 5505032 | tf_op jit(solution)/shard_map/ppermute | solution.py:24
  458.9 13.8 %collective-permute-start.31 = (f16[1,64,3712]{2,1,0:T(8,128)(2,1)S(1)}, f16[1,64,3712]{2,1,0:T(8,128)(2,1)S(1)}, u32[]{:S(2)}, u32[]{:S(2)}) collective-permute-start(f16[1,64,3712]{2,1,0:T(8,128)(2,1)S(1)} %convert_element_type.179), channel_id=1, source_target_pairs={{0,2},{1,3},{2,0},{3,1},{4,6},{5,7},{6,4},{7,5},{8,10},{9,11},{10,... | collective-permute-start | bytes 1425416 | tf_op jit(solution)/shard_map/ppermute | solution.py:24
  461.4 20.5 %collective-permute-start.26 = (bf16[64,3584]{1,0:T(8,128)(2,1)S(1)}, bf16[64,3584]{1,0:T(8,128)(2,1)S(1)}, u32[]{:S(2)}, u32[]{:S(2)}) collective-permute-start(bf16[64,3584]{1,0:T(8,128)(2,1)S(1)} %fusion.12.refs_4_), channel_id=1, source_target_pairs={{0,2},{1,3},{2,0},{3,1},{4,6},{5,7},{6,4},{7,5},{8,10},{9,11},{10,... | collective-permute-start | bytes 1376264 | tf_op jit(solution)/shard_map/ppermute | solution.py:24
  478.5 23.6 %collective-permute-start.53 = (f32[1,128,3584]{2,1,0:T(8,128)S(1)}, f32[1,128,3584]{2,1,0:T(8,128)S(1)}, u32[]{:S(2)}, u32[]{:S(2)}) collective-permute-start(f32[1,128,3584]{2,1,0:T(8,128)S(1)} %get-tuple-element.74), channel_id=1, source_target_pairs={{0,1},{1,0},{2,3},{3,2},{4,5},{5,4},{6,7},{7,6},{8,9},{9,8},{10,11... | collective-permute-start | bytes 5505032 | tf_op jit(solution)/shard_map/ppermute | solution.py:24
  480.1 21.9 %collective-permute-start.48 = (f16[1,64,3712]{2,1,0:T(8,128)(2,1)S(1)}, f16[1,64,3712]{2,1,0:T(8,128)(2,1)S(1)}, u32[]{:S(2)}, u32[]{:S(2)}) collective-permute-start(f16[1,64,3712]{2,1,0:T(8,128)(2,1)S(1)} %convert_element_type.198), channel_id=1, source_target_pairs={{0,2},{1,3},{2,0},{3,1},{4,6},{5,7},{6,4},{7,5},{8,10},{9,11},{10,... | collective-permute-start | bytes 1425416 | tf_op jit(solution)/shard_map/ppermute | solution.py:24
  483.0 55.2 %collective-permute-start.27 = (bf16[128,3584]{1,0:T(8,128)(2,1)}, bf16[128,3584]{1,0:T(8,128)(2,1)}, u32[]{:S(2)}, u32[]{:S(2)}) collective-permute-start(bf16[128,3584]{1,0:T(8,128)(2,1)} %pad_maximum_fusion.10), channel_id=1, source_target_pairs={{0,1},{1,0},{2,3},{3,2},{4,5},{5,4},{6,7},{7,6},{8,9},{9,8},{10,11... | collective-permute-start | bytes 2752520 | tf_op jit(solution)/shard_map/ppermute | solution.py:24
  493.3 44.9 %collective-permute-start.33 = (bf16[128,3584]{1,0:T(8,128)(2,1)}, bf16[128,3584]{1,0:T(8,128)(2,1)}, u32[]{:S(2)}, u32[]{:S(2)}) collective-permute-start(bf16[128,3584]{1,0:T(8,128)(2,1)} %pad_maximum_fusion.11), channel_id=1, source_target_pairs={{0,1},{1,0},{2,3},{3,2},{4,5},{5,4},{6,7},{7,6},{8,9},{9,8},{10,11... | collective-permute-start | bytes 2752520 | tf_op jit(solution)/shard_map/ppermute | solution.py:24
  502.5 13.8 %collective-permute-start.54 = (f16[1,64,3712]{2,1,0:T(8,128)(2,1)S(1)}, f16[1,64,3712]{2,1,0:T(8,128)(2,1)S(1)}, u32[]{:S(2)}, u32[]{:S(2)}) collective-permute-start(f16[1,64,3712]{2,1,0:T(8,128)(2,1)S(1)} %convert_element_type.202), channel_id=1, source_target_pairs={{0,2},{1,3},{2,0},{3,1},{4,6},{5,7},{6,4},{7,5},{8,10},{9,11},{10,... | collective-permute-start | bytes 1425416 | tf_op jit(solution)/shard_map/ppermute | solution.py:24
  503.9 22.3 %collective-permute-start.49 = (bf16[64,3584]{1,0:T(8,128)(2,1)S(1)}, bf16[64,3584]{1,0:T(8,128)(2,1)S(1)}, u32[]{:S(2)}, u32[]{:S(2)}) collective-permute-start(bf16[64,3584]{1,0:T(8,128)(2,1)S(1)} %fusion.15.refs_10_), channel_id=1, source_target_pairs={{0,2},{1,3},{2,0},{3,1},{4,6},{5,7},{6,4},{7,5},{8,10},{9,11},{10,... | collective-permute-start | bytes 1376264 | tf_op jit(solution)/shard_map/ppermute | solution.py:24
  516.7 18.0 %collective-permute-start.55 = (bf16[64,3584]{1,0:T(8,128)(2,1)S(1)}, bf16[64,3584]{1,0:T(8,128)(2,1)S(1)}, u32[]{:S(2)}, u32[]{:S(2)}) collective-permute-start(bf16[64,3584]{1,0:T(8,128)(2,1)S(1)} %fusion.16.refs_13_), channel_id=1, source_target_pairs={{0,2},{1,3},{2,0},{3,1},{4,6},{5,7},{6,4},{7,5},{8,10},{9,11},{10,... | collective-permute-start | bytes 1376264 | tf_op jit(solution)/shard_map/ppermute | solution.py:24
  (93 other events, 1058.0 us)

commit v3 on v2

v3 whole, which is shorter than its diff:
```python
import functools

import jax
import jax.numpy as jnp
from jax import lax
from jax.experimental import pallas as pl
from jax.experimental.pallas import tpu as pltpu
from jax.sharding import PartitionSpec as P

TOP_BITS = 14
LEAST_TOP = 1e-30
FACTORS = 4
LANES = 128
MIB = 1024 * 1024
A_CUTS = (0, 1, 2, 4)
ORDER = [(0, 0), (0, 1), (1, 0), (0, 2), (1, 1)]


def slot_masks(count):
    bits = count.bit_length() - 1
    assert 1 << bits == count
    return [sum(((s >> b) & 1) << (bits - 1 - b) for b in range(bits)) for s in range(count)]


def swap(values, axis, mask):
    count = lax.axis_size(axis)
    return lax.ppermute(values, axis, [(i, i ^ mask) for i in range(count)])


def shift(values, axis, by=1):
    count = lax.axis_size(axis)
    return lax.ppermute(values, axis, [(i, (i + by) % count) for i in range(count)])


def scaled_rows(values):
    top = jnp.max(jnp.abs(values), axis=-1, keepdims=True)
    power = jnp.ceil(jnp.log2(jnp.maximum(top, LEAST_TOP))) - TOP_BITS
    factors, left = [], power
    for _ in range(FACTORS):
        factors.append(jnp.clip(left, -14.0, 15.0))
        left = left - factors[-1]
    power = power - left
    return values * jnp.exp2(-power), [jnp.exp2(factor) for factor in factors]


def coded(values):
    body, factors = scaled_rows(values)
    width = LANES // FACTORS
    marks = [jnp.broadcast_to(f, (*values.shape[:-1], width)) for f in factors]
    return jnp.concatenate([body, *marks], axis=-1)


def decoded(code):
    width = code.shape[-1] - LANES
    values = code[..., :width].astype(jnp.float32)
    for i in range(FACTORS):
        at = width + i * (LANES // FACTORS)
        values = values * code[..., at : at + 1].astype(jnp.float32)
    return values


def tile_of(size, tile):
    return tile if size % tile == 0 else size


PARAMS = pltpu.CompilerParams(vmem_limit_bytes=58 * MIB)
ANYWHERE = pl.BlockSpec(memory_space=pl.ANY)


def cost(rows, depth, width, moved):
    return pl.CostEstimate(
        flops=2 * rows * depth * width, bytes_accessed=moved, transcendentals=0
    )


def fixed(array):
    return pl.BlockSpec(array.shape, lambda j: (0,) * array.ndim)


def split_kernel(pieces, count, turned, *refs):
    xs, weights = refs[:pieces], refs[pieces : pieces + count]
    keep_ref, give_ref, held = refs[-3:]
    rows = xs[0].shape[0]
    half = rows // 2

    @pl.when(pl.program_id(0) == 0)
    def _():
        for i in range(pieces):
            held[i * rows : (i + 1) * rows] = xs[i][...]

    contract = (((1,), (1,)), ((), ())) if turned else (((1,), (0,)), ((), ()))
    for at in range(count):
        part = lax.dot_general(
            held[...], weights[at][...], contract, preferred_element_type=jnp.float32
        )
        for i in range(pieces):
            to = slice(i * half, (i + 1) * half)
            keep_ref[at, to] = part[i * rows : i * rows + half]
            give_ref[at, to] = part[i * rows + half : (i + 1) * rows]


def split_products(xs, weights, after=(), turned=False):
    rows, depth = len(xs) * xs[0].shape[0], xs[0].shape[1]
    width = weights[0].shape[0 if turned else 1]
    count = len(weights)
    tile = tile_of(width, 512)
    spec = (
        pl.BlockSpec((tile, depth), lambda j: (j, 0))
        if turned
        else pl.BlockSpec((depth, tile), lambda j: (0, j))
    )
    out = pl.BlockSpec((count, rows // 2, tile), lambda j: (0, 0, j))
    return pl.pallas_call(
        functools.partial(split_kernel, len(xs), count, turned),
        grid=(width // tile,),
        out_shape=[jax.ShapeDtypeStruct((count, rows // 2, width), jnp.float32)] * 2,
        in_specs=[fixed(x) for x in xs] + [spec] * count + [ANYWHERE] * len(after),
        out_specs=[out, out],
        scratch_shapes=[pltpu.VMEM((rows, depth), jnp.bfloat16)],
        compiler_params=PARAMS,
        cost_estimate=cost(
            rows, depth, width * count, count * width * (depth * 2 + rows * 4) + rows * depth * 2
        ),
    )(*xs, *weights, *after)


def fold_kernel(pieces, code, keep_ref, got_ref, own_ref, code_ref):
    width = own_ref.shape[2]
    rows = own_ref.shape[1] // pieces
    for i in range(pieces):
        to, at = slice(i * rows, (i + 1) * rows), 2 * i * rows
        own_ref[0, to] = keep_ref[0, at : at + rows] + got_ref[0, at : at + rows]
        at += rows
        lower = keep_ref[0, at : at + rows] + got_ref[0, at : at + rows]
        if not code:
            code_ref[0, to] = lower.astype(jnp.bfloat16)
            continue
        body, factors = scaled_rows(lower)
        code_ref[0, to, :width] = body
        marks = jnp.concatenate(
            [jnp.broadcast_to(f, (rows, LANES // FACTORS)) for f in factors], axis=-1
        )
        code_ref[0, to, width:] = marks


def fold(keep, got, pieces, code):
    count, both, width = keep.shape
    rows = both // 2
    if width % LANES or rows // pieces % 16:
        total = (keep + got).reshape(count, pieces, 2, rows // pieces, width)
        own, lower = (total[:, :, i].reshape(count, rows, width) for i in range(2))
        return own, coded(lower) if code else lower.astype(jnp.bfloat16)
    taken = pl.BlockSpec((1, both, width), lambda i: (i, 0, 0))
    sent = jax.ShapeDtypeStruct(
        (count, rows, width + LANES if code else width), jnp.float32 if code else jnp.bfloat16
    )
    return pl.pallas_call(
        functools.partial(fold_kernel, pieces, code),
        grid=(count,),
        out_shape=[jax.ShapeDtypeStruct((count, rows, width), jnp.float32), sent],
        in_specs=[taken, taken],
        out_specs=[
            pl.BlockSpec((1, rows, width), lambda i: (i, 0, 0)),
            pl.BlockSpec((1, *sent.shape[1:]), lambda i: (i, 0, 0)),
        ],
        compiler_params=PARAMS,
        cost_estimate=cost(1, count * both, width, count * both * width * 12),
    )(keep, got)


def placed(parts, pieces):
    total = sum(part.shape[0] for part in parts)
    least = min(part.shape[0] for part in parts)
    slots, rows = total // least, least // pieces
    if rows % 16:
        whole = jnp.concatenate(parts, axis=0).reshape(slots, pieces, rows, -1)
        return [whole.swapaxes(0, 1).reshape(total, -1)], [[(0, 0, total)]]
    runs, slot = [], 0
    for part in parts:
        runs.append([])
        for at in range(part.shape[0] // least):
            for i in range(pieces):
                runs[-1].append((at * least + i * rows, (i * slots + slot) * rows, rows))
            slot += 1
    return parts, runs


def put(runs, refs, held, base=0):
    for part, ref in zip(runs, refs):
        for source, to, rows in part:
            held[base + to : base + to + rows] = ref[source : source + rows]


def out_kernel(runs, first, *refs):
    weight_ref, outs, held = refs[len(runs)], refs[len(runs) + 1 : -1], refs[-1]

    @pl.when(pl.program_id(0) == 0)
    def _():
        put(runs, refs, held)

    part = jnp.dot(held[...], weight_ref[...], preferred_element_type=jnp.float32)
    rows = outs[0].shape[0]
    for i, out_ref in enumerate(outs):
        out_ref[...] = part[i * rows : (i + 1) * rows].astype(out_ref.dtype)


def out_product(parts, weight, pieces, first):
    parts, runs = placed(parts, pieces)
    rows = sum(part.shape[0] for part in parts)
    depth, width = weight.shape
    tile = tile_of(width, 256)
    types = [jnp.float32 if first and i == 0 else jnp.bfloat16 for i in range(pieces)]
    return pl.pallas_call(
        functools.partial(out_kernel, runs, first),
        grid=(width // tile,),
        out_shape=[jax.ShapeDtypeStruct((rows // pieces, width), t) for t in types],
        in_specs=[fixed(part) for part in parts]
        + [pl.BlockSpec((depth, tile), lambda j: (0, j))],
        out_specs=[pl.BlockSpec((rows // pieces, tile), lambda j: (0, j))] * pieces,
        scratch_shapes=[pltpu.VMEM((rows, depth), jnp.bfloat16)],
        compiler_params=PARAMS,
        cost_estimate=cost(rows, depth, width, (depth * width + rows * (depth + width)) * 2),
    )(*parts, weight)


def last_kernel(scale, runs, bases, parts, *refs):
    turned, bars = refs[:parts], refs[parts:-3]
    out_ref, left, right = refs[-3:]
    height = out_ref.shape[0]
    step = tile_of(height, 512)

    @pl.when(pl.program_id(0) == 0)
    def _():
        at = 0
        for part in turned:
            left[:, at : at + part.shape[1]] = part[...]
            at += part.shape[1]

    at = 0
    for run, base in zip(runs, bases):
        put(run, bars[at : at + len(run)], right, base)
        at += len(run)

    @pl.loop(0, height // step)
    def _(at):
        rows = pl.ds(pl.multiple_of(at * step, step), step)
        total = jnp.dot(left[rows, :], right[...], preferred_element_type=jnp.float32)
        out_ref[rows, :] = total * scale


def last_product(turned, steps, tokens):
    bars, runs, bases, base = [], [], [], 0
    for parts, pieces in steps:
        parts, run = placed(parts, pieces)
        bars += parts
        runs.append(run)
        bases.append(base)
        base += sum(part.shape[0] for part in parts)
    features, hidden = turned[0].shape[0], bars[0].shape[1]
    tile = tile_of(hidden, 512)
    return pl.pallas_call(
        functools.partial(last_kernel, 1.0 / tokens, runs, bases, len(turned)),
        grid=(hidden // tile,),
        out_shape=jax.ShapeDtypeStruct((features, hidden), jnp.float32),
        in_specs=[fixed(t) for t in turned]
        + [pl.BlockSpec((b.shape[0], tile), lambda j: (0, j)) for b in bars],
        out_specs=pl.BlockSpec((features, tile), lambda j: (0, j)),
        scratch_shapes=[
            pltpu.VMEM((features, tokens), jnp.bfloat16),
            pltpu.VMEM((tokens, tile), jnp.bfloat16),
        ],
        compiler_params=PARAMS,
        cost_estimate=cost(
            features, tokens, hidden, features * hidden * 4 + tokens * (features + hidden) * 2
        ),
    )(*turned, *bars)


def per_device(inputs, w_gate, w_up, w_down, query, curvature):
    ring, count = lax.axis_size("row"), lax.axis_size("col")
    assert lax.axis_size("grp") == 2 and ring % 4 == 0 and count >= 4
    shard, width = inputs.shape
    tokens = shard * ring
    rows = shard // 2 // count
    masks = slot_masks(count)
    place, grp, me = lax.axis_index("col"), lax.axis_index("grp"), lax.axis_index("row")

    def own_rows(array, start, half):
        begin = start + half * (shard // 2)
        return jnp.concatenate(
            [
                lax.dynamic_slice_in_dim(array, begin + (place ^ mask) * rows, rows, 0)
                for mask in masks
            ]
        )

    def spans(*cuts):
        ends = [cut * ring // 4 for cut in cuts]
        return [list(range(a, b)) for a, b in zip(ends, ends[1:])]

    steps = [spans(*A_CUTS), spans(0, 2, 4)]
    halves = (grp, 1 - grp)

    acts = [[own_rows(inputs, 0, half)] for half in halves]
    for k in range(1, ring):
        acts[0].append(shift(acts[0][-1], "row"))
        acts[1].append(swap(acts[0][-1], "grp", 1))
    curvs = [own_rows(curvature, me * shard, half) for half in halves]

    def sum_over_col(xs, weights, after, code, turned=False):
        keep, give = split_products(xs, weights, after, turned)
        own, sent = fold(keep, swap(give, "col", 1), len(xs), code)
        mark, mask = sent, 2
        while True:
            if code:
                own = own + decoded(swap(sent.astype(jnp.float16), "col", mask))
            else:
                own = own + swap(sent, "col", mask).astype(jnp.float32)
            mask *= 2
            if mask >= count:
                return own, mark
            both = own.reshape(own.shape[0], len(xs), 2, -1, own.shape[2])
            own, sent = (both[:, :, i].reshape(own.shape[0], -1, own.shape[2]) for i in range(2))
            sent = coded(sent) if code else sent.astype(jnp.bfloat16)

    def gather_over_col(values):
        parts, mask = [values], count // 2
        while mask >= 1:
            block = parts[0] if len(parts) == 1 else jnp.concatenate(parts, axis=0)
            parts.append(swap(block, "col", mask))
            mask //= 2
        return parts

    gains = [[None] * ring, [None] * ring]

    def gain_of(half, step):
        kept = [gains[half][k] for k in step]
        return kept[0] if len(kept) == 1 else jnp.concatenate(kept, axis=0)

    def hidden(half, step, own):
        if half == 0:
            gate_out, up_out = own[0], own[1]
            sigmas = jax.nn.sigmoid(gate_out)
            gain = sigmas * (1.0 + gate_out * (1.0 - sigmas)) * up_out
            other = swap(gain, "grp", 1)
            for i, k in enumerate(step):
                gains[0][k] = gain[i * rows : (i + 1) * rows]
                gains[1][k] = other[i * rows : (i + 1) * rows]
        else:
            gain = gain_of(1, step)
        return (gain * own[-1]).astype(jnp.bfloat16)

    totals = [[None] * ring, [None] * ring]
    after = []
    for half, at in ORDER:
        step = steps[half][at]
        weights = [w_gate, w_up, query] if half == 0 else [query]
        xs = [acts[half][k] for k in step]
        own, mark = sum_over_col(xs, weights, after, True)
        after = [mark]
        parts = gather_over_col(hidden(half, step, own))
        outs = out_product(parts, w_down, len(step), step[0] == 0)
        for k, out in zip(step, outs):
            totals[half][k] = shift(out, "row", -k) if k else out

    turned, bars = [], []
    for half in range(2):
        total = totals[half][0]
        for k in range(1, ring):
            total = total + totals[half][k].astype(jnp.float32)
        pieces = [(curvs[half] * total).astype(jnp.bfloat16)]
        for _ in range(ring - 1):
            pieces.append(shift(pieces[-1], "row"))
        for step in spans(0, 2, 4):
            kept = [acts[half][k] for k in step]
            if kept[0].shape[0] % LANES:
                kept = [jnp.concatenate(kept, axis=0)]
            turned += [array.T for array in kept]
            xs = [pieces[k] for k in step]
            own, mark = sum_over_col(xs, [w_down], after, False, True)
            after = [mark] + turned[-len(kept) :]
            bar = (own[0] * gain_of(half, step)).astype(jnp.bfloat16)
            bars.append((gather_over_col(bar), len(step)))
    return last_product(turned, bars, tokens)


def solution(mesh):
    in_specs = (
        P("row", "col"),
        P("col", "row"),
        P("col", "row"),
        P("row", "col"),
        P(("grp", "col"), "row"),
        P("grp", "col"),
    )
    out_specs = P(("grp", "col"), "row")
    return jax.shard_map(
        per_device, mesh=mesh, in_specs=in_specs, out_specs=out_specs, check_vma=False
    )
```

time: 575 us -> 615 us (1.070)
  Pallas kernels: 167 us -> 248 us
  local copies, waits for them, and re-layouts: 90.4 us -> 29.6 us
  waiting for transfers between devices: 230 us -> 258 us
  other arithmetic: 48.5 us -> 35.7 us
    pallas_call x24, Pallas kernels: 167 us -> 248 us  [the longest x9 131 us: split_products(): pl.pallas_call(functools.partial(split_kernel, len(xs), count, turned), g...]
    unnamed x174 -> x111, local copies, waits for them, and re-layouts: 76.8 us -> 8.84 us
    ppermute x15, waiting for transfers between devices: 104 us -> 158 us  [shift(): lax.ppermute(values, axis, [(i, (i + by) % count) for i in range(count)])]
    ppermute x42, waiting for transfers between devices: 126 us -> 100 us  [swap(): return lax.ppermute(values, axis, [(i, i ^ mask) for i in range(count)])]
    ppermute x0 -> x6, local copies, waits for them, and re-layouts: none -> 12.4 us  [the longest x3 6.21 us: swap(): return lax.ppermute(values, axis, [(i, i ^ mask) for i in range(count)])]
    concatenate x12 -> x2, other arithmetic: 12.2 us -> 2.19 us  [own_rows(): jnp.concatenate([lax.dynamic_slice_in_dim(array, begin + (place ^ mask) *...]
    exp2 x21 -> x0, other arithmetic: 7 us -> none  [the longest x15 6.91 us: decoded(): unit = jnp.exp2(code[..., width:width + 1].astype(jnp.float32) - TOP_BITS)]
    reshape x4 -> x0, local copies, waits for them, and re-layouts: 6.7 us -> none  [joined(): return jnp.concatenate(pieces, axis=1).reshape(-1, pieces[0].shape[-1])]
  transfers between devices with their start and end apart: 57 -> 57, of which waited for: 30 -> 21; matrix products, arithmetic and copies ran while one was open for 11% -> 9% of each run, Pallas kernels for 19% -> 20%
where the time goes in v3:
time: 615 us; the launch traced here: 612 us
  waiting for transfers between devices  258 us (42%)
  Pallas kernels  248 us (40%)
  starting transfers between devices  39.4 us (6%)
  other arithmetic  35.7 us (6%)
  local copies, waits for them, and re-layouts  29.6 us (5%)
    ppermute x15, waiting for transfers between devices, shift(): lax.ppermute(values, axis, [(i, (i + by) % count) for i in range(count)])  158 us
    pallas_call x9, Pallas kernels, split_products(): pl.pallas_call(functools.partial(split_kernel, len(xs), count, turned), g...  131 us
    ppermute x42, waiting for transfers between devices, swap(): return lax.ppermute(values, axis, [(i, i ^ mask) for i in range(count)])  100 us
    pallas_call x5, Pallas kernels, out_product(): pl.pallas_call(functools.partial(out_kernel, runs, first), grid=(width //...  52.9 us
    pallas_call x9, Pallas kernels, fold(): pl.pallas_call(functools.partial(fold_kernel, pieces, code), grid=(count,...  37.9 us
    ppermute x42, starting transfers between devices, swap(): return lax.ppermute(values, axis, [(i, i ^ mask) for i in range(count)])  29.9 us
    pallas_call x1, Pallas kernels, last_product(): pl.pallas_call(functools.partial(last_kernel, 1.0 / tokens, runs, bases,...  26.8 us
  transfers between devices with their start and end apart: 57, of which 21 were waited for; matrix products, arithmetic and copies ran while one was open for 9% of the time, Pallas kernels for 20%

profile of v3, /device:TPU:0, one launch (start us, length us, event | category | flops | bytes accessed | tf_op | source)
XLA Modules:
  0.0 612.4 jit_solution(14826275488654627131)
XLA Ops:
  4.3 19.2 %shard_map.64 = (f32[3,64,3584]{2,1,0:T(8,128)}, f32[3,64,3584]{2,1,0:T(8,128)}) custom-call(bf16[128,2048]{1,0:T(8,128)(2,1)} %copy.31.refs_0_, bf16[2048,3584]{1,0:T(8,128)(2,1)} %refs_2_.12, bf16[2048,3584]{1,0:T(8,128)(2,1)} %refs_3_.12, bf16[2048,3584]{1,0:T(8,128)(2,1)} %refs_2_.13), custom_call_target="tpu_custom_call" | custom-call | flops 5637144576 | bytes 50069504 | tf_op jit(solution)/shard_map/pallas_call | solution.py:113
  23.9 2.6 collective-permute-start
  26.5 14.7 %collective-permute-done = bf16[128,2048]{0,1:T(8,128)(2,1)} collective-permute-done((bf16[128,2048]{0,1:T(8,128)(2,1)S(1)}, bf16[128,2048]{0,1:T(8,128)(2,1)}, u32[]{:S(2)}, u32[]{:S(2)}) %collective-permute-start) | collective-permute-done | bytes 524320 | tf_op jit(solution)/shard_map/ppermute | solution.py:32
  43.3 5.0 shard_map.65
  48.3 19.2 %shard_map.67 = (f32[3,64,3584]{2,1,0:T(8,128)}, f32[3,64,3584]{2,1,0:T(8,128)}) custom-call(bf16[128,2048]{1,0:T(8,128)(2,1)} %copy.32.refs_0_, bf16[2048,3584]{1,0:T(8,128)(2,1)} %refs_2_.12, bf16[2048,3584]{1,0:T(8,128)(2,1)} %refs_3_.12, bf16[2048,3584]{1,0:T(8,128)(2,1)} %refs_2_.13, f32[3,32,3712]{2,1,0:T(8,128)} %get-tuple-element.50.refs_4_), custom_call_target="tpu_custom_call" | custom-call | flops 5637144576 | bytes 50069504 | tf_op jit(solution)/shard_map/pallas_call | solution.py:113
  73.7 8.4 %collective-permute-done.3 = bf16[128,2048]{0,1:T(8,128)(2,1)} collective-permute-done((bf16[128,2048]{0,1:T(8,128)(2,1)}, bf16[128,2048]{0,1:T(8,128)(2,1)}, u32[]{:S(2)}, u32[]{:S(2)}) %collective-permute-start.3) | collective-permute-done | bytes 524320 | tf_op jit(solution)/shard_map/ppermute | solution.py:27
  84.2 4.9 shard_map.68
  89.1 11.4 %shard_map.70 = (f32[1,128,3584]{2,1,0:T(8,128)}, f32[1,128,3584]{2,1,0:T(8,128)}) custom-call(bf16[128,2048]{1,0:T(8,128)(2,1)} %copy.33.refs_0_, bf16[128,2048]{1,0:T(8,128)(2,1)} %copy.34.refs_1_, bf16[2048,3584]{1,0:T(8,128)(2,1)} %refs_2_.13, f32[3,32,3712]{2,1,0:T(8,128)} %get-tuple-element.54.refs_3_), custom_call_target="tpu_custom_call" | custom-call | flops 3758096384 | bytes 19398656 | tf_op jit(solution)/shard_map/pallas_call | solution.py:113
  100.6 16.4 %collective-permute-done.1 = bf16[128,2048]{0,1:T(8,128)(2,1)} collective-permute-done((bf16[128,2048]{0,1:T(8,128)(2,1)}, bf16[128,2048]{0,1:T(8,128)(2,1)}, u32[]{:S(2)}, u32[]{:S(2)}) %collective-permute-start.1) | collective-permute-done | bytes 524320 | tf_op jit(solution)/shard_map/ppermute | solution.py:32
  119.1 13.6 %collective-permute-done.2 = bf16[128,2048]{0,1:T(8,128)(2,1)} collective-permute-done((bf16[128,2048]{0,1:T(8,128)(2,1)}, bf16[128,2048]{0,1:T(8,128)(2,1)}, u32[]{:S(2)}, u32[]{:S(2)}) %collective-permute-start.2) | collective-permute-done | bytes 524320 | tf_op jit(solution)/shard_map/ppermute | solution.py:32
  134.7 3.6 shard_map.71
  138.3 24.3 %shard_map.72 = (f32[3,128,3584]{2,1,0:T(8,128)}, f32[3,128,3584]{2,1,0:T(8,128)}) custom-call(bf16[128,2048]{1,0:T(8,128)(2,1)} %copy.35.refs_0_, bf16[128,2048]{1,0:T(8,128)(2,1)} %copy.36.refs_1_, bf16[2048,3584]{1,0:T(8,128)(2,1)} %refs_2_.12, bf16[2048,3584]{1,0:T(8,128)(2,1)} %refs_3_.12, bf16[2048,3584]{1,0:T(8,128)(2,1)} %refs_2_.13, ...), custom_call_target="tpu_custom_call" | custom-call | flops 11274289152 | bytes 56098816 | tf_op jit(solution)/shard_map/pallas_call | solution.py:113
  167.1 15.2 %collective-permute-done.7 = f16[3,32,3712]{2,1,0:T(8,128)(2,1)} collective-permute-done((f16[3,32,3712]{2,1,0:T(8,128)(2,1)}, f16[3,32,3712]{2,1,0:T(8,128)(2,1)}, u32[]{:S(2)}, u32[]{:S(2)}) %collective-permute-start.7) | collective-permute-done | bytes 712736 | tf_op jit(solution)/shard_map/ppermute | solution.py:27
  189.4 2.9 constant_dynamic-slice_fusion.3
  197.9 7.5 %shard_map.73 = (f32[3,64,3584]{2,1,0:T(8,128)}, f32[3,64,3712]{2,1,0:T(8,128)}) custom-call(f32[3,128,3584]{2,1,0:T(8,128)} %get-tuple-element.58.keep_ref, f32[3,128,3584]{2,1,0:T(8,128)} %collective-permute-done.16.got_ref), custom_call_target="tpu_custom_call" | custom-call | flops 2752512 | bytes 16515072 | tf_op jit(solution)/shard_map/pallas_call | solution.py:157
  213.6 26.3 %collective-permute-done.17 = f16[3,64,3712]{2,1,0:T(8,128)(2,1)S(1)} collective-permute-done((f16[3,64,3712]{2,1,0:T(8,128)(2,1)S(1)}, f16[3,64,3712]{2,1,0:T(8,128)(2,1)S(1)}, u32[]{:S(2)}, u32[]{:S(2)}) %collective-permute-start.17) | collective-permute-done | bytes 1425440 | tf_op jit(solution)/shard_map/ppermute | solution.py:27
  244.6 11.5 %shard_map.75 = (f32[1,128,3584]{2,1,0:T(8,128)}, f32[1,128,3584]{2,1,0:T(8,128)}) custom-call(bf16[128,2048]{1,0:T(8,128)(2,1)} %copy.37.refs_0_, bf16[128,2048]{1,0:T(8,128)(2,1)} %copy.38.refs_1_, bf16[2048,3584]{1,0:T(8,128)(2,1)} %refs_2_.13, f32[3,64,3712]{2,1,0:T(8,128)} %get-tuple-element.61.refs_3_), custom_call_target="tpu_custom_call" | custom-call | flops 3758096384 | bytes 19398656 | tf_op jit(solution)/shard_map/pallas_call | solution.py:113
  258.0 9.8 %shard_map.66 = f32[128,2048]{1,0:T(8,128)} custom-call(bf16[32,3584]{1,0:T(8,128)(2,1)} %copy-done.14, bf16[32,3584]{1,0:T(8,128)(2,1)} %collective-permute-done.8.refs_1_, bf16[64,3584]{1,0:T(8,128)(2,1)} %collective-permute-done.9.refs_2_, bf16[3584,2048]{1,0:T(8,128)(2,1)} %refs_2_.17), custom_call_target="tpu_custom_call" | custom-call | flops 1879048192 | bytes 16121856 | tf_op jit(solution)/shard_map/pallas_call | solution.py:213
  269.8 9.7 %shard_map.69 = bf16[128,2048]{1,0:T(8,128)(2,1)} custom-call(bf16[32,3584]{1,0:T(8,128)(2,1)} %copy-done.15, bf16[32,3584]{1,0:T(8,128)(2,1)} %copy-done.32, bf16[64,3584]{1,0:T(8,128)(2,1)} %collective-permute-done.13.refs_2_, bf16[3584,2048]{1,0:T(8,128)(2,1)} %refs_2_.17), custom_call_target="tpu_custom_call" | custom-call | flops 1879048192 | bytes 16121856 | tf_op jit(solution)/shard_map/pallas_call | solution.py:213
  281.1 11.1 %shard_map.74 = (bf16[128,2048]{1,0:T(8,128)(2,1)}, bf16[128,2048]{1,0:T(8,128)(2,1)}) custom-call(bf16[64,3584]{1,0:T(8,128)(2,1)} %copy-done.9, bf16[64,3584]{1,0:T(8,128)(2,1)} %copy-done.19, bf16[128,3584]{1,0:T(8,128)(2,1)} %collective-permute-done.19.refs_2_, bf16[3584,2048]{1,0:T(8,128)(2,1)} %refs_2_.17), custom_call_target="tpu_custom_call" | custom-call | flops 3758096384 | bytes 17563648 | tf_op jit(solution)/shard_map/pallas_call | solution.py:213
  296.2 3.7 shard_map.76
  301.9 27.7 %collective-permute-done.20 = bf16[128,2048]{1,0:T(8,128)(2,1)} collective-permute-done((bf16[128,2048]{1,0:T(8,128)(2,1)}, bf16[128,2048]{1,0:T(8,128)(2,1)}, u32[]{:S(2)}, u32[]{:S(2)}) %collective-permute-start.20) | collective-permute-done | bytes 524320 | tf_op jit(solution)/shard_map/ppermute | solution.py:32
  329.6 2.1 fusion.refs_0_
  334.5 12.3 %collective-permute-done.22.refs_1_ = bf16[128,2048]{1,0:T(8,128)(2,1)} collective-permute-done((bf16[128,2048]{1,0:T(8,128)(2,1)S(1)}, bf16[128,2048]{1,0:T(8,128)(2,1)}, u32[]{:S(2)}, u32[]{:S(2)}) %collective-permute-start.22) | collective-permute-done | bytes 524320 | tf_op jit(solution)/shard_map/ppermute | solution.py:32
  346.8 11.2 %shard_map.77 = (f32[1,128,3584]{2,1,0:T(8,128)}, f32[1,128,3584]{2,1,0:T(8,128)}) custom-call(bf16[128,2048]{1,0:T(8,128)(2,1)} %copy-done.12, bf16[128,2048]{1,0:T(8,128)(2,1)} %collective-permute-done.22.refs_1_, bf16[3584,2048]{1,0:T(8,128)(2,1)} %refs_2_.17, f32[1,64,3712]{2,1,0:T(8,128)} %get-tuple-element.66.refs_3_), custom_call_target="tpu_custom_call" | custom-call | flops 3758096384 | bytes 19398656 | tf_op jit(solution)/shard_map/pallas_call | solution.py:113
  360.7 12.0 %collective-permute-done.42.refs_1_ = bf16[64,3584]{1,0:T(8,128)(2,1)S(1)} collective-permute-done((bf16[64,3584]{1,0:T(8,128)(2,1)S(1)}, bf16[64,3584]{1,0:T(8,128)(2,1)S(1)}, u32[]{:S(2)}, u32[]{:S(2)}) %collective-permute-start.42) | collective-permute-done | bytes 458784 | tf_op jit(solution)/shard_map/ppermute | solution.py:27
  373.8 3.0 collective-permute-done.28.refs_0_
  378.3 11.1 %shard_map.81 = (f32[128,2048]{1,0:T(8,128)}, bf16[128,2048]{1,0:T(8,128)(2,1)}) custom-call(bf16[64,3584]{1,0:T(8,128)(2,1)} %copy-done.7, bf16[64,3584]{1,0:T(8,128)(2,1)} %copy-done.20, bf16[128,3584]{1,0:T(8,128)(2,1)} %collective-permute-done.38.refs_2_, bf16[3584,2048]{1,0:T(8,128)(2,1)} %refs_2_.17), custom_call_target="tpu_custom_call" | custom-call | flops 3758096384 | bytes 17563648 | tf_op jit(solution)/shard_map/pallas_call | solution.py:213
  389.4 3.8 collective-permute-start.39
  393.2 3.3 shard_map.78
  396.6 11.3 %shard_map.79 = (f32[1,128,3584]{2,1,0:T(8,128)}, f32[1,128,3584]{2,1,0:T(8,128)}) custom-call(bf16[128,2048]{1,0:T(8,128)(2,1)} %copy-done.40, bf16[128,2048]{1,0:T(8,128)(2,1)} %collective-permute-done.29.refs_1_, bf16[3584,2048]{1,0:T(8,128)(2,1)} %refs_2_.17, bf16[1,64,3584]{2,1,0:T(8,128)(2,1)} %get-tuple-element.70.refs_3_, ...), custom_call_target="tpu_custom_call" | custom-call | flops 3758096384 | bytes 19398656 | tf_op jit(solution)/shard_map/pallas_call | solution.py:113
  408.0 11.2 %shard_map.82 = (bf16[128,2048]{1,0:T(8,128)(2,1)}, bf16[128,2048]{1,0:T(8,128)(2,1)}) custom-call(bf16[64,3584]{1,0:T(8,128)(2,1)} %copy-done.8, bf16[64,3584]{1,0:T(8,128)(2,1)} %copy-done.21, bf16[128,3584]{1,0:T(8,128)(2,1)} %collective-permute-done.43.refs_2_, bf16[3584,2048]{1,0:T(8,128)(2,1)} %refs_2_.17), custom_call_target="tpu_custom_call" | custom-call | flops 3758096384 | bytes 17563648 | tf_op jit(solution)/shard_map/pallas_call | solution.py:213
  419.7 34.9 %collective-permute-done.44 = bf16[128,2048]{1,0:T(8,128)(2,1)S(1)} collective-permute-done((bf16[128,2048]{1,0:T(8,128)(2,1)}, bf16[128,2048]{1,0:T(8,128)(2,1)S(1)}, u32[]{:S(2)}, u32[]{:S(2)}) %collective-permute-start.44) | collective-permute-done | bytes 524320 | tf_op jit(solution)/shard_map/ppermute | solution.py:32
  456.5 3.4 shard_map.80
  459.8 12.3 %collective-permute-done.46.refs_1_ = bf16[128,2048]{1,0:T(8,128)(2,1)S(1)} collective-permute-done((bf16[128,2048]{1,0:T(8,128)(2,1)S(1)}, bf16[128,2048]{1,0:T(8,128)(2,1)S(1)}, u32[]{:S(2)}, u32[]{:S(2)}) %collective-permute-start.46) | collective-permute-done | bytes 524320 | tf_op jit(solution)/shard_map/ppermute | solution.py:32
  473.0 11.2 %shard_map.83 = (f32[1,128,3584]{2,1,0:T(8,128)}, f32[1,128,3584]{2,1,0:T(8,128)}) custom-call(bf16[128,2048]{1,0:T(8,128)(2,1)} %copy-done.13, bf16[128,2048]{1,0:T(8,128)(2,1)} %copy-done.43, bf16[3584,2048]{1,0:T(8,128)(2,1)} %refs_2_.17, bf16[1,64,3584]{2,1,0:T(8,128)(2,1)} %get-tuple-element.74.refs_3_, bf16[2048,128]{1,0:T(8,128)(2,1)} %bitcast.2.refs_4_.refs_2_, ...), custom_call_target="tpu_custom_call" | custom-call | flops 3758096384 | bytes 19398656 | tf_op jit(solution)/shard_map/pallas_call | solution.py:113
  487.5 13.2 %collective-permute-done.51.refs_0_ = bf16[128,2048]{1,0:T(8,128)(2,1)S(1)} collective-permute-done((bf16[128,2048]{1,0:T(8,128)(2,1)}, bf16[128,2048]{1,0:T(8,128)(2,1)S(1)}, u32[]{:S(2)}, u32[]{:S(2)}) %collective-permute-start.51) | collective-permute-done | bytes 524320 | tf_op jit(solution)/shard_map/ppermute | solution.py:32
  502.9 3.3 shard_map.84
  506.2 9.7 %collective-permute-done.52.refs_1_ = bf16[128,2048]{1,0:T(8,128)(2,1)S(1)} collective-permute-done((bf16[128,2048]{1,0:T(8,128)(2,1)S(1)}, bf16[128,2048]{1,0:T(8,128)(2,1)S(1)}, u32[]{:S(2)}, u32[]{:S(2)}) %collective-permute-start.52) | collective-permute-done | bytes 524320 | tf_op jit(solution)/shard_map/ppermute | solution.py:32
  516.8 11.3 %shard_map.85 = (f32[1,128,3584]{2,1,0:T(8,128)}, f32[1,128,3584]{2,1,0:T(8,128)}) custom-call(bf16[128,2048]{1,0:T(8,128)(2,1)} %copy-done.41, bf16[128,2048]{1,0:T(8,128)(2,1)} %copy-done.42, bf16[3584,2048]{1,0:T(8,128)(2,1)} %refs_2_.17, bf16[1,64,3584]{2,1,0:T(8,128)(2,1)} %get-tuple-element.84.refs_3_, bf16[2048,128]{1,0:T(8,128)(2,1)} %fusion.20.refs_4_, ...), custom_call_target="tpu_custom_call" | custom-call | flops 3758096384 | bytes 19398656 | tf_op jit(solution)/shard_map/pallas_call | solution.py:113
  533.0 9.9 %collective-permute-done.32.refs_12_ = bf16[64,3584]{1,0:T(8,128)(2,1)S(1)} collective-permute-done((bf16[64,3584]{1,0:T(8,128)(2,1)S(1)}, bf16[64,3584]{1,0:T(8,128)(2,1)S(1)}, u32[]{:S(2)}, u32[]{:S(2)}) %collective-permute-start.32) | collective-permute-done | bytes 458784 | tf_op jit(solution)/shard_map/ppermute | solution.py:27
  545.3 3.3 shard_map.86
  550.1 2.6 collective-permute-done.48
  556.5 6.1 collective-permute-done.54
  564.3 8.1 %collective-permute-done.49.refs_15_ = bf16[64,3584]{1,0:T(8,128)(2,1)S(1)} collective-permute-done((bf16[64,3584]{1,0:T(8,128)(2,1)S(1)}, bf16[64,3584]{1,0:T(8,128)(2,1)S(1)}, u32[]{:S(2)}, u32[]{:S(2)}) %collective-permute-start.49) | collective-permute-done | bytes 458784 | tf_op jit(solution)/shard_map/ppermute | solution.py:27
  572.6 9.3 %collective-permute-done.55.refs_18_ = bf16[64,3584]{1,0:T(8,128)(2,1)S(1)} collective-permute-done((bf16[64,3584]{1,0:T(8,128)(2,1)S(1)}, bf16[64,3584]{1,0:T(8,128)(2,1)S(1)}, u32[]{:S(2)}, u32[]{:S(2)}) %collective-permute-start.55) | collective-permute-done | bytes 458784 | tf_op jit(solution)/shard_map/ppermute | solution.py:27
  582.0 2.4 collective-permute-done.56.refs_19_
  585.4 26.8 %shard_map.87 = f32[2048,3584]{1,0:T(8,128)} custom-call(bf16[2048,128]{1,0:T(8,128)(2,1)} %fusion.21.refs_4_.refs_0_, bf16[2048,128]{1,0:T(8,128)(2,1)} %bitcast.1.refs_5_.refs_1_, bf16[2048,128]{1,0:T(8,128)(2,1)} %bitcast.2.refs_4_.refs_2_, bf16[2048,128]{1,0:T(8,128)(2,1)} %bitcast.3.refs_5_.refs_3_, bf16[2048,128]{1,0:T(8,128)(2,1)} %fusion.20.refs_4_, ...), custom_call_target="tpu_custom_call" | custom-call | flops 15032385536 | bytes 40894464 | tf_op jit(solution)/shard_map/pallas_call | solution.py:261
  (249 shorter events, 93.5 us)
Async XLA Ops:
  23.5 19.8 %collective-permute-start.6 = (f32[3,64,3584]{2,1,0:T(8,128)}, f32[3,64,3584]{2,1,0:T(8,128)}, u32[]{:S(2)}, u32[]{:S(2)}) collective-permute-start(f32[3,64,3584]{2,1,0:T(8,128)} %get-tuple-element.48), channel_id=1, source_target_pairs={{0,1},{1,0},{2,3},{3,2},{4,5},{5,4},{6,7},{7,6},{8,9},{9,8},{10,11... | collective-permute-start | bytes 8257544 | tf_op jit(solution)/shard_map/ppermute | solution.py:27
  23.9 17.3 %collective-permute-start = (bf16[128,2048]{0,1:T(8,128)(2,1)S(1)}, bf16[128,2048]{0,1:T(8,128)(2,1)}, u32[]{:S(2)}, u32[]{:S(2)}) collective-permute-start(bf16[128,2048]{0,1:T(8,128)(2,1)S(1)} %pad_maximum_fusion.7), channel_id=1, source_target_pairs={{0,4},{4,8},{8,12},{12,0},{1,5},{5,9},{9,13},{13,1},{2,6},{6,10},{... | collective-permute-start | bytes 1572872 | tf_op jit(solution)/shard_map/ppermute | solution.py:32
  67.5 16.7 %collective-permute-start.10 = (f32[3,64,3584]{2,1,0:T(8,128)}, f32[3,64,3584]{2,1,0:T(8,128)}, u32[]{:S(2)}, u32[]{:S(2)}) collective-permute-start(f32[3,64,3584]{2,1,0:T(8,128)} %get-tuple-element.52), channel_id=1, source_target_pairs={{0,1},{1,0},{2,3},{3,2},{4,5},{5,4},{6,7},{7,6},{8,9},{9,8},{10,11... | collective-permute-start | bytes 8257544 | tf_op jit(solution)/shard_map/ppermute | solution.py:27
  100.6 34.2 %collective-permute-start.15 = (f32[1,128,3584]{2,1,0:T(8,128)}, f32[1,128,3584]{2,1,0:T(8,128)}, u32[]{:S(2)}, u32[]{:S(2)}) collective-permute-start(f32[1,128,3584]{2,1,0:T(8,128)} %get-tuple-element.56), channel_id=1, source_target_pairs={{0,1},{1,0},{2,3},{3,2},{4,5},{5,4},{6,7},{7,6},{8,9},{9,8},{10,11... | collective-permute-start | bytes 5505032 | tf_op jit(solution)/shard_map/ppermute | solution.py:27
  100.6 16.4 %collective-permute-start.1 = (bf16[128,2048]{0,1:T(8,128)(2,1)}, bf16[128,2048]{0,1:T(8,128)(2,1)}, u32[]{:S(2)}, u32[]{:S(2)}) collective-permute-start(bf16[128,2048]{0,1:T(8,128)(2,1)} %collective-permute-done), channel_id=1, source_target_pairs={{0,4},{4,8},{8,12},{12,0},{1,5},{5,9},{9,13},{13,1},{2,6},{6,10},{... | collective-permute-start | bytes 1572872 | tf_op jit(solution)/shard_map/ppermute | solution.py:32
  117.0 15.7 %collective-permute-start.2 = (bf16[128,2048]{0,1:T(8,128)(2,1)}, bf16[128,2048]{0,1:T(8,128)(2,1)}, u32[]{:S(2)}, u32[]{:S(2)}) collective-permute-start(bf16[128,2048]{0,1:T(8,128)(2,1)} %collective-permute-done.1), channel_id=1, source_target_pairs={{0,4},{4,8},{8,12},{12,0},{1,5},{5,9},{9,13},{13,1},{2,6},{6,10},{... | collective-permute-start | bytes 1572872 | tf_op jit(solution)/shard_map/ppermute | solution.py:32
  162.6 35.3 %collective-permute-start.16 = (f32[3,128,3584]{2,1,0:T(8,128)}, f32[3,128,3584]{2,1,0:T(8,128)}, u32[]{:S(2)}, u32[]{:S(2)}) collective-permute-start(f32[3,128,3584]{2,1,0:T(8,128)} %get-tuple-element.59), channel_id=1, source_target_pairs={{0,1},{1,0},{2,3},{3,2},{4,5},{5,4},{6,7},{7,6},{8,9},{9,8},{10,11... | collective-permute-start | bytes 16515080 | tf_op jit(solution)/shard_map/ppermute | solution.py:27
  163.6 18.7 %collective-permute-start.7 = (f16[3,32,3712]{2,1,0:T(8,128)(2,1)}, f16[3,32,3712]{2,1,0:T(8,128)(2,1)}, u32[]{:S(2)}, u32[]{:S(2)}) collective-permute-start(f16[3,32,3712]{2,1,0:T(8,128)(2,1)} %convert_element_type.113), channel_id=1, source_target_pairs={{0,2},{1,3},{2,0},{3,1},{4,6},{5,7},{6,4},{7,5},{8,10},{9,11},{10,... | collective-permute-start | bytes 2138120 | tf_op jit(solution)/shard_map/ppermute | solution.py:27
  165.1 27.2 %collective-permute-start.4 = (bf16[128,2048]{0,1:T(8,128)(2,1)}, bf16[128,2048]{0,1:T(8,128)(2,1)}, u32[]{:S(2)}, u32[]{:S(2)}) collective-permute-start(bf16[128,2048]{0,1:T(8,128)(2,1)} %collective-permute-done.1), channel_id=1, source_target_pairs={{0,16},{16,0},{1,17},{17,1},{2,18},{18,2},{3,19},{19,3},{4,20},{20... | collective-permute-start | bytes 1572872 | tf_op jit(solution)/shard_map/ppermute | solution.py:27
  166.6 27.8 %collective-permute-start.5 = (bf16[128,2048]{0,1:T(8,128)(2,1)}, bf16[128,2048]{0,1:T(8,128)(2,1)}, u32[]{:S(2)}, u32[]{:S(2)}) collective-permute-start(bf16[128,2048]{0,1:T(8,128)(2,1)} %collective-permute-done.2), channel_id=1, source_target_pairs={{0,16},{16,0},{1,17},{17,1},{2,18},{18,2},{3,19},{19,3},{4,20},{20... | collective-permute-start | bytes 1572872 | tf_op jit(solution)/shard_map/ppermute | solution.py:27
  186.4 22.6 %collective-permute-start.8 = (bf16[32,3584]{1,0:T(8,128)(2,1)S(1)}, bf16[32,3584]{1,0:T(8,128)(2,1)}, u32[]{:S(2)}, u32[]{:S(2)}) collective-permute-start(bf16[32,3584]{1,0:T(8,128)(2,1)S(1)} %get-tuple-element.111.refs_0_), channel_id=1, source_target_pairs={{0,2},{1,3},{2,0},{3,1},{4,6},{5,7},{6,4},{7,5},{8,10},{9,11},{10,... | collective-permute-start | bytes 688136 | tf_op jit(solution)/shard_map/ppermute | solution.py:27
  188.8 21.9 %collective-permute-start.11 = (f16[3,32,3712]{2,1,0:T(8,128)(2,1)}, f16[3,32,3712]{2,1,0:T(8,128)(2,1)}, u32[]{:S(2)}, u32[]{:S(2)}) collective-permute-start(f16[3,32,3712]{2,1,0:T(8,128)(2,1)} %convert_element_type.116), channel_id=1, source_target_pairs={{0,2},{1,3},{2,0},{3,1},{4,6},{5,7},{6,4},{7,5},{8,10},{9,11},{10,... | collective-permute-start | bytes 2138120 | tf_op jit(solution)/shard_map/ppermute | solution.py:27
  196.4 61.6 %collective-permute-start.34 = (f32[32,3584]{1,0:T(8,128)}, f32[32,3584]{1,0:T(8,128)S(1)}, u32[]{:S(2)}, u32[]{:S(2)}) collective-permute-start(f32[32,3584]{1,0:T(8,128)} %get-tuple-element.112), channel_id=1, source_target_pairs={{0,16},{16,0},{1,17},{17,1},{2,18},{18,2},{3,19},{19,3},{4,20},{20... | collective-permute-start | bytes 1376264 | tf_op jit(solution)/shard_map/ppermute | solution.py:27
  207.5 32.3 %collective-permute-start.17 = (f16[3,64,3712]{2,1,0:T(8,128)(2,1)S(1)}, f16[3,64,3712]{2,1,0:T(8,128)(2,1)S(1)}, u32[]{:S(2)}, u32[]{:S(2)}) collective-permute-start(f16[3,64,3712]{2,1,0:T(8,128)(2,1)S(1)} %convert_element_type.120), channel_id=1, source_target_pairs={{0,2},{1,3},{2,0},{3,1},{4,6},{5,7},{6,4},{7,5},{8,10},{9,11},{10,... | collective-permute-start | bytes 4276232 | tf_op jit(solution)/shard_map/ppermute | solution.py:27
  210.8 47.3 %collective-permute-start.9 = (bf16[64,3584]{1,0:T(8,128)(2,1)}, bf16[64,3584]{1,0:T(8,128)(2,1)}, u32[]{:S(2)}, u32[]{:S(2)}) collective-permute-start(bf16[64,3584]{1,0:T(8,128)(2,1)} %pad_maximum_fusion.9), channel_id=1, source_target_pairs={{0,1},{1,0},{2,3},{3,2},{4,5},{5,4},{6,7},{7,6},{8,9},{9,8},{10,11... | collective-permute-start | bytes 1376264 | tf_op jit(solution)/shard_map/ppermute | solution.py:27
  256.1 40.1 %collective-permute-start.23 = (f32[1,128,3584]{2,1,0:T(8,128)}, f32[1,128,3584]{2,1,0:T(8,128)}, u32[]{:S(2)}, u32[]{:S(2)}) collective-permute-start(f32[1,128,3584]{2,1,0:T(8,128)} %get-tuple-element.65), channel_id=1, source_target_pairs={{0,1},{1,0},{2,3},{3,2},{4,5},{5,4},{6,7},{7,6},{8,9},{9,8},{10,11... | collective-permute-start | bytes 5505032 | tf_op jit(solution)/shard_map/ppermute | solution.py:27
  257.3 23.8 %collective-permute-start.19 = (bf16[128,3584]{1,0:T(8,128)(2,1)}, bf16[128,3584]{1,0:T(8,128)(2,1)}, u32[]{:S(2)}, u32[]{:S(2)}) collective-permute-start(bf16[128,3584]{1,0:T(8,128)(2,1)} %pad_maximum_fusion), channel_id=1, source_target_pairs={{0,1},{1,0},{2,3},{3,2},{4,5},{5,4},{6,7},{7,6},{8,9},{9,8},{10,11... | collective-permute-start | bytes 2752520 | tf_op jit(solution)/shard_map/ppermute | solution.py:27
  267.9 24.3 %collective-permute-start.35 = (f32[32,3584]{1,0:T(8,128)S(1)}, f32[32,3584]{1,0:T(8,128)}, u32[]{:S(2)}, u32[]{:S(2)}) collective-permute-start(f32[32,3584]{1,0:T(8,128)S(1)} %get-tuple-element.110), channel_id=1, source_target_pairs={{0,16},{16,0},{1,17},{17,1},{2,18},{18,2},{3,19},{19,3},{4,20},{20... | collective-permute-start | bytes 1376264 | tf_op jit(solution)/shard_map/ppermute | solution.py:27
  279.5 22.4 %collective-permute-start.14 = (bf16[128,2048]{1,0:T(8,128)(2,1)}, bf16[128,2048]{1,0:T(8,128)(2,1)}, u32[]{:S(2)}, u32[]{:S(2)}) collective-permute-start(bf16[128,2048]{1,0:T(8,128)(2,1)} %shard_map.69), channel_id=1, source_target_pairs={{0,12},{4,0},{8,4},{12,8},{1,13},{5,1},{9,5},{13,9},{2,14},{6,2},{... | collective-permute-start | bytes 1572872 | tf_op jit(solution)/shard_map/ppermute | solution.py:32
  279.5 15.8 %collective-permute-start.36 = (f16[1,64,3712]{2,1,0:T(8,128)(2,1)S(1)}, f16[1,64,3712]{2,1,0:T(8,128)(2,1)S(1)}, u32[]{:S(2)}, u32[]{:S(2)}) collective-permute-start(f16[1,64,3712]{2,1,0:T(8,128)(2,1)S(1)} %convert_element_type.130), channel_id=1, source_target_pairs={{0,2},{1,3},{2,0},{3,1},{4,6},{5,7},{6,4},{7,5},{8,10},{9,11},{10,... | collective-permute-start | bytes 1425416 | tf_op jit(solution)/shard_map/ppermute | solution.py:27
  292.2 37.4 %collective-permute-start.20 = (bf16[128,2048]{1,0:T(8,128)(2,1)}, bf16[128,2048]{1,0:T(8,128)(2,1)}, u32[]{:S(2)}, u32[]{:S(2)}) collective-permute-start(bf16[128,2048]{1,0:T(8,128)(2,1)} %get-tuple-element.62), channel_id=1, source_target_pairs={{0,8},{4,12},{8,0},{12,4},{1,9},{5,13},{9,1},{13,5},{2,10},{6,14},... | collective-permute-start | bytes 1572872 | tf_op jit(solution)/shard_map/ppermute | solution.py:32
  292.2 37.4 %collective-permute-start.21 = (bf16[128,2048]{1,0:T(8,128)(2,1)}, bf16[128,2048]{1,0:T(8,128)(2,1)}, u32[]{:S(2)}, u32[]{:S(2)}) collective-permute-start(bf16[128,2048]{1,0:T(8,128)(2,1)} %get-tuple-element.63), channel_id=1, source_target_pairs={{0,4},{4,8},{8,12},{12,0},{1,5},{5,9},{9,13},{13,1},{2,6},{6,10},{... | collective-permute-start | bytes 1572872 | tf_op jit(solution)/shard_map/ppermute | solution.py:32
  296.1 61.9 %collective-permute-start.40 = (f32[64,3584]{1,0:T(8,128)}, f32[64,3584]{1,0:T(8,128)S(1)}, u32[]{:S(2)}, u32[]{:S(2)}) collective-permute-start(f32[64,3584]{1,0:T(8,128)} %get-tuple-element.114), channel_id=1, source_target_pairs={{0,16},{16,0},{1,17},{17,1},{2,18},{18,2},{3,19},{19,3},{4,20},{20... | collective-permute-start | bytes 2752520 | tf_op jit(solution)/shard_map/ppermute | solution.py:27
  301.1 32.4 %collective-permute-start.41 = (f16[1,64,3712]{2,1,0:T(8,128)(2,1)S(1)}, f16[1,64,3712]{2,1,0:T(8,128)(2,1)S(1)}, u32[]{:S(2)}, u32[]{:S(2)}) collective-permute-start(f16[1,64,3712]{2,1,0:T(8,128)(2,1)S(1)} %convert_element_type.134), channel_id=1, source_target_pairs={{0,2},{1,3},{2,0},{3,1},{4,6},{5,7},{6,4},{7,5},{8,10},{9,11},{10,... | collective-permute-start | bytes 1425416 | tf_op jit(solution)/shard_map/ppermute | solution.py:27
  331.8 15.1 %collective-permute-start.22 = (bf16[128,2048]{1,0:T(8,128)(2,1)S(1)}, bf16[128,2048]{1,0:T(8,128)(2,1)}, u32[]{:S(2)}, u32[]{:S(2)}) collective-permute-start(bf16[128,2048]{1,0:T(8,128)(2,1)S(1)} %fusion.refs_0_), channel_id=1, source_target_pairs={{0,4},{4,8},{8,12},{12,0},{1,5},{5,9},{9,13},{13,1},{2,6},{6,10},{... | collective-permute-start | bytes 1572872 | tf_op jit(solution)/shard_map/ppermute | solution.py:32
  332.9 27.4 %collective-permute-start.37 = (bf16[64,3584]{1,0:T(8,128)(2,1)S(1)}, bf16[64,3584]{1,0:T(8,128)(2,1)S(1)}, u32[]{:S(2)}, u32[]{:S(2)}) collective-permute-start(bf16[64,3584]{1,0:T(8,128)(2,1)S(1)} %fusion.9.refs_0_), channel_id=1, source_target_pairs={{0,2},{1,3},{2,0},{3,1},{4,6},{5,7},{6,4},{7,5},{8,10},{9,11},{10,... | collective-permute-start | bytes 1376264 | tf_op jit(solution)/shard_map/ppermute | solution.py:27
  358.0 35.2 %collective-permute-start.24 = (f32[1,128,3584]{2,1,0:T(8,128)}, f32[1,128,3584]{2,1,0:T(8,128)}, u32[]{:S(2)}, u32[]{:S(2)}) collective-permute-start(f32[1,128,3584]{2,1,0:T(8,128)} %get-tuple-element.68), channel_id=1, source_target_pairs={{0,1},{1,0},{2,3},{3,2},{4,5},{5,4},{6,7},{7,6},{8,9},{9,8},{10,11... | collective-permute-start | bytes 5505032 | tf_op jit(solution)/shard_map/ppermute | solution.py:27
  360.4 17.9 %collective-permute-start.38 = (bf16[128,3584]{1,0:T(8,128)(2,1)S(1)}, bf16[128,3584]{1,0:T(8,128)(2,1)}, u32[]{:S(2)}, u32[]{:S(2)}) collective-permute-start(bf16[128,3584]{1,0:T(8,128)(2,1)S(1)} %pad_maximum_fusion.3), channel_id=1, source_target_pairs={{0,1},{1,0},{2,3},{3,2},{4,5},{5,4},{6,7},{7,6},{8,9},{9,8},{10,11... | collective-permute-start | bytes 2752520 | tf_op jit(solution)/shard_map/ppermute | solution.py:27
  360.6 16.1 %collective-permute-start.28 = (bf16[128,2048]{1,0:T(8,128)(2,1)}, bf16[128,2048]{1,0:T(8,128)(2,1)S(1)}, u32[]{:S(2)}, u32[]{:S(2)}) collective-permute-start(bf16[128,2048]{1,0:T(8,128)(2,1)} %collective-permute-done.22.refs_1_), channel_id=1, source_target_pairs={{0,4},{4,8},{8,12},{12,0},{1,5},{5,9},{9,13},{13,1},{2,6},{6,10},{... | collective-permute-start | bytes 1572872 | tf_op jit(solution)/shard_map/ppermute | solution.py:32
  373.8 34.1 %collective-permute-start.43 = (bf16[128,3584]{1,0:T(8,128)(2,1)}, bf16[128,3584]{1,0:T(8,128)(2,1)}, u32[]{:S(2)}, u32[]{:S(2)}) collective-permute-start(bf16[128,3584]{1,0:T(8,128)(2,1)} %pad_maximum_fusion.4), channel_id=1, source_target_pairs={{0,1},{1,0},{2,3},{3,2},{4,5},{5,4},{6,7},{7,6},{8,9},{9,8},{10,11... | collective-permute-start | bytes 2752520 | tf_op jit(solution)/shard_map/ppermute | solution.py:27
  376.8 19.8 %collective-permute-start.29 = (bf16[128,2048]{1,0:T(8,128)(2,1)S(1)}, bf16[128,2048]{1,0:T(8,128)(2,1)}, u32[]{:S(2)}, u32[]{:S(2)}) collective-permute-start(bf16[128,2048]{1,0:T(8,128)(2,1)S(1)} %collective-permute-done.28.refs_0_), channel_id=1, source_target_pairs={{0,4},{4,8},{8,12},{12,0},{1,5},{5,9},{9,13},{13,1},{2,6},{6,10},{... | collective-permute-start | bytes 1572872 | tf_op jit(solution)/shard_map/ppermute | solution.py:32
  389.4 30.3 %collective-permute-start.39 = (bf16[128,2048]{1,0:T(8,128)(2,1)}, bf16[128,2048]{1,0:T(8,128)(2,1)S(1)}, u32[]{:S(2)}, u32[]{:S(2)}) collective-permute-start(bf16[128,2048]{1,0:T(8,128)(2,1)} %get-tuple-element.77), channel_id=1, source_target_pairs={{0,12},{4,0},{8,4},{12,8},{1,13},{5,1},{9,5},{13,9},{2,14},{6,2},{... | collective-permute-start | bytes 1572872 | tf_op jit(solution)/shard_map/ppermute | solution.py:32
  407.9 48.6 %collective-permute-start.30 = (f32[1,128,3584]{2,1,0:T(8,128)}, f32[1,128,3584]{2,1,0:T(8,128)}, u32[]{:S(2)}, u32[]{:S(2)}) collective-permute-start(f32[1,128,3584]{2,1,0:T(8,128)} %get-tuple-element.72), channel_id=1, source_target_pairs={{0,1},{1,0},{2,3},{3,2},{4,5},{5,4},{6,7},{7,6},{8,9},{9,8},{10,11... | collective-permute-start | bytes 5505032 | tf_op jit(solution)/shard_map/ppermute | solution.py:27
  419.1 35.5 %collective-permute-start.44 = (bf16[128,2048]{1,0:T(8,128)(2,1)}, bf16[128,2048]{1,0:T(8,128)(2,1)S(1)}, u32[]{:S(2)}, u32[]{:S(2)}) collective-permute-start(bf16[128,2048]{1,0:T(8,128)(2,1)} %get-tuple-element.79), channel_id=1, source_target_pairs={{0,8},{4,12},{8,0},{12,4},{1,9},{5,13},{9,1},{13,5},{2,10},{6,14},... | collective-permute-start | bytes 1572872 | tf_op jit(solution)/shard_map/ppermute | solution.py:32
  419.1 35.5 %collective-permute-start.45 = (bf16[128,2048]{1,0:T(8,128)(2,1)}, bf16[128,2048]{1,0:T(8,128)(2,1)S(1)}, u32[]{:S(2)}, u32[]{:S(2)}) collective-permute-start(bf16[128,2048]{1,0:T(8,128)(2,1)} %get-tuple-element.80), channel_id=1, source_target_pairs={{0,4},{4,8},{8,12},{12,0},{1,5},{5,9},{9,13},{13,1},{2,6},{6,10},{... | collective-permute-start | bytes 1572872 | tf_op jit(solution)/shard_map/ppermute | solution.py:32
  456.4 15.7 %collective-permute-start.46 = (bf16[128,2048]{1,0:T(8,128)(2,1)S(1)}, bf16[128,2048]{1,0:T(8,128)(2,1)S(1)}, u32[]{:S(2)}, u32[]{:S(2)}) collective-permute-start(bf16[128,2048]{1,0:T(8,128)(2,1)S(1)} %fusion.1.refs_0_), channel_id=1, source_target_pairs={{0,4},{4,8},{8,12},{12,0},{1,5},{5,9},{9,13},{13,1},{2,6},{6,10},{... | collective-permute-start | bytes 1572872 | tf_op jit(solution)/shard_map/ppermute | solution.py:32
  484.2 18.7 %collective-permute-start.47 = (f32[1,128,3584]{2,1,0:T(8,128)}, f32[1,128,3584]{2,1,0:T(8,128)}, u32[]{:S(2)}, u32[]{:S(2)}) collective-permute-start(f32[1,128,3584]{2,1,0:T(8,128)} %get-tuple-element.82), channel_id=1, source_target_pairs={{0,1},{1,0},{2,3},{3,2},{4,5},{5,4},{6,7},{7,6},{8,9},{9,8},{10,11... | collective-permute-start | bytes 5505032 | tf_op jit(solution)/shard_map/ppermute | solution.py:27
  484.3 16.3 %collective-permute-start.51 = (bf16[128,2048]{1,0:T(8,128)(2,1)}, bf16[128,2048]{1,0:T(8,128)(2,1)S(1)}, u32[]{:S(2)}, u32[]{:S(2)}) collective-permute-start(bf16[128,2048]{1,0:T(8,128)(2,1)} %copy-done.43), channel_id=1, source_target_pairs={{0,4},{4,8},{8,12},{12,0},{1,5},{5,9},{9,13},{13,1},{2,6},{6,10},{... | collective-permute-start | bytes 1572872 | tf_op jit(solution)/shard_map/ppermute | solution.py:32
  484.4 17.8 %collective-permute-start.25 = (bf16[1,64,3584]{2,1,0:T(8,128)(2,1)}, bf16[1,64,3584]{2,1,0:T(8,128)(2,1)S(1)}, u32[]{:S(2)}, u32[]{:S(2)}) collective-permute-start(bf16[1,64,3584]{2,1,0:T(8,128)(2,1)} %get-tuple-element.70.refs_3_), channel_id=1, source_target_pairs={{0,2},{1,3},{2,0},{3,1},{4,6},{5,7},{6,4},{7,5},{8,10},{9,11},{10,... | collective-permute-start | bytes 1376264 | tf_op jit(solution)/shard_map/ppermute | solution.py:27
  500.7 15.3 %collective-permute-start.52 = (bf16[128,2048]{1,0:T(8,128)(2,1)S(1)}, bf16[128,2048]{1,0:T(8,128)(2,1)S(1)}, u32[]{:S(2)}, u32[]{:S(2)}) collective-permute-start(bf16[128,2048]{1,0:T(8,128)(2,1)S(1)} %collective-permute-done.51.refs_0_), channel_id=1, source_target_pairs={{0,4},{4,8},{8,12},{12,0},{1,5},{5,9},{9,13},{13,1},{2,6},{6,10},{... | collective-permute-start | bytes 1572872 | tf_op jit(solution)/shard_map/ppermute | solution.py:32
  500.7 27.4 %collective-permute-start.31 = (bf16[1,64,3584]{2,1,0:T(8,128)(2,1)}, bf16[1,64,3584]{2,1,0:T(8,128)(2,1)}, u32[]{:S(2)}, u32[]{:S(2)}) collective-permute-start(bf16[1,64,3584]{2,1,0:T(8,128)(2,1)} %get-tuple-element.74.refs_3_), channel_id=1, source_target_pairs={{0,2},{1,3},{2,0},{3,1},{4,6},{5,7},{6,4},{7,5},{8,10},{9,11},{10,... | collective-permute-start | bytes 1376264 | tf_op jit(solution)/shard_map/ppermute | solution.py:27
  502.3 28.7 %collective-permute-start.26 = (bf16[64,3584]{1,0:T(8,128)(2,1)S(1)}, bf16[64,3584]{1,0:T(8,128)(2,1)}, u32[]{:S(2)}, u32[]{:S(2)}) collective-permute-start(bf16[64,3584]{1,0:T(8,128)(2,1)S(1)} %fusion.5.refs_8_), channel_id=1, source_target_pairs={{0,2},{1,3},{2,0},{3,1},{4,6},{5,7},{6,4},{7,5},{8,10},{9,11},{10,... | collective-permute-start | bytes 1376264 | tf_op jit(solution)/shard_map/ppermute | solution.py:27
  528.1 16.0 %collective-permute-start.53 = (f32[1,128,3584]{2,1,0:T(8,128)}, f32[1,128,3584]{2,1,0:T(8,128)S(1)}, u32[]{:S(2)}, u32[]{:S(2)}) collective-permute-start(f32[1,128,3584]{2,1,0:T(8,128)} %get-tuple-element.86), channel_id=1, source_target_pairs={{0,1},{1,0},{2,3},{3,2},{4,5},{5,4},{6,7},{7,6},{8,9},{9,8},{10,11... | collective-permute-start | bytes 5505032 | tf_op jit(solution)/shard_map/ppermute | solution.py:27
  532.2 49.8 %collective-permute-start.27 = (bf16[128,3584]{1,0:T(8,128)(2,1)S(1)}, bf16[128,3584]{1,0:T(8,128)(2,1)}, u32[]{:S(2)}, u32[]{:S(2)}) collective-permute-start(bf16[128,3584]{1,0:T(8,128)(2,1)S(1)} %pad_maximum_fusion.1), channel_id=1, source_target_pairs={{0,1},{1,0},{2,3},{3,2},{4,5},{5,4},{6,7},{7,6},{8,9},{9,8},{10,11... | collective-permute-start | bytes 2752520 | tf_op jit(solution)/shard_map/ppermute | solution.py:27
  532.5 20.3 %collective-permute-start.48 = (bf16[1,64,3584]{2,1,0:T(8,128)(2,1)}, bf16[1,64,3584]{2,1,0:T(8,128)(2,1)S(1)}, u32[]{:S(2)}, u32[]{:S(2)}) collective-permute-start(bf16[1,64,3584]{2,1,0:T(8,128)(2,1)} %get-tuple-element.84.refs_3_), channel_id=1, source_target_pairs={{0,2},{1,3},{2,0},{3,1},{4,6},{5,7},{6,4},{7,5},{8,10},{9,11},{10,... | collective-permute-start | bytes 1376264 | tf_op jit(solution)/shard_map/ppermute | solution.py:27
  544.1 37.9 %collective-permute-start.33 = (bf16[128,3584]{1,0:T(8,128)(2,1)}, bf16[128,3584]{1,0:T(8,128)(2,1)}, u32[]{:S(2)}, u32[]{:S(2)}) collective-permute-start(bf16[128,3584]{1,0:T(8,128)(2,1)} %pad_maximum_fusion.2), channel_id=1, source_target_pairs={{0,1},{1,0},{2,3},{3,2},{4,5},{5,4},{6,7},{7,6},{8,9},{9,8},{10,11... | collective-permute-start | bytes 2752520 | tf_op jit(solution)/shard_map/ppermute | solution.py:27
  554.9 17.5 %collective-permute-start.49 = (bf16[64,3584]{1,0:T(8,128)(2,1)S(1)}, bf16[64,3584]{1,0:T(8,128)(2,1)S(1)}, u32[]{:S(2)}, u32[]{:S(2)}) collective-permute-start(bf16[64,3584]{1,0:T(8,128)(2,1)S(1)} %fusion.7.refs_14_), channel_id=1, source_target_pairs={{0,2},{1,3},{2,0},{3,1},{4,6},{5,7},{6,4},{7,5},{8,10},{9,11},{10,... | collective-permute-start | bytes 1376264 | tf_op jit(solution)/shard_map/ppermute | solution.py:27
  562.7 19.1 %collective-permute-start.55 = (bf16[64,3584]{1,0:T(8,128)(2,1)S(1)}, bf16[64,3584]{1,0:T(8,128)(2,1)S(1)}, u32[]{:S(2)}, u32[]{:S(2)}) collective-permute-start(bf16[64,3584]{1,0:T(8,128)(2,1)S(1)} %fusion.6.refs_17_), channel_id=1, source_target_pairs={{0,2},{1,3},{2,0},{3,1},{4,6},{5,7},{6,4},{7,5},{8,10},{9,11},{10,... | collective-permute-start | bytes 1376264 | tf_op jit(solution)/shard_map/ppermute | solution.py:27
  (60 other events, 841.0 us)

commit v4 on v1

v4 whole, which is shorter than its diff:
```python
import functools

import jax
import jax.numpy as jnp
from jax import lax
from jax.experimental import pallas as pl
from jax.experimental.pallas import tpu as pltpu
from jax.sharding import PartitionSpec as P

TOP_BITS = 14
LEAST_TOP = 1e-30
FACTORS = 4
LANES = 128
GROUPS = 2


def matmul(left, right):
    return jnp.dot(left, right, preferred_element_type=jnp.float32)


def times_down(left, w_down):
    return lax.dot_general(
        left, w_down, (((1,), (1,)), ((), ())), preferred_element_type=jnp.float32
    )


def slot_masks(count):
    bits = count.bit_length() - 1
    assert 1 << bits == count
    return [sum(((s >> b) & 1) << (bits - 1 - b) for b in range(bits)) for s in range(count)]


def swap(values, axis, mask):
    count = lax.axis_size(axis)
    return lax.ppermute(values, axis, [(i, i ^ mask) for i in range(count)])


def shift(values, axis, by=1):
    count = lax.axis_size(axis)
    return lax.ppermute(values, axis, [(i, (i + by) % count) for i in range(count)])


def coded(values):
    top = jnp.max(jnp.abs(values), axis=-1, keepdims=True)
    power = jnp.ceil(jnp.log2(jnp.maximum(top, LEAST_TOP))) - TOP_BITS
    factors, left = [], power
    for _ in range(FACTORS):
        factors.append(jnp.clip(left, -14.0, 15.0))
        left = left - factors[-1]
    shape = (*values.shape[:-1], LANES // FACTORS)
    marks = [jnp.broadcast_to(jnp.exp2(factor), shape) for factor in factors]
    body = values * jnp.exp2(left - power)
    return jnp.concatenate([body, *marks], axis=-1).astype(jnp.float16)


def decoded(code):
    width = code.shape[-1] - LANES
    values = code[..., :width].astype(jnp.float32)
    for i in range(FACTORS):
        at = width + i * (LANES // FACTORS)
        values = values * code[..., at : at + 1].astype(jnp.float32)
    return values


def tie(values, after):
    return lax.optimization_barrier((values, *after))[0] if after else values


def last_kernel(scale, parts, *refs):
    turned, bars, out_ref = refs[:parts], refs[parts : 2 * parts], refs[2 * parts]
    height = out_ref.shape[0]
    step = 512 if height % 512 == 0 else height

    @pl.loop(0, height // step)
    def _(at):
        rows = pl.ds(pl.multiple_of(at * step, step), step)
        total = jnp.dot(turned[0][rows, :], bars[0][...], preferred_element_type=jnp.float32)
        for left, right in zip(turned[1:], bars[1:]):
            total += jnp.dot(left[rows, :], right[...], preferred_element_type=jnp.float32)
        out_ref[rows, :] = total * scale


def last_product(turned, bars, tokens):
    features, hidden = turned[0].shape[0], bars[0].shape[1]
    tile = 512 if hidden % 512 == 0 else hidden
    depth = sum(t.shape[1] for t in turned)
    return pl.pallas_call(
        functools.partial(last_kernel, 1.0 / tokens, len(turned)),
        grid=(hidden // tile,),
        out_shape=jax.ShapeDtypeStruct((features, hidden), jnp.float32),
        in_specs=[pl.BlockSpec(t.shape, lambda j: (0, 0)) for t in turned]
        + [pl.BlockSpec((b.shape[0], tile), lambda j: (0, j)) for b in bars],
        out_specs=pl.BlockSpec((features, tile), lambda j: (0, j)),
        compiler_params=pltpu.CompilerParams(vmem_limit_bytes=40 * 1024 * 1024),
        cost_estimate=pl.CostEstimate(
            flops=2 * features * hidden * depth,
            bytes_accessed=features * hidden * 4 + depth * (features + hidden) * 2,
            transcendentals=0,
        ),
    )(*turned, *bars)


def per_device(inputs, w_gate, w_up, w_down, query, curvature):
    ring, count = lax.axis_size("row"), lax.axis_size("col")
    assert lax.axis_size("grp") == 2 and ring % GROUPS == 0 and count >= 4
    shard, width = inputs.shape
    tokens = shard * ring
    rows = shard // 2 // count
    per_group = ring // GROUPS
    masks = slot_masks(count)
    place, grp, me = lax.axis_index("col"), lax.axis_index("grp"), lax.axis_index("row")

    def own_rows(array, start, half):
        begin = start + half * (shard // 2)
        return jnp.stack(
            [
                lax.dynamic_slice_in_dim(array, begin + (place ^ mask) * rows, rows, 0)
                for mask in masks
            ]
        )

    def joined(pieces, j):
        return jnp.concatenate(pieces[j * per_group : (j + 1) * per_group], axis=1).reshape(
            count * per_group * rows, width
        )

    halves = (grp, 1 - grp)
    acts = [[own_rows(inputs, 0, half)] for half in halves]
    for k in range(1, per_group):
        acts[0].append(shift(acts[0][-1], "row"))
        acts[1].append(swap(acts[0][-1], "grp", 1))

    def fetch(j, after):
        acts[0].append(shift(acts[0][-1], "row"))
        for _ in range(1, per_group):
            acts[0].append(shift(tie(acts[0][-1], after), "row"))
        for piece in acts[0][-per_group:]:
            acts[1].append(swap(tie(piece, after), "grp", 1))

    def sum_over_col(parts, code):
        part, mask, marks = None, 1, []
        while mask < count:
            if part is None:
                half = parts[0].shape[0] // 2
                marks.append(jnp.stack([p[half:] for p in parts]))
                got = swap(marks[-1], "col", mask)
                halves_of = [
                    jnp.stack([p[at : at + half // 2] for p in parts])
                    + got[:, at : at + half // 2]
                    for at in (0, half // 2)
                ]
            else:
                half = part.shape[1] // 2
                halves_of = [part[:, :half], part[:, half:]]
            part, give = halves_of
            mask *= 2
            marks.append(coded(give) if code else give.astype(jnp.bfloat16))
            got = swap(marks[-1], "col", mask)
            part = part + (decoded(got) if code else got.astype(jnp.float32))
            if mask * 2 >= count:
                return part, marks

    def gather_over_col(values):
        mask = count // 2
        while mask >= 1:
            values = jnp.concatenate([values, swap(values, "col", mask)], axis=0)
            mask //= 2
        return values

    gains = [[None] * GROUPS, [None] * GROUPS]
    totals = [[], []]

    def project(half, j, after):
        x = joined([tie(piece, after) for piece in acts[half]], j)
        weights = [w_gate, w_up, query] if half == 0 else [query]
        return sum_over_col([matmul(x, w) for w in weights], True)

    def hidden(half, j, own):
        if half == 0:
            gate_out, up_out = own[0], own[1]
            sigmas = jax.nn.sigmoid(gate_out)
            gains[0][j] = sigmas * (1.0 + gate_out * (1.0 - sigmas)) * up_out
            gains[1][j] = swap(gains[0][j], "grp", 1)
        return (gains[half][j] * own[-1]).astype(jnp.bfloat16)

    def out_pieces(half, j, values):
        out = matmul(gather_over_col(values), w_down).reshape(count, per_group, rows, width)
        for i in range(per_group):
            k = j * per_group + i
            piece = out[:, i]
            totals[half].append(shift(piece.astype(jnp.bfloat16), "row", -k) if k else piece)

    after = [[], []]
    for j in range(GROUPS):
        for half in range(2):
            own, marks = project(half, j, after[-2] if half == 0 else after[-1])
            if half == 0 and j + 1 < GROUPS:
                fetch(j + 1, marks[:1])
            after.append(marks[-1:] if half == 0 else marks[:1])
            out_pieces(half, j, hidden(half, j, own))

    turned, bars = [], []
    for half in range(2):
        total = totals[half][0]
        for moved in totals[half][1:]:
            total = total + moved.astype(jnp.float32)
        curv = own_rows(curvature, me * shard, halves[half])
        pieces = [(curv * total).astype(jnp.bfloat16)]
        for _ in range(ring - 1):
            pieces.append(shift(pieces[-1], "row"))
        for j in range(GROUPS):
            turned.append(joined([tie(piece, pieces[:1]) for piece in acts[half]], j).T)
            x = joined(pieces, j)
            own, _ = sum_over_col([times_down(x, w_down)], False)
            bars.append(gather_over_col((own[0] * gains[half][j]).astype(jnp.bfloat16)))
    return last_product(turned, bars, tokens)


def solution(mesh):
    in_specs = (
        P("row", "col"),
        P("col", "row"),
        P("col", "row"),
        P("row", "col"),
        P(("grp", "col"), "row"),
        P("grp", "col"),
    )
    out_specs = P(("grp", "col"), "row")
    return jax.shard_map(
        per_device, mesh=mesh, in_specs=in_specs, out_specs=out_specs, check_vma=False
    )
```

time: 489 us -> 544 us (1.11)
  other arithmetic: 40 us -> 67.4 us
  local copies, waits for them, and re-layouts: 25.5 us -> 42.9 us
  matrix products: 114 us -> 124 us
  starting transfers between devices: 52.4 us -> 46.2 us
    ppermute x21 -> x15, waiting for transfers between devices: 105 us -> 123 us  [shift(): lax.ppermute(values, axis, [(i, (i + by) % count) for i in range(count)])]
    ppermute x57 -> x37, starting transfers between devices: 44.1 us -> 26.7 us  [swap(): return lax.ppermute(values, axis, [(i, i ^ mask) for i in range(count)])]
    another operation x0 -> x16, local copies, waits for them, and re-layouts: none -> 16.1 us  [the longest x5 9.18 us: sum_over_col(): jnp.stack([p[at:at + half // 2] for p in parts]) + got[:, at:at + half // 2]]
    slice x12 -> x0, local copies, waits for them, and re-layouts: 14.6 us -> none  [sum_over_col(): keep, give = (part[:half], part[half:])]
    concatenate x20 -> x24, other arithmetic: 8.26 us -> 22 us  [the longest x12 15.9 us: joined(): jnp.concatenate(pieces[j * per_group:(j + 1) * per_group], axis=1)]
    ppermute x57 -> x37, waiting for transfers between devices: 122 us -> 109 us  [swap(): return lax.ppermute(values, axis, [(i, i ^ mask) for i in range(count)])]
    another operation x0 -> x12, other arithmetic: none -> 12 us
    ppermute x21 -> x15, starting transfers between devices: 8.34 us -> 19.4 us  [shift(): lax.ppermute(values, axis, [(i, (i + by) % count) for i in range(count)])]
  transfers between devices with their start and end apart: 78 -> 52, of which waited for: 31 -> 22; matrix products, arithmetic and copies ran while one was open for 35% -> 38% of each run, Pallas kernels for 0% -> 0%
where the time goes in v4:
time: 544 us; the launch traced here: 536 us
  waiting for transfers between devices  232 us (43%)
  matrix products  124 us (23%)
  other arithmetic  67.4 us (12%)
  starting transfers between devices  46.2 us (8%)
  local copies, waits for them, and re-layouts  42.9 us (8%)
  Pallas kernels  22.5 us (4%)
    ppermute x15, waiting for transfers between devices, shift(): lax.ppermute(values, axis, [(i, (i + by) % count) for i in range(count)])  123 us
    ppermute x37, waiting for transfers between devices, swap(): return lax.ppermute(values, axis, [(i, i ^ mask) for i in range(count)])  109 us
    dot_general x12, matrix products, matmul(): return jnp.dot(left, right, preferred_element_type=jnp.float32)  91.4 us
    dot_general x4, matrix products, times_down(): lax.dot_general(left, w_down, (((1,), (1,)), ((), ())), preferred_element...  33 us
    ppermute x37, starting transfers between devices, swap(): return lax.ppermute(values, axis, [(i, i ^ mask) for i in range(count)])  26.7 us
    pallas_call x1, Pallas kernels, last_product(): pl.pallas_call(functools.partial(last_kernel, 1.0 / tokens, len(turned)),...  22.5 us
    ppermute x15, starting transfers between devices, shift(): lax.ppermute(values, axis, [(i, (i + by) % count) for i in range(count)])  19.4 us
    concatenate x12, other arithmetic, joined(): jnp.concatenate(pieces[j * per_group:(j + 1) * per_group], axis=1)  15.9 us
  transfers between devices with their start and end apart: 52, of which 22 were waited for; matrix products, arithmetic and copies ran while one was open for 38% of the time, Pallas kernels for 0%

profile of v4, /device:TPU:0, one launch (start us, length us, event | category | flops | bytes accessed | tf_op | source)
XLA Modules:
  0.0 536.4 jit_solution(6918653890573078454)
XLA Ops:
  2.2 3.0 collective-permute-start
  5.3 13.9 %collective-permute-done = bf16[4,32,2048]{2,1,0:T(8,128)(2,1)S(1)} collective-permute-done((bf16[4,32,2048]{2,1,0:T(8,128)(2,1)S(1)}, bf16[4,32,2048]{2,1,0:T(8,128)(2,1)S(1)}, u32[]{:S(2)}, u32[]{:S(2)}) %collective-permute-start) | collective-permute-done | bytes 524320 | tf_op jit(solution)/shard_map/ppermute | solution.py:40
  19.3 7.5 %fusion.118 = f32[256,3584]{1,0:T(8,128)S(1)} fusion(bf16[256,2048]{1,0:T(8,128)(2,1)S(1)} %bitcast.312, bf16[2048,3584]{1,0:T(8,128)(2,1)} %param.10), kind=kOutput, calls=%fused_computation.290 | convolution fusion | flops 3758096384 | bytes 19398656 | tf_op jit(solution)/shard_map/dot_general | solution.py:18
  28.8 3.9 fusion.117
  32.8 8.6 %fusion.116 = f32[256,3584]{1,0:T(8,128)S(1)} fusion(bf16[256,2048]{1,0:T(8,128)(2,1)S(1)} %bitcast.314, bf16[2048,3584]{1,0:T(8,128)(2,1)} %param.7), kind=kOutput, calls=%fused_computation.288 | convolution fusion | flops 3758096384 | bytes 19398656 | tf_op jit(solution)/shard_map/dot_general | solution.py:18
  43.6 2.8 pad_maximum_fusion
  46.5 3.1 dynamic-slice_bitcast_fusion.3
  49.7 3.2 slice_bitcast_fusion.38
  54.3 11.5 %collective-permute-done.6 = bf16[4,32,2048]{2,1,0:T(8,128)(2,1)} collective-permute-done((bf16[4,32,2048]{2,1,0:T(8,128)(2,1)S(1)}, bf16[4,32,2048]{2,1,0:T(8,128)(2,1)}, u32[]{:S(2)}, u32[]{:S(2)}) %collective-permute-start.6) | collective-permute-done | bytes 524320 | tf_op jit(solution)/shard_map/ppermute | solution.py:40
  68.5 13.0 %collective-permute-done.7 = bf16[4,32,2048]{2,1,0:T(8,128)(2,1)} collective-permute-done((bf16[4,32,2048]{2,1,0:T(8,128)(2,1)}, bf16[4,32,2048]{2,1,0:T(8,128)(2,1)}, u32[]{:S(2)}, u32[]{:S(2)}) %collective-permute-start.7) | collective-permute-done | bytes 524320 | tf_op jit(solution)/shard_map/ppermute | solution.py:40
  91.3 7.3 %fusion.121 = f32[256,3584]{1,0:T(8,128)S(1)} fusion(bf16[256,2048]{1,0:T(8,128)(2,1)S(1)} %bitcast.317, bf16[2048,3584]{1,0:T(8,128)(2,1)} %param.10), kind=kOutput, calls=%fused_computation.293 | convolution fusion | flops 3758096384 | bytes 19398656 | tf_op jit(solution)/shard_map/dot_general | solution.py:18
  98.6 7.3 %fusion.120 = f32[256,3584]{1,0:T(8,128)S(1)} fusion(bf16[256,2048]{1,0:T(8,128)(2,1)S(1)} %bitcast.318, bf16[2048,3584]{1,0:T(8,128)(2,1)} %param.8), kind=kOutput, calls=%fused_computation.292 | convolution fusion | flops 3758096384 | bytes 19398656 | tf_op jit(solution)/shard_map/dot_general | solution.py:18
  105.9 7.3 %fusion.119 = f32[256,3584]{1,0:T(8,128)S(1)} fusion(bf16[256,2048]{1,0:T(8,128)(2,1)S(1)} %bitcast.319, bf16[2048,3584]{1,0:T(8,128)(2,1)} %param.7), kind=kOutput, calls=%fused_computation.291 | convolution fusion | flops 3758096384 | bytes 19398656 | tf_op jit(solution)/shard_map/dot_general | solution.py:18
  115.8 7.3 %fusion.122 = f32[256,3584]{1,0:T(8,128)S(1)} fusion(bf16[256,2048]{1,0:T(8,128)(2,1)S(1)} %bitcast.324, bf16[2048,3584]{1,0:T(8,128)(2,1)} %param.10), kind=kOutput, calls=%fused_computation.294 | convolution fusion | flops 3758096384 | bytes 19398656 | tf_op jit(solution)/shard_map/dot_general | solution.py:18
  123.6 3.2 pad_maximum_fusion.1
  128.8 2.9 fusion.1
  139.3 2.5 slice_bitcast_fusion.31
  141.8 5.1 collective-permute-done.3
  149.6 6.5 %collective-permute-done.17 = f16[1,64,3712]{2,1,0:T(8,128)(2,1)S(1)} collective-permute-done((f16[1,64,3712]{2,1,0:T(8,128)(2,1)}, f16[1,64,3712]{2,1,0:T(8,128)(2,1)S(1)}, u32[]{:S(2)}, u32[]{:S(2)}) %collective-permute-start.17) | collective-permute-done | bytes 475168 | tf_op jit(solution)/shard_map/ppermute | solution.py:35
  160.6 8.0 %fusion.2 = f32[256,2048]{1,0:T(8,128)S(1)} fusion(bf16[3584,2048]{1,0:T(8,128)(2,1)} %param.9, bf16[128,3584]{1,0:T(8,128)(2,1)S(1)} %collective-permute-done.4, bf16[64,3584]{1,0:T(8,128)(2,1)} %collective-permute-done.3, bf16[64,3584]{1,0:T(8,128)(2,1)} %get-tuple-element.59), kind=kOutput, calls=%fused_computation.26 | convolution fusion | flops 3763601408 | bytes 18612224 | tf_op jit(solution)/shard_map/dot_general | solution.py:18
  174.6 2.4 multiply_convert_fusion
  181.2 7.3 %fusion.123 = f32[256,3584]{1,0:T(8,128)S(1)} fusion(bf16[256,2048]{1,0:T(8,128)(2,1)S(1)} %bitcast.325, bf16[2048,3584]{1,0:T(8,128)(2,1)} %param.10), kind=kOutput, calls=%fused_computation.295 | convolution fusion | flops 3758096384 | bytes 19398656 | tf_op jit(solution)/shard_map/dot_general | solution.py:18
  188.9 24.3 %collective-permute-done.9 = f16[3,64,3712]{2,1,0:T(8,128)(2,1)S(1)} collective-permute-done((f16[3,64,3712]{2,1,0:T(8,128)(2,1)}, f16[3,64,3712]{2,1,0:T(8,128)(2,1)S(1)}, u32[]{:S(2)}, u32[]{:S(2)}) %collective-permute-start.9) | collective-permute-done | bytes 1425440 | tf_op jit(solution)/shard_map/ppermute | solution.py:35
  213.5 2.9 fusion
  225.0 7.7 %fusion.13 = f32[256,2048]{1,0:T(8,128)S(1)} fusion(bf16[3584,2048]{1,0:T(8,128)(2,1)} %param.9, bf16[128,3584]{1,0:T(8,128)(2,1)} %collective-permute-done.19, bf16[64,3584]{1,0:T(8,128)(2,1)} %copy-done.44, bf16[64,3584]{1,0:T(8,128)(2,1)S(1)} %copy-done.31), kind=kOutput, calls=%fused_computation.37 | convolution fusion | flops 3763601408 | bytes 18612224 | tf_op jit(solution)/shard_map/dot_general | solution.py:18
  234.7 5.7 %collective-permute-done.25 = f16[1,64,3712]{2,1,0:T(8,128)(2,1)S(1)} collective-permute-done((f16[1,64,3712]{2,1,0:T(8,128)(2,1)}, f16[1,64,3712]{2,1,0:T(8,128)(2,1)S(1)}, u32[]{:S(2)}, u32[]{:S(2)}) %collective-permute-start.25) | collective-permute-done | bytes 475168 | tf_op jit(solution)/shard_map/ppermute | solution.py:35
  243.8 9.6 %convolution_convert_fusion.1 = bf16[256,2048]{1,0:T(8,128)(2,1)S(1)} fusion(bf16[3584,2048]{1,0:T(8,128)(2,1)} %param.9, bf16[128,3584]{1,0:T(8,128)(2,1)S(1)} %collective-permute-done.11, bf16[64,3584]{1,0:T(8,128)(2,1)} %collective-permute-done.10, bf16[64,3584]{1,0:T(8,128)(2,1)} %get-tuple-element.57), kind=kOutput, calls=%fused_computation.13 | convolution fusion | flops 3764125696 | bytes 17563648 | tf_op jit(solution)/shard_map/dot_general | solution.py:18
  254.9 3.5 collective-permute-start.20
  259.4 29.5 %collective-permute-done.12 = bf16[4,32,2048]{2,1,0:T(8,128)(2,1)S(1)} collective-permute-done((bf16[4,32,2048]{2,1,0:T(8,128)(2,1)S(1)}, bf16[4,32,2048]{2,1,0:T(8,128)(2,1)S(1)}, u32[]{:S(2)}, u32[]{:S(2)}) %collective-permute-start.12) | collective-permute-done | bytes 524320 | tf_op jit(solution)/shard_map/ppermute | solution.py:40
  291.2 8.6 %collective-permute-start.30 = (bf16[4,32,2048]{2,1,0:T(8,128)(2,1)}, bf16[4,32,2048]{2,1,0:T(8,128)(2,1)}, u32[]{:S(2)}, u32[]{:S(2)}) collective-permute-start(bf16[4,32,2048]{2,1,0:T(8,128)(2,1)} %fusion.33), channel_id=1, source_target_pairs={{0,4},{4,8},{8,12},{12,0},{1,5},{5,9},{9,13},{13,1},{2,6},{6,10},{... | collective-permute-start | bytes 1572872 | tf_op jit(solution)/shard_map/ppermute | solution.py:40
  303.6 9.7 %convolution_convert_fusion = bf16[256,2048]{1,0:T(8,128)(2,1)S(1)} fusion(bf16[3584,2048]{1,0:T(8,128)(2,1)} %param.9, bf16[128,3584]{1,0:T(8,128)(2,1)} %collective-permute-done.27, bf16[64,3584]{1,0:T(8,128)(2,1)} %copy-done.45, bf16[64,3584]{1,0:T(8,128)(2,1)} %copy-done.32), kind=kOutput, calls=%fused_computation.12 | convolution fusion | flops 3764125696 | bytes 17563648 | tf_op jit(solution)/shard_map/dot_general | solution.py:18
  318.2 7.4 %fusion.124 = f32[256,3584]{1,0:T(8,128)S(1)} fusion(bf16[256,2048]{1,0:T(8,128)(2,1)S(1)} %bitcast.322, bf16[3584,2048]{1,0:T(8,128)(2,1)} %param.9), kind=kOutput, calls=%fused_computation.296 | convolution fusion | flops 3758096384 | bytes 19398656 | tf_op jit(solution)/shard_map/dot_general | solution.py:22
  326.7 35.0 %collective-permute-done.28 = bf16[4,32,2048]{2,1,0:T(8,128)(2,1)} collective-permute-done((bf16[4,32,2048]{2,1,0:T(8,128)(2,1)}, bf16[4,32,2048]{2,1,0:T(8,128)(2,1)}, u32[]{:S(2)}, u32[]{:S(2)}) %collective-permute-start.28) | collective-permute-done | bytes 524320 | tf_op jit(solution)/shard_map/ppermute | solution.py:40
  361.7 2.8 fusion.28
  374.4 4.1 collective-permute-done.41
  379.8 7.3 %fusion.126 = f32[256,3584]{1,0:T(8,128)S(1)} fusion(bf16[256,2048]{1,0:T(8,128)(2,1)S(1)} %bitcast.323, bf16[3584,2048]{1,0:T(8,128)(2,1)} %param.9), kind=kOutput, calls=%fused_computation.298 | convolution fusion | flops 3758096384 | bytes 19398656 | tf_op jit(solution)/shard_map/dot_general | solution.py:22
  388.6 2.4 collective-permute-done.36
  392.3 9.1 %fusion.125 = f32[256,3584]{1,0:T(8,128)} fusion(bf16[256,2048]{1,0:T(8,128)(2,1)S(1)} %bitcast.320, bf16[3584,2048]{1,0:T(8,128)(2,1)} %param.9), kind=kOutput, calls=%fused_computation.297 | convolution fusion | flops 3758096384 | bytes 19398656 | tf_op jit(solution)/shard_map/dot_general | solution.py:22
  401.4 3.0 slice_bitcast_fusion.2
  408.6 12.4 %collective-permute-done.47 = bf16[4,32,2048]{2,1,0:T(8,128)(2,1)S(1)} collective-permute-done((bf16[4,32,2048]{2,1,0:T(8,128)(2,1)}, bf16[4,32,2048]{2,1,0:T(8,128)(2,1)S(1)}, u32[]{:S(2)}, u32[]{:S(2)}) %collective-permute-start.47) | collective-permute-done | bytes 524320 | tf_op jit(solution)/shard_map/ppermute | solution.py:40
  422.1 9.1 %fusion.127 = f32[256,3584]{1,0:T(8,128)} fusion(bf16[256,2048]{1,0:T(8,128)(2,1)S(1)} %bitcast.321, bf16[3584,2048]{1,0:T(8,128)(2,1)} %param.9), kind=kOutput, calls=%fused_computation.299 | convolution fusion | flops 3758096384 | bytes 19398656 | tf_op jit(solution)/shard_map/dot_general | solution.py:22
  434.7 10.1 %collective-permute-done.33 = bf16[64,3584]{1,0:T(8,128)(2,1)S(1)} collective-permute-done((bf16[64,3584]{1,0:T(8,128)(2,1)S(1)}, bf16[64,3584]{1,0:T(8,128)(2,1)S(1)}, u32[]{:S(2)}, u32[]{:S(2)}) %collective-permute-start.33) | collective-permute-done | bytes 458784 | tf_op jit(solution)/shard_map/ppermute | solution.py:35
  449.7 10.0 %collective-permute-done.43 = bf16[1,64,3584]{2,1,0:T(8,128)(2,1)S(1)} collective-permute-done((bf16[1,64,3584]{2,1,0:T(8,128)(2,1)S(1)}, bf16[1,64,3584]{2,1,0:T(8,128)(2,1)S(1)}, u32[]{:S(2)}, u32[]{:S(2)}) %collective-permute-start.43) | collective-permute-done | bytes 458784 | tf_op jit(solution)/shard_map/ppermute | solution.py:35
  462.4 7.1 %collective-permute-done.38 = bf16[1,64,3584]{2,1,0:T(8,128)(2,1)S(1)} collective-permute-done((bf16[1,64,3584]{2,1,0:T(8,128)(2,1)S(1)}, bf16[1,64,3584]{2,1,0:T(8,128)(2,1)S(1)}, u32[]{:S(2)}, u32[]{:S(2)}) %collective-permute-start.38) | collective-permute-done | bytes 458784 | tf_op jit(solution)/shard_map/ppermute | solution.py:35
  473.5 5.8 %collective-permute-done.44 = bf16[64,3584]{1,0:T(8,128)(2,1)S(1)} collective-permute-done((bf16[64,3584]{1,0:T(8,128)(2,1)S(1)}, bf16[64,3584]{1,0:T(8,128)(2,1)S(1)}, u32[]{:S(2)}, u32[]{:S(2)}) %collective-permute-start.44) | collective-permute-done | bytes 458784 | tf_op jit(solution)/shard_map/ppermute | solution.py:35
  479.5 19.1 %collective-permute-done.49 = bf16[1,64,3584]{2,1,0:T(8,128)(2,1)S(1)} collective-permute-done((bf16[1,64,3584]{2,1,0:T(8,128)(2,1)S(1)}, bf16[1,64,3584]{2,1,0:T(8,128)(2,1)S(1)}, u32[]{:S(2)}, u32[]{:S(2)}) %collective-permute-start.49) | collective-permute-done | bytes 458784 | tf_op jit(solution)/shard_map/ppermute | solution.py:35
  500.2 10.7 %collective-permute-done.50 = bf16[64,3584]{1,0:T(8,128)(2,1)S(1)} collective-permute-done((bf16[64,3584]{1,0:T(8,128)(2,1)S(1)}, bf16[64,3584]{1,0:T(8,128)(2,1)S(1)}, u32[]{:S(2)}, u32[]{:S(2)}) %collective-permute-start.50) | collective-permute-done | bytes 458784 | tf_op jit(solution)/shard_map/ppermute | solution.py:35
  513.7 22.5 %shard_map.64 = f32[2048,3584]{1,0:T(8,128)} custom-call(bf16[2048,256]{1,0:T(8,128)(2,1)S(1)} %bitcast.301, bf16[2048,256]{1,0:T(8,128)(2,1)S(1)} %bitcast.300, bf16[2048,256]{1,0:T(8,128)(2,1)S(1)} %bitcast.303, bf16[2048,256]{1,0:T(8,128)(2,1)S(1)} %bitcast.302, bf16[256,3584]{1,0:T(8,128)(2,1)S(1)} %pad_maximum_fusion.2.refs_4_, ...), custom_call_target="tpu_custom_call" | custom-call | flops 15032385536 | bytes 40894464 | tf_op jit(solution)/shard_map/pallas_call | solution.py:87
  (282 shorter events, 117.8 us)
Async XLA Ops:
  2.2 17.0 %collective-permute-start = (bf16[4,32,2048]{2,1,0:T(8,128)(2,1)S(1)}, bf16[4,32,2048]{2,1,0:T(8,128)(2,1)S(1)}, u32[]{:S(2)}, u32[]{:S(2)}) collective-permute-start(bf16[4,32,2048]{2,1,0:T(8,128)(2,1)S(1)} %pad_maximum_fusion.26), channel_id=1, source_target_pairs={{0,4},{4,8},{8,12},{12,0},{1,5},{5,9},{9,13},{13,1},{2,6},{6,10},{... | collective-permute-start | bytes 1572872 | tf_op jit(solution)/shard_map/ppermute | solution.py:40
  46.4 35.1 %collective-permute-start.1 = (f32[3,128,3584]{2,1,0:T(8,128)}, f32[3,128,3584]{2,1,0:T(8,128)}, u32[]{:S(2)}, u32[]{:S(2)}) collective-permute-start(f32[3,128,3584]{2,1,0:T(8,128)} %pad_maximum_fusion), channel_id=1, source_target_pairs={{0,1},{1,0},{2,3},{3,2},{4,5},{5,4},{6,7},{7,6},{8,9},{9,8},{10,11... | collective-permute-start | bytes 16515080 | tf_op jit(solution)/shard_map/ppermute | solution.py:35
  49.6 16.2 %collective-permute-start.6 = (bf16[4,32,2048]{2,1,0:T(8,128)(2,1)S(1)}, bf16[4,32,2048]{2,1,0:T(8,128)(2,1)}, u32[]{:S(2)}, u32[]{:S(2)}) collective-permute-start(bf16[4,32,2048]{2,1,0:T(8,128)(2,1)S(1)} %collective-permute-done), channel_id=1, source_target_pairs={{0,4},{4,8},{8,12},{12,0},{1,5},{5,9},{9,13},{13,1},{2,6},{6,10},{... | collective-permute-start | bytes 1572872 | tf_op jit(solution)/shard_map/ppermute | solution.py:40
  52.8 61.7 %collective-permute-start.15 = (bf16[4,32,2048]{2,1,0:T(8,128)(2,1)S(1)}, bf16[4,32,2048]{2,1,0:T(8,128)(2,1)}, u32[]{:S(2)}, u32[]{:S(2)}) collective-permute-start(bf16[4,32,2048]{2,1,0:T(8,128)(2,1)S(1)} %collective-permute-done), channel_id=1, source_target_pairs={{0,16},{16,0},{1,17},{17,1},{2,18},{18,2},{3,19},{19,3},{4,20},{20... | collective-permute-start | bytes 1572872 | tf_op jit(solution)/shard_map/ppermute | solution.py:35
  65.9 15.7 %collective-permute-start.7 = (bf16[4,32,2048]{2,1,0:T(8,128)(2,1)}, bf16[4,32,2048]{2,1,0:T(8,128)(2,1)}, u32[]{:S(2)}, u32[]{:S(2)}) collective-permute-start(bf16[4,32,2048]{2,1,0:T(8,128)(2,1)} %collective-permute-done.6), channel_id=1, source_target_pairs={{0,4},{4,8},{8,12},{12,0},{1,5},{5,9},{9,13},{13,1},{2,6},{6,10},{... | collective-permute-start | bytes 1572872 | tf_op jit(solution)/shard_map/ppermute | solution.py:40
  67.0 112.9 %collective-permute-start.22 = (bf16[4,32,2048]{2,1,0:T(8,128)(2,1)}, bf16[4,32,2048]{2,1,0:T(8,128)(2,1)}, u32[]{:S(2)}, u32[]{:S(2)}) collective-permute-start(bf16[4,32,2048]{2,1,0:T(8,128)(2,1)} %collective-permute-done.6), channel_id=1, source_target_pairs={{0,16},{16,0},{1,17},{17,1},{2,18},{18,2},{3,19},{19,3},{4,20},{20... | collective-permute-start | bytes 1572872 | tf_op jit(solution)/shard_map/ppermute | solution.py:35
  88.6 39.4 %collective-permute-start.2 = (f16[3,64,3712]{2,1,0:T(8,128)(2,1)}, f16[3,64,3712]{2,1,0:T(8,128)(2,1)S(1)}, u32[]{:S(2)}, u32[]{:S(2)}) collective-permute-start(f16[3,64,3712]{2,1,0:T(8,128)(2,1)} %concatenate.125), channel_id=1, source_target_pairs={{0,2},{1,3},{2,0},{3,1},{4,6},{5,7},{6,4},{7,5},{8,10},{9,11},{10,... | collective-permute-start | bytes 4276232 | tf_op jit(solution)/shard_map/ppermute | solution.py:35
  123.2 12.0 %collective-permute-start.16 = (f32[1,128,3584]{2,1,0:T(8,128)S(1)}, f32[1,128,3584]{2,1,0:T(8,128)S(1)}, u32[]{:S(2)}, u32[]{:S(2)}) collective-permute-start(f32[1,128,3584]{2,1,0:T(8,128)S(1)} %slice_bitcast_fusion.5), channel_id=1, source_target_pairs={{0,1},{1,0},{2,3},{3,2},{4,5},{5,4},{6,7},{7,6},{8,9},{9,8},{10,11... | collective-permute-start | bytes 5505032 | tf_op jit(solution)/shard_map/ppermute | solution.py:35
  126.7 45.6 %collective-permute-start.8 = (f32[3,128,3584]{2,1,0:T(8,128)}, f32[3,128,3584]{2,1,0:T(8,128)}, u32[]{:S(2)}, u32[]{:S(2)}) collective-permute-start(f32[3,128,3584]{2,1,0:T(8,128)} %pad_maximum_fusion.1), channel_id=1, source_target_pairs={{0,1},{1,0},{2,3},{3,2},{4,5},{5,4},{6,7},{7,6},{8,9},{9,8},{10,11... | collective-permute-start | bytes 16515080 | tf_op jit(solution)/shard_map/ppermute | solution.py:35
  133.2 13.7 %collective-permute-start.3 = (bf16[64,3584]{1,0:T(8,128)(2,1)}, bf16[64,3584]{1,0:T(8,128)(2,1)}, u32[]{:S(2)}, u32[]{:S(2)}) collective-permute-start(bf16[64,3584]{1,0:T(8,128)(2,1)} %get-tuple-element.59), channel_id=1, source_target_pairs={{0,2},{1,3},{2,0},{3,1},{4,6},{5,7},{6,4},{7,5},{8,10},{9,11},{10,... | collective-permute-start | bytes 1376264 | tf_op jit(solution)/shard_map/ppermute | solution.py:35
  133.7 23.5 %collective-permute-start.14 = (f32[64,3584]{1,0:T(8,128)}, f32[64,3584]{1,0:T(8,128)S(1)}, u32[]{:S(2)}, u32[]{:S(2)}) collective-permute-start(f32[64,3584]{1,0:T(8,128)} %get-tuple-element.60), channel_id=1, source_target_pairs={{0,16},{16,0},{1,17},{17,1},{2,18},{18,2},{3,19},{19,3},{4,20},{20... | collective-permute-start | bytes 2752520 | tf_op jit(solution)/shard_map/ppermute | solution.py:35
  137.7 18.4 %collective-permute-start.17 = (f16[1,64,3712]{2,1,0:T(8,128)(2,1)}, f16[1,64,3712]{2,1,0:T(8,128)(2,1)S(1)}, u32[]{:S(2)}, u32[]{:S(2)}) collective-permute-start(f16[1,64,3712]{2,1,0:T(8,128)(2,1)} %concatenate.135), channel_id=1, source_target_pairs={{0,2},{1,3},{2,0},{3,1},{4,6},{5,7},{6,4},{7,5},{8,10},{9,11},{10,... | collective-permute-start | bytes 1425416 | tf_op jit(solution)/shard_map/ppermute | solution.py:35
  146.9 33.0 %collective-permute-start.23 = (bf16[4,32,2048]{2,1,0:T(8,128)(2,1)}, bf16[4,32,2048]{2,1,0:T(8,128)(2,1)}, u32[]{:S(2)}, u32[]{:S(2)}) collective-permute-start(bf16[4,32,2048]{2,1,0:T(8,128)(2,1)} %collective-permute-done.7), channel_id=1, source_target_pairs={{0,16},{16,0},{1,17},{17,1},{2,18},{18,2},{3,19},{19,3},{4,20},{20... | collective-permute-start | bytes 1572872 | tf_op jit(solution)/shard_map/ppermute | solution.py:35
  159.1 12.2 %collective-permute-start.18 = (bf16[64,3584]{1,0:T(8,128)(2,1)S(1)}, bf16[64,3584]{1,0:T(8,128)(2,1)S(1)}, u32[]{:S(2)}, u32[]{:S(2)}) collective-permute-start(bf16[64,3584]{1,0:T(8,128)(2,1)S(1)} %fusion.61), channel_id=1, source_target_pairs={{0,2},{1,3},{2,0},{3,1},{4,6},{5,7},{6,4},{7,5},{8,10},{9,11},{10,... | collective-permute-start | bytes 1376264 | tf_op jit(solution)/shard_map/ppermute | solution.py:35
  169.6 89.8 %collective-permute-start.5 = (bf16[4,32,2048]{2,1,0:T(8,128)(2,1)}, bf16[4,32,2048]{2,1,0:T(8,128)(2,1)}, u32[]{:S(2)}, u32[]{:S(2)}) collective-permute-start(bf16[4,32,2048]{2,1,0:T(8,128)(2,1)} %fusion.68), channel_id=1, source_target_pairs={{0,12},{4,0},{8,4},{12,8},{1,13},{5,1},{9,5},{13,9},{2,14},{6,2},{... | collective-permute-start | bytes 1572872 | tf_op jit(solution)/shard_map/ppermute | solution.py:40
  172.3 52.7 %collective-permute-start.19 = (bf16[128,3584]{1,0:T(8,128)(2,1)}, bf16[128,3584]{1,0:T(8,128)(2,1)}, u32[]{:S(2)}, u32[]{:S(2)}) collective-permute-start(bf16[128,3584]{1,0:T(8,128)(2,1)} %pad_maximum_fusion.20), channel_id=1, source_target_pairs={{0,1},{1,0},{2,3},{3,2},{4,5},{5,4},{6,7},{7,6},{8,9},{9,8},{10,11... | collective-permute-start | bytes 2752520 | tf_op jit(solution)/shard_map/ppermute | solution.py:35
  179.3 33.9 %collective-permute-start.9 = (f16[3,64,3712]{2,1,0:T(8,128)(2,1)}, f16[3,64,3712]{2,1,0:T(8,128)(2,1)S(1)}, u32[]{:S(2)}, u32[]{:S(2)}) collective-permute-start(f16[3,64,3712]{2,1,0:T(8,128)(2,1)} %concatenate.129), channel_id=1, source_target_pairs={{0,2},{1,3},{2,0},{3,1},{4,6},{5,7},{6,4},{7,5},{8,10},{9,11},{10,... | collective-permute-start | bytes 4276232 | tf_op jit(solution)/shard_map/ppermute | solution.py:35
  188.6 31.3 %collective-permute-start.24 = (f32[1,128,3584]{2,1,0:T(8,128)S(1)}, f32[1,128,3584]{2,1,0:T(8,128)S(1)}, u32[]{:S(2)}, u32[]{:S(2)}) collective-permute-start(f32[1,128,3584]{2,1,0:T(8,128)S(1)} %slice_bitcast_fusion.4), channel_id=1, source_target_pairs={{0,1},{1,0},{2,3},{3,2},{4,5},{5,4},{6,7},{7,6},{8,9},{9,8},{10,11... | collective-permute-start | bytes 5505032 | tf_op jit(solution)/shard_map/ppermute | solution.py:35
  217.9 14.8 %collective-permute-start.10 = (bf16[64,3584]{1,0:T(8,128)(2,1)}, bf16[64,3584]{1,0:T(8,128)(2,1)}, u32[]{:S(2)}, u32[]{:S(2)}) collective-permute-start(bf16[64,3584]{1,0:T(8,128)(2,1)} %get-tuple-element.57), channel_id=1, source_target_pairs={{0,2},{1,3},{2,0},{3,1},{4,6},{5,7},{6,4},{7,5},{8,10},{9,11},{10,... | collective-permute-start | bytes 1376264 | tf_op jit(solution)/shard_map/ppermute | solution.py:35
  218.4 22.2 %collective-permute-start.21 = (f32[64,3584]{1,0:T(8,128)}, f32[64,3584]{1,0:T(8,128)S(1)}, u32[]{:S(2)}, u32[]{:S(2)}) collective-permute-start(f32[64,3584]{1,0:T(8,128)} %get-tuple-element.58), channel_id=1, source_target_pairs={{0,16},{16,0},{1,17},{17,1},{2,18},{18,2},{3,19},{19,3},{4,20},{20... | collective-permute-start | bytes 2752520 | tf_op jit(solution)/shard_map/ppermute | solution.py:35
  223.5 16.9 %collective-permute-start.25 = (f16[1,64,3712]{2,1,0:T(8,128)(2,1)}, f16[1,64,3712]{2,1,0:T(8,128)(2,1)S(1)}, u32[]{:S(2)}, u32[]{:S(2)}) collective-permute-start(f16[1,64,3712]{2,1,0:T(8,128)(2,1)} %concatenate.139), channel_id=1, source_target_pairs={{0,2},{1,3},{2,0},{3,1},{4,6},{5,7},{6,4},{7,5},{8,10},{9,11},{10,... | collective-permute-start | bytes 1425416 | tf_op jit(solution)/shard_map/ppermute | solution.py:35
  242.6 15.8 %collective-permute-start.26 = (bf16[64,3584]{1,0:T(8,128)(2,1)S(1)}, bf16[64,3584]{1,0:T(8,128)(2,1)S(1)}, u32[]{:S(2)}, u32[]{:S(2)}) collective-permute-start(bf16[64,3584]{1,0:T(8,128)(2,1)S(1)} %fusion.57), channel_id=1, source_target_pairs={{0,2},{1,3},{2,0},{3,1},{4,6},{5,7},{6,4},{7,5},{8,10},{9,11},{10,... | collective-permute-start | bytes 1376264 | tf_op jit(solution)/shard_map/ppermute | solution.py:35
  253.5 35.4 %collective-permute-start.12 = (bf16[4,32,2048]{2,1,0:T(8,128)(2,1)S(1)}, bf16[4,32,2048]{2,1,0:T(8,128)(2,1)S(1)}, u32[]{:S(2)}, u32[]{:S(2)}) collective-permute-start(bf16[4,32,2048]{2,1,0:T(8,128)(2,1)S(1)} %get-tuple-element.91), channel_id=1, source_target_pairs={{0,8},{4,12},{8,0},{12,4},{1,9},{5,13},{9,1},{13,5},{2,10},{6,14},... | collective-permute-start | bytes 1572872 | tf_op jit(solution)/shard_map/ppermute | solution.py:40
  253.6 35.3 %collective-permute-start.13 = (bf16[4,32,2048]{2,1,0:T(8,128)(2,1)S(1)}, bf16[4,32,2048]{2,1,0:T(8,128)(2,1)S(1)}, u32[]{:S(2)}, u32[]{:S(2)}) collective-permute-start(bf16[4,32,2048]{2,1,0:T(8,128)(2,1)S(1)} %get-tuple-element.92), channel_id=1, source_target_pairs={{0,4},{4,8},{8,12},{12,0},{1,5},{5,9},{9,13},{13,1},{2,6},{6,10},{... | collective-permute-start | bytes 1572872 | tf_op jit(solution)/shard_map/ppermute | solution.py:40
  254.9 71.8 %collective-permute-start.20 = (bf16[4,32,2048]{2,1,0:T(8,128)(2,1)}, bf16[4,32,2048]{2,1,0:T(8,128)(2,1)}, u32[]{:S(2)}, u32[]{:S(2)}) collective-permute-start(bf16[4,32,2048]{2,1,0:T(8,128)(2,1)} %fusion.69), channel_id=1, source_target_pairs={{0,12},{4,0},{8,4},{12,8},{1,13},{5,1},{9,5},{13,9},{2,14},{6,2},{... | collective-permute-start | bytes 1572872 | tf_op jit(solution)/shard_map/ppermute | solution.py:40
  259.4 44.2 %collective-permute-start.27 = (bf16[128,3584]{1,0:T(8,128)(2,1)}, bf16[128,3584]{1,0:T(8,128)(2,1)}, u32[]{:S(2)}, u32[]{:S(2)}) collective-permute-start(bf16[128,3584]{1,0:T(8,128)(2,1)} %pad_maximum_fusion.21), channel_id=1, source_target_pairs={{0,1},{1,0},{2,3},{3,2},{4,5},{5,4},{6,7},{7,6},{8,9},{9,8},{10,11... | collective-permute-start | bytes 2752520 | tf_op jit(solution)/shard_map/ppermute | solution.py:35
  291.2 25.7 %collective-permute-start.30 = (bf16[4,32,2048]{2,1,0:T(8,128)(2,1)}, bf16[4,32,2048]{2,1,0:T(8,128)(2,1)}, u32[]{:S(2)}, u32[]{:S(2)}) collective-permute-start(bf16[4,32,2048]{2,1,0:T(8,128)(2,1)} %fusion.33), channel_id=1, source_target_pairs={{0,4},{4,8},{8,12},{12,0},{1,5},{5,9},{9,13},{13,1},{2,6},{6,10},{... | collective-permute-start | bytes 1572872 | tf_op jit(solution)/shard_map/ppermute | solution.py:40
  314.4 47.3 %collective-permute-start.28 = (bf16[4,32,2048]{2,1,0:T(8,128)(2,1)}, bf16[4,32,2048]{2,1,0:T(8,128)(2,1)}, u32[]{:S(2)}, u32[]{:S(2)}) collective-permute-start(bf16[4,32,2048]{2,1,0:T(8,128)(2,1)} %get-tuple-element.81), channel_id=1, source_target_pairs={{0,8},{4,12},{8,0},{12,4},{1,9},{5,13},{9,1},{13,5},{2,10},{6,14},... | collective-permute-start | bytes 1572872 | tf_op jit(solution)/shard_map/ppermute | solution.py:40
  316.3 45.4 %collective-permute-start.29 = (bf16[4,32,2048]{2,1,0:T(8,128)(2,1)}, bf16[4,32,2048]{2,1,0:T(8,128)(2,1)}, u32[]{:S(2)}, u32[]{:S(2)}) collective-permute-start(bf16[4,32,2048]{2,1,0:T(8,128)(2,1)} %get-tuple-element.82), channel_id=1, source_target_pairs={{0,4},{4,8},{8,12},{12,0},{1,5},{5,9},{9,13},{13,1},{2,6},{6,10},{... | collective-permute-start | bytes 1572872 | tf_op jit(solution)/shard_map/ppermute | solution.py:40
  325.6 48.7 %collective-permute-start.35 = (bf16[4,32,2048]{2,1,0:T(8,128)(2,1)}, bf16[4,32,2048]{2,1,0:T(8,128)(2,1)}, u32[]{:S(2)}, u32[]{:S(2)}) collective-permute-start(bf16[4,32,2048]{2,1,0:T(8,128)(2,1)} %collective-permute-done.30), channel_id=1, source_target_pairs={{0,4},{4,8},{8,12},{12,0},{1,5},{5,9},{9,13},{13,1},{2,6},{6,10},{... | collective-permute-start | bytes 1572872 | tf_op jit(solution)/shard_map/ppermute | solution.py:40
  364.6 14.0 %collective-permute-start.41 = (bf16[4,32,2048]{2,1,0:T(8,128)(2,1)}, bf16[4,32,2048]{2,1,0:T(8,128)(2,1)}, u32[]{:S(2)}, u32[]{:S(2)}) collective-permute-start(bf16[4,32,2048]{2,1,0:T(8,128)(2,1)} %fusion.28), channel_id=1, source_target_pairs={{0,4},{4,8},{8,12},{12,0},{1,5},{5,9},{9,13},{13,1},{2,6},{6,10},{... | collective-permute-start | bytes 1572872 | tf_op jit(solution)/shard_map/ppermute | solution.py:40
  365.9 39.3 %collective-permute-start.31 = (f32[1,128,3584]{2,1,0:T(8,128)}, f32[1,128,3584]{2,1,0:T(8,128)}, u32[]{:S(2)}, u32[]{:S(2)}) collective-permute-start(f32[1,128,3584]{2,1,0:T(8,128)} %slice_bitcast_fusion.3), channel_id=1, source_target_pairs={{0,1},{1,0},{2,3},{3,2},{4,5},{5,4},{6,7},{7,6},{8,9},{9,8},{10,11... | collective-permute-start | bytes 5505032 | tf_op jit(solution)/shard_map/ppermute | solution.py:35
  374.3 16.7 %collective-permute-start.36 = (bf16[4,32,2048]{2,1,0:T(8,128)(2,1)}, bf16[4,32,2048]{2,1,0:T(8,128)(2,1)}, u32[]{:S(2)}, u32[]{:S(2)}) collective-permute-start(bf16[4,32,2048]{2,1,0:T(8,128)(2,1)} %collective-permute-done.35), channel_id=1, source_target_pairs={{0,4},{4,8},{8,12},{12,0},{1,5},{5,9},{9,13},{13,1},{2,6},{6,10},{... | collective-permute-start | bytes 1572872 | tf_op jit(solution)/shard_map/ppermute | solution.py:40
  388.6 56.4 %collective-permute-start.42 = (f32[1,128,3584]{2,1,0:T(8,128)}, f32[1,128,3584]{2,1,0:T(8,128)}, u32[]{:S(2)}, u32[]{:S(2)}) collective-permute-start(f32[1,128,3584]{2,1,0:T(8,128)} %slice_bitcast_fusion.1), channel_id=1, source_target_pairs={{0,1},{1,0},{2,3},{3,2},{4,5},{5,4},{6,7},{7,6},{8,9},{9,8},{10,11... | collective-permute-start | bytes 5505032 | tf_op jit(solution)/shard_map/ppermute | solution.py:35
  388.6 16.4 %collective-permute-start.46 = (bf16[4,32,2048]{2,1,0:T(8,128)(2,1)}, bf16[4,32,2048]{2,1,0:T(8,128)(2,1)}, u32[]{:S(2)}, u32[]{:S(2)}) collective-permute-start(bf16[4,32,2048]{2,1,0:T(8,128)(2,1)} %collective-permute-done.41), channel_id=1, source_target_pairs={{0,4},{4,8},{8,12},{12,0},{1,5},{5,9},{9,13},{13,1},{2,6},{6,10},{... | collective-permute-start | bytes 1572872 | tf_op jit(solution)/shard_map/ppermute | solution.py:40
  404.5 43.1 %collective-permute-start.37 = (f32[1,128,3584]{2,1,0:T(8,128)}, f32[1,128,3584]{2,1,0:T(8,128)}, u32[]{:S(2)}, u32[]{:S(2)}) collective-permute-start(f32[1,128,3584]{2,1,0:T(8,128)} %slice_bitcast_fusion.2), channel_id=1, source_target_pairs={{0,1},{1,0},{2,3},{3,2},{4,5},{5,4},{6,7},{7,6},{8,9},{9,8},{10,11... | collective-permute-start | bytes 5505032 | tf_op jit(solution)/shard_map/ppermute | solution.py:35
  405.0 16.0 %collective-permute-start.47 = (bf16[4,32,2048]{2,1,0:T(8,128)(2,1)}, bf16[4,32,2048]{2,1,0:T(8,128)(2,1)S(1)}, u32[]{:S(2)}, u32[]{:S(2)}) collective-permute-start(bf16[4,32,2048]{2,1,0:T(8,128)(2,1)} %collective-permute-done.46), channel_id=1, source_target_pairs={{0,4},{4,8},{8,12},{12,0},{1,5},{5,9},{9,13},{13,1},{2,6},{6,10},{... | collective-permute-start | bytes 1572872 | tf_op jit(solution)/shard_map/ppermute | solution.py:40
  407.4 23.9 %collective-permute-start.32 = (bf16[1,64,3584]{2,1,0:T(8,128)(2,1)}, bf16[1,64,3584]{2,1,0:T(8,128)(2,1)}, u32[]{:S(2)}, u32[]{:S(2)}) collective-permute-start(bf16[1,64,3584]{2,1,0:T(8,128)(2,1)} %fusion.49), channel_id=1, source_target_pairs={{0,2},{1,3},{2,0},{3,1},{4,6},{5,7},{6,4},{7,5},{8,10},{9,11},{10,... | collective-permute-start | bytes 1376264 | tf_op jit(solution)/shard_map/ppermute | solution.py:35
  433.2 11.6 %collective-permute-start.33 = (bf16[64,3584]{1,0:T(8,128)(2,1)S(1)}, bf16[64,3584]{1,0:T(8,128)(2,1)S(1)}, u32[]{:S(2)}, u32[]{:S(2)}) collective-permute-start(bf16[64,3584]{1,0:T(8,128)(2,1)S(1)} %fusion.53), channel_id=1, source_target_pairs={{0,2},{1,3},{2,0},{3,1},{4,6},{5,7},{6,4},{7,5},{8,10},{9,11},{10,... | collective-permute-start | bytes 1376264 | tf_op jit(solution)/shard_map/ppermute | solution.py:35
  434.6 37.9 %collective-permute-start.48 = (f32[1,128,3584]{2,1,0:T(8,128)S(1)}, f32[1,128,3584]{2,1,0:T(8,128)S(1)}, u32[]{:S(2)}, u32[]{:S(2)}) collective-permute-start(f32[1,128,3584]{2,1,0:T(8,128)S(1)} %slice_bitcast_fusion), channel_id=1, source_target_pairs={{0,1},{1,0},{2,3},{3,2},{4,5},{5,4},{6,7},{7,6},{8,9},{9,8},{10,11... | collective-permute-start | bytes 5505032 | tf_op jit(solution)/shard_map/ppermute | solution.py:35
  444.9 27.5 %collective-permute-start.34 = (bf16[128,3584]{1,0:T(8,128)(2,1)S(1)}, bf16[128,3584]{1,0:T(8,128)(2,1)S(1)}, u32[]{:S(2)}, u32[]{:S(2)}) collective-permute-start(bf16[128,3584]{1,0:T(8,128)(2,1)S(1)} %pad_maximum_fusion.22), channel_id=1, source_target_pairs={{0,1},{1,0},{2,3},{3,2},{4,5},{5,4},{6,7},{7,6},{8,9},{9,8},{10,11... | collective-permute-start | bytes 2752520 | tf_op jit(solution)/shard_map/ppermute | solution.py:35
  446.3 13.4 %collective-permute-start.43 = (bf16[1,64,3584]{2,1,0:T(8,128)(2,1)S(1)}, bf16[1,64,3584]{2,1,0:T(8,128)(2,1)S(1)}, u32[]{:S(2)}, u32[]{:S(2)}) collective-permute-start(bf16[1,64,3584]{2,1,0:T(8,128)(2,1)S(1)} %fusion.39), channel_id=1, source_target_pairs={{0,2},{1,3},{2,0},{3,1},{4,6},{5,7},{6,4},{7,5},{8,10},{9,11},{10,... | collective-permute-start | bytes 1376264 | tf_op jit(solution)/shard_map/ppermute | solution.py:35
  448.8 20.7 %collective-permute-start.38 = (bf16[1,64,3584]{2,1,0:T(8,128)(2,1)S(1)}, bf16[1,64,3584]{2,1,0:T(8,128)(2,1)S(1)}, u32[]{:S(2)}, u32[]{:S(2)}) collective-permute-start(bf16[1,64,3584]{2,1,0:T(8,128)(2,1)S(1)} %fusion.44), channel_id=1, source_target_pairs={{0,2},{1,3},{2,0},{3,1},{4,6},{5,7},{6,4},{7,5},{8,10},{9,11},{10,... | collective-permute-start | bytes 1376264 | tf_op jit(solution)/shard_map/ppermute | solution.py:35
  461.1 18.2 %collective-permute-start.44 = (bf16[64,3584]{1,0:T(8,128)(2,1)S(1)}, bf16[64,3584]{1,0:T(8,128)(2,1)S(1)}, u32[]{:S(2)}, u32[]{:S(2)}) collective-permute-start(bf16[64,3584]{1,0:T(8,128)(2,1)S(1)} %fusion.43), channel_id=1, source_target_pairs={{0,2},{1,3},{2,0},{3,1},{4,6},{5,7},{6,4},{7,5},{8,10},{9,11},{10,... | collective-permute-start | bytes 1376264 | tf_op jit(solution)/shard_map/ppermute | solution.py:35
  471.1 29.0 %collective-permute-start.39 = (bf16[64,3584]{1,0:T(8,128)(2,1)S(1)}, bf16[64,3584]{1,0:T(8,128)(2,1)S(1)}, u32[]{:S(2)}, u32[]{:S(2)}) collective-permute-start(bf16[64,3584]{1,0:T(8,128)(2,1)S(1)} %fusion.48), channel_id=1, source_target_pairs={{0,2},{1,3},{2,0},{3,1},{4,6},{5,7},{6,4},{7,5},{8,10},{9,11},{10,... | collective-permute-start | bytes 1376264 | tf_op jit(solution)/shard_map/ppermute | solution.py:35
  472.6 25.9 %collective-permute-start.49 = (bf16[1,64,3584]{2,1,0:T(8,128)(2,1)S(1)}, bf16[1,64,3584]{2,1,0:T(8,128)(2,1)S(1)}, u32[]{:S(2)}, u32[]{:S(2)}) collective-permute-start(bf16[1,64,3584]{2,1,0:T(8,128)(2,1)S(1)} %fusion.34), channel_id=1, source_target_pairs={{0,2},{1,3},{2,0},{3,1},{4,6},{5,7},{6,4},{7,5},{8,10},{9,11},{10,... | collective-permute-start | bytes 1376264 | tf_op jit(solution)/shard_map/ppermute | solution.py:35
  479.4 31.7 %collective-permute-start.45 = (bf16[128,3584]{1,0:T(8,128)(2,1)S(1)}, bf16[128,3584]{1,0:T(8,128)(2,1)S(1)}, u32[]{:S(2)}, u32[]{:S(2)}) collective-permute-start(bf16[128,3584]{1,0:T(8,128)(2,1)S(1)} %pad_maximum_fusion.24), channel_id=1, source_target_pairs={{0,1},{1,0},{2,3},{3,2},{4,5},{5,4},{6,7},{7,6},{8,9},{9,8},{10,11... | collective-permute-start | bytes 2752520 | tf_op jit(solution)/shard_map/ppermute | solution.py:35
  498.8 12.2 %collective-permute-start.50 = (bf16[64,3584]{1,0:T(8,128)(2,1)S(1)}, bf16[64,3584]{1,0:T(8,128)(2,1)S(1)}, u32[]{:S(2)}, u32[]{:S(2)}) collective-permute-start(bf16[64,3584]{1,0:T(8,128)(2,1)S(1)} %fusion.38), channel_id=1, source_target_pairs={{0,2},{1,3},{2,0},{3,1},{4,6},{5,7},{6,4},{7,5},{8,10},{9,11},{10,... | collective-permute-start | bytes 1376264 | tf_op jit(solution)/shard_map/ppermute | solution.py:35
  (54 other events, 970.5 us)

commit v5 on v4

--- a/solution.py
+++ b/solution.py
@@ -1,4 +1,5 @@
 import functools
+import math
 
 import jax
 import jax.numpy as jnp
@@ -125,40 +126,48 @@
         )
 
     halves = (grp, 1 - grp)
-    acts = [[own_rows(inputs, 0, half)] for half in halves]
-    for k in range(1, per_group):
-        acts[0].append(shift(acts[0][-1], "row"))
-        acts[1].append(swap(acts[0][-1], "grp", 1))
-
-    def fetch(j, after):
-        acts[0].append(shift(acts[0][-1], "row"))
-        for _ in range(1, per_group):
-            acts[0].append(shift(tie(acts[0][-1], after), "row"))
-        for piece in acts[0][-per_group:]:
-            acts[1].append(swap(tie(piece, after), "grp", 1))
-
-    def sum_over_col(parts, code):
-        part, mask, marks = None, 1, []
-        while mask < count:
-            if part is None:
-                half = parts[0].shape[0] // 2
-                marks.append(jnp.stack([p[half:] for p in parts]))
-                got = swap(marks[-1], "col", mask)
-                halves_of = [
-                    jnp.stack([p[at : at + half // 2] for p in parts])
-                    + got[:, at : at + half // 2]
-                    for at in (0, half // 2)
-                ]
-            else:
-                half = part.shape[1] // 2
-                halves_of = [part[:, :half], part[:, half:]]
-            part, give = halves_of
+    acts = [[None] * ring, [None] * ring]
+    for half in range(2):
+        acts[half][0] = own_rows(inputs, 0, halves[half])
+
+    def fetch(step, after):
+        for k in step:
+            if k:
+                acts[0][k] = shift(tie(acts[0][0], after), "row", k)
+
+    def fetch_other(step, after):
+        for k in step:
+            if k:
+                acts[1][k] = swap(tie(acts[0][k], after), "grp", 1)
+
+    gate_scale = 2.0 ** math.floor(math.log2(65504.0 / (0.375 * width * count)))
+
+    def pack(values, form):
+        if form == "gate":
+            return (values * gate_scale).astype(jnp.float16)
+        return coded(values) if form == "up" else values.astype(jnp.bfloat16)
+
+    def unpack(values, form):
+        if form == "up":
+            return decoded(values)
+        values = values.astype(jnp.float32)
+        return values * (1.0 / gate_scale) if form == "gate" else values
+
+    def sum_over_col(part, form):
+        half = part.shape[0] // 2
+        got = swap(part[half:], "col", 1)
+        cut = half // 2
+        own, give = part[:cut] + got[:cut], part[cut:half] + got[cut:]
+        mask, mark = 2, None
+        while True:
+            sent = pack(give, form)
+            mark = sent if mark is None else mark
+            own = own + unpack(swap(sent, "col", mask), form)
             mask *= 2
-            marks.append(coded(give) if code else give.astype(jnp.bfloat16))
-            got = swap(marks[-1], "col", mask)
-            part = part + (decoded(got) if code else got.astype(jnp.float32))
-            if mask * 2 >= count:
-                return part, marks
+            if mask >= count:
+                return own, mark
+            cut = own.shape[0] // 2
+            own, give = own[:cut], own[cut:]
 
     def gather_over_col(values):
         mask = count // 2
@@ -167,52 +176,60 @@
             mask //= 2
         return values
 
+    steps = [list(range(j * per_group, (j + 1) * per_group)) for j in range(GROUPS)]
+    fetch(steps[0], [])
+    first = acts[0][1:per_group]
+    for step in steps[1:]:
+        fetch(step, first)
+    fetch_other(steps[0], [])
+
+    sums, marks = {}, []
+    for half in range(2):
+        for j in range(GROUPS):
+            x = None
+            for form in ("gate", "up", "tangent") if half == 0 else ("tangent",):
+                after = marks[-2:-1]
+                if x is None:
+                    x = joined([p if p is None else tie(p, after) for p in acts[half]], j)
+                else:
+                    x = tie(x, after)
+                weight = {"gate": w_gate, "up": w_up, "tangent": query}[form]
+                sums[half, j, form], mark = sum_over_col(matmul(x, weight), form)
+                marks.append(mark)
+            if half == 0 and j + 1 < GROUPS:
+                fetch_other(steps[j + 1], marks[-1:])
+
     gains = [[None] * GROUPS, [None] * GROUPS]
-    totals = [[], []]
-
-    def project(half, j, after):
-        x = joined([tie(piece, after) for piece in acts[half]], j)
-        weights = [w_gate, w_up, query] if half == 0 else [query]
-        return sum_over_col([matmul(x, w) for w in weights], True)
-
-    def hidden(half, j, own):
-        if half == 0:
-            gate_out, up_out = own[0], own[1]
-            sigmas = jax.nn.sigmoid(gate_out)
-            gains[0][j] = sigmas * (1.0 + gate_out * (1.0 - sigmas)) * up_out
-            gains[1][j] = swap(gains[0][j], "grp", 1)
-        return (gains[half][j] * own[-1]).astype(jnp.bfloat16)
-
-    def out_pieces(half, j, values):
-        out = matmul(gather_over_col(values), w_down).reshape(count, per_group, rows, width)
-        for i in range(per_group):
-            k = j * per_group + i
-            piece = out[:, i]
-            totals[half].append(shift(piece.astype(jnp.bfloat16), "row", -k) if k else piece)
-
-    after = [[], []]
     for j in range(GROUPS):
-        for half in range(2):
-            own, marks = project(half, j, after[-2] if half == 0 else after[-1])
-            if half == 0 and j + 1 < GROUPS:
-                fetch(j + 1, marks[:1])
-            after.append(marks[-1:] if half == 0 else marks[:1])
-            out_pieces(half, j, hidden(half, j, own))
-
+        gate_out, up_out = sums[0, j, "gate"], sums[0, j, "up"]
+        sigmas = jax.nn.sigmoid(gate_out)
+        gains[0][j] = sigmas * (1.0 + gate_out * (1.0 - sigmas)) * up_out
+        gains[1][j] = swap(gains[0][j], "grp", 1)
+
+    last = ring - 1
     turned, bars = [], []
     for half in range(2):
-        total = totals[half][0]
-        for moved in totals[half][1:]:
-            total = total + moved.astype(jnp.float32)
-        curv = own_rows(curvature, me * shard, halves[half])
-        pieces = [(curv * total).astype(jnp.bfloat16)]
-        for _ in range(ring - 1):
-            pieces.append(shift(pieces[-1], "row"))
+        moved = []
         for j in range(GROUPS):
-            turned.append(joined([tie(piece, pieces[:1]) for piece in acts[half]], j).T)
-            x = joined(pieces, j)
-            own, _ = sum_over_col([times_down(x, w_down)], False)
-            bars.append(gather_over_col((own[0] * gains[half][j]).astype(jnp.bfloat16)))
+            hidden = (gains[half][j] * sums[half, j, "tangent"]).astype(jnp.bfloat16)
+            out = matmul(gather_over_col(hidden), w_down).reshape(count, per_group, rows, width)
+            for i, k in enumerate(steps[j]):
+                piece = out[:, i]
+                if k < last:
+                    piece = shift(piece.astype(jnp.bfloat16), "row", last - k).astype(jnp.float32)
+                moved.append(piece)
+        total = moved[-1]
+        for piece in moved[:-1]:
+            total = total + piece
+        curv = own_rows(curvature, (me + 1) % ring * shard, halves[half])
+        pieces = [None] * last + [(curv * total).astype(jnp.bfloat16)]
+        for k in reversed(range(last)):
+            pieces[k] = shift(pieces[k + 1], "row", -1)
+        for j in reversed(range(GROUPS)):
+            after = pieces[last:]
+            turned.append(joined([tie(piece, after) for piece in acts[half]], j).T)
+            own, _ = sum_over_col(times_down(joined(pieces, j), w_down), "back")
+            bars.append(gather_over_col((own * gains[half][j]).astype(jnp.bfloat16)))
     return last_product(turned, bars, tokens)
 
 

time: 544 us -> 485 us (0.89)
  waiting for transfers between devices: 232 us -> 181 us
  starting transfers between devices: 46.2 us -> 71.4 us
  matrix products: 124 us -> 113 us
  other arithmetic: 67.4 us -> 57.2 us
  local copies, waits for them, and re-layouts: 42.9 us -> 32.9 us
    ppermute x37 -> x45, waiting for transfers between devices: 109 us -> 82.9 us  [swap(): return lax.ppermute(values, axis, [(i, i ^ mask) for i in range(count)])]
    ppermute x15, waiting for transfers between devices: 123 us -> 98.2 us  [shift(): lax.ppermute(values, axis, [(i, (i + by) % count) for i in range(count)])]
    ppermute x15, starting transfers between devices: 19.4 us -> 40.7 us  [shift(): lax.ppermute(values, axis, [(i, (i + by) % count) for i in range(count)])]
    another operation x16 -> x0, local copies, waits for them, and re-layouts: 16.1 us -> none  [the longest x5 9.18 us: sum_over_col(): jnp.stack([p[at:at + half // 2] for p in parts]) + got[:, at:at + half // 2]]
    slice x0 -> x12, local copies, waits for them, and re-layouts: none -> 12.2 us  [sum_over_col(): got = swap(part[half:], 'col', 1)]
    another operation x12 -> x6, other arithmetic: 12 us -> 0.58 us
    dot_general x12, matrix products: 91.4 us -> 81.9 us  [matmul(): return jnp.dot(left, right, preferred_element_type=jnp.float32)]
    convert_element_type x14 -> x20, other arithmetic: 21.7 us -> 29.7 us  [the longest x8 8.18 us: pack(): return coded(values) if form == 'up' else values.astype(jnp.bfloat16)]
  transfers between devices with their start and end apart: 52 -> 60, of which waited for: 22 -> 24; matrix products, arithmetic and copies ran while one was open for 38% -> 36% of each run, Pallas kernels for 0% -> 0%
where the time goes in v5:
time: 485 us; the launch traced here: 480 us
  waiting for transfers between devices  181 us (37%)
  matrix products  113 us (23%)
  starting transfers between devices  71.4 us (15%)
  other arithmetic  57.2 us (12%)
  local copies, waits for them, and re-layouts  32.9 us (7%)
  Pallas kernels  22.5 us (5%)
    ppermute x15, waiting for transfers between devices, shift(): lax.ppermute(values, axis, [(i, (i + by) % count) for i in range(count)])  98.2 us
    ppermute x45, waiting for transfers between devices, swap(): return lax.ppermute(values, axis, [(i, i ^ mask) for i in range(count)])  82.9 us
    dot_general x12, matrix products, matmul(): return jnp.dot(left, right, preferred_element_type=jnp.float32)  81.9 us
    ppermute x15, starting transfers between devices, shift(): lax.ppermute(values, axis, [(i, (i + by) % count) for i in range(count)])  40.7 us
    dot_general x4, matrix products, times_down(): lax.dot_general(left, w_down, (((1,), (1,)), ((), ())), preferred_element...  31.4 us
    ppermute x45, starting transfers between devices, swap(): return lax.ppermute(values, axis, [(i, i ^ mask) for i in range(count)])  30.7 us
    pallas_call x1, Pallas kernels, last_product(): pl.pallas_call(functools.partial(last_kernel, 1.0 / tokens, len(turned)),...  22.5 us
    concatenate x12, other arithmetic, joined(): jnp.concatenate(pieces[j * per_group:(j + 1) * per_group], axis=1)  18.4 us
  transfers between devices with their start and end apart: 60, of which 24 were waited for; matrix products, arithmetic and copies ran while one was open for 36% of the time, Pallas kernels for 0%

profile of v5, /device:TPU:0, one launch (start us, length us, event | category | flops | bytes accessed | tf_op | source)
XLA Modules:
  0.0 480.1 jit_solution(2948102777572138657)
XLA Ops:
  2.2 3.1 collective-permute-start
  5.3 14.1 %collective-permute-done = bf16[4,32,2048]{2,1,0:T(8,128)(2,1)} collective-permute-done((bf16[4,32,2048]{2,1,0:T(8,128)(2,1)S(1)}, bf16[4,32,2048]{2,1,0:T(8,128)(2,1)}, u32[]{:S(2)}, u32[]{:S(2)}) %collective-permute-start) | collective-permute-done | bytes 524320 | tf_op jit(solution)/shard_map/ppermute | solution.py:41
  20.6 7.8 %fusion.100 = f32[256,3584]{1,0:T(8,128)S(1)} fusion(bf16[256,2048]{1,0:T(8,128)(2,1)S(1)} %bitcast.143, bf16[2048,3584]{1,0:T(8,128)(2,1)} %param.8), kind=kOutput, calls=%fused_computation.206 | convolution fusion | flops 3758096384 | bytes 19398656 | tf_op jit(solution)/shard_map/dot_general | solution.py:19
  29.5 3.9 fusion.102
  38.9 11.8 %collective-permute-done.3 = bf16[4,32,2048]{2,1,0:T(8,128)(2,1)S(1)} collective-permute-done((bf16[4,32,2048]{2,1,0:T(8,128)(2,1)S(1)}, bf16[4,32,2048]{2,1,0:T(8,128)(2,1)S(1)}, u32[]{:S(2)}, u32[]{:S(2)}) %collective-permute-start.3) | collective-permute-done | bytes 524320 | tf_op jit(solution)/shard_map/ppermute | solution.py:41
  50.8 20.6 %collective-permute-done.1 = bf16[4,32,2048]{2,1,0:T(8,128)(2,1)} collective-permute-done((bf16[4,32,2048]{2,1,0:T(8,128)(2,1)S(1)}, bf16[4,32,2048]{2,1,0:T(8,128)(2,1)}, u32[]{:S(2)}, u32[]{:S(2)}) %collective-permute-start.1) | collective-permute-done | bytes 524320 | tf_op jit(solution)/shard_map/ppermute | solution.py:41
  73.9 7.5 %fusion.103 = f32[256,3584]{1,0:T(8,128)S(1)} fusion(bf16[256,2048]{1,0:T(8,128)(2,1)S(1)} %bitcast.145, bf16[2048,3584]{1,0:T(8,128)(2,1)} %param.10), kind=kOutput, calls=%fused_computation.209 | convolution fusion | flops 3758096384 | bytes 19398656 | tf_op jit(solution)/shard_map/dot_general | solution.py:19
  84.4 3.9 fusion.101
  93.4 2.9 dynamic-slice_bitcast_fusion.3
  98.4 7.1 %collective-permute-done.15 = f16[64,3712]{1,0:T(8,128)(2,1)S(1)} collective-permute-done((f16[64,3712]{1,0:T(8,128)(2,1)S(1)}, f16[64,3712]{1,0:T(8,128)(2,1)S(1)}, u32[]{:S(2)}, u32[]{:S(2)}) %collective-permute-start.15) | collective-permute-done | bytes 475168 | tf_op jit(solution)/shard_map/ppermute | solution.py:36
  111.6 7.6 %fusion.104 = f32[256,3584]{1,0:T(8,128)S(1)} fusion(bf16[256,2048]{1,0:T(8,128)(2,1)S(1)} %bitcast.141, bf16[2048,3584]{1,0:T(8,128)(2,1)} %param.8), kind=kOutput, calls=%fused_computation.210 | convolution fusion | flops 3758096384 | bytes 19398656 | tf_op jit(solution)/shard_map/dot_general | solution.py:19
  121.1 4.1 collective-permute-done.16
  125.2 2.8 fusion.58
  129.6 3.9 fusion.105
  134.9 9.3 %collective-permute-done.17 = bf16[64,3584]{1,0:T(8,128)(2,1)S(1)} collective-permute-done((bf16[64,3584]{1,0:T(8,128)(2,1)S(1)}, bf16[64,3584]{1,0:T(8,128)(2,1)S(1)}, u32[]{:S(2)}, u32[]{:S(2)}) %collective-permute-start.17) | collective-permute-done | bytes 458784 | tf_op jit(solution)/shard_map/ppermute | solution.py:36
  150.7 7.4 %fusion.107 = f32[256,3584]{1,0:T(8,128)S(1)} fusion(bf16[256,2048]{1,0:T(8,128)(2,1)S(1)} %bitcast.152, bf16[2048,3584]{1,0:T(8,128)(2,1)} %param.10), kind=kOutput, calls=%fused_computation.213 | convolution fusion | flops 3758096384 | bytes 19398656 | tf_op jit(solution)/shard_map/dot_general | solution.py:19
  164.7 7.3 %fusion.106 = f32[256,3584]{1,0:T(8,128)S(1)} fusion(bf16[256,2048]{1,0:T(8,128)(2,1)S(1)} %bitcast.153, bf16[2048,3584]{1,0:T(8,128)(2,1)} %param.10), kind=kOutput, calls=%fused_computation.212 | convolution fusion | flops 3758096384 | bytes 19398656 | tf_op jit(solution)/shard_map/dot_general | solution.py:19
  173.2 7.5 %convolution_convert_fusion.1 = bf16[256,2048]{1,0:T(8,128)(2,1)S(1)} fusion(bf16[3584,2048]{1,0:T(8,128)(2,1)} %param.9, bf16[128,3584]{1,0:T(8,128)(2,1)S(1)} %collective-permute-done.18, bf16[64,3584]{1,0:T(8,128)(2,1)S(1)} %copy-done.53, bf16[64,3584]{1,0:T(8,128)(2,1)S(1)} %copy-done.32), kind=kOutput, calls=%fused_computation.1 | convolution fusion | flops 3764125696 | bytes 17563648 | tf_op jit(solution)/shard_map/dot_general | solution.py:19
  181.0 2.9 collective-permute-done.11
  183.9 3.0 fusion.65
  188.6 3.9 collective-permute-start.19
  192.5 5.7 %collective-permute-done.12 = bf16[64,3584]{1,0:T(8,128)(2,1)S(1)} collective-permute-done((bf16[64,3584]{1,0:T(8,128)(2,1)S(1)}, bf16[64,3584]{1,0:T(8,128)(2,1)S(1)}, u32[]{:S(2)}, u32[]{:S(2)}) %collective-permute-start.12) | collective-permute-done | bytes 458784 | tf_op jit(solution)/shard_map/ppermute | solution.py:36
  204.1 7.5 %fusion = f32[256,2048]{1,0:T(8,128)S(1)} fusion(bf16[3584,2048]{1,0:T(8,128)(2,1)} %param.9, bf16[128,3584]{1,0:T(8,128)(2,1)S(1)} %collective-permute-done.13, bf16[64,3584]{1,0:T(8,128)(2,1)S(1)} %collective-permute-done.12, bf16[64,3584]{1,0:T(8,128)(2,1)S(1)} %get-tuple-element.55), kind=kOutput, calls=%fused_computation.2 | convolution fusion | flops 3763601408 | bytes 18612224 | tf_op jit(solution)/shard_map/dot_general | solution.py:19
  212.3 3.6 collective-permute-done.32
  216.0 4.2 collective-permute-start.21
  222.7 3.1 collective-permute-done.26
  228.2 6.9 %collective-permute-done.20 = bf16[4,32,2048]{2,1,0:T(8,128)(2,1)S(1)} collective-permute-done((bf16[4,32,2048]{2,1,0:T(8,128)(2,1)S(1)}, bf16[4,32,2048]{2,1,0:T(8,128)(2,1)S(1)}, u32[]{:S(2)}, u32[]{:S(2)}) %collective-permute-start.20) | collective-permute-done | bytes 524320 | tf_op jit(solution)/shard_map/ppermute | solution.py:41
  236.3 5.3 %collective-permute-start.38 = (bf16[4,32,2048]{2,1,0:T(8,128)(2,1)}, bf16[4,32,2048]{2,1,0:T(8,128)(2,1)}, u32[]{:S(2)}, u32[]{:S(2)}) collective-permute-start(bf16[4,32,2048]{2,1,0:T(8,128)(2,1)} %fusion.31), channel_id=1, source_target_pairs={{0,12},{4,0},{8,4},{12,8},{1,13},{5,1},{9,5},{13,9},{2,14},{6,2},{... | collective-permute-start | bytes 1572872 | tf_op jit(solution)/shard_map/ppermute | solution.py:41
  254.7 4.3 collective-permute-start.43
  259.0 7.3 %fusion.108 = f32[256,3584]{1,0:T(8,128)S(1)} fusion(bf16[256,2048]{1,0:T(8,128)(2,1)S(1)} %bitcast.149, bf16[3584,2048]{1,0:T(8,128)(2,1)} %param.9), kind=kOutput, calls=%fused_computation.214 | convolution fusion | flops 3758096384 | bytes 19398656 | tf_op jit(solution)/shard_map/dot_general | solution.py:23
  270.0 4.3 collective-permute-start.44
  274.3 9.7 %convolution_convert_fusion = bf16[256,2048]{1,0:T(8,128)(2,1)S(1)} fusion(bf16[3584,2048]{1,0:T(8,128)(2,1)} %param.9, bf16[128,3584]{1,0:T(8,128)(2,1)} %collective-permute-done.34, bf16[64,3584]{1,0:T(8,128)(2,1)} %collective-permute-done.33, bf16[64,3584]{1,0:T(8,128)(2,1)} %fusion.51), kind=kOutput, calls=%fused_computation | convolution fusion | flops 3764125696 | bytes 17563648 | tf_op jit(solution)/shard_map/dot_general | solution.py:19
  285.1 7.8 %fusion.11 = f32[256,2048]{1,0:T(8,128)S(1)} fusion(bf16[3584,2048]{1,0:T(8,128)(2,1)} %param.9, bf16[128,3584]{1,0:T(8,128)(2,1)} %collective-permute-done.28, bf16[64,3584]{1,0:T(8,128)(2,1)} %collective-permute-done.27, bf16[64,3584]{1,0:T(8,128)(2,1)} %fusion.55), kind=kOutput, calls=%fused_computation.13 | convolution fusion | flops 3763601408 | bytes 18612224 | tf_op jit(solution)/shard_map/dot_general | solution.py:19
  296.4 7.3 %fusion.109 = f32[256,3584]{1,0:T(8,128)S(1)} fusion(bf16[256,2048]{1,0:T(8,128)(2,1)S(1)} %bitcast.151, bf16[3584,2048]{1,0:T(8,128)(2,1)} %param.9), kind=kOutput, calls=%fused_computation.215 | convolution fusion | flops 3758096384 | bytes 19398656 | tf_op jit(solution)/shard_map/dot_general | solution.py:23
  305.2 23.0 %collective-permute-done.36 = bf16[4,32,2048]{2,1,0:T(8,128)(2,1)} collective-permute-done((bf16[4,32,2048]{2,1,0:T(8,128)(2,1)}, bf16[4,32,2048]{2,1,0:T(8,128)(2,1)}, u32[]{:S(2)}, u32[]{:S(2)}) %collective-permute-start.36) | collective-permute-done | bytes 524320 | tf_op jit(solution)/shard_map/ppermute | solution.py:41
  328.2 2.6 fusion.26
  341.7 10.2 %collective-permute-done.49 = bf16[4,32,2048]{2,1,0:T(8,128)(2,1)} collective-permute-done((bf16[4,32,2048]{2,1,0:T(8,128)(2,1)}, bf16[4,32,2048]{2,1,0:T(8,128)(2,1)}, u32[]{:S(2)}, u32[]{:S(2)}) %collective-permute-start.49) | collective-permute-done | bytes 524320 | tf_op jit(solution)/shard_map/ppermute | solution.py:41
  351.9 7.7 %collective-permute-start.54 = (bf16[4,32,2048]{2,1,0:T(8,128)(2,1)}, bf16[4,32,2048]{2,1,0:T(8,128)(2,1)}, u32[]{:S(2)}, u32[]{:S(2)}) collective-permute-start(bf16[4,32,2048]{2,1,0:T(8,128)(2,1)} %collective-permute-done.49), channel_id=1, source_target_pairs={{0,12},{4,0},{8,4},{12,8},{1,13},{5,1},{9,5},{13,9},{2,14},{6,2},{... | collective-permute-start | bytes 1572872 | tf_op jit(solution)/shard_map/ppermute | solution.py:41
  364.5 6.8 %collective-permute-done.54 = bf16[4,32,2048]{2,1,0:T(8,128)(2,1)} collective-permute-done((bf16[4,32,2048]{2,1,0:T(8,128)(2,1)}, bf16[4,32,2048]{2,1,0:T(8,128)(2,1)}, u32[]{:S(2)}, u32[]{:S(2)}) %collective-permute-start.54) | collective-permute-done | bytes 524320 | tf_op jit(solution)/shard_map/ppermute | solution.py:41
  371.3 3.4 collective-permute-start.55
  374.7 7.6 %fusion.110 = f32[256,3584]{1,0:T(8,128)S(1)} fusion(bf16[256,2048]{1,0:T(8,128)(2,1)} %bitcast.147, bf16[3584,2048]{1,0:T(8,128)(2,1)} %param.9), kind=kOutput, calls=%fused_computation.216 | convolution fusion | flops 3758096384 | bytes 19398656 | tf_op jit(solution)/shard_map/dot_general | solution.py:23
  389.2 9.1 %fusion.111 = f32[256,3584]{1,0:T(8,128)} fusion(bf16[256,2048]{1,0:T(8,128)(2,1)S(1)} %bitcast.148, bf16[3584,2048]{1,0:T(8,128)(2,1)} %param.9), kind=kOutput, calls=%fused_computation.217 | convolution fusion | flops 3758096384 | bytes 19398656 | tf_op jit(solution)/shard_map/dot_general | solution.py:23
  407.6 8.7 %collective-permute-done.47 = bf16[64,3584]{1,0:T(8,128)(2,1)S(1)} collective-permute-done((bf16[64,3584]{1,0:T(8,128)(2,1)S(1)}, bf16[64,3584]{1,0:T(8,128)(2,1)S(1)}, u32[]{:S(2)}, u32[]{:S(2)}) %collective-permute-start.47) | collective-permute-done | bytes 458784 | tf_op jit(solution)/shard_map/ppermute | solution.py:36
  417.7 8.5 %collective-permute-done.51 = bf16[64,3584]{1,0:T(8,128)(2,1)S(1)} collective-permute-done((bf16[64,3584]{1,0:T(8,128)(2,1)S(1)}, bf16[64,3584]{1,0:T(8,128)(2,1)S(1)}, u32[]{:S(2)}, u32[]{:S(2)}) %collective-permute-start.51) | collective-permute-done | bytes 458784 | tf_op jit(solution)/shard_map/ppermute | solution.py:36
  428.6 7.4 %collective-permute-done.57 = bf16[64,3584]{1,0:T(8,128)(2,1)S(1)} collective-permute-done((bf16[64,3584]{1,0:T(8,128)(2,1)S(1)}, bf16[64,3584]{1,0:T(8,128)(2,1)S(1)}, u32[]{:S(2)}, u32[]{:S(2)}) %collective-permute-start.57) | collective-permute-done | bytes 458784 | tf_op jit(solution)/shard_map/ppermute | solution.py:36
  437.3 8.5 %collective-permute-done.52 = bf16[64,3584]{1,0:T(8,128)(2,1)S(1)} collective-permute-done((bf16[64,3584]{1,0:T(8,128)(2,1)S(1)}, bf16[64,3584]{1,0:T(8,128)(2,1)S(1)}, u32[]{:S(2)}, u32[]{:S(2)}) %collective-permute-start.52) | collective-permute-done | bytes 458784 | tf_op jit(solution)/shard_map/ppermute | solution.py:36
  446.0 8.5 %collective-permute-done.58 = bf16[64,3584]{1,0:T(8,128)(2,1)S(1)} collective-permute-done((bf16[64,3584]{1,0:T(8,128)(2,1)S(1)}, bf16[64,3584]{1,0:T(8,128)(2,1)S(1)}, u32[]{:S(2)}, u32[]{:S(2)}) %collective-permute-start.58) | collective-permute-done | bytes 458784 | tf_op jit(solution)/shard_map/ppermute | solution.py:36
  457.2 22.5 %shard_map.64 = f32[2048,3584]{1,0:T(8,128)} custom-call(bf16[2048,256]{1,0:T(8,128)(2,1)S(1)} %bitcast.129, bf16[2048,256]{1,0:T(8,128)(2,1)S(1)} %bitcast.128, bf16[2048,256]{1,0:T(8,128)(2,1)S(1)} %bitcast.131, bf16[2048,256]{1,0:T(8,128)(2,1)S(1)} %bitcast.130, bf16[256,3584]{1,0:T(8,128)(2,1)S(1)} %pad_maximum_fusion.refs_4_, ...), custom_call_target="tpu_custom_call" | custom-call | flops 15032385536 | bytes 40894464 | tf_op jit(solution)/shard_map/pallas_call | solution.py:88
  (314 shorter events, 124.1 us)
Async XLA Ops:
  2.2 17.1 %collective-permute-start = (bf16[4,32,2048]{2,1,0:T(8,128)(2,1)S(1)}, bf16[4,32,2048]{2,1,0:T(8,128)(2,1)}, u32[]{:S(2)}, u32[]{:S(2)}) collective-permute-start(bf16[4,32,2048]{2,1,0:T(8,128)(2,1)S(1)} %pad_maximum_fusion.24), channel_id=1, source_target_pairs={{0,4},{4,8},{8,12},{12,0},{1,5},{5,9},{9,13},{13,1},{2,6},{6,10},{... | collective-permute-start | bytes 1572872 | tf_op jit(solution)/shard_map/ppermute | solution.py:41
  34.9 36.5 %collective-permute-start.6 = (f32[128,3584]{1,0:T(8,128)}, f32[128,3584]{1,0:T(8,128)}, u32[]{:S(2)}, u32[]{:S(2)}) collective-permute-start(f32[128,3584]{1,0:T(8,128)} %slice.327), channel_id=1, source_target_pairs={{0,1},{1,0},{2,3},{3,2},{4,5},{5,4},{6,7},{7,6},{8,9},{9,8},{10,11... | collective-permute-start | bytes 5505032 | tf_op jit(solution)/shard_map/ppermute | solution.py:36
  34.9 15.9 %collective-permute-start.3 = (bf16[4,32,2048]{2,1,0:T(8,128)(2,1)S(1)}, bf16[4,32,2048]{2,1,0:T(8,128)(2,1)S(1)}, u32[]{:S(2)}, u32[]{:S(2)}) collective-permute-start(bf16[4,32,2048]{2,1,0:T(8,128)(2,1)S(1)} %pad_maximum_fusion.24), channel_id=1, source_target_pairs={{0,12},{4,0},{8,4},{12,8},{1,13},{5,1},{9,5},{13,9},{2,14},{6,2},{... | collective-permute-start | bytes 1572872 | tf_op jit(solution)/shard_map/ppermute | solution.py:41
  37.1 34.3 %collective-permute-start.1 = (bf16[4,32,2048]{2,1,0:T(8,128)(2,1)S(1)}, bf16[4,32,2048]{2,1,0:T(8,128)(2,1)}, u32[]{:S(2)}, u32[]{:S(2)}) collective-permute-start(bf16[4,32,2048]{2,1,0:T(8,128)(2,1)S(1)} %pad_maximum_fusion.24), channel_id=1, source_target_pairs={{0,8},{4,12},{8,0},{12,4},{1,9},{5,13},{9,1},{13,5},{2,10},{6,14},... | collective-permute-start | bytes 1572872 | tf_op jit(solution)/shard_map/ppermute | solution.py:41
  82.9 22.8 %collective-permute-start.7 = (f32[128,3584]{1,0:T(8,128)}, f32[128,3584]{1,0:T(8,128)}, u32[]{:S(2)}, u32[]{:S(2)}) collective-permute-start(f32[128,3584]{1,0:T(8,128)} %slice.330), channel_id=1, source_target_pairs={{0,1},{1,0},{2,3},{3,2},{4,5},{5,4},{6,7},{7,6},{8,9},{9,8},{10,11... | collective-permute-start | bytes 5505032 | tf_op jit(solution)/shard_map/ppermute | solution.py:36
  91.7 17.1 %collective-permute-start.4 = (f32[128,3584]{1,0:T(8,128)}, f32[128,3584]{1,0:T(8,128)}, u32[]{:S(2)}, u32[]{:S(2)}) collective-permute-start(f32[128,3584]{1,0:T(8,128)} %slice.322), channel_id=1, source_target_pairs={{0,1},{1,0},{2,3},{3,2},{4,5},{5,4},{6,7},{7,6},{8,9},{9,8},{10,11... | collective-permute-start | bytes 5505032 | tf_op jit(solution)/shard_map/ppermute | solution.py:36
  96.3 52.7 %collective-permute-start.30 = (bf16[4,32,2048]{2,1,0:T(8,128)(2,1)}, bf16[4,32,2048]{2,1,0:T(8,128)(2,1)}, u32[]{:S(2)}, u32[]{:S(2)}) collective-permute-start(bf16[4,32,2048]{2,1,0:T(8,128)(2,1)} %collective-permute-done), channel_id=1, source_target_pairs={{0,16},{16,0},{1,17},{17,1},{2,18},{18,2},{3,19},{19,3},{4,20},{20... | collective-permute-start | bytes 1572872 | tf_op jit(solution)/shard_map/ppermute | solution.py:36
  97.9 23.1 %collective-permute-start.14 = (f16[64,3584]{1,0:T(8,128)(2,1)S(1)}, f16[64,3584]{1,0:T(8,128)(2,1)S(1)}, u32[]{:S(2)}, u32[]{:S(2)}) collective-permute-start(f16[64,3584]{1,0:T(8,128)(2,1)S(1)} %copy-done.54), channel_id=1, source_target_pairs={{0,2},{1,3},{2,0},{3,1},{4,6},{5,7},{6,4},{7,5},{8,10},{9,11},{10,... | collective-permute-start | bytes 1376264 | tf_op jit(solution)/shard_map/ppermute | solution.py:36
  107.2 18.0 %collective-permute-start.16 = (bf16[64,3584]{1,0:T(8,128)(2,1)S(1)}, bf16[64,3584]{1,0:T(8,128)(2,1)S(1)}, u32[]{:S(2)}, u32[]{:S(2)}) collective-permute-start(bf16[64,3584]{1,0:T(8,128)(2,1)S(1)} %fusion.68), channel_id=1, source_target_pairs={{0,2},{1,3},{2,0},{3,1},{4,6},{5,7},{6,4},{7,5},{8,10},{9,11},{10,... | collective-permute-start | bytes 1376264 | tf_op jit(solution)/shard_map/ppermute | solution.py:36
  111.0 70.0 %collective-permute-start.5 = (f16[64,3584]{1,0:T(8,128)(2,1)}, f16[64,3584]{1,0:T(8,128)(2,1)}, u32[]{:S(2)}, u32[]{:S(2)}) collective-permute-start(f16[64,3584]{1,0:T(8,128)(2,1)} %fusion.72), channel_id=1, source_target_pairs={{0,2},{1,3},{2,0},{3,1},{4,6},{5,7},{6,4},{7,5},{8,10},{9,11},{10,... | collective-permute-start | bytes 1376264 | tf_op jit(solution)/shard_map/ppermute | solution.py:36
  119.3 43.8 %collective-permute-start.22 = (bf16[4,32,2048]{2,1,0:T(8,128)(2,1)}, bf16[4,32,2048]{2,1,0:T(8,128)(2,1)}, u32[]{:S(2)}, u32[]{:S(2)}) collective-permute-start(bf16[4,32,2048]{2,1,0:T(8,128)(2,1)} %collective-permute-done.1), channel_id=1, source_target_pairs={{0,16},{16,0},{1,17},{17,1},{2,18},{18,2},{3,19},{19,3},{4,20},{20... | collective-permute-start | bytes 1572872 | tf_op jit(solution)/shard_map/ppermute | solution.py:36
  121.0 25.8 %collective-permute-start.8 = (f32[128,3584]{1,0:T(8,128)S(1)}, f32[128,3584]{1,0:T(8,128)S(1)}, u32[]{:S(2)}, u32[]{:S(2)}) collective-permute-start(f32[128,3584]{1,0:T(8,128)S(1)} %slice.333), channel_id=1, source_target_pairs={{0,1},{1,0},{2,3},{3,2},{4,5},{5,4},{6,7},{7,6},{8,9},{9,8},{10,11... | collective-permute-start | bytes 5505032 | tf_op jit(solution)/shard_map/ppermute | solution.py:36
  128.0 16.2 %collective-permute-start.17 = (bf16[64,3584]{1,0:T(8,128)(2,1)S(1)}, bf16[64,3584]{1,0:T(8,128)(2,1)S(1)}, u32[]{:S(2)}, u32[]{:S(2)}) collective-permute-start(bf16[64,3584]{1,0:T(8,128)(2,1)S(1)} %get-tuple-element.53), channel_id=1, source_target_pairs={{0,2},{1,3},{2,0},{3,1},{4,6},{5,7},{6,4},{7,5},{8,10},{9,11},{10,... | collective-permute-start | bytes 1376264 | tf_op jit(solution)/shard_map/ppermute | solution.py:36
  144.3 17.2 %collective-permute-start.24 = (bf16[4,32,2048]{2,1,0:T(8,128)(2,1)S(1)}, bf16[4,32,2048]{2,1,0:T(8,128)(2,1)S(1)}, u32[]{:S(2)}, u32[]{:S(2)}) collective-permute-start(bf16[4,32,2048]{2,1,0:T(8,128)(2,1)S(1)} %copy-done.27), channel_id=1, source_target_pairs={{0,16},{16,0},{1,17},{17,1},{2,18},{18,2},{3,19},{19,3},{4,20},{20... | collective-permute-start | bytes 1572872 | tf_op jit(solution)/shard_map/ppermute | solution.py:36
  149.1 62.6 %collective-permute-start.29 = (f32[64,3584]{1,0:T(8,128)S(1)}, f32[64,3584]{1,0:T(8,128)S(1)}, u32[]{:S(2)}, u32[]{:S(2)}) collective-permute-start(f32[64,3584]{1,0:T(8,128)S(1)} %get-tuple-element.54), channel_id=1, source_target_pairs={{0,16},{16,0},{1,17},{17,1},{2,18},{18,2},{3,19},{19,3},{4,20},{20... | collective-permute-start | bytes 2752520 | tf_op jit(solution)/shard_map/ppermute | solution.py:36
  161.5 19.2 %collective-permute-start.9 = (f16[64,3712]{1,0:T(8,128)(2,1)S(1)}, f16[64,3712]{1,0:T(8,128)(2,1)S(1)}, u32[]{:S(2)}, u32[]{:S(2)}) collective-permute-start(f16[64,3712]{1,0:T(8,128)(2,1)S(1)} %copy-done.51), channel_id=1, source_target_pairs={{0,2},{1,3},{2,0},{3,1},{4,6},{5,7},{6,4},{7,5},{8,10},{9,11},{10,... | collective-permute-start | bytes 1425416 | tf_op jit(solution)/shard_map/ppermute | solution.py:36
  163.0 20.9 %collective-permute-start.11 = (bf16[64,3584]{1,0:T(8,128)(2,1)S(1)}, bf16[64,3584]{1,0:T(8,128)(2,1)S(1)}, u32[]{:S(2)}, u32[]{:S(2)}) collective-permute-start(bf16[64,3584]{1,0:T(8,128)(2,1)S(1)} %fusion.62), channel_id=1, source_target_pairs={{0,2},{1,3},{2,0},{3,1},{4,6},{5,7},{6,4},{7,5},{8,10},{9,11},{10,... | collective-permute-start | bytes 1376264 | tf_op jit(solution)/shard_map/ppermute | solution.py:36
  172.2 26.1 %collective-permute-start.31 = (f32[128,3584]{1,0:T(8,128)S(1)}, f32[128,3584]{1,0:T(8,128)S(1)}, u32[]{:S(2)}, u32[]{:S(2)}) collective-permute-start(f32[128,3584]{1,0:T(8,128)S(1)} %slice.369), channel_id=1, source_target_pairs={{0,1},{1,0},{2,3},{3,2},{4,5},{5,4},{6,7},{7,6},{8,9},{9,8},{10,11... | collective-permute-start | bytes 5505032 | tf_op jit(solution)/shard_map/ppermute | solution.py:36
  180.7 19.3 %collective-permute-start.25 = (f32[128,3584]{1,0:T(8,128)S(1)}, f32[128,3584]{1,0:T(8,128)S(1)}, u32[]{:S(2)}, u32[]{:S(2)}) collective-permute-start(f32[128,3584]{1,0:T(8,128)S(1)} %slice.363), channel_id=1, source_target_pairs={{0,1},{1,0},{2,3},{3,2},{4,5},{5,4},{6,7},{7,6},{8,9},{9,8},{10,11... | collective-permute-start | bytes 5505032 | tf_op jit(solution)/shard_map/ppermute | solution.py:36
  188.6 39.6 %collective-permute-start.19 = (bf16[4,32,2048]{2,1,0:T(8,128)(2,1)S(1)}, bf16[4,32,2048]{2,1,0:T(8,128)(2,1)S(1)}, u32[]{:S(2)}, u32[]{:S(2)}) collective-permute-start(bf16[4,32,2048]{2,1,0:T(8,128)(2,1)S(1)} %get-tuple-element.79), channel_id=1, source_target_pairs={{0,12},{4,0},{8,4},{12,8},{1,13},{5,1},{9,5},{13,9},{2,14},{6,2},{... | collective-permute-start | bytes 1572872 | tf_op jit(solution)/shard_map/ppermute | solution.py:41
  198.3 36.9 %collective-permute-start.20 = (bf16[4,32,2048]{2,1,0:T(8,128)(2,1)S(1)}, bf16[4,32,2048]{2,1,0:T(8,128)(2,1)S(1)}, u32[]{:S(2)}, u32[]{:S(2)}) collective-permute-start(bf16[4,32,2048]{2,1,0:T(8,128)(2,1)S(1)} %get-tuple-element.80), channel_id=1, source_target_pairs={{0,8},{4,12},{8,0},{12,4},{1,9},{5,13},{9,1},{13,5},{2,10},{6,14},... | collective-permute-start | bytes 1572872 | tf_op jit(solution)/shard_map/ppermute | solution.py:41
  198.3 22.7 %collective-permute-start.23 = (f32[64,3584]{1,0:T(8,128)S(1)}, f32[64,3584]{1,0:T(8,128)S(1)}, u32[]{:S(2)}, u32[]{:S(2)}) collective-permute-start(f32[64,3584]{1,0:T(8,128)S(1)} %get-tuple-element.56), channel_id=1, source_target_pairs={{0,16},{16,0},{1,17},{17,1},{2,18},{18,2},{3,19},{19,3},{4,20},{20... | collective-permute-start | bytes 2752520 | tf_op jit(solution)/shard_map/ppermute | solution.py:36
  211.7 14.1 %collective-permute-start.26 = (bf16[64,3584]{1,0:T(8,128)(2,1)S(1)}, bf16[64,3584]{1,0:T(8,128)(2,1)S(1)}, u32[]{:S(2)}, u32[]{:S(2)}) collective-permute-start(bf16[64,3584]{1,0:T(8,128)(2,1)S(1)} %fusion.52), channel_id=1, source_target_pairs={{0,2},{1,3},{2,0},{3,1},{4,6},{5,7},{6,4},{7,5},{8,10},{9,11},{10,... | collective-permute-start | bytes 1376264 | tf_op jit(solution)/shard_map/ppermute | solution.py:36
  216.0 19.2 %collective-permute-start.21 = (bf16[4,32,2048]{2,1,0:T(8,128)(2,1)S(1)}, bf16[4,32,2048]{2,1,0:T(8,128)(2,1)S(1)}, u32[]{:S(2)}, u32[]{:S(2)}) collective-permute-start(bf16[4,32,2048]{2,1,0:T(8,128)(2,1)S(1)} %fusion.74), channel_id=1, source_target_pairs={{0,4},{4,8},{8,12},{12,0},{1,5},{5,9},{9,13},{13,1},{2,6},{6,10},{... | collective-permute-start | bytes 1572872 | tf_op jit(solution)/shard_map/ppermute | solution.py:41
  221.1 25.8 %collective-permute-start.33 = (bf16[64,3584]{1,0:T(8,128)(2,1)}, bf16[64,3584]{1,0:T(8,128)(2,1)}, u32[]{:S(2)}, u32[]{:S(2)}) collective-permute-start(bf16[64,3584]{1,0:T(8,128)(2,1)} %fusion.51), channel_id=1, source_target_pairs={{0,2},{1,3},{2,0},{3,1},{4,6},{5,7},{6,4},{7,5},{8,10},{9,11},{10,... | collective-permute-start | bytes 1376264 | tf_op jit(solution)/shard_map/ppermute | solution.py:36
  226.7 22.3 %collective-permute-start.27 = (bf16[64,3584]{1,0:T(8,128)(2,1)}, bf16[64,3584]{1,0:T(8,128)(2,1)}, u32[]{:S(2)}, u32[]{:S(2)}) collective-permute-start(bf16[64,3584]{1,0:T(8,128)(2,1)} %fusion.55), channel_id=1, source_target_pairs={{0,2},{1,3},{2,0},{3,1},{4,6},{5,7},{6,4},{7,5},{8,10},{9,11},{10,... | collective-permute-start | bytes 1376264 | tf_op jit(solution)/shard_map/ppermute | solution.py:36
  236.3 17.1 %collective-permute-start.38 = (bf16[4,32,2048]{2,1,0:T(8,128)(2,1)}, bf16[4,32,2048]{2,1,0:T(8,128)(2,1)}, u32[]{:S(2)}, u32[]{:S(2)}) collective-permute-start(bf16[4,32,2048]{2,1,0:T(8,128)(2,1)} %fusion.31), channel_id=1, source_target_pairs={{0,12},{4,0},{8,4},{12,8},{1,13},{5,1},{9,5},{13,9},{2,14},{6,2},{... | collective-permute-start | bytes 1572872 | tf_op jit(solution)/shard_map/ppermute | solution.py:41
  249.0 25.2 %collective-permute-start.34 = (bf16[128,3584]{1,0:T(8,128)(2,1)}, bf16[128,3584]{1,0:T(8,128)(2,1)}, u32[]{:S(2)}, u32[]{:S(2)}) collective-permute-start(bf16[128,3584]{1,0:T(8,128)(2,1)} %pad_maximum_fusion.19), channel_id=1, source_target_pairs={{0,1},{1,0},{2,3},{3,2},{4,5},{5,4},{6,7},{7,6},{8,9},{9,8},{10,11... | collective-permute-start | bytes 2752520 | tf_op jit(solution)/shard_map/ppermute | solution.py:36
  250.3 34.8 %collective-permute-start.28 = (bf16[128,3584]{1,0:T(8,128)(2,1)S(1)}, bf16[128,3584]{1,0:T(8,128)(2,1)}, u32[]{:S(2)}, u32[]{:S(2)}) collective-permute-start(bf16[128,3584]{1,0:T(8,128)(2,1)S(1)} %pad_maximum_fusion.18), channel_id=1, source_target_pairs={{0,1},{1,0},{2,3},{3,2},{4,5},{5,4},{6,7},{7,6},{8,9},{9,8},{10,11... | collective-permute-start | bytes 2752520 | tf_op jit(solution)/shard_map/ppermute | solution.py:36
  254.7 15.3 %collective-permute-start.43 = (bf16[4,32,2048]{2,1,0:T(8,128)(2,1)}, bf16[4,32,2048]{2,1,0:T(8,128)(2,1)}, u32[]{:S(2)}, u32[]{:S(2)}) collective-permute-start(bf16[4,32,2048]{2,1,0:T(8,128)(2,1)} %collective-permute-done.38), channel_id=1, source_target_pairs={{0,12},{4,0},{8,4},{12,8},{1,13},{5,1},{9,5},{13,9},{2,14},{6,2},{... | collective-permute-start | bytes 1572872 | tf_op jit(solution)/shard_map/ppermute | solution.py:41
  267.8 66.6 %collective-permute-start.39 = (f32[128,3584]{1,0:T(8,128)}, f32[128,3584]{1,0:T(8,128)}, u32[]{:S(2)}, u32[]{:S(2)}) collective-permute-start(f32[128,3584]{1,0:T(8,128)} %slice.377), channel_id=1, source_target_pairs={{0,1},{1,0},{2,3},{3,2},{4,5},{5,4},{6,7},{7,6},{8,9},{9,8},{10,11... | collective-permute-start | bytes 5505032 | tf_op jit(solution)/shard_map/ppermute | solution.py:36
  270.0 25.3 %collective-permute-start.44 = (bf16[4,32,2048]{2,1,0:T(8,128)(2,1)}, bf16[4,32,2048]{2,1,0:T(8,128)(2,1)S(1)}, u32[]{:S(2)}, u32[]{:S(2)}) collective-permute-start(bf16[4,32,2048]{2,1,0:T(8,128)(2,1)} %collective-permute-done.43), channel_id=1, source_target_pairs={{0,12},{4,0},{8,4},{12,8},{1,13},{5,1},{9,5},{13,9},{2,14},{6,2},{... | collective-permute-start | bytes 1572872 | tf_op jit(solution)/shard_map/ppermute | solution.py:41
  285.1 20.2 %collective-permute-start.35 = (bf16[4,32,2048]{2,1,0:T(8,128)(2,1)}, bf16[4,32,2048]{2,1,0:T(8,128)(2,1)}, u32[]{:S(2)}, u32[]{:S(2)}) collective-permute-start(bf16[4,32,2048]{2,1,0:T(8,128)(2,1)} %get-tuple-element.69), channel_id=1, source_target_pairs={{0,12},{4,0},{8,4},{12,8},{1,13},{5,1},{9,5},{13,9},{2,14},{6,2},{... | collective-permute-start | bytes 1572872 | tf_op jit(solution)/shard_map/ppermute | solution.py:41
  285.1 43.1 %collective-permute-start.36 = (bf16[4,32,2048]{2,1,0:T(8,128)(2,1)}, bf16[4,32,2048]{2,1,0:T(8,128)(2,1)}, u32[]{:S(2)}, u32[]{:S(2)}) collective-permute-start(bf16[4,32,2048]{2,1,0:T(8,128)(2,1)} %get-tuple-element.70), channel_id=1, source_target_pairs={{0,8},{4,12},{8,0},{12,4},{1,9},{5,13},{9,1},{13,5},{2,10},{6,14},... | collective-permute-start | bytes 1572872 | tf_op jit(solution)/shard_map/ppermute | solution.py:41
  292.9 35.2 %collective-permute-start.37 = (bf16[4,32,2048]{2,1,0:T(8,128)(2,1)S(1)}, bf16[4,32,2048]{2,1,0:T(8,128)(2,1)}, u32[]{:S(2)}, u32[]{:S(2)}) collective-permute-start(bf16[4,32,2048]{2,1,0:T(8,128)(2,1)S(1)} %fusion.75), channel_id=1, source_target_pairs={{0,4},{4,8},{8,12},{12,0},{1,5},{5,9},{9,13},{13,1},{2,6},{6,10},{... | collective-permute-start | bytes 1572872 | tf_op jit(solution)/shard_map/ppermute | solution.py:41
  305.2 81.3 %collective-permute-start.45 = (f32[128,3584]{1,0:T(8,128)}, f32[128,3584]{1,0:T(8,128)}, u32[]{:S(2)}, u32[]{:S(2)}) collective-permute-start(f32[128,3584]{1,0:T(8,128)} %slice.382), channel_id=1, source_target_pairs={{0,1},{1,0},{2,3},{3,2},{4,5},{5,4},{6,7},{7,6},{8,9},{9,8},{10,11... | collective-permute-start | bytes 5505032 | tf_op jit(solution)/shard_map/ppermute | solution.py:36
  330.8 21.1 %collective-permute-start.49 = (bf16[4,32,2048]{2,1,0:T(8,128)(2,1)}, bf16[4,32,2048]{2,1,0:T(8,128)(2,1)}, u32[]{:S(2)}, u32[]{:S(2)}) collective-permute-start(bf16[4,32,2048]{2,1,0:T(8,128)(2,1)} %fusion.26), channel_id=1, source_target_pairs={{0,12},{4,0},{8,4},{12,8},{1,13},{5,1},{9,5},{13,9},{2,14},{6,2},{... | collective-permute-start | bytes 1572872 | tf_op jit(solution)/shard_map/ppermute | solution.py:41
  336.8 25.1 %collective-permute-start.40 = (bf16[64,3584]{1,0:T(8,128)(2,1)}, bf16[64,3584]{1,0:T(8,128)(2,1)}, u32[]{:S(2)}, u32[]{:S(2)}) collective-permute-start(bf16[64,3584]{1,0:T(8,128)(2,1)} %fusion.44), channel_id=1, source_target_pairs={{0,2},{1,3},{2,0},{3,1},{4,6},{5,7},{6,4},{7,5},{8,10},{9,11},{10,... | collective-permute-start | bytes 1376264 | tf_op jit(solution)/shard_map/ppermute | solution.py:36
  351.9 19.4 %collective-permute-start.54 = (bf16[4,32,2048]{2,1,0:T(8,128)(2,1)}, bf16[4,32,2048]{2,1,0:T(8,128)(2,1)}, u32[]{:S(2)}, u32[]{:S(2)}) collective-permute-start(bf16[4,32,2048]{2,1,0:T(8,128)(2,1)} %collective-permute-done.49), channel_id=1, source_target_pairs={{0,12},{4,0},{8,4},{12,8},{1,13},{5,1},{9,5},{13,9},{2,14},{6,2},{... | collective-permute-start | bytes 1572872 | tf_op jit(solution)/shard_map/ppermute | solution.py:41
  363.7 20.1 %collective-permute-start.41 = (bf16[64,3584]{1,0:T(8,128)(2,1)S(1)}, bf16[64,3584]{1,0:T(8,128)(2,1)S(1)}, u32[]{:S(2)}, u32[]{:S(2)}) collective-permute-start(bf16[64,3584]{1,0:T(8,128)(2,1)S(1)} %fusion.47), channel_id=1, source_target_pairs={{0,2},{1,3},{2,0},{3,1},{4,6},{5,7},{6,4},{7,5},{8,10},{9,11},{10,... | collective-permute-start | bytes 1376264 | tf_op jit(solution)/shard_map/ppermute | solution.py:36
  383.8 20.1 %collective-permute-start.50 = (f32[128,3584]{1,0:T(8,128)}, f32[128,3584]{1,0:T(8,128)}, u32[]{:S(2)}, u32[]{:S(2)}) collective-permute-start(f32[128,3584]{1,0:T(8,128)} %slice.387), channel_id=1, source_target_pairs={{0,1},{1,0},{2,3},{3,2},{4,5},{5,4},{6,7},{7,6},{8,9},{9,8},{10,11... | collective-permute-start | bytes 5505032 | tf_op jit(solution)/shard_map/ppermute | solution.py:36
  385.1 21.2 %collective-permute-start.42 = (bf16[128,3584]{1,0:T(8,128)(2,1)}, bf16[128,3584]{1,0:T(8,128)(2,1)}, u32[]{:S(2)}, u32[]{:S(2)}) collective-permute-start(bf16[128,3584]{1,0:T(8,128)(2,1)} %pad_maximum_fusion.20), channel_id=1, source_target_pairs={{0,1},{1,0},{2,3},{3,2},{4,5},{5,4},{6,7},{7,6},{8,9},{9,8},{10,11... | collective-permute-start | bytes 2752520 | tf_op jit(solution)/shard_map/ppermute | solution.py:36
  400.1 16.4 %collective-permute-start.56 = (f32[128,3584]{1,0:T(8,128)S(1)}, f32[128,3584]{1,0:T(8,128)S(1)}, u32[]{:S(2)}, u32[]{:S(2)}) collective-permute-start(f32[128,3584]{1,0:T(8,128)S(1)} %slice.392), channel_id=1, source_target_pairs={{0,1},{1,0},{2,3},{3,2},{4,5},{5,4},{6,7},{7,6},{8,9},{9,8},{10,11... | collective-permute-start | bytes 5505032 | tf_op jit(solution)/shard_map/ppermute | solution.py:36
  405.2 21.0 %collective-permute-start.51 = (bf16[64,3584]{1,0:T(8,128)(2,1)S(1)}, bf16[64,3584]{1,0:T(8,128)(2,1)S(1)}, u32[]{:S(2)}, u32[]{:S(2)}) collective-permute-start(bf16[64,3584]{1,0:T(8,128)(2,1)S(1)} %fusion.36), channel_id=1, source_target_pairs={{0,2},{1,3},{2,0},{3,1},{4,6},{5,7},{6,4},{7,5},{8,10},{9,11},{10,... | collective-permute-start | bytes 1376264 | tf_op jit(solution)/shard_map/ppermute | solution.py:36
  416.4 38.2 %collective-permute-start.48 = (bf16[128,3584]{1,0:T(8,128)(2,1)S(1)}, bf16[128,3584]{1,0:T(8,128)(2,1)S(1)}, u32[]{:S(2)}, u32[]{:S(2)}) collective-permute-start(bf16[128,3584]{1,0:T(8,128)(2,1)S(1)} %pad_maximum_fusion.21), channel_id=1, source_target_pairs={{0,1},{1,0},{2,3},{3,2},{4,5},{5,4},{6,7},{7,6},{8,9},{9,8},{10,11... | collective-permute-start | bytes 2752520 | tf_op jit(solution)/shard_map/ppermute | solution.py:36
  416.6 19.4 %collective-permute-start.57 = (bf16[64,3584]{1,0:T(8,128)(2,1)S(1)}, bf16[64,3584]{1,0:T(8,128)(2,1)S(1)}, u32[]{:S(2)}, u32[]{:S(2)}) collective-permute-start(bf16[64,3584]{1,0:T(8,128)(2,1)S(1)} %fusion.32), channel_id=1, source_target_pairs={{0,2},{1,3},{2,0},{3,1},{4,6},{5,7},{6,4},{7,5},{8,10},{9,11},{10,... | collective-permute-start | bytes 1376264 | tf_op jit(solution)/shard_map/ppermute | solution.py:36
  427.5 18.3 %collective-permute-start.52 = (bf16[64,3584]{1,0:T(8,128)(2,1)S(1)}, bf16[64,3584]{1,0:T(8,128)(2,1)S(1)}, u32[]{:S(2)}, u32[]{:S(2)}) collective-permute-start(bf16[64,3584]{1,0:T(8,128)(2,1)S(1)} %fusion.39), channel_id=1, source_target_pairs={{0,2},{1,3},{2,0},{3,1},{4,6},{5,7},{6,4},{7,5},{8,10},{9,11},{10,... | collective-permute-start | bytes 1376264 | tf_op jit(solution)/shard_map/ppermute | solution.py:36
  436.2 18.2 %collective-permute-start.58 = (bf16[64,3584]{1,0:T(8,128)(2,1)S(1)}, bf16[64,3584]{1,0:T(8,128)(2,1)S(1)}, u32[]{:S(2)}, u32[]{:S(2)}) collective-permute-start(bf16[64,3584]{1,0:T(8,128)(2,1)S(1)} %fusion.35), channel_id=1, source_target_pairs={{0,2},{1,3},{2,0},{3,1},{4,6},{5,7},{6,4},{7,5},{8,10},{9,11},{10,... | collective-permute-start | bytes 1376264 | tf_op jit(solution)/shard_map/ppermute | solution.py:36
  (79 other events, 920.6 us)

commit v6 on v5

--- a/solution.py
+++ b/solution.py
@@ -120,25 +120,20 @@
             ]
         )
 
-    def joined(pieces, j):
-        return jnp.concatenate(pieces[j * per_group : (j + 1) * per_group], axis=1).reshape(
-            count * per_group * rows, width
-        )
+    def joined(pieces):
+        return jnp.concatenate(pieces, axis=1).reshape(-1, pieces[0].shape[-1])
 
     halves = (grp, 1 - grp)
-    acts = [[None] * ring, [None] * ring]
-    for half in range(2):
-        acts[half][0] = own_rows(inputs, 0, halves[half])
-
-    def fetch(step, after):
-        for k in step:
-            if k:
-                acts[0][k] = shift(tie(acts[0][0], after), "row", k)
-
-    def fetch_other(step, after):
-        for k in step:
-            if k:
-                acts[1][k] = swap(tie(acts[0][k], after), "grp", 1)
+    own = [own_rows(inputs, 0, half) for half in halves]
+    near = shift(own[0], "row")
+    spread = [lax.all_gather(own[0], "row")]
+
+    def piece_of(half, k):
+        if k == 0:
+            return own[half]
+        if k == 1 and half == 0:
+            return near
+        return lax.dynamic_index_in_dim(spread[half], (me + ring - k) % ring, 0, keepdims=False)
 
     gate_scale = 2.0 ** math.floor(math.log2(65504.0 / (0.375 * width * count)))
 
@@ -155,7 +150,8 @@
 
     def sum_over_col(part, form):
         half = part.shape[0] // 2
-        got = swap(part[half:], "col", 1)
+        first = part[half:]
+        got = swap(first, "col", 1)
         cut = half // 2
         own, give = part[:cut] + got[:cut], part[cut:half] + got[cut:]
         mask, mark = 2, None
@@ -165,71 +161,117 @@
             own = own + unpack(swap(sent, "col", mask), form)
             mask *= 2
             if mask >= count:
-                return own, mark
+                return own, mark, first
             cut = own.shape[0] // 2
             own, give = own[:cut], own[cut:]
 
     def gather_over_col(values):
-        mask = count // 2
+        mask, mark = count // 2, None
         while mask >= 1:
-            values = jnp.concatenate([values, swap(values, "col", mask)], axis=0)
+            got = swap(values, "col", mask)
+            mark = got if mark is None else mark
+            values = jnp.concatenate([values, got], axis=0)
             mask //= 2
-        return values
+        return values, mark
 
     steps = [list(range(j * per_group, (j + 1) * per_group)) for j in range(GROUPS)]
-    fetch(steps[0], [])
-    first = acts[0][1:per_group]
-    for step in steps[1:]:
-        fetch(step, first)
-    fetch_other(steps[0], [])
-
-    sums, marks = {}, []
-    for half in range(2):
-        for j in range(GROUPS):
-            x = None
-            for form in ("gate", "up", "tangent") if half == 0 else ("tangent",):
-                after = marks[-2:-1]
-                if x is None:
-                    x = joined([p if p is None else tie(p, after) for p in acts[half]], j)
-                else:
-                    x = tie(x, after)
-                weight = {"gate": w_gate, "up": w_up, "tangent": query}[form]
-                sums[half, j, form], mark = sum_over_col(matmul(x, weight), form)
-                marks.append(mark)
-            if half == 0 and j + 1 < GROUPS:
-                fetch_other(steps[j + 1], marks[-1:])
-
+    last = ring - 1
+    sums, marks, xs = {}, [], {}
     gains = [[None] * GROUPS, [None] * GROUPS]
-    for j in range(GROUPS):
-        gate_out, up_out = sums[0, j, "gate"], sums[0, j, "up"]
-        sigmas = jax.nn.sigmoid(gate_out)
-        gains[0][j] = sigmas * (1.0 + gate_out * (1.0 - sigmas)) * up_out
-        gains[1][j] = swap(gains[0][j], "grp", 1)
-
-    last = ring - 1
-    turned, bars = [], []
-    for half in range(2):
-        moved = []
-        for j in range(GROUPS):
-            hidden = (gains[half][j] * sums[half, j, "tangent"]).astype(jnp.bfloat16)
-            out = matmul(gather_over_col(hidden), w_down).reshape(count, per_group, rows, width)
-            for i, k in enumerate(steps[j]):
-                piece = out[:, i]
-                if k < last:
-                    piece = shift(piece.astype(jnp.bfloat16), "row", last - k).astype(jnp.float32)
-                moved.append(piece)
-        total = moved[-1]
-        for piece in moved[:-1]:
-            total = total + piece
+    moved = {}
+
+    def project(half, j, form, after):
+        after = after + [mark for mark, _ in marks[-2:-1]] + [total for _, total in marks[-3:-2]]
+        if (half, j) in xs:
+            x = tie(xs[half, j], after)
+        else:
+            xs[half, j] = x = joined([tie(piece_of(half, k), after) for k in steps[j]])
+        weight = {"gate": w_gate, "up": w_up, "tangent": query}[form]
+        sums[half, j, form], mark, start = sum_over_col(matmul(x, weight), form)
+        marks.append((mark, sums[half, j, form]))
+        return [start]
+
+    def hidden_rows(half, j, after):
+        if half == 0:
+            gate_out, up_out = sums[0, j, "gate"], sums[0, j, "up"]
+            sigmas = jax.nn.sigmoid(gate_out)
+            gains[0][j] = sigmas * (1.0 + gate_out * (1.0 - sigmas)) * up_out
+        tangent = tie(sums[half, j, "tangent"], after)
+        hidden = (gains[half][j] * tangent).astype(jnp.bfloat16)
+        return gather_over_col(hidden)
+
+    def share_gain(j, after):
+        both = lax.all_gather(tie(gains[0][j], after), "grp")
+        gains[1][j] = lax.dynamic_index_in_dim(both, 1 - grp, 0, keepdims=False)
+
+    def out_sums(half, j, hidden, after):
+        out = matmul(tie(hidden, after), w_down).reshape(count, per_group, rows, width)
+        for i, k in enumerate(steps[j]):
+            piece = out[:, i]
+            if k < last:
+                piece = piece.astype(jnp.bfloat16)
+                mark = piece
+                piece = shift(piece, "row", last - k)
+            moved[half, k] = piece
+        return mark
+
+    def scaled_pieces(half, after):
+        total = moved[half, last]
+        for k in range(last):
+            total = total + tie(moved[half, k], after).astype(jnp.float32)
         curv = own_rows(curvature, (me + 1) % ring * shard, halves[half])
         pieces = [None] * last + [(curv * total).astype(jnp.bfloat16)]
         for k in reversed(range(last)):
             pieces[k] = shift(pieces[k + 1], "row", -1)
-        for j in reversed(range(GROUPS)):
-            after = pieces[last:]
-            turned.append(joined([tie(piece, after) for piece in acts[half]], j).T)
-            own, _ = sum_over_col(times_down(joined(pieces, j), w_down), "back")
-            bars.append(gather_over_col((own * gains[half][j]).astype(jnp.bfloat16)))
+        return pieces
+
+    turned, bars = [], []
+
+    def back(half, j, pieces, after):
+        x = joined([pieces[k] for k in steps[j]])
+        turned.append(tie(xs[half, j], pieces[last:]).T)
+        own, mark, _ = sum_over_col(times_down(tie(x, after), w_down), "back")
+        bar = (own * gains[half][j]).astype(jnp.bfloat16)
+        whole, near = gather_over_col(bar)
+        bars.append(whole)
+        return mark, bar, near
+
+    tail = GROUPS - 1
+    early = []
+    for j in range(GROUPS):
+        start = project(0, j, "up", [])
+        if j:
+            early.append(hidden_rows(0, j - 1, start))
+        project(0, j, "gate", [])
+        start = project(0, j, "tangent", [])
+        if j == 0:
+            spread.append(lax.all_gather(tie(own[1], spread + start), "row"))
+        else:
+            share_gain(j - 1, start)
+    start = project(1, 0, "tangent", [near for _, near in early])
+    ready = [out_sums(0, j, early[j][0], []) for j in range(tail)]
+    hidden, _ = hidden_rows(0, tail, start)
+    for j in range(1, GROUPS):
+        start = project(1, j, "tangent", ready)
+    share_gain(tail, start)
+    ready = [out_sums(0, tail, hidden, [])]
+    pieces = scaled_pieces(0, [])
+
+    hidden = [hidden_rows(1, j, []) for j in range(GROUPS)]
+    for j in range(tail):
+        ready = [out_sums(1, j, hidden[j][0], ready)]
+    mark, bar, near = back(0, tail, pieces, ready)
+    out_sums(1, tail, hidden[tail][0], [mark])
+    after = [mark]
+    for j in reversed(range(tail)):
+        mark, nextbar, nextnear = back(0, j, pieces, after)
+        after = [mark, bar]
+        bar, lastnear, near = nextbar, near, nextnear
+    pieces = scaled_pieces(1, after)
+    after = [lastnear, bar]
+    for j in reversed(range(GROUPS)):
+        mark, bar, nextnear = back(1, j, pieces, after)
+        after, near = [mark, near], nextnear
     return last_product(turned, bars, tokens)
 
 

time: 485 us -> 473 us (0.975)
  waiting for transfers between devices: 181 us -> 143 us
  between operations: 1.71 us -> 14.6 us
  local copies, waits for them, and re-layouts: 32.9 us -> 44.1 us
  starting transfers between devices: 71.4 us -> 62.8 us
  matrix products: 113 us -> 121 us
    ppermute x15 -> x13, waiting for transfers between devices: 98.2 us -> 64.7 us  [shift(): lax.ppermute(values, axis, [(i, (i + by) % count) for i in range(count)])]
    ppermute x45 -> x40, waiting for transfers between devices: 82.9 us -> 67.7 us  [swap(): return lax.ppermute(values, axis, [(i, i ^ mask) for i in range(count)])]
    concatenate x24 -> x22, other arithmetic: 26 us -> 14.2 us  [the longest x14 10.4 us: gather_over_col(): values = jnp.concatenate([values, got], axis=0)]
    all_gather x0 -> x4, waiting for transfers between devices: none -> 10.9 us  [the longest x1 10.9 us: per_device(): spread = [lax.all_gather(own[0], 'row')]]
    unnamed x134 -> x106, local copies, waits for them, and re-layouts: 6.1 us -> 14.3 us
    add x0 -> x4, other arithmetic: none -> 7.49 us  [sum_over_col(): own = own + unpack(swap(sent, 'col', mask), form)]
    dot_general x12, matrix products: 81.9 us -> 89.4 us  [matmul(): return jnp.dot(left, right, preferred_element_type=jnp.float32)]
    ppermute x45 -> x40, starting transfers between devices: 30.7 us -> 24.9 us  [swap(): return lax.ppermute(values, axis, [(i, i ^ mask) for i in range(count)])]
  transfers between devices with their start and end apart: 60 -> 57, of which waited for: 24 -> 21; matrix products, arithmetic and copies ran while one was open for 36% -> 40% of each run, Pallas kernels for 0% -> 0%
where the time goes in v6:
time: 473 us; the launch traced here: 466 us
  waiting for transfers between devices  143 us (30%)
  matrix products  121 us (26%)
  starting transfers between devices  62.8 us (13%)
  other arithmetic  58 us (12%)
  local copies, waits for them, and re-layouts  44.1 us (9%)
  Pallas kernels  22.5 us (5%)
  between operations  14.6 us (3%)
    dot_general x12, matrix products, matmul(): return jnp.dot(left, right, preferred_element_type=jnp.float32)  89.4 us
    ppermute x40, waiting for transfers between devices, swap(): return lax.ppermute(values, axis, [(i, i ^ mask) for i in range(count)])  67.7 us
    ppermute x13, waiting for transfers between devices, shift(): lax.ppermute(values, axis, [(i, (i + by) % count) for i in range(count)])  64.7 us
    ppermute x13, starting transfers between devices, shift(): lax.ppermute(values, axis, [(i, (i + by) % count) for i in range(count)])  37.4 us
    dot_general x4, matrix products, times_down(): lax.dot_general(left, w_down, (((1,), (1,)), ((), ())), preferred_element...  31.5 us
    ppermute x40, starting transfers between devices, swap(): return lax.ppermute(values, axis, [(i, i ^ mask) for i in range(count)])  24.9 us
    pallas_call x1, Pallas kernels, last_product(): pl.pallas_call(functools.partial(last_kernel, 1.0 / tokens, len(turned)),...  22.5 us
    unnamed x106, local copies, waits for them, and re-layouts  14.3 us
  transfers between devices with their start and end apart: 57, of which 21 were waited for; matrix products, arithmetic and copies ran while one was open for 40% of the time, Pallas kernels for 0%

profile of v6, /device:TPU:0, one launch (start us, length us, event | category | flops | bytes accessed | tf_op | source)
XLA Modules:
  0.0 466.2 jit_solution(14283092201516204522)
XLA Ops:
  8.7 3.1 collective-permute-start
  11.8 13.9 %collective-permute-done = bf16[4,32,2048]{2,1,0:T(8,128)(2,1)S(1)} collective-permute-done((bf16[4,32,2048]{2,1,0:T(8,128)(2,1)S(1)}, bf16[4,32,2048]{2,1,0:T(8,128)(2,1)S(1)}, u32[]{:S(2)}, u32[]{:S(2)}) %collective-permute-start) | collective-permute-done | bytes 524320 | tf_op jit(solution)/shard_map/ppermute | solution.py:41
  25.8 7.6 %fusion.82 = f32[256,3584]{1,0:T(8,128)S(1)} fusion(bf16[256,2048]{1,0:T(8,128)(2,1)S(1)} %bitcast.146, bf16[2048,3584]{1,0:T(8,128)(2,1)} %param.8), kind=kOutput, calls=%fused_computation.195 | convolution fusion | flops 3758096384 | bytes 19398656 | tf_op jit(solution)/shard_map/dot_general | solution.py:19
  38.8 2.8 dynamic-slice_bitcast_fusion.8
  41.7 7.8 %fusion.81 = f32[256,3584]{1,0:T(8,128)S(1)} fusion(bf16[256,2048]{1,0:T(8,128)(2,1)S(1)} %bitcast.147, bf16[2048,3584]{1,0:T(8,128)(2,1)} %param.7), kind=kOutput, calls=%fused_computation.194 | convolution fusion | flops 3758096384 | bytes 19398656 | tf_op jit(solution)/shard_map/dot_general | solution.py:19
  56.8 7.3 %fusion.83 = f32[256,3584]{1,0:T(8,128)S(1)} fusion(bf16[256,2048]{1,0:T(8,128)(2,1)S(1)} %bitcast.148, bf16[2048,3584]{1,0:T(8,128)(2,1)} %param.10), kind=kOutput, calls=%fused_computation.196 | convolution fusion | flops 3758096384 | bytes 19398656 | tf_op jit(solution)/shard_map/dot_general | solution.py:19
  65.9 2.5 fusion.56
  69.1 2.4 fusion.54
  71.6 10.9 %all-gather.9.cloned.1.call-done = bf16[16,32,2048]{2,1,0:T(8,128)(2,1)} async-done(((bf16[4,32,2048]{2,1,0:T(8,128)(2,1)}), bf16[16,32,2048]{2,1,0:T(8,128)(2,1)}) %all-gather.9.cloned.1.call-update) | async-done | bytes 2097168 | tf_op jit(solution)/shard_map/all_gather | solution.py:129
  88.0 7.8 %fusion.85 = f32[256,3584]{1,0:T(8,128)S(1)} fusion(bf16[256,2048]{1,0:T(8,128)(2,1)S(1)} %bitcast.150, bf16[2048,3584]{1,0:T(8,128)(2,1)} %param.8), kind=kOutput, calls=%fused_computation.198 | convolution fusion | flops 3758096384 | bytes 19398656 | tf_op jit(solution)/shard_map/dot_general | solution.py:19
  96.0 2.8 collective-permute-done.10
  100.1 3.0 multiply_convert_fusion.1
  104.6 7.3 %fusion.84 = f32[256,3584]{1,0:T(8,128)S(1)} fusion(bf16[256,2048]{1,0:T(8,128)(2,1)S(1)} %bitcast.151, bf16[2048,3584]{1,0:T(8,128)(2,1)} %param.7), kind=kOutput, calls=%fused_computation.197 | convolution fusion | flops 3758096384 | bytes 19398656 | tf_op jit(solution)/shard_map/dot_general | solution.py:19
  116.5 7.3 %fusion.86 = f32[256,3584]{1,0:T(8,128)S(1)} fusion(bf16[256,2048]{1,0:T(8,128)(2,1)S(1)} %bitcast.152, bf16[2048,3584]{1,0:T(8,128)(2,1)} %param.10), kind=kOutput, calls=%fused_computation.199 | convolution fusion | flops 3758096384 | bytes 19398656 | tf_op jit(solution)/shard_map/dot_general | solution.py:19
  132.2 10.3 %convolution_convert_fusion.1 = bf16[256,2048]{1,0:T(8,128)(2,1)S(1)} fusion(bf16[3584,2048]{1,0:T(8,128)(2,1)} %param.9, bf16[128,3584]{1,0:T(8,128)(2,1)S(1)} %collective-permute-done.16, bf16[64,3584]{1,0:T(8,128)(2,1)} %collective-permute-done.13, bf16[64,3584]{1,0:T(8,128)(2,1)} %get-tuple-element.70), kind=kOutput, calls=%fused_computation.1 | convolution fusion | flops 3764125696 | bytes 17563648 | tf_op jit(solution)/shard_map/dot_general | solution.py:19
  152.2 7.4 %fusion.87 = f32[256,3584]{1,0:T(8,128)S(1)} fusion(bf16[256,2048]{1,0:T(8,128)(2,1)S(1)} %bitcast.154, bf16[2048,3584]{1,0:T(8,128)(2,1)} %param.10), kind=kOutput, calls=%fused_computation.200 | convolution fusion | flops 3758096384 | bytes 19398656 | tf_op jit(solution)/shard_map/dot_general | solution.py:19
  159.9 10.5 %collective-permute-done.12 = bf16[64,3584]{1,0:T(8,128)(2,1)S(1)} collective-permute-done((bf16[64,3584]{1,0:T(8,128)(2,1)S(1)}, bf16[64,3584]{1,0:T(8,128)(2,1)S(1)}, u32[]{:S(2)}, u32[]{:S(2)}) %collective-permute-start.12) | collective-permute-done | bytes 458784 | tf_op jit(solution)/shard_map/ppermute | solution.py:36
  171.7 2.9 multiply_convert_fusion
  176.2 3.9 fusion.88
  182.6 3.6 collective-permute-done.14
  190.4 7.8 %fusion = f32[256,2048]{1,0:T(8,128)S(1)} fusion(bf16[3584,2048]{1,0:T(8,128)(2,1)} %param.9, bf16[128,3584]{1,0:T(8,128)(2,1)S(1)} %collective-permute-done.15, bf16[64,3584]{1,0:T(8,128)(2,1)} %collective-permute-done.14, bf16[64,3584]{1,0:T(8,128)(2,1)S(1)} %get-tuple-element.67), kind=kOutput, calls=%fused_computation.2 | convolution fusion | flops 3763601408 | bytes 18612224 | tf_op jit(solution)/shard_map/dot_general | solution.py:19
  208.5 7.1 %collective-permute-done.19 = bf16[4,32,2048]{2,1,0:T(8,128)(2,1)S(1)} collective-permute-done((bf16[4,32,2048]{2,1,0:T(8,128)(2,1)S(1)}, bf16[4,32,2048]{2,1,0:T(8,128)(2,1)S(1)}, u32[]{:S(2)}, u32[]{:S(2)}) %collective-permute-start.19) | collective-permute-done | bytes 524320 | tf_op jit(solution)/shard_map/ppermute | solution.py:41
  219.4 6.8 %collective-permute-done.21 = bf16[64,3584]{1,0:T(8,128)(2,1)S(1)} collective-permute-done((bf16[64,3584]{1,0:T(8,128)(2,1)}, bf16[64,3584]{1,0:T(8,128)(2,1)S(1)}, u32[]{:S(2)}, u32[]{:S(2)}) %collective-permute-start.21) | collective-permute-done | bytes 458784 | tf_op jit(solution)/shard_map/ppermute | solution.py:36
  230.6 3.2 collective-permute-start.31
  236.3 7.6 %convolution_convert_fusion = bf16[256,2048]{1,0:T(8,128)(2,1)S(1)} fusion(bf16[256,3584]{1,0:T(8,128)(2,1)S(1)} %pad_maximum_fusion.1, bf16[3584,2048]{1,0:T(8,128)(2,1)} %param.9), kind=kOutput, calls=%fused_computation | convolution fusion | flops 3758620672 | bytes 17563648 | tf_op jit(solution)/shard_map/dot_general | solution.py:19
  244.9 7.3 %fusion.89 = f32[256,3584]{1,0:T(8,128)S(1)} fusion(bf16[256,2048]{1,0:T(8,128)(2,1)S(1)} %bitcast.168, bf16[3584,2048]{1,0:T(8,128)(2,1)} %param.9), kind=kOutput, calls=%fused_computation.202 | convolution fusion | flops 3758096384 | bytes 19398656 | tf_op jit(solution)/shard_map/dot_general | solution.py:23
  253.7 3.8 collective-permute-start.30
  257.5 11.0 %collective-permute-done.32 = bf16[4,32,2048]{2,1,0:T(8,128)(2,1)S(1)} collective-permute-done((bf16[4,32,2048]{2,1,0:T(8,128)(2,1)}, bf16[4,32,2048]{2,1,0:T(8,128)(2,1)S(1)}, u32[]{:S(2)}, u32[]{:S(2)}) %collective-permute-start.32) | collective-permute-done | bytes 524320 | tf_op jit(solution)/shard_map/ppermute | solution.py:41
  273.1 7.6 %fusion.91 = f32[256,3584]{1,0:T(8,128)S(1)} fusion(bf16[256,2048]{1,0:T(8,128)(2,1)} %bitcast.167, bf16[3584,2048]{1,0:T(8,128)(2,1)} %param.9), kind=kOutput, calls=%fused_computation.204 | convolution fusion | flops 3758096384 | bytes 19398656 | tf_op jit(solution)/shard_map/dot_general | solution.py:23
  281.0 2.6 copy-done.33
  283.6 7.2 %fusion.90 = f32[256,2048]{1,0:T(8,128)S(1)} fusion(bf16[256,3584]{1,0:T(8,128)(2,1)S(1)} %copy-done.33, bf16[3584,2048]{1,0:T(8,128)(2,1)} %param.9), kind=kOutput, calls=%fused_computation.203 | convolution fusion | flops 3758096384 | bytes 18612224 | tf_op jit(solution)/shard_map/dot_general | solution.py:19
  290.9 9.8 %collective-permute-start.36 = (bf16[4,32,2048]{2,1,0:T(8,128)(2,1)S(1)}, bf16[4,32,2048]{2,1,0:T(8,128)(2,1)S(1)}, u32[]{:S(2)}, u32[]{:S(2)}) collective-permute-start(bf16[4,32,2048]{2,1,0:T(8,128)(2,1)S(1)} %fusion.58), channel_id=1, source_target_pairs={{0,4},{4,8},{8,12},{12,0},{1,5},{5,9},{9,13},{13,1},{2,6},{6,10},{... | collective-permute-start | bytes 1572872 | tf_op jit(solution)/shard_map/ppermute | solution.py:41
  304.4 5.5 %collective-permute-done.36 = bf16[4,32,2048]{2,1,0:T(8,128)(2,1)S(1)} collective-permute-done((bf16[4,32,2048]{2,1,0:T(8,128)(2,1)S(1)}, bf16[4,32,2048]{2,1,0:T(8,128)(2,1)S(1)}, u32[]{:S(2)}, u32[]{:S(2)}) %collective-permute-start.36) | collective-permute-done | bytes 524320 | tf_op jit(solution)/shard_map/ppermute | solution.py:41
  311.7 4.3 collective-permute-start.42
  316.0 6.1 %collective-permute-done.39 = bf16[64,3584]{1,0:T(8,128)(2,1)S(1)} collective-permute-done((bf16[64,3584]{1,0:T(8,128)(2,1)S(1)}, bf16[64,3584]{1,0:T(8,128)(2,1)S(1)}, u32[]{:S(2)}, u32[]{:S(2)}) %collective-permute-start.39) | collective-permute-done | bytes 458784 | tf_op jit(solution)/shard_map/ppermute | solution.py:36
  322.3 5.0 %collective-permute-done.42 = bf16[4,32,2048]{2,1,0:T(8,128)(2,1)S(1)} collective-permute-done((bf16[4,32,2048]{2,1,0:T(8,128)(2,1)S(1)}, bf16[4,32,2048]{2,1,0:T(8,128)(2,1)S(1)}, u32[]{:S(2)}, u32[]{:S(2)}) %collective-permute-start.42) | collective-permute-done | bytes 524320 | tf_op jit(solution)/shard_map/ppermute | solution.py:41
  327.5 9.3 %fusion.92 = f32[256,3584]{1,0:T(8,128)} fusion(bf16[256,2048]{1,0:T(8,128)(2,1)S(1)} %bitcast.171, bf16[3584,2048]{1,0:T(8,128)(2,1)} %param.9), kind=kOutput, calls=%fused_computation.205 | convolution fusion | flops 3758096384 | bytes 19398656 | tf_op jit(solution)/shard_map/dot_general | solution.py:23
  338.5 4.5 collective-permute-start.47
  343.1 11.8 %collective-permute-done.47 = bf16[4,32,2048]{2,1,0:T(8,128)(2,1)S(1)} collective-permute-done((bf16[4,32,2048]{2,1,0:T(8,128)(2,1)S(1)}, bf16[4,32,2048]{2,1,0:T(8,128)(2,1)S(1)}, u32[]{:S(2)}, u32[]{:S(2)}) %collective-permute-start.47) | collective-permute-done | bytes 524320 | tf_op jit(solution)/shard_map/ppermute | solution.py:41
  354.9 4.3 collective-permute-start.48
  361.0 9.2 %collective-permute-done.48 = bf16[4,32,2048]{2,1,0:T(8,128)(2,1)S(1)} collective-permute-done((bf16[4,32,2048]{2,1,0:T(8,128)(2,1)S(1)}, bf16[4,32,2048]{2,1,0:T(8,128)(2,1)S(1)}, u32[]{:S(2)}, u32[]{:S(2)}) %collective-permute-start.48) | collective-permute-done | bytes 524320 | tf_op jit(solution)/shard_map/ppermute | solution.py:41
  370.3 2.8 fusion.25
  373.8 7.3 %fusion.93 = f32[256,3584]{1,0:T(8,128)S(1)} fusion(bf16[256,2048]{1,0:T(8,128)(2,1)S(1)} %bitcast.169, bf16[3584,2048]{1,0:T(8,128)(2,1)} %param.9), kind=kOutput, calls=%fused_computation.206 | convolution fusion | flops 3758096384 | bytes 19398656 | tf_op jit(solution)/shard_map/dot_general | solution.py:23
  395.4 10.2 %collective-permute-done.44 = bf16[64,3584]{1,0:T(8,128)(2,1)S(1)} collective-permute-done((bf16[64,3584]{1,0:T(8,128)(2,1)}, bf16[64,3584]{1,0:T(8,128)(2,1)S(1)}, u32[]{:S(2)}, u32[]{:S(2)}) %collective-permute-start.44) | collective-permute-done | bytes 458784 | tf_op jit(solution)/shard_map/ppermute | solution.py:36
  407.9 7.5 %collective-permute-done.50 = bf16[64,3584]{1,0:T(8,128)(2,1)S(1)} collective-permute-done((bf16[64,3584]{1,0:T(8,128)(2,1)S(1)}, bf16[64,3584]{1,0:T(8,128)(2,1)S(1)}, u32[]{:S(2)}, u32[]{:S(2)}) %collective-permute-start.50) | collective-permute-done | bytes 458784 | tf_op jit(solution)/shard_map/ppermute | solution.py:36
  417.7 7.6 %collective-permute-done.45 = bf16[64,3584]{1,0:T(8,128)(2,1)S(1)} collective-permute-done((bf16[64,3584]{1,0:T(8,128)(2,1)S(1)}, bf16[64,3584]{1,0:T(8,128)(2,1)S(1)}, u32[]{:S(2)}, u32[]{:S(2)}) %collective-permute-start.45) | collective-permute-done | bytes 458784 | tf_op jit(solution)/shard_map/ppermute | solution.py:36
  425.4 8.8 %collective-permute-done.51 = bf16[64,3584]{1,0:T(8,128)(2,1)S(1)} collective-permute-done((bf16[64,3584]{1,0:T(8,128)(2,1)S(1)}, bf16[64,3584]{1,0:T(8,128)(2,1)S(1)}, u32[]{:S(2)}, u32[]{:S(2)}) %collective-permute-start.51) | collective-permute-done | bytes 458784 | tf_op jit(solution)/shard_map/ppermute | solution.py:36
  437.0 22.5 %shard_map.64 = f32[2048,3584]{1,0:T(8,128)} custom-call(bf16[2048,256]{1,0:T(8,128)(2,1)S(1)} %bitcast.143, bf16[2048,256]{1,0:T(8,128)(2,1)S(1)} %bitcast.142, bf16[2048,256]{1,0:T(8,128)(2,1)S(1)} %bitcast.145, bf16[2048,256]{1,0:T(8,128)(2,1)S(1)} %bitcast.144, bf16[256,3584]{1,0:T(8,128)(2,1)S(1)} %pad_maximum_fusion.2.refs_4_, ...), custom_call_target="tpu_custom_call" | custom-call | flops 15032385536 | bytes 40894464 | tf_op jit(solution)/shard_map/pallas_call | solution.py:88
  (286 shorter events, 117.9 us)
Async XLA Ops:
  6.5 75.9 %all-gather.9.cloned.1.call-start = ((), (), s32[]{:S(2)}) async-start(), calls=%async_computation | async-start | bytes 2621440 | tf_op jit(solution)/shard_map/all_gather | solution.py:129
  8.7 17.0 %collective-permute-start = (bf16[4,32,2048]{2,1,0:T(8,128)(2,1)S(1)}, bf16[4,32,2048]{2,1,0:T(8,128)(2,1)S(1)}, u32[]{:S(2)}, u32[]{:S(2)}) collective-permute-start(bf16[4,32,2048]{2,1,0:T(8,128)(2,1)S(1)} %pad_maximum_fusion.22), channel_id=1, source_target_pairs={{0,4},{4,8},{8,12},{12,0},{1,5},{5,9},{9,13},{13,1},{2,6},{6,10},{... | collective-permute-start | bytes 1572872 | tf_op jit(solution)/shard_map/ppermute | solution.py:41
  36.8 14.6 %collective-permute-start.2 = (f32[128,3584]{1,0:T(8,128)}, f32[128,3584]{1,0:T(8,128)S(1)}, u32[]{:S(2)}, u32[]{:S(2)}) collective-permute-start(f32[128,3584]{1,0:T(8,128)} %slice.322), channel_id=1, source_target_pairs={{0,1},{1,0},{2,3},{3,2},{4,5},{5,4},{6,7},{7,6},{8,9},{9,8},{10,11... | collective-permute-start | bytes 5505032 | tf_op jit(solution)/shard_map/ppermute | solution.py:36
  36.8 108.1 %all-gather.11.cloned.1.call-start = ((), (), s32[]{:S(2)}) async-start(), calls=%async_computation.1 | async-start | bytes 2621440 | tf_op jit(solution)/shard_map/all_gather | solution.py:248
  50.9 15.0 %collective-permute-start.1 = (f32[128,3584]{1,0:T(8,128)}, f32[128,3584]{1,0:T(8,128)}, u32[]{:S(2)}, u32[]{:S(2)}) collective-permute-start(f32[128,3584]{1,0:T(8,128)} %slice.319), channel_id=1, source_target_pairs={{0,1},{1,0},{2,3},{3,2},{4,5},{5,4},{6,7},{7,6},{8,9},{9,8},{10,11... | collective-permute-start | bytes 5505032 | tf_op jit(solution)/shard_map/ppermute | solution.py:36
  55.4 13.6 %collective-permute-start.3 = (f16[64,3712]{1,0:T(8,128)(2,1)}, f16[64,3712]{1,0:T(8,128)(2,1)S(1)}, u32[]{:S(2)}, u32[]{:S(2)}) collective-permute-start(f16[64,3712]{1,0:T(8,128)(2,1)} %concatenate.89), channel_id=1, source_target_pairs={{0,2},{1,3},{2,0},{3,1},{4,6},{5,7},{6,4},{7,5},{8,10},{9,11},{10,... | collective-permute-start | bytes 1425416 | tf_op jit(solution)/shard_map/ppermute | solution.py:36
  65.7 18.7 %collective-permute-start.4 = (f32[128,3584]{1,0:T(8,128)}, f32[128,3584]{1,0:T(8,128)}, u32[]{:S(2)}, u32[]{:S(2)}) collective-permute-start(f32[128,3584]{1,0:T(8,128)} %slice.332), channel_id=1, source_target_pairs={{0,1},{1,0},{2,3},{3,2},{4,5},{5,4},{6,7},{7,6},{8,9},{9,8},{10,11... | collective-permute-start | bytes 5505032 | tf_op jit(solution)/shard_map/ppermute | solution.py:36
  68.4 31.7 %collective-permute-start.5 = (f16[64,3584]{1,0:T(8,128)(2,1)}, f16[64,3584]{1,0:T(8,128)(2,1)S(1)}, u32[]{:S(2)}, u32[]{:S(2)}) collective-permute-start(f16[64,3584]{1,0:T(8,128)(2,1)} %fusion.56), channel_id=1, source_target_pairs={{0,2},{1,3},{2,0},{3,1},{4,6},{5,7},{6,4},{7,5},{8,10},{9,11},{10,... | collective-permute-start | bytes 1376264 | tf_op jit(solution)/shard_map/ppermute | solution.py:36
  82.4 118.5 %all-gather.15.cloned.1.call-start = ((), (), s32[]{:S(2)}) async-start(), calls=%async_computation.3 | async-start | bytes 2752512 | tf_op jit(solution)/shard_map/all_gather | solution.py:204
  95.9 17.6 %collective-permute-start.8 = (f32[128,3584]{1,0:T(8,128)S(1)}, f32[128,3584]{1,0:T(8,128)S(1)}, u32[]{:S(2)}, u32[]{:S(2)}) collective-permute-start(f32[128,3584]{1,0:T(8,128)S(1)} %slice.342), channel_id=1, source_target_pairs={{0,1},{1,0},{2,3},{3,2},{4,5},{5,4},{6,7},{7,6},{8,9},{9,8},{10,11... | collective-permute-start | bytes 5505032 | tf_op jit(solution)/shard_map/ppermute | solution.py:36
  103.2 24.0 %collective-permute-start.13 = (bf16[64,3584]{1,0:T(8,128)(2,1)}, bf16[64,3584]{1,0:T(8,128)(2,1)}, u32[]{:S(2)}, u32[]{:S(2)}) collective-permute-start(bf16[64,3584]{1,0:T(8,128)(2,1)} %get-tuple-element.70), channel_id=1, source_target_pairs={{0,2},{1,3},{2,0},{3,1},{4,6},{5,7},{6,4},{7,5},{8,10},{9,11},{10,... | collective-permute-start | bytes 1376264 | tf_op jit(solution)/shard_map/ppermute | solution.py:36
  113.5 33.0 %collective-permute-start.6 = (f32[128,3584]{1,0:T(8,128)}, f32[128,3584]{1,0:T(8,128)}, u32[]{:S(2)}, u32[]{:S(2)}) collective-permute-start(f32[128,3584]{1,0:T(8,128)} %slice.337), channel_id=1, source_target_pairs={{0,1},{1,0},{2,3},{3,2},{4,5},{5,4},{6,7},{7,6},{8,9},{9,8},{10,11... | collective-permute-start | bytes 5505032 | tf_op jit(solution)/shard_map/ppermute | solution.py:36
  127.1 22.7 %collective-permute-start.11 = (f32[128,3584]{1,0:T(8,128)}, f32[128,3584]{1,0:T(8,128)}, u32[]{:S(2)}, u32[]{:S(2)}) collective-permute-start(f32[128,3584]{1,0:T(8,128)} %slice.354), channel_id=1, source_target_pairs={{0,1},{1,0},{2,3},{3,2},{4,5},{5,4},{6,7},{7,6},{8,9},{9,8},{10,11... | collective-permute-start | bytes 5505032 | tf_op jit(solution)/shard_map/ppermute | solution.py:36
  127.1 92.3 %all-gather.13.cloned.1.call-start = ((), (), s32[]{:S(2)}) async-start(), calls=%async_computation.2 | async-start | bytes 2752512 | tf_op jit(solution)/shard_map/all_gather | solution.py:204
  143.6 64.8 %collective-permute-start.17 = (bf16[4,32,2048]{2,1,0:T(8,128)(2,1)}, bf16[4,32,2048]{2,1,0:T(8,128)(2,1)}, u32[]{:S(2)}, u32[]{:S(2)}) collective-permute-start(bf16[4,32,2048]{2,1,0:T(8,128)(2,1)} %get-tuple-element.92), channel_id=1, source_target_pairs={{0,12},{4,0},{8,4},{12,8},{1,13},{5,1},{9,5},{13,9},{2,14},{6,2},{... | collective-permute-start | bytes 1572872 | tf_op jit(solution)/shard_map/ppermute | solution.py:41
  144.9 63.6 %collective-permute-start.18 = (bf16[4,32,2048]{2,1,0:T(8,128)(2,1)}, bf16[4,32,2048]{2,1,0:T(8,128)(2,1)}, u32[]{:S(2)}, u32[]{:S(2)}) collective-permute-start(bf16[4,32,2048]{2,1,0:T(8,128)(2,1)} %get-tuple-element.93), channel_id=1, source_target_pairs={{0,8},{4,12},{8,0},{12,4},{1,9},{5,13},{9,1},{13,5},{2,10},{6,14},... | collective-permute-start | bytes 1572872 | tf_op jit(solution)/shard_map/ppermute | solution.py:41
  148.2 23.5 %collective-permute-start.7 = (f16[64,3584]{1,0:T(8,128)(2,1)S(1)}, f16[64,3584]{1,0:T(8,128)(2,1)S(1)}, u32[]{:S(2)}, u32[]{:S(2)}) collective-permute-start(f16[64,3584]{1,0:T(8,128)(2,1)S(1)} %fusion.50), channel_id=1, source_target_pairs={{0,2},{1,3},{2,0},{3,1},{4,6},{5,7},{6,4},{7,5},{8,10},{9,11},{10,... | collective-permute-start | bytes 1376264 | tf_op jit(solution)/shard_map/ppermute | solution.py:36
  151.5 18.9 %collective-permute-start.12 = (bf16[64,3584]{1,0:T(8,128)(2,1)S(1)}, bf16[64,3584]{1,0:T(8,128)(2,1)S(1)}, u32[]{:S(2)}, u32[]{:S(2)}) collective-permute-start(bf16[64,3584]{1,0:T(8,128)(2,1)S(1)} %fusion.45), channel_id=1, source_target_pairs={{0,2},{1,3},{2,0},{3,1},{4,6},{5,7},{6,4},{7,5},{8,10},{9,11},{10,... | collective-permute-start | bytes 1376264 | tf_op jit(solution)/shard_map/ppermute | solution.py:36
  159.8 27.5 %collective-permute-start.25 = (f32[128,3584]{1,0:T(8,128)S(1)}, f32[128,3584]{1,0:T(8,128)}, u32[]{:S(2)}, u32[]{:S(2)}) collective-permute-start(f32[128,3584]{1,0:T(8,128)S(1)} %slice.358), channel_id=1, source_target_pairs={{0,1},{1,0},{2,3},{3,2},{4,5},{5,4},{6,7},{7,6},{8,9},{9,8},{10,11... | collective-permute-start | bytes 5505032 | tf_op jit(solution)/shard_map/ppermute | solution.py:36
  182.6 22.9 %collective-permute-start.20 = (f32[128,3584]{1,0:T(8,128)}, f32[128,3584]{1,0:T(8,128)}, u32[]{:S(2)}, u32[]{:S(2)}) collective-permute-start(f32[128,3584]{1,0:T(8,128)} %slice.363), channel_id=1, source_target_pairs={{0,1},{1,0},{2,3},{3,2},{4,5},{5,4},{6,7},{7,6},{8,9},{9,8},{10,11... | collective-permute-start | bytes 5505032 | tf_op jit(solution)/shard_map/ppermute | solution.py:36
  188.9 13.0 %collective-permute-start.26 = (bf16[64,3584]{1,0:T(8,128)(2,1)S(1)}, bf16[64,3584]{1,0:T(8,128)(2,1)S(1)}, u32[]{:S(2)}, u32[]{:S(2)}) collective-permute-start(bf16[64,3584]{1,0:T(8,128)(2,1)S(1)} %fusion.37), channel_id=1, source_target_pairs={{0,2},{1,3},{2,0},{3,1},{4,6},{5,7},{6,4},{7,5},{8,10},{9,11},{10,... | collective-permute-start | bytes 1376264 | tf_op jit(solution)/shard_map/ppermute | solution.py:36
  199.6 15.9 %collective-permute-start.19 = (bf16[4,32,2048]{2,1,0:T(8,128)(2,1)S(1)}, bf16[4,32,2048]{2,1,0:T(8,128)(2,1)S(1)}, u32[]{:S(2)}, u32[]{:S(2)}) collective-permute-start(bf16[4,32,2048]{2,1,0:T(8,128)(2,1)S(1)} %fusion.57), channel_id=1, source_target_pairs={{0,4},{4,8},{8,12},{12,0},{1,5},{5,9},{9,13},{13,1},{2,6},{6,10},{... | collective-permute-start | bytes 1572872 | tf_op jit(solution)/shard_map/ppermute | solution.py:41
  204.0 14.4 %collective-permute-start.27 = (bf16[64,3584]{1,0:T(8,128)(2,1)S(1)}, bf16[64,3584]{1,0:T(8,128)(2,1)S(1)}, u32[]{:S(2)}, u32[]{:S(2)}) collective-permute-start(bf16[64,3584]{1,0:T(8,128)(2,1)S(1)} %fusion.40), channel_id=1, source_target_pairs={{0,2},{1,3},{2,0},{3,1},{4,6},{5,7},{6,4},{7,5},{8,10},{9,11},{10,... | collective-permute-start | bytes 1376264 | tf_op jit(solution)/shard_map/ppermute | solution.py:36
  207.8 18.4 %collective-permute-start.21 = (bf16[64,3584]{1,0:T(8,128)(2,1)}, bf16[64,3584]{1,0:T(8,128)(2,1)S(1)}, u32[]{:S(2)}, u32[]{:S(2)}) collective-permute-start(bf16[64,3584]{1,0:T(8,128)(2,1)} %fusion.41), channel_id=1, source_target_pairs={{0,2},{1,3},{2,0},{3,1},{4,6},{5,7},{6,4},{7,5},{8,10},{9,11},{10,... | collective-permute-start | bytes 1376264 | tf_op jit(solution)/shard_map/ppermute | solution.py:36
  217.1 13.4 %collective-permute-start.24 = (bf16[4,32,2048]{2,1,0:T(8,128)(2,1)S(1)}, bf16[4,32,2048]{2,1,0:T(8,128)(2,1)}, u32[]{:S(2)}, u32[]{:S(2)}) collective-permute-start(bf16[4,32,2048]{2,1,0:T(8,128)(2,1)S(1)} %fusion.20), channel_id=1, source_target_pairs={{0,12},{4,0},{8,4},{12,8},{1,13},{5,1},{9,5},{13,9},{2,14},{6,2},{... | collective-permute-start | bytes 1572872 | tf_op jit(solution)/shard_map/ppermute | solution.py:41
  219.4 15.5 %collective-permute-start.28 = (bf16[128,3584]{1,0:T(8,128)(2,1)}, bf16[128,3584]{1,0:T(8,128)(2,1)}, u32[]{:S(2)}, u32[]{:S(2)}) collective-permute-start(bf16[128,3584]{1,0:T(8,128)(2,1)} %pad_maximum_fusion.17), channel_id=1, source_target_pairs={{0,1},{1,0},{2,3},{3,2},{4,5},{5,4},{6,7},{7,6},{8,9},{9,8},{10,11... | collective-permute-start | bytes 2752520 | tf_op jit(solution)/shard_map/ppermute | solution.py:36
  228.1 24.4 %collective-permute-start.22 = (bf16[64,3584]{1,0:T(8,128)(2,1)S(1)}, bf16[64,3584]{1,0:T(8,128)(2,1)S(1)}, u32[]{:S(2)}, u32[]{:S(2)}) collective-permute-start(bf16[64,3584]{1,0:T(8,128)(2,1)S(1)} %fusion.44), channel_id=1, source_target_pairs={{0,2},{1,3},{2,0},{3,1},{4,6},{5,7},{6,4},{7,5},{8,10},{9,11},{10,... | collective-permute-start | bytes 1376264 | tf_op jit(solution)/shard_map/ppermute | solution.py:36
  230.6 22.6 %collective-permute-start.31 = (bf16[4,32,2048]{2,1,0:T(8,128)(2,1)}, bf16[4,32,2048]{2,1,0:T(8,128)(2,1)}, u32[]{:S(2)}, u32[]{:S(2)}) collective-permute-start(bf16[4,32,2048]{2,1,0:T(8,128)(2,1)} %collective-permute-done.24), channel_id=1, source_target_pairs={{0,12},{4,0},{8,4},{12,8},{1,13},{5,1},{9,5},{13,9},{2,14},{6,2},{... | collective-permute-start | bytes 1572872 | tf_op jit(solution)/shard_map/ppermute | solution.py:41
  252.4 19.6 %collective-permute-start.29 = (f32[128,3584]{1,0:T(8,128)S(1)}, f32[128,3584]{1,0:T(8,128)S(1)}, u32[]{:S(2)}, u32[]{:S(2)}) collective-permute-start(f32[128,3584]{1,0:T(8,128)S(1)} %slice.374), channel_id=1, source_target_pairs={{0,1},{1,0},{2,3},{3,2},{4,5},{5,4},{6,7},{7,6},{8,9},{9,8},{10,11... | collective-permute-start | bytes 5505032 | tf_op jit(solution)/shard_map/ppermute | solution.py:36
  252.6 18.1 %collective-permute-start.23 = (bf16[128,3584]{1,0:T(8,128)(2,1)S(1)}, bf16[128,3584]{1,0:T(8,128)(2,1)S(1)}, u32[]{:S(2)}, u32[]{:S(2)}) collective-permute-start(bf16[128,3584]{1,0:T(8,128)(2,1)S(1)} %pad_maximum_fusion.16), channel_id=1, source_target_pairs={{0,1},{1,0},{2,3},{3,2},{4,5},{5,4},{6,7},{7,6},{8,9},{9,8},{10,11... | collective-permute-start | bytes 2752520 | tf_op jit(solution)/shard_map/ppermute | solution.py:36
  253.1 15.4 %collective-permute-start.32 = (bf16[4,32,2048]{2,1,0:T(8,128)(2,1)}, bf16[4,32,2048]{2,1,0:T(8,128)(2,1)S(1)}, u32[]{:S(2)}, u32[]{:S(2)}) collective-permute-start(bf16[4,32,2048]{2,1,0:T(8,128)(2,1)} %collective-permute-done.31), channel_id=1, source_target_pairs={{0,12},{4,0},{8,4},{12,8},{1,13},{5,1},{9,5},{13,9},{2,14},{6,2},{... | collective-permute-start | bytes 1572872 | tf_op jit(solution)/shard_map/ppermute | solution.py:41
  253.1 51.3 %collective-permute-start.35 = (bf16[4,32,2048]{2,1,0:T(8,128)(2,1)}, bf16[4,32,2048]{2,1,0:T(8,128)(2,1)}, u32[]{:S(2)}, u32[]{:S(2)}) collective-permute-start(bf16[4,32,2048]{2,1,0:T(8,128)(2,1)} %get-tuple-element.91), channel_id=1, source_target_pairs={{0,8},{4,12},{8,0},{12,4},{1,9},{5,13},{9,1},{13,5},{2,10},{6,14},... | collective-permute-start | bytes 1572872 | tf_op jit(solution)/shard_map/ppermute | solution.py:41
  253.7 50.7 %collective-permute-start.30 = (bf16[4,32,2048]{2,1,0:T(8,128)(2,1)S(1)}, bf16[4,32,2048]{2,1,0:T(8,128)(2,1)}, u32[]{:S(2)}, u32[]{:S(2)}) collective-permute-start(bf16[4,32,2048]{2,1,0:T(8,128)(2,1)S(1)} %copy-done.48), channel_id=1, source_target_pairs={{0,12},{4,0},{8,4},{12,8},{1,13},{5,1},{9,5},{13,9},{2,14},{6,2},{... | collective-permute-start | bytes 1572872 | tf_op jit(solution)/shard_map/ppermute | solution.py:41
  272.2 28.5 %collective-permute-start.34 = (bf16[64,3584]{1,0:T(8,128)(2,1)S(1)}, bf16[64,3584]{1,0:T(8,128)(2,1)S(1)}, u32[]{:S(2)}, u32[]{:S(2)}) collective-permute-start(bf16[64,3584]{1,0:T(8,128)(2,1)S(1)} %fusion.36), channel_id=1, source_target_pairs={{0,2},{1,3},{2,0},{3,1},{4,6},{5,7},{6,4},{7,5},{8,10},{9,11},{10,... | collective-permute-start | bytes 1376264 | tf_op jit(solution)/shard_map/ppermute | solution.py:36
  280.9 22.5 %collective-permute-start.33 = (f32[128,3584]{1,0:T(8,128)S(1)}, f32[128,3584]{1,0:T(8,128)S(1)}, u32[]{:S(2)}, u32[]{:S(2)}) collective-permute-start(f32[128,3584]{1,0:T(8,128)S(1)} %slice.379), channel_id=1, source_target_pairs={{0,1},{1,0},{2,3},{3,2},{4,5},{5,4},{6,7},{7,6},{8,9},{9,8},{10,11... | collective-permute-start | bytes 5505032 | tf_op jit(solution)/shard_map/ppermute | solution.py:36
  290.9 19.0 %collective-permute-start.36 = (bf16[4,32,2048]{2,1,0:T(8,128)(2,1)S(1)}, bf16[4,32,2048]{2,1,0:T(8,128)(2,1)S(1)}, u32[]{:S(2)}, u32[]{:S(2)}) collective-permute-start(bf16[4,32,2048]{2,1,0:T(8,128)(2,1)S(1)} %fusion.58), channel_id=1, source_target_pairs={{0,4},{4,8},{8,12},{12,0},{1,5},{5,9},{9,13},{13,1},{2,6},{6,10},{... | collective-permute-start | bytes 1572872 | tf_op jit(solution)/shard_map/ppermute | solution.py:41
  302.2 25.3 %collective-permute-start.37 = (bf16[64,3584]{1,0:T(8,128)(2,1)S(1)}, bf16[64,3584]{1,0:T(8,128)(2,1)S(1)}, u32[]{:S(2)}, u32[]{:S(2)}) collective-permute-start(bf16[64,3584]{1,0:T(8,128)(2,1)S(1)} %fusion.34), channel_id=1, source_target_pairs={{0,2},{1,3},{2,0},{3,1},{4,6},{5,7},{6,4},{7,5},{8,10},{9,11},{10,... | collective-permute-start | bytes 1376264 | tf_op jit(solution)/shard_map/ppermute | solution.py:36
  303.5 18.6 %collective-permute-start.39 = (bf16[64,3584]{1,0:T(8,128)(2,1)S(1)}, bf16[64,3584]{1,0:T(8,128)(2,1)S(1)}, u32[]{:S(2)}, u32[]{:S(2)}) collective-permute-start(bf16[64,3584]{1,0:T(8,128)(2,1)S(1)} %fusion.35), channel_id=1, source_target_pairs={{0,2},{1,3},{2,0},{3,1},{4,6},{5,7},{6,4},{7,5},{8,10},{9,11},{10,... | collective-permute-start | bytes 1376264 | tf_op jit(solution)/shard_map/ppermute | solution.py:36
  311.7 15.7 %collective-permute-start.42 = (bf16[4,32,2048]{2,1,0:T(8,128)(2,1)S(1)}, bf16[4,32,2048]{2,1,0:T(8,128)(2,1)S(1)}, u32[]{:S(2)}, u32[]{:S(2)}) collective-permute-start(bf16[4,32,2048]{2,1,0:T(8,128)(2,1)S(1)} %fusion.15), channel_id=1, source_target_pairs={{0,12},{4,0},{8,4},{12,8},{1,13},{5,1},{9,5},{13,9},{2,14},{6,2},{... | collective-permute-start | bytes 1572872 | tf_op jit(solution)/shard_map/ppermute | solution.py:41
  338.4 31.8 %collective-permute-start.43 = (f32[128,3584]{1,0:T(8,128)S(1)}, f32[128,3584]{1,0:T(8,128)S(1)}, u32[]{:S(2)}, u32[]{:S(2)}) collective-permute-start(f32[128,3584]{1,0:T(8,128)S(1)} %slice.387), channel_id=1, source_target_pairs={{0,1},{1,0},{2,3},{3,2},{4,5},{5,4},{6,7},{7,6},{8,9},{9,8},{10,11... | collective-permute-start | bytes 5505032 | tf_op jit(solution)/shard_map/ppermute | solution.py:36
  338.5 16.4 %collective-permute-start.47 = (bf16[4,32,2048]{2,1,0:T(8,128)(2,1)S(1)}, bf16[4,32,2048]{2,1,0:T(8,128)(2,1)S(1)}, u32[]{:S(2)}, u32[]{:S(2)}) collective-permute-start(bf16[4,32,2048]{2,1,0:T(8,128)(2,1)S(1)} %collective-permute-done.42), channel_id=1, source_target_pairs={{0,12},{4,0},{8,4},{12,8},{1,13},{5,1},{9,5},{13,9},{2,14},{6,2},{... | collective-permute-start | bytes 1572872 | tf_op jit(solution)/shard_map/ppermute | solution.py:41
  354.9 15.3 %collective-permute-start.48 = (bf16[4,32,2048]{2,1,0:T(8,128)(2,1)S(1)}, bf16[4,32,2048]{2,1,0:T(8,128)(2,1)S(1)}, u32[]{:S(2)}, u32[]{:S(2)}) collective-permute-start(bf16[4,32,2048]{2,1,0:T(8,128)(2,1)S(1)} %collective-permute-done.47), channel_id=1, source_target_pairs={{0,12},{4,0},{8,4},{12,8},{1,13},{5,1},{9,5},{13,9},{2,14},{6,2},{... | collective-permute-start | bytes 1572872 | tf_op jit(solution)/shard_map/ppermute | solution.py:41
  360.1 28.3 %collective-permute-start.38 = (bf16[128,3584]{1,0:T(8,128)(2,1)}, bf16[128,3584]{1,0:T(8,128)(2,1)}, u32[]{:S(2)}, u32[]{:S(2)}) collective-permute-start(bf16[128,3584]{1,0:T(8,128)(2,1)} %pad_maximum_fusion.18), channel_id=1, source_target_pairs={{0,1},{1,0},{2,3},{3,2},{4,5},{5,4},{6,7},{7,6},{8,9},{9,8},{10,11... | collective-permute-start | bytes 2752520 | tf_op jit(solution)/shard_map/ppermute | solution.py:36
  391.4 42.9 %collective-permute-start.41 = (bf16[128,3584]{1,0:T(8,128)(2,1)S(1)}, bf16[128,3584]{1,0:T(8,128)(2,1)S(1)}, u32[]{:S(2)}, u32[]{:S(2)}) collective-permute-start(bf16[128,3584]{1,0:T(8,128)(2,1)S(1)} %pad_maximum_fusion.19), channel_id=1, source_target_pairs={{0,1},{1,0},{2,3},{3,2},{4,5},{5,4},{6,7},{7,6},{8,9},{9,8},{10,11... | collective-permute-start | bytes 2752520 | tf_op jit(solution)/shard_map/ppermute | solution.py:36
  392.0 13.6 %collective-permute-start.44 = (bf16[64,3584]{1,0:T(8,128)(2,1)}, bf16[64,3584]{1,0:T(8,128)(2,1)S(1)}, u32[]{:S(2)}, u32[]{:S(2)}) collective-permute-start(bf16[64,3584]{1,0:T(8,128)(2,1)} %fusion.25), channel_id=1, source_target_pairs={{0,2},{1,3},{2,0},{3,1},{4,6},{5,7},{6,4},{7,5},{8,10},{9,11},{10,... | collective-permute-start | bytes 1376264 | tf_op jit(solution)/shard_map/ppermute | solution.py:36
  394.2 21.3 %collective-permute-start.50 = (bf16[64,3584]{1,0:T(8,128)(2,1)S(1)}, bf16[64,3584]{1,0:T(8,128)(2,1)S(1)}, u32[]{:S(2)}, u32[]{:S(2)}) collective-permute-start(bf16[64,3584]{1,0:T(8,128)(2,1)S(1)} %fusion.21), channel_id=1, source_target_pairs={{0,2},{1,3},{2,0},{3,1},{4,6},{5,7},{6,4},{7,5},{8,10},{9,11},{10,... | collective-permute-start | bytes 1376264 | tf_op jit(solution)/shard_map/ppermute | solution.py:36
  407.0 18.3 %collective-permute-start.45 = (bf16[64,3584]{1,0:T(8,128)(2,1)S(1)}, bf16[64,3584]{1,0:T(8,128)(2,1)S(1)}, u32[]{:S(2)}, u32[]{:S(2)}) collective-permute-start(bf16[64,3584]{1,0:T(8,128)(2,1)S(1)} %fusion.28), channel_id=1, source_target_pairs={{0,2},{1,3},{2,0},{3,1},{4,6},{5,7},{6,4},{7,5},{8,10},{9,11},{10,... | collective-permute-start | bytes 1376264 | tf_op jit(solution)/shard_map/ppermute | solution.py:36
  416.8 17.4 %collective-permute-start.51 = (bf16[64,3584]{1,0:T(8,128)(2,1)S(1)}, bf16[64,3584]{1,0:T(8,128)(2,1)S(1)}, u32[]{:S(2)}, u32[]{:S(2)}) collective-permute-start(bf16[64,3584]{1,0:T(8,128)(2,1)S(1)} %fusion.24), channel_id=1, source_target_pairs={{0,2},{1,3},{2,0},{3,1},{4,6},{5,7},{6,4},{7,5},{8,10},{9,11},{10,... | collective-permute-start | bytes 1376264 | tf_op jit(solution)/shard_map/ppermute | solution.py:36
  (62 other events, 751.3 us)
Sparse Core Ops, SparseCore 0:
  36.9 45.4 all-gather.8
  84.0 44.6 all-gather.10
  130.2 28.8 all-gather.14
  182.7 30.2 all-gather.12

commit v7 on v6

--- a/solution.py
+++ b/solution.py
@@ -154,14 +154,15 @@
         got = swap(first, "col", 1)
         cut = half // 2
         own, give = part[:cut] + got[:cut], part[cut:half] + got[cut:]
-        mask, mark = 2, None
+        mask, marks = 2, None
         while True:
             sent = pack(give, form)
-            mark = sent if mark is None else mark
-            own = own + unpack(swap(sent, "col", mask), form)
+            got = swap(sent, "col", mask)
+            marks = marks or ([first], [sent], [got])
+            own = own + unpack(got, form)
             mask *= 2
             if mask >= count:
-                return own, mark, first
+                return own, *marks
             cut = own.shape[0] // 2
             own, give = own[:cut], own[cut:]
 
@@ -181,15 +182,16 @@
     moved = {}
 
     def project(half, j, form, after):
-        after = after + [mark for mark, _ in marks[-2:-1]] + [total for _, total in marks[-3:-2]]
+        for sent in [mark[1] for mark in marks[-2:-1]] + [mark[2] for mark in marks[-3:-2]]:
+            after = after + sent
         if (half, j) in xs:
             x = tie(xs[half, j], after)
         else:
             xs[half, j] = x = joined([tie(piece_of(half, k), after) for k in steps[j]])
         weight = {"gate": w_gate, "up": w_up, "tangent": query}[form]
-        sums[half, j, form], mark, start = sum_over_col(matmul(x, weight), form)
-        marks.append((mark, sums[half, j, form]))
-        return [start]
+        sums[half, j, form], *mark = sum_over_col(matmul(x, weight), form)
+        marks.append(mark)
+        return mark[0]
 
     def hidden_rows(half, j, after):
         if half == 0:
@@ -221,57 +223,56 @@
             total = total + tie(moved[half, k], after).astype(jnp.float32)
         curv = own_rows(curvature, (me + 1) % ring * shard, halves[half])
         pieces = [None] * last + [(curv * total).astype(jnp.bfloat16)]
-        for k in reversed(range(last)):
+        cut = ring // 4
+        for k in reversed(range(cut, last)):
             pieces[k] = shift(pieces[k + 1], "row", -1)
+        piece = tie(pieces[last], [pieces[steps[-1][0]]])
+        for k in range(cut):
+            pieces[k] = piece = shift(piece, "row")
         return pieces
 
     turned, bars = [], []
 
     def back(half, j, pieces, after):
-        x = joined([pieces[k] for k in steps[j]])
+        x = joined([tie(pieces[k], after) for k in steps[j]])
         turned.append(tie(xs[half, j], pieces[last:]).T)
-        own, mark, _ = sum_over_col(times_down(tie(x, after), w_down), "back")
-        bar = (own * gains[half][j]).astype(jnp.bfloat16)
-        whole, near = gather_over_col(bar)
+        own, first, sent, got = sum_over_col(times_down(x, w_down), "back")
+        whole, near = gather_over_col((own * gains[half][j]).astype(jnp.bfloat16))
         bars.append(whole)
-        return mark, bar, near
+        return first, sent, got, [near]
 
     tail = GROUPS - 1
     early = []
     for j in range(GROUPS):
-        start = project(0, j, "up", [])
+        first = project(0, j, "up", [])
         if j:
-            early.append(hidden_rows(0, j - 1, start))
+            early.append(hidden_rows(0, j - 1, first))
         project(0, j, "gate", [])
-        start = project(0, j, "tangent", [])
+        first = project(0, j, "tangent", [] if j else spread[:])
         if j == 0:
-            spread.append(lax.all_gather(tie(own[1], spread + start), "row"))
+            spread.append(lax.all_gather(tie(own[1], spread + first), "row"))
         else:
-            share_gain(j - 1, start)
-    start = project(1, 0, "tangent", [near for _, near in early])
-    ready = [out_sums(0, j, early[j][0], []) for j in range(tail)]
-    hidden, _ = hidden_rows(0, tail, start)
+            share_gain(j - 1, first)
+    ready = [out_sums(0, j, early[j][0], marks[-2][1]) for j in range(tail)]
+    first = project(1, 0, "tangent", ready)
+    hidden, _ = hidden_rows(0, tail, first)
     for j in range(1, GROUPS):
-        start = project(1, j, "tangent", ready)
-    share_gain(tail, start)
+        first = project(1, j, "tangent", [])
+    share_gain(tail, first)
     ready = [out_sums(0, tail, hidden, [])]
     pieces = scaled_pieces(0, [])
 
     hidden = [hidden_rows(1, j, []) for j in range(GROUPS)]
-    for j in range(tail):
-        ready = [out_sums(1, j, hidden[j][0], ready)]
-    mark, bar, near = back(0, tail, pieces, ready)
-    out_sums(1, tail, hidden[tail][0], [mark])
-    after = [mark]
+    first, sent, got, near = back(0, tail, pieces, [])
+    ready = [out_sums(1, j, hidden[j][0], first) for j in range(tail)]
+    ready = [out_sums(1, tail, hidden[tail][0], ready + sent)]
     for j in reversed(range(tail)):
-        mark, nextbar, nextnear = back(0, j, pieces, after)
-        after = [mark, bar]
-        bar, lastnear, near = nextbar, near, nextnear
-    pieces = scaled_pieces(1, after)
-    after = [lastnear, bar]
+        _, sent, nextgot, nextnear = back(0, j, pieces, ready + got)
+    pieces = scaled_pieces(1, sent + near)
+    after = nextgot
     for j in reversed(range(GROUPS)):
-        mark, bar, nextnear = back(1, j, pieces, after)
-        after, near = [mark, near], nextnear
+        _, sent, _, near = back(1, j, pieces, after)
+        after, nextnear = sent + nextnear, near
     return last_product(turned, bars, tokens)
 
 

time: 473 us -> 533 us (1.13)
  waiting for transfers between devices: 143 us -> 187 us
  matrix products: 121 us -> 109 us
  other arithmetic: 58 us -> 67.9 us
  starting transfers between devices: 62.8 us -> 72.3 us
  local copies, waits for them, and re-layouts: 44.1 us -> 53.1 us
    ppermute x13, waiting for transfers between devices: 64.7 us -> 92.3 us  [shift(): lax.ppermute(values, axis, [(i, (i + by) % count) for i in range(count)])]
    all_gather x1, waiting for transfers between devices: 10.9 us -> 26.8 us  [per_device(): spread = [lax.all_gather(own[0], 'row')]]
    dot_general x12, matrix products: 89.4 us -> 75.6 us  [matmul(): return jnp.dot(left, right, preferred_element_type=jnp.float32)]
    all_gather x2, starting transfers between devices: 0.37 us -> 12.3 us  [share_gain(): both = lax.all_gather(tie(gains[0][j], after), 'grp')]
    unnamed x106 -> x142, local copies, waits for them, and re-layouts: 14.3 us -> 19.1 us
    concatenate x14 -> x15, other arithmetic: 10.4 us -> 12.5 us  [gather_over_col(): values = jnp.concatenate([values, got], axis=0)]
  transfers between devices with their start and end apart: 57 -> 57, of which waited for: 21 -> 19; matrix products, arithmetic and copies ran while one was open for 40% -> 33% of each run, Pallas kernels for 0% -> 0%
where the time goes in v7:
time: 533 us; the launch traced here: 527 us
  waiting for transfers between devices  187 us (35%)
  matrix products  109 us (20%)
  starting transfers between devices  72.3 us (14%)
  other arithmetic  67.9 us (13%)
  local copies, waits for them, and re-layouts  53.1 us (10%)
  Pallas kernels  22.5 us (4%)
  between operations  14.5 us (3%)
    ppermute x13, waiting for transfers between devices, shift(): lax.ppermute(values, axis, [(i, (i + by) % count) for i in range(count)])  92.3 us
    dot_general x12, matrix products, matmul(): return jnp.dot(left, right, preferred_element_type=jnp.float32)  75.6 us
    ppermute x40, waiting for transfers between devices, swap(): return lax.ppermute(values, axis, [(i, i ^ mask) for i in range(count)])  65.3 us
    ppermute x13, starting transfers between devices, shift(): lax.ppermute(values, axis, [(i, (i + by) % count) for i in range(count)])  34.2 us
    dot_general x4, matrix products, times_down(): lax.dot_general(left, w_down, (((1,), (1,)), ((), ())), preferred_element...  33.8 us
    all_gather x1, waiting for transfers between devices, per_device(): spread = [lax.all_gather(own[0], 'row')]  26.8 us
    ppermute x40, starting transfers between devices, swap(): return lax.ppermute(values, axis, [(i, i ^ mask) for i in range(count)])  25.8 us
    pallas_call x1, Pallas kernels, last_product(): pl.pallas_call(functools.partial(last_kernel, 1.0 / tokens, len(turned)),...  22.5 us
  transfers between devices with their start and end apart: 57, of which 19 were waited for; matrix products, arithmetic and copies ran while one was open for 33% of the time, Pallas kernels for 0%

profile of v7, /device:TPU:0, one launch (start us, length us, event | category | flops | bytes accessed | tf_op | source)
XLA Modules:
  0.0 526.8 jit_solution(17179939599902471060)
XLA Ops:
  8.7 3.1 collective-permute-start
  11.8 13.9 %collective-permute-done = bf16[4,32,2048]{2,1,0:T(8,128)(2,1)S(1)} collective-permute-done((bf16[4,32,2048]{2,1,0:T(8,128)(2,1)S(1)}, bf16[4,32,2048]{2,1,0:T(8,128)(2,1)S(1)}, u32[]{:S(2)}, u32[]{:S(2)}) %collective-permute-start) | collective-permute-done | bytes 524320 | tf_op jit(solution)/shard_map/ppermute | solution.py:41
  25.8 7.6 %fusion.78 = f32[256,3584]{1,0:T(8,128)S(1)} fusion(bf16[256,2048]{1,0:T(8,128)(2,1)S(1)} %bitcast.143, bf16[2048,3584]{1,0:T(8,128)(2,1)} %param.8), kind=kOutput, calls=%fused_computation.190 | convolution fusion | flops 3758096384 | bytes 19398656 | tf_op jit(solution)/shard_map/dot_general | solution.py:19
  36.8 7.3 %fusion.77 = f32[256,3584]{1,0:T(8,128)S(1)} fusion(bf16[256,2048]{1,0:T(8,128)(2,1)S(1)} %bitcast.144, bf16[2048,3584]{1,0:T(8,128)(2,1)} %param.7), kind=kOutput, calls=%fused_computation.189 | convolution fusion | flops 3758096384 | bytes 19398656 | tf_op jit(solution)/shard_map/dot_general | solution.py:19
  53.2 2.4 fusion.53
  55.6 26.8 %all-gather.9.cloned.1.call-done = bf16[16,32,2048]{2,1,0:T(8,128)(2,1)} async-done(((bf16[4,32,2048]{2,1,0:T(8,128)(2,1)}), bf16[16,32,2048]{2,1,0:T(8,128)(2,1)}) %all-gather.9.cloned.1.call-update) | async-done | bytes 2097168 | tf_op jit(solution)/shard_map/all_gather | solution.py:129
  82.4 7.4 %fusion.79 = f32[256,3584]{1,0:T(8,128)S(1)} fusion(bf16[256,2048]{1,0:T(8,128)(2,1)S(1)} %bitcast.145, bf16[2048,3584]{1,0:T(8,128)(2,1)} %param.10), kind=kOutput, calls=%fused_computation.191 | convolution fusion | flops 3758096384 | bytes 19398656 | tf_op jit(solution)/shard_map/dot_general | solution.py:19
  91.2 3.1 copy-done.50
  94.5 3.9 fusion.81
  105.3 12.3 %all-gather.15.cloned.1.call-start = ((), (), s32[]{:S(2)}) async-start(), calls=%async_computation.3 | async-start | bytes 2752512 | tf_op jit(solution)/shard_map/all_gather | solution.py:206
  117.6 2.4 fusion.51
  128.4 7.3 %fusion.80 = f32[256,3584]{1,0:T(8,128)S(1)} fusion(bf16[256,2048]{1,0:T(8,128)(2,1)S(1)} %bitcast.148, bf16[2048,3584]{1,0:T(8,128)(2,1)} %param.7), kind=kOutput, calls=%fused_computation.192 | convolution fusion | flops 3758096384 | bytes 19398656 | tf_op jit(solution)/shard_map/dot_general | solution.py:19
  139.9 3.5 multiply_convert_fusion.1
  144.0 7.2 %fusion.82 = f32[256,3584]{1,0:T(8,128)S(1)} fusion(bf16[256,2048]{1,0:T(8,128)(2,1)S(1)} %bitcast.149, bf16[2048,3584]{1,0:T(8,128)(2,1)} %param.10), kind=kOutput, calls=%fused_computation.194 | convolution fusion | flops 3758096384 | bytes 19398656 | tf_op jit(solution)/shard_map/dot_general | solution.py:19
  163.6 7.7 %convolution_convert_fusion.1 = bf16[256,2048]{1,0:T(8,128)(2,1)S(1)} fusion(bf16[256,3584]{1,0:T(8,128)(2,1)S(1)} %pad_maximum_fusion, bf16[3584,2048]{1,0:T(8,128)(2,1)} %param.9), kind=kOutput, calls=%fused_computation.1 | convolution fusion | flops 3758620672 | bytes 17563648 | tf_op jit(solution)/shard_map/dot_general | solution.py:19
  176.4 3.9 fusion.83
  182.8 5.1 collective-permute-done.12
  189.2 3.6 multiply_convert_fusion
  193.6 3.9 fusion.84
  200.0 2.6 dynamic-slice_bitcast_fusion.8
  209.9 2.5 fusion.36
  213.0 7.6 %fusion = f32[256,2048]{1,0:T(8,128)S(1)} fusion(bf16[3584,2048]{1,0:T(8,128)(2,1)} %param.9, bf16[128,3584]{1,0:T(8,128)(2,1)S(1)} %collective-permute-done.16, bf16[64,3584]{1,0:T(8,128)(2,1)} %collective-permute-done.15, bf16[64,3584]{1,0:T(8,128)(2,1)S(1)} %get-tuple-element.77), kind=kOutput, calls=%fused_computation.3 | convolution fusion | flops 3763601408 | bytes 18612224 | tf_op jit(solution)/shard_map/dot_general | solution.py:19
  227.5 4.6 collective-permute-done.21
  232.1 2.6 all-gather.13.cloned.1.call-done
  242.7 12.7 %collective-permute-start.28 = (bf16[4,32,2048]{2,1,0:T(8,128)(2,1)S(1)}, bf16[4,32,2048]{2,1,0:T(8,128)(2,1)S(1)}, u32[]{:S(2)}, u32[]{:S(2)}) collective-permute-start(bf16[4,32,2048]{2,1,0:T(8,128)(2,1)S(1)} %fusion.15), channel_id=1, source_target_pairs={{0,12},{4,0},{8,4},{12,8},{1,13},{5,1},{9,5},{13,9},{2,14},{6,2},{... | collective-permute-start | bytes 1572872 | tf_op jit(solution)/shard_map/ppermute | solution.py:41
  257.9 8.8 %collective-permute-done.28 = bf16[4,32,2048]{2,1,0:T(8,128)(2,1)S(1)} collective-permute-done((bf16[4,32,2048]{2,1,0:T(8,128)(2,1)S(1)}, bf16[4,32,2048]{2,1,0:T(8,128)(2,1)S(1)}, u32[]{:S(2)}, u32[]{:S(2)}) %collective-permute-start.28) | collective-permute-done | bytes 524320 | tf_op jit(solution)/shard_map/ppermute | solution.py:41
  269.1 7.6 %fusion.85 = f32[256,3584]{1,0:T(8,128)S(1)} fusion(bf16[256,2048]{1,0:T(8,128)(2,1)} %bitcast.168, bf16[3584,2048]{1,0:T(8,128)(2,1)} %param.9), kind=kOutput, calls=%fused_computation.197 | convolution fusion | flops 3758096384 | bytes 19398656 | tf_op jit(solution)/shard_map/dot_general | solution.py:23
  278.1 3.2 collective-permute-start.33
  282.6 7.7 %convolution_convert_fusion = bf16[256,2048]{1,0:T(8,128)(2,1)S(1)} fusion(bf16[256,3584]{1,0:T(8,128)(2,1)S(1)} %pad_maximum_fusion.2, bf16[3584,2048]{1,0:T(8,128)(2,1)} %param.9), kind=kOutput, calls=%fused_computation | convolution fusion | flops 3758620672 | bytes 17563648 | tf_op jit(solution)/shard_map/dot_general | solution.py:19
  294.2 3.9 fusion.86
  299.1 5.2 collective-permute-done.32
  306.6 7.6 %fusion.87 = f32[256,3584]{1,0:T(8,128)S(1)} fusion(bf16[256,2048]{1,0:T(8,128)(2,1)} %bitcast.166, bf16[3584,2048]{1,0:T(8,128)(2,1)} %param.9), kind=kOutput, calls=%fused_computation.199 | convolution fusion | flops 3758096384 | bytes 19398656 | tf_op jit(solution)/shard_map/dot_general | solution.py:23
  321.3 30.6 %collective-permute-done.37 = bf16[4,32,2048]{2,1,0:T(8,128)(2,1)S(1)} collective-permute-done((bf16[4,32,2048]{2,1,0:T(8,128)(2,1)S(1)}, bf16[4,32,2048]{2,1,0:T(8,128)(2,1)S(1)}, u32[]{:S(2)}, u32[]{:S(2)}) %collective-permute-start.37) | collective-permute-done | bytes 524320 | tf_op jit(solution)/shard_map/ppermute | solution.py:41
  353.1 2.6 collective-permute-start.42
  357.0 9.7 %collective-permute-done.39 = bf16[64,3584]{1,0:T(8,128)(2,1)} collective-permute-done((bf16[64,3584]{1,0:T(8,128)(2,1)S(1)}, bf16[64,3584]{1,0:T(8,128)(2,1)}, u32[]{:S(2)}, u32[]{:S(2)}) %collective-permute-start.39) | collective-permute-done | bytes 458784 | tf_op jit(solution)/shard_map/ppermute | solution.py:36
  366.7 20.3 %collective-permute-done.42 = bf16[4,32,2048]{2,1,0:T(8,128)(2,1)S(1)} collective-permute-done((bf16[4,32,2048]{2,1,0:T(8,128)(2,1)S(1)}, bf16[4,32,2048]{2,1,0:T(8,128)(2,1)S(1)}, u32[]{:S(2)}, u32[]{:S(2)}) %collective-permute-start.42) | collective-permute-done | bytes 524320 | tf_op jit(solution)/shard_map/ppermute | solution.py:41
  388.8 11.3 %fusion.88 = f32[256,3584]{1,0:T(8,128)} fusion(bf16[256,2048]{1,0:T(8,128)(2,1)} %bitcast.169, bf16[3584,2048]{1,0:T(8,128)(2,1)} %param.9), kind=kOutput, calls=%fused_computation.200 | convolution fusion | flops 3758096384 | bytes 19398656 | tf_op jit(solution)/shard_map/dot_general | solution.py:23
  406.2 2.5 collective-permute-start.47
  410.0 2.8 fusion.20
  412.8 4.5 collective-permute-done.40
  417.3 15.5 %collective-permute-done.48 = bf16[4,32,2048]{2,1,0:T(8,128)(2,1)S(1)} collective-permute-done((bf16[4,32,2048]{2,1,0:T(8,128)(2,1)S(1)}, bf16[4,32,2048]{2,1,0:T(8,128)(2,1)S(1)}, u32[]{:S(2)}, u32[]{:S(2)}) %collective-permute-start.48) | collective-permute-done | bytes 524320 | tf_op jit(solution)/shard_map/ppermute | solution.py:41
  433.0 7.3 %fusion.89 = f32[256,3584]{1,0:T(8,128)S(1)} fusion(bf16[256,2048]{1,0:T(8,128)(2,1)S(1)} %bitcast.167, bf16[3584,2048]{1,0:T(8,128)(2,1)} %param.9), kind=kOutput, calls=%fused_computation.201 | convolution fusion | flops 3758096384 | bytes 19398656 | tf_op jit(solution)/shard_map/dot_general | solution.py:23
  446.2 2.3 copy.33
  456.3 9.9 %collective-permute-done.44 = bf16[64,3584]{1,0:T(8,128)(2,1)S(1)} collective-permute-done((bf16[64,3584]{1,0:T(8,128)(2,1)}, bf16[64,3584]{1,0:T(8,128)(2,1)S(1)}, u32[]{:S(2)}, u32[]{:S(2)}) %collective-permute-start.44) | collective-permute-done | bytes 458784 | tf_op jit(solution)/shard_map/ppermute | solution.py:36
  468.3 7.8 %collective-permute-done.50 = bf16[64,3584]{1,0:T(8,128)(2,1)S(1)} collective-permute-done((bf16[64,3584]{1,0:T(8,128)(2,1)S(1)}, bf16[64,3584]{1,0:T(8,128)(2,1)S(1)}, u32[]{:S(2)}, u32[]{:S(2)}) %collective-permute-start.50) | collective-permute-done | bytes 458784 | tf_op jit(solution)/shard_map/ppermute | solution.py:36
  478.4 7.5 %collective-permute-done.45 = bf16[64,3584]{1,0:T(8,128)(2,1)S(1)} collective-permute-done((bf16[64,3584]{1,0:T(8,128)(2,1)S(1)}, bf16[64,3584]{1,0:T(8,128)(2,1)S(1)}, u32[]{:S(2)}, u32[]{:S(2)}) %collective-permute-start.45) | collective-permute-done | bytes 458784 | tf_op jit(solution)/shard_map/ppermute | solution.py:36
  486.0 8.8 %collective-permute-done.51 = bf16[64,3584]{1,0:T(8,128)(2,1)S(1)} collective-permute-done((bf16[64,3584]{1,0:T(8,128)(2,1)S(1)}, bf16[64,3584]{1,0:T(8,128)(2,1)S(1)}, u32[]{:S(2)}, u32[]{:S(2)}) %collective-permute-start.51) | collective-permute-done | bytes 458784 | tf_op jit(solution)/shard_map/ppermute | solution.py:36
  497.6 22.5 %shard_map.64 = f32[2048,3584]{1,0:T(8,128)} custom-call(bf16[2048,256]{1,0:T(8,128)(2,1)S(1)} %bitcast.140, bf16[2048,256]{1,0:T(8,128)(2,1)S(1)} %bitcast.139, bf16[2048,256]{1,0:T(8,128)(2,1)S(1)} %bitcast.142, bf16[2048,256]{1,0:T(8,128)(2,1)S(1)} %bitcast.141, bf16[256,3584]{1,0:T(8,128)(2,1)S(1)} %pad_maximum_fusion.3.refs_4_, ...), custom_call_target="tpu_custom_call" | custom-call | flops 15032385536 | bytes 40894464 | tf_op jit(solution)/shard_map/pallas_call | solution.py:88
  (323 shorter events, 137.6 us)
Async XLA Ops:
  6.5 75.8 %all-gather.9.cloned.1.call-start = ((), (), s32[]{:S(2)}) async-start(), calls=%async_computation | async-start | bytes 2621440 | tf_op jit(solution)/shard_map/all_gather | solution.py:129
  8.7 17.0 %collective-permute-start = (bf16[4,32,2048]{2,1,0:T(8,128)(2,1)S(1)}, bf16[4,32,2048]{2,1,0:T(8,128)(2,1)S(1)}, u32[]{:S(2)}, u32[]{:S(2)}) collective-permute-start(bf16[4,32,2048]{2,1,0:T(8,128)(2,1)S(1)} %pad_maximum_fusion.23), channel_id=1, source_target_pairs={{0,4},{4,8},{8,12},{12,0},{1,5},{5,9},{9,13},{13,1},{2,6},{6,10},{... | collective-permute-start | bytes 1572872 | tf_op jit(solution)/shard_map/ppermute | solution.py:41
  36.7 11.0 %collective-permute-start.2 = (f32[128,3584]{1,0:T(8,128)}, f32[128,3584]{1,0:T(8,128)S(1)}, u32[]{:S(2)}, u32[]{:S(2)}) collective-permute-start(f32[128,3584]{1,0:T(8,128)} %slice.322), channel_id=1, source_target_pairs={{0,1},{1,0},{2,3},{3,2},{4,5},{5,4},{6,7},{7,6},{8,9},{9,8},{10,11... | collective-permute-start | bytes 5505032 | tf_op jit(solution)/shard_map/ppermute | solution.py:36
  36.7 120.5 %all-gather.11.cloned.1.call-start = ((), (), s32[]{:S(2)}) async-start(), calls=%async_computation.1 | async-start | bytes 2621440 | tf_op jit(solution)/shard_map/all_gather | solution.py:253
  51.6 42.7 %collective-permute-start.3 = (f16[64,3712]{1,0:T(8,128)(2,1)S(1)}, f16[64,3712]{1,0:T(8,128)(2,1)S(1)}, u32[]{:S(2)}, u32[]{:S(2)}) collective-permute-start(f16[64,3712]{1,0:T(8,128)(2,1)S(1)} %concatenate.89), channel_id=1, source_target_pairs={{0,2},{1,3},{2,0},{3,1},{4,6},{5,7},{6,4},{7,5},{8,10},{9,11},{10,... | collective-permute-start | bytes 1425416 | tf_op jit(solution)/shard_map/ppermute | solution.py:36
  91.1 26.4 %collective-permute-start.4 = (f32[128,3584]{1,0:T(8,128)}, f32[128,3584]{1,0:T(8,128)}, u32[]{:S(2)}, u32[]{:S(2)}) collective-permute-start(f32[128,3584]{1,0:T(8,128)} %slice.325), channel_id=1, source_target_pairs={{0,1},{1,0},{2,3},{3,2},{4,5},{5,4},{6,7},{7,6},{8,9},{9,8},{10,11... | collective-permute-start | bytes 5505032 | tf_op jit(solution)/shard_map/ppermute | solution.py:36
  101.7 18.8 %collective-permute-start.8 = (f32[128,3584]{1,0:T(8,128)}, f32[128,3584]{1,0:T(8,128)S(1)}, u32[]{:S(2)}, u32[]{:S(2)}) collective-permute-start(f32[128,3584]{1,0:T(8,128)} %slice.333), channel_id=1, source_target_pairs={{0,1},{1,0},{2,3},{3,2},{4,5},{5,4},{6,7},{7,6},{8,9},{9,8},{10,11... | collective-permute-start | bytes 5505032 | tf_op jit(solution)/shard_map/ppermute | solution.py:36
  102.6 17.9 %collective-permute-start.5 = (f16[64,3584]{1,0:T(8,128)(2,1)}, f16[64,3584]{1,0:T(8,128)(2,1)}, u32[]{:S(2)}, u32[]{:S(2)}) collective-permute-start(f16[64,3584]{1,0:T(8,128)(2,1)} %fusion.53), channel_id=1, source_target_pairs={{0,2},{1,3},{2,0},{3,1},{4,6},{5,7},{6,4},{7,5},{8,10},{9,11},{10,... | collective-permute-start | bytes 1376264 | tf_op jit(solution)/shard_map/ppermute | solution.py:36
  105.3 118.8 %all-gather.15.cloned.1.call-start = ((), (), s32[]{:S(2)}) async-start(), calls=%async_computation.3 | async-start | bytes 2752512 | tf_op jit(solution)/shard_map/all_gather | solution.py:206
  119.9 17.3 %collective-permute-start.10 = (bf16[64,3584]{1,0:T(8,128)(2,1)}, bf16[64,3584]{1,0:T(8,128)(2,1)}, u32[]{:S(2)}, u32[]{:S(2)}) collective-permute-start(bf16[64,3584]{1,0:T(8,128)(2,1)} %fusion.51), channel_id=1, source_target_pairs={{0,2},{1,3},{2,0},{3,1},{4,6},{5,7},{6,4},{7,5},{8,10},{9,11},{10,... | collective-permute-start | bytes 1376264 | tf_op jit(solution)/shard_map/ppermute | solution.py:36
  127.0 27.5 %collective-permute-start.9 = (f16[64,3712]{1,0:T(8,128)(2,1)}, f16[64,3712]{1,0:T(8,128)(2,1)}, u32[]{:S(2)}, u32[]{:S(2)}) collective-permute-start(f16[64,3712]{1,0:T(8,128)(2,1)} %concatenate.91), channel_id=1, source_target_pairs={{0,2},{1,3},{2,0},{3,1},{4,6},{5,7},{6,4},{7,5},{8,10},{9,11},{10,... | collective-permute-start | bytes 1425416 | tf_op jit(solution)/shard_map/ppermute | solution.py:36
  137.3 21.5 %collective-permute-start.6 = (f32[128,3584]{1,0:T(8,128)}, f32[128,3584]{1,0:T(8,128)}, u32[]{:S(2)}, u32[]{:S(2)}) collective-permute-start(f32[128,3584]{1,0:T(8,128)} %slice.328), channel_id=1, source_target_pairs={{0,1},{1,0},{2,3},{3,2},{4,5},{5,4},{6,7},{7,6},{8,9},{9,8},{10,11... | collective-permute-start | bytes 5505032 | tf_op jit(solution)/shard_map/ppermute | solution.py:36
  143.4 12.2 %collective-permute-start.13 = (bf16[64,3584]{1,0:T(8,128)(2,1)S(1)}, bf16[64,3584]{1,0:T(8,128)(2,1)S(1)}, u32[]{:S(2)}, u32[]{:S(2)}) collective-permute-start(bf16[64,3584]{1,0:T(8,128)(2,1)S(1)} %get-tuple-element.79), channel_id=1, source_target_pairs={{0,2},{1,3},{2,0},{3,1},{4,6},{5,7},{6,4},{7,5},{8,10},{9,11},{10,... | collective-permute-start | bytes 1376264 | tf_op jit(solution)/shard_map/ppermute | solution.py:36
  154.5 18.1 %collective-permute-start.11 = (f32[128,3584]{1,0:T(8,128)}, f32[128,3584]{1,0:T(8,128)}, u32[]{:S(2)}, u32[]{:S(2)}) collective-permute-start(f32[128,3584]{1,0:T(8,128)} %slice.343), channel_id=1, source_target_pairs={{0,1},{1,0},{2,3},{3,2},{4,5},{5,4},{6,7},{7,6},{8,9},{9,8},{10,11... | collective-permute-start | bytes 5505032 | tf_op jit(solution)/shard_map/ppermute | solution.py:36
  154.5 80.2 %all-gather.13.cloned.1.call-start = ((), (), s32[]{:S(2)}) async-start(), calls=%async_computation.2 | async-start | bytes 2752512 | tf_op jit(solution)/shard_map/all_gather | solution.py:206
  160.5 21.4 %collective-permute-start.7 = (f16[64,3584]{1,0:T(8,128)(2,1)S(1)}, f16[64,3584]{1,0:T(8,128)(2,1)S(1)}, u32[]{:S(2)}, u32[]{:S(2)}) collective-permute-start(f16[64,3584]{1,0:T(8,128)(2,1)S(1)} %fusion.49), channel_id=1, source_target_pairs={{0,2},{1,3},{2,0},{3,1},{4,6},{5,7},{6,4},{7,5},{8,10},{9,11},{10,... | collective-permute-start | bytes 1376264 | tf_op jit(solution)/shard_map/ppermute | solution.py:36
  175.6 12.3 %collective-permute-start.12 = (bf16[64,3584]{1,0:T(8,128)(2,1)S(1)}, bf16[64,3584]{1,0:T(8,128)(2,1)S(1)}, u32[]{:S(2)}, u32[]{:S(2)}) collective-permute-start(bf16[64,3584]{1,0:T(8,128)(2,1)S(1)} %fusion.44), channel_id=1, source_target_pairs={{0,2},{1,3},{2,0},{3,1},{4,6},{5,7},{6,4},{7,5},{8,10},{9,11},{10,... | collective-permute-start | bytes 1376264 | tf_op jit(solution)/shard_map/ppermute | solution.py:36
  181.9 24.4 %collective-permute-start.24 = (f32[128,3584]{1,0:T(8,128)}, f32[128,3584]{1,0:T(8,128)}, u32[]{:S(2)}, u32[]{:S(2)}) collective-permute-start(f32[128,3584]{1,0:T(8,128)} %slice.359), channel_id=1, source_target_pairs={{0,1},{1,0},{2,3},{3,2},{4,5},{5,4},{6,7},{7,6},{8,9},{9,8},{10,11... | collective-permute-start | bytes 5505032 | tf_op jit(solution)/shard_map/ppermute | solution.py:36
  192.8 12.4 %collective-permute-start.15 = (bf16[64,3584]{1,0:T(8,128)(2,1)S(1)}, bf16[64,3584]{1,0:T(8,128)(2,1)}, u32[]{:S(2)}, u32[]{:S(2)}) collective-permute-start(bf16[64,3584]{1,0:T(8,128)(2,1)S(1)} %get-tuple-element.77), channel_id=1, source_target_pairs={{0,2},{1,3},{2,0},{3,1},{4,6},{5,7},{6,4},{7,5},{8,10},{9,11},{10,... | collective-permute-start | bytes 1376264 | tf_op jit(solution)/shard_map/ppermute | solution.py:36
  202.6 38.1 %collective-permute-start.18 = (bf16[4,32,2048]{2,1,0:T(8,128)(2,1)}, bf16[4,32,2048]{2,1,0:T(8,128)(2,1)}, u32[]{:S(2)}, u32[]{:S(2)}) collective-permute-start(bf16[4,32,2048]{2,1,0:T(8,128)(2,1)} %get-tuple-element.101), channel_id=1, source_target_pairs={{0,8},{4,12},{8,0},{12,4},{1,9},{5,13},{9,1},{13,5},{2,10},{6,14},... | collective-permute-start | bytes 1572872 | tf_op jit(solution)/shard_map/ppermute | solution.py:41
  203.8 36.8 %collective-permute-start.17 = (bf16[4,32,2048]{2,1,0:T(8,128)(2,1)}, bf16[4,32,2048]{2,1,0:T(8,128)(2,1)}, u32[]{:S(2)}, u32[]{:S(2)}) collective-permute-start(bf16[4,32,2048]{2,1,0:T(8,128)(2,1)} %get-tuple-element.100), channel_id=1, source_target_pairs={{0,12},{4,0},{8,4},{12,8},{1,13},{5,1},{9,5},{13,9},{2,14},{6,2},{... | collective-permute-start | bytes 1572872 | tf_op jit(solution)/shard_map/ppermute | solution.py:41
  208.6 15.5 %collective-permute-start.25 = (bf16[64,3584]{1,0:T(8,128)(2,1)}, bf16[64,3584]{1,0:T(8,128)(2,1)}, u32[]{:S(2)}, u32[]{:S(2)}) collective-permute-start(bf16[64,3584]{1,0:T(8,128)(2,1)} %fusion.32), channel_id=1, source_target_pairs={{0,2},{1,3},{2,0},{3,1},{4,6},{5,7},{6,4},{7,5},{8,10},{9,11},{10,... | collective-permute-start | bytes 1376264 | tf_op jit(solution)/shard_map/ppermute | solution.py:36
  212.4 19.7 %collective-permute-start.21 = (bf16[64,3584]{1,0:T(8,128)(2,1)}, bf16[64,3584]{1,0:T(8,128)(2,1)}, u32[]{:S(2)}, u32[]{:S(2)}) collective-permute-start(bf16[64,3584]{1,0:T(8,128)(2,1)} %fusion.36), channel_id=1, source_target_pairs={{0,2},{1,3},{2,0},{3,1},{4,6},{5,7},{6,4},{7,5},{8,10},{9,11},{10,... | collective-permute-start | bytes 1376264 | tf_op jit(solution)/shard_map/ppermute | solution.py:36
  222.8 17.9 %collective-permute-start.19 = (bf16[4,32,2048]{2,1,0:T(8,128)(2,1)}, bf16[4,32,2048]{2,1,0:T(8,128)(2,1)}, u32[]{:S(2)}, u32[]{:S(2)}) collective-permute-start(bf16[4,32,2048]{2,1,0:T(8,128)(2,1)} %fusion.54), channel_id=1, source_target_pairs={{0,4},{4,8},{8,12},{12,0},{1,5},{5,9},{9,13},{13,1},{2,6},{6,10},{... | collective-permute-start | bytes 1572872 | tf_op jit(solution)/shard_map/ppermute | solution.py:41
  226.2 29.2 %collective-permute-start.26 = (bf16[64,3584]{1,0:T(8,128)(2,1)S(1)}, bf16[64,3584]{1,0:T(8,128)(2,1)S(1)}, u32[]{:S(2)}, u32[]{:S(2)}) collective-permute-start(bf16[64,3584]{1,0:T(8,128)(2,1)S(1)} %fusion.35), channel_id=1, source_target_pairs={{0,2},{1,3},{2,0},{3,1},{4,6},{5,7},{6,4},{7,5},{8,10},{9,11},{10,... | collective-permute-start | bytes 1376264 | tf_op jit(solution)/shard_map/ppermute | solution.py:36
  236.8 19.6 %collective-permute-start.22 = (bf16[64,3584]{1,0:T(8,128)(2,1)S(1)}, bf16[64,3584]{1,0:T(8,128)(2,1)S(1)}, u32[]{:S(2)}, u32[]{:S(2)}) collective-permute-start(bf16[64,3584]{1,0:T(8,128)(2,1)S(1)} %fusion.39), channel_id=1, source_target_pairs={{0,2},{1,3},{2,0},{3,1},{4,6},{5,7},{6,4},{7,5},{8,10},{9,11},{10,... | collective-permute-start | bytes 1376264 | tf_op jit(solution)/shard_map/ppermute | solution.py:36
  242.7 24.1 %collective-permute-start.28 = (bf16[4,32,2048]{2,1,0:T(8,128)(2,1)S(1)}, bf16[4,32,2048]{2,1,0:T(8,128)(2,1)S(1)}, u32[]{:S(2)}, u32[]{:S(2)}) collective-permute-start(bf16[4,32,2048]{2,1,0:T(8,128)(2,1)S(1)} %fusion.15), channel_id=1, source_target_pairs={{0,12},{4,0},{8,4},{12,8},{1,13},{5,1},{9,5},{13,9},{2,14},{6,2},{... | collective-permute-start | bytes 1572872 | tf_op jit(solution)/shard_map/ppermute | solution.py:41
  256.4 24.9 %collective-permute-start.27 = (bf16[128,3584]{1,0:T(8,128)(2,1)}, bf16[128,3584]{1,0:T(8,128)(2,1)}, u32[]{:S(2)}, u32[]{:S(2)}) collective-permute-start(bf16[128,3584]{1,0:T(8,128)(2,1)} %pad_maximum_fusion.18), channel_id=1, source_target_pairs={{0,1},{1,0},{2,3},{3,2},{4,5},{5,4},{6,7},{7,6},{8,9},{9,8},{10,11... | collective-permute-start | bytes 2752520 | tf_op jit(solution)/shard_map/ppermute | solution.py:36
  257.4 33.9 %collective-permute-start.23 = (bf16[128,3584]{1,0:T(8,128)(2,1)}, bf16[128,3584]{1,0:T(8,128)(2,1)}, u32[]{:S(2)}, u32[]{:S(2)}) collective-permute-start(bf16[128,3584]{1,0:T(8,128)(2,1)} %pad_maximum_fusion.17), channel_id=1, source_target_pairs={{0,1},{1,0},{2,3},{3,2},{4,5},{5,4},{6,7},{7,6},{8,9},{9,8},{10,11... | collective-permute-start | bytes 2752520 | tf_op jit(solution)/shard_map/ppermute | solution.py:36
  266.8 37.6 %collective-permute-start.31 = (bf16[4,32,2048]{2,1,0:T(8,128)(2,1)S(1)}, bf16[4,32,2048]{2,1,0:T(8,128)(2,1)}, u32[]{:S(2)}, u32[]{:S(2)}) collective-permute-start(bf16[4,32,2048]{2,1,0:T(8,128)(2,1)S(1)} %fusion.15), channel_id=1, source_target_pairs={{0,4},{4,8},{8,12},{12,0},{1,5},{5,9},{9,13},{13,1},{2,6},{6,10},{... | collective-permute-start | bytes 1572872 | tf_op jit(solution)/shard_map/ppermute | solution.py:41
  276.8 15.8 %collective-permute-start.29 = (f32[128,3584]{1,0:T(8,128)S(1)}, f32[128,3584]{1,0:T(8,128)S(1)}, u32[]{:S(2)}, u32[]{:S(2)}) collective-permute-start(f32[128,3584]{1,0:T(8,128)S(1)} %slice.372), channel_id=1, source_target_pairs={{0,1},{1,0},{2,3},{3,2},{4,5},{5,4},{6,7},{7,6},{8,9},{9,8},{10,11... | collective-permute-start | bytes 5505032 | tf_op jit(solution)/shard_map/ppermute | solution.py:36
  278.1 21.0 %collective-permute-start.33 = (bf16[4,32,2048]{2,1,0:T(8,128)(2,1)S(1)}, bf16[4,32,2048]{2,1,0:T(8,128)(2,1)S(1)}, u32[]{:S(2)}, u32[]{:S(2)}) collective-permute-start(bf16[4,32,2048]{2,1,0:T(8,128)(2,1)S(1)} %copy-done.52), channel_id=1, source_target_pairs={{0,12},{4,0},{8,4},{12,8},{1,13},{5,1},{9,5},{13,9},{2,14},{6,2},{... | collective-permute-start | bytes 1572872 | tf_op jit(solution)/shard_map/ppermute | solution.py:41
  292.8 11.5 %collective-permute-start.32 = (bf16[64,3584]{1,0:T(8,128)(2,1)S(1)}, bf16[64,3584]{1,0:T(8,128)(2,1)S(1)}, u32[]{:S(2)}, u32[]{:S(2)}) collective-permute-start(bf16[64,3584]{1,0:T(8,128)(2,1)S(1)} %fusion.31), channel_id=1, source_target_pairs={{0,2},{1,3},{2,0},{3,1},{4,6},{5,7},{6,4},{7,5},{8,10},{9,11},{10,... | collective-permute-start | bytes 1376264 | tf_op jit(solution)/shard_map/ppermute | solution.py:36
  314.4 37.4 %collective-permute-start.36 = (bf16[4,32,2048]{2,1,0:T(8,128)(2,1)}, bf16[4,32,2048]{2,1,0:T(8,128)(2,1)S(1)}, u32[]{:S(2)}, u32[]{:S(2)}) collective-permute-start(bf16[4,32,2048]{2,1,0:T(8,128)(2,1)} %get-tuple-element.99), channel_id=1, source_target_pairs={{0,8},{4,12},{8,0},{12,4},{1,9},{5,13},{9,1},{13,5},{2,10},{6,14},... | collective-permute-start | bytes 1572872 | tf_op jit(solution)/shard_map/ppermute | solution.py:41
  316.1 36.6 %collective-permute-start.30 = (bf16[4,32,2048]{2,1,0:T(8,128)(2,1)}, bf16[4,32,2048]{2,1,0:T(8,128)(2,1)S(1)}, u32[]{:S(2)}, u32[]{:S(2)}) collective-permute-start(bf16[4,32,2048]{2,1,0:T(8,128)(2,1)} %get-tuple-element.98), channel_id=1, source_target_pairs={{0,12},{4,0},{8,4},{12,8},{1,13},{5,1},{9,5},{13,9},{2,14},{6,2},{... | collective-permute-start | bytes 1572872 | tf_op jit(solution)/shard_map/ppermute | solution.py:41
  316.5 35.3 %collective-permute-start.37 = (bf16[4,32,2048]{2,1,0:T(8,128)(2,1)S(1)}, bf16[4,32,2048]{2,1,0:T(8,128)(2,1)S(1)}, u32[]{:S(2)}, u32[]{:S(2)}) collective-permute-start(bf16[4,32,2048]{2,1,0:T(8,128)(2,1)S(1)} %copy-done.49), channel_id=1, source_target_pairs={{0,4},{4,8},{8,12},{12,0},{1,5},{5,9},{9,13},{13,1},{2,6},{6,10},{... | collective-permute-start | bytes 1572872 | tf_op jit(solution)/shard_map/ppermute | solution.py:41
  319.8 32.1 %collective-permute-start.35 = (bf16[64,3584]{1,0:T(8,128)(2,1)S(1)}, bf16[64,3584]{1,0:T(8,128)(2,1)S(1)}, u32[]{:S(2)}, u32[]{:S(2)}) collective-permute-start(bf16[64,3584]{1,0:T(8,128)(2,1)S(1)} %fusion.29), channel_id=1, source_target_pairs={{0,2},{1,3},{2,0},{3,1},{4,6},{5,7},{6,4},{7,5},{8,10},{9,11},{10,... | collective-permute-start | bytes 1376264 | tf_op jit(solution)/shard_map/ppermute | solution.py:36
  353.1 33.9 %collective-permute-start.42 = (bf16[4,32,2048]{2,1,0:T(8,128)(2,1)S(1)}, bf16[4,32,2048]{2,1,0:T(8,128)(2,1)S(1)}, u32[]{:S(2)}, u32[]{:S(2)}) collective-permute-start(bf16[4,32,2048]{2,1,0:T(8,128)(2,1)S(1)} %fusion.10), channel_id=1, source_target_pairs={{0,12},{4,0},{8,4},{12,8},{1,13},{5,1},{9,5},{13,9},{2,14},{6,2},{... | collective-permute-start | bytes 1572872 | tf_op jit(solution)/shard_map/ppermute | solution.py:41
  355.7 11.0 %collective-permute-start.39 = (bf16[64,3584]{1,0:T(8,128)(2,1)S(1)}, bf16[64,3584]{1,0:T(8,128)(2,1)}, u32[]{:S(2)}, u32[]{:S(2)}) collective-permute-start(bf16[64,3584]{1,0:T(8,128)(2,1)S(1)} %fusion.30), channel_id=1, source_target_pairs={{0,2},{1,3},{2,0},{3,1},{4,6},{5,7},{6,4},{7,5},{8,10},{9,11},{10,... | collective-permute-start | bytes 1376264 | tf_op jit(solution)/shard_map/ppermute | solution.py:36
  403.0 41.7 %collective-permute-start.38 = (bf16[128,3584]{1,0:T(8,128)(2,1)}, bf16[128,3584]{1,0:T(8,128)(2,1)}, u32[]{:S(2)}, u32[]{:S(2)}) collective-permute-start(bf16[128,3584]{1,0:T(8,128)(2,1)} %pad_maximum_fusion.19), channel_id=1, source_target_pairs={{0,1},{1,0},{2,3},{3,2},{4,5},{5,4},{6,7},{7,6},{8,9},{9,8},{10,11... | collective-permute-start | bytes 2752520 | tf_op jit(solution)/shard_map/ppermute | solution.py:36
  404.8 12.6 %collective-permute-start.40 = (bf16[64,3584]{1,0:T(8,128)(2,1)S(1)}, bf16[64,3584]{1,0:T(8,128)(2,1)S(1)}, u32[]{:S(2)}, u32[]{:S(2)}) collective-permute-start(bf16[64,3584]{1,0:T(8,128)(2,1)S(1)} %fusion.26), channel_id=1, source_target_pairs={{0,2},{1,3},{2,0},{3,1},{4,6},{5,7},{6,4},{7,5},{8,10},{9,11},{10,... | collective-permute-start | bytes 1376264 | tf_op jit(solution)/shard_map/ppermute | solution.py:36
  406.2 26.7 %collective-permute-start.47 = (bf16[4,32,2048]{2,1,0:T(8,128)(2,1)S(1)}, bf16[4,32,2048]{2,1,0:T(8,128)(2,1)S(1)}, u32[]{:S(2)}, u32[]{:S(2)}) collective-permute-start(bf16[4,32,2048]{2,1,0:T(8,128)(2,1)S(1)} %fusion.10), channel_id=1, source_target_pairs={{0,4},{4,8},{8,12},{12,0},{1,5},{5,9},{9,13},{13,1},{2,6},{6,10},{... | collective-permute-start | bytes 1572872 | tf_op jit(solution)/shard_map/ppermute | solution.py:41
  408.7 24.2 %collective-permute-start.48 = (bf16[4,32,2048]{2,1,0:T(8,128)(2,1)S(1)}, bf16[4,32,2048]{2,1,0:T(8,128)(2,1)S(1)}, u32[]{:S(2)}, u32[]{:S(2)}) collective-permute-start(bf16[4,32,2048]{2,1,0:T(8,128)(2,1)S(1)} %copy-done.54), channel_id=1, source_target_pairs={{0,12},{4,0},{8,4},{12,8},{1,13},{5,1},{9,5},{13,9},{2,14},{6,2},{... | collective-permute-start | bytes 1572872 | tf_op jit(solution)/shard_map/ppermute | solution.py:41
  452.1 42.9 %collective-permute-start.41 = (bf16[128,3584]{1,0:T(8,128)(2,1)S(1)}, bf16[128,3584]{1,0:T(8,128)(2,1)S(1)}, u32[]{:S(2)}, u32[]{:S(2)}) collective-permute-start(bf16[128,3584]{1,0:T(8,128)(2,1)S(1)} %pad_maximum_fusion.20), channel_id=1, source_target_pairs={{0,1},{1,0},{2,3},{3,2},{4,5},{5,4},{6,7},{7,6},{8,9},{9,8},{10,11... | collective-permute-start | bytes 2752520 | tf_op jit(solution)/shard_map/ppermute | solution.py:36
  452.6 13.6 %collective-permute-start.44 = (bf16[64,3584]{1,0:T(8,128)(2,1)}, bf16[64,3584]{1,0:T(8,128)(2,1)S(1)}, u32[]{:S(2)}, u32[]{:S(2)}) collective-permute-start(bf16[64,3584]{1,0:T(8,128)(2,1)} %fusion.20), channel_id=1, source_target_pairs={{0,2},{1,3},{2,0},{3,1},{4,6},{5,7},{6,4},{7,5},{8,10},{9,11},{10,... | collective-permute-start | bytes 1376264 | tf_op jit(solution)/shard_map/ppermute | solution.py:36
  454.8 21.2 %collective-permute-start.50 = (bf16[64,3584]{1,0:T(8,128)(2,1)S(1)}, bf16[64,3584]{1,0:T(8,128)(2,1)S(1)}, u32[]{:S(2)}, u32[]{:S(2)}) collective-permute-start(bf16[64,3584]{1,0:T(8,128)(2,1)S(1)} %fusion.16), channel_id=1, source_target_pairs={{0,2},{1,3},{2,0},{3,1},{4,6},{5,7},{6,4},{7,5},{8,10},{9,11},{10,... | collective-permute-start | bytes 1376264 | tf_op jit(solution)/shard_map/ppermute | solution.py:36
  467.6 18.3 %collective-permute-start.45 = (bf16[64,3584]{1,0:T(8,128)(2,1)S(1)}, bf16[64,3584]{1,0:T(8,128)(2,1)S(1)}, u32[]{:S(2)}, u32[]{:S(2)}) collective-permute-start(bf16[64,3584]{1,0:T(8,128)(2,1)S(1)} %fusion.23), channel_id=1, source_target_pairs={{0,2},{1,3},{2,0},{3,1},{4,6},{5,7},{6,4},{7,5},{8,10},{9,11},{10,... | collective-permute-start | bytes 1376264 | tf_op jit(solution)/shard_map/ppermute | solution.py:36
  477.7 17.2 %collective-permute-start.51 = (bf16[64,3584]{1,0:T(8,128)(2,1)S(1)}, bf16[64,3584]{1,0:T(8,128)(2,1)S(1)}, u32[]{:S(2)}, u32[]{:S(2)}) collective-permute-start(bf16[64,3584]{1,0:T(8,128)(2,1)S(1)} %fusion.19), channel_id=1, source_target_pairs={{0,2},{1,3},{2,0},{3,1},{4,6},{5,7},{6,4},{7,5},{8,10},{9,11},{10,... | collective-permute-start | bytes 1376264 | tf_op jit(solution)/shard_map/ppermute | solution.py:36
  (80 other events, 812.2 us)
Sparse Core Ops, SparseCore 0:
  36.8 45.4 all-gather.8
  105.4 43.8 all-gather.10
  154.6 29.0 all-gather.14
  205.3 29.3 all-gather.12

commit v8 on v7

--- a/solution.py
+++ b/solution.py
@@ -125,15 +125,16 @@
 
     halves = (grp, 1 - grp)
     own = [own_rows(inputs, 0, half) for half in halves]
-    near = shift(own[0], "row")
-    spread = [lax.all_gather(own[0], "row")]
-
-    def piece_of(half, k):
-        if k == 0:
-            return own[half]
-        if k == 1 and half == 0:
-            return near
-        return lax.dynamic_index_in_dim(spread[half], (me + ring - k) % ring, 0, keepdims=False)
+    fetched = {(0, 0): own[0], (1, 0): own[1]}
+    for k in range(1, ring):
+        needed = [fetched[0, i] for i in range(1, per_group)] if k >= per_group else []
+        fetched[0, k] = shift(tie(own[0], needed), "row", k)
+
+    def fetch_other(step, after):
+        for k in step:
+            if k:
+                fetched[1, k] = swap(tie(fetched[0, k], after), "grp", 1)
+        return [fetched[1, k] for k in step if k]
 
     gate_scale = 2.0 ** math.floor(math.log2(65504.0 / (0.375 * width * count)))
 
@@ -187,7 +188,7 @@
         if (half, j) in xs:
             x = tie(xs[half, j], after)
         else:
-            xs[half, j] = x = joined([tie(piece_of(half, k), after) for k in steps[j]])
+            xs[half, j] = x = joined([tie(fetched[half, k], after) for k in steps[j]])
         weight = {"gate": w_gate, "up": w_up, "tangent": query}[form]
         sums[half, j, form], *mark = sum_over_col(matmul(x, weight), form)
         marks.append(mark)
@@ -242,37 +243,37 @@
         return first, sent, got, [near]
 
     tail = GROUPS - 1
-    early = []
+    early, others = [], []
     for j in range(GROUPS):
         first = project(0, j, "up", [])
         if j:
             early.append(hidden_rows(0, j - 1, first))
-        project(0, j, "gate", [])
-        first = project(0, j, "tangent", [] if j else spread[:])
-        if j == 0:
-            spread.append(lax.all_gather(tie(own[1], spread + first), "row"))
-        else:
+        project(0, j, "gate", others[-1] if j == tail else [])
+        first = project(0, j, "tangent", [])
+        others.append(fetch_other(steps[j], first))
+        if j:
             share_gain(j - 1, first)
     ready = [out_sums(0, j, early[j][0], marks[-2][1]) for j in range(tail)]
     first = project(1, 0, "tangent", ready)
     hidden, _ = hidden_rows(0, tail, first)
     for j in range(1, GROUPS):
-        first = project(1, j, "tangent", [])
+        first = project(1, j, "tangent", others[j])
     share_gain(tail, first)
     ready = [out_sums(0, tail, hidden, [])]
     pieces = scaled_pieces(0, [])
 
     hidden = [hidden_rows(1, j, []) for j in range(GROUPS)]
-    first, sent, got, near = back(0, tail, pieces, [])
-    ready = [out_sums(1, j, hidden[j][0], first) for j in range(tail)]
-    ready = [out_sums(1, tail, hidden[tail][0], ready + sent)]
+    ready = [out_sums(1, j, hidden[j][0], []) for j in range(tail)]
+    first, sent, got, near = back(0, tail, pieces, ready)
+    ready = [out_sums(1, tail, hidden[tail][0], sent + [moved[1, 0]])]
     for j in reversed(range(tail)):
-        _, sent, nextgot, nextnear = back(0, j, pieces, ready + got)
+        come = [moved[1, k] for k in range(1, per_group)]
+        _, sent, nextgot, _ = back(0, j, pieces, ready + got + come)
     pieces = scaled_pieces(1, sent + near)
     after = nextgot
     for j in reversed(range(GROUPS)):
-        _, sent, _, near = back(1, j, pieces, after)
-        after, nextnear = sent + nextnear, near
+        _, sent, got, near = back(1, j, pieces, after)
+        after = got + near
     return last_product(turned, bars, tokens)
 
 

time: 533 us -> 486 us (0.912)
  other arithmetic: 67.9 us -> 45.5 us
  starting transfers between devices: 72.3 us -> 61.1 us
  waiting for transfers between devices: 187 us -> 178 us
  local copies, waits for them, and re-layouts: 53.1 us -> 46.2 us
    ppermute x40 -> x43, waiting for transfers between devices: 65.3 us -> 98.4 us  [swap(): return lax.ppermute(values, axis, [(i, i ^ mask) for i in range(count)])]
    all_gather x2 -> x0, waiting for transfers between devices: 26.8 us -> none  [the longest x1 26.8 us: per_device(): spread = [lax.all_gather(own[0], 'row')]]
    ppermute x13 -> x15, waiting for transfers between devices: 92.3 us -> 79.9 us  [shift(): lax.ppermute(values, axis, [(i, (i + by) % count) for i in range(count)])]
    all_gather x2, starting transfers between devices: 12.3 us -> 0.04 us  [share_gain(): both = lax.all_gather(tie(gains[0][j], after), 'grp')]
    dot_general x12, matrix products: 75.6 us -> 83.9 us  [matmul(): return jnp.dot(left, right, preferred_element_type=jnp.float32)]
    concatenate x15 -> x14, other arithmetic: 12.5 us -> 5.61 us  [gather_over_col(): values = jnp.concatenate([values, got], axis=0)]
    convert_element_type x8, other arithmetic: 12.9 us -> 6.98 us  [pack(): return coded(values) if form == 'up' else values.astype(jnp.bfloat16)]
    unnamed x142 -> x124, local copies, waits for them, and re-layouts: 19.1 us -> 14 us
  transfers between devices with their start and end apart: 57 -> 60, of which waited for: 19 -> 25; matrix products, arithmetic and copies ran while one was open for 33% -> 34% of each run, Pallas kernels for 0% -> 0%
where the time goes in v8:
time: 486 us; the launch traced here: 481 us
  waiting for transfers between devices  178 us (37%)
  matrix products  113 us (23%)
  starting transfers between devices  61.1 us (13%)
  local copies, waits for them, and re-layouts  46.2 us (10%)
  other arithmetic  45.5 us (9%)
  Pallas kernels  22.5 us (5%)
  between operations  14.8 us (3%)
    ppermute x43, waiting for transfers between devices, swap(): return lax.ppermute(values, axis, [(i, i ^ mask) for i in range(count)])  98.4 us
    dot_general x12, matrix products, matmul(): return jnp.dot(left, right, preferred_element_type=jnp.float32)  83.9 us
    ppermute x15, waiting for transfers between devices, shift(): lax.ppermute(values, axis, [(i, (i + by) % count) for i in range(count)])  79.9 us
    ppermute x15, starting transfers between devices, shift(): lax.ppermute(values, axis, [(i, (i + by) % count) for i in range(count)])  32.5 us
    dot_general x4, matrix products, times_down(): lax.dot_general(left, w_down, (((1,), (1,)), ((), ())), preferred_element...  29.3 us
    ppermute x43, starting transfers between devices, swap(): return lax.ppermute(values, axis, [(i, i ^ mask) for i in range(count)])  28.5 us
    pallas_call x1, Pallas kernels, last_product(): pl.pallas_call(functools.partial(last_kernel, 1.0 / tokens, len(turned)),...  22.5 us
    unnamed x124, local copies, waits for them, and re-layouts  14 us
  transfers between devices with their start and end apart: 60, of which 25 were waited for; matrix products, arithmetic and copies ran while one was open for 34% of the time, Pallas kernels for 0%

profile of v8, /device:TPU:0, one launch (start us, length us, event | category | flops | bytes accessed | tf_op | source)
XLA Modules:
  0.0 481.5 jit_solution(10346343083735384521)
XLA Ops:
  8.0 3.1 collective-permute-start
  11.1 13.9 %collective-permute-done = bf16[4,32,2048]{2,1,0:T(8,128)(2,1)S(1)} collective-permute-done((bf16[4,32,2048]{2,1,0:T(8,128)(2,1)S(1)}, bf16[4,32,2048]{2,1,0:T(8,128)(2,1)S(1)}, u32[]{:S(2)}, u32[]{:S(2)}) %collective-permute-start) | collective-permute-done | bytes 524320 | tf_op jit(solution)/shard_map/ppermute | solution.py:41
  25.9 7.2 %fusion.84 = f32[256,3584]{1,0:T(8,128)S(1)} fusion(bf16[256,2048]{1,0:T(8,128)(2,1)S(1)} %bitcast.130, bf16[2048,3584]{1,0:T(8,128)(2,1)} %param.8), kind=kOutput, calls=%fused_computation.190 | convolution fusion | flops 3758096384 | bytes 19398656 | tf_op jit(solution)/shard_map/dot_general | solution.py:19
  36.4 2.8 dynamic-slice_bitcast_fusion.3
  41.2 7.2 %fusion.83 = f32[256,3584]{1,0:T(8,128)S(1)} fusion(bf16[256,2048]{1,0:T(8,128)(2,1)S(1)} %bitcast.131, bf16[2048,3584]{1,0:T(8,128)(2,1)} %param.7), kind=kOutput, calls=%fused_computation.189 | convolution fusion | flops 3758096384 | bytes 19398656 | tf_op jit(solution)/shard_map/dot_general | solution.py:19
  50.2 2.3 copy-done.5
  60.6 7.3 %fusion.85 = f32[256,3584]{1,0:T(8,128)S(1)} fusion(bf16[256,2048]{1,0:T(8,128)(2,1)S(1)} %bitcast.132, bf16[2048,3584]{1,0:T(8,128)(2,1)} %param.10), kind=kOutput, calls=%fused_computation.191 | convolution fusion | flops 3758096384 | bytes 19398656 | tf_op jit(solution)/shard_map/dot_general | solution.py:19
  72.1 3.4 collective-permute-done.1
  76.8 7.3 %fusion.87 = f32[256,3584]{1,0:T(8,128)S(1)} fusion(bf16[256,2048]{1,0:T(8,128)(2,1)S(1)} %bitcast.134, bf16[2048,3584]{1,0:T(8,128)(2,1)} %param.8), kind=kOutput, calls=%fused_computation.193 | convolution fusion | flops 3758096384 | bytes 19398656 | tf_op jit(solution)/shard_map/dot_general | solution.py:19
  86.2 7.2 %fusion.86 = f32[256,3584]{1,0:T(8,128)S(1)} fusion(bf16[256,2048]{1,0:T(8,128)(2,1)S(1)} %bitcast.135, bf16[2048,3584]{1,0:T(8,128)(2,1)} %param.7), kind=kOutput, calls=%fused_computation.192 | convolution fusion | flops 3758096384 | bytes 19398656 | tf_op jit(solution)/shard_map/dot_general | solution.py:19
  95.1 2.5 collective-permute-done.13
  97.8 3.5 multiply_convert_fusion.1
  108.7 7.5 %fusion.88 = f32[256,3584]{1,0:T(8,128)S(1)} fusion(bf16[256,2048]{1,0:T(8,128)(2,1)S(1)} %bitcast.136, bf16[2048,3584]{1,0:T(8,128)(2,1)} %param.10), kind=kOutput, calls=%fused_computation.194 | convolution fusion | flops 3758096384 | bytes 19398656 | tf_op jit(solution)/shard_map/dot_general | solution.py:19
  128.1 8.1 %convolution_convert_fusion.1 = bf16[256,2048]{1,0:T(8,128)(2,1)S(1)} fusion(bf16[256,3584]{1,0:T(8,128)(2,1)S(1)} %pad_maximum_fusion, bf16[3584,2048]{1,0:T(8,128)(2,1)} %param.9), kind=kOutput, calls=%fused_computation.1 | convolution fusion | flops 3758620672 | bytes 17563648 | tf_op jit(solution)/shard_map/dot_general | solution.py:19
  138.4 3.9 fusion.89
  143.8 4.1 collective-permute-start.20
  149.3 10.6 %collective-permute-done.24 = bf16[4,32,2048]{2,1,0:T(8,128)(2,1)S(1)} collective-permute-done((bf16[4,32,2048]{2,1,0:T(8,128)(2,1)}, bf16[4,32,2048]{2,1,0:T(8,128)(2,1)S(1)}, u32[]{:S(2)}, u32[]{:S(2)}) %collective-permute-start.24) | collective-permute-done | bytes 524320 | tf_op jit(solution)/shard_map/ppermute | solution.py:36
  161.4 3.9 fusion.90
  166.9 4.5 collective-permute-done.15
  172.7 3.6 multiply_convert_fusion
  177.6 2.3 fusion.37
  180.7 9.1 %collective-permute-done.18 = bf16[64,3584]{1,0:T(8,128)(2,1)S(1)} collective-permute-done((bf16[64,3584]{1,0:T(8,128)(2,1)S(1)}, bf16[64,3584]{1,0:T(8,128)(2,1)S(1)}, u32[]{:S(2)}, u32[]{:S(2)}) %collective-permute-start.18) | collective-permute-done | bytes 458784 | tf_op jit(solution)/shard_map/ppermute | solution.py:36
  190.7 5.9 %collective-permute-done.31 = bf16[64,3584]{1,0:T(8,128)(2,1)S(1)} collective-permute-done((bf16[64,3584]{1,0:T(8,128)(2,1)}, bf16[64,3584]{1,0:T(8,128)(2,1)S(1)}, u32[]{:S(2)}, u32[]{:S(2)}) %collective-permute-start.31) | collective-permute-done | bytes 458784 | tf_op jit(solution)/shard_map/ppermute | solution.py:36
  203.2 7.5 %fusion = f32[256,2048]{1,0:T(8,128)S(1)} fusion(bf16[3584,2048]{1,0:T(8,128)(2,1)} %param.9, bf16[128,3584]{1,0:T(8,128)(2,1)} %collective-permute-done.19, bf16[64,3584]{1,0:T(8,128)(2,1)S(1)} %collective-permute-done.18, bf16[64,3584]{1,0:T(8,128)(2,1)S(1)} %get-tuple-element.85), kind=kOutput, calls=%fused_computation.3 | convolution fusion | flops 3763601408 | bytes 18612224 | tf_op jit(solution)/shard_map/dot_general | solution.py:19
  214.1 5.1 %collective-permute-done.26 = bf16[64,3584]{1,0:T(8,128)(2,1)} collective-permute-done((bf16[64,3584]{1,0:T(8,128)(2,1)S(1)}, bf16[64,3584]{1,0:T(8,128)(2,1)}, u32[]{:S(2)}, u32[]{:S(2)}) %collective-permute-start.26) | collective-permute-done | bytes 458784 | tf_op jit(solution)/shard_map/ppermute | solution.py:36
  226.6 2.4 collective-permute-start.29
  229.0 9.4 %convolution_convert_fusion = bf16[256,2048]{1,0:T(8,128)(2,1)S(1)} fusion(bf16[3584,2048]{1,0:T(8,128)(2,1)} %param.9, bf16[128,3584]{1,0:T(8,128)(2,1)} %collective-permute-done.33, bf16[64,3584]{1,0:T(8,128)(2,1)S(1)} %copy-done.56, bf16[64,3584]{1,0:T(8,128)(2,1)S(1)} %fusion.40), kind=kOutput, calls=%fused_computation | convolution fusion | flops 3764125696 | bytes 17563648 | tf_op jit(solution)/shard_map/dot_general | solution.py:19
  240.2 7.3 %fusion.91 = f32[256,3584]{1,0:T(8,128)S(1)} fusion(bf16[256,2048]{1,0:T(8,128)(2,1)S(1)} %bitcast.154, bf16[3584,2048]{1,0:T(8,128)(2,1)} %param.9), kind=kOutput, calls=%fused_computation.197 | convolution fusion | flops 3758096384 | bytes 19398656 | tf_op jit(solution)/shard_map/dot_general | solution.py:23
  249.0 3.3 collective-permute-start.39
  256.4 39.1 %collective-permute-done.35 = bf16[4,32,2048]{2,1,0:T(8,128)(2,1)} collective-permute-done((bf16[4,32,2048]{2,1,0:T(8,128)(2,1)S(1)}, bf16[4,32,2048]{2,1,0:T(8,128)(2,1)}, u32[]{:S(2)}, u32[]{:S(2)}) %collective-permute-start.35) | collective-permute-done | bytes 524320 | tf_op jit(solution)/shard_map/ppermute | solution.py:41
  295.5 7.2 %fusion.92 = f32[256,2048]{1,0:T(8,128)S(1)} fusion(bf16[256,3584]{1,0:T(8,128)(2,1)S(1)} %pad_maximum_fusion.1, bf16[3584,2048]{1,0:T(8,128)(2,1)} %param.9), kind=kOutput, calls=%fused_computation.198 | convolution fusion | flops 3758096384 | bytes 18612224 | tf_op jit(solution)/shard_map/dot_general | solution.py:19
  304.3 7.3 %fusion.93 = f32[256,3584]{1,0:T(8,128)S(1)} fusion(bf16[256,2048]{1,0:T(8,128)(2,1)S(1)} %bitcast.152, bf16[3584,2048]{1,0:T(8,128)(2,1)} %param.9), kind=kOutput, calls=%fused_computation.199 | convolution fusion | flops 3758096384 | bytes 19398656 | tf_op jit(solution)/shard_map/dot_general | solution.py:23
  311.9 12.4 %collective-permute-start.42 = (bf16[4,32,2048]{2,1,0:T(8,128)(2,1)S(1)}, bf16[4,32,2048]{2,1,0:T(8,128)(2,1)S(1)}, u32[]{:S(2)}, u32[]{:S(2)}) collective-permute-start(bf16[4,32,2048]{2,1,0:T(8,128)(2,1)S(1)} %fusion.60), channel_id=1, source_target_pairs={{0,4},{4,8},{8,12},{12,0},{1,5},{5,9},{9,13},{13,1},{2,6},{6,10},{... | collective-permute-start | bytes 1572872 | tf_op jit(solution)/shard_map/ppermute | solution.py:41
  327.1 9.0 %collective-permute-done.42 = bf16[4,32,2048]{2,1,0:T(8,128)(2,1)S(1)} collective-permute-done((bf16[4,32,2048]{2,1,0:T(8,128)(2,1)S(1)}, bf16[4,32,2048]{2,1,0:T(8,128)(2,1)S(1)}, u32[]{:S(2)}, u32[]{:S(2)}) %collective-permute-start.42) | collective-permute-done | bytes 524320 | tf_op jit(solution)/shard_map/ppermute | solution.py:41
  336.1 2.3 collective-permute-done.41
  341.5 10.6 %collective-permute-done.44 = bf16[64,3584]{1,0:T(8,128)(2,1)S(1)} collective-permute-done((bf16[64,3584]{1,0:T(8,128)(2,1)S(1)}, bf16[64,3584]{1,0:T(8,128)(2,1)S(1)}, u32[]{:S(2)}, u32[]{:S(2)}) %collective-permute-start.44) | collective-permute-done | bytes 458784 | tf_op jit(solution)/shard_map/ppermute | solution.py:36
  354.2 7.3 %fusion.94 = f32[256,3584]{1,0:T(8,128)S(1)} fusion(bf16[256,2048]{1,0:T(8,128)(2,1)S(1)} %bitcast.155, bf16[3584,2048]{1,0:T(8,128)(2,1)} %param.9), kind=kOutput, calls=%fused_computation.200 | convolution fusion | flops 3758096384 | bytes 19398656 | tf_op jit(solution)/shard_map/dot_general | solution.py:23
  361.7 3.8 collective-permute-done.48
  367.4 3.3 collective-permute-start.53
  370.7 7.6 %collective-permute-done.49 = bf16[64,3584]{1,0:T(8,128)(2,1)S(1)} collective-permute-done((bf16[64,3584]{1,0:T(8,128)(2,1)S(1)}, bf16[64,3584]{1,0:T(8,128)(2,1)S(1)}, u32[]{:S(2)}, u32[]{:S(2)}) %collective-permute-start.49) | collective-permute-done | bytes 458784 | tf_op jit(solution)/shard_map/ppermute | solution.py:36
  380.8 11.3 %collective-permute-done.53 = bf16[4,32,2048]{2,1,0:T(8,128)(2,1)S(1)} collective-permute-done((bf16[4,32,2048]{2,1,0:T(8,128)(2,1)S(1)}, bf16[4,32,2048]{2,1,0:T(8,128)(2,1)S(1)}, u32[]{:S(2)}, u32[]{:S(2)}) %collective-permute-start.53) | collective-permute-done | bytes 524320 | tf_op jit(solution)/shard_map/ppermute | solution.py:41
  392.8 7.3 %fusion.95 = f32[256,3584]{1,0:T(8,128)S(1)} fusion(bf16[256,2048]{1,0:T(8,128)(2,1)S(1)} %bitcast.153, bf16[3584,2048]{1,0:T(8,128)(2,1)} %param.9), kind=kOutput, calls=%fused_computation.201 | convolution fusion | flops 3758096384 | bytes 19398656 | tf_op jit(solution)/shard_map/dot_general | solution.py:23
  406.0 2.3 copy.22
  408.3 2.3 copy.21
  416.2 9.9 %collective-permute-done.45 = bf16[64,3584]{1,0:T(8,128)(2,1)S(1)} collective-permute-done((bf16[64,3584]{1,0:T(8,128)(2,1)S(1)}, bf16[64,3584]{1,0:T(8,128)(2,1)S(1)}, u32[]{:S(2)}, u32[]{:S(2)}) %collective-permute-start.45) | collective-permute-done | bytes 458784 | tf_op jit(solution)/shard_map/ppermute | solution.py:36
  426.3 9.3 %collective-permute-done.55 = bf16[64,3584]{1,0:T(8,128)(2,1)S(1)} collective-permute-done((bf16[64,3584]{1,0:T(8,128)(2,1)S(1)}, bf16[64,3584]{1,0:T(8,128)(2,1)S(1)}, u32[]{:S(2)}, u32[]{:S(2)}) %collective-permute-start.55) | collective-permute-done | bytes 458784 | tf_op jit(solution)/shard_map/ppermute | solution.py:36
  438.3 10.9 %collective-permute-done.56 = bf16[64,3584]{1,0:T(8,128)(2,1)S(1)} collective-permute-done((bf16[64,3584]{1,0:T(8,128)(2,1)S(1)}, bf16[64,3584]{1,0:T(8,128)(2,1)S(1)}, u32[]{:S(2)}, u32[]{:S(2)}) %collective-permute-start.56) | collective-permute-done | bytes 458784 | tf_op jit(solution)/shard_map/ppermute | solution.py:36
  451.9 22.5 %shard_map.64 = f32[2048,3584]{1,0:T(8,128)} custom-call(bf16[2048,256]{1,0:T(8,128)(2,1)S(1)} %bitcast.127, bf16[2048,256]{1,0:T(8,128)(2,1)S(1)} %bitcast.126, bf16[2048,256]{1,0:T(8,128)(2,1)S(1)} %bitcast.129, bf16[2048,256]{1,0:T(8,128)(2,1)S(1)} %bitcast.128, bf16[256,3584]{1,0:T(8,128)(2,1)S(1)} %pad_maximum_fusion.2.refs_4_, ...), custom_call_target="tpu_custom_call" | custom-call | flops 15032385536 | bytes 40894464 | tf_op jit(solution)/shard_map/pallas_call | solution.py:88
  (304 shorter events, 114.7 us)
Async XLA Ops:
  6.5 184.2 %all-gather.7.cloned.1.call-start = ((), (), s32[]{:S(2)}) async-start(), calls=%async_computation.1 | async-start | bytes 2752512 | tf_op jit(solution)/shard_map/all_gather | solution.py:207
  8.0 17.0 %collective-permute-start = (bf16[4,32,2048]{2,1,0:T(8,128)(2,1)S(1)}, bf16[4,32,2048]{2,1,0:T(8,128)(2,1)S(1)}, u32[]{:S(2)}, u32[]{:S(2)}) collective-permute-start(bf16[4,32,2048]{2,1,0:T(8,128)(2,1)S(1)} %pad_maximum_fusion.22), channel_id=1, source_target_pairs={{0,4},{4,8},{8,12},{12,0},{1,5},{5,9},{9,13},{13,1},{2,6},{6,10},{... | collective-permute-start | bytes 1572872 | tf_op jit(solution)/shard_map/ppermute | solution.py:41
  36.4 13.8 %collective-permute-start.3 = (f32[128,3584]{1,0:T(8,128)}, f32[128,3584]{1,0:T(8,128)}, u32[]{:S(2)}, u32[]{:S(2)}) collective-permute-start(f32[128,3584]{1,0:T(8,128)} %slice.322), channel_id=1, source_target_pairs={{0,1},{1,0},{2,3},{3,2},{4,5},{5,4},{6,7},{7,6},{8,9},{9,8},{10,11... | collective-permute-start | bytes 5505032 | tf_op jit(solution)/shard_map/ppermute | solution.py:36
  39.3 32.0 %collective-permute-start.5 = (bf16[4,32,2048]{2,1,0:T(8,128)(2,1)S(1)}, bf16[4,32,2048]{2,1,0:T(8,128)(2,1)S(1)}, u32[]{:S(2)}, u32[]{:S(2)}) collective-permute-start(bf16[4,32,2048]{2,1,0:T(8,128)(2,1)S(1)} %pad_maximum_fusion.22), channel_id=1, source_target_pairs={{0,12},{4,0},{8,4},{12,8},{1,13},{5,1},{9,5},{13,9},{2,14},{6,2},{... | collective-permute-start | bytes 1572872 | tf_op jit(solution)/shard_map/ppermute | solution.py:41
  41.2 34.3 %collective-permute-start.1 = (bf16[4,32,2048]{2,1,0:T(8,128)(2,1)S(1)}, bf16[4,32,2048]{2,1,0:T(8,128)(2,1)}, u32[]{:S(2)}, u32[]{:S(2)}) collective-permute-start(bf16[4,32,2048]{2,1,0:T(8,128)(2,1)S(1)} %pad_maximum_fusion.22), channel_id=1, source_target_pairs={{0,8},{4,12},{8,0},{12,4},{1,9},{5,13},{9,1},{13,5},{2,10},{6,14},... | collective-permute-start | bytes 1572872 | tf_op jit(solution)/shard_map/ppermute | solution.py:41
  49.9 18.2 %collective-permute-start.2 = (f32[128,3584]{1,0:T(8,128)}, f32[128,3584]{1,0:T(8,128)}, u32[]{:S(2)}, u32[]{:S(2)}) collective-permute-start(f32[128,3584]{1,0:T(8,128)} %slice.319), channel_id=1, source_target_pairs={{0,1},{1,0},{2,3},{3,2},{4,5},{5,4},{6,7},{7,6},{8,9},{9,8},{10,11... | collective-permute-start | bytes 5505032 | tf_op jit(solution)/shard_map/ppermute | solution.py:36
  59.0 13.1 %collective-permute-start.4 = (f16[64,3712]{1,0:T(8,128)(2,1)S(1)}, f16[64,3712]{1,0:T(8,128)(2,1)S(1)}, u32[]{:S(2)}, u32[]{:S(2)}) collective-permute-start(f16[64,3712]{1,0:T(8,128)(2,1)S(1)} %concatenate.89), channel_id=1, source_target_pairs={{0,2},{1,3},{2,0},{3,1},{4,6},{5,7},{6,4},{7,5},{8,10},{9,11},{10,... | collective-permute-start | bytes 1425416 | tf_op jit(solution)/shard_map/ppermute | solution.py:36
  68.0 16.5 %collective-permute-start.7 = (f32[128,3584]{1,0:T(8,128)S(1)}, f32[128,3584]{1,0:T(8,128)S(1)}, u32[]{:S(2)}, u32[]{:S(2)}) collective-permute-start(f32[128,3584]{1,0:T(8,128)S(1)} %slice.324), channel_id=1, source_target_pairs={{0,1},{1,0},{2,3},{3,2},{4,5},{5,4},{6,7},{7,6},{8,9},{9,8},{10,11... | collective-permute-start | bytes 5505032 | tf_op jit(solution)/shard_map/ppermute | solution.py:36
  68.1 18.1 %collective-permute-start.6 = (bf16[4,32,2048]{2,1,0:T(8,128)(2,1)S(1)}, bf16[4,32,2048]{2,1,0:T(8,128)(2,1)}, u32[]{:S(2)}, u32[]{:S(2)}) collective-permute-start(bf16[4,32,2048]{2,1,0:T(8,128)(2,1)S(1)} %copy-done.45), channel_id=1, source_target_pairs={{0,16},{16,0},{1,17},{17,1},{2,18},{18,2},{3,19},{19,3},{4,20},{20... | collective-permute-start | bytes 1572872 | tf_op jit(solution)/shard_map/ppermute | solution.py:36
  71.3 14.9 %collective-permute-start.8 = (f16[64,3584]{1,0:T(8,128)(2,1)S(1)}, f16[64,3584]{1,0:T(8,128)(2,1)S(1)}, u32[]{:S(2)}, u32[]{:S(2)}) collective-permute-start(f16[64,3584]{1,0:T(8,128)(2,1)S(1)} %fusion.58), channel_id=1, source_target_pairs={{0,2},{1,3},{2,0},{3,1},{4,6},{5,7},{6,4},{7,5},{8,10},{9,11},{10,... | collective-permute-start | bytes 1376264 | tf_op jit(solution)/shard_map/ppermute | solution.py:36
  84.2 18.5 %collective-permute-start.11 = (f32[128,3584]{1,0:T(8,128)S(1)}, f32[128,3584]{1,0:T(8,128)S(1)}, u32[]{:S(2)}, u32[]{:S(2)}) collective-permute-start(f32[128,3584]{1,0:T(8,128)S(1)} %slice.333), channel_id=1, source_target_pairs={{0,1},{1,0},{2,3},{3,2},{4,5},{5,4},{6,7},{7,6},{8,9},{9,8},{10,11... | collective-permute-start | bytes 5505032 | tf_op jit(solution)/shard_map/ppermute | solution.py:36
  84.6 13.0 %collective-permute-start.13 = (bf16[64,3584]{1,0:T(8,128)(2,1)S(1)}, bf16[64,3584]{1,0:T(8,128)(2,1)S(1)}, u32[]{:S(2)}, u32[]{:S(2)}) collective-permute-start(bf16[64,3584]{1,0:T(8,128)(2,1)S(1)} %fusion.56), channel_id=1, source_target_pairs={{0,2},{1,3},{2,0},{3,1},{4,6},{5,7},{6,4},{7,5},{8,10},{9,11},{10,... | collective-permute-start | bytes 1376264 | tf_op jit(solution)/shard_map/ppermute | solution.py:36
  94.9 29.9 %collective-permute-start.9 = (f32[128,3584]{1,0:T(8,128)}, f32[128,3584]{1,0:T(8,128)}, u32[]{:S(2)}, u32[]{:S(2)}) collective-permute-start(f32[128,3584]{1,0:T(8,128)} %slice.328), channel_id=1, source_target_pairs={{0,1},{1,0},{2,3},{3,2},{4,5},{5,4},{6,7},{7,6},{8,9},{9,8},{10,11... | collective-permute-start | bytes 5505032 | tf_op jit(solution)/shard_map/ppermute | solution.py:36
  101.2 19.9 %collective-permute-start.16 = (bf16[64,3584]{1,0:T(8,128)(2,1)S(1)}, bf16[64,3584]{1,0:T(8,128)(2,1)S(1)}, u32[]{:S(2)}, u32[]{:S(2)}) collective-permute-start(bf16[64,3584]{1,0:T(8,128)(2,1)S(1)} %get-tuple-element.87), channel_id=1, source_target_pairs={{0,2},{1,3},{2,0},{3,1},{4,6},{5,7},{6,4},{7,5},{8,10},{9,11},{10,... | collective-permute-start | bytes 1376264 | tf_op jit(solution)/shard_map/ppermute | solution.py:36
  108.1 15.5 %collective-permute-start.12 = (f16[64,3712]{1,0:T(8,128)(2,1)}, f16[64,3712]{1,0:T(8,128)(2,1)}, u32[]{:S(2)}, u32[]{:S(2)}) collective-permute-start(f16[64,3712]{1,0:T(8,128)(2,1)} %concatenate.91), channel_id=1, source_target_pairs={{0,2},{1,3},{2,0},{3,1},{4,6},{5,7},{6,4},{7,5},{8,10},{9,11},{10,... | collective-permute-start | bytes 1425416 | tf_op jit(solution)/shard_map/ppermute | solution.py:36
  119.4 24.4 %collective-permute-start.14 = (f32[128,3584]{1,0:T(8,128)}, f32[128,3584]{1,0:T(8,128)}, u32[]{:S(2)}, u32[]{:S(2)}) collective-permute-start(f32[128,3584]{1,0:T(8,128)} %slice.343), channel_id=1, source_target_pairs={{0,1},{1,0},{2,3},{3,2},{4,5},{5,4},{6,7},{7,6},{8,9},{9,8},{10,11... | collective-permute-start | bytes 5505032 | tf_op jit(solution)/shard_map/ppermute | solution.py:36
  119.4 99.8 %all-gather.5.cloned.1.call-start = ((), (), s32[]{:S(2)}) async-start(), calls=%async_computation | async-start | bytes 2752512 | tf_op jit(solution)/shard_map/all_gather | solution.py:207
  119.5 29.7 %collective-permute-start.23 = (bf16[4,32,2048]{2,1,0:T(8,128)(2,1)}, bf16[4,32,2048]{2,1,0:T(8,128)(2,1)S(1)}, u32[]{:S(2)}, u32[]{:S(2)}) collective-permute-start(bf16[4,32,2048]{2,1,0:T(8,128)(2,1)} %collective-permute-done.1), channel_id=1, source_target_pairs={{0,16},{16,0},{1,17},{17,1},{2,18},{18,2},{3,19},{19,3},{4,20},{20... | collective-permute-start | bytes 1572872 | tf_op jit(solution)/shard_map/ppermute | solution.py:36
  121.1 38.9 %collective-permute-start.24 = (bf16[4,32,2048]{2,1,0:T(8,128)(2,1)}, bf16[4,32,2048]{2,1,0:T(8,128)(2,1)S(1)}, u32[]{:S(2)}, u32[]{:S(2)}) collective-permute-start(bf16[4,32,2048]{2,1,0:T(8,128)(2,1)} %copy-done.43), channel_id=1, source_target_pairs={{0,16},{16,0},{1,17},{17,1},{2,18},{18,2},{3,19},{19,3},{4,20},{20... | collective-permute-start | bytes 1572872 | tf_op jit(solution)/shard_map/ppermute | solution.py:36
  126.4 34.9 %collective-permute-start.10 = (f16[64,3584]{1,0:T(8,128)(2,1)S(1)}, f16[64,3584]{1,0:T(8,128)(2,1)S(1)}, u32[]{:S(2)}, u32[]{:S(2)}) collective-permute-start(f16[64,3584]{1,0:T(8,128)(2,1)S(1)} %fusion.54), channel_id=1, source_target_pairs={{0,2},{1,3},{2,0},{3,1},{4,6},{5,7},{6,4},{7,5},{8,10},{9,11},{10,... | collective-permute-start | bytes 1376264 | tf_op jit(solution)/shard_map/ppermute | solution.py:36
  137.2 85.5 %collective-permute-start.21 = (bf16[4,32,2048]{2,1,0:T(8,128)(2,1)}, bf16[4,32,2048]{2,1,0:T(8,128)(2,1)}, u32[]{:S(2)}, u32[]{:S(2)}) collective-permute-start(bf16[4,32,2048]{2,1,0:T(8,128)(2,1)} %get-tuple-element.104), channel_id=1, source_target_pairs={{0,8},{4,12},{8,0},{12,4},{1,9},{5,13},{9,1},{13,5},{2,10},{6,14},... | collective-permute-start | bytes 1572872 | tf_op jit(solution)/shard_map/ppermute | solution.py:41
  143.8 79.0 %collective-permute-start.20 = (bf16[4,32,2048]{2,1,0:T(8,128)(2,1)}, bf16[4,32,2048]{2,1,0:T(8,128)(2,1)}, u32[]{:S(2)}, u32[]{:S(2)}) collective-permute-start(bf16[4,32,2048]{2,1,0:T(8,128)(2,1)} %get-tuple-element.103), channel_id=1, source_target_pairs={{0,12},{4,0},{8,4},{12,8},{1,13},{5,1},{9,5},{13,9},{2,14},{6,2},{... | collective-permute-start | bytes 1572872 | tf_op jit(solution)/shard_map/ppermute | solution.py:41
  149.2 28.3 %collective-permute-start.30 = (f32[128,3584]{1,0:T(8,128)}, f32[128,3584]{1,0:T(8,128)}, u32[]{:S(2)}, u32[]{:S(2)}) collective-permute-start(f32[128,3584]{1,0:T(8,128)} %slice.359), channel_id=1, source_target_pairs={{0,1},{1,0},{2,3},{3,2},{4,5},{5,4},{6,7},{7,6},{8,9},{9,8},{10,11... | collective-permute-start | bytes 5505032 | tf_op jit(solution)/shard_map/ppermute | solution.py:36
  166.9 34.0 %collective-permute-start.25 = (f32[128,3584]{1,0:T(8,128)}, f32[128,3584]{1,0:T(8,128)}, u32[]{:S(2)}, u32[]{:S(2)}) collective-permute-start(f32[128,3584]{1,0:T(8,128)} %slice.363), channel_id=1, source_target_pairs={{0,1},{1,0},{2,3},{3,2},{4,5},{5,4},{6,7},{7,6},{8,9},{9,8},{10,11... | collective-permute-start | bytes 5505032 | tf_op jit(solution)/shard_map/ppermute | solution.py:36
  176.3 13.5 %collective-permute-start.18 = (bf16[64,3584]{1,0:T(8,128)(2,1)S(1)}, bf16[64,3584]{1,0:T(8,128)(2,1)S(1)}, u32[]{:S(2)}, u32[]{:S(2)}) collective-permute-start(bf16[64,3584]{1,0:T(8,128)(2,1)S(1)} %get-tuple-element.85), channel_id=1, source_target_pairs={{0,2},{1,3},{2,0},{3,1},{4,6},{5,7},{6,4},{7,5},{8,10},{9,11},{10,... | collective-permute-start | bytes 1376264 | tf_op jit(solution)/shard_map/ppermute | solution.py:36
  179.9 16.7 %collective-permute-start.31 = (bf16[64,3584]{1,0:T(8,128)(2,1)}, bf16[64,3584]{1,0:T(8,128)(2,1)S(1)}, u32[]{:S(2)}, u32[]{:S(2)}) collective-permute-start(bf16[64,3584]{1,0:T(8,128)(2,1)} %fusion.37), channel_id=1, source_target_pairs={{0,2},{1,3},{2,0},{3,1},{4,6},{5,7},{6,4},{7,5},{8,10},{9,11},{10,... | collective-permute-start | bytes 1376264 | tf_op jit(solution)/shard_map/ppermute | solution.py:36
  199.5 13.5 %collective-permute-start.32 = (bf16[64,3584]{1,0:T(8,128)(2,1)S(1)}, bf16[64,3584]{1,0:T(8,128)(2,1)S(1)}, u32[]{:S(2)}, u32[]{:S(2)}) collective-permute-start(bf16[64,3584]{1,0:T(8,128)(2,1)S(1)} %fusion.40), channel_id=1, source_target_pairs={{0,2},{1,3},{2,0},{3,1},{4,6},{5,7},{6,4},{7,5},{8,10},{9,11},{10,... | collective-permute-start | bytes 1376264 | tf_op jit(solution)/shard_map/ppermute | solution.py:36
  202.4 16.8 %collective-permute-start.26 = (bf16[64,3584]{1,0:T(8,128)(2,1)S(1)}, bf16[64,3584]{1,0:T(8,128)(2,1)}, u32[]{:S(2)}, u32[]{:S(2)}) collective-permute-start(bf16[64,3584]{1,0:T(8,128)(2,1)S(1)} %fusion.41), channel_id=1, source_target_pairs={{0,2},{1,3},{2,0},{3,1},{4,6},{5,7},{6,4},{7,5},{8,10},{9,11},{10,... | collective-permute-start | bytes 1376264 | tf_op jit(solution)/shard_map/ppermute | solution.py:36
  211.7 13.0 %collective-permute-start.22 = (bf16[4,32,2048]{2,1,0:T(8,128)(2,1)}, bf16[4,32,2048]{2,1,0:T(8,128)(2,1)}, u32[]{:S(2)}, u32[]{:S(2)}) collective-permute-start(bf16[4,32,2048]{2,1,0:T(8,128)(2,1)} %fusion.59), channel_id=1, source_target_pairs={{0,4},{4,8},{8,12},{12,0},{1,5},{5,9},{9,13},{13,1},{2,6},{6,10},{... | collective-permute-start | bytes 1572872 | tf_op jit(solution)/shard_map/ppermute | solution.py:41
  214.1 14.8 %collective-permute-start.33 = (bf16[128,3584]{1,0:T(8,128)(2,1)}, bf16[128,3584]{1,0:T(8,128)(2,1)}, u32[]{:S(2)}, u32[]{:S(2)}) collective-permute-start(bf16[128,3584]{1,0:T(8,128)(2,1)} %pad_maximum_fusion.17), channel_id=1, source_target_pairs={{0,1},{1,0},{2,3},{3,2},{4,5},{5,4},{6,7},{7,6},{8,9},{9,8},{10,11... | collective-permute-start | bytes 2752520 | tf_op jit(solution)/shard_map/ppermute | solution.py:36
  221.4 26.4 %collective-permute-start.27 = (bf16[64,3584]{1,0:T(8,128)(2,1)S(1)}, bf16[64,3584]{1,0:T(8,128)(2,1)S(1)}, u32[]{:S(2)}, u32[]{:S(2)}) collective-permute-start(bf16[64,3584]{1,0:T(8,128)(2,1)S(1)} %fusion.44), channel_id=1, source_target_pairs={{0,2},{1,3},{2,0},{3,1},{4,6},{5,7},{6,4},{7,5},{8,10},{9,11},{10,... | collective-permute-start | bytes 1376264 | tf_op jit(solution)/shard_map/ppermute | solution.py:36
  226.6 12.8 %collective-permute-start.29 = (bf16[4,32,2048]{2,1,0:T(8,128)(2,1)S(1)}, bf16[4,32,2048]{2,1,0:T(8,128)(2,1)S(1)}, u32[]{:S(2)}, u32[]{:S(2)}) collective-permute-start(bf16[4,32,2048]{2,1,0:T(8,128)(2,1)S(1)} %fusion.20), channel_id=1, source_target_pairs={{0,12},{4,0},{8,4},{12,8},{1,13},{5,1},{9,5},{13,9},{2,14},{6,2},{... | collective-permute-start | bytes 1572872 | tf_op jit(solution)/shard_map/ppermute | solution.py:41
  248.4 54.4 %collective-permute-start.36 = (bf16[4,32,2048]{2,1,0:T(8,128)(2,1)S(1)}, bf16[4,32,2048]{2,1,0:T(8,128)(2,1)S(1)}, u32[]{:S(2)}, u32[]{:S(2)}) collective-permute-start(bf16[4,32,2048]{2,1,0:T(8,128)(2,1)S(1)} %fusion.20), channel_id=1, source_target_pairs={{0,4},{4,8},{8,12},{12,0},{1,5},{5,9},{9,13},{13,1},{2,6},{6,10},{... | collective-permute-start | bytes 1572872 | tf_op jit(solution)/shard_map/ppermute | solution.py:41
  249.0 53.8 %collective-permute-start.39 = (bf16[4,32,2048]{2,1,0:T(8,128)(2,1)S(1)}, bf16[4,32,2048]{2,1,0:T(8,128)(2,1)S(1)}, u32[]{:S(2)}, u32[]{:S(2)}) collective-permute-start(bf16[4,32,2048]{2,1,0:T(8,128)(2,1)S(1)} %copy-done.47), channel_id=1, source_target_pairs={{0,12},{4,0},{8,4},{12,8},{1,13},{5,1},{9,5},{13,9},{2,14},{6,2},{... | collective-permute-start | bytes 1572872 | tf_op jit(solution)/shard_map/ppermute | solution.py:41
  252.3 50.6 %collective-permute-start.38 = (bf16[4,32,2048]{2,1,0:T(8,128)(2,1)S(1)}, bf16[4,32,2048]{2,1,0:T(8,128)(2,1)S(1)}, u32[]{:S(2)}, u32[]{:S(2)}) collective-permute-start(bf16[4,32,2048]{2,1,0:T(8,128)(2,1)S(1)} %copy-done.48), channel_id=1, source_target_pairs={{0,8},{4,12},{8,0},{12,4},{1,9},{5,13},{9,1},{13,5},{2,10},{6,14},... | collective-permute-start | bytes 1572872 | tf_op jit(solution)/shard_map/ppermute | solution.py:41
  252.9 42.6 %collective-permute-start.35 = (bf16[4,32,2048]{2,1,0:T(8,128)(2,1)S(1)}, bf16[4,32,2048]{2,1,0:T(8,128)(2,1)}, u32[]{:S(2)}, u32[]{:S(2)}) collective-permute-start(bf16[4,32,2048]{2,1,0:T(8,128)(2,1)S(1)} %copy-done.49), channel_id=1, source_target_pairs={{0,12},{4,0},{8,4},{12,8},{1,13},{5,1},{9,5},{13,9},{2,14},{6,2},{... | collective-permute-start | bytes 1572872 | tf_op jit(solution)/shard_map/ppermute | solution.py:41
  255.6 47.2 %collective-permute-start.37 = (bf16[64,3584]{1,0:T(8,128)(2,1)S(1)}, bf16[64,3584]{1,0:T(8,128)(2,1)S(1)}, u32[]{:S(2)}, u32[]{:S(2)}) collective-permute-start(bf16[64,3584]{1,0:T(8,128)(2,1)S(1)} %fusion.36), channel_id=1, source_target_pairs={{0,2},{1,3},{2,0},{3,1},{4,6},{5,7},{6,4},{7,5},{8,10},{9,11},{10,... | collective-permute-start | bytes 1376264 | tf_op jit(solution)/shard_map/ppermute | solution.py:36
  311.8 15.1 %collective-permute-start.40 = (f32[128,3584]{1,0:T(8,128)S(1)}, f32[128,3584]{1,0:T(8,128)S(1)}, u32[]{:S(2)}, u32[]{:S(2)}) collective-permute-start(f32[128,3584]{1,0:T(8,128)S(1)} %slice.380), channel_id=1, source_target_pairs={{0,1},{1,0},{2,3},{3,2},{4,5},{5,4},{6,7},{7,6},{8,9},{9,8},{10,11... | collective-permute-start | bytes 5505032 | tf_op jit(solution)/shard_map/ppermute | solution.py:36
  311.9 24.2 %collective-permute-start.42 = (bf16[4,32,2048]{2,1,0:T(8,128)(2,1)S(1)}, bf16[4,32,2048]{2,1,0:T(8,128)(2,1)S(1)}, u32[]{:S(2)}, u32[]{:S(2)}) collective-permute-start(bf16[4,32,2048]{2,1,0:T(8,128)(2,1)S(1)} %fusion.60), channel_id=1, source_target_pairs={{0,4},{4,8},{8,12},{12,0},{1,5},{5,9},{9,13},{13,1},{2,6},{6,10},{... | collective-permute-start | bytes 1572872 | tf_op jit(solution)/shard_map/ppermute | solution.py:41
  325.7 12.7 %collective-permute-start.41 = (bf16[64,3584]{1,0:T(8,128)(2,1)S(1)}, bf16[64,3584]{1,0:T(8,128)(2,1)S(1)}, u32[]{:S(2)}, u32[]{:S(2)}) collective-permute-start(bf16[64,3584]{1,0:T(8,128)(2,1)S(1)} %fusion.34), channel_id=1, source_target_pairs={{0,2},{1,3},{2,0},{3,1},{4,6},{5,7},{6,4},{7,5},{8,10},{9,11},{10,... | collective-permute-start | bytes 1376264 | tf_op jit(solution)/shard_map/ppermute | solution.py:36
  340.0 13.4 %collective-permute-start.47 = (bf16[4,32,2048]{2,1,0:T(8,128)(2,1)S(1)}, bf16[4,32,2048]{2,1,0:T(8,128)(2,1)S(1)}, u32[]{:S(2)}, u32[]{:S(2)}) collective-permute-start(bf16[4,32,2048]{2,1,0:T(8,128)(2,1)S(1)} %fusion.15), channel_id=1, source_target_pairs={{0,12},{4,0},{8,4},{12,8},{1,13},{5,1},{9,5},{13,9},{2,14},{6,2},{... | collective-permute-start | bytes 1572872 | tf_op jit(solution)/shard_map/ppermute | solution.py:41
  366.9 25.2 %collective-permute-start.52 = (bf16[4,32,2048]{2,1,0:T(8,128)(2,1)S(1)}, bf16[4,32,2048]{2,1,0:T(8,128)(2,1)S(1)}, u32[]{:S(2)}, u32[]{:S(2)}) collective-permute-start(bf16[4,32,2048]{2,1,0:T(8,128)(2,1)S(1)} %fusion.15), channel_id=1, source_target_pairs={{0,4},{4,8},{8,12},{12,0},{1,5},{5,9},{9,13},{13,1},{2,6},{6,10},{... | collective-permute-start | bytes 1572872 | tf_op jit(solution)/shard_map/ppermute | solution.py:41
  367.4 24.6 %collective-permute-start.53 = (bf16[4,32,2048]{2,1,0:T(8,128)(2,1)S(1)}, bf16[4,32,2048]{2,1,0:T(8,128)(2,1)S(1)}, u32[]{:S(2)}, u32[]{:S(2)}) collective-permute-start(bf16[4,32,2048]{2,1,0:T(8,128)(2,1)S(1)} %copy-done.51), channel_id=1, source_target_pairs={{0,12},{4,0},{8,4},{12,8},{1,13},{5,1},{9,5},{13,9},{2,14},{6,2},{... | collective-permute-start | bytes 1572872 | tf_op jit(solution)/shard_map/ppermute | solution.py:41
  378.5 13.6 %collective-permute-start.50 = (bf16[64,3584]{1,0:T(8,128)(2,1)S(1)}, bf16[64,3584]{1,0:T(8,128)(2,1)S(1)}, u32[]{:S(2)}, u32[]{:S(2)}) collective-permute-start(bf16[64,3584]{1,0:T(8,128)(2,1)S(1)} %fusion.28), channel_id=1, source_target_pairs={{0,2},{1,3},{2,0},{3,1},{4,6},{5,7},{6,4},{7,5},{8,10},{9,11},{10,... | collective-permute-start | bytes 1376264 | tf_op jit(solution)/shard_map/ppermute | solution.py:36
  380.8 23.7 %collective-permute-start.43 = (bf16[128,3584]{1,0:T(8,128)(2,1)}, bf16[128,3584]{1,0:T(8,128)(2,1)}, u32[]{:S(2)}, u32[]{:S(2)}) collective-permute-start(bf16[128,3584]{1,0:T(8,128)(2,1)} %pad_maximum_fusion.18), channel_id=1, source_target_pairs={{0,1},{1,0},{2,3},{3,2},{4,5},{5,4},{6,7},{7,6},{8,9},{9,8},{10,11... | collective-permute-start | bytes 2752520 | tf_op jit(solution)/shard_map/ppermute | solution.py:36
  412.7 13.4 %collective-permute-start.45 = (bf16[64,3584]{1,0:T(8,128)(2,1)S(1)}, bf16[64,3584]{1,0:T(8,128)(2,1)S(1)}, u32[]{:S(2)}, u32[]{:S(2)}) collective-permute-start(bf16[64,3584]{1,0:T(8,128)(2,1)S(1)} %fusion.31), channel_id=1, source_target_pairs={{0,2},{1,3},{2,0},{3,1},{4,6},{5,7},{6,4},{7,5},{8,10},{9,11},{10,... | collective-permute-start | bytes 1376264 | tf_op jit(solution)/shard_map/ppermute | solution.py:36
  415.2 20.4 %collective-permute-start.55 = (bf16[64,3584]{1,0:T(8,128)(2,1)S(1)}, bf16[64,3584]{1,0:T(8,128)(2,1)S(1)}, u32[]{:S(2)}, u32[]{:S(2)}) collective-permute-start(bf16[64,3584]{1,0:T(8,128)(2,1)S(1)} %fusion.21), channel_id=1, source_target_pairs={{0,2},{1,3},{2,0},{3,1},{4,6},{5,7},{6,4},{7,5},{8,10},{9,11},{10,... | collective-permute-start | bytes 1376264 | tf_op jit(solution)/shard_map/ppermute | solution.py:36
  426.2 23.1 %collective-permute-start.46 = (bf16[128,3584]{1,0:T(8,128)(2,1)S(1)}, bf16[128,3584]{1,0:T(8,128)(2,1)S(1)}, u32[]{:S(2)}, u32[]{:S(2)}) collective-permute-start(bf16[128,3584]{1,0:T(8,128)(2,1)S(1)} %pad_maximum_fusion.19), channel_id=1, source_target_pairs={{0,1},{1,0},{2,3},{3,2},{4,5},{5,4},{6,7},{7,6},{8,9},{9,8},{10,11... | collective-permute-start | bytes 2752520 | tf_op jit(solution)/shard_map/ppermute | solution.py:36
  (74 other events, 684.5 us)
Sparse Core Ops, SparseCore 0:
  119.6 45.6 all-gather.6
  177.7 31.8 all-gather.4

commit v9 on v8

--- a/solution.py
+++ b/solution.py
@@ -48,10 +48,13 @@
     for _ in range(FACTORS):
         factors.append(jnp.clip(left, -14.0, 15.0))
         left = left - factors[-1]
-    shape = (*values.shape[:-1], LANES // FACTORS)
-    marks = [jnp.broadcast_to(jnp.exp2(factor), shape) for factor in factors]
+    shape = (*values.shape[:-1], LANES)
+    at = lax.broadcasted_iota(jnp.int32, shape, len(shape) - 1) // (LANES // FACTORS)
+    factor = factors[0]
+    for i in range(1, FACTORS):
+        factor = jnp.where(at == i, factors[i], factor)
     body = values * jnp.exp2(left - power)
-    return jnp.concatenate([body, *marks], axis=-1).astype(jnp.float16)
+    return jnp.concatenate([body, jnp.exp2(factor)], axis=-1).astype(jnp.float16)
 
 
 def decoded(code):
@@ -127,14 +130,7 @@
     own = [own_rows(inputs, 0, half) for half in halves]
     fetched = {(0, 0): own[0], (1, 0): own[1]}
     for k in range(1, ring):
-        needed = [fetched[0, i] for i in range(1, per_group)] if k >= per_group else []
-        fetched[0, k] = shift(tie(own[0], needed), "row", k)
-
-    def fetch_other(step, after):
-        for k in step:
-            if k:
-                fetched[1, k] = swap(tie(fetched[0, k], after), "grp", 1)
-        return [fetched[1, k] for k in step if k]
+        fetched[0, k] = shift(own[0], "row", k)
 
     gate_scale = 2.0 ** math.floor(math.log2(65504.0 / (0.375 * width * count)))
 
@@ -176,58 +172,37 @@
             mask //= 2
         return values, mark
 
-    steps = [list(range(j * per_group, (j + 1) * per_group)) for j in range(GROUPS)]
     last = ring - 1
-    sums, marks, xs = {}, [], {}
-    gains = [[None] * GROUPS, [None] * GROUPS]
-    moved = {}
-
-    def project(half, j, form, after):
+    sums, marks, gains, moved = {}, [], {}, {}
+
+    def project(half, x, form, after):
         for sent in [mark[1] for mark in marks[-2:-1]] + [mark[2] for mark in marks[-3:-2]]:
             after = after + sent
-        if (half, j) in xs:
-            x = tie(xs[half, j], after)
-        else:
-            xs[half, j] = x = joined([tie(fetched[half, k], after) for k in steps[j]])
         weight = {"gate": w_gate, "up": w_up, "tangent": query}[form]
-        sums[half, j, form], *mark = sum_over_col(matmul(x, weight), form)
+        sums[half, form], *mark = sum_over_col(matmul(tie(x, after), weight), form)
         marks.append(mark)
         return mark[0]
 
-    def hidden_rows(half, j, after):
-        if half == 0:
-            gate_out, up_out = sums[0, j, "gate"], sums[0, j, "up"]
-            sigmas = jax.nn.sigmoid(gate_out)
-            gains[0][j] = sigmas * (1.0 + gate_out * (1.0 - sigmas)) * up_out
-        tangent = tie(sums[half, j, "tangent"], after)
-        hidden = (gains[half][j] * tangent).astype(jnp.bfloat16)
-        return gather_over_col(hidden)
-
-    def share_gain(j, after):
-        both = lax.all_gather(tie(gains[0][j], after), "grp")
-        gains[1][j] = lax.dynamic_index_in_dim(both, 1 - grp, 0, keepdims=False)
-
-    def out_sums(half, j, hidden, after):
-        out = matmul(tie(hidden, after), w_down).reshape(count, per_group, rows, width)
-        for i, k in enumerate(steps[j]):
-            piece = out[:, i]
-            if k < last:
-                piece = piece.astype(jnp.bfloat16)
-                mark = piece
-                piece = shift(piece, "row", last - k)
-            moved[half, k] = piece
-        return mark
-
-    def scaled_pieces(half, after):
+    def out_sums(half, early, late):
+        hidden = (gains[half] * tie(sums[half, "tangent"], early)).astype(jnp.bfloat16)
+        whole, _ = gather_over_col(hidden)
+        out = matmul(tie(whole, late), w_down).reshape(count, ring, rows, width)
+        sent = [out[:, k].astype(jnp.bfloat16) for k in range(last)]
+        for k in range(last):
+            moved[half, k] = shift(sent[k], "row", last - k)
+        moved[half, last] = out[:, last]
+        return sent
+
+    def scaled_pieces(half):
         total = moved[half, last]
         for k in range(last):
-            total = total + tie(moved[half, k], after).astype(jnp.float32)
+            total = total + moved[half, k].astype(jnp.float32)
         curv = own_rows(curvature, (me + 1) % ring * shard, halves[half])
         pieces = [None] * last + [(curv * total).astype(jnp.bfloat16)]
         cut = ring // 4
         for k in reversed(range(cut, last)):
             pieces[k] = shift(pieces[k + 1], "row", -1)
-        piece = tie(pieces[last], [pieces[steps[-1][0]]])
+        piece = tie(pieces[last], [pieces[ring - per_group]])
         for k in range(cut):
             pieces[k] = piece = shift(piece, "row")
         return pieces
@@ -235,45 +210,40 @@
     turned, bars = [], []
 
     def back(half, j, pieces, after):
-        x = joined([tie(pieces[k], after) for k in steps[j]])
-        turned.append(tie(xs[half, j], pieces[last:]).T)
+        step = slice(j * per_group, (j + 1) * per_group)
+        x = joined([tie(piece, after) for piece in pieces[step]])
+        act = tie(xs[half], pieces[last:]).reshape(count, ring, rows, width)
+        turned.append(act[:, step].reshape(-1, width).T)
         own, first, sent, got = sum_over_col(times_down(x, w_down), "back")
-        whole, near = gather_over_col((own * gains[half][j]).astype(jnp.bfloat16))
+        gain = gains[half].reshape(ring, rows, -1)[step].reshape(own.shape)
+        whole, near = gather_over_col((own * gain).astype(jnp.bfloat16))
         bars.append(whole)
         return first, sent, got, [near]
 
-    tail = GROUPS - 1
-    early, others = [], []
-    for j in range(GROUPS):
-        first = project(0, j, "up", [])
-        if j:
-            early.append(hidden_rows(0, j - 1, first))
-        project(0, j, "gate", others[-1] if j == tail else [])
-        first = project(0, j, "tangent", [])
-        others.append(fetch_other(steps[j], first))
-        if j:
-            share_gain(j - 1, first)
-    ready = [out_sums(0, j, early[j][0], marks[-2][1]) for j in range(tail)]
-    first = project(1, 0, "tangent", ready)
-    hidden, _ = hidden_rows(0, tail, first)
-    for j in range(1, GROUPS):
-        first = project(1, j, "tangent", others[j])
-    share_gain(tail, first)
-    ready = [out_sums(0, tail, hidden, [])]
-    pieces = scaled_pieces(0, [])
-
-    hidden = [hidden_rows(1, j, []) for j in range(GROUPS)]
-    ready = [out_sums(1, j, hidden[j][0], []) for j in range(tail)]
-    first, sent, got, near = back(0, tail, pieces, ready)
-    ready = [out_sums(1, tail, hidden[tail][0], sent + [moved[1, 0]])]
-    for j in reversed(range(tail)):
-        come = [moved[1, k] for k in range(1, per_group)]
-        _, sent, nextgot, _ = back(0, j, pieces, ready + got + come)
-    pieces = scaled_pieces(1, sent + near)
-    after = nextgot
+    xs = [joined([fetched[0, k] for k in range(ring)])]
+    first = project(0, xs[0], "up", [])
+    for k in range(1, ring):
+        fetched[1, k] = swap(tie(fetched[0, k], first), "grp", 1)
+    project(0, xs[0], "gate", [])
+    project(0, xs[0], "tangent", [])
+    xs.append(joined([tie(fetched[1, k], marks[-2][1]) for k in range(ring)]))
+    first = project(1, xs[1], "tangent", [])
+
+    gate_out = sums[0, "gate"]
+    sigmas = jax.nn.sigmoid(gate_out)
+    gains[0] = sigmas * (1.0 + gate_out * (1.0 - sigmas)) * sums[0, "up"]
+    gains[1] = swap(gains[0], "grp", 1)
+    out_sums(0, first, marks[-1][1])
+    after = out_sums(1, [], [])
+    pieces = scaled_pieces(0)
+    near = []
     for j in reversed(range(GROUPS)):
-        _, sent, got, near = back(1, j, pieces, after)
-        after = got + near
+        _, sent, got, nextnear = back(0, j, pieces, after)
+        after, near = got + near, nextnear
+    pieces = scaled_pieces(1)
+    for j in reversed(range(GROUPS)):
+        _, sent, got, nextnear = back(1, j, pieces, after)
+        after, near = got + near, nextnear
     return last_product(turned, bars, tokens)
 
 

time: 486 us -> 588 us (1.21)
  waiting for transfers between devices: 178 us -> 316 us
  other arithmetic: 45.5 us -> 28.7 us
  between operations: 14.8 us -> 1.16 us
  matrix products: 113 us -> 103 us
  starting transfers between devices: 61.1 us -> 70.5 us
  local copies, waits for them, and re-layouts: 46.2 us -> 37.2 us
    ppermute x43 -> x32, waiting for transfers between devices: 98.4 us -> 170 us  [swap(): return lax.ppermute(values, axis, [(i, i ^ mask) for i in range(count)])]
    ppermute x15, waiting for transfers between devices: 79.9 us -> 146 us  [shift(): lax.ppermute(values, axis, [(i, (i + by) % count) for i in range(count)])]
    ppermute x15, starting transfers between devices: 32.5 us -> 50.7 us  [shift(): lax.ppermute(values, axis, [(i, (i + by) % count) for i in range(count)])]
    dot_general x12 -> x6, matrix products: 83.9 us -> 67.4 us  [matmul(): return jnp.dot(left, right, preferred_element_type=jnp.float32)]
    convert_element_type x8 -> x4, other arithmetic: 16.4 us -> 7.6 us  [the longest x2 4.03 us: back(): whole, near = gather_over_col((own * gain).astype(jnp.bfloat16))]
    ppermute x43 -> x32, starting transfers between devices: 28.5 us -> 19.8 us  [swap(): return lax.ppermute(values, axis, [(i, i ^ mask) for i in range(count)])]
    optimization_barrier x4 -> x0, local copies, waits for them, and re-layouts: 6.41 us -> none  [tie(): return lax.optimization_barrier((values, *after))[0] if after else values]
    dot_general x4, matrix products: 29.3 us -> 35.3 us  [times_down(): lax.dot_general(left, w_down, (((1,), (1,)), ((), ())), preferred_element...]
  transfers between devices with their start and end apart: 60 -> 47, of which waited for: 25 -> 22; matrix products, arithmetic and copies ran while one was open for 34% -> 18% of each run, Pallas kernels for 0% -> 0%
where the time goes in v9:
time: 588 us; the launch traced here: 579 us
  waiting for transfers between devices  316 us (54%)
  matrix products  103 us (18%)
  starting transfers between devices  70.5 us (12%)
  local copies, waits for them, and re-layouts  37.2 us (6%)
  other arithmetic  28.7 us (5%)
  Pallas kernels  22.5 us (4%)
    ppermute x32, waiting for transfers between devices, swap(): return lax.ppermute(values, axis, [(i, i ^ mask) for i in range(count)])  170 us
    ppermute x15, waiting for transfers between devices, shift(): lax.ppermute(values, axis, [(i, (i + by) % count) for i in range(count)])  146 us
    dot_general x6, matrix products, matmul(): return jnp.dot(left, right, preferred_element_type=jnp.float32)  67.4 us
    ppermute x15, starting transfers between devices, shift(): lax.ppermute(values, axis, [(i, (i + by) % count) for i in range(count)])  50.7 us
    dot_general x4, matrix products, times_down(): lax.dot_general(left, w_down, (((1,), (1,)), ((), ())), preferred_element...  35.3 us
    pallas_call x1, Pallas kernels, last_product(): pl.pallas_call(functools.partial(last_kernel, 1.0 / tokens, len(turned)),...  22.5 us
    ppermute x32, starting transfers between devices, swap(): return lax.ppermute(values, axis, [(i, i ^ mask) for i in range(count)])  19.8 us
  transfers between devices with their start and end apart: 47, of which 22 were waited for; matrix products, arithmetic and copies ran while one was open for 18% of the time, Pallas kernels for 0%

profile of v9, /device:TPU:0, one launch (start us, length us, event | category | flops | bytes accessed | tf_op | source)
XLA Modules:
  0.0 579.1 jit_solution(7224043481435095746)
XLA Ops:
  1.4 5.1 collective-permute-start.2
  7.6 11.4 %collective-permute-done.2 = bf16[4,32,2048]{2,1,0:T(8,128)(2,1)S(1)} collective-permute-done((bf16[4,32,2048]{2,1,0:T(8,128)(2,1)S(1)}, bf16[4,32,2048]{2,1,0:T(8,128)(2,1)S(1)}, u32[]{:S(2)}, u32[]{:S(2)}) %collective-permute-start.2) | collective-permute-done | bytes 524320 | tf_op jit(solution)/shard_map/ppermute | solution.py:41
  18.9 32.4 %collective-permute-done.1 = bf16[4,32,2048]{2,1,0:T(8,128)(2,1)S(1)} collective-permute-done((bf16[4,32,2048]{2,1,0:T(8,128)(2,1)S(1)}, bf16[4,32,2048]{2,1,0:T(8,128)(2,1)S(1)}, u32[]{:S(2)}, u32[]{:S(2)}) %collective-permute-start.1) | collective-permute-done | bytes 524320 | tf_op jit(solution)/shard_map/ppermute | solution.py:41
  51.6 11.0 %fusion.48 = f32[512,3584]{1,0:T(8,128)S(1)} fusion(bf16[512,2048]{1,0:T(8,128)(2,1)S(1)} %bitcast.121, bf16[2048,3584]{1,0:T(8,128)(2,1)} %param.8), kind=kOutput, calls=%fused_computation.132 | convolution fusion | flops 7516192768 | bytes 24117248 | tf_op jit(solution)/shard_map/dot_general | solution.py:19
  63.0 11.1 %fusion.47 = f32[512,3584]{1,0:T(8,128)S(1)} fusion(bf16[512,2048]{1,0:T(8,128)(2,1)S(1)} %bitcast.122, bf16[2048,3584]{1,0:T(8,128)(2,1)} %param.7), kind=kOutput, calls=%fused_computation.131 | convolution fusion | flops 7516192768 | bytes 24117248 | tf_op jit(solution)/shard_map/dot_general | solution.py:19
  74.1 2.3 slice.255
  78.8 11.0 %fusion.49 = f32[512,3584]{1,0:T(8,128)S(1)} fusion(bf16[512,2048]{1,0:T(8,128)(2,1)S(1)} %bitcast.123, bf16[2048,3584]{1,0:T(8,128)(2,1)} %param.10), kind=kOutput, calls=%fused_computation.133 | convolution fusion | flops 7516192768 | bytes 24117248 | tf_op jit(solution)/shard_map/dot_general | solution.py:19
  97.3 2.7 fusion.15
  100.0 7.0 %collective-permute-done.11 = bf16[4,32,2048]{2,1,0:T(8,128)(2,1)S(1)} collective-permute-done((bf16[4,32,2048]{2,1,0:T(8,128)(2,1)S(1)}, bf16[4,32,2048]{2,1,0:T(8,128)(2,1)S(1)}, u32[]{:S(2)}, u32[]{:S(2)}) %collective-permute-start.11) | collective-permute-done | bytes 524320 | tf_op jit(solution)/shard_map/ppermute | solution.py:36
  107.0 11.2 %collective-permute-done.10 = bf16[4,32,2048]{2,1,0:T(8,128)(2,1)S(1)} collective-permute-done((bf16[4,32,2048]{2,1,0:T(8,128)(2,1)S(1)}, bf16[4,32,2048]{2,1,0:T(8,128)(2,1)S(1)}, u32[]{:S(2)}, u32[]{:S(2)}) %collective-permute-start.10) | collective-permute-done | bytes 524320 | tf_op jit(solution)/shard_map/ppermute | solution.py:36
  118.2 10.6 %collective-permute-done.9 = bf16[4,32,2048]{2,1,0:T(8,128)(2,1)S(1)} collective-permute-done((bf16[4,32,2048]{2,1,0:T(8,128)(2,1)S(1)}, bf16[4,32,2048]{2,1,0:T(8,128)(2,1)S(1)}, u32[]{:S(2)}, u32[]{:S(2)}) %collective-permute-start.9) | collective-permute-done | bytes 524320 | tf_op jit(solution)/shard_map/ppermute | solution.py:36
  130.1 11.2 %fusion.50 = f32[512,3584]{1,0:T(8,128)S(1)} fusion(bf16[512,2048]{1,0:T(8,128)(2,1)S(1)} %bitcast.125, bf16[2048,3584]{1,0:T(8,128)(2,1)} %param.10), kind=kOutput, calls=%fused_computation.134 | convolution fusion | flops 7516192768 | bytes 24117248 | tf_op jit(solution)/shard_map/dot_general | solution.py:19
  141.4 2.1 slice.274
  147.7 20.9 %collective-permute-done.8 = bf16[128,3584]{1,0:T(8,128)(2,1)S(1)} collective-permute-done((bf16[128,3584]{1,0:T(8,128)(2,1)S(1)}, bf16[128,3584]{1,0:T(8,128)(2,1)S(1)}, u32[]{:S(2)}, u32[]{:S(2)}) %collective-permute-start.8) | collective-permute-done | bytes 917536 | tf_op jit(solution)/shard_map/ppermute | solution.py:36
  170.5 17.3 %collective-permute-done.4 = f16[128,3584]{1,0:T(8,128)(2,1)S(1)} collective-permute-done((f16[128,3584]{1,0:T(8,128)(2,1)S(1)}, f16[128,3584]{1,0:T(8,128)(2,1)S(1)}, u32[]{:S(2)}, u32[]{:S(2)}) %collective-permute-start.4) | collective-permute-done | bytes 917536 | tf_op jit(solution)/shard_map/ppermute | solution.py:36
  187.7 3.0 multiply_convert_fusion
  194.7 19.4 %collective-permute-done.12 = bf16[128,3584]{1,0:T(8,128)(2,1)S(1)} collective-permute-done((bf16[128,3584]{1,0:T(8,128)(2,1)S(1)}, bf16[128,3584]{1,0:T(8,128)(2,1)S(1)}, u32[]{:S(2)}, u32[]{:S(2)}) %collective-permute-start.12) | collective-permute-done | bytes 917536 | tf_op jit(solution)/shard_map/ppermute | solution.py:36
  214.3 18.0 %collective-permute-done.19 = bf16[128,3584]{1,0:T(8,128)(2,1)S(1)} collective-permute-done((bf16[128,3584]{1,0:T(8,128)(2,1)S(1)}, bf16[128,3584]{1,0:T(8,128)(2,1)S(1)}, u32[]{:S(2)}, u32[]{:S(2)}) %collective-permute-start.19) | collective-permute-done | bytes 917536 | tf_op jit(solution)/shard_map/ppermute | solution.py:36
  235.3 20.1 %collective-permute-done.20 = bf16[128,3584]{1,0:T(8,128)(2,1)S(1)} collective-permute-done((bf16[128,3584]{1,0:T(8,128)(2,1)S(1)}, bf16[128,3584]{1,0:T(8,128)(2,1)S(1)}, u32[]{:S(2)}, u32[]{:S(2)}) %collective-permute-start.20) | collective-permute-done | bytes 917536 | tf_op jit(solution)/shard_map/ppermute | solution.py:36
  257.3 11.3 %fusion.51 = f32[512,2048]{1,0:T(8,128)S(1)} fusion(bf16[512,3584]{1,0:T(8,128)(2,1)S(1)} %pad_maximum_fusion, bf16[3584,2048]{1,0:T(8,128)(2,1)} %param.9), kind=kOutput, calls=%fused_computation.135 | convolution fusion | flops 7516192768 | bytes 22544384 | tf_op jit(solution)/shard_map/dot_general | solution.py:19
  274.6 2.9 collective-permute-start.15
  277.5 2.5 dynamic-slice_bitcast_fusion.3
  280.0 8.8 %collective-permute-done.17 = bf16[4,32,2048]{2,1,0:T(8,128)(2,1)} collective-permute-done((bf16[4,32,2048]{2,1,0:T(8,128)(2,1)}, bf16[4,32,2048]{2,1,0:T(8,128)(2,1)}, u32[]{:S(2)}, u32[]{:S(2)}) %collective-permute-start.17) | collective-permute-done | bytes 524320 | tf_op jit(solution)/shard_map/ppermute | solution.py:41
  288.8 22.0 %collective-permute-done.16 = bf16[4,32,2048]{2,1,0:T(8,128)(2,1)} collective-permute-done((bf16[4,32,2048]{2,1,0:T(8,128)(2,1)}, bf16[4,32,2048]{2,1,0:T(8,128)(2,1)}, u32[]{:S(2)}, u32[]{:S(2)}) %collective-permute-start.16) | collective-permute-done | bytes 524320 | tf_op jit(solution)/shard_map/ppermute | solution.py:41
  310.8 2.1 fusion.26
  312.9 13.1 %collective-permute-start.25 = (bf16[4,32,2048]{2,1,0:T(8,128)(2,1)S(1)}, bf16[4,32,2048]{2,1,0:T(8,128)(2,1)S(1)}, u32[]{:S(2)}, u32[]{:S(2)}) collective-permute-start(bf16[4,32,2048]{2,1,0:T(8,128)(2,1)S(1)} %fusion.26), channel_id=1, source_target_pairs={{0,12},{4,0},{8,4},{12,8},{1,13},{5,1},{9,5},{13,9},{2,14},{6,2},{... | collective-permute-start | bytes 1572872 | tf_op jit(solution)/shard_map/ppermute | solution.py:41
  326.0 11.7 %fusion = f32[512,2048]{1,0:T(8,128)S(1)} fusion(bf16[3584,2048]{1,0:T(8,128)(2,1)} %param.9, bf16[256,3584]{1,0:T(8,128)(2,1)} %collective-permute-done.21, bf16[128,3584]{1,0:T(8,128)(2,1)S(1)} %copy-done.28, bf16[128,3584]{1,0:T(8,128)(2,1)S(1)} %fusion.8), kind=kOutput, calls=%fused_computation.1 | convolution fusion | flops 7527202816 | bytes 22544384 | tf_op jit(solution)/shard_map/dot_general | solution.py:19
  341.1 11.3 %fusion.52 = f32[256,3584]{1,0:T(8,128)} fusion(bf16[256,2048]{1,0:T(8,128)(2,1)} %bitcast.137, bf16[3584,2048]{1,0:T(8,128)(2,1)} %param.9), kind=kOutput, calls=%fused_computation.136 | convolution fusion | flops 3758096384 | bytes 19398656 | tf_op jit(solution)/shard_map/dot_general | solution.py:23
  354.3 3.8 collective-permute-start.31
  361.3 18.5 %collective-permute-done.31 = bf16[4,32,2048]{2,1,0:T(8,128)(2,1)S(1)} collective-permute-done((bf16[4,32,2048]{2,1,0:T(8,128)(2,1)S(1)}, bf16[4,32,2048]{2,1,0:T(8,128)(2,1)S(1)}, u32[]{:S(2)}, u32[]{:S(2)}) %collective-permute-start.31) | collective-permute-done | bytes 524320 | tf_op jit(solution)/shard_map/ppermute | solution.py:41
  380.6 9.1 %fusion.53 = f32[256,3584]{1,0:T(8,128)} fusion(bf16[256,2048]{1,0:T(8,128)(2,1)S(1)} %bitcast.135, bf16[3584,2048]{1,0:T(8,128)(2,1)} %param.9), kind=kOutput, calls=%fused_computation.137 | convolution fusion | flops 3758096384 | bytes 19398656 | tf_op jit(solution)/shard_map/dot_general | solution.py:23
  394.3 2.7 collective-permute-start.22
  397.7 10.8 %collective-permute-done.24 = bf16[4,32,2048]{2,1,0:T(8,128)(2,1)S(1)} collective-permute-done((bf16[4,32,2048]{2,1,0:T(8,128)(2,1)}, bf16[4,32,2048]{2,1,0:T(8,128)(2,1)S(1)}, u32[]{:S(2)}, u32[]{:S(2)}) %collective-permute-start.24) | collective-permute-done | bytes 524320 | tf_op jit(solution)/shard_map/ppermute | solution.py:41
  408.6 22.0 %collective-permute-done.23 = bf16[4,32,2048]{2,1,0:T(8,128)(2,1)S(1)} collective-permute-done((bf16[4,32,2048]{2,1,0:T(8,128)(2,1)}, bf16[4,32,2048]{2,1,0:T(8,128)(2,1)S(1)}, u32[]{:S(2)}, u32[]{:S(2)}) %collective-permute-start.23) | collective-permute-done | bytes 524320 | tf_op jit(solution)/shard_map/ppermute | solution.py:41
  431.0 12.7 %collective-permute-start.36 = (bf16[4,32,2048]{2,1,0:T(8,128)(2,1)S(1)}, bf16[4,32,2048]{2,1,0:T(8,128)(2,1)S(1)}, u32[]{:S(2)}, u32[]{:S(2)}) collective-permute-start(bf16[4,32,2048]{2,1,0:T(8,128)(2,1)S(1)} %fusion.21), channel_id=1, source_target_pairs={{0,12},{4,0},{8,4},{12,8},{1,13},{5,1},{9,5},{13,9},{2,14},{6,2},{... | collective-permute-start | bytes 1572872 | tf_op jit(solution)/shard_map/ppermute | solution.py:41
  446.7 11.2 %collective-permute-done.28 = bf16[64,3584]{1,0:T(8,128)(2,1)S(1)} collective-permute-done((bf16[64,3584]{1,0:T(8,128)(2,1)S(1)}, bf16[64,3584]{1,0:T(8,128)(2,1)S(1)}, u32[]{:S(2)}, u32[]{:S(2)}) %collective-permute-start.28) | collective-permute-done | bytes 458784 | tf_op jit(solution)/shard_map/ppermute | solution.py:36
  458.9 7.6 %fusion.54 = f32[256,3584]{1,0:T(8,128)S(1)} fusion(bf16[256,2048]{1,0:T(8,128)(2,1)S(1)} %bitcast.138, bf16[3584,2048]{1,0:T(8,128)(2,1)} %param.9), kind=kOutput, calls=%fused_computation.138 | convolution fusion | flops 3758096384 | bytes 19398656 | tf_op jit(solution)/shard_map/dot_general | solution.py:23
  468.0 2.5 collective-permute-start.42
  472.8 20.4 %collective-permute-done.42 = bf16[4,32,2048]{2,1,0:T(8,128)(2,1)S(1)} collective-permute-done((bf16[4,32,2048]{2,1,0:T(8,128)(2,1)S(1)}, bf16[4,32,2048]{2,1,0:T(8,128)(2,1)S(1)}, u32[]{:S(2)}, u32[]{:S(2)}) %collective-permute-start.42) | collective-permute-done | bytes 524320 | tf_op jit(solution)/shard_map/ppermute | solution.py:41
  494.2 7.3 %fusion.55 = f32[256,3584]{1,0:T(8,128)S(1)} fusion(bf16[256,2048]{1,0:T(8,128)(2,1)S(1)} %bitcast.136, bf16[3584,2048]{1,0:T(8,128)(2,1)} %param.9), kind=kOutput, calls=%fused_computation.139 | convolution fusion | flops 3758096384 | bytes 19398656 | tf_op jit(solution)/shard_map/dot_general | solution.py:23
  506.4 3.2 fusion.45
  511.1 2.3 copy.23
  517.7 11.8 %collective-permute-done.44 = bf16[64,3584]{1,0:T(8,128)(2,1)S(1)} collective-permute-done((bf16[64,3584]{1,0:T(8,128)(2,1)S(1)}, bf16[64,3584]{1,0:T(8,128)(2,1)S(1)}, u32[]{:S(2)}, u32[]{:S(2)}) %collective-permute-start.44) | collective-permute-done | bytes 458784 | tf_op jit(solution)/shard_map/ppermute | solution.py:36
  529.5 2.3 fusion.27
  534.1 11.2 %collective-permute-done.39 = bf16[64,3584]{1,0:T(8,128)(2,1)S(1)} collective-permute-done((bf16[64,3584]{1,0:T(8,128)(2,1)S(1)}, bf16[64,3584]{1,0:T(8,128)(2,1)S(1)}, u32[]{:S(2)}, u32[]{:S(2)}) %collective-permute-start.39) | collective-permute-done | bytes 458784 | tf_op jit(solution)/shard_map/ppermute | solution.py:36
  545.5 7.9 %collective-permute-done.45 = bf16[64,3584]{1,0:T(8,128)(2,1)S(1)} collective-permute-done((bf16[64,3584]{1,0:T(8,128)(2,1)S(1)}, bf16[64,3584]{1,0:T(8,128)(2,1)S(1)}, u32[]{:S(2)}, u32[]{:S(2)}) %collective-permute-start.45) | collective-permute-done | bytes 458784 | tf_op jit(solution)/shard_map/ppermute | solution.py:36
  553.8 2.2 collective-permute-done.46
  556.2 22.5 %shard_map.64 = f32[2048,3584]{1,0:T(8,128)} custom-call(bf16[2048,256]{1,0:T(8,128)(2,1)S(1)} %bitcast.117, bf16[2048,256]{1,0:T(8,128)(2,1)S(1)} %bitcast.118, bf16[2048,256]{1,0:T(8,128)(2,1)S(1)} %bitcast.119, bf16[2048,256]{1,0:T(8,128)(2,1)S(1)} %bitcast.120, bf16[256,3584]{1,0:T(8,128)(2,1)S(1)} %pad_maximum_fusion.5.refs_4_, ...), custom_call_target="tpu_custom_call" | custom-call | flops 15032385536 | bytes 40894464 | tf_op jit(solution)/shard_map/pallas_call | solution.py:91
  (195 shorter events, 72.3 us)
Async XLA Ops:
  1.4 17.5 %collective-permute-start.2 = (bf16[4,32,2048]{2,1,0:T(8,128)(2,1)S(1)}, bf16[4,32,2048]{2,1,0:T(8,128)(2,1)S(1)}, u32[]{:S(2)}, u32[]{:S(2)}) collective-permute-start(bf16[4,32,2048]{2,1,0:T(8,128)(2,1)S(1)} %pad_maximum_fusion.18), channel_id=1, source_target_pairs={{0,12},{4,0},{8,4},{12,8},{1,13},{5,1},{9,5},{13,9},{2,14},{6,2},{... | collective-permute-start | bytes 1572872 | tf_op jit(solution)/shard_map/ppermute | solution.py:41
  6.5 44.8 %collective-permute-start.1 = (bf16[4,32,2048]{2,1,0:T(8,128)(2,1)S(1)}, bf16[4,32,2048]{2,1,0:T(8,128)(2,1)S(1)}, u32[]{:S(2)}, u32[]{:S(2)}) collective-permute-start(bf16[4,32,2048]{2,1,0:T(8,128)(2,1)S(1)} %pad_maximum_fusion.18), channel_id=1, source_target_pairs={{0,8},{4,12},{8,0},{12,4},{1,9},{5,13},{9,1},{13,5},{2,10},{6,14},... | collective-permute-start | bytes 1572872 | tf_op jit(solution)/shard_map/ppermute | solution.py:41
  6.6 44.8 %collective-permute-start = (bf16[4,32,2048]{2,1,0:T(8,128)(2,1)S(1)}, bf16[4,32,2048]{2,1,0:T(8,128)(2,1)S(1)}, u32[]{:S(2)}, u32[]{:S(2)}) collective-permute-start(bf16[4,32,2048]{2,1,0:T(8,128)(2,1)S(1)} %pad_maximum_fusion.18), channel_id=1, source_target_pairs={{0,4},{4,8},{8,12},{12,0},{1,5},{5,9},{9,13},{13,1},{2,6},{6,10},{... | collective-permute-start | bytes 1572872 | tf_op jit(solution)/shard_map/ppermute | solution.py:41
  62.9 14.0 %collective-permute-start.5 = (f32[256,3584]{1,0:T(8,128)S(1)}, f32[256,3584]{1,0:T(8,128)S(1)}, u32[]{:S(2)}, u32[]{:S(2)}) collective-permute-start(f32[256,3584]{1,0:T(8,128)S(1)} %slice.260), channel_id=1, source_target_pairs={{0,1},{1,0},{2,3},{3,2},{4,5},{5,4},{6,7},{7,6},{8,9},{9,8},{10,11... | collective-permute-start | bytes 11010056 | tf_op jit(solution)/shard_map/ppermute | solution.py:36
  76.3 19.5 %collective-permute-start.3 = (f32[256,3584]{1,0:T(8,128)}, f32[256,3584]{1,0:T(8,128)}, u32[]{:S(2)}, u32[]{:S(2)}) collective-permute-start(f32[256,3584]{1,0:T(8,128)} %slice.255), channel_id=1, source_target_pairs={{0,1},{1,0},{2,3},{3,2},{4,5},{5,4},{6,7},{7,6},{8,9},{9,8},{10,11... | collective-permute-start | bytes 11010056 | tf_op jit(solution)/shard_map/ppermute | solution.py:36
  91.9 51.5 %collective-permute-start.7 = (f32[256,3584]{1,0:T(8,128)}, f32[256,3584]{1,0:T(8,128)}, u32[]{:S(2)}, u32[]{:S(2)}) collective-permute-start(f32[256,3584]{1,0:T(8,128)} %slice.270), channel_id=1, source_target_pairs={{0,1},{1,0},{2,3},{3,2},{4,5},{5,4},{6,7},{7,6},{8,9},{9,8},{10,11... | collective-permute-start | bytes 11010056 | tf_op jit(solution)/shard_map/ppermute | solution.py:36
  92.2 14.8 %collective-permute-start.11 = (bf16[4,32,2048]{2,1,0:T(8,128)(2,1)S(1)}, bf16[4,32,2048]{2,1,0:T(8,128)(2,1)S(1)}, u32[]{:S(2)}, u32[]{:S(2)}) collective-permute-start(bf16[4,32,2048]{2,1,0:T(8,128)(2,1)S(1)} %collective-permute-done.2), channel_id=1, source_target_pairs={{0,16},{16,0},{1,17},{17,1},{2,18},{18,2},{3,19},{19,3},{4,20},{20... | collective-permute-start | bytes 1572872 | tf_op jit(solution)/shard_map/ppermute | solution.py:36
  93.8 24.5 %collective-permute-start.10 = (bf16[4,32,2048]{2,1,0:T(8,128)(2,1)S(1)}, bf16[4,32,2048]{2,1,0:T(8,128)(2,1)S(1)}, u32[]{:S(2)}, u32[]{:S(2)}) collective-permute-start(bf16[4,32,2048]{2,1,0:T(8,128)(2,1)S(1)} %collective-permute-done.1), channel_id=1, source_target_pairs={{0,16},{16,0},{1,17},{17,1},{2,18},{18,2},{3,19},{19,3},{4,20},{20... | collective-permute-start | bytes 1572872 | tf_op jit(solution)/shard_map/ppermute | solution.py:36
  94.3 34.6 %collective-permute-start.9 = (bf16[4,32,2048]{2,1,0:T(8,128)(2,1)S(1)}, bf16[4,32,2048]{2,1,0:T(8,128)(2,1)S(1)}, u32[]{:S(2)}, u32[]{:S(2)}) collective-permute-start(bf16[4,32,2048]{2,1,0:T(8,128)(2,1)S(1)} %collective-permute-done), channel_id=1, source_target_pairs={{0,16},{16,0},{1,17},{17,1},{2,18},{18,2},{3,19},{19,3},{4,20},{20... | collective-permute-start | bytes 1572872 | tf_op jit(solution)/shard_map/ppermute | solution.py:36
  95.8 33.3 %collective-permute-start.6 = (f16[128,3712]{1,0:T(8,128)(2,1)}, f16[128,3712]{1,0:T(8,128)(2,1)S(1)}, u32[]{:S(2)}, u32[]{:S(2)}) collective-permute-start(f16[128,3712]{1,0:T(8,128)(2,1)} %pad_maximum_fusion.13), channel_id=1, source_target_pairs={{0,2},{1,3},{2,0},{3,1},{4,6},{5,7},{6,4},{7,5},{8,10},{9,11},{10,... | collective-permute-start | bytes 2850824 | tf_op jit(solution)/shard_map/ppermute | solution.py:36
  143.5 50.4 %collective-permute-start.14 = (f32[256,3584]{1,0:T(8,128)}, f32[256,3584]{1,0:T(8,128)S(1)}, u32[]{:S(2)}, u32[]{:S(2)}) collective-permute-start(f32[256,3584]{1,0:T(8,128)} %slice.274), channel_id=1, source_target_pairs={{0,1},{1,0},{2,3},{3,2},{4,5},{5,4},{6,7},{7,6},{8,9},{9,8},{10,11... | collective-permute-start | bytes 11010056 | tf_op jit(solution)/shard_map/ppermute | solution.py:36
  145.4 23.2 %collective-permute-start.8 = (bf16[128,3584]{1,0:T(8,128)(2,1)S(1)}, bf16[128,3584]{1,0:T(8,128)(2,1)S(1)}, u32[]{:S(2)}, u32[]{:S(2)}) collective-permute-start(bf16[128,3584]{1,0:T(8,128)(2,1)S(1)} %fusion.10), channel_id=1, source_target_pairs={{0,2},{1,3},{2,0},{3,1},{4,6},{5,7},{6,4},{7,5},{8,10},{9,11},{10,... | collective-permute-start | bytes 2752520 | tf_op jit(solution)/shard_map/ppermute | solution.py:36
  146.9 40.8 %collective-permute-start.4 = (f16[128,3584]{1,0:T(8,128)(2,1)S(1)}, f16[128,3584]{1,0:T(8,128)(2,1)S(1)}, u32[]{:S(2)}, u32[]{:S(2)}) collective-permute-start(f16[128,3584]{1,0:T(8,128)(2,1)S(1)} %copy-done.29), channel_id=1, source_target_pairs={{0,2},{1,3},{2,0},{3,1},{4,6},{5,7},{6,4},{7,5},{8,10},{9,11},{10,... | collective-permute-start | bytes 2752520 | tf_op jit(solution)/shard_map/ppermute | solution.py:36
  190.8 23.3 %collective-permute-start.12 = (bf16[128,3584]{1,0:T(8,128)(2,1)S(1)}, bf16[128,3584]{1,0:T(8,128)(2,1)S(1)}, u32[]{:S(2)}, u32[]{:S(2)}) collective-permute-start(bf16[128,3584]{1,0:T(8,128)(2,1)S(1)} %get-tuple-element.55), channel_id=1, source_target_pairs={{0,2},{1,3},{2,0},{3,1},{4,6},{5,7},{6,4},{7,5},{8,10},{9,11},{10,... | collective-permute-start | bytes 2752520 | tf_op jit(solution)/shard_map/ppermute | solution.py:36
  192.3 41.2 %collective-permute-start.18 = (f32[128,3584]{1,0:T(8,128)S(1)}, f32[128,3584]{1,0:T(8,128)S(1)}, u32[]{:S(2)}, u32[]{:S(2)}) collective-permute-start(f32[128,3584]{1,0:T(8,128)S(1)} %get-tuple-element.56), channel_id=1, source_target_pairs={{0,16},{16,0},{1,17},{17,1},{2,18},{18,2},{3,19},{19,3},{4,20},{20... | collective-permute-start | bytes 5505032 | tf_op jit(solution)/shard_map/ppermute | solution.py:36
  194.1 38.2 %collective-permute-start.19 = (bf16[128,3584]{1,0:T(8,128)(2,1)S(1)}, bf16[128,3584]{1,0:T(8,128)(2,1)S(1)}, u32[]{:S(2)}, u32[]{:S(2)}) collective-permute-start(bf16[128,3584]{1,0:T(8,128)(2,1)S(1)} %fusion.9), channel_id=1, source_target_pairs={{0,2},{1,3},{2,0},{3,1},{4,6},{5,7},{6,4},{7,5},{8,10},{9,11},{10,... | collective-permute-start | bytes 2752520 | tf_op jit(solution)/shard_map/ppermute | solution.py:36
  214.2 42.7 %collective-permute-start.13 = (bf16[256,3584]{1,0:T(8,128)(2,1)S(1)}, bf16[256,3584]{1,0:T(8,128)(2,1)S(1)}, u32[]{:S(2)}, u32[]{:S(2)}) collective-permute-start(bf16[256,3584]{1,0:T(8,128)(2,1)S(1)} %pad_maximum_fusion.3), channel_id=1, source_target_pairs={{0,1},{1,0},{2,3},{3,2},{4,5},{5,4},{6,7},{7,6},{8,9},{9,8},{10,11... | collective-permute-start | bytes 5505032 | tf_op jit(solution)/shard_map/ppermute | solution.py:36
  234.8 20.6 %collective-permute-start.20 = (bf16[128,3584]{1,0:T(8,128)(2,1)S(1)}, bf16[128,3584]{1,0:T(8,128)(2,1)S(1)}, u32[]{:S(2)}, u32[]{:S(2)}) collective-permute-start(bf16[128,3584]{1,0:T(8,128)(2,1)S(1)} %fusion.8), channel_id=1, source_target_pairs={{0,2},{1,3},{2,0},{3,1},{4,6},{5,7},{6,4},{7,5},{8,10},{9,11},{10,... | collective-permute-start | bytes 2752520 | tf_op jit(solution)/shard_map/ppermute | solution.py:36
  256.9 69.0 %collective-permute-start.21 = (bf16[256,3584]{1,0:T(8,128)(2,1)}, bf16[256,3584]{1,0:T(8,128)(2,1)}, u32[]{:S(2)}, u32[]{:S(2)}) collective-permute-start(bf16[256,3584]{1,0:T(8,128)(2,1)} %pad_maximum_fusion.4), channel_id=1, source_target_pairs={{0,1},{1,0},{2,3},{3,2},{4,5},{5,4},{6,7},{7,6},{8,9},{9,8},{10,11... | collective-permute-start | bytes 5505032 | tf_op jit(solution)/shard_map/ppermute | solution.py:36
  271.8 17.0 %collective-permute-start.17 = (bf16[4,32,2048]{2,1,0:T(8,128)(2,1)}, bf16[4,32,2048]{2,1,0:T(8,128)(2,1)}, u32[]{:S(2)}, u32[]{:S(2)}) collective-permute-start(bf16[4,32,2048]{2,1,0:T(8,128)(2,1)} %get-tuple-element.76), channel_id=1, source_target_pairs={{0,4},{4,8},{8,12},{12,0},{1,5},{5,9},{9,13},{13,1},{2,6},{6,10},{... | collective-permute-start | bytes 1572872 | tf_op jit(solution)/shard_map/ppermute | solution.py:41
  272.7 38.1 %collective-permute-start.16 = (bf16[4,32,2048]{2,1,0:T(8,128)(2,1)}, bf16[4,32,2048]{2,1,0:T(8,128)(2,1)}, u32[]{:S(2)}, u32[]{:S(2)}) collective-permute-start(bf16[4,32,2048]{2,1,0:T(8,128)(2,1)} %get-tuple-element.77), channel_id=1, source_target_pairs={{0,8},{4,12},{8,0},{12,4},{1,9},{5,13},{9,1},{13,5},{2,10},{6,14},... | collective-permute-start | bytes 1572872 | tf_op jit(solution)/shard_map/ppermute | solution.py:41
  274.6 36.2 %collective-permute-start.15 = (bf16[4,32,2048]{2,1,0:T(8,128)(2,1)}, bf16[4,32,2048]{2,1,0:T(8,128)(2,1)}, u32[]{:S(2)}, u32[]{:S(2)}) collective-permute-start(bf16[4,32,2048]{2,1,0:T(8,128)(2,1)} %get-tuple-element.75), channel_id=1, source_target_pairs={{0,12},{4,0},{8,4},{12,8},{1,13},{5,1},{9,5},{13,9},{2,14},{6,2},{... | collective-permute-start | bytes 1572872 | tf_op jit(solution)/shard_map/ppermute | solution.py:41
  312.9 26.3 %collective-permute-start.25 = (bf16[4,32,2048]{2,1,0:T(8,128)(2,1)S(1)}, bf16[4,32,2048]{2,1,0:T(8,128)(2,1)S(1)}, u32[]{:S(2)}, u32[]{:S(2)}) collective-permute-start(bf16[4,32,2048]{2,1,0:T(8,128)(2,1)S(1)} %fusion.26), channel_id=1, source_target_pairs={{0,12},{4,0},{8,4},{12,8},{1,13},{5,1},{9,5},{13,9},{2,14},{6,2},{... | collective-permute-start | bytes 1572872 | tf_op jit(solution)/shard_map/ppermute | solution.py:41
  354.1 4.0 collective-permute-start.26
  354.2 26.4 %collective-permute-start.30 = (bf16[4,32,2048]{2,1,0:T(8,128)(2,1)S(1)}, bf16[4,32,2048]{2,1,0:T(8,128)(2,1)S(1)}, u32[]{:S(2)}, u32[]{:S(2)}) collective-permute-start(bf16[4,32,2048]{2,1,0:T(8,128)(2,1)S(1)} %fusion.26), channel_id=1, source_target_pairs={{0,4},{4,8},{8,12},{12,0},{1,5},{5,9},{9,13},{13,1},{2,6},{6,10},{... | collective-permute-start | bytes 1572872 | tf_op jit(solution)/shard_map/ppermute | solution.py:41
  354.3 25.5 %collective-permute-start.31 = (bf16[4,32,2048]{2,1,0:T(8,128)(2,1)S(1)}, bf16[4,32,2048]{2,1,0:T(8,128)(2,1)S(1)}, u32[]{:S(2)}, u32[]{:S(2)}) collective-permute-start(bf16[4,32,2048]{2,1,0:T(8,128)(2,1)S(1)} %copy-done.33), channel_id=1, source_target_pairs={{0,12},{4,0},{8,4},{12,8},{1,13},{5,1},{9,5},{13,9},{2,14},{6,2},{... | collective-permute-start | bytes 1572872 | tf_op jit(solution)/shard_map/ppermute | solution.py:41
  360.6 19.1 %collective-permute-start.27 = (bf16[64,3584]{1,0:T(8,128)(2,1)S(1)}, bf16[64,3584]{1,0:T(8,128)(2,1)S(1)}, u32[]{:S(2)}, u32[]{:S(2)}) collective-permute-start(bf16[64,3584]{1,0:T(8,128)(2,1)S(1)} %fusion.37), channel_id=1, source_target_pairs={{0,2},{1,3},{2,0},{3,1},{4,6},{5,7},{6,4},{7,5},{8,10},{9,11},{10,... | collective-permute-start | bytes 1376264 | tf_op jit(solution)/shard_map/ppermute | solution.py:36
  389.8 40.8 %copy-start.26 = (f32[1,32,2048]{2,1,0:T(8,128)S(1)}, f32[1,32,2048]{2,1,0:T(8,128)}, u32[]{:S(2)}) copy-start(f32[1,32,2048]{2,1,0:T(8,128)} %get-tuple-element.67) | copy-start | bytes 786436
  391.6 5.5 collective-permute-start.32
  391.6 16.9 %collective-permute-start.24 = (bf16[4,32,2048]{2,1,0:T(8,128)(2,1)}, bf16[4,32,2048]{2,1,0:T(8,128)(2,1)S(1)}, u32[]{:S(2)}, u32[]{:S(2)}) collective-permute-start(bf16[4,32,2048]{2,1,0:T(8,128)(2,1)} %get-tuple-element.71), channel_id=1, source_target_pairs={{0,4},{4,8},{8,12},{12,0},{1,5},{5,9},{9,13},{13,1},{2,6},{6,10},{... | collective-permute-start | bytes 1572872 | tf_op jit(solution)/shard_map/ppermute | solution.py:41
  392.8 37.8 %collective-permute-start.23 = (bf16[4,32,2048]{2,1,0:T(8,128)(2,1)}, bf16[4,32,2048]{2,1,0:T(8,128)(2,1)S(1)}, u32[]{:S(2)}, u32[]{:S(2)}) collective-permute-start(bf16[4,32,2048]{2,1,0:T(8,128)(2,1)} %get-tuple-element.72), channel_id=1, source_target_pairs={{0,8},{4,12},{8,0},{12,4},{1,9},{5,13},{9,1},{13,5},{2,10},{6,14},... | collective-permute-start | bytes 1572872 | tf_op jit(solution)/shard_map/ppermute | solution.py:41
  394.3 36.3 %collective-permute-start.22 = (bf16[4,32,2048]{2,1,0:T(8,128)(2,1)}, bf16[4,32,2048]{2,1,0:T(8,128)(2,1)S(1)}, u32[]{:S(2)}, u32[]{:S(2)}) collective-permute-start(bf16[4,32,2048]{2,1,0:T(8,128)(2,1)} %get-tuple-element.70), channel_id=1, source_target_pairs={{0,12},{4,0},{8,4},{12,8},{1,13},{5,1},{9,5},{13,9},{2,14},{6,2},{... | collective-permute-start | bytes 1572872 | tf_op jit(solution)/shard_map/ppermute | solution.py:41
  397.1 46.5 %collective-permute-start.33 = (bf16[64,3584]{1,0:T(8,128)(2,1)S(1)}, bf16[64,3584]{1,0:T(8,128)(2,1)S(1)}, u32[]{:S(2)}, u32[]{:S(2)}) collective-permute-start(bf16[64,3584]{1,0:T(8,128)(2,1)S(1)} %fusion.34), channel_id=1, source_target_pairs={{0,2},{1,3},{2,0},{3,1},{4,6},{5,7},{6,4},{7,5},{8,10},{9,11},{10,... | collective-permute-start | bytes 1376264 | tf_op jit(solution)/shard_map/ppermute | solution.py:36
  431.0 27.0 %collective-permute-start.36 = (bf16[4,32,2048]{2,1,0:T(8,128)(2,1)S(1)}, bf16[4,32,2048]{2,1,0:T(8,128)(2,1)S(1)}, u32[]{:S(2)}, u32[]{:S(2)}) collective-permute-start(bf16[4,32,2048]{2,1,0:T(8,128)(2,1)S(1)} %fusion.21), channel_id=1, source_target_pairs={{0,12},{4,0},{8,4},{12,8},{1,13},{5,1},{9,5},{13,9},{2,14},{6,2},{... | collective-permute-start | bytes 1572872 | tf_op jit(solution)/shard_map/ppermute | solution.py:41
  446.2 11.8 %collective-permute-start.28 = (bf16[64,3584]{1,0:T(8,128)(2,1)S(1)}, bf16[64,3584]{1,0:T(8,128)(2,1)S(1)}, u32[]{:S(2)}, u32[]{:S(2)}) collective-permute-start(bf16[64,3584]{1,0:T(8,128)(2,1)S(1)} %get-tuple-element.81), channel_id=1, source_target_pairs={{0,2},{1,3},{2,0},{3,1},{4,6},{5,7},{6,4},{7,5},{8,10},{9,11},{10,... | collective-permute-start | bytes 1376264 | tf_op jit(solution)/shard_map/ppermute | solution.py:36
  466.6 4.5 collective-permute-start.37
  466.7 26.6 %collective-permute-start.41 = (bf16[4,32,2048]{2,1,0:T(8,128)(2,1)S(1)}, bf16[4,32,2048]{2,1,0:T(8,128)(2,1)S(1)}, u32[]{:S(2)}, u32[]{:S(2)}) collective-permute-start(bf16[4,32,2048]{2,1,0:T(8,128)(2,1)S(1)} %fusion.21), channel_id=1, source_target_pairs={{0,4},{4,8},{8,12},{12,0},{1,5},{5,9},{9,13},{13,1},{2,6},{6,10},{... | collective-permute-start | bytes 1572872 | tf_op jit(solution)/shard_map/ppermute | solution.py:41
  468.0 25.2 %collective-permute-start.42 = (bf16[4,32,2048]{2,1,0:T(8,128)(2,1)S(1)}, bf16[4,32,2048]{2,1,0:T(8,128)(2,1)S(1)}, u32[]{:S(2)}, u32[]{:S(2)}) collective-permute-start(bf16[4,32,2048]{2,1,0:T(8,128)(2,1)S(1)} %copy-done.31), channel_id=1, source_target_pairs={{0,12},{4,0},{8,4},{12,8},{1,13},{5,1},{9,5},{13,9},{2,14},{6,2},{... | collective-permute-start | bytes 1572872 | tf_op jit(solution)/shard_map/ppermute | solution.py:41
  470.6 22.7 %collective-permute-start.34 = (bf16[64,3584]{1,0:T(8,128)(2,1)S(1)}, bf16[64,3584]{1,0:T(8,128)(2,1)S(1)}, u32[]{:S(2)}, u32[]{:S(2)}) collective-permute-start(bf16[64,3584]{1,0:T(8,128)(2,1)S(1)} %get-tuple-element.80), channel_id=1, source_target_pairs={{0,2},{1,3},{2,0},{3,1},{4,6},{5,7},{6,4},{7,5},{8,10},{9,11},{10,... | collective-permute-start | bytes 1376264 | tf_op jit(solution)/shard_map/ppermute | solution.py:36
  471.3 22.0 %collective-permute-start.38 = (bf16[64,3584]{1,0:T(8,128)(2,1)S(1)}, bf16[64,3584]{1,0:T(8,128)(2,1)S(1)}, u32[]{:S(2)}, u32[]{:S(2)}) collective-permute-start(bf16[64,3584]{1,0:T(8,128)(2,1)S(1)} %fusion.31), channel_id=1, source_target_pairs={{0,2},{1,3},{2,0},{3,1},{4,6},{5,7},{6,4},{7,5},{8,10},{9,11},{10,... | collective-permute-start | bytes 1376264 | tf_op jit(solution)/shard_map/ppermute | solution.py:36
  503.0 12.1 %collective-permute-start.43 = (f32[128,3584]{1,0:T(8,128)}, f32[128,3584]{1,0:T(8,128)}, u32[]{:S(2)}, u32[]{:S(2)}) collective-permute-start(f32[128,3584]{1,0:T(8,128)} %slice.310), channel_id=1, source_target_pairs={{0,1},{1,0},{2,3},{3,2},{4,5},{5,4},{6,7},{7,6},{8,9},{9,8},{10,11... | collective-permute-start | bytes 5505032 | tf_op jit(solution)/shard_map/ppermute | solution.py:36
  514.7 17.7 %collective-permute-start.29 = (bf16[128,3584]{1,0:T(8,128)(2,1)S(1)}, bf16[128,3584]{1,0:T(8,128)(2,1)S(1)}, u32[]{:S(2)}, u32[]{:S(2)}) collective-permute-start(bf16[128,3584]{1,0:T(8,128)(2,1)S(1)} %pad_maximum_fusion.14), channel_id=1, source_target_pairs={{0,1},{1,0},{2,3},{3,2},{4,5},{5,4},{6,7},{7,6},{8,9},{9,8},{10,11... | collective-permute-start | bytes 2752520 | tf_op jit(solution)/shard_map/ppermute | solution.py:36
  516.9 12.6 %collective-permute-start.44 = (bf16[64,3584]{1,0:T(8,128)(2,1)S(1)}, bf16[64,3584]{1,0:T(8,128)(2,1)S(1)}, u32[]{:S(2)}, u32[]{:S(2)}) collective-permute-start(bf16[64,3584]{1,0:T(8,128)(2,1)S(1)} %fusion.28), channel_id=1, source_target_pairs={{0,2},{1,3},{2,0},{3,1},{4,6},{5,7},{6,4},{7,5},{8,10},{9,11},{10,... | collective-permute-start | bytes 1376264 | tf_op jit(solution)/shard_map/ppermute | solution.py:36
  517.6 35.9 %collective-permute-start.35 = (bf16[128,3584]{1,0:T(8,128)(2,1)S(1)}, bf16[128,3584]{1,0:T(8,128)(2,1)S(1)}, u32[]{:S(2)}, u32[]{:S(2)}) collective-permute-start(bf16[128,3584]{1,0:T(8,128)(2,1)S(1)} %pad_maximum_fusion.15), channel_id=1, source_target_pairs={{0,1},{1,0},{2,3},{3,2},{4,5},{5,4},{6,7},{7,6},{8,9},{9,8},{10,11... | collective-permute-start | bytes 2752520 | tf_op jit(solution)/shard_map/ppermute | solution.py:36
  531.8 13.5 %collective-permute-start.39 = (bf16[64,3584]{1,0:T(8,128)(2,1)S(1)}, bf16[64,3584]{1,0:T(8,128)(2,1)S(1)}, u32[]{:S(2)}, u32[]{:S(2)}) collective-permute-start(bf16[64,3584]{1,0:T(8,128)(2,1)S(1)} %get-tuple-element.79), channel_id=1, source_target_pairs={{0,2},{1,3},{2,0},{3,1},{4,6},{5,7},{6,4},{7,5},{8,10},{9,11},{10,... | collective-permute-start | bytes 1376264 | tf_op jit(solution)/shard_map/ppermute | solution.py:36
  532.6 20.8 %collective-permute-start.45 = (bf16[64,3584]{1,0:T(8,128)(2,1)S(1)}, bf16[64,3584]{1,0:T(8,128)(2,1)S(1)}, u32[]{:S(2)}, u32[]{:S(2)}) collective-permute-start(bf16[64,3584]{1,0:T(8,128)(2,1)S(1)} %get-tuple-element.78), channel_id=1, source_target_pairs={{0,2},{1,3},{2,0},{3,1},{4,6},{5,7},{6,4},{7,5},{8,10},{9,11},{10,... | collective-permute-start | bytes 1376264 | tf_op jit(solution)/shard_map/ppermute | solution.py:36
  545.4 8.3 %collective-permute-start.40 = (bf16[128,3584]{1,0:T(8,128)(2,1)S(1)}, bf16[128,3584]{1,0:T(8,128)(2,1)S(1)}, u32[]{:S(2)}, u32[]{:S(2)}) collective-permute-start(bf16[128,3584]{1,0:T(8,128)(2,1)S(1)} %pad_maximum_fusion.16), channel_id=1, source_target_pairs={{0,1},{1,0},{2,3},{3,2},{4,5},{5,4},{6,7},{7,6},{8,9},{9,8},{10,11... | collective-permute-start | bytes 2752520 | tf_op jit(solution)/shard_map/ppermute | solution.py:36
  553.5 2.5 collective-permute-start.46
  (37 other events, 304.9 us)

commit v10 on v8

--- a/solution.py
+++ b/solution.py
@@ -48,10 +48,13 @@
     for _ in range(FACTORS):
         factors.append(jnp.clip(left, -14.0, 15.0))
         left = left - factors[-1]
-    shape = (*values.shape[:-1], LANES // FACTORS)
-    marks = [jnp.broadcast_to(jnp.exp2(factor), shape) for factor in factors]
+    shape = (*values.shape[:-1], LANES)
+    at = lax.broadcasted_iota(jnp.int32, shape, len(shape) - 1) // (LANES // FACTORS)
+    factor = factors[0]
+    for i in range(1, FACTORS):
+        factor = jnp.where(at == i, factors[i], factor)
     body = values * jnp.exp2(left - power)
-    return jnp.concatenate([body, *marks], axis=-1).astype(jnp.float16)
+    return jnp.concatenate([body, jnp.exp2(factor)], axis=-1).astype(jnp.float16)
 
 
 def decoded(code):
@@ -246,11 +249,11 @@
     early, others = [], []
     for j in range(GROUPS):
         first = project(0, j, "up", [])
+        others.append(fetch_other(steps[j], first))
         if j:
             early.append(hidden_rows(0, j - 1, first))
-        project(0, j, "gate", others[-1] if j == tail else [])
+        project(0, j, "gate", others[0] if j == tail else [])
         first = project(0, j, "tangent", [])
-        others.append(fetch_other(steps[j], first))
         if j:
             share_gain(j - 1, first)
     ready = [out_sums(0, j, early[j][0], marks[-2][1]) for j in range(tail)]
@@ -265,15 +268,12 @@
     hidden = [hidden_rows(1, j, []) for j in range(GROUPS)]
     ready = [out_sums(1, j, hidden[j][0], []) for j in range(tail)]
     first, sent, got, near = back(0, tail, pieces, ready)
-    ready = [out_sums(1, tail, hidden[tail][0], sent + [moved[1, 0]])]
+    ready = [out_sums(1, tail, hidden[tail][0], sent)]
+    others = scaled_pieces(1, near)
     for j in reversed(range(tail)):
-        come = [moved[1, k] for k in range(1, per_group)]
-        _, sent, nextgot, _ = back(0, j, pieces, ready + got + come)
-    pieces = scaled_pieces(1, sent + near)
-    after = nextgot
+        back(0, j, pieces, ready + got + others[last:])
     for j in reversed(range(GROUPS)):
-        _, sent, got, near = back(1, j, pieces, after)
-        after = got + near
+        back(1, j, others, others)
     return last_product(turned, bars, tokens)
 
 

time: 486 us -> 473 us (0.973)
  waiting for transfers between devices: 178 us -> 153 us
  starting transfers between devices: 61.1 us -> 79.5 us
  local copies, waits for them, and re-layouts: 46.2 us -> 36.5 us
    ppermute x15, starting transfers between devices: 32.5 us -> 53.8 us  [shift(): lax.ppermute(values, axis, [(i, (i + by) % count) for i in range(count)])]
    ppermute x15, waiting for transfers between devices: 79.9 us -> 61.1 us  [shift(): lax.ppermute(values, axis, [(i, (i + by) % count) for i in range(count)])]
    ppermute x43, waiting for transfers between devices: 98.4 us -> 92.1 us  [swap(): return lax.ppermute(values, axis, [(i, i ^ mask) for i in range(count)])]
    unnamed x124 -> x108, local copies, waits for them, and re-layouts: 14 us -> 9.73 us
  transfers between devices with their start and end apart: 60 -> 60, of which waited for: 25 -> 24; matrix products, arithmetic and copies ran while one was open for 34% -> 38% of each run, Pallas kernels for 0% -> 0%
where the time goes in v10:
time: 473 us; the launch traced here: 470 us
  waiting for transfers between devices  153 us (32%)
  matrix products  117 us (25%)
  starting transfers between devices  79.5 us (17%)
  other arithmetic  46.4 us (10%)
  local copies, waits for them, and re-layouts  36.5 us (8%)
  Pallas kernels  22.5 us (5%)
  between operations  14.9 us (3%)
    ppermute x43, waiting for transfers between devices, swap(): return lax.ppermute(values, axis, [(i, i ^ mask) for i in range(count)])  92.1 us
    dot_general x12, matrix products, matmul(): return jnp.dot(left, right, preferred_element_type=jnp.float32)  83.8 us
    ppermute x15, waiting for transfers between devices, shift(): lax.ppermute(values, axis, [(i, (i + by) % count) for i in range(count)])  61.1 us
    ppermute x15, starting transfers between devices, shift(): lax.ppermute(values, axis, [(i, (i + by) % count) for i in range(count)])  53.8 us
    dot_general x4, matrix products, times_down(): lax.dot_general(left, w_down, (((1,), (1,)), ((), ())), preferred_element...  32.9 us
    ppermute x43, starting transfers between devices, swap(): return lax.ppermute(values, axis, [(i, i ^ mask) for i in range(count)])  25.7 us
    pallas_call x1, Pallas kernels, last_product(): pl.pallas_call(functools.partial(last_kernel, 1.0 / tokens, len(turned)),...  22.5 us
    slice x12, local copies, waits for them, and re-layouts, sum_over_col(): first = part[half:]  13.8 us
  transfers between devices with their start and end apart: 60, of which 24 were waited for; matrix products, arithmetic and copies ran while one was open for 38% of the time, Pallas kernels for 0%

profile of v10, /device:TPU:0, one launch (start us, length us, event | category | flops | bytes accessed | tf_op | source)
XLA Modules:
  0.0 469.7 jit_solution(1417594721624954146)
XLA Ops:
  8.7 3.1 collective-permute-start
  11.8 13.9 %collective-permute-done = bf16[4,32,2048]{2,1,0:T(8,128)(2,1)S(1)} collective-permute-done((bf16[4,32,2048]{2,1,0:T(8,128)(2,1)S(1)}, bf16[4,32,2048]{2,1,0:T(8,128)(2,1)S(1)}, u32[]{:S(2)}, u32[]{:S(2)}) %collective-permute-start) | collective-permute-done | bytes 524320 | tf_op jit(solution)/shard_map/ppermute | solution.py:41
  26.5 7.2 %fusion.86 = f32[256,3584]{1,0:T(8,128)S(1)} fusion(bf16[256,2048]{1,0:T(8,128)(2,1)S(1)} %bitcast.130, bf16[2048,3584]{1,0:T(8,128)(2,1)} %param.8), kind=kOutput, calls=%fused_computation.192 | convolution fusion | flops 3758096384 | bytes 19398656 | tf_op jit(solution)/shard_map/dot_general | solution.py:19
  38.2 2.9 dynamic-slice_bitcast_fusion.3
  44.7 7.2 %fusion.85 = f32[256,3584]{1,0:T(8,128)S(1)} fusion(bf16[256,2048]{1,0:T(8,128)(2,1)S(1)} %bitcast.131, bf16[2048,3584]{1,0:T(8,128)(2,1)} %param.7), kind=kOutput, calls=%fused_computation.191 | convolution fusion | flops 3758096384 | bytes 19398656 | tf_op jit(solution)/shard_map/dot_general | solution.py:19
  56.7 7.2 %fusion.87 = f32[256,3584]{1,0:T(8,128)S(1)} fusion(bf16[256,2048]{1,0:T(8,128)(2,1)S(1)} %bitcast.132, bf16[2048,3584]{1,0:T(8,128)(2,1)} %param.10), kind=kOutput, calls=%fused_computation.193 | convolution fusion | flops 3758096384 | bytes 19398656 | tf_op jit(solution)/shard_map/dot_general | solution.py:19
  64.9 3.3 collective-permute-done.4
  68.2 9.2 %collective-permute-done.1 = bf16[4,32,2048]{2,1,0:T(8,128)(2,1)} collective-permute-done((bf16[4,32,2048]{2,1,0:T(8,128)(2,1)S(1)}, bf16[4,32,2048]{2,1,0:T(8,128)(2,1)}, u32[]{:S(2)}, u32[]{:S(2)}) %collective-permute-start.1) | collective-permute-done | bytes 524320 | tf_op jit(solution)/shard_map/ppermute | solution.py:41
  78.7 7.3 %fusion.89 = f32[256,3584]{1,0:T(8,128)S(1)} fusion(bf16[256,2048]{1,0:T(8,128)(2,1)S(1)} %bitcast.134, bf16[2048,3584]{1,0:T(8,128)(2,1)} %param.8), kind=kOutput, calls=%fused_computation.195 | convolution fusion | flops 3758096384 | bytes 19398656 | tf_op jit(solution)/shard_map/dot_general | solution.py:19
  90.2 7.2 %fusion.88 = f32[256,3584]{1,0:T(8,128)S(1)} fusion(bf16[256,2048]{1,0:T(8,128)(2,1)S(1)} %bitcast.135, bf16[2048,3584]{1,0:T(8,128)(2,1)} %param.7), kind=kOutput, calls=%fused_computation.194 | convolution fusion | flops 3758096384 | bytes 19398656 | tf_op jit(solution)/shard_map/dot_general | solution.py:19
  106.3 7.6 %fusion.90 = f32[256,3584]{1,0:T(8,128)S(1)} fusion(bf16[256,2048]{1,0:T(8,128)(2,1)S(1)} %bitcast.136, bf16[2048,3584]{1,0:T(8,128)(2,1)} %param.10), kind=kOutput, calls=%fused_computation.196 | convolution fusion | flops 3758096384 | bytes 19398656 | tf_op jit(solution)/shard_map/dot_general | solution.py:19
  118.5 6.3 %collective-permute-done.12 = f16[64,3712]{1,0:T(8,128)(2,1)} collective-permute-done((f16[64,3712]{1,0:T(8,128)(2,1)}, f16[64,3712]{1,0:T(8,128)(2,1)}, u32[]{:S(2)}, u32[]{:S(2)}) %collective-permute-start.12) | collective-permute-done | bytes 475168 | tf_op jit(solution)/shard_map/ppermute | solution.py:36
  130.4 7.7 %convolution_convert_fusion.1 = bf16[256,2048]{1,0:T(8,128)(2,1)S(1)} fusion(bf16[256,3584]{1,0:T(8,128)(2,1)S(1)} %pad_maximum_fusion, bf16[3584,2048]{1,0:T(8,128)(2,1)} %param.9), kind=kOutput, calls=%fused_computation.1 | convolution fusion | flops 3758620672 | bytes 17563648 | tf_op jit(solution)/shard_map/dot_general | solution.py:19
  139.4 3.9 fusion.91
  144.9 3.6 collective-permute-start.20
  150.7 3.9 fusion.92
  156.3 5.3 %collective-permute-done.15 = bf16[64,3584]{1,0:T(8,128)(2,1)S(1)} collective-permute-done((bf16[64,3584]{1,0:T(8,128)(2,1)S(1)}, bf16[64,3584]{1,0:T(8,128)(2,1)S(1)}, u32[]{:S(2)}, u32[]{:S(2)}) %collective-permute-start.15) | collective-permute-done | bytes 458784 | tf_op jit(solution)/shard_map/ppermute | solution.py:36
  161.7 3.6 multiply_convert_fusion
  166.0 2.4 fusion.37
  169.7 9.0 %collective-permute-done.18 = bf16[64,3584]{1,0:T(8,128)(2,1)S(1)} collective-permute-done((bf16[64,3584]{1,0:T(8,128)(2,1)S(1)}, bf16[64,3584]{1,0:T(8,128)(2,1)S(1)}, u32[]{:S(2)}, u32[]{:S(2)}) %collective-permute-start.18) | collective-permute-done | bytes 458784 | tf_op jit(solution)/shard_map/ppermute | solution.py:36
  179.7 7.6 %collective-permute-done.31 = bf16[64,3584]{1,0:T(8,128)(2,1)S(1)} collective-permute-done((bf16[64,3584]{1,0:T(8,128)(2,1)}, bf16[64,3584]{1,0:T(8,128)(2,1)S(1)}, u32[]{:S(2)}, u32[]{:S(2)}) %collective-permute-start.31) | collective-permute-done | bytes 458784 | tf_op jit(solution)/shard_map/ppermute | solution.py:36
  193.8 7.7 %fusion = f32[256,2048]{1,0:T(8,128)S(1)} fusion(bf16[3584,2048]{1,0:T(8,128)(2,1)} %param.9, bf16[128,3584]{1,0:T(8,128)(2,1)} %collective-permute-done.19, bf16[64,3584]{1,0:T(8,128)(2,1)S(1)} %collective-permute-done.18, bf16[64,3584]{1,0:T(8,128)(2,1)S(1)} %get-tuple-element.85), kind=kOutput, calls=%fused_computation.3 | convolution fusion | flops 3763601408 | bytes 18612224 | tf_op jit(solution)/shard_map/dot_general | solution.py:19
  202.5 2.9 collective-permute-start.22
  206.6 4.9 %collective-permute-done.26 = bf16[64,3584]{1,0:T(8,128)(2,1)} collective-permute-done((bf16[64,3584]{1,0:T(8,128)(2,1)S(1)}, bf16[64,3584]{1,0:T(8,128)(2,1)}, u32[]{:S(2)}, u32[]{:S(2)}) %collective-permute-start.26) | collective-permute-done | bytes 458784 | tf_op jit(solution)/shard_map/ppermute | solution.py:36
  214.5 2.4 collective-permute-done.22
  216.9 2.6 fusion.20
  220.0 9.4 %convolution_convert_fusion = bf16[256,2048]{1,0:T(8,128)(2,1)S(1)} fusion(bf16[3584,2048]{1,0:T(8,128)(2,1)} %param.9, bf16[128,3584]{1,0:T(8,128)(2,1)} %collective-permute-done.33, bf16[64,3584]{1,0:T(8,128)(2,1)S(1)} %copy-done.48, bf16[64,3584]{1,0:T(8,128)(2,1)S(1)} %fusion.40), kind=kOutput, calls=%fused_computation | convolution fusion | flops 3764125696 | bytes 17563648 | tf_op jit(solution)/shard_map/dot_general | solution.py:19
  232.4 7.3 %fusion.93 = f32[256,3584]{1,0:T(8,128)S(1)} fusion(bf16[256,2048]{1,0:T(8,128)(2,1)S(1)} %bitcast.155, bf16[3584,2048]{1,0:T(8,128)(2,1)} %param.9), kind=kOutput, calls=%fused_computation.199 | convolution fusion | flops 3758096384 | bytes 19398656 | tf_op jit(solution)/shard_map/dot_general | solution.py:23
  246.0 7.2 %fusion.94 = f32[256,2048]{1,0:T(8,128)S(1)} fusion(bf16[256,3584]{1,0:T(8,128)(2,1)S(1)} %pad_maximum_fusion.1, bf16[3584,2048]{1,0:T(8,128)(2,1)} %param.9), kind=kOutput, calls=%fused_computation.200 | convolution fusion | flops 3758096384 | bytes 18612224 | tf_op jit(solution)/shard_map/dot_general | solution.py:19
  254.7 3.2 collective-permute-done.36
  260.1 8.0 %collective-permute-done.38 = bf16[4,32,2048]{2,1,0:T(8,128)(2,1)S(1)} collective-permute-done((bf16[4,32,2048]{2,1,0:T(8,128)(2,1)S(1)}, bf16[4,32,2048]{2,1,0:T(8,128)(2,1)S(1)}, u32[]{:S(2)}, u32[]{:S(2)}) %collective-permute-start.38) | collective-permute-done | bytes 524320 | tf_op jit(solution)/shard_map/ppermute | solution.py:41
  268.1 12.1 %collective-permute-start.42 = (bf16[4,32,2048]{2,1,0:T(8,128)(2,1)}, bf16[4,32,2048]{2,1,0:T(8,128)(2,1)}, u32[]{:S(2)}, u32[]{:S(2)}) collective-permute-start(bf16[4,32,2048]{2,1,0:T(8,128)(2,1)} %collective-permute-done.29), channel_id=1, source_target_pairs={{0,12},{4,0},{8,4},{12,8},{1,13},{5,1},{9,5},{13,9},{2,14},{6,2},{... | collective-permute-start | bytes 1572872 | tf_op jit(solution)/shard_map/ppermute | solution.py:41
  282.2 11.3 %collective-permute-start.47 = (bf16[4,32,2048]{2,1,0:T(8,128)(2,1)}, bf16[4,32,2048]{2,1,0:T(8,128)(2,1)}, u32[]{:S(2)}, u32[]{:S(2)}) collective-permute-start(bf16[4,32,2048]{2,1,0:T(8,128)(2,1)} %fusion.15), channel_id=1, source_target_pairs={{0,12},{4,0},{8,4},{12,8},{1,13},{5,1},{9,5},{13,9},{2,14},{6,2},{... | collective-permute-start | bytes 1572872 | tf_op jit(solution)/shard_map/ppermute | solution.py:41
  294.6 6.3 %collective-permute-done.42 = bf16[4,32,2048]{2,1,0:T(8,128)(2,1)} collective-permute-done((bf16[4,32,2048]{2,1,0:T(8,128)(2,1)}, bf16[4,32,2048]{2,1,0:T(8,128)(2,1)}, u32[]{:S(2)}, u32[]{:S(2)}) %collective-permute-start.42) | collective-permute-done | bytes 524320 | tf_op jit(solution)/shard_map/ppermute | solution.py:41
  302.2 12.0 %collective-permute-done.47 = bf16[4,32,2048]{2,1,0:T(8,128)(2,1)} collective-permute-done((bf16[4,32,2048]{2,1,0:T(8,128)(2,1)}, bf16[4,32,2048]{2,1,0:T(8,128)(2,1)}, u32[]{:S(2)}, u32[]{:S(2)}) %collective-permute-start.47) | collective-permute-done | bytes 524320 | tf_op jit(solution)/shard_map/ppermute | solution.py:41
  314.1 9.5 %collective-permute-start.48 = (bf16[4,32,2048]{2,1,0:T(8,128)(2,1)}, bf16[4,32,2048]{2,1,0:T(8,128)(2,1)}, u32[]{:S(2)}, u32[]{:S(2)}) collective-permute-start(bf16[4,32,2048]{2,1,0:T(8,128)(2,1)} %fusion.15), channel_id=1, source_target_pairs={{0,4},{4,8},{8,12},{12,0},{1,5},{5,9},{9,13},{13,1},{2,6},{6,10},{... | collective-permute-start | bytes 1572872 | tf_op jit(solution)/shard_map/ppermute | solution.py:41
  323.6 2.9 collective-permute-start.49
  326.5 7.3 %fusion.95 = f32[256,3584]{1,0:T(8,128)S(1)} fusion(bf16[256,2048]{1,0:T(8,128)(2,1)S(1)} %bitcast.150, bf16[3584,2048]{1,0:T(8,128)(2,1)} %param.9), kind=kOutput, calls=%fused_computation.201 | convolution fusion | flops 3758096384 | bytes 19398656 | tf_op jit(solution)/shard_map/dot_general | solution.py:23
  341.1 8.6 %collective-permute-done.49 = bf16[4,32,2048]{2,1,0:T(8,128)(2,1)} collective-permute-done((bf16[4,32,2048]{2,1,0:T(8,128)(2,1)}, bf16[4,32,2048]{2,1,0:T(8,128)(2,1)}, u32[]{:S(2)}, u32[]{:S(2)}) %collective-permute-start.49) | collective-permute-done | bytes 524320 | tf_op jit(solution)/shard_map/ppermute | solution.py:41
  350.9 9.1 %fusion.97 = f32[256,3584]{1,0:T(8,128)} fusion(bf16[256,2048]{1,0:T(8,128)(2,1)S(1)} %bitcast.154, bf16[3584,2048]{1,0:T(8,128)(2,1)} %param.9), kind=kOutput, calls=%fused_computation.203 | convolution fusion | flops 3758096384 | bytes 19398656 | tf_op jit(solution)/shard_map/dot_general | solution.py:23
  360.0 3.0 slice.392
  367.4 9.1 %fusion.96 = f32[256,3584]{1,0:T(8,128)} fusion(bf16[256,2048]{1,0:T(8,128)(2,1)S(1)} %bitcast.151, bf16[3584,2048]{1,0:T(8,128)(2,1)} %param.9), kind=kOutput, calls=%fused_computation.202 | convolution fusion | flops 3758096384 | bytes 19398656 | tf_op jit(solution)/shard_map/dot_general | solution.py:23
  383.7 9.8 %collective-permute-done.45 = bf16[64,3584]{1,0:T(8,128)(2,1)S(1)} collective-permute-done((bf16[64,3584]{1,0:T(8,128)(2,1)S(1)}, bf16[64,3584]{1,0:T(8,128)(2,1)S(1)}, u32[]{:S(2)}, u32[]{:S(2)}) %collective-permute-start.45) | collective-permute-done | bytes 458784 | tf_op jit(solution)/shard_map/ppermute | solution.py:36
  397.4 11.1 %collective-permute-done.55 = bf16[64,3584]{1,0:T(8,128)(2,1)S(1)} collective-permute-done((bf16[64,3584]{1,0:T(8,128)(2,1)S(1)}, bf16[64,3584]{1,0:T(8,128)(2,1)S(1)}, u32[]{:S(2)}, u32[]{:S(2)}) %collective-permute-start.55) | collective-permute-done | bytes 458784 | tf_op jit(solution)/shard_map/ppermute | solution.py:36
  410.9 7.4 %collective-permute-done.51 = bf16[64,3584]{1,0:T(8,128)(2,1)S(1)} collective-permute-done((bf16[64,3584]{1,0:T(8,128)(2,1)S(1)}, bf16[64,3584]{1,0:T(8,128)(2,1)S(1)}, u32[]{:S(2)}, u32[]{:S(2)}) %collective-permute-start.51) | collective-permute-done | bytes 458784 | tf_op jit(solution)/shard_map/ppermute | solution.py:36
  419.5 8.6 %collective-permute-done.56 = bf16[64,3584]{1,0:T(8,128)(2,1)S(1)} collective-permute-done((bf16[64,3584]{1,0:T(8,128)(2,1)S(1)}, bf16[64,3584]{1,0:T(8,128)(2,1)S(1)}, u32[]{:S(2)}, u32[]{:S(2)}) %collective-permute-start.56) | collective-permute-done | bytes 458784 | tf_op jit(solution)/shard_map/ppermute | solution.py:36
  428.3 9.1 %collective-permute-done.52 = bf16[64,3584]{1,0:T(8,128)(2,1)S(1)} collective-permute-done((bf16[64,3584]{1,0:T(8,128)(2,1)S(1)}, bf16[64,3584]{1,0:T(8,128)(2,1)S(1)}, u32[]{:S(2)}, u32[]{:S(2)}) %collective-permute-start.52) | collective-permute-done | bytes 458784 | tf_op jit(solution)/shard_map/ppermute | solution.py:36
  440.2 22.5 %shard_map.64 = f32[2048,3584]{1,0:T(8,128)} custom-call(bf16[2048,256]{1,0:T(8,128)(2,1)S(1)} %bitcast.127, bf16[2048,256]{1,0:T(8,128)(2,1)S(1)} %bitcast.126, bf16[2048,256]{1,0:T(8,128)(2,1)S(1)} %bitcast.129, bf16[2048,256]{1,0:T(8,128)(2,1)S(1)} %bitcast.128, bf16[256,3584]{1,0:T(8,128)(2,1)S(1)} %pad_maximum_fusion.2.refs_4_, ...), custom_call_target="tpu_custom_call" | custom-call | flops 15032385536 | bytes 40894464 | tf_op jit(solution)/shard_map/pallas_call | solution.py:91
  (285 shorter events, 109.7 us)
Async XLA Ops:
  6.5 173.2 %all-gather.7.cloned.1.call-start = ((), (), s32[]{:S(2)}) async-start(), calls=%async_computation.1 | async-start | bytes 2752512 | tf_op jit(solution)/shard_map/all_gather | solution.py:210
  8.7 17.0 %collective-permute-start = (bf16[4,32,2048]{2,1,0:T(8,128)(2,1)S(1)}, bf16[4,32,2048]{2,1,0:T(8,128)(2,1)S(1)}, u32[]{:S(2)}, u32[]{:S(2)}) collective-permute-start(bf16[4,32,2048]{2,1,0:T(8,128)(2,1)S(1)} %pad_maximum_fusion.22), channel_id=1, source_target_pairs={{0,4},{4,8},{8,12},{12,0},{1,5},{5,9},{9,13},{13,1},{2,6},{6,10},{... | collective-permute-start | bytes 1572872 | tf_op jit(solution)/shard_map/ppermute | solution.py:41
  37.0 15.1 %collective-permute-start.3 = (f32[128,3584]{1,0:T(8,128)}, f32[128,3584]{1,0:T(8,128)S(1)}, u32[]{:S(2)}, u32[]{:S(2)}) collective-permute-start(f32[128,3584]{1,0:T(8,128)} %slice.322), channel_id=1, source_target_pairs={{0,1},{1,0},{2,3},{3,2},{4,5},{5,4},{6,7},{7,6},{8,9},{9,8},{10,11... | collective-permute-start | bytes 5505032 | tf_op jit(solution)/shard_map/ppermute | solution.py:36
  41.1 23.1 %collective-permute-start.5 = (bf16[4,32,2048]{2,1,0:T(8,128)(2,1)S(1)}, bf16[4,32,2048]{2,1,0:T(8,128)(2,1)}, u32[]{:S(2)}, u32[]{:S(2)}) collective-permute-start(bf16[4,32,2048]{2,1,0:T(8,128)(2,1)S(1)} %copy-done.40), channel_id=1, source_target_pairs={{0,12},{4,0},{8,4},{12,8},{1,13},{5,1},{9,5},{13,9},{2,14},{6,2},{... | collective-permute-start | bytes 1572872 | tf_op jit(solution)/shard_map/ppermute | solution.py:41
  43.1 34.3 %collective-permute-start.1 = (bf16[4,32,2048]{2,1,0:T(8,128)(2,1)S(1)}, bf16[4,32,2048]{2,1,0:T(8,128)(2,1)}, u32[]{:S(2)}, u32[]{:S(2)}) collective-permute-start(bf16[4,32,2048]{2,1,0:T(8,128)(2,1)S(1)} %copy-done.40), channel_id=1, source_target_pairs={{0,8},{4,12},{8,0},{12,4},{1,9},{5,13},{9,1},{13,5},{2,10},{6,14},... | collective-permute-start | bytes 1572872 | tf_op jit(solution)/shard_map/ppermute | solution.py:41
  43.1 45.5 %collective-permute-start.6 = (bf16[4,32,2048]{2,1,0:T(8,128)(2,1)S(1)}, bf16[4,32,2048]{2,1,0:T(8,128)(2,1)S(1)}, u32[]{:S(2)}, u32[]{:S(2)}) collective-permute-start(bf16[4,32,2048]{2,1,0:T(8,128)(2,1)S(1)} %copy-done.42), channel_id=1, source_target_pairs={{0,16},{16,0},{1,17},{17,1},{2,18},{18,2},{3,19},{19,3},{4,20},{20... | collective-permute-start | bytes 1572872 | tf_op jit(solution)/shard_map/ppermute | solution.py:36
  64.1 23.9 %collective-permute-start.7 = (f32[128,3584]{1,0:T(8,128)S(1)}, f32[128,3584]{1,0:T(8,128)S(1)}, u32[]{:S(2)}, u32[]{:S(2)}) collective-permute-start(f32[128,3584]{1,0:T(8,128)S(1)} %slice.325), channel_id=1, source_target_pairs={{0,1},{1,0},{2,3},{3,2},{4,5},{5,4},{6,7},{7,6},{8,9},{9,8},{10,11... | collective-permute-start | bytes 5505032 | tf_op jit(solution)/shard_map/ppermute | solution.py:36
  64.3 25.9 %collective-permute-start.8 = (f16[64,3584]{1,0:T(8,128)(2,1)S(1)}, f16[64,3584]{1,0:T(8,128)(2,1)S(1)}, u32[]{:S(2)}, u32[]{:S(2)}) collective-permute-start(f16[64,3584]{1,0:T(8,128)(2,1)S(1)} %fusion.58), channel_id=1, source_target_pairs={{0,2},{1,3},{2,0},{3,1},{4,6},{5,7},{6,4},{7,5},{8,10},{9,11},{10,... | collective-permute-start | bytes 1376264 | tf_op jit(solution)/shard_map/ppermute | solution.py:36
  86.1 18.2 %collective-permute-start.11 = (f32[128,3584]{1,0:T(8,128)S(1)}, f32[128,3584]{1,0:T(8,128)S(1)}, u32[]{:S(2)}, u32[]{:S(2)}) collective-permute-start(f32[128,3584]{1,0:T(8,128)S(1)} %slice.333), channel_id=1, source_target_pairs={{0,1},{1,0},{2,3},{3,2},{4,5},{5,4},{6,7},{7,6},{8,9},{9,8},{10,11... | collective-permute-start | bytes 5505032 | tf_op jit(solution)/shard_map/ppermute | solution.py:36
  86.1 62.4 %collective-permute-start.23 = (bf16[4,32,2048]{2,1,0:T(8,128)(2,1)}, bf16[4,32,2048]{2,1,0:T(8,128)(2,1)}, u32[]{:S(2)}, u32[]{:S(2)}) collective-permute-start(bf16[4,32,2048]{2,1,0:T(8,128)(2,1)} %collective-permute-done.1), channel_id=1, source_target_pairs={{0,16},{16,0},{1,17},{17,1},{2,18},{18,2},{3,19},{19,3},{4,20},{20... | collective-permute-start | bytes 1572872 | tf_op jit(solution)/shard_map/ppermute | solution.py:36
  88.0 60.7 %collective-permute-start.24 = (bf16[4,32,2048]{2,1,0:T(8,128)(2,1)}, bf16[4,32,2048]{2,1,0:T(8,128)(2,1)}, u32[]{:S(2)}, u32[]{:S(2)}) collective-permute-start(bf16[4,32,2048]{2,1,0:T(8,128)(2,1)} %collective-permute-done.5), channel_id=1, source_target_pairs={{0,16},{16,0},{1,17},{17,1},{2,18},{18,2},{3,19},{19,3},{4,20},{20... | collective-permute-start | bytes 1572872 | tf_op jit(solution)/shard_map/ppermute | solution.py:36
  99.0 26.9 %collective-permute-start.9 = (f32[128,3584]{1,0:T(8,128)}, f32[128,3584]{1,0:T(8,128)}, u32[]{:S(2)}, u32[]{:S(2)}) collective-permute-start(f32[128,3584]{1,0:T(8,128)} %slice.328), channel_id=1, source_target_pairs={{0,1},{1,0},{2,3},{3,2},{4,5},{5,4},{6,7},{7,6},{8,9},{9,8},{10,11... | collective-permute-start | bytes 5505032 | tf_op jit(solution)/shard_map/ppermute | solution.py:36
  102.8 14.5 %collective-permute-start.16 = (bf16[64,3584]{1,0:T(8,128)(2,1)S(1)}, bf16[64,3584]{1,0:T(8,128)(2,1)}, u32[]{:S(2)}, u32[]{:S(2)}) collective-permute-start(bf16[64,3584]{1,0:T(8,128)(2,1)S(1)} %get-tuple-element.87), channel_id=1, source_target_pairs={{0,2},{1,3},{2,0},{3,1},{4,6},{5,7},{6,4},{7,5},{8,10},{9,11},{10,... | collective-permute-start | bytes 1376264 | tf_op jit(solution)/shard_map/ppermute | solution.py:36
  105.8 19.0 %collective-permute-start.12 = (f16[64,3712]{1,0:T(8,128)(2,1)}, f16[64,3712]{1,0:T(8,128)(2,1)}, u32[]{:S(2)}, u32[]{:S(2)}) collective-permute-start(f16[64,3712]{1,0:T(8,128)(2,1)} %pad_maximum_fusion.25), channel_id=1, source_target_pairs={{0,2},{1,3},{2,0},{3,1},{4,6},{5,7},{6,4},{7,5},{8,10},{9,11},{10,... | collective-permute-start | bytes 1425416 | tf_op jit(solution)/shard_map/ppermute | solution.py:36
  117.2 94.3 %all-gather.5.cloned.1.call-start = ((), (), s32[]{:S(2)}) async-start(), calls=%async_computation | async-start | bytes 2752512 | tf_op jit(solution)/shard_map/all_gather | solution.py:210
  117.3 27.6 %collective-permute-start.14 = (f32[128,3584]{1,0:T(8,128)}, f32[128,3584]{1,0:T(8,128)S(1)}, u32[]{:S(2)}, u32[]{:S(2)}) collective-permute-start(f32[128,3584]{1,0:T(8,128)} %slice.343), channel_id=1, source_target_pairs={{0,1},{1,0},{2,3},{3,2},{4,5},{5,4},{6,7},{7,6},{8,9},{9,8},{10,11... | collective-permute-start | bytes 5505032 | tf_op jit(solution)/shard_map/ppermute | solution.py:36
  127.5 21.9 %collective-permute-start.10 = (f16[64,3584]{1,0:T(8,128)(2,1)S(1)}, f16[64,3584]{1,0:T(8,128)(2,1)S(1)}, u32[]{:S(2)}, u32[]{:S(2)}) collective-permute-start(f16[64,3584]{1,0:T(8,128)(2,1)S(1)} %fusion.54), channel_id=1, source_target_pairs={{0,2},{1,3},{2,0},{3,1},{4,6},{5,7},{6,4},{7,5},{8,10},{9,11},{10,... | collective-permute-start | bytes 1376264 | tf_op jit(solution)/shard_map/ppermute | solution.py:36
  139.2 75.3 %collective-permute-start.21 = (bf16[4,32,2048]{2,1,0:T(8,128)(2,1)}, bf16[4,32,2048]{2,1,0:T(8,128)(2,1)}, u32[]{:S(2)}, u32[]{:S(2)}) collective-permute-start(bf16[4,32,2048]{2,1,0:T(8,128)(2,1)} %get-tuple-element.106), channel_id=1, source_target_pairs={{0,8},{4,12},{8,0},{12,4},{1,9},{5,13},{9,1},{13,5},{2,10},{6,14},... | collective-permute-start | bytes 1572872 | tf_op jit(solution)/shard_map/ppermute | solution.py:41
  144.9 69.6 %collective-permute-start.20 = (bf16[4,32,2048]{2,1,0:T(8,128)(2,1)}, bf16[4,32,2048]{2,1,0:T(8,128)(2,1)}, u32[]{:S(2)}, u32[]{:S(2)}) collective-permute-start(bf16[4,32,2048]{2,1,0:T(8,128)(2,1)} %get-tuple-element.105), channel_id=1, source_target_pairs={{0,12},{4,0},{8,4},{12,8},{1,13},{5,1},{9,5},{13,9},{2,14},{6,2},{... | collective-permute-start | bytes 1572872 | tf_op jit(solution)/shard_map/ppermute | solution.py:41
  148.6 17.4 %collective-permute-start.30 = (f32[128,3584]{1,0:T(8,128)}, f32[128,3584]{1,0:T(8,128)}, u32[]{:S(2)}, u32[]{:S(2)}) collective-permute-start(f32[128,3584]{1,0:T(8,128)} %slice.359), channel_id=1, source_target_pairs={{0,1},{1,0},{2,3},{3,2},{4,5},{5,4},{6,7},{7,6},{8,9},{9,8},{10,11... | collective-permute-start | bytes 5505032 | tf_op jit(solution)/shard_map/ppermute | solution.py:36
  156.2 34.7 %collective-permute-start.25 = (f32[128,3584]{1,0:T(8,128)}, f32[128,3584]{1,0:T(8,128)}, u32[]{:S(2)}, u32[]{:S(2)}) collective-permute-start(f32[128,3584]{1,0:T(8,128)} %slice.363), channel_id=1, source_target_pairs={{0,1},{1,0},{2,3},{3,2},{4,5},{5,4},{6,7},{7,6},{8,9},{9,8},{10,11... | collective-permute-start | bytes 5505032 | tf_op jit(solution)/shard_map/ppermute | solution.py:36
  165.3 13.4 %collective-permute-start.18 = (bf16[64,3584]{1,0:T(8,128)(2,1)S(1)}, bf16[64,3584]{1,0:T(8,128)(2,1)S(1)}, u32[]{:S(2)}, u32[]{:S(2)}) collective-permute-start(bf16[64,3584]{1,0:T(8,128)(2,1)S(1)} %get-tuple-element.85), channel_id=1, source_target_pairs={{0,2},{1,3},{2,0},{3,1},{4,6},{5,7},{6,4},{7,5},{8,10},{9,11},{10,... | collective-permute-start | bytes 1376264 | tf_op jit(solution)/shard_map/ppermute | solution.py:36
  168.3 19.0 %collective-permute-start.31 = (bf16[64,3584]{1,0:T(8,128)(2,1)}, bf16[64,3584]{1,0:T(8,128)(2,1)S(1)}, u32[]{:S(2)}, u32[]{:S(2)}) collective-permute-start(bf16[64,3584]{1,0:T(8,128)(2,1)} %fusion.37), channel_id=1, source_target_pairs={{0,2},{1,3},{2,0},{3,1},{4,6},{5,7},{6,4},{7,5},{8,10},{9,11},{10,... | collective-permute-start | bytes 1376264 | tf_op jit(solution)/shard_map/ppermute | solution.py:36
  179.7 14.1 %collective-permute-start.19 = (bf16[128,3584]{1,0:T(8,128)(2,1)}, bf16[128,3584]{1,0:T(8,128)(2,1)}, u32[]{:S(2)}, u32[]{:S(2)}) collective-permute-start(bf16[128,3584]{1,0:T(8,128)(2,1)} %pad_maximum_fusion.15), channel_id=1, source_target_pairs={{0,1},{1,0},{2,3},{3,2},{4,5},{5,4},{6,7},{7,6},{8,9},{9,8},{10,11... | collective-permute-start | bytes 2752520 | tf_op jit(solution)/shard_map/ppermute | solution.py:36
  190.1 15.3 %collective-permute-start.32 = (bf16[64,3584]{1,0:T(8,128)(2,1)S(1)}, bf16[64,3584]{1,0:T(8,128)(2,1)S(1)}, u32[]{:S(2)}, u32[]{:S(2)}) collective-permute-start(bf16[64,3584]{1,0:T(8,128)(2,1)S(1)} %fusion.40), channel_id=1, source_target_pairs={{0,2},{1,3},{2,0},{3,1},{4,6},{5,7},{6,4},{7,5},{8,10},{9,11},{10,... | collective-permute-start | bytes 1376264 | tf_op jit(solution)/shard_map/ppermute | solution.py:36
  192.4 19.1 %collective-permute-start.26 = (bf16[64,3584]{1,0:T(8,128)(2,1)S(1)}, bf16[64,3584]{1,0:T(8,128)(2,1)}, u32[]{:S(2)}, u32[]{:S(2)}) collective-permute-start(bf16[64,3584]{1,0:T(8,128)(2,1)S(1)} %fusion.41), channel_id=1, source_target_pairs={{0,2},{1,3},{2,0},{3,1},{4,6},{5,7},{6,4},{7,5},{8,10},{9,11},{10,... | collective-permute-start | bytes 1376264 | tf_op jit(solution)/shard_map/ppermute | solution.py:36
  202.5 14.4 %collective-permute-start.22 = (bf16[4,32,2048]{2,1,0:T(8,128)(2,1)}, bf16[4,32,2048]{2,1,0:T(8,128)(2,1)}, u32[]{:S(2)}, u32[]{:S(2)}) collective-permute-start(bf16[4,32,2048]{2,1,0:T(8,128)(2,1)} %fusion.59), channel_id=1, source_target_pairs={{0,4},{4,8},{8,12},{12,0},{1,5},{5,9},{9,13},{13,1},{2,6},{6,10},{... | collective-permute-start | bytes 1572872 | tf_op jit(solution)/shard_map/ppermute | solution.py:41
  206.5 13.5 %collective-permute-start.33 = (bf16[128,3584]{1,0:T(8,128)(2,1)}, bf16[128,3584]{1,0:T(8,128)(2,1)}, u32[]{:S(2)}, u32[]{:S(2)}) collective-permute-start(bf16[128,3584]{1,0:T(8,128)(2,1)} %pad_maximum_fusion.17), channel_id=1, source_target_pairs={{0,1},{1,0},{2,3},{3,2},{4,5},{5,4},{6,7},{7,6},{8,9},{9,8},{10,11... | collective-permute-start | bytes 2752520 | tf_op jit(solution)/shard_map/ppermute | solution.py:36
  213.7 26.2 %collective-permute-start.27 = (bf16[64,3584]{1,0:T(8,128)(2,1)S(1)}, bf16[64,3584]{1,0:T(8,128)(2,1)S(1)}, u32[]{:S(2)}, u32[]{:S(2)}) collective-permute-start(bf16[64,3584]{1,0:T(8,128)(2,1)S(1)} %fusion.44), channel_id=1, source_target_pairs={{0,2},{1,3},{2,0},{3,1},{4,6},{5,7},{6,4},{7,5},{8,10},{9,11},{10,... | collective-permute-start | bytes 1376264 | tf_op jit(solution)/shard_map/ppermute | solution.py:36
  240.7 27.3 %collective-permute-start.38 = (bf16[4,32,2048]{2,1,0:T(8,128)(2,1)S(1)}, bf16[4,32,2048]{2,1,0:T(8,128)(2,1)S(1)}, u32[]{:S(2)}, u32[]{:S(2)}) collective-permute-start(bf16[4,32,2048]{2,1,0:T(8,128)(2,1)S(1)} %copy-done.46), channel_id=1, source_target_pairs={{0,8},{4,12},{8,0},{12,4},{1,9},{5,13},{9,1},{13,5},{2,10},{6,14},... | collective-permute-start | bytes 1572872 | tf_op jit(solution)/shard_map/ppermute | solution.py:41
  242.1 38.9 %collective-permute-start.35 = (bf16[4,32,2048]{2,1,0:T(8,128)(2,1)S(1)}, bf16[4,32,2048]{2,1,0:T(8,128)(2,1)S(1)}, u32[]{:S(2)}, u32[]{:S(2)}) collective-permute-start(bf16[4,32,2048]{2,1,0:T(8,128)(2,1)S(1)} %copy-done.45), channel_id=1, source_target_pairs={{0,12},{4,0},{8,4},{12,8},{1,13},{5,1},{9,5},{13,9},{2,14},{6,2},{... | collective-permute-start | bytes 1572872 | tf_op jit(solution)/shard_map/ppermute | solution.py:41
  253.4 27.6 %collective-permute-start.39 = (bf16[4,32,2048]{2,1,0:T(8,128)(2,1)S(1)}, bf16[4,32,2048]{2,1,0:T(8,128)(2,1)S(1)}, u32[]{:S(2)}, u32[]{:S(2)}) collective-permute-start(bf16[4,32,2048]{2,1,0:T(8,128)(2,1)S(1)} %fusion.60), channel_id=1, source_target_pairs={{0,4},{4,8},{8,12},{12,0},{1,5},{5,9},{9,13},{13,1},{2,6},{6,10},{... | collective-permute-start | bytes 1572872 | tf_op jit(solution)/shard_map/ppermute | solution.py:41
  258.1 22.2 %collective-permute-start.37 = (bf16[64,3584]{1,0:T(8,128)(2,1)S(1)}, bf16[64,3584]{1,0:T(8,128)(2,1)S(1)}, u32[]{:S(2)}, u32[]{:S(2)}) collective-permute-start(bf16[64,3584]{1,0:T(8,128)(2,1)S(1)} %fusion.35), channel_id=1, source_target_pairs={{0,2},{1,3},{2,0},{3,1},{4,6},{5,7},{6,4},{7,5},{8,10},{9,11},{10,... | collective-permute-start | bytes 1376264 | tf_op jit(solution)/shard_map/ppermute | solution.py:36
  258.8 42.1 %collective-permute-start.41 = (bf16[4,32,2048]{2,1,0:T(8,128)(2,1)}, bf16[4,32,2048]{2,1,0:T(8,128)(2,1)}, u32[]{:S(2)}, u32[]{:S(2)}) collective-permute-start(bf16[4,32,2048]{2,1,0:T(8,128)(2,1)} %fusion.20), channel_id=1, source_target_pairs={{0,4},{4,8},{8,12},{12,0},{1,5},{5,9},{9,13},{13,1},{2,6},{6,10},{... | collective-permute-start | bytes 1572872 | tf_op jit(solution)/shard_map/ppermute | solution.py:41
  268.1 32.8 %collective-permute-start.42 = (bf16[4,32,2048]{2,1,0:T(8,128)(2,1)}, bf16[4,32,2048]{2,1,0:T(8,128)(2,1)}, u32[]{:S(2)}, u32[]{:S(2)}) collective-permute-start(bf16[4,32,2048]{2,1,0:T(8,128)(2,1)} %collective-permute-done.29), channel_id=1, source_target_pairs={{0,12},{4,0},{8,4},{12,8},{1,13},{5,1},{9,5},{13,9},{2,14},{6,2},{... | collective-permute-start | bytes 1572872 | tf_op jit(solution)/shard_map/ppermute | solution.py:41
  282.2 31.9 %collective-permute-start.47 = (bf16[4,32,2048]{2,1,0:T(8,128)(2,1)}, bf16[4,32,2048]{2,1,0:T(8,128)(2,1)}, u32[]{:S(2)}, u32[]{:S(2)}) collective-permute-start(bf16[4,32,2048]{2,1,0:T(8,128)(2,1)} %fusion.15), channel_id=1, source_target_pairs={{0,12},{4,0},{8,4},{12,8},{1,13},{5,1},{9,5},{13,9},{2,14},{6,2},{... | collective-permute-start | bytes 1572872 | tf_op jit(solution)/shard_map/ppermute | solution.py:41
  314.1 26.9 %collective-permute-start.48 = (bf16[4,32,2048]{2,1,0:T(8,128)(2,1)}, bf16[4,32,2048]{2,1,0:T(8,128)(2,1)}, u32[]{:S(2)}, u32[]{:S(2)}) collective-permute-start(bf16[4,32,2048]{2,1,0:T(8,128)(2,1)} %fusion.15), channel_id=1, source_target_pairs={{0,4},{4,8},{8,12},{12,0},{1,5},{5,9},{9,13},{13,1},{2,6},{6,10},{... | collective-permute-start | bytes 1572872 | tf_op jit(solution)/shard_map/ppermute | solution.py:41
  323.6 26.0 %collective-permute-start.49 = (bf16[4,32,2048]{2,1,0:T(8,128)(2,1)}, bf16[4,32,2048]{2,1,0:T(8,128)(2,1)}, u32[]{:S(2)}, u32[]{:S(2)}) collective-permute-start(bf16[4,32,2048]{2,1,0:T(8,128)(2,1)} %collective-permute-done.47), channel_id=1, source_target_pairs={{0,12},{4,0},{8,4},{12,8},{1,13},{5,1},{9,5},{13,9},{2,14},{6,2},{... | collective-permute-start | bytes 1572872 | tf_op jit(solution)/shard_map/ppermute | solution.py:41
  335.3 29.1 %collective-permute-start.43 = (f32[128,3584]{1,0:T(8,128)}, f32[128,3584]{1,0:T(8,128)}, u32[]{:S(2)}, u32[]{:S(2)}) collective-permute-start(f32[128,3584]{1,0:T(8,128)} %slice.382), channel_id=1, source_target_pairs={{0,1},{1,0},{2,3},{3,2},{4,5},{5,4},{6,7},{7,6},{8,9},{9,8},{10,11... | collective-permute-start | bytes 5505032 | tf_op jit(solution)/shard_map/ppermute | solution.py:36
  341.1 41.1 %collective-permute-start.40 = (bf16[128,3584]{1,0:T(8,128)(2,1)}, bf16[128,3584]{1,0:T(8,128)(2,1)}, u32[]{:S(2)}, u32[]{:S(2)}) collective-permute-start(bf16[128,3584]{1,0:T(8,128)(2,1)} %pad_maximum_fusion.18), channel_id=1, source_target_pairs={{0,1},{1,0},{2,3},{3,2},{4,5},{5,4},{6,7},{7,6},{8,9},{9,8},{10,11... | collective-permute-start | bytes 2752520 | tf_op jit(solution)/shard_map/ppermute | solution.py:36
  363.1 30.6 %collective-permute-start.54 = (f32[128,3584]{1,0:T(8,128)}, f32[128,3584]{1,0:T(8,128)}, u32[]{:S(2)}, u32[]{:S(2)}) collective-permute-start(f32[128,3584]{1,0:T(8,128)} %slice.392), channel_id=1, source_target_pairs={{0,1},{1,0},{2,3},{3,2},{4,5},{5,4},{6,7},{7,6},{8,9},{9,8},{10,11... | collective-permute-start | bytes 5505032 | tf_op jit(solution)/shard_map/ppermute | solution.py:36
  366.5 13.2 %collective-permute-start.44 = (bf16[64,3584]{1,0:T(8,128)(2,1)}, bf16[64,3584]{1,0:T(8,128)(2,1)}, u32[]{:S(2)}, u32[]{:S(2)}) collective-permute-start(bf16[64,3584]{1,0:T(8,128)(2,1)} %fusion.29), channel_id=1, source_target_pairs={{0,2},{1,3},{2,0},{3,1},{4,6},{5,7},{6,4},{7,5},{8,10},{9,11},{10,... | collective-permute-start | bytes 1376264 | tf_op jit(solution)/shard_map/ppermute | solution.py:36
  378.2 17.8 %collective-permute-start.50 = (f32[128,3584]{1,0:T(8,128)S(1)}, f32[128,3584]{1,0:T(8,128)S(1)}, u32[]{:S(2)}, u32[]{:S(2)}) collective-permute-start(f32[128,3584]{1,0:T(8,128)S(1)} %slice.387), channel_id=1, source_target_pairs={{0,1},{1,0},{2,3},{3,2},{4,5},{5,4},{6,7},{7,6},{8,9},{9,8},{10,11... | collective-permute-start | bytes 5505032 | tf_op jit(solution)/shard_map/ppermute | solution.py:36
  393.5 44.0 %collective-permute-start.46 = (bf16[128,3584]{1,0:T(8,128)(2,1)S(1)}, bf16[128,3584]{1,0:T(8,128)(2,1)S(1)}, u32[]{:S(2)}, u32[]{:S(2)}) collective-permute-start(bf16[128,3584]{1,0:T(8,128)(2,1)S(1)} %pad_maximum_fusion.19), channel_id=1, source_target_pairs={{0,1},{1,0},{2,3},{3,2},{4,5},{5,4},{6,7},{7,6},{8,9},{9,8},{10,11... | collective-permute-start | bytes 2752520 | tf_op jit(solution)/shard_map/ppermute | solution.py:36
  395.1 13.4 %collective-permute-start.55 = (bf16[64,3584]{1,0:T(8,128)(2,1)S(1)}, bf16[64,3584]{1,0:T(8,128)(2,1)S(1)}, u32[]{:S(2)}, u32[]{:S(2)}) collective-permute-start(bf16[64,3584]{1,0:T(8,128)(2,1)S(1)} %fusion.21), channel_id=1, source_target_pairs={{0,2},{1,3},{2,0},{3,1},{4,6},{5,7},{6,4},{7,5},{8,10},{9,11},{10,... | collective-permute-start | bytes 1376264 | tf_op jit(solution)/shard_map/ppermute | solution.py:36
  396.2 22.1 %collective-permute-start.51 = (bf16[64,3584]{1,0:T(8,128)(2,1)S(1)}, bf16[64,3584]{1,0:T(8,128)(2,1)S(1)}, u32[]{:S(2)}, u32[]{:S(2)}) collective-permute-start(bf16[64,3584]{1,0:T(8,128)(2,1)S(1)} %fusion.25), channel_id=1, source_target_pairs={{0,2},{1,3},{2,0},{3,1},{4,6},{5,7},{6,4},{7,5},{8,10},{9,11},{10,... | collective-permute-start | bytes 1376264 | tf_op jit(solution)/shard_map/ppermute | solution.py:36
  409.9 18.2 %collective-permute-start.56 = (bf16[64,3584]{1,0:T(8,128)(2,1)S(1)}, bf16[64,3584]{1,0:T(8,128)(2,1)S(1)}, u32[]{:S(2)}, u32[]{:S(2)}) collective-permute-start(bf16[64,3584]{1,0:T(8,128)(2,1)S(1)} %fusion.24), channel_id=1, source_target_pairs={{0,2},{1,3},{2,0},{3,1},{4,6},{5,7},{6,4},{7,5},{8,10},{9,11},{10,... | collective-permute-start | bytes 1376264 | tf_op jit(solution)/shard_map/ppermute | solution.py:36
  418.6 18.9 %collective-permute-start.52 = (bf16[64,3584]{1,0:T(8,128)(2,1)S(1)}, bf16[64,3584]{1,0:T(8,128)(2,1)S(1)}, u32[]{:S(2)}, u32[]{:S(2)}) collective-permute-start(bf16[64,3584]{1,0:T(8,128)(2,1)S(1)} %fusion.28), channel_id=1, source_target_pairs={{0,2},{1,3},{2,0},{3,1},{4,6},{5,7},{6,4},{7,5},{8,10},{9,11},{10,... | collective-permute-start | bytes 1376264 | tf_op jit(solution)/shard_map/ppermute | solution.py:36
  (66 other events, 525.8 us)
Sparse Core Ops, SparseCore 0:
  117.4 31.4 all-gather.6
  166.1 30.6 all-gather.4

commit v11 on v10

--- a/solution.py
+++ b/solution.py
@@ -230,7 +230,7 @@
         cut = ring // 4
         for k in reversed(range(cut, last)):
             pieces[k] = shift(pieces[k + 1], "row", -1)
-        piece = tie(pieces[last], [pieces[steps[-1][0]]])
+        piece = pieces[last]
         for k in range(cut):
             pieces[k] = piece = shift(piece, "row")
         return pieces
@@ -267,13 +267,16 @@
 
     hidden = [hidden_rows(1, j, []) for j in range(GROUPS)]
     ready = [out_sums(1, j, hidden[j][0], []) for j in range(tail)]
-    first, sent, got, near = back(0, tail, pieces, ready)
+    first, sent, got, near = back(0, tail, pieces, ready + pieces[:1])
     ready = [out_sums(1, tail, hidden[tail][0], sent)]
     others = scaled_pieces(1, near)
+    after = ready + got + others[last:]
     for j in reversed(range(tail)):
-        back(0, j, pieces, ready + got + others[last:])
+        _, _, after, near = back(0, j, pieces, after)
+    after = after + others[:1]
     for j in reversed(range(GROUPS)):
-        back(1, j, others, others)
+        _, after, _, _ = back(1, j, others, after)
+        after = after + near
     return last_product(turned, bars, tokens)
 
 

time: 473 us -> 467 us (0.987)
  waiting for transfers between devices: 153 us -> 170 us
  starting transfers between devices: 79.5 us -> 63.1 us
    ppermute x15, waiting for transfers between devices: 61.1 us -> 87.6 us  [shift(): lax.ppermute(values, axis, [(i, (i + by) % count) for i in range(count)])]
    ppermute x15, starting transfers between devices: 53.8 us -> 34.2 us  [shift(): lax.ppermute(values, axis, [(i, (i + by) % count) for i in range(count)])]
    ppermute x43, waiting for transfers between devices: 92.1 us -> 82.4 us  [swap(): return lax.ppermute(values, axis, [(i, i ^ mask) for i in range(count)])]
    unnamed x108 -> x116, local copies, waits for them, and re-layouts: 9.73 us -> 10.7 us
  transfers between devices with their start and end apart: 60 -> 60, of which waited for: 24 -> 27; matrix products, arithmetic and copies ran while one was open for 38% -> 33% of each run, Pallas kernels for 0% -> 0%
where the time goes in v11:
time: 467 us; the launch traced here: 463 us
  waiting for transfers between devices  170 us (36%)
  matrix products  115 us (25%)
  starting transfers between devices  63.1 us (14%)
  other arithmetic  43.3 us (9%)
  local copies, waits for them, and re-layouts  34 us (7%)
  Pallas kernels  22.5 us (5%)
  between operations  14.9 us (3%)
    ppermute x15, waiting for transfers between devices, shift(): lax.ppermute(values, axis, [(i, (i + by) % count) for i in range(count)])  87.6 us
    dot_general x12, matrix products, matmul(): return jnp.dot(left, right, preferred_element_type=jnp.float32)  83.8 us
    ppermute x43, waiting for transfers between devices, swap(): return lax.ppermute(values, axis, [(i, i ^ mask) for i in range(count)])  82.4 us
    ppermute x15, starting transfers between devices, shift(): lax.ppermute(values, axis, [(i, (i + by) % count) for i in range(count)])  34.2 us
    dot_general x4, matrix products, times_down(): lax.dot_general(left, w_down, (((1,), (1,)), ((), ())), preferred_element...  31.3 us
    ppermute x43, starting transfers between devices, swap(): return lax.ppermute(values, axis, [(i, i ^ mask) for i in range(count)])  28.9 us
    pallas_call x1, Pallas kernels, last_product(): pl.pallas_call(functools.partial(last_kernel, 1.0 / tokens, len(turned)),...  22.5 us
    slice x12, local copies, waits for them, and re-layouts, sum_over_col(): first = part[half:]  11 us
  transfers between devices with their start and end apart: 60, of which 27 were waited for; matrix products, arithmetic and copies ran while one was open for 33% of the time, Pallas kernels for 0%

profile of v11, /device:TPU:0, one launch (start us, length us, event | category | flops | bytes accessed | tf_op | source)
XLA Modules:
  0.0 462.8 jit_solution(3152029488110139089)
XLA Ops:
  8.0 3.1 collective-permute-start
  11.1 13.9 %collective-permute-done = bf16[4,32,2048]{2,1,0:T(8,128)(2,1)S(1)} collective-permute-done((bf16[4,32,2048]{2,1,0:T(8,128)(2,1)S(1)}, bf16[4,32,2048]{2,1,0:T(8,128)(2,1)S(1)}, u32[]{:S(2)}, u32[]{:S(2)}) %collective-permute-start) | collective-permute-done | bytes 524320 | tf_op jit(solution)/shard_map/ppermute | solution.py:41
  25.8 7.2 %fusion.86 = f32[256,3584]{1,0:T(8,128)S(1)} fusion(bf16[256,2048]{1,0:T(8,128)(2,1)S(1)} %bitcast.130, bf16[2048,3584]{1,0:T(8,128)(2,1)} %param.8), kind=kOutput, calls=%fused_computation.192 | convolution fusion | flops 3758096384 | bytes 19398656 | tf_op jit(solution)/shard_map/dot_general | solution.py:19
  36.4 2.9 dynamic-slice_bitcast_fusion.3
  42.8 7.2 %fusion.85 = f32[256,3584]{1,0:T(8,128)S(1)} fusion(bf16[256,2048]{1,0:T(8,128)(2,1)S(1)} %bitcast.131, bf16[2048,3584]{1,0:T(8,128)(2,1)} %param.7), kind=kOutput, calls=%fused_computation.191 | convolution fusion | flops 3758096384 | bytes 19398656 | tf_op jit(solution)/shard_map/dot_general | solution.py:19
  56.8 7.2 %fusion.87 = f32[256,3584]{1,0:T(8,128)S(1)} fusion(bf16[256,2048]{1,0:T(8,128)(2,1)S(1)} %bitcast.132, bf16[2048,3584]{1,0:T(8,128)(2,1)} %param.10), kind=kOutput, calls=%fused_computation.193 | convolution fusion | flops 3758096384 | bytes 19398656 | tf_op jit(solution)/shard_map/dot_general | solution.py:19
  65.0 3.3 collective-permute-done.4
  68.3 7.3 %collective-permute-done.1 = bf16[4,32,2048]{2,1,0:T(8,128)(2,1)} collective-permute-done((bf16[4,32,2048]{2,1,0:T(8,128)(2,1)S(1)}, bf16[4,32,2048]{2,1,0:T(8,128)(2,1)}, u32[]{:S(2)}, u32[]{:S(2)}) %collective-permute-start.1) | collective-permute-done | bytes 524320 | tf_op jit(solution)/shard_map/ppermute | solution.py:41
  76.9 7.3 %fusion.89 = f32[256,3584]{1,0:T(8,128)S(1)} fusion(bf16[256,2048]{1,0:T(8,128)(2,1)S(1)} %bitcast.134, bf16[2048,3584]{1,0:T(8,128)(2,1)} %param.8), kind=kOutput, calls=%fused_computation.195 | convolution fusion | flops 3758096384 | bytes 19398656 | tf_op jit(solution)/shard_map/dot_general | solution.py:19
  88.4 7.2 %fusion.88 = f32[256,3584]{1,0:T(8,128)S(1)} fusion(bf16[256,2048]{1,0:T(8,128)(2,1)S(1)} %bitcast.135, bf16[2048,3584]{1,0:T(8,128)(2,1)} %param.7), kind=kOutput, calls=%fused_computation.194 | convolution fusion | flops 3758096384 | bytes 19398656 | tf_op jit(solution)/shard_map/dot_general | solution.py:19
  99.4 2.8 multiply_convert_fusion.1
  105.7 7.6 %fusion.90 = f32[256,3584]{1,0:T(8,128)S(1)} fusion(bf16[256,2048]{1,0:T(8,128)(2,1)S(1)} %bitcast.136, bf16[2048,3584]{1,0:T(8,128)(2,1)} %param.10), kind=kOutput, calls=%fused_computation.196 | convolution fusion | flops 3758096384 | bytes 19398656 | tf_op jit(solution)/shard_map/dot_general | solution.py:19
  116.8 7.2 %collective-permute-done.12 = f16[64,3712]{1,0:T(8,128)(2,1)} collective-permute-done((f16[64,3712]{1,0:T(8,128)(2,1)}, f16[64,3712]{1,0:T(8,128)(2,1)}, u32[]{:S(2)}, u32[]{:S(2)}) %collective-permute-start.12) | collective-permute-done | bytes 475168 | tf_op jit(solution)/shard_map/ppermute | solution.py:36
  128.6 7.7 %convolution_convert_fusion.1 = bf16[256,2048]{1,0:T(8,128)(2,1)S(1)} fusion(bf16[256,3584]{1,0:T(8,128)(2,1)S(1)} %pad_maximum_fusion, bf16[3584,2048]{1,0:T(8,128)(2,1)} %param.9), kind=kOutput, calls=%fused_computation.1 | convolution fusion | flops 3758620672 | bytes 17563648 | tf_op jit(solution)/shard_map/dot_general | solution.py:19
  138.5 3.9 fusion.91
  143.9 3.6 collective-permute-start.20
  149.6 3.9 fusion.92
  155.2 5.4 %collective-permute-done.15 = bf16[64,3584]{1,0:T(8,128)(2,1)S(1)} collective-permute-done((bf16[64,3584]{1,0:T(8,128)(2,1)S(1)}, bf16[64,3584]{1,0:T(8,128)(2,1)S(1)}, u32[]{:S(2)}, u32[]{:S(2)}) %collective-permute-start.15) | collective-permute-done | bytes 458784 | tf_op jit(solution)/shard_map/ppermute | solution.py:36
  160.8 3.5 multiply_convert_fusion
  164.9 2.4 fusion.37
  168.7 9.0 %collective-permute-done.18 = bf16[64,3584]{1,0:T(8,128)(2,1)S(1)} collective-permute-done((bf16[64,3584]{1,0:T(8,128)(2,1)S(1)}, bf16[64,3584]{1,0:T(8,128)(2,1)S(1)}, u32[]{:S(2)}, u32[]{:S(2)}) %collective-permute-start.18) | collective-permute-done | bytes 458784 | tf_op jit(solution)/shard_map/ppermute | solution.py:36
  178.7 7.6 %collective-permute-done.31 = bf16[64,3584]{1,0:T(8,128)(2,1)S(1)} collective-permute-done((bf16[64,3584]{1,0:T(8,128)(2,1)}, bf16[64,3584]{1,0:T(8,128)(2,1)S(1)}, u32[]{:S(2)}, u32[]{:S(2)}) %collective-permute-start.31) | collective-permute-done | bytes 458784 | tf_op jit(solution)/shard_map/ppermute | solution.py:36
  192.9 7.7 %fusion = f32[256,2048]{1,0:T(8,128)S(1)} fusion(bf16[3584,2048]{1,0:T(8,128)(2,1)} %param.9, bf16[128,3584]{1,0:T(8,128)(2,1)} %collective-permute-done.19, bf16[64,3584]{1,0:T(8,128)(2,1)S(1)} %collective-permute-done.18, bf16[64,3584]{1,0:T(8,128)(2,1)S(1)} %get-tuple-element.81), kind=kOutput, calls=%fused_computation.3 | convolution fusion | flops 3763601408 | bytes 18612224 | tf_op jit(solution)/shard_map/dot_general | solution.py:19
  204.9 5.7 %collective-permute-done.26 = bf16[64,3584]{1,0:T(8,128)(2,1)} collective-permute-done((bf16[64,3584]{1,0:T(8,128)(2,1)S(1)}, bf16[64,3584]{1,0:T(8,128)(2,1)}, u32[]{:S(2)}, u32[]{:S(2)}) %collective-permute-start.26) | collective-permute-done | bytes 458784 | tf_op jit(solution)/shard_map/ppermute | solution.py:36
  213.4 2.5 collective-permute-done.22
  218.0 3.6 collective-permute-start.29
  221.6 9.4 %convolution_convert_fusion = bf16[256,2048]{1,0:T(8,128)(2,1)S(1)} fusion(bf16[3584,2048]{1,0:T(8,128)(2,1)} %param.9, bf16[128,3584]{1,0:T(8,128)(2,1)} %collective-permute-done.33, bf16[64,3584]{1,0:T(8,128)(2,1)S(1)} %copy-done.50, bf16[64,3584]{1,0:T(8,128)(2,1)S(1)} %fusion.40), kind=kOutput, calls=%fused_computation | convolution fusion | flops 3764125696 | bytes 17563648 | tf_op jit(solution)/shard_map/dot_general | solution.py:19
  232.1 2.4 collective-permute-done.34
  235.2 5.2 %collective-permute-done.29 = bf16[4,32,2048]{2,1,0:T(8,128)(2,1)S(1)} collective-permute-done((bf16[4,32,2048]{2,1,0:T(8,128)(2,1)S(1)}, bf16[4,32,2048]{2,1,0:T(8,128)(2,1)S(1)}, u32[]{:S(2)}, u32[]{:S(2)}) %collective-permute-start.29) | collective-permute-done | bytes 524320 | tf_op jit(solution)/shard_map/ppermute | solution.py:41
  240.5 7.3 %fusion.93 = f32[256,3584]{1,0:T(8,128)S(1)} fusion(bf16[256,2048]{1,0:T(8,128)(2,1)S(1)} %bitcast.154, bf16[3584,2048]{1,0:T(8,128)(2,1)} %param.9), kind=kOutput, calls=%fused_computation.199 | convolution fusion | flops 3758096384 | bytes 19398656 | tf_op jit(solution)/shard_map/dot_general | solution.py:23
  254.3 7.2 %fusion.94 = f32[256,2048]{1,0:T(8,128)S(1)} fusion(bf16[256,3584]{1,0:T(8,128)(2,1)S(1)} %pad_maximum_fusion.1, bf16[3584,2048]{1,0:T(8,128)(2,1)} %param.9), kind=kOutput, calls=%fused_computation.200 | convolution fusion | flops 3758096384 | bytes 18612224 | tf_op jit(solution)/shard_map/dot_general | solution.py:19
  262.0 4.0 collective-permute-done.37
  269.2 6.6 %collective-permute-done.39 = bf16[4,32,2048]{2,1,0:T(8,128)(2,1)S(1)} collective-permute-done((bf16[4,32,2048]{2,1,0:T(8,128)(2,1)S(1)}, bf16[4,32,2048]{2,1,0:T(8,128)(2,1)S(1)}, u32[]{:S(2)}, u32[]{:S(2)}) %collective-permute-start.39) | collective-permute-done | bytes 524320 | tf_op jit(solution)/shard_map/ppermute | solution.py:41
  278.0 10.2 %collective-permute-done.36 = bf16[4,32,2048]{2,1,0:T(8,128)(2,1)S(1)} collective-permute-done((bf16[4,32,2048]{2,1,0:T(8,128)(2,1)S(1)}, bf16[4,32,2048]{2,1,0:T(8,128)(2,1)S(1)}, u32[]{:S(2)}, u32[]{:S(2)}) %collective-permute-start.36) | collective-permute-done | bytes 524320 | tf_op jit(solution)/shard_map/ppermute | solution.py:41
  288.5 9.7 %collective-permute-done.42 = bf16[4,32,2048]{2,1,0:T(8,128)(2,1)S(1)} collective-permute-done((bf16[4,32,2048]{2,1,0:T(8,128)(2,1)S(1)}, bf16[4,32,2048]{2,1,0:T(8,128)(2,1)S(1)}, u32[]{:S(2)}, u32[]{:S(2)}) %collective-permute-start.42) | collective-permute-done | bytes 524320 | tf_op jit(solution)/shard_map/ppermute | solution.py:41
  298.4 7.5 %fusion.95 = f32[256,3584]{1,0:T(8,128)S(1)} fusion(bf16[256,2048]{1,0:T(8,128)(2,1)S(1)} %bitcast.152, bf16[3584,2048]{1,0:T(8,128)(2,1)} %param.9), kind=kOutput, calls=%fused_computation.201 | convolution fusion | flops 3758096384 | bytes 19398656 | tf_op jit(solution)/shard_map/dot_general | solution.py:23
  306.1 10.6 %collective-permute-start.48 = (bf16[4,32,2048]{2,1,0:T(8,128)(2,1)S(1)}, bf16[4,32,2048]{2,1,0:T(8,128)(2,1)S(1)}, u32[]{:S(2)}, u32[]{:S(2)}) collective-permute-start(bf16[4,32,2048]{2,1,0:T(8,128)(2,1)S(1)} %fusion.15), channel_id=1, source_target_pairs={{0,4},{4,8},{8,12},{12,0},{1,5},{5,9},{9,13},{13,1},{2,6},{6,10},{... | collective-permute-start | bytes 1572872 | tf_op jit(solution)/shard_map/ppermute | solution.py:41
  320.1 11.3 %collective-permute-done.48 = bf16[4,32,2048]{2,1,0:T(8,128)(2,1)S(1)} collective-permute-done((bf16[4,32,2048]{2,1,0:T(8,128)(2,1)S(1)}, bf16[4,32,2048]{2,1,0:T(8,128)(2,1)S(1)}, u32[]{:S(2)}, u32[]{:S(2)}) %collective-permute-start.48) | collective-permute-done | bytes 524320 | tf_op jit(solution)/shard_map/ppermute | solution.py:41
  331.5 10.9 %collective-permute-done.47 = bf16[4,32,2048]{2,1,0:T(8,128)(2,1)S(1)} collective-permute-done((bf16[4,32,2048]{2,1,0:T(8,128)(2,1)S(1)}, bf16[4,32,2048]{2,1,0:T(8,128)(2,1)S(1)}, u32[]{:S(2)}, u32[]{:S(2)}) %collective-permute-start.47) | collective-permute-done | bytes 524320 | tf_op jit(solution)/shard_map/ppermute | solution.py:41
  343.2 9.1 %fusion.96 = f32[256,3584]{1,0:T(8,128)} fusion(bf16[256,2048]{1,0:T(8,128)(2,1)S(1)} %bitcast.155, bf16[3584,2048]{1,0:T(8,128)(2,1)} %param.9), kind=kOutput, calls=%fused_computation.202 | convolution fusion | flops 3758096384 | bytes 19398656 | tf_op jit(solution)/shard_map/dot_general | solution.py:23
  359.3 2.8 fusion.25
  362.0 7.5 %collective-permute-done.53 = bf16[4,32,2048]{2,1,0:T(8,128)(2,1)S(1)} collective-permute-done((bf16[4,32,2048]{2,1,0:T(8,128)(2,1)S(1)}, bf16[4,32,2048]{2,1,0:T(8,128)(2,1)S(1)}, u32[]{:S(2)}, u32[]{:S(2)}) %collective-permute-start.53) | collective-permute-done | bytes 524320 | tf_op jit(solution)/shard_map/ppermute | solution.py:41
  370.2 7.3 %fusion.97 = f32[256,3584]{1,0:T(8,128)S(1)} fusion(bf16[256,2048]{1,0:T(8,128)(2,1)S(1)} %bitcast.153, bf16[3584,2048]{1,0:T(8,128)(2,1)} %param.9), kind=kOutput, calls=%fused_computation.203 | convolution fusion | flops 3758096384 | bytes 19398656 | tf_op jit(solution)/shard_map/dot_general | solution.py:23
  391.7 10.2 %collective-permute-done.50 = bf16[64,3584]{1,0:T(8,128)(2,1)S(1)} collective-permute-done((bf16[64,3584]{1,0:T(8,128)(2,1)}, bf16[64,3584]{1,0:T(8,128)(2,1)S(1)}, u32[]{:S(2)}, u32[]{:S(2)}) %collective-permute-start.50) | collective-permute-done | bytes 458784 | tf_op jit(solution)/shard_map/ppermute | solution.py:36
  404.9 6.8 %collective-permute-done.55 = bf16[64,3584]{1,0:T(8,128)(2,1)S(1)} collective-permute-done((bf16[64,3584]{1,0:T(8,128)(2,1)S(1)}, bf16[64,3584]{1,0:T(8,128)(2,1)S(1)}, u32[]{:S(2)}, u32[]{:S(2)}) %collective-permute-start.55) | collective-permute-done | bytes 458784 | tf_op jit(solution)/shard_map/ppermute | solution.py:36
  414.7 6.8 %collective-permute-done.51 = bf16[64,3584]{1,0:T(8,128)(2,1)S(1)} collective-permute-done((bf16[64,3584]{1,0:T(8,128)(2,1)S(1)}, bf16[64,3584]{1,0:T(8,128)(2,1)S(1)}, u32[]{:S(2)}, u32[]{:S(2)}) %collective-permute-start.51) | collective-permute-done | bytes 458784 | tf_op jit(solution)/shard_map/ppermute | solution.py:36
  421.7 8.8 %collective-permute-done.56 = bf16[64,3584]{1,0:T(8,128)(2,1)S(1)} collective-permute-done((bf16[64,3584]{1,0:T(8,128)(2,1)S(1)}, bf16[64,3584]{1,0:T(8,128)(2,1)S(1)}, u32[]{:S(2)}, u32[]{:S(2)}) %collective-permute-start.56) | collective-permute-done | bytes 458784 | tf_op jit(solution)/shard_map/ppermute | solution.py:36
  433.3 22.5 %shard_map.64 = f32[2048,3584]{1,0:T(8,128)} custom-call(bf16[2048,256]{1,0:T(8,128)(2,1)S(1)} %bitcast.127, bf16[2048,256]{1,0:T(8,128)(2,1)S(1)} %bitcast.126, bf16[2048,256]{1,0:T(8,128)(2,1)S(1)} %bitcast.129, bf16[2048,256]{1,0:T(8,128)(2,1)S(1)} %bitcast.128, bf16[256,3584]{1,0:T(8,128)(2,1)S(1)} %pad_maximum_fusion.2.refs_4_, ...), custom_call_target="tpu_custom_call" | custom-call | flops 15032385536 | bytes 40894464 | tf_op jit(solution)/shard_map/pallas_call | solution.py:91
  (293 shorter events, 112.7 us)
Async XLA Ops:
  6.5 172.2 %all-gather.7.cloned.1.call-start = ((), (), s32[]{:S(2)}) async-start(), calls=%async_computation.1 | async-start | bytes 2752512 | tf_op jit(solution)/shard_map/all_gather | solution.py:210
  8.0 17.0 %collective-permute-start = (bf16[4,32,2048]{2,1,0:T(8,128)(2,1)S(1)}, bf16[4,32,2048]{2,1,0:T(8,128)(2,1)S(1)}, u32[]{:S(2)}, u32[]{:S(2)}) collective-permute-start(bf16[4,32,2048]{2,1,0:T(8,128)(2,1)S(1)} %pad_maximum_fusion.22), channel_id=1, source_target_pairs={{0,4},{4,8},{8,12},{12,0},{1,5},{5,9},{9,13},{13,1},{2,6},{6,10},{... | collective-permute-start | bytes 1572872 | tf_op jit(solution)/shard_map/ppermute | solution.py:41
  36.3 14.0 %collective-permute-start.3 = (f32[128,3584]{1,0:T(8,128)}, f32[128,3584]{1,0:T(8,128)}, u32[]{:S(2)}, u32[]{:S(2)}) collective-permute-start(f32[128,3584]{1,0:T(8,128)} %slice.322), channel_id=1, source_target_pairs={{0,1},{1,0},{2,3},{3,2},{4,5},{5,4},{6,7},{7,6},{8,9},{9,8},{10,11... | collective-permute-start | bytes 5505032 | tf_op jit(solution)/shard_map/ppermute | solution.py:36
  39.4 25.0 %collective-permute-start.5 = (bf16[4,32,2048]{2,1,0:T(8,128)(2,1)S(1)}, bf16[4,32,2048]{2,1,0:T(8,128)(2,1)}, u32[]{:S(2)}, u32[]{:S(2)}) collective-permute-start(bf16[4,32,2048]{2,1,0:T(8,128)(2,1)S(1)} %pad_maximum_fusion.22), channel_id=1, source_target_pairs={{0,12},{4,0},{8,4},{12,8},{1,13},{5,1},{9,5},{13,9},{2,14},{6,2},{... | collective-permute-start | bytes 1572872 | tf_op jit(solution)/shard_map/ppermute | solution.py:41
  41.3 34.3 %collective-permute-start.1 = (bf16[4,32,2048]{2,1,0:T(8,128)(2,1)S(1)}, bf16[4,32,2048]{2,1,0:T(8,128)(2,1)}, u32[]{:S(2)}, u32[]{:S(2)}) collective-permute-start(bf16[4,32,2048]{2,1,0:T(8,128)(2,1)S(1)} %pad_maximum_fusion.22), channel_id=1, source_target_pairs={{0,8},{4,12},{8,0},{12,4},{1,9},{5,13},{9,1},{13,5},{2,10},{6,14},... | collective-permute-start | bytes 1572872 | tf_op jit(solution)/shard_map/ppermute | solution.py:41
  41.3 45.5 %collective-permute-start.6 = (bf16[4,32,2048]{2,1,0:T(8,128)(2,1)S(1)}, bf16[4,32,2048]{2,1,0:T(8,128)(2,1)S(1)}, u32[]{:S(2)}, u32[]{:S(2)}) collective-permute-start(bf16[4,32,2048]{2,1,0:T(8,128)(2,1)S(1)} %copy-done.38), channel_id=1, source_target_pairs={{0,16},{16,0},{1,17},{17,1},{2,18},{18,2},{3,19},{19,3},{4,20},{20... | collective-permute-start | bytes 1572872 | tf_op jit(solution)/shard_map/ppermute | solution.py:36
  50.2 13.9 %collective-permute-start.2 = (f32[128,3584]{1,0:T(8,128)S(1)}, f32[128,3584]{1,0:T(8,128)S(1)}, u32[]{:S(2)}, u32[]{:S(2)}) collective-permute-start(f32[128,3584]{1,0:T(8,128)S(1)} %slice.319), channel_id=1, source_target_pairs={{0,1},{1,0},{2,3},{3,2},{4,5},{5,4},{6,7},{7,6},{8,9},{9,8},{10,11... | collective-permute-start | bytes 5505032 | tf_op jit(solution)/shard_map/ppermute | solution.py:36
  55.2 13.1 %collective-permute-start.4 = (f16[64,3712]{1,0:T(8,128)(2,1)S(1)}, f16[64,3712]{1,0:T(8,128)(2,1)S(1)}, u32[]{:S(2)}, u32[]{:S(2)}) collective-permute-start(f16[64,3712]{1,0:T(8,128)(2,1)S(1)} %pad_maximum_fusion.24), channel_id=1, source_target_pairs={{0,2},{1,3},{2,0},{3,1},{4,6},{5,7},{6,4},{7,5},{8,10},{9,11},{10,... | collective-permute-start | bytes 1425416 | tf_op jit(solution)/shard_map/ppermute | solution.py:36
  64.2 22.0 %collective-permute-start.7 = (f32[128,3584]{1,0:T(8,128)S(1)}, f32[128,3584]{1,0:T(8,128)S(1)}, u32[]{:S(2)}, u32[]{:S(2)}) collective-permute-start(f32[128,3584]{1,0:T(8,128)S(1)} %slice.325), channel_id=1, source_target_pairs={{0,1},{1,0},{2,3},{3,2},{4,5},{5,4},{6,7},{7,6},{8,9},{9,8},{10,11... | collective-permute-start | bytes 5505032 | tf_op jit(solution)/shard_map/ppermute | solution.py:36
  64.4 24.0 %collective-permute-start.8 = (f16[64,3584]{1,0:T(8,128)(2,1)S(1)}, f16[64,3584]{1,0:T(8,128)(2,1)S(1)}, u32[]{:S(2)}, u32[]{:S(2)}) collective-permute-start(f16[64,3584]{1,0:T(8,128)(2,1)S(1)} %fusion.58), channel_id=1, source_target_pairs={{0,2},{1,3},{2,0},{3,1},{4,6},{5,7},{6,4},{7,5},{8,10},{9,11},{10,... | collective-permute-start | bytes 1376264 | tf_op jit(solution)/shard_map/ppermute | solution.py:36
  84.3 19.4 %collective-permute-start.11 = (f32[128,3584]{1,0:T(8,128)S(1)}, f32[128,3584]{1,0:T(8,128)S(1)}, u32[]{:S(2)}, u32[]{:S(2)}) collective-permute-start(f32[128,3584]{1,0:T(8,128)S(1)} %slice.333), channel_id=1, source_target_pairs={{0,1},{1,0},{2,3},{3,2},{4,5},{5,4},{6,7},{7,6},{8,9},{9,8},{10,11... | collective-permute-start | bytes 5505032 | tf_op jit(solution)/shard_map/ppermute | solution.py:36
  84.4 63.2 %collective-permute-start.23 = (bf16[4,32,2048]{2,1,0:T(8,128)(2,1)}, bf16[4,32,2048]{2,1,0:T(8,128)(2,1)}, u32[]{:S(2)}, u32[]{:S(2)}) collective-permute-start(bf16[4,32,2048]{2,1,0:T(8,128)(2,1)} %collective-permute-done.1), channel_id=1, source_target_pairs={{0,16},{16,0},{1,17},{17,1},{2,18},{18,2},{3,19},{19,3},{4,20},{20... | collective-permute-start | bytes 1572872 | tf_op jit(solution)/shard_map/ppermute | solution.py:36
  86.2 61.5 %collective-permute-start.24 = (bf16[4,32,2048]{2,1,0:T(8,128)(2,1)}, bf16[4,32,2048]{2,1,0:T(8,128)(2,1)}, u32[]{:S(2)}, u32[]{:S(2)}) collective-permute-start(bf16[4,32,2048]{2,1,0:T(8,128)(2,1)} %collective-permute-done.5), channel_id=1, source_target_pairs={{0,16},{16,0},{1,17},{17,1},{2,18},{18,2},{3,19},{19,3},{4,20},{20... | collective-permute-start | bytes 1572872 | tf_op jit(solution)/shard_map/ppermute | solution.py:36
  97.2 28.0 %collective-permute-start.9 = (f32[128,3584]{1,0:T(8,128)}, f32[128,3584]{1,0:T(8,128)}, u32[]{:S(2)}, u32[]{:S(2)}) collective-permute-start(f32[128,3584]{1,0:T(8,128)} %slice.328), channel_id=1, source_target_pairs={{0,1},{1,0},{2,3},{3,2},{4,5},{5,4},{6,7},{7,6},{8,9},{9,8},{10,11... | collective-permute-start | bytes 5505032 | tf_op jit(solution)/shard_map/ppermute | solution.py:36
  102.2 14.5 %collective-permute-start.16 = (bf16[64,3584]{1,0:T(8,128)(2,1)S(1)}, bf16[64,3584]{1,0:T(8,128)(2,1)S(1)}, u32[]{:S(2)}, u32[]{:S(2)}) collective-permute-start(bf16[64,3584]{1,0:T(8,128)(2,1)S(1)} %get-tuple-element.83), channel_id=1, source_target_pairs={{0,2},{1,3},{2,0},{3,1},{4,6},{5,7},{6,4},{7,5},{8,10},{9,11},{10,... | collective-permute-start | bytes 1376264 | tf_op jit(solution)/shard_map/ppermute | solution.py:36
  105.2 18.8 %collective-permute-start.12 = (f16[64,3712]{1,0:T(8,128)(2,1)}, f16[64,3712]{1,0:T(8,128)(2,1)}, u32[]{:S(2)}, u32[]{:S(2)}) collective-permute-start(f16[64,3712]{1,0:T(8,128)(2,1)} %pad_maximum_fusion.25), channel_id=1, source_target_pairs={{0,2},{1,3},{2,0},{3,1},{4,6},{5,7},{6,4},{7,5},{8,10},{9,11},{10,... | collective-permute-start | bytes 1425416 | tf_op jit(solution)/shard_map/ppermute | solution.py:36
  116.6 94.0 %all-gather.5.cloned.1.call-start = ((), (), s32[]{:S(2)}) async-start(), calls=%async_computation | async-start | bytes 2752512 | tf_op jit(solution)/shard_map/all_gather | solution.py:210
  116.7 27.2 %collective-permute-start.14 = (f32[128,3584]{1,0:T(8,128)}, f32[128,3584]{1,0:T(8,128)S(1)}, u32[]{:S(2)}, u32[]{:S(2)}) collective-permute-start(f32[128,3584]{1,0:T(8,128)} %slice.343), channel_id=1, source_target_pairs={{0,1},{1,0},{2,3},{3,2},{4,5},{5,4},{6,7},{7,6},{8,9},{9,8},{10,11... | collective-permute-start | bytes 5505032 | tf_op jit(solution)/shard_map/ppermute | solution.py:36
  126.8 21.4 %collective-permute-start.10 = (f16[64,3584]{1,0:T(8,128)(2,1)S(1)}, f16[64,3584]{1,0:T(8,128)(2,1)S(1)}, u32[]{:S(2)}, u32[]{:S(2)}) collective-permute-start(f16[64,3584]{1,0:T(8,128)(2,1)S(1)} %fusion.54), channel_id=1, source_target_pairs={{0,2},{1,3},{2,0},{3,1},{4,6},{5,7},{6,4},{7,5},{8,10},{9,11},{10,... | collective-permute-start | bytes 1376264 | tf_op jit(solution)/shard_map/ppermute | solution.py:36
  137.5 75.9 %collective-permute-start.21 = (bf16[4,32,2048]{2,1,0:T(8,128)(2,1)}, bf16[4,32,2048]{2,1,0:T(8,128)(2,1)}, u32[]{:S(2)}, u32[]{:S(2)}) collective-permute-start(bf16[4,32,2048]{2,1,0:T(8,128)(2,1)} %get-tuple-element.102), channel_id=1, source_target_pairs={{0,8},{4,12},{8,0},{12,4},{1,9},{5,13},{9,1},{13,5},{2,10},{6,14},... | collective-permute-start | bytes 1572872 | tf_op jit(solution)/shard_map/ppermute | solution.py:41
  143.9 69.5 %collective-permute-start.20 = (bf16[4,32,2048]{2,1,0:T(8,128)(2,1)}, bf16[4,32,2048]{2,1,0:T(8,128)(2,1)}, u32[]{:S(2)}, u32[]{:S(2)}) collective-permute-start(bf16[4,32,2048]{2,1,0:T(8,128)(2,1)} %get-tuple-element.101), channel_id=1, source_target_pairs={{0,12},{4,0},{8,4},{12,8},{1,13},{5,1},{9,5},{13,9},{2,14},{6,2},{... | collective-permute-start | bytes 1572872 | tf_op jit(solution)/shard_map/ppermute | solution.py:41
  147.6 17.3 %collective-permute-start.30 = (f32[128,3584]{1,0:T(8,128)}, f32[128,3584]{1,0:T(8,128)}, u32[]{:S(2)}, u32[]{:S(2)}) collective-permute-start(f32[128,3584]{1,0:T(8,128)} %slice.359), channel_id=1, source_target_pairs={{0,1},{1,0},{2,3},{3,2},{4,5},{5,4},{6,7},{7,6},{8,9},{9,8},{10,11... | collective-permute-start | bytes 5505032 | tf_op jit(solution)/shard_map/ppermute | solution.py:36
  147.7 12.9 %collective-permute-start.15 = (bf16[64,3584]{1,0:T(8,128)(2,1)S(1)}, bf16[64,3584]{1,0:T(8,128)(2,1)S(1)}, u32[]{:S(2)}, u32[]{:S(2)}) collective-permute-start(bf16[64,3584]{1,0:T(8,128)(2,1)S(1)} %fusion.49), channel_id=1, source_target_pairs={{0,2},{1,3},{2,0},{3,1},{4,6},{5,7},{6,4},{7,5},{8,10},{9,11},{10,... | collective-permute-start | bytes 1376264 | tf_op jit(solution)/shard_map/ppermute | solution.py:36
  155.1 34.7 %collective-permute-start.25 = (f32[128,3584]{1,0:T(8,128)}, f32[128,3584]{1,0:T(8,128)}, u32[]{:S(2)}, u32[]{:S(2)}) collective-permute-start(f32[128,3584]{1,0:T(8,128)} %slice.363), channel_id=1, source_target_pairs={{0,1},{1,0},{2,3},{3,2},{4,5},{5,4},{6,7},{7,6},{8,9},{9,8},{10,11... | collective-permute-start | bytes 5505032 | tf_op jit(solution)/shard_map/ppermute | solution.py:36
  164.3 13.4 %collective-permute-start.18 = (bf16[64,3584]{1,0:T(8,128)(2,1)S(1)}, bf16[64,3584]{1,0:T(8,128)(2,1)S(1)}, u32[]{:S(2)}, u32[]{:S(2)}) collective-permute-start(bf16[64,3584]{1,0:T(8,128)(2,1)S(1)} %get-tuple-element.81), channel_id=1, source_target_pairs={{0,2},{1,3},{2,0},{3,1},{4,6},{5,7},{6,4},{7,5},{8,10},{9,11},{10,... | collective-permute-start | bytes 1376264 | tf_op jit(solution)/shard_map/ppermute | solution.py:36
  167.2 19.1 %collective-permute-start.31 = (bf16[64,3584]{1,0:T(8,128)(2,1)}, bf16[64,3584]{1,0:T(8,128)(2,1)S(1)}, u32[]{:S(2)}, u32[]{:S(2)}) collective-permute-start(bf16[64,3584]{1,0:T(8,128)(2,1)} %fusion.37), channel_id=1, source_target_pairs={{0,2},{1,3},{2,0},{3,1},{4,6},{5,7},{6,4},{7,5},{8,10},{9,11},{10,... | collective-permute-start | bytes 1376264 | tf_op jit(solution)/shard_map/ppermute | solution.py:36
  178.7 14.1 %collective-permute-start.19 = (bf16[128,3584]{1,0:T(8,128)(2,1)}, bf16[128,3584]{1,0:T(8,128)(2,1)}, u32[]{:S(2)}, u32[]{:S(2)}) collective-permute-start(bf16[128,3584]{1,0:T(8,128)(2,1)} %pad_maximum_fusion.15), channel_id=1, source_target_pairs={{0,1},{1,0},{2,3},{3,2},{4,5},{5,4},{6,7},{7,6},{8,9},{9,8},{10,11... | collective-permute-start | bytes 2752520 | tf_op jit(solution)/shard_map/ppermute | solution.py:36
  189.2 14.5 %collective-permute-start.32 = (bf16[64,3584]{1,0:T(8,128)(2,1)S(1)}, bf16[64,3584]{1,0:T(8,128)(2,1)S(1)}, u32[]{:S(2)}, u32[]{:S(2)}) collective-permute-start(bf16[64,3584]{1,0:T(8,128)(2,1)S(1)} %fusion.40), channel_id=1, source_target_pairs={{0,2},{1,3},{2,0},{3,1},{4,6},{5,7},{6,4},{7,5},{8,10},{9,11},{10,... | collective-permute-start | bytes 1376264 | tf_op jit(solution)/shard_map/ppermute | solution.py:36
  191.3 19.2 %collective-permute-start.26 = (bf16[64,3584]{1,0:T(8,128)(2,1)S(1)}, bf16[64,3584]{1,0:T(8,128)(2,1)}, u32[]{:S(2)}, u32[]{:S(2)}) collective-permute-start(bf16[64,3584]{1,0:T(8,128)(2,1)S(1)} %fusion.41), channel_id=1, source_target_pairs={{0,2},{1,3},{2,0},{3,1},{4,6},{5,7},{6,4},{7,5},{8,10},{9,11},{10,... | collective-permute-start | bytes 1376264 | tf_op jit(solution)/shard_map/ppermute | solution.py:36
  201.5 14.4 %collective-permute-start.22 = (bf16[4,32,2048]{2,1,0:T(8,128)(2,1)}, bf16[4,32,2048]{2,1,0:T(8,128)(2,1)}, u32[]{:S(2)}, u32[]{:S(2)}) collective-permute-start(bf16[4,32,2048]{2,1,0:T(8,128)(2,1)} %fusion.59), channel_id=1, source_target_pairs={{0,4},{4,8},{8,12},{12,0},{1,5},{5,9},{9,13},{13,1},{2,6},{6,10},{... | collective-permute-start | bytes 1572872 | tf_op jit(solution)/shard_map/ppermute | solution.py:41
  204.8 16.8 %collective-permute-start.33 = (bf16[128,3584]{1,0:T(8,128)(2,1)}, bf16[128,3584]{1,0:T(8,128)(2,1)}, u32[]{:S(2)}, u32[]{:S(2)}) collective-permute-start(bf16[128,3584]{1,0:T(8,128)(2,1)} %pad_maximum_fusion.17), channel_id=1, source_target_pairs={{0,1},{1,0},{2,3},{3,2},{4,5},{5,4},{6,7},{7,6},{8,9},{9,8},{10,11... | collective-permute-start | bytes 2752520 | tf_op jit(solution)/shard_map/ppermute | solution.py:36
  212.7 35.3 %collective-permute-start.27 = (bf16[64,3584]{1,0:T(8,128)(2,1)S(1)}, bf16[64,3584]{1,0:T(8,128)(2,1)S(1)}, u32[]{:S(2)}, u32[]{:S(2)}) collective-permute-start(bf16[64,3584]{1,0:T(8,128)(2,1)S(1)} %fusion.44), channel_id=1, source_target_pairs={{0,2},{1,3},{2,0},{3,1},{4,6},{5,7},{6,4},{7,5},{8,10},{9,11},{10,... | collective-permute-start | bytes 1376264 | tf_op jit(solution)/shard_map/ppermute | solution.py:36
  217.7 16.7 %collective-permute-start.34 = (bf16[4,32,2048]{2,1,0:T(8,128)(2,1)S(1)}, bf16[4,32,2048]{2,1,0:T(8,128)(2,1)S(1)}, u32[]{:S(2)}, u32[]{:S(2)}) collective-permute-start(bf16[4,32,2048]{2,1,0:T(8,128)(2,1)S(1)} %fusion.20), channel_id=1, source_target_pairs={{0,4},{4,8},{8,12},{12,0},{1,5},{5,9},{9,13},{13,1},{2,6},{6,10},{... | collective-permute-start | bytes 1572872 | tf_op jit(solution)/shard_map/ppermute | solution.py:41
  218.0 22.4 %collective-permute-start.29 = (bf16[4,32,2048]{2,1,0:T(8,128)(2,1)S(1)}, bf16[4,32,2048]{2,1,0:T(8,128)(2,1)S(1)}, u32[]{:S(2)}, u32[]{:S(2)}) collective-permute-start(bf16[4,32,2048]{2,1,0:T(8,128)(2,1)S(1)} %fusion.20), channel_id=1, source_target_pairs={{0,12},{4,0},{8,4},{12,8},{1,13},{5,1},{9,5},{13,9},{2,14},{6,2},{... | collective-permute-start | bytes 1572872 | tf_op jit(solution)/shard_map/ppermute | solution.py:41
  248.9 26.9 %collective-permute-start.39 = (bf16[4,32,2048]{2,1,0:T(8,128)(2,1)S(1)}, bf16[4,32,2048]{2,1,0:T(8,128)(2,1)S(1)}, u32[]{:S(2)}, u32[]{:S(2)}) collective-permute-start(bf16[4,32,2048]{2,1,0:T(8,128)(2,1)S(1)} %copy-done.44), channel_id=1, source_target_pairs={{0,8},{4,12},{8,0},{12,4},{1,9},{5,13},{9,1},{13,5},{2,10},{6,14},... | collective-permute-start | bytes 1572872 | tf_op jit(solution)/shard_map/ppermute | solution.py:41
  251.2 36.9 %collective-permute-start.36 = (bf16[4,32,2048]{2,1,0:T(8,128)(2,1)S(1)}, bf16[4,32,2048]{2,1,0:T(8,128)(2,1)S(1)}, u32[]{:S(2)}, u32[]{:S(2)}) collective-permute-start(bf16[4,32,2048]{2,1,0:T(8,128)(2,1)S(1)} %copy-done.43), channel_id=1, source_target_pairs={{0,12},{4,0},{8,4},{12,8},{1,13},{5,1},{9,5},{13,9},{2,14},{6,2},{... | collective-permute-start | bytes 1572872 | tf_op jit(solution)/shard_map/ppermute | solution.py:41
  261.6 26.5 %collective-permute-start.40 = (bf16[4,32,2048]{2,1,0:T(8,128)(2,1)S(1)}, bf16[4,32,2048]{2,1,0:T(8,128)(2,1)S(1)}, u32[]{:S(2)}, u32[]{:S(2)}) collective-permute-start(bf16[4,32,2048]{2,1,0:T(8,128)(2,1)S(1)} %fusion.60), channel_id=1, source_target_pairs={{0,4},{4,8},{8,12},{12,0},{1,5},{5,9},{9,13},{13,1},{2,6},{6,10},{... | collective-permute-start | bytes 1572872 | tf_op jit(solution)/shard_map/ppermute | solution.py:41
  267.1 31.2 %collective-permute-start.42 = (bf16[4,32,2048]{2,1,0:T(8,128)(2,1)S(1)}, bf16[4,32,2048]{2,1,0:T(8,128)(2,1)S(1)}, u32[]{:S(2)}, u32[]{:S(2)}) collective-permute-start(bf16[4,32,2048]{2,1,0:T(8,128)(2,1)S(1)} %collective-permute-done.29), channel_id=1, source_target_pairs={{0,12},{4,0},{8,4},{12,8},{1,13},{5,1},{9,5},{13,9},{2,14},{6,2},{... | collective-permute-start | bytes 1572872 | tf_op jit(solution)/shard_map/ppermute | solution.py:41
  306.0 12.7 %collective-permute-start.43 = (f32[128,3584]{1,0:T(8,128)S(1)}, f32[128,3584]{1,0:T(8,128)S(1)}, u32[]{:S(2)}, u32[]{:S(2)}) collective-permute-start(f32[128,3584]{1,0:T(8,128)S(1)} %slice.382), channel_id=1, source_target_pairs={{0,1},{1,0},{2,3},{3,2},{4,5},{5,4},{6,7},{7,6},{8,9},{9,8},{10,11... | collective-permute-start | bytes 5505032 | tf_op jit(solution)/shard_map/ppermute | solution.py:36
  306.1 25.3 %collective-permute-start.48 = (bf16[4,32,2048]{2,1,0:T(8,128)(2,1)S(1)}, bf16[4,32,2048]{2,1,0:T(8,128)(2,1)S(1)}, u32[]{:S(2)}, u32[]{:S(2)}) collective-permute-start(bf16[4,32,2048]{2,1,0:T(8,128)(2,1)S(1)} %fusion.15), channel_id=1, source_target_pairs={{0,4},{4,8},{8,12},{12,0},{1,5},{5,9},{9,13},{13,1},{2,6},{6,10},{... | collective-permute-start | bytes 1572872 | tf_op jit(solution)/shard_map/ppermute | solution.py:41
  316.7 25.6 %collective-permute-start.47 = (bf16[4,32,2048]{2,1,0:T(8,128)(2,1)S(1)}, bf16[4,32,2048]{2,1,0:T(8,128)(2,1)S(1)}, u32[]{:S(2)}, u32[]{:S(2)}) collective-permute-start(bf16[4,32,2048]{2,1,0:T(8,128)(2,1)S(1)} %fusion.15), channel_id=1, source_target_pairs={{0,12},{4,0},{8,4},{12,8},{1,13},{5,1},{9,5},{13,9},{2,14},{6,2},{... | collective-permute-start | bytes 1572872 | tf_op jit(solution)/shard_map/ppermute | solution.py:41
  355.3 29.5 %collective-permute-start.41 = (bf16[128,3584]{1,0:T(8,128)(2,1)}, bf16[128,3584]{1,0:T(8,128)(2,1)}, u32[]{:S(2)}, u32[]{:S(2)}) collective-permute-start(bf16[128,3584]{1,0:T(8,128)(2,1)} %pad_maximum_fusion.18), channel_id=1, source_target_pairs={{0,1},{1,0},{2,3},{3,2},{4,5},{5,4},{6,7},{7,6},{8,9},{9,8},{10,11... | collective-permute-start | bytes 2752520 | tf_op jit(solution)/shard_map/ppermute | solution.py:36
  355.7 13.9 %collective-permute-start.53 = (bf16[4,32,2048]{2,1,0:T(8,128)(2,1)S(1)}, bf16[4,32,2048]{2,1,0:T(8,128)(2,1)S(1)}, u32[]{:S(2)}, u32[]{:S(2)}) collective-permute-start(bf16[4,32,2048]{2,1,0:T(8,128)(2,1)S(1)} %copy-done.48), channel_id=1, source_target_pairs={{0,12},{4,0},{8,4},{12,8},{1,13},{5,1},{9,5},{13,9},{2,14},{6,2},{... | collective-permute-start | bytes 1572872 | tf_op jit(solution)/shard_map/ppermute | solution.py:41
  387.8 42.9 %collective-permute-start.46 = (bf16[128,3584]{1,0:T(8,128)(2,1)S(1)}, bf16[128,3584]{1,0:T(8,128)(2,1)S(1)}, u32[]{:S(2)}, u32[]{:S(2)}) collective-permute-start(bf16[128,3584]{1,0:T(8,128)(2,1)S(1)} %pad_maximum_fusion.19), channel_id=1, source_target_pairs={{0,1},{1,0},{2,3},{3,2},{4,5},{5,4},{6,7},{7,6},{8,9},{9,8},{10,11... | collective-permute-start | bytes 2752520 | tf_op jit(solution)/shard_map/ppermute | solution.py:36
  388.3 13.6 %collective-permute-start.50 = (bf16[64,3584]{1,0:T(8,128)(2,1)}, bf16[64,3584]{1,0:T(8,128)(2,1)S(1)}, u32[]{:S(2)}, u32[]{:S(2)}) collective-permute-start(bf16[64,3584]{1,0:T(8,128)(2,1)} %fusion.25), channel_id=1, source_target_pairs={{0,2},{1,3},{2,0},{3,1},{4,6},{5,7},{6,4},{7,5},{8,10},{9,11},{10,... | collective-permute-start | bytes 1376264 | tf_op jit(solution)/shard_map/ppermute | solution.py:36
  391.2 20.6 %collective-permute-start.55 = (bf16[64,3584]{1,0:T(8,128)(2,1)S(1)}, bf16[64,3584]{1,0:T(8,128)(2,1)S(1)}, u32[]{:S(2)}, u32[]{:S(2)}) collective-permute-start(bf16[64,3584]{1,0:T(8,128)(2,1)S(1)} %fusion.21), channel_id=1, source_target_pairs={{0,2},{1,3},{2,0},{3,1},{4,6},{5,7},{6,4},{7,5},{8,10},{9,11},{10,... | collective-permute-start | bytes 1376264 | tf_op jit(solution)/shard_map/ppermute | solution.py:36
  403.3 18.2 %collective-permute-start.51 = (bf16[64,3584]{1,0:T(8,128)(2,1)S(1)}, bf16[64,3584]{1,0:T(8,128)(2,1)S(1)}, u32[]{:S(2)}, u32[]{:S(2)}) collective-permute-start(bf16[64,3584]{1,0:T(8,128)(2,1)S(1)} %fusion.28), channel_id=1, source_target_pairs={{0,2},{1,3},{2,0},{3,1},{4,6},{5,7},{6,4},{7,5},{8,10},{9,11},{10,... | collective-permute-start | bytes 1376264 | tf_op jit(solution)/shard_map/ppermute | solution.py:36
  413.2 17.4 %collective-permute-start.56 = (bf16[64,3584]{1,0:T(8,128)(2,1)S(1)}, bf16[64,3584]{1,0:T(8,128)(2,1)S(1)}, u32[]{:S(2)}, u32[]{:S(2)}) collective-permute-start(bf16[64,3584]{1,0:T(8,128)(2,1)S(1)} %fusion.24), channel_id=1, source_target_pairs={{0,2},{1,3},{2,0},{3,1},{4,6},{5,7},{6,4},{7,5},{8,10},{9,11},{10,... | collective-permute-start | bytes 1376264 | tf_op jit(solution)/shard_map/ppermute | solution.py:36
  (70 other events, 722.6 us)
Sparse Core Ops, SparseCore 0:
  116.7 31.4 all-gather.6
  165.0 30.3 all-gather.4

commit v12 on v11

--- a/solution.py
+++ b/solution.py
@@ -253,10 +253,10 @@
         if j:
             early.append(hidden_rows(0, j - 1, first))
         project(0, j, "gate", others[0] if j == tail else [])
-        first = project(0, j, "tangent", [])
+        first = project(0, j, "tangent", marks[-1][1] if j == tail else [])
         if j:
             share_gain(j - 1, first)
-    ready = [out_sums(0, j, early[j][0], marks[-2][1]) for j in range(tail)]
+    ready = [out_sums(0, j, early[j][0], marks[-1][1]) for j in range(tail)]
     first = project(1, 0, "tangent", ready)
     hidden, _ = hidden_rows(0, tail, first)
     for j in range(1, GROUPS):
@@ -268,15 +268,15 @@
     hidden = [hidden_rows(1, j, []) for j in range(GROUPS)]
     ready = [out_sums(1, j, hidden[j][0], []) for j in range(tail)]
     first, sent, got, near = back(0, tail, pieces, ready + pieces[:1])
-    ready = [out_sums(1, tail, hidden[tail][0], sent)]
-    others = scaled_pieces(1, near)
-    after = ready + got + others[last:]
+    ready = [out_sums(1, tail, hidden[tail][0], sent + pieces)]
+    after = ready + got + [moved[1, k] for j in range(tail) for k in steps[j]]
     for j in reversed(range(tail)):
-        _, _, after, near = back(0, j, pieces, after)
-    after = after + others[:1]
+        _, _, after, nextnear = back(0, j, pieces, after)
+    pieces = scaled_pieces(1, near)
+    after = after + pieces[:1]
     for j in reversed(range(GROUPS)):
-        _, after, _, _ = back(1, j, others, after)
-        after = after + near
+        _, after, _, _ = back(1, j, pieces, after)
+        after = after + nextnear
     return last_product(turned, bars, tokens)
 
 

time: 467 us -> 482 us (1.032)
  starting transfers between devices: 63.1 us -> 77.6 us
  waiting for transfers between devices: 170 us -> 160 us
  matrix products: 115 us -> 122 us
    ppermute x15, starting transfers between devices: 34.2 us -> 44.4 us  [shift(): lax.ppermute(values, axis, [(i, (i + by) % count) for i in range(count)])]
    ppermute x43, waiting for transfers between devices: 82.4 us -> 73.3 us  [swap(): return lax.ppermute(values, axis, [(i, i ^ mask) for i in range(count)])]
    dot_general x12, matrix products: 83.8 us -> 88.9 us  [matmul(): return jnp.dot(left, right, preferred_element_type=jnp.float32)]
    unnamed x116 -> x120, local copies, waits for them, and re-layouts: 10.7 us -> 11.4 us
  transfers between devices with their start and end apart: 60 -> 60, of which waited for: 27 -> 21; matrix products, arithmetic and copies ran while one was open for 33% -> 36% of each run, Pallas kernels for 0% -> 0%
where the time goes in v12:
time: 482 us; the launch traced here: 478 us
  waiting for transfers between devices  160 us (33%)
  matrix products  122 us (25%)
  starting transfers between devices  77.6 us (16%)
  other arithmetic  47.4 us (10%)
  local copies, waits for them, and re-layouts  34.2 us (7%)
  Pallas kernels  22.5 us (5%)
  between operations  15 us (3%)
    dot_general x12, matrix products, matmul(): return jnp.dot(left, right, preferred_element_type=jnp.float32)  88.9 us
    ppermute x15, waiting for transfers between devices, shift(): lax.ppermute(values, axis, [(i, (i + by) % count) for i in range(count)])  86.6 us
    ppermute x43, waiting for transfers between devices, swap(): return lax.ppermute(values, axis, [(i, i ^ mask) for i in range(count)])  73.3 us
    ppermute x15, starting transfers between devices, shift(): lax.ppermute(values, axis, [(i, (i + by) % count) for i in range(count)])  44.4 us
    ppermute x43, starting transfers between devices, swap(): return lax.ppermute(values, axis, [(i, i ^ mask) for i in range(count)])  33.2 us
    dot_general x4, matrix products, times_down(): lax.dot_general(left, w_down, (((1,), (1,)), ((), ())), preferred_element...  32.9 us
    pallas_call x1, Pallas kernels, last_product(): pl.pallas_call(functools.partial(last_kernel, 1.0 / tokens, len(turned)),...  22.5 us
    unnamed x120, local copies, waits for them, and re-layouts  11.4 us
  transfers between devices with their start and end apart: 60, of which 21 were waited for; matrix products, arithmetic and copies ran while one was open for 36% of the time, Pallas kernels for 0%

profile of v12, /device:TPU:0, one launch (start us, length us, event | category | flops | bytes accessed | tf_op | source)
XLA Modules:
  0.0 478.5 jit_solution(7371303943420237686)
XLA Ops:
  8.0 3.1 collective-permute-start
  11.1 13.9 %collective-permute-done = bf16[4,32,2048]{2,1,0:T(8,128)(2,1)S(1)} collective-permute-done((bf16[4,32,2048]{2,1,0:T(8,128)(2,1)S(1)}, bf16[4,32,2048]{2,1,0:T(8,128)(2,1)S(1)}, u32[]{:S(2)}, u32[]{:S(2)}) %collective-permute-start) | collective-permute-done | bytes 524320 | tf_op jit(solution)/shard_map/ppermute | solution.py:41
  25.1 7.6 %fusion.86 = f32[256,3584]{1,0:T(8,128)S(1)} fusion(bf16[256,2048]{1,0:T(8,128)(2,1)S(1)} %bitcast.130, bf16[2048,3584]{1,0:T(8,128)(2,1)} %param.8), kind=kOutput, calls=%fused_computation.192 | convolution fusion | flops 3758096384 | bytes 19398656 | tf_op jit(solution)/shard_map/dot_general | solution.py:19
  36.5 7.2 %fusion.85 = f32[256,3584]{1,0:T(8,128)S(1)} fusion(bf16[256,2048]{1,0:T(8,128)(2,1)S(1)} %bitcast.131, bf16[2048,3584]{1,0:T(8,128)(2,1)} %param.7), kind=kOutput, calls=%fused_computation.191 | convolution fusion | flops 3758096384 | bytes 19398656 | tf_op jit(solution)/shard_map/dot_general | solution.py:19
  46.2 7.2 %fusion.87 = f32[256,3584]{1,0:T(8,128)S(1)} fusion(bf16[256,2048]{1,0:T(8,128)(2,1)S(1)} %bitcast.132, bf16[2048,3584]{1,0:T(8,128)(2,1)} %param.10), kind=kOutput, calls=%fused_computation.193 | convolution fusion | flops 3758096384 | bytes 19398656 | tf_op jit(solution)/shard_map/dot_general | solution.py:19
  54.6 3.8 collective-permute-done.4
  58.4 10.9 %collective-permute-done.1 = bf16[4,32,2048]{2,1,0:T(8,128)(2,1)} collective-permute-done((bf16[4,32,2048]{2,1,0:T(8,128)(2,1)S(1)}, bf16[4,32,2048]{2,1,0:T(8,128)(2,1)}, u32[]{:S(2)}, u32[]{:S(2)}) %collective-permute-start.1) | collective-permute-done | bytes 524320 | tf_op jit(solution)/shard_map/ppermute | solution.py:41
  70.6 7.3 %fusion.89 = f32[256,3584]{1,0:T(8,128)S(1)} fusion(bf16[256,2048]{1,0:T(8,128)(2,1)S(1)} %bitcast.134, bf16[2048,3584]{1,0:T(8,128)(2,1)} %param.8), kind=kOutput, calls=%fused_computation.195 | convolution fusion | flops 3758096384 | bytes 19398656 | tf_op jit(solution)/shard_map/dot_general | solution.py:19
  80.8 7.2 %fusion.88 = f32[256,3584]{1,0:T(8,128)S(1)} fusion(bf16[256,2048]{1,0:T(8,128)(2,1)S(1)} %bitcast.135, bf16[2048,3584]{1,0:T(8,128)(2,1)} %param.7), kind=kOutput, calls=%fused_computation.194 | convolution fusion | flops 3758096384 | bytes 19398656 | tf_op jit(solution)/shard_map/dot_general | solution.py:19
  88.4 2.9 collective-permute-done.13
  97.7 7.5 %fusion.90 = f32[256,3584]{1,0:T(8,128)S(1)} fusion(bf16[256,2048]{1,0:T(8,128)(2,1)S(1)} %bitcast.136, bf16[2048,3584]{1,0:T(8,128)(2,1)} %param.10), kind=kOutput, calls=%fused_computation.196 | convolution fusion | flops 3758096384 | bytes 19398656 | tf_op jit(solution)/shard_map/dot_general | solution.py:19
  111.7 9.7 %collective-permute-done.12 = f16[64,3712]{1,0:T(8,128)(2,1)S(1)} collective-permute-done((f16[64,3712]{1,0:T(8,128)(2,1)S(1)}, f16[64,3712]{1,0:T(8,128)(2,1)S(1)}, u32[]{:S(2)}, u32[]{:S(2)}) %collective-permute-start.12) | collective-permute-done | bytes 475168 | tf_op jit(solution)/shard_map/ppermute | solution.py:36
  128.7 9.2 %convolution_convert_fusion.1 = bf16[256,2048]{1,0:T(8,128)(2,1)S(1)} fusion(bf16[256,3584]{1,0:T(8,128)(2,1)S(1)} %pad_maximum_fusion, bf16[3584,2048]{1,0:T(8,128)(2,1)} %param.9), kind=kOutput, calls=%fused_computation.1 | convolution fusion | flops 3758620672 | bytes 17563648 | tf_op jit(solution)/shard_map/dot_general | solution.py:19
  139.6 3.9 fusion.91
  149.0 3.3 multiply_convert_fusion
  152.2 3.9 fusion.92
  158.5 2.9 dynamic-slice_bitcast_fusion.3
  161.4 4.2 collective-permute-start.20
  166.8 2.3 fusion.37
  171.1 2.5 fusion.41
  173.6 11.1 %fusion = f32[256,2048]{1,0:T(8,128)} fusion(bf16[3584,2048]{1,0:T(8,128)(2,1)} %param.9, bf16[128,3584]{1,0:T(8,128)(2,1)S(1)} %collective-permute-done.19, bf16[64,3584]{1,0:T(8,128)(2,1)} %collective-permute-done.18, bf16[64,3584]{1,0:T(8,128)(2,1)S(1)} %get-tuple-element.81), kind=kOutput, calls=%fused_computation.3 | convolution fusion | flops 3763601408 | bytes 18612224 | tf_op jit(solution)/shard_map/dot_general | solution.py:19
  191.4 10.6 %collective-permute-done.32 = bf16[64,3584]{1,0:T(8,128)(2,1)S(1)} collective-permute-done((bf16[64,3584]{1,0:T(8,128)(2,1)S(1)}, bf16[64,3584]{1,0:T(8,128)(2,1)S(1)}, u32[]{:S(2)}, u32[]{:S(2)}) %collective-permute-start.32) | collective-permute-done | bytes 458784 | tf_op jit(solution)/shard_map/ppermute | solution.py:36
  209.6 3.3 collective-permute-start.34
  213.5 9.4 %convolution_convert_fusion = bf16[256,2048]{1,0:T(8,128)(2,1)S(1)} fusion(bf16[3584,2048]{1,0:T(8,128)(2,1)} %param.9, bf16[128,3584]{1,0:T(8,128)(2,1)} %collective-permute-done.33, bf16[64,3584]{1,0:T(8,128)(2,1)S(1)} %copy-done.55, bf16[64,3584]{1,0:T(8,128)(2,1)S(1)} %fusion.40), kind=kOutput, calls=%fused_computation | convolution fusion | flops 3764125696 | bytes 17563648 | tf_op jit(solution)/shard_map/dot_general | solution.py:19
  223.8 2.4 collective-permute-done.34
  226.3 10.5 %collective-permute-done.29 = bf16[4,32,2048]{2,1,0:T(8,128)(2,1)S(1)} collective-permute-done((bf16[4,32,2048]{2,1,0:T(8,128)(2,1)S(1)}, bf16[4,32,2048]{2,1,0:T(8,128)(2,1)S(1)}, u32[]{:S(2)}, u32[]{:S(2)}) %collective-permute-start.29) | collective-permute-done | bytes 524320 | tf_op jit(solution)/shard_map/ppermute | solution.py:41
  237.6 7.3 %fusion.93 = f32[256,3584]{1,0:T(8,128)S(1)} fusion(bf16[256,2048]{1,0:T(8,128)(2,1)S(1)} %bitcast.154, bf16[3584,2048]{1,0:T(8,128)(2,1)} %param.9), kind=kOutput, calls=%fused_computation.199 | convolution fusion | flops 3758096384 | bytes 19398656 | tf_op jit(solution)/shard_map/dot_general | solution.py:23
  246.0 2.4 collective-permute-start.36
  252.9 8.7 %collective-permute-done.36 = bf16[4,32,2048]{2,1,0:T(8,128)(2,1)S(1)} collective-permute-done((bf16[4,32,2048]{2,1,0:T(8,128)(2,1)S(1)}, bf16[4,32,2048]{2,1,0:T(8,128)(2,1)S(1)}, u32[]{:S(2)}, u32[]{:S(2)}) %collective-permute-start.36) | collective-permute-done | bytes 524320 | tf_op jit(solution)/shard_map/ppermute | solution.py:41
  261.6 7.2 %fusion.94 = f32[256,2048]{1,0:T(8,128)S(1)} fusion(bf16[256,3584]{1,0:T(8,128)(2,1)S(1)} %pad_maximum_fusion.1, bf16[3584,2048]{1,0:T(8,128)(2,1)} %param.9), kind=kOutput, calls=%fused_computation.200 | convolution fusion | flops 3758096384 | bytes 18612224 | tf_op jit(solution)/shard_map/dot_general | solution.py:19
  271.1 10.6 %collective-permute-start.41 = (bf16[4,32,2048]{2,1,0:T(8,128)(2,1)}, bf16[4,32,2048]{2,1,0:T(8,128)(2,1)}, u32[]{:S(2)}, u32[]{:S(2)}) collective-permute-start(bf16[4,32,2048]{2,1,0:T(8,128)(2,1)} %fusion.60), channel_id=1, source_target_pairs={{0,4},{4,8},{8,12},{12,0},{1,5},{5,9},{9,13},{13,1},{2,6},{6,10},{... | collective-permute-start | bytes 1572872 | tf_op jit(solution)/shard_map/ppermute | solution.py:41
  283.2 11.3 %collective-permute-done.40 = bf16[4,32,2048]{2,1,0:T(8,128)(2,1)S(1)} collective-permute-done((bf16[4,32,2048]{2,1,0:T(8,128)(2,1)S(1)}, bf16[4,32,2048]{2,1,0:T(8,128)(2,1)S(1)}, u32[]{:S(2)}, u32[]{:S(2)}) %collective-permute-start.40) | collective-permute-done | bytes 524320 | tf_op jit(solution)/shard_map/ppermute | solution.py:41
  295.3 9.1 %fusion.95 = f32[256,3584]{1,0:T(8,128)} fusion(bf16[256,2048]{1,0:T(8,128)(2,1)S(1)} %bitcast.152, bf16[3584,2048]{1,0:T(8,128)(2,1)} %param.9), kind=kOutput, calls=%fused_computation.201 | convolution fusion | flops 3758096384 | bytes 19398656 | tf_op jit(solution)/shard_map/dot_general | solution.py:23
  309.8 11.0 %collective-permute-done.39 = bf16[64,3584]{1,0:T(8,128)(2,1)S(1)} collective-permute-done((bf16[64,3584]{1,0:T(8,128)(2,1)S(1)}, bf16[64,3584]{1,0:T(8,128)(2,1)S(1)}, u32[]{:S(2)}, u32[]{:S(2)}) %collective-permute-start.39) | collective-permute-done | bytes 458784 | tf_op jit(solution)/shard_map/ppermute | solution.py:36
  322.5 11.1 %collective-permute-start.48 = (bf16[4,32,2048]{2,1,0:T(8,128)(2,1)S(1)}, bf16[4,32,2048]{2,1,0:T(8,128)(2,1)S(1)}, u32[]{:S(2)}, u32[]{:S(2)}) collective-permute-start(bf16[4,32,2048]{2,1,0:T(8,128)(2,1)S(1)} %fusion.15), channel_id=1, source_target_pairs={{0,4},{4,8},{8,12},{12,0},{1,5},{5,9},{9,13},{13,1},{2,6},{6,10},{... | collective-permute-start | bytes 1572872 | tf_op jit(solution)/shard_map/ppermute | solution.py:41
  335.6 10.4 %collective-permute-done.48 = bf16[4,32,2048]{2,1,0:T(8,128)(2,1)S(1)} collective-permute-done((bf16[4,32,2048]{2,1,0:T(8,128)(2,1)S(1)}, bf16[4,32,2048]{2,1,0:T(8,128)(2,1)S(1)}, u32[]{:S(2)}, u32[]{:S(2)}) %collective-permute-start.48) | collective-permute-done | bytes 524320 | tf_op jit(solution)/shard_map/ppermute | solution.py:41
  345.9 10.1 %collective-permute-done.47 = bf16[4,32,2048]{2,1,0:T(8,128)(2,1)S(1)} collective-permute-done((bf16[4,32,2048]{2,1,0:T(8,128)(2,1)S(1)}, bf16[4,32,2048]{2,1,0:T(8,128)(2,1)S(1)}, u32[]{:S(2)}, u32[]{:S(2)}) %collective-permute-start.47) | collective-permute-done | bytes 524320 | tf_op jit(solution)/shard_map/ppermute | solution.py:41
  356.2 9.1 %fusion.96 = f32[256,3584]{1,0:T(8,128)} fusion(bf16[256,2048]{1,0:T(8,128)(2,1)S(1)} %bitcast.155, bf16[3584,2048]{1,0:T(8,128)(2,1)} %param.9), kind=kOutput, calls=%fused_computation.202 | convolution fusion | flops 3758096384 | bytes 19398656 | tf_op jit(solution)/shard_map/dot_general | solution.py:23
  368.7 4.5 collective-permute-start.53
  374.9 2.8 fusion.25
  377.7 6.9 %collective-permute-done.53 = bf16[4,32,2048]{2,1,0:T(8,128)(2,1)S(1)} collective-permute-done((bf16[4,32,2048]{2,1,0:T(8,128)(2,1)S(1)}, bf16[4,32,2048]{2,1,0:T(8,128)(2,1)S(1)}, u32[]{:S(2)}, u32[]{:S(2)}) %collective-permute-start.53) | collective-permute-done | bytes 524320 | tf_op jit(solution)/shard_map/ppermute | solution.py:41
  385.8 7.3 %fusion.97 = f32[256,3584]{1,0:T(8,128)S(1)} fusion(bf16[256,2048]{1,0:T(8,128)(2,1)S(1)} %bitcast.153, bf16[3584,2048]{1,0:T(8,128)(2,1)} %param.9), kind=kOutput, calls=%fused_computation.203 | convolution fusion | flops 3758096384 | bytes 19398656 | tf_op jit(solution)/shard_map/dot_general | solution.py:23
  398.1 2.3 copy.21
  407.4 10.2 %collective-permute-done.50 = bf16[64,3584]{1,0:T(8,128)(2,1)S(1)} collective-permute-done((bf16[64,3584]{1,0:T(8,128)(2,1)}, bf16[64,3584]{1,0:T(8,128)(2,1)S(1)}, u32[]{:S(2)}, u32[]{:S(2)}) %collective-permute-start.50) | collective-permute-done | bytes 458784 | tf_op jit(solution)/shard_map/ppermute | solution.py:36
  420.5 6.9 %collective-permute-done.55 = bf16[64,3584]{1,0:T(8,128)(2,1)S(1)} collective-permute-done((bf16[64,3584]{1,0:T(8,128)(2,1)S(1)}, bf16[64,3584]{1,0:T(8,128)(2,1)S(1)}, u32[]{:S(2)}, u32[]{:S(2)}) %collective-permute-start.55) | collective-permute-done | bytes 458784 | tf_op jit(solution)/shard_map/ppermute | solution.py:36
  430.3 6.9 %collective-permute-done.51 = bf16[64,3584]{1,0:T(8,128)(2,1)S(1)} collective-permute-done((bf16[64,3584]{1,0:T(8,128)(2,1)S(1)}, bf16[64,3584]{1,0:T(8,128)(2,1)S(1)}, u32[]{:S(2)}, u32[]{:S(2)}) %collective-permute-start.51) | collective-permute-done | bytes 458784 | tf_op jit(solution)/shard_map/ppermute | solution.py:36
  437.3 8.8 %collective-permute-done.56 = bf16[64,3584]{1,0:T(8,128)(2,1)S(1)} collective-permute-done((bf16[64,3584]{1,0:T(8,128)(2,1)S(1)}, bf16[64,3584]{1,0:T(8,128)(2,1)S(1)}, u32[]{:S(2)}, u32[]{:S(2)}) %collective-permute-start.56) | collective-permute-done | bytes 458784 | tf_op jit(solution)/shard_map/ppermute | solution.py:36
  448.9 22.5 %shard_map.64 = f32[2048,3584]{1,0:T(8,128)} custom-call(bf16[2048,256]{1,0:T(8,128)(2,1)S(1)} %bitcast.127, bf16[2048,256]{1,0:T(8,128)(2,1)S(1)} %bitcast.126, bf16[2048,256]{1,0:T(8,128)(2,1)S(1)} %bitcast.129, bf16[2048,256]{1,0:T(8,128)(2,1)S(1)} %bitcast.128, bf16[256,3584]{1,0:T(8,128)(2,1)S(1)} %pad_maximum_fusion.2.refs_4_, ...), custom_call_target="tpu_custom_call" | custom-call | flops 15032385536 | bytes 40894464 | tf_op jit(solution)/shard_map/pallas_call | solution.py:91
  (297 shorter events, 108.1 us)
Async XLA Ops:
  6.5 178.2 %all-gather.7.cloned.1.call-start = ((), (), s32[]{:S(2)}) async-start(), calls=%async_computation.1 | async-start | bytes 2752512 | tf_op jit(solution)/shard_map/all_gather | solution.py:210
  8.0 17.0 %collective-permute-start = (bf16[4,32,2048]{2,1,0:T(8,128)(2,1)S(1)}, bf16[4,32,2048]{2,1,0:T(8,128)(2,1)S(1)}, u32[]{:S(2)}, u32[]{:S(2)}) collective-permute-start(bf16[4,32,2048]{2,1,0:T(8,128)(2,1)S(1)} %pad_maximum_fusion.22), channel_id=1, source_target_pairs={{0,4},{4,8},{8,12},{12,0},{1,5},{5,9},{9,13},{13,1},{2,6},{6,10},{... | collective-permute-start | bytes 1572872 | tf_op jit(solution)/shard_map/ppermute | solution.py:41
  33.0 21.1 %collective-permute-start.5 = (bf16[4,32,2048]{2,1,0:T(8,128)(2,1)S(1)}, bf16[4,32,2048]{2,1,0:T(8,128)(2,1)}, u32[]{:S(2)}, u32[]{:S(2)}) collective-permute-start(bf16[4,32,2048]{2,1,0:T(8,128)(2,1)S(1)} %pad_maximum_fusion.22), channel_id=1, source_target_pairs={{0,12},{4,0},{8,4},{12,8},{1,13},{5,1},{9,5},{13,9},{2,14},{6,2},{... | collective-permute-start | bytes 1572872 | tf_op jit(solution)/shard_map/ppermute | solution.py:41
  35.0 34.3 %collective-permute-start.1 = (bf16[4,32,2048]{2,1,0:T(8,128)(2,1)S(1)}, bf16[4,32,2048]{2,1,0:T(8,128)(2,1)}, u32[]{:S(2)}, u32[]{:S(2)}) collective-permute-start(bf16[4,32,2048]{2,1,0:T(8,128)(2,1)S(1)} %pad_maximum_fusion.22), channel_id=1, source_target_pairs={{0,8},{4,12},{8,0},{12,4},{1,9},{5,13},{9,1},{13,5},{2,10},{6,14},... | collective-permute-start | bytes 1572872 | tf_op jit(solution)/shard_map/ppermute | solution.py:41
  35.0 45.0 %collective-permute-start.6 = (bf16[4,32,2048]{2,1,0:T(8,128)(2,1)S(1)}, bf16[4,32,2048]{2,1,0:T(8,128)(2,1)S(1)}, u32[]{:S(2)}, u32[]{:S(2)}) collective-permute-start(bf16[4,32,2048]{2,1,0:T(8,128)(2,1)S(1)} %collective-permute-done), channel_id=1, source_target_pairs={{0,16},{16,0},{1,17},{17,1},{2,18},{18,2},{3,19},{19,3},{4,20},{20... | collective-permute-start | bytes 1572872 | tf_op jit(solution)/shard_map/ppermute | solution.py:36
  44.7 13.7 %collective-permute-start.4 = (f16[64,3712]{1,0:T(8,128)(2,1)S(1)}, f16[64,3712]{1,0:T(8,128)(2,1)S(1)}, u32[]{:S(2)}, u32[]{:S(2)}) collective-permute-start(f16[64,3712]{1,0:T(8,128)(2,1)S(1)} %pad_maximum_fusion.24), channel_id=1, source_target_pairs={{0,2},{1,3},{2,0},{3,1},{4,6},{5,7},{6,4},{7,5},{8,10},{9,11},{10,... | collective-permute-start | bytes 1425416 | tf_op jit(solution)/shard_map/ppermute | solution.py:36
  53.6 24.7 %collective-permute-start.7 = (f32[128,3584]{1,0:T(8,128)S(1)}, f32[128,3584]{1,0:T(8,128)S(1)}, u32[]{:S(2)}, u32[]{:S(2)}) collective-permute-start(f32[128,3584]{1,0:T(8,128)S(1)} %slice.325), channel_id=1, source_target_pairs={{0,1},{1,0},{2,3},{3,2},{4,5},{5,4},{6,7},{7,6},{8,9},{9,8},{10,11... | collective-permute-start | bytes 5505032 | tf_op jit(solution)/shard_map/ppermute | solution.py:36
  54.0 26.7 %collective-permute-start.8 = (f16[64,3584]{1,0:T(8,128)(2,1)S(1)}, f16[64,3584]{1,0:T(8,128)(2,1)S(1)}, u32[]{:S(2)}, u32[]{:S(2)}) collective-permute-start(f16[64,3584]{1,0:T(8,128)(2,1)S(1)} %fusion.58), channel_id=1, source_target_pairs={{0,2},{1,3},{2,0},{3,1},{4,6},{5,7},{6,4},{7,5},{8,10},{9,11},{10,... | collective-permute-start | bytes 1376264 | tf_op jit(solution)/shard_map/ppermute | solution.py:36
  78.0 16.7 %collective-permute-start.11 = (f32[128,3584]{1,0:T(8,128)S(1)}, f32[128,3584]{1,0:T(8,128)S(1)}, u32[]{:S(2)}, u32[]{:S(2)}) collective-permute-start(f32[128,3584]{1,0:T(8,128)S(1)} %slice.333), channel_id=1, source_target_pairs={{0,1},{1,0},{2,3},{3,2},{4,5},{5,4},{6,7},{7,6},{8,9},{9,8},{10,11... | collective-permute-start | bytes 5505032 | tf_op jit(solution)/shard_map/ppermute | solution.py:36
  78.4 13.0 %collective-permute-start.13 = (bf16[64,3584]{1,0:T(8,128)(2,1)S(1)}, bf16[64,3584]{1,0:T(8,128)(2,1)S(1)}, u32[]{:S(2)}, u32[]{:S(2)}) collective-permute-start(bf16[64,3584]{1,0:T(8,128)(2,1)S(1)} %fusion.56), channel_id=1, source_target_pairs={{0,2},{1,3},{2,0},{3,1},{4,6},{5,7},{6,4},{7,5},{8,10},{9,11},{10,... | collective-permute-start | bytes 1376264 | tf_op jit(solution)/shard_map/ppermute | solution.py:36
  93.2 13.5 %collective-permute-start.16 = (bf16[64,3584]{1,0:T(8,128)(2,1)S(1)}, bf16[64,3584]{1,0:T(8,128)(2,1)S(1)}, u32[]{:S(2)}, u32[]{:S(2)}) collective-permute-start(bf16[64,3584]{1,0:T(8,128)(2,1)S(1)} %get-tuple-element.83), channel_id=1, source_target_pairs={{0,2},{1,3},{2,0},{3,1},{4,6},{5,7},{6,4},{7,5},{8,10},{9,11},{10,... | collective-permute-start | bytes 1376264 | tf_op jit(solution)/shard_map/ppermute | solution.py:36
  106.7 18.0 %collective-permute-start.14 = (f32[128,3584]{1,0:T(8,128)}, f32[128,3584]{1,0:T(8,128)}, u32[]{:S(2)}, u32[]{:S(2)}) collective-permute-start(f32[128,3584]{1,0:T(8,128)} %slice.343), channel_id=1, source_target_pairs={{0,1},{1,0},{2,3},{3,2},{4,5},{5,4},{6,7},{7,6},{8,9},{9,8},{10,11... | collective-permute-start | bytes 5505032 | tf_op jit(solution)/shard_map/ppermute | solution.py:36
  108.1 15.0 %collective-permute-start.17 = (bf16[128,3584]{1,0:T(8,128)(2,1)}, bf16[128,3584]{1,0:T(8,128)(2,1)}, u32[]{:S(2)}, u32[]{:S(2)}) collective-permute-start(bf16[128,3584]{1,0:T(8,128)(2,1)} %pad_maximum_fusion.14), channel_id=1, source_target_pairs={{0,1},{1,0},{2,3},{3,2},{4,5},{5,4},{6,7},{7,6},{8,9},{9,8},{10,11... | collective-permute-start | bytes 2752520 | tf_op jit(solution)/shard_map/ppermute | solution.py:36
  108.3 13.2 %collective-permute-start.12 = (f16[64,3712]{1,0:T(8,128)(2,1)S(1)}, f16[64,3712]{1,0:T(8,128)(2,1)S(1)}, u32[]{:S(2)}, u32[]{:S(2)}) collective-permute-start(f16[64,3712]{1,0:T(8,128)(2,1)S(1)} %pad_maximum_fusion.25), channel_id=1, source_target_pairs={{0,2},{1,3},{2,0},{3,1},{4,6},{5,7},{6,4},{7,5},{8,10},{9,11},{10,... | collective-permute-start | bytes 1425416 | tf_op jit(solution)/shard_map/ppermute | solution.py:36
  109.7 33.9 %collective-permute-start.23 = (bf16[4,32,2048]{2,1,0:T(8,128)(2,1)}, bf16[4,32,2048]{2,1,0:T(8,128)(2,1)}, u32[]{:S(2)}, u32[]{:S(2)}) collective-permute-start(bf16[4,32,2048]{2,1,0:T(8,128)(2,1)} %collective-permute-done.1), channel_id=1, source_target_pairs={{0,16},{16,0},{1,17},{17,1},{2,18},{18,2},{3,19},{19,3},{4,20},{20... | collective-permute-start | bytes 1572872 | tf_op jit(solution)/shard_map/ppermute | solution.py:36
  111.2 32.4 %collective-permute-start.24 = (bf16[4,32,2048]{2,1,0:T(8,128)(2,1)}, bf16[4,32,2048]{2,1,0:T(8,128)(2,1)}, u32[]{:S(2)}, u32[]{:S(2)}) collective-permute-start(bf16[4,32,2048]{2,1,0:T(8,128)(2,1)} %collective-permute-done.5), channel_id=1, source_target_pairs={{0,16},{16,0},{1,17},{17,1},{2,18},{18,2},{3,19},{19,3},{4,20},{20... | collective-permute-start | bytes 1572872 | tf_op jit(solution)/shard_map/ppermute | solution.py:36
  122.4 21.2 %collective-permute-start.10 = (f16[64,3584]{1,0:T(8,128)(2,1)}, f16[64,3584]{1,0:T(8,128)(2,1)}, u32[]{:S(2)}, u32[]{:S(2)}) collective-permute-start(f16[64,3584]{1,0:T(8,128)(2,1)} %fusion.54), channel_id=1, source_target_pairs={{0,2},{1,3},{2,0},{3,1},{4,6},{5,7},{6,4},{7,5},{8,10},{9,11},{10,... | collective-permute-start | bytes 1376264 | tf_op jit(solution)/shard_map/ppermute | solution.py:36
  123.0 80.8 %all-gather.5.cloned.1.call-start = ((), (), s32[]{:S(2)}) async-start(), calls=%async_computation | async-start | bytes 2752512 | tf_op jit(solution)/shard_map/all_gather | solution.py:210
  127.2 19.6 %collective-permute-start.15 = (bf16[64,3584]{1,0:T(8,128)(2,1)S(1)}, bf16[64,3584]{1,0:T(8,128)(2,1)S(1)}, u32[]{:S(2)}, u32[]{:S(2)}) collective-permute-start(bf16[64,3584]{1,0:T(8,128)(2,1)S(1)} %fusion.49), channel_id=1, source_target_pairs={{0,2},{1,3},{2,0},{3,1},{4,6},{5,7},{6,4},{7,5},{8,10},{9,11},{10,... | collective-permute-start | bytes 1376264 | tf_op jit(solution)/shard_map/ppermute | solution.py:36
  145.2 21.6 %collective-permute-start.30 = (f32[128,3584]{1,0:T(8,128)}, f32[128,3584]{1,0:T(8,128)}, u32[]{:S(2)}, u32[]{:S(2)}) collective-permute-start(f32[128,3584]{1,0:T(8,128)} %slice.359), channel_id=1, source_target_pairs={{0,1},{1,0},{2,3},{3,2},{4,5},{5,4},{6,7},{7,6},{8,9},{9,8},{10,11... | collective-permute-start | bytes 5505032 | tf_op jit(solution)/shard_map/ppermute | solution.py:36
  152.2 13.4 %collective-permute-start.18 = (bf16[64,3584]{1,0:T(8,128)(2,1)S(1)}, bf16[64,3584]{1,0:T(8,128)(2,1)}, u32[]{:S(2)}, u32[]{:S(2)}) collective-permute-start(bf16[64,3584]{1,0:T(8,128)(2,1)S(1)} %get-tuple-element.81), channel_id=1, source_target_pairs={{0,2},{1,3},{2,0},{3,1},{4,6},{5,7},{6,4},{7,5},{8,10},{9,11},{10,... | collective-permute-start | bytes 1376264 | tf_op jit(solution)/shard_map/ppermute | solution.py:36
  158.2 13.0 %collective-permute-start.25 = (f32[128,3584]{1,0:T(8,128)S(1)}, f32[128,3584]{1,0:T(8,128)}, u32[]{:S(2)}, u32[]{:S(2)}) collective-permute-start(f32[128,3584]{1,0:T(8,128)S(1)} %slice.363), channel_id=1, source_target_pairs={{0,1},{1,0},{2,3},{3,2},{4,5},{5,4},{6,7},{7,6},{8,9},{9,8},{10,11... | collective-permute-start | bytes 5505032 | tf_op jit(solution)/shard_map/ppermute | solution.py:36
  161.4 46.4 %collective-permute-start.21 = (bf16[4,32,2048]{2,1,0:T(8,128)(2,1)}, bf16[4,32,2048]{2,1,0:T(8,128)(2,1)}, u32[]{:S(2)}, u32[]{:S(2)}) collective-permute-start(bf16[4,32,2048]{2,1,0:T(8,128)(2,1)} %get-tuple-element.102), channel_id=1, source_target_pairs={{0,8},{4,12},{8,0},{12,4},{1,9},{5,13},{9,1},{13,5},{2,10},{6,14},... | collective-permute-start | bytes 1572872 | tf_op jit(solution)/shard_map/ppermute | solution.py:41
  161.4 46.4 %collective-permute-start.20 = (bf16[4,32,2048]{2,1,0:T(8,128)(2,1)}, bf16[4,32,2048]{2,1,0:T(8,128)(2,1)}, u32[]{:S(2)}, u32[]{:S(2)}) collective-permute-start(bf16[4,32,2048]{2,1,0:T(8,128)(2,1)} %get-tuple-element.101), channel_id=1, source_target_pairs={{0,12},{4,0},{8,4},{12,8},{1,13},{5,1},{9,5},{13,9},{2,14},{6,2},{... | collective-permute-start | bytes 1572872 | tf_op jit(solution)/shard_map/ppermute | solution.py:41
  169.1 15.6 %collective-permute-start.31 = (bf16[64,3584]{1,0:T(8,128)(2,1)}, bf16[64,3584]{1,0:T(8,128)(2,1)}, u32[]{:S(2)}, u32[]{:S(2)}) collective-permute-start(bf16[64,3584]{1,0:T(8,128)(2,1)} %fusion.37), channel_id=1, source_target_pairs={{0,2},{1,3},{2,0},{3,1},{4,6},{5,7},{6,4},{7,5},{8,10},{9,11},{10,... | collective-permute-start | bytes 1376264 | tf_op jit(solution)/shard_map/ppermute | solution.py:36
  173.6 30.3 %collective-permute-start.26 = (bf16[64,3584]{1,0:T(8,128)(2,1)}, bf16[64,3584]{1,0:T(8,128)(2,1)S(1)}, u32[]{:S(2)}, u32[]{:S(2)}) collective-permute-start(bf16[64,3584]{1,0:T(8,128)(2,1)} %fusion.41), channel_id=1, source_target_pairs={{0,2},{1,3},{2,0},{3,1},{4,6},{5,7},{6,4},{7,5},{8,10},{9,11},{10,... | collective-permute-start | bytes 1376264 | tf_op jit(solution)/shard_map/ppermute | solution.py:36
  186.7 15.3 %collective-permute-start.32 = (bf16[64,3584]{1,0:T(8,128)(2,1)S(1)}, bf16[64,3584]{1,0:T(8,128)(2,1)S(1)}, u32[]{:S(2)}, u32[]{:S(2)}) collective-permute-start(bf16[64,3584]{1,0:T(8,128)(2,1)S(1)} %fusion.40), channel_id=1, source_target_pairs={{0,2},{1,3},{2,0},{3,1},{4,6},{5,7},{6,4},{7,5},{8,10},{9,11},{10,... | collective-permute-start | bytes 1376264 | tf_op jit(solution)/shard_map/ppermute | solution.py:36
  190.9 16.9 %collective-permute-start.22 = (bf16[4,32,2048]{2,1,0:T(8,128)(2,1)}, bf16[4,32,2048]{2,1,0:T(8,128)(2,1)}, u32[]{:S(2)}, u32[]{:S(2)}) collective-permute-start(bf16[4,32,2048]{2,1,0:T(8,128)(2,1)} %fusion.59), channel_id=1, source_target_pairs={{0,4},{4,8},{8,12},{12,0},{1,5},{5,9},{9,13},{13,1},{2,6},{6,10},{... | collective-permute-start | bytes 1572872 | tf_op jit(solution)/shard_map/ppermute | solution.py:41
  206.0 39.2 %collective-permute-start.27 = (bf16[64,3584]{1,0:T(8,128)(2,1)S(1)}, bf16[64,3584]{1,0:T(8,128)(2,1)S(1)}, u32[]{:S(2)}, u32[]{:S(2)}) collective-permute-start(bf16[64,3584]{1,0:T(8,128)(2,1)S(1)} %fusion.44), channel_id=1, source_target_pairs={{0,2},{1,3},{2,0},{3,1},{4,6},{5,7},{6,4},{7,5},{8,10},{9,11},{10,... | collective-permute-start | bytes 1376264 | tf_op jit(solution)/shard_map/ppermute | solution.py:36
  209.6 16.6 %collective-permute-start.34 = (bf16[4,32,2048]{2,1,0:T(8,128)(2,1)S(1)}, bf16[4,32,2048]{2,1,0:T(8,128)(2,1)S(1)}, u32[]{:S(2)}, u32[]{:S(2)}) collective-permute-start(bf16[4,32,2048]{2,1,0:T(8,128)(2,1)S(1)} %fusion.20), channel_id=1, source_target_pairs={{0,4},{4,8},{8,12},{12,0},{1,5},{5,9},{9,13},{13,1},{2,6},{6,10},{... | collective-permute-start | bytes 1572872 | tf_op jit(solution)/shard_map/ppermute | solution.py:41
  212.9 23.9 %collective-permute-start.29 = (bf16[4,32,2048]{2,1,0:T(8,128)(2,1)S(1)}, bf16[4,32,2048]{2,1,0:T(8,128)(2,1)S(1)}, u32[]{:S(2)}, u32[]{:S(2)}) collective-permute-start(bf16[4,32,2048]{2,1,0:T(8,128)(2,1)S(1)} %fusion.20), channel_id=1, source_target_pairs={{0,12},{4,0},{8,4},{12,8},{1,13},{5,1},{9,5},{13,9},{2,14},{6,2},{... | collective-permute-start | bytes 1572872 | tf_op jit(solution)/shard_map/ppermute | solution.py:41
  246.0 15.6 %collective-permute-start.36 = (bf16[4,32,2048]{2,1,0:T(8,128)(2,1)S(1)}, bf16[4,32,2048]{2,1,0:T(8,128)(2,1)S(1)}, u32[]{:S(2)}, u32[]{:S(2)}) collective-permute-start(bf16[4,32,2048]{2,1,0:T(8,128)(2,1)S(1)} %copy-done.49), channel_id=1, source_target_pairs={{0,12},{4,0},{8,4},{12,8},{1,13},{5,1},{9,5},{13,9},{2,14},{6,2},{... | collective-permute-start | bytes 1572872 | tf_op jit(solution)/shard_map/ppermute | solution.py:41
  248.4 46.1 %collective-permute-start.40 = (bf16[4,32,2048]{2,1,0:T(8,128)(2,1)S(1)}, bf16[4,32,2048]{2,1,0:T(8,128)(2,1)S(1)}, u32[]{:S(2)}, u32[]{:S(2)}) collective-permute-start(bf16[4,32,2048]{2,1,0:T(8,128)(2,1)S(1)} %get-tuple-element.100), channel_id=1, source_target_pairs={{0,8},{4,12},{8,0},{12,4},{1,9},{5,13},{9,1},{13,5},{2,10},{6,14},... | collective-permute-start | bytes 1572872 | tf_op jit(solution)/shard_map/ppermute | solution.py:41
  248.4 34.8 %collective-permute-start.37 = (bf16[4,32,2048]{2,1,0:T(8,128)(2,1)S(1)}, bf16[4,32,2048]{2,1,0:T(8,128)(2,1)S(1)}, u32[]{:S(2)}, u32[]{:S(2)}) collective-permute-start(bf16[4,32,2048]{2,1,0:T(8,128)(2,1)S(1)} %copy-done.47), channel_id=1, source_target_pairs={{0,12},{4,0},{8,4},{12,8},{1,13},{5,1},{9,5},{13,9},{2,14},{6,2},{... | collective-permute-start | bytes 1572872 | tf_op jit(solution)/shard_map/ppermute | solution.py:41
  250.8 43.7 %collective-permute-start.38 = (bf16[64,3584]{1,0:T(8,128)(2,1)S(1)}, bf16[64,3584]{1,0:T(8,128)(2,1)}, u32[]{:S(2)}, u32[]{:S(2)}) collective-permute-start(bf16[64,3584]{1,0:T(8,128)(2,1)S(1)} %fusion.36), channel_id=1, source_target_pairs={{0,2},{1,3},{2,0},{3,1},{4,6},{5,7},{6,4},{7,5},{8,10},{9,11},{10,... | collective-permute-start | bytes 1376264 | tf_op jit(solution)/shard_map/ppermute | solution.py:36
  271.1 49.8 %collective-permute-start.41 = (bf16[4,32,2048]{2,1,0:T(8,128)(2,1)}, bf16[4,32,2048]{2,1,0:T(8,128)(2,1)}, u32[]{:S(2)}, u32[]{:S(2)}) collective-permute-start(bf16[4,32,2048]{2,1,0:T(8,128)(2,1)} %fusion.60), channel_id=1, source_target_pairs={{0,4},{4,8},{8,12},{12,0},{1,5},{5,9},{9,13},{13,1},{2,6},{6,10},{... | collective-permute-start | bytes 1572872 | tf_op jit(solution)/shard_map/ppermute | solution.py:41
  306.2 27.4 %collective-permute-start.43 = (f32[128,3584]{1,0:T(8,128)S(1)}, f32[128,3584]{1,0:T(8,128)S(1)}, u32[]{:S(2)}, u32[]{:S(2)}) collective-permute-start(f32[128,3584]{1,0:T(8,128)S(1)} %slice.382), channel_id=1, source_target_pairs={{0,1},{1,0},{2,3},{3,2},{4,5},{5,4},{6,7},{7,6},{8,9},{9,8},{10,11... | collective-permute-start | bytes 5505032 | tf_op jit(solution)/shard_map/ppermute | solution.py:36
  307.8 13.1 %collective-permute-start.39 = (bf16[64,3584]{1,0:T(8,128)(2,1)S(1)}, bf16[64,3584]{1,0:T(8,128)(2,1)S(1)}, u32[]{:S(2)}, u32[]{:S(2)}) collective-permute-start(bf16[64,3584]{1,0:T(8,128)(2,1)S(1)} %fusion.35), channel_id=1, source_target_pairs={{0,2},{1,3},{2,0},{3,1},{4,6},{5,7},{6,4},{7,5},{8,10},{9,11},{10,... | collective-permute-start | bytes 1376264 | tf_op jit(solution)/shard_map/ppermute | solution.py:36
  322.5 23.4 %collective-permute-start.48 = (bf16[4,32,2048]{2,1,0:T(8,128)(2,1)S(1)}, bf16[4,32,2048]{2,1,0:T(8,128)(2,1)S(1)}, u32[]{:S(2)}, u32[]{:S(2)}) collective-permute-start(bf16[4,32,2048]{2,1,0:T(8,128)(2,1)S(1)} %fusion.15), channel_id=1, source_target_pairs={{0,4},{4,8},{8,12},{12,0},{1,5},{5,9},{9,13},{13,1},{2,6},{6,10},{... | collective-permute-start | bytes 1572872 | tf_op jit(solution)/shard_map/ppermute | solution.py:41
  333.6 22.4 %collective-permute-start.47 = (bf16[4,32,2048]{2,1,0:T(8,128)(2,1)S(1)}, bf16[4,32,2048]{2,1,0:T(8,128)(2,1)S(1)}, u32[]{:S(2)}, u32[]{:S(2)}) collective-permute-start(bf16[4,32,2048]{2,1,0:T(8,128)(2,1)S(1)} %fusion.15), channel_id=1, source_target_pairs={{0,12},{4,0},{8,4},{12,8},{1,13},{5,1},{9,5},{13,9},{2,14},{6,2},{... | collective-permute-start | bytes 1572872 | tf_op jit(solution)/shard_map/ppermute | solution.py:41
  368.2 32.2 %collective-permute-start.42 = (bf16[128,3584]{1,0:T(8,128)(2,1)}, bf16[128,3584]{1,0:T(8,128)(2,1)}, u32[]{:S(2)}, u32[]{:S(2)}) collective-permute-start(bf16[128,3584]{1,0:T(8,128)(2,1)} %pad_maximum_fusion.18), channel_id=1, source_target_pairs={{0,1},{1,0},{2,3},{3,2},{4,5},{5,4},{6,7},{7,6},{8,9},{9,8},{10,11... | collective-permute-start | bytes 2752520 | tf_op jit(solution)/shard_map/ppermute | solution.py:36
  368.7 15.8 %collective-permute-start.53 = (bf16[4,32,2048]{2,1,0:T(8,128)(2,1)S(1)}, bf16[4,32,2048]{2,1,0:T(8,128)(2,1)S(1)}, u32[]{:S(2)}, u32[]{:S(2)}) collective-permute-start(bf16[4,32,2048]{2,1,0:T(8,128)(2,1)S(1)} %collective-permute-done.47), channel_id=1, source_target_pairs={{0,12},{4,0},{8,4},{12,8},{1,13},{5,1},{9,5},{13,9},{2,14},{6,2},{... | collective-permute-start | bytes 1572872 | tf_op jit(solution)/shard_map/ppermute | solution.py:41
  373.4 12.3 %collective-permute-start.45 = (bf16[64,3584]{1,0:T(8,128)(2,1)S(1)}, bf16[64,3584]{1,0:T(8,128)(2,1)}, u32[]{:S(2)}, u32[]{:S(2)}) collective-permute-start(bf16[64,3584]{1,0:T(8,128)(2,1)S(1)} %fusion.32), channel_id=1, source_target_pairs={{0,2},{1,3},{2,0},{3,1},{4,6},{5,7},{6,4},{7,5},{8,10},{9,11},{10,... | collective-permute-start | bytes 1376264 | tf_op jit(solution)/shard_map/ppermute | solution.py:36
  403.4 42.9 %collective-permute-start.46 = (bf16[128,3584]{1,0:T(8,128)(2,1)S(1)}, bf16[128,3584]{1,0:T(8,128)(2,1)S(1)}, u32[]{:S(2)}, u32[]{:S(2)}) collective-permute-start(bf16[128,3584]{1,0:T(8,128)(2,1)S(1)} %pad_maximum_fusion.19), channel_id=1, source_target_pairs={{0,1},{1,0},{2,3},{3,2},{4,5},{5,4},{6,7},{7,6},{8,9},{9,8},{10,11... | collective-permute-start | bytes 2752520 | tf_op jit(solution)/shard_map/ppermute | solution.py:36
  404.0 13.6 %collective-permute-start.50 = (bf16[64,3584]{1,0:T(8,128)(2,1)}, bf16[64,3584]{1,0:T(8,128)(2,1)S(1)}, u32[]{:S(2)}, u32[]{:S(2)}) collective-permute-start(bf16[64,3584]{1,0:T(8,128)(2,1)} %fusion.25), channel_id=1, source_target_pairs={{0,2},{1,3},{2,0},{3,1},{4,6},{5,7},{6,4},{7,5},{8,10},{9,11},{10,... | collective-permute-start | bytes 1376264 | tf_op jit(solution)/shard_map/ppermute | solution.py:36
  406.7 20.7 %collective-permute-start.55 = (bf16[64,3584]{1,0:T(8,128)(2,1)S(1)}, bf16[64,3584]{1,0:T(8,128)(2,1)S(1)}, u32[]{:S(2)}, u32[]{:S(2)}) collective-permute-start(bf16[64,3584]{1,0:T(8,128)(2,1)S(1)} %fusion.21), channel_id=1, source_target_pairs={{0,2},{1,3},{2,0},{3,1},{4,6},{5,7},{6,4},{7,5},{8,10},{9,11},{10,... | collective-permute-start | bytes 1376264 | tf_op jit(solution)/shard_map/ppermute | solution.py:36
  419.0 18.2 %collective-permute-start.51 = (bf16[64,3584]{1,0:T(8,128)(2,1)S(1)}, bf16[64,3584]{1,0:T(8,128)(2,1)S(1)}, u32[]{:S(2)}, u32[]{:S(2)}) collective-permute-start(bf16[64,3584]{1,0:T(8,128)(2,1)S(1)} %fusion.28), channel_id=1, source_target_pairs={{0,2},{1,3},{2,0},{3,1},{4,6},{5,7},{6,4},{7,5},{8,10},{9,11},{10,... | collective-permute-start | bytes 1376264 | tf_op jit(solution)/shard_map/ppermute | solution.py:36
  428.8 17.4 %collective-permute-start.56 = (bf16[64,3584]{1,0:T(8,128)(2,1)S(1)}, bf16[64,3584]{1,0:T(8,128)(2,1)S(1)}, u32[]{:S(2)}, u32[]{:S(2)}) collective-permute-start(bf16[64,3584]{1,0:T(8,128)(2,1)S(1)} %fusion.24), channel_id=1, source_target_pairs={{0,2},{1,3},{2,0},{3,1},{4,6},{5,7},{6,4},{7,5},{8,10},{9,11},{10,... | collective-permute-start | bytes 1376264 | tf_op jit(solution)/shard_map/ppermute | solution.py:36
  (72 other events, 687.8 us)
Sparse Core Ops, SparseCore 0:
  123.2 31.7 all-gather.6
  165.7 30.1 all-gather.4

commit v13 on v11

--- a/solution.py
+++ b/solution.py
@@ -270,13 +270,12 @@
     first, sent, got, near = back(0, tail, pieces, ready + pieces[:1])
     ready = [out_sums(1, tail, hidden[tail][0], sent)]
     others = scaled_pieces(1, near)
-    after = ready + got + others[last:]
+    after = ready + got + others[:1]
     for j in reversed(range(tail)):
-        _, _, after, near = back(0, j, pieces, after)
-    after = after + others[:1]
+        first, _, _, _ = back(0, j, pieces, after)
+    after = others[:1] + first
     for j in reversed(range(GROUPS)):
-        _, after, _, _ = back(1, j, others, after)
-        after = after + near
+        _, _, after, _ = back(1, j, others, after)
     return last_product(turned, bars, tokens)
 
 

time: 467 us -> 475 us (1.017)
  starting transfers between devices: 63.1 us -> 82.5 us
  waiting for transfers between devices: 170 us -> 156 us
    ppermute x15, waiting for transfers between devices: 87.6 us -> 65.7 us  [shift(): lax.ppermute(values, axis, [(i, (i + by) % count) for i in range(count)])]
    ppermute x15, starting transfers between devices: 34.2 us -> 55 us  [shift(): lax.ppermute(values, axis, [(i, (i + by) % count) for i in range(count)])]
    ppermute x43, waiting for transfers between devices: 82.4 us -> 90.7 us  [swap(): return lax.ppermute(values, axis, [(i, i ^ mask) for i in range(count)])]
    unnamed x116 -> x114, local copies, waits for them, and re-layouts: 10.7 us -> 9.09 us
  transfers between devices with their start and end apart: 60 -> 60, of which waited for: 27 -> 25; matrix products, arithmetic and copies ran while one was open for 33% -> 35% of each run, Pallas kernels for 0% -> 0%
where the time goes in v13:
time: 475 us; the launch traced here: 471 us
  waiting for transfers between devices  156 us (33%)
  matrix products  116 us (24%)
  starting transfers between devices  82.5 us (17%)
  other arithmetic  44.7 us (9%)
  local copies, waits for them, and re-layouts  34.5 us (7%)
  Pallas kernels  22.5 us (5%)
  between operations  14.9 us (3%)
    ppermute x43, waiting for transfers between devices, swap(): return lax.ppermute(values, axis, [(i, i ^ mask) for i in range(count)])  90.7 us
    dot_general x12, matrix products, matmul(): return jnp.dot(left, right, preferred_element_type=jnp.float32)  83.8 us
    ppermute x15, waiting for transfers between devices, shift(): lax.ppermute(values, axis, [(i, (i + by) % count) for i in range(count)])  65.7 us
    ppermute x15, starting transfers between devices, shift(): lax.ppermute(values, axis, [(i, (i + by) % count) for i in range(count)])  55 us
    dot_general x4, matrix products, times_down(): lax.dot_general(left, w_down, (((1,), (1,)), ((), ())), preferred_element...  31.9 us
    ppermute x43, starting transfers between devices, swap(): return lax.ppermute(values, axis, [(i, i ^ mask) for i in range(count)])  27.5 us
    pallas_call x1, Pallas kernels, last_product(): pl.pallas_call(functools.partial(last_kernel, 1.0 / tokens, len(turned)),...  22.5 us
    slice x12, local copies, waits for them, and re-layouts, sum_over_col(): first = part[half:]  12.4 us
  transfers between devices with their start and end apart: 60, of which 25 were waited for; matrix products, arithmetic and copies ran while one was open for 35% of the time, Pallas kernels for 0%

profile of v13, /device:TPU:0, one launch (start us, length us, event | category | flops | bytes accessed | tf_op | source)
XLA Modules:
  0.0 471.3 jit_solution(2044444210500993651)
XLA Ops:
  8.7 3.1 collective-permute-start
  11.8 13.9 %collective-permute-done = bf16[4,32,2048]{2,1,0:T(8,128)(2,1)S(1)} collective-permute-done((bf16[4,32,2048]{2,1,0:T(8,128)(2,1)S(1)}, bf16[4,32,2048]{2,1,0:T(8,128)(2,1)S(1)}, u32[]{:S(2)}, u32[]{:S(2)}) %collective-permute-start) | collective-permute-done | bytes 524320 | tf_op jit(solution)/shard_map/ppermute | solution.py:41
  26.5 7.2 %fusion.86 = f32[256,3584]{1,0:T(8,128)S(1)} fusion(bf16[256,2048]{1,0:T(8,128)(2,1)S(1)} %bitcast.130, bf16[2048,3584]{1,0:T(8,128)(2,1)} %param.8), kind=kOutput, calls=%fused_computation.192 | convolution fusion | flops 3758096384 | bytes 19398656 | tf_op jit(solution)/shard_map/dot_general | solution.py:19
  38.2 2.9 dynamic-slice_bitcast_fusion.3
  44.7 7.2 %fusion.85 = f32[256,3584]{1,0:T(8,128)S(1)} fusion(bf16[256,2048]{1,0:T(8,128)(2,1)S(1)} %bitcast.131, bf16[2048,3584]{1,0:T(8,128)(2,1)} %param.7), kind=kOutput, calls=%fused_computation.191 | convolution fusion | flops 3758096384 | bytes 19398656 | tf_op jit(solution)/shard_map/dot_general | solution.py:19
  56.7 7.2 %fusion.87 = f32[256,3584]{1,0:T(8,128)S(1)} fusion(bf16[256,2048]{1,0:T(8,128)(2,1)S(1)} %bitcast.132, bf16[2048,3584]{1,0:T(8,128)(2,1)} %param.10), kind=kOutput, calls=%fused_computation.193 | convolution fusion | flops 3758096384 | bytes 19398656 | tf_op jit(solution)/shard_map/dot_general | solution.py:19
  64.9 3.3 collective-permute-done.4
  68.2 9.2 %collective-permute-done.1 = bf16[4,32,2048]{2,1,0:T(8,128)(2,1)} collective-permute-done((bf16[4,32,2048]{2,1,0:T(8,128)(2,1)S(1)}, bf16[4,32,2048]{2,1,0:T(8,128)(2,1)}, u32[]{:S(2)}, u32[]{:S(2)}) %collective-permute-start.1) | collective-permute-done | bytes 524320 | tf_op jit(solution)/shard_map/ppermute | solution.py:41
  78.7 7.3 %fusion.89 = f32[256,3584]{1,0:T(8,128)S(1)} fusion(bf16[256,2048]{1,0:T(8,128)(2,1)S(1)} %bitcast.134, bf16[2048,3584]{1,0:T(8,128)(2,1)} %param.8), kind=kOutput, calls=%fused_computation.195 | convolution fusion | flops 3758096384 | bytes 19398656 | tf_op jit(solution)/shard_map/dot_general | solution.py:19
  90.2 7.3 %fusion.88 = f32[256,3584]{1,0:T(8,128)S(1)} fusion(bf16[256,2048]{1,0:T(8,128)(2,1)S(1)} %bitcast.135, bf16[2048,3584]{1,0:T(8,128)(2,1)} %param.7), kind=kOutput, calls=%fused_computation.194 | convolution fusion | flops 3758096384 | bytes 19398656 | tf_op jit(solution)/shard_map/dot_general | solution.py:19
  106.3 7.6 %fusion.90 = f32[256,3584]{1,0:T(8,128)S(1)} fusion(bf16[256,2048]{1,0:T(8,128)(2,1)S(1)} %bitcast.136, bf16[2048,3584]{1,0:T(8,128)(2,1)} %param.10), kind=kOutput, calls=%fused_computation.196 | convolution fusion | flops 3758096384 | bytes 19398656 | tf_op jit(solution)/shard_map/dot_general | solution.py:19
  118.4 6.3 %collective-permute-done.12 = f16[64,3712]{1,0:T(8,128)(2,1)} collective-permute-done((f16[64,3712]{1,0:T(8,128)(2,1)}, f16[64,3712]{1,0:T(8,128)(2,1)}, u32[]{:S(2)}, u32[]{:S(2)}) %collective-permute-start.12) | collective-permute-done | bytes 475168 | tf_op jit(solution)/shard_map/ppermute | solution.py:36
  130.4 7.7 %convolution_convert_fusion.1 = bf16[256,2048]{1,0:T(8,128)(2,1)S(1)} fusion(bf16[256,3584]{1,0:T(8,128)(2,1)S(1)} %pad_maximum_fusion, bf16[3584,2048]{1,0:T(8,128)(2,1)} %param.9), kind=kOutput, calls=%fused_computation.1 | convolution fusion | flops 3758620672 | bytes 17563648 | tf_op jit(solution)/shard_map/dot_general | solution.py:19
  139.4 3.9 fusion.91
  144.9 3.6 collective-permute-start.20
  150.7 3.9 fusion.92
  156.3 5.3 %collective-permute-done.15 = bf16[64,3584]{1,0:T(8,128)(2,1)S(1)} collective-permute-done((bf16[64,3584]{1,0:T(8,128)(2,1)S(1)}, bf16[64,3584]{1,0:T(8,128)(2,1)S(1)}, u32[]{:S(2)}, u32[]{:S(2)}) %collective-permute-start.15) | collective-permute-done | bytes 458784 | tf_op jit(solution)/shard_map/ppermute | solution.py:36
  161.7 3.6 multiply_convert_fusion
  166.0 2.3 fusion.37
  169.7 9.0 %collective-permute-done.18 = bf16[64,3584]{1,0:T(8,128)(2,1)S(1)} collective-permute-done((bf16[64,3584]{1,0:T(8,128)(2,1)S(1)}, bf16[64,3584]{1,0:T(8,128)(2,1)S(1)}, u32[]{:S(2)}, u32[]{:S(2)}) %collective-permute-start.18) | collective-permute-done | bytes 458784 | tf_op jit(solution)/shard_map/ppermute | solution.py:36
  179.7 7.6 %collective-permute-done.31 = bf16[64,3584]{1,0:T(8,128)(2,1)S(1)} collective-permute-done((bf16[64,3584]{1,0:T(8,128)(2,1)}, bf16[64,3584]{1,0:T(8,128)(2,1)S(1)}, u32[]{:S(2)}, u32[]{:S(2)}) %collective-permute-start.31) | collective-permute-done | bytes 458784 | tf_op jit(solution)/shard_map/ppermute | solution.py:36
  193.8 7.7 %fusion = f32[256,2048]{1,0:T(8,128)S(1)} fusion(bf16[3584,2048]{1,0:T(8,128)(2,1)} %param.9, bf16[128,3584]{1,0:T(8,128)(2,1)} %collective-permute-done.19, bf16[64,3584]{1,0:T(8,128)(2,1)S(1)} %collective-permute-done.18, bf16[64,3584]{1,0:T(8,128)(2,1)S(1)} %get-tuple-element.81), kind=kOutput, calls=%fused_computation.3 | convolution fusion | flops 3763601408 | bytes 18612224 | tf_op jit(solution)/shard_map/dot_general | solution.py:19
  202.5 2.9 collective-permute-start.22
  206.6 4.9 %collective-permute-done.26 = bf16[64,3584]{1,0:T(8,128)(2,1)} collective-permute-done((bf16[64,3584]{1,0:T(8,128)(2,1)S(1)}, bf16[64,3584]{1,0:T(8,128)(2,1)}, u32[]{:S(2)}, u32[]{:S(2)}) %collective-permute-start.26) | collective-permute-done | bytes 458784 | tf_op jit(solution)/shard_map/ppermute | solution.py:36
  214.4 2.4 collective-permute-done.22
  219.7 2.8 collective-permute-start.29
  222.5 9.4 %convolution_convert_fusion = bf16[256,2048]{1,0:T(8,128)(2,1)S(1)} fusion(bf16[3584,2048]{1,0:T(8,128)(2,1)} %param.9, bf16[128,3584]{1,0:T(8,128)(2,1)} %collective-permute-done.33, bf16[64,3584]{1,0:T(8,128)(2,1)S(1)} %copy-done.51, bf16[64,3584]{1,0:T(8,128)(2,1)S(1)} %fusion.40), kind=kOutput, calls=%fused_computation | convolution fusion | flops 3764125696 | bytes 17563648 | tf_op jit(solution)/shard_map/dot_general | solution.py:19
  233.0 2.4 collective-permute-done.34
  235.3 6.5 %collective-permute-done.29 = bf16[4,32,2048]{2,1,0:T(8,128)(2,1)S(1)} collective-permute-done((bf16[4,32,2048]{2,1,0:T(8,128)(2,1)S(1)}, bf16[4,32,2048]{2,1,0:T(8,128)(2,1)S(1)}, u32[]{:S(2)}, u32[]{:S(2)}) %collective-permute-start.29) | collective-permute-done | bytes 524320 | tf_op jit(solution)/shard_map/ppermute | solution.py:41
  242.7 7.3 %fusion.93 = f32[256,3584]{1,0:T(8,128)S(1)} fusion(bf16[256,2048]{1,0:T(8,128)(2,1)S(1)} %bitcast.154, bf16[3584,2048]{1,0:T(8,128)(2,1)} %param.9), kind=kOutput, calls=%fused_computation.199 | convolution fusion | flops 3758096384 | bytes 19398656 | tf_op jit(solution)/shard_map/dot_general | solution.py:23
  256.7 7.2 %fusion.94 = f32[256,2048]{1,0:T(8,128)S(1)} fusion(bf16[256,3584]{1,0:T(8,128)(2,1)S(1)} %pad_maximum_fusion.1, bf16[3584,2048]{1,0:T(8,128)(2,1)} %param.9), kind=kOutput, calls=%fused_computation.200 | convolution fusion | flops 3758096384 | bytes 18612224 | tf_op jit(solution)/shard_map/dot_general | solution.py:19
  264.5 3.7 collective-permute-done.37
  272.8 5.8 %collective-permute-done.39 = bf16[4,32,2048]{2,1,0:T(8,128)(2,1)S(1)} collective-permute-done((bf16[4,32,2048]{2,1,0:T(8,128)(2,1)S(1)}, bf16[4,32,2048]{2,1,0:T(8,128)(2,1)S(1)}, u32[]{:S(2)}, u32[]{:S(2)}) %collective-permute-start.39) | collective-permute-done | bytes 524320 | tf_op jit(solution)/shard_map/ppermute | solution.py:41
  278.6 2.8 collective-permute-done.38
  281.4 7.0 %collective-permute-done.36 = bf16[4,32,2048]{2,1,0:T(8,128)(2,1)S(1)} collective-permute-done((bf16[4,32,2048]{2,1,0:T(8,128)(2,1)S(1)}, bf16[4,32,2048]{2,1,0:T(8,128)(2,1)S(1)}, u32[]{:S(2)}, u32[]{:S(2)}) %collective-permute-start.36) | collective-permute-done | bytes 524320 | tf_op jit(solution)/shard_map/ppermute | solution.py:41
  290.1 20.2 %collective-permute-start.42 = (bf16[4,32,2048]{2,1,0:T(8,128)(2,1)S(1)}, bf16[4,32,2048]{2,1,0:T(8,128)(2,1)S(1)}, u32[]{:S(2)}, u32[]{:S(2)}) collective-permute-start(bf16[4,32,2048]{2,1,0:T(8,128)(2,1)S(1)} %fusion.15), channel_id=1, source_target_pairs={{0,4},{4,8},{8,12},{12,0},{1,5},{5,9},{9,13},{13,1},{2,6},{6,10},{... | collective-permute-start | bytes 1572872 | tf_op jit(solution)/shard_map/ppermute | solution.py:41
  312.6 12.8 %collective-permute-done.42 = bf16[4,32,2048]{2,1,0:T(8,128)(2,1)S(1)} collective-permute-done((bf16[4,32,2048]{2,1,0:T(8,128)(2,1)S(1)}, bf16[4,32,2048]{2,1,0:T(8,128)(2,1)S(1)}, u32[]{:S(2)}, u32[]{:S(2)}) %collective-permute-start.42) | collective-permute-done | bytes 524320 | tf_op jit(solution)/shard_map/ppermute | solution.py:41
  326.5 7.8 %fusion.95 = f32[256,3584]{1,0:T(8,128)S(1)} fusion(bf16[256,2048]{1,0:T(8,128)(2,1)} %bitcast.152, bf16[3584,2048]{1,0:T(8,128)(2,1)} %param.9), kind=kOutput, calls=%fused_computation.201 | convolution fusion | flops 3758096384 | bytes 19398656 | tf_op jit(solution)/shard_map/dot_general | solution.py:23
  337.2 7.6 %fusion.96 = f32[256,3584]{1,0:T(8,128)S(1)} fusion(bf16[256,2048]{1,0:T(8,128)(2,1)} %bitcast.155, bf16[3584,2048]{1,0:T(8,128)(2,1)} %param.9), kind=kOutput, calls=%fused_computation.202 | convolution fusion | flops 3758096384 | bytes 19398656 | tf_op jit(solution)/shard_map/dot_general | solution.py:23
  352.9 11.7 %collective-permute-start.53 = (bf16[4,32,2048]{2,1,0:T(8,128)(2,1)}, bf16[4,32,2048]{2,1,0:T(8,128)(2,1)S(1)}, u32[]{:S(2)}, u32[]{:S(2)}) collective-permute-start(bf16[4,32,2048]{2,1,0:T(8,128)(2,1)} %copy-done.49), channel_id=1, source_target_pairs={{0,12},{4,0},{8,4},{12,8},{1,13},{5,1},{9,5},{13,9},{2,14},{6,2},{... | collective-permute-start | bytes 1572872 | tf_op jit(solution)/shard_map/ppermute | solution.py:41
  369.0 2.3 fusion.29
  372.2 4.4 collective-permute-done.53
  376.6 4.8 %collective-permute-done.50 = bf16[64,3584]{1,0:T(8,128)(2,1)} collective-permute-done((bf16[64,3584]{1,0:T(8,128)(2,1)S(1)}, bf16[64,3584]{1,0:T(8,128)(2,1)}, u32[]{:S(2)}, u32[]{:S(2)}) %collective-permute-start.50) | collective-permute-done | bytes 458784 | tf_op jit(solution)/shard_map/ppermute | solution.py:36
  381.5 9.2 %fusion.97 = f32[256,3584]{1,0:T(8,128)} fusion(bf16[256,2048]{1,0:T(8,128)(2,1)S(1)} %bitcast.153, bf16[3584,2048]{1,0:T(8,128)(2,1)} %param.9), kind=kOutput, calls=%fused_computation.203 | convolution fusion | flops 3758096384 | bytes 19398656 | tf_op jit(solution)/shard_map/dot_general | solution.py:23
  399.6 8.1 %collective-permute-done.46 = bf16[64,3584]{1,0:T(8,128)(2,1)S(1)} collective-permute-done((bf16[64,3584]{1,0:T(8,128)(2,1)S(1)}, bf16[64,3584]{1,0:T(8,128)(2,1)S(1)}, u32[]{:S(2)}, u32[]{:S(2)}) %collective-permute-start.46) | collective-permute-done | bytes 458784 | tf_op jit(solution)/shard_map/ppermute | solution.py:36
  407.8 19.0 %collective-permute-done.55 = bf16[64,3584]{1,0:T(8,128)(2,1)S(1)} collective-permute-done((bf16[64,3584]{1,0:T(8,128)(2,1)S(1)}, bf16[64,3584]{1,0:T(8,128)(2,1)S(1)}, u32[]{:S(2)}, u32[]{:S(2)}) %collective-permute-start.55) | collective-permute-done | bytes 458784 | tf_op jit(solution)/shard_map/ppermute | solution.py:36
  428.3 10.7 %collective-permute-done.56 = bf16[64,3584]{1,0:T(8,128)(2,1)S(1)} collective-permute-done((bf16[64,3584]{1,0:T(8,128)(2,1)S(1)}, bf16[64,3584]{1,0:T(8,128)(2,1)S(1)}, u32[]{:S(2)}, u32[]{:S(2)}) %collective-permute-start.56) | collective-permute-done | bytes 458784 | tf_op jit(solution)/shard_map/ppermute | solution.py:36
  441.7 22.5 %shard_map.64 = f32[2048,3584]{1,0:T(8,128)} custom-call(bf16[2048,256]{1,0:T(8,128)(2,1)S(1)} %bitcast.127, bf16[2048,256]{1,0:T(8,128)(2,1)S(1)} %bitcast.126, bf16[2048,256]{1,0:T(8,128)(2,1)S(1)} %bitcast.129, bf16[2048,256]{1,0:T(8,128)(2,1)S(1)} %bitcast.128, bf16[256,3584]{1,0:T(8,128)(2,1)S(1)} %pad_maximum_fusion.2.refs_4_, ...), custom_call_target="tpu_custom_call" | custom-call | flops 15032385536 | bytes 40894464 | tf_op jit(solution)/shard_map/pallas_call | solution.py:91
  (291 shorter events, 112.8 us)
Async XLA Ops:
  6.5 173.1 %all-gather.7.cloned.1.call-start = ((), (), s32[]{:S(2)}) async-start(), calls=%async_computation.1 | async-start | bytes 2752512 | tf_op jit(solution)/shard_map/all_gather | solution.py:210
  8.7 17.0 %collective-permute-start = (bf16[4,32,2048]{2,1,0:T(8,128)(2,1)S(1)}, bf16[4,32,2048]{2,1,0:T(8,128)(2,1)S(1)}, u32[]{:S(2)}, u32[]{:S(2)}) collective-permute-start(bf16[4,32,2048]{2,1,0:T(8,128)(2,1)S(1)} %pad_maximum_fusion.22), channel_id=1, source_target_pairs={{0,4},{4,8},{8,12},{12,0},{1,5},{5,9},{9,13},{13,1},{2,6},{6,10},{... | collective-permute-start | bytes 1572872 | tf_op jit(solution)/shard_map/ppermute | solution.py:41
  37.0 15.2 %collective-permute-start.3 = (f32[128,3584]{1,0:T(8,128)}, f32[128,3584]{1,0:T(8,128)S(1)}, u32[]{:S(2)}, u32[]{:S(2)}) collective-permute-start(f32[128,3584]{1,0:T(8,128)} %slice.322), channel_id=1, source_target_pairs={{0,1},{1,0},{2,3},{3,2},{4,5},{5,4},{6,7},{7,6},{8,9},{9,8},{10,11... | collective-permute-start | bytes 5505032 | tf_op jit(solution)/shard_map/ppermute | solution.py:36
  41.1 23.1 %collective-permute-start.5 = (bf16[4,32,2048]{2,1,0:T(8,128)(2,1)S(1)}, bf16[4,32,2048]{2,1,0:T(8,128)(2,1)}, u32[]{:S(2)}, u32[]{:S(2)}) collective-permute-start(bf16[4,32,2048]{2,1,0:T(8,128)(2,1)S(1)} %copy-done.36), channel_id=1, source_target_pairs={{0,12},{4,0},{8,4},{12,8},{1,13},{5,1},{9,5},{13,9},{2,14},{6,2},{... | collective-permute-start | bytes 1572872 | tf_op jit(solution)/shard_map/ppermute | solution.py:41
  43.1 34.3 %collective-permute-start.1 = (bf16[4,32,2048]{2,1,0:T(8,128)(2,1)S(1)}, bf16[4,32,2048]{2,1,0:T(8,128)(2,1)}, u32[]{:S(2)}, u32[]{:S(2)}) collective-permute-start(bf16[4,32,2048]{2,1,0:T(8,128)(2,1)S(1)} %copy-done.36), channel_id=1, source_target_pairs={{0,8},{4,12},{8,0},{12,4},{1,9},{5,13},{9,1},{13,5},{2,10},{6,14},... | collective-permute-start | bytes 1572872 | tf_op jit(solution)/shard_map/ppermute | solution.py:41
  43.1 45.5 %collective-permute-start.6 = (bf16[4,32,2048]{2,1,0:T(8,128)(2,1)S(1)}, bf16[4,32,2048]{2,1,0:T(8,128)(2,1)S(1)}, u32[]{:S(2)}, u32[]{:S(2)}) collective-permute-start(bf16[4,32,2048]{2,1,0:T(8,128)(2,1)S(1)} %copy-done.38), channel_id=1, source_target_pairs={{0,16},{16,0},{1,17},{17,1},{2,18},{18,2},{3,19},{19,3},{4,20},{20... | collective-permute-start | bytes 1572872 | tf_op jit(solution)/shard_map/ppermute | solution.py:36
  55.2 13.0 %collective-permute-start.4 = (f16[64,3712]{1,0:T(8,128)(2,1)S(1)}, f16[64,3712]{1,0:T(8,128)(2,1)S(1)}, u32[]{:S(2)}, u32[]{:S(2)}) collective-permute-start(f16[64,3712]{1,0:T(8,128)(2,1)S(1)} %pad_maximum_fusion.24), channel_id=1, source_target_pairs={{0,2},{1,3},{2,0},{3,1},{4,6},{5,7},{6,4},{7,5},{8,10},{9,11},{10,... | collective-permute-start | bytes 1425416 | tf_op jit(solution)/shard_map/ppermute | solution.py:36
  64.1 23.9 %collective-permute-start.7 = (f32[128,3584]{1,0:T(8,128)S(1)}, f32[128,3584]{1,0:T(8,128)S(1)}, u32[]{:S(2)}, u32[]{:S(2)}) collective-permute-start(f32[128,3584]{1,0:T(8,128)S(1)} %slice.325), channel_id=1, source_target_pairs={{0,1},{1,0},{2,3},{3,2},{4,5},{5,4},{6,7},{7,6},{8,9},{9,8},{10,11... | collective-permute-start | bytes 5505032 | tf_op jit(solution)/shard_map/ppermute | solution.py:36
  64.3 25.9 %collective-permute-start.8 = (f16[64,3584]{1,0:T(8,128)(2,1)S(1)}, f16[64,3584]{1,0:T(8,128)(2,1)S(1)}, u32[]{:S(2)}, u32[]{:S(2)}) collective-permute-start(f16[64,3584]{1,0:T(8,128)(2,1)S(1)} %fusion.58), channel_id=1, source_target_pairs={{0,2},{1,3},{2,0},{3,1},{4,6},{5,7},{6,4},{7,5},{8,10},{9,11},{10,... | collective-permute-start | bytes 1376264 | tf_op jit(solution)/shard_map/ppermute | solution.py:36
  86.1 18.2 %collective-permute-start.11 = (f32[128,3584]{1,0:T(8,128)S(1)}, f32[128,3584]{1,0:T(8,128)S(1)}, u32[]{:S(2)}, u32[]{:S(2)}) collective-permute-start(f32[128,3584]{1,0:T(8,128)S(1)} %slice.333), channel_id=1, source_target_pairs={{0,1},{1,0},{2,3},{3,2},{4,5},{5,4},{6,7},{7,6},{8,9},{9,8},{10,11... | collective-permute-start | bytes 5505032 | tf_op jit(solution)/shard_map/ppermute | solution.py:36
  86.1 62.4 %collective-permute-start.23 = (bf16[4,32,2048]{2,1,0:T(8,128)(2,1)}, bf16[4,32,2048]{2,1,0:T(8,128)(2,1)}, u32[]{:S(2)}, u32[]{:S(2)}) collective-permute-start(bf16[4,32,2048]{2,1,0:T(8,128)(2,1)} %collective-permute-done.1), channel_id=1, source_target_pairs={{0,16},{16,0},{1,17},{17,1},{2,18},{18,2},{3,19},{19,3},{4,20},{20... | collective-permute-start | bytes 1572872 | tf_op jit(solution)/shard_map/ppermute | solution.py:36
  88.0 60.7 %collective-permute-start.24 = (bf16[4,32,2048]{2,1,0:T(8,128)(2,1)}, bf16[4,32,2048]{2,1,0:T(8,128)(2,1)}, u32[]{:S(2)}, u32[]{:S(2)}) collective-permute-start(bf16[4,32,2048]{2,1,0:T(8,128)(2,1)} %collective-permute-done.5), channel_id=1, source_target_pairs={{0,16},{16,0},{1,17},{17,1},{2,18},{18,2},{3,19},{19,3},{4,20},{20... | collective-permute-start | bytes 1572872 | tf_op jit(solution)/shard_map/ppermute | solution.py:36
  99.0 26.9 %collective-permute-start.9 = (f32[128,3584]{1,0:T(8,128)}, f32[128,3584]{1,0:T(8,128)}, u32[]{:S(2)}, u32[]{:S(2)}) collective-permute-start(f32[128,3584]{1,0:T(8,128)} %slice.328), channel_id=1, source_target_pairs={{0,1},{1,0},{2,3},{3,2},{4,5},{5,4},{6,7},{7,6},{8,9},{9,8},{10,11... | collective-permute-start | bytes 5505032 | tf_op jit(solution)/shard_map/ppermute | solution.py:36
  102.8 14.5 %collective-permute-start.16 = (bf16[64,3584]{1,0:T(8,128)(2,1)S(1)}, bf16[64,3584]{1,0:T(8,128)(2,1)}, u32[]{:S(2)}, u32[]{:S(2)}) collective-permute-start(bf16[64,3584]{1,0:T(8,128)(2,1)S(1)} %get-tuple-element.83), channel_id=1, source_target_pairs={{0,2},{1,3},{2,0},{3,1},{4,6},{5,7},{6,4},{7,5},{8,10},{9,11},{10,... | collective-permute-start | bytes 1376264 | tf_op jit(solution)/shard_map/ppermute | solution.py:36
  105.8 19.0 %collective-permute-start.12 = (f16[64,3712]{1,0:T(8,128)(2,1)}, f16[64,3712]{1,0:T(8,128)(2,1)}, u32[]{:S(2)}, u32[]{:S(2)}) collective-permute-start(f16[64,3712]{1,0:T(8,128)(2,1)} %pad_maximum_fusion.25), channel_id=1, source_target_pairs={{0,2},{1,3},{2,0},{3,1},{4,6},{5,7},{6,4},{7,5},{8,10},{9,11},{10,... | collective-permute-start | bytes 1425416 | tf_op jit(solution)/shard_map/ppermute | solution.py:36
  117.2 94.3 %all-gather.5.cloned.1.call-start = ((), (), s32[]{:S(2)}) async-start(), calls=%async_computation | async-start | bytes 2752512 | tf_op jit(solution)/shard_map/all_gather | solution.py:210
  117.3 27.6 %collective-permute-start.14 = (f32[128,3584]{1,0:T(8,128)}, f32[128,3584]{1,0:T(8,128)S(1)}, u32[]{:S(2)}, u32[]{:S(2)}) collective-permute-start(f32[128,3584]{1,0:T(8,128)} %slice.343), channel_id=1, source_target_pairs={{0,1},{1,0},{2,3},{3,2},{4,5},{5,4},{6,7},{7,6},{8,9},{9,8},{10,11... | collective-permute-start | bytes 5505032 | tf_op jit(solution)/shard_map/ppermute | solution.py:36
  127.5 21.9 %collective-permute-start.10 = (f16[64,3584]{1,0:T(8,128)(2,1)S(1)}, f16[64,3584]{1,0:T(8,128)(2,1)S(1)}, u32[]{:S(2)}, u32[]{:S(2)}) collective-permute-start(f16[64,3584]{1,0:T(8,128)(2,1)S(1)} %fusion.54), channel_id=1, source_target_pairs={{0,2},{1,3},{2,0},{3,1},{4,6},{5,7},{6,4},{7,5},{8,10},{9,11},{10,... | collective-permute-start | bytes 1376264 | tf_op jit(solution)/shard_map/ppermute | solution.py:36
  139.2 75.2 %collective-permute-start.21 = (bf16[4,32,2048]{2,1,0:T(8,128)(2,1)}, bf16[4,32,2048]{2,1,0:T(8,128)(2,1)}, u32[]{:S(2)}, u32[]{:S(2)}) collective-permute-start(bf16[4,32,2048]{2,1,0:T(8,128)(2,1)} %get-tuple-element.102), channel_id=1, source_target_pairs={{0,8},{4,12},{8,0},{12,4},{1,9},{5,13},{9,1},{13,5},{2,10},{6,14},... | collective-permute-start | bytes 1572872 | tf_op jit(solution)/shard_map/ppermute | solution.py:41
  144.9 69.6 %collective-permute-start.20 = (bf16[4,32,2048]{2,1,0:T(8,128)(2,1)}, bf16[4,32,2048]{2,1,0:T(8,128)(2,1)}, u32[]{:S(2)}, u32[]{:S(2)}) collective-permute-start(bf16[4,32,2048]{2,1,0:T(8,128)(2,1)} %get-tuple-element.101), channel_id=1, source_target_pairs={{0,12},{4,0},{8,4},{12,8},{1,13},{5,1},{9,5},{13,9},{2,14},{6,2},{... | collective-permute-start | bytes 1572872 | tf_op jit(solution)/shard_map/ppermute | solution.py:41
  148.6 17.4 %collective-permute-start.30 = (f32[128,3584]{1,0:T(8,128)}, f32[128,3584]{1,0:T(8,128)}, u32[]{:S(2)}, u32[]{:S(2)}) collective-permute-start(f32[128,3584]{1,0:T(8,128)} %slice.359), channel_id=1, source_target_pairs={{0,1},{1,0},{2,3},{3,2},{4,5},{5,4},{6,7},{7,6},{8,9},{9,8},{10,11... | collective-permute-start | bytes 5505032 | tf_op jit(solution)/shard_map/ppermute | solution.py:36
  156.2 34.7 %collective-permute-start.25 = (f32[128,3584]{1,0:T(8,128)}, f32[128,3584]{1,0:T(8,128)}, u32[]{:S(2)}, u32[]{:S(2)}) collective-permute-start(f32[128,3584]{1,0:T(8,128)} %slice.363), channel_id=1, source_target_pairs={{0,1},{1,0},{2,3},{3,2},{4,5},{5,4},{6,7},{7,6},{8,9},{9,8},{10,11... | collective-permute-start | bytes 5505032 | tf_op jit(solution)/shard_map/ppermute | solution.py:36
  165.3 13.4 %collective-permute-start.18 = (bf16[64,3584]{1,0:T(8,128)(2,1)S(1)}, bf16[64,3584]{1,0:T(8,128)(2,1)S(1)}, u32[]{:S(2)}, u32[]{:S(2)}) collective-permute-start(bf16[64,3584]{1,0:T(8,128)(2,1)S(1)} %get-tuple-element.81), channel_id=1, source_target_pairs={{0,2},{1,3},{2,0},{3,1},{4,6},{5,7},{6,4},{7,5},{8,10},{9,11},{10,... | collective-permute-start | bytes 1376264 | tf_op jit(solution)/shard_map/ppermute | solution.py:36
  168.3 19.0 %collective-permute-start.31 = (bf16[64,3584]{1,0:T(8,128)(2,1)}, bf16[64,3584]{1,0:T(8,128)(2,1)S(1)}, u32[]{:S(2)}, u32[]{:S(2)}) collective-permute-start(bf16[64,3584]{1,0:T(8,128)(2,1)} %fusion.37), channel_id=1, source_target_pairs={{0,2},{1,3},{2,0},{3,1},{4,6},{5,7},{6,4},{7,5},{8,10},{9,11},{10,... | collective-permute-start | bytes 1376264 | tf_op jit(solution)/shard_map/ppermute | solution.py:36
  179.7 14.1 %collective-permute-start.19 = (bf16[128,3584]{1,0:T(8,128)(2,1)}, bf16[128,3584]{1,0:T(8,128)(2,1)}, u32[]{:S(2)}, u32[]{:S(2)}) collective-permute-start(bf16[128,3584]{1,0:T(8,128)(2,1)} %pad_maximum_fusion.15), channel_id=1, source_target_pairs={{0,1},{1,0},{2,3},{3,2},{4,5},{5,4},{6,7},{7,6},{8,9},{9,8},{10,11... | collective-permute-start | bytes 2752520 | tf_op jit(solution)/shard_map/ppermute | solution.py:36
  190.1 15.3 %collective-permute-start.32 = (bf16[64,3584]{1,0:T(8,128)(2,1)S(1)}, bf16[64,3584]{1,0:T(8,128)(2,1)S(1)}, u32[]{:S(2)}, u32[]{:S(2)}) collective-permute-start(bf16[64,3584]{1,0:T(8,128)(2,1)S(1)} %fusion.40), channel_id=1, source_target_pairs={{0,2},{1,3},{2,0},{3,1},{4,6},{5,7},{6,4},{7,5},{8,10},{9,11},{10,... | collective-permute-start | bytes 1376264 | tf_op jit(solution)/shard_map/ppermute | solution.py:36
  192.4 19.1 %collective-permute-start.26 = (bf16[64,3584]{1,0:T(8,128)(2,1)S(1)}, bf16[64,3584]{1,0:T(8,128)(2,1)}, u32[]{:S(2)}, u32[]{:S(2)}) collective-permute-start(bf16[64,3584]{1,0:T(8,128)(2,1)S(1)} %fusion.41), channel_id=1, source_target_pairs={{0,2},{1,3},{2,0},{3,1},{4,6},{5,7},{6,4},{7,5},{8,10},{9,11},{10,... | collective-permute-start | bytes 1376264 | tf_op jit(solution)/shard_map/ppermute | solution.py:36
  202.5 14.4 %collective-permute-start.22 = (bf16[4,32,2048]{2,1,0:T(8,128)(2,1)}, bf16[4,32,2048]{2,1,0:T(8,128)(2,1)}, u32[]{:S(2)}, u32[]{:S(2)}) collective-permute-start(bf16[4,32,2048]{2,1,0:T(8,128)(2,1)} %fusion.59), channel_id=1, source_target_pairs={{0,4},{4,8},{8,12},{12,0},{1,5},{5,9},{9,13},{13,1},{2,6},{6,10},{... | collective-permute-start | bytes 1572872 | tf_op jit(solution)/shard_map/ppermute | solution.py:41
  206.5 16.0 %collective-permute-start.33 = (bf16[128,3584]{1,0:T(8,128)(2,1)}, bf16[128,3584]{1,0:T(8,128)(2,1)}, u32[]{:S(2)}, u32[]{:S(2)}) collective-permute-start(bf16[128,3584]{1,0:T(8,128)(2,1)} %pad_maximum_fusion.17), channel_id=1, source_target_pairs={{0,1},{1,0},{2,3},{3,2},{4,5},{5,4},{6,7},{7,6},{8,9},{9,8},{10,11... | collective-permute-start | bytes 2752520 | tf_op jit(solution)/shard_map/ppermute | solution.py:36
  213.7 36.6 %collective-permute-start.27 = (bf16[64,3584]{1,0:T(8,128)(2,1)S(1)}, bf16[64,3584]{1,0:T(8,128)(2,1)S(1)}, u32[]{:S(2)}, u32[]{:S(2)}) collective-permute-start(bf16[64,3584]{1,0:T(8,128)(2,1)S(1)} %fusion.44), channel_id=1, source_target_pairs={{0,2},{1,3},{2,0},{3,1},{4,6},{5,7},{6,4},{7,5},{8,10},{9,11},{10,... | collective-permute-start | bytes 1376264 | tf_op jit(solution)/shard_map/ppermute | solution.py:36
  218.6 16.7 %collective-permute-start.34 = (bf16[4,32,2048]{2,1,0:T(8,128)(2,1)S(1)}, bf16[4,32,2048]{2,1,0:T(8,128)(2,1)S(1)}, u32[]{:S(2)}, u32[]{:S(2)}) collective-permute-start(bf16[4,32,2048]{2,1,0:T(8,128)(2,1)S(1)} %fusion.20), channel_id=1, source_target_pairs={{0,4},{4,8},{8,12},{12,0},{1,5},{5,9},{9,13},{13,1},{2,6},{6,10},{... | collective-permute-start | bytes 1572872 | tf_op jit(solution)/shard_map/ppermute | solution.py:41
  219.7 22.2 %collective-permute-start.29 = (bf16[4,32,2048]{2,1,0:T(8,128)(2,1)S(1)}, bf16[4,32,2048]{2,1,0:T(8,128)(2,1)S(1)}, u32[]{:S(2)}, u32[]{:S(2)}) collective-permute-start(bf16[4,32,2048]{2,1,0:T(8,128)(2,1)S(1)} %fusion.20), channel_id=1, source_target_pairs={{0,12},{4,0},{8,4},{12,8},{1,13},{5,1},{9,5},{13,9},{2,14},{6,2},{... | collective-permute-start | bytes 1572872 | tf_op jit(solution)/shard_map/ppermute | solution.py:41
  251.4 27.1 %collective-permute-start.39 = (bf16[4,32,2048]{2,1,0:T(8,128)(2,1)S(1)}, bf16[4,32,2048]{2,1,0:T(8,128)(2,1)S(1)}, u32[]{:S(2)}, u32[]{:S(2)}) collective-permute-start(bf16[4,32,2048]{2,1,0:T(8,128)(2,1)S(1)} %copy-done.48), channel_id=1, source_target_pairs={{0,8},{4,12},{8,0},{12,4},{1,9},{5,13},{9,1},{13,5},{2,10},{6,14},... | collective-permute-start | bytes 1572872 | tf_op jit(solution)/shard_map/ppermute | solution.py:41
  253.2 35.2 %collective-permute-start.36 = (bf16[4,32,2048]{2,1,0:T(8,128)(2,1)S(1)}, bf16[4,32,2048]{2,1,0:T(8,128)(2,1)S(1)}, u32[]{:S(2)}, u32[]{:S(2)}) collective-permute-start(bf16[4,32,2048]{2,1,0:T(8,128)(2,1)S(1)} %copy-done.47), channel_id=1, source_target_pairs={{0,12},{4,0},{8,4},{12,8},{1,13},{5,1},{9,5},{13,9},{2,14},{6,2},{... | collective-permute-start | bytes 1572872 | tf_op jit(solution)/shard_map/ppermute | solution.py:41
  264.1 25.7 %collective-permute-start.40 = (bf16[4,32,2048]{2,1,0:T(8,128)(2,1)S(1)}, bf16[4,32,2048]{2,1,0:T(8,128)(2,1)S(1)}, u32[]{:S(2)}, u32[]{:S(2)}) collective-permute-start(bf16[4,32,2048]{2,1,0:T(8,128)(2,1)S(1)} %fusion.60), channel_id=1, source_target_pairs={{0,4},{4,8},{8,12},{12,0},{1,5},{5,9},{9,13},{13,1},{2,6},{6,10},{... | collective-permute-start | bytes 1572872 | tf_op jit(solution)/shard_map/ppermute | solution.py:41
  270.7 41.9 %collective-permute-start.43 = (bf16[4,32,2048]{2,1,0:T(8,128)(2,1)S(1)}, bf16[4,32,2048]{2,1,0:T(8,128)(2,1)S(1)}, u32[]{:S(2)}, u32[]{:S(2)}) collective-permute-start(bf16[4,32,2048]{2,1,0:T(8,128)(2,1)S(1)} %copy-done.44), channel_id=1, source_target_pairs={{0,12},{4,0},{8,4},{12,8},{1,13},{5,1},{9,5},{13,9},{2,14},{6,2},{... | collective-permute-start | bytes 1572872 | tf_op jit(solution)/shard_map/ppermute | solution.py:41
  290.1 35.3 %collective-permute-start.42 = (bf16[4,32,2048]{2,1,0:T(8,128)(2,1)S(1)}, bf16[4,32,2048]{2,1,0:T(8,128)(2,1)S(1)}, u32[]{:S(2)}, u32[]{:S(2)}) collective-permute-start(bf16[4,32,2048]{2,1,0:T(8,128)(2,1)S(1)} %fusion.15), channel_id=1, source_target_pairs={{0,4},{4,8},{8,12},{12,0},{1,5},{5,9},{9,13},{13,1},{2,6},{6,10},{... | collective-permute-start | bytes 1572872 | tf_op jit(solution)/shard_map/ppermute | solution.py:41
  310.4 25.5 %collective-permute-start.48 = (bf16[4,32,2048]{2,1,0:T(8,128)(2,1)S(1)}, bf16[4,32,2048]{2,1,0:T(8,128)(2,1)S(1)}, u32[]{:S(2)}, u32[]{:S(2)}) collective-permute-start(bf16[4,32,2048]{2,1,0:T(8,128)(2,1)S(1)} %fusion.15), channel_id=1, source_target_pairs={{0,12},{4,0},{8,4},{12,8},{1,13},{5,1},{9,5},{13,9},{2,14},{6,2},{... | collective-permute-start | bytes 1572872 | tf_op jit(solution)/shard_map/ppermute | solution.py:41
  346.3 19.9 %collective-permute-start.49 = (f32[128,3584]{1,0:T(8,128)}, f32[128,3584]{1,0:T(8,128)}, u32[]{:S(2)}, u32[]{:S(2)}) collective-permute-start(f32[128,3584]{1,0:T(8,128)} %slice.387), channel_id=1, source_target_pairs={{0,1},{1,0},{2,3},{3,2},{4,5},{5,4},{6,7},{7,6},{8,9},{9,8},{10,11... | collective-permute-start | bytes 5505032 | tf_op jit(solution)/shard_map/ppermute | solution.py:36
  347.6 17.1 %collective-permute-start.41 = (bf16[128,3584]{1,0:T(8,128)(2,1)}, bf16[128,3584]{1,0:T(8,128)(2,1)}, u32[]{:S(2)}, u32[]{:S(2)}) collective-permute-start(bf16[128,3584]{1,0:T(8,128)(2,1)} %pad_maximum_fusion.18), channel_id=1, source_target_pairs={{0,1},{1,0},{2,3},{3,2},{4,5},{5,4},{6,7},{7,6},{8,9},{9,8},{10,11... | collective-permute-start | bytes 2752520 | tf_op jit(solution)/shard_map/ppermute | solution.py:36
  347.9 21.2 %collective-permute-start.44 = (f32[128,3584]{1,0:T(8,128)}, f32[128,3584]{1,0:T(8,128)}, u32[]{:S(2)}, u32[]{:S(2)}) collective-permute-start(f32[128,3584]{1,0:T(8,128)} %slice.382), channel_id=1, source_target_pairs={{0,1},{1,0},{2,3},{3,2},{4,5},{5,4},{6,7},{7,6},{8,9},{9,8},{10,11... | collective-permute-start | bytes 5505032 | tf_op jit(solution)/shard_map/ppermute | solution.py:36
  352.9 23.7 %collective-permute-start.53 = (bf16[4,32,2048]{2,1,0:T(8,128)(2,1)}, bf16[4,32,2048]{2,1,0:T(8,128)(2,1)S(1)}, u32[]{:S(2)}, u32[]{:S(2)}) collective-permute-start(bf16[4,32,2048]{2,1,0:T(8,128)(2,1)} %copy-done.49), channel_id=1, source_target_pairs={{0,12},{4,0},{8,4},{12,8},{1,13},{5,1},{9,5},{13,9},{2,14},{6,2},{... | collective-permute-start | bytes 1572872 | tf_op jit(solution)/shard_map/ppermute | solution.py:41
  367.8 13.6 %collective-permute-start.50 = (bf16[64,3584]{1,0:T(8,128)(2,1)S(1)}, bf16[64,3584]{1,0:T(8,128)(2,1)}, u32[]{:S(2)}, u32[]{:S(2)}) collective-permute-start(bf16[64,3584]{1,0:T(8,128)(2,1)S(1)} %fusion.25), channel_id=1, source_target_pairs={{0,2},{1,3},{2,0},{3,1},{4,6},{5,7},{6,4},{7,5},{8,10},{9,11},{10,... | collective-permute-start | bytes 1376264 | tf_op jit(solution)/shard_map/ppermute | solution.py:36
  371.4 21.1 %collective-permute-start.45 = (bf16[64,3584]{1,0:T(8,128)(2,1)}, bf16[64,3584]{1,0:T(8,128)(2,1)S(1)}, u32[]{:S(2)}, u32[]{:S(2)}) collective-permute-start(bf16[64,3584]{1,0:T(8,128)(2,1)} %fusion.29), channel_id=1, source_target_pairs={{0,2},{1,3},{2,0},{3,1},{4,6},{5,7},{6,4},{7,5},{8,10},{9,11},{10,... | collective-permute-start | bytes 1376264 | tf_op jit(solution)/shard_map/ppermute | solution.py:36
  394.3 13.4 %collective-permute-start.46 = (bf16[64,3584]{1,0:T(8,128)(2,1)S(1)}, bf16[64,3584]{1,0:T(8,128)(2,1)S(1)}, u32[]{:S(2)}, u32[]{:S(2)}) collective-permute-start(bf16[64,3584]{1,0:T(8,128)(2,1)S(1)} %fusion.32), channel_id=1, source_target_pairs={{0,2},{1,3},{2,0},{3,1},{4,6},{5,7},{6,4},{7,5},{8,10},{9,11},{10,... | collective-permute-start | bytes 1376264 | tf_op jit(solution)/shard_map/ppermute | solution.py:36
  397.3 30.9 %collective-permute-start.51 = (bf16[64,3584]{1,0:T(8,128)(2,1)S(1)}, bf16[64,3584]{1,0:T(8,128)(2,1)S(1)}, u32[]{:S(2)}, u32[]{:S(2)}) collective-permute-start(bf16[64,3584]{1,0:T(8,128)(2,1)S(1)} %fusion.28), channel_id=1, source_target_pairs={{0,2},{1,3},{2,0},{3,1},{4,6},{5,7},{6,4},{7,5},{8,10},{9,11},{10,... | collective-permute-start | bytes 1376264 | tf_op jit(solution)/shard_map/ppermute | solution.py:36
  398.5 28.3 %collective-permute-start.55 = (bf16[64,3584]{1,0:T(8,128)(2,1)S(1)}, bf16[64,3584]{1,0:T(8,128)(2,1)S(1)}, u32[]{:S(2)}, u32[]{:S(2)}) collective-permute-start(bf16[64,3584]{1,0:T(8,128)(2,1)S(1)} %fusion.21), channel_id=1, source_target_pairs={{0,2},{1,3},{2,0},{3,1},{4,6},{5,7},{6,4},{7,5},{8,10},{9,11},{10,... | collective-permute-start | bytes 1376264 | tf_op jit(solution)/shard_map/ppermute | solution.py:36
  407.8 31.4 %collective-permute-start.47 = (bf16[128,3584]{1,0:T(8,128)(2,1)S(1)}, bf16[128,3584]{1,0:T(8,128)(2,1)S(1)}, u32[]{:S(2)}, u32[]{:S(2)}) collective-permute-start(bf16[128,3584]{1,0:T(8,128)(2,1)S(1)} %pad_maximum_fusion.19), channel_id=1, source_target_pairs={{0,1},{1,0},{2,3},{3,2},{4,5},{5,4},{6,7},{7,6},{8,9},{9,8},{10,11... | collective-permute-start | bytes 2752520 | tf_op jit(solution)/shard_map/ppermute | solution.py:36
  (69 other events, 665.6 us)
Sparse Core Ops, SparseCore 0:
  117.3 31.4 all-gather.6
  166.1 30.7 all-gather.4

commit v14 on v11

--- a/solution.py
+++ b/solution.py
@@ -275,7 +275,7 @@
         _, _, after, near = back(0, j, pieces, after)
     after = after + others[:1]
     for j in reversed(range(GROUPS)):
-        _, after, _, _ = back(1, j, others, after)
+        _, _, after, _ = back(1, j, others, after)
         after = after + near
     return last_product(turned, bars, tokens)
 

time: 467 us -> 468 us (level)
    unnamed x116 -> x120, local copies, waits for them, and re-layouts: 10.7 us -> 11.3 us
where the time goes in v14:
time: 468 us; the launch traced here: 464 us
  waiting for transfers between devices  173 us (37%)
  matrix products  115 us (25%)
  starting transfers between devices  61.8 us (13%)
  other arithmetic  42.6 us (9%)
  local copies, waits for them, and re-layouts  34.6 us (7%)
  Pallas kernels  22.5 us (5%)
  between operations  14.9 us (3%)
    ppermute x43, waiting for transfers between devices, swap(): return lax.ppermute(values, axis, [(i, i ^ mask) for i in range(count)])  86.9 us
    ppermute x15, waiting for transfers between devices, shift(): lax.ppermute(values, axis, [(i, (i + by) % count) for i in range(count)])  86.1 us
    dot_general x12, matrix products, matmul(): return jnp.dot(left, right, preferred_element_type=jnp.float32)  83.8 us
    ppermute x15, starting transfers between devices, shift(): lax.ppermute(values, axis, [(i, (i + by) % count) for i in range(count)])  34.2 us
    dot_general x4, matrix products, times_down(): lax.dot_general(left, w_down, (((1,), (1,)), ((), ())), preferred_element...  31.3 us
    ppermute x43, starting transfers between devices, swap(): return lax.ppermute(values, axis, [(i, i ^ mask) for i in range(count)])  27.5 us
    pallas_call x1, Pallas kernels, last_product(): pl.pallas_call(functools.partial(last_kernel, 1.0 / tokens, len(turned)),...  22.5 us
    unnamed x120, local copies, waits for them, and re-layouts  11.3 us
  transfers between devices with their start and end apart: 60, of which 27 were waited for; matrix products, arithmetic and copies ran while one was open for 33% of the time, Pallas kernels for 0%

profile of v14, /device:TPU:0, one launch (start us, length us, event | category | flops | bytes accessed | tf_op | source)
XLA Modules:
  0.0 464.5 jit_solution(11432311414548726155)
XLA Ops:
  8.0 3.1 collective-permute-start
  11.1 13.9 %collective-permute-done = bf16[4,32,2048]{2,1,0:T(8,128)(2,1)S(1)} collective-permute-done((bf16[4,32,2048]{2,1,0:T(8,128)(2,1)S(1)}, bf16[4,32,2048]{2,1,0:T(8,128)(2,1)S(1)}, u32[]{:S(2)}, u32[]{:S(2)}) %collective-permute-start) | collective-permute-done | bytes 524320 | tf_op jit(solution)/shard_map/ppermute | solution.py:41
  25.8 7.2 %fusion.86 = f32[256,3584]{1,0:T(8,128)S(1)} fusion(bf16[256,2048]{1,0:T(8,128)(2,1)S(1)} %bitcast.130, bf16[2048,3584]{1,0:T(8,128)(2,1)} %param.8), kind=kOutput, calls=%fused_computation.192 | convolution fusion | flops 3758096384 | bytes 19398656 | tf_op jit(solution)/shard_map/dot_general | solution.py:19
  36.5 2.9 dynamic-slice_bitcast_fusion.3
  42.8 7.2 %fusion.85 = f32[256,3584]{1,0:T(8,128)S(1)} fusion(bf16[256,2048]{1,0:T(8,128)(2,1)S(1)} %bitcast.131, bf16[2048,3584]{1,0:T(8,128)(2,1)} %param.7), kind=kOutput, calls=%fused_computation.191 | convolution fusion | flops 3758096384 | bytes 19398656 | tf_op jit(solution)/shard_map/dot_general | solution.py:19
  56.7 7.2 %fusion.87 = f32[256,3584]{1,0:T(8,128)S(1)} fusion(bf16[256,2048]{1,0:T(8,128)(2,1)S(1)} %bitcast.132, bf16[2048,3584]{1,0:T(8,128)(2,1)} %param.10), kind=kOutput, calls=%fused_computation.193 | convolution fusion | flops 3758096384 | bytes 19398656 | tf_op jit(solution)/shard_map/dot_general | solution.py:19
  64.9 3.3 collective-permute-done.4
  68.2 7.3 %collective-permute-done.1 = bf16[4,32,2048]{2,1,0:T(8,128)(2,1)} collective-permute-done((bf16[4,32,2048]{2,1,0:T(8,128)(2,1)S(1)}, bf16[4,32,2048]{2,1,0:T(8,128)(2,1)}, u32[]{:S(2)}, u32[]{:S(2)}) %collective-permute-start.1) | collective-permute-done | bytes 524320 | tf_op jit(solution)/shard_map/ppermute | solution.py:41
  76.8 7.3 %fusion.89 = f32[256,3584]{1,0:T(8,128)S(1)} fusion(bf16[256,2048]{1,0:T(8,128)(2,1)S(1)} %bitcast.134, bf16[2048,3584]{1,0:T(8,128)(2,1)} %param.8), kind=kOutput, calls=%fused_computation.195 | convolution fusion | flops 3758096384 | bytes 19398656 | tf_op jit(solution)/shard_map/dot_general | solution.py:19
  88.4 7.2 %fusion.88 = f32[256,3584]{1,0:T(8,128)S(1)} fusion(bf16[256,2048]{1,0:T(8,128)(2,1)S(1)} %bitcast.135, bf16[2048,3584]{1,0:T(8,128)(2,1)} %param.7), kind=kOutput, calls=%fused_computation.194 | convolution fusion | flops 3758096384 | bytes 19398656 | tf_op jit(solution)/shard_map/dot_general | solution.py:19
  99.3 2.8 multiply_convert_fusion.1
  105.7 7.6 %fusion.90 = f32[256,3584]{1,0:T(8,128)S(1)} fusion(bf16[256,2048]{1,0:T(8,128)(2,1)S(1)} %bitcast.136, bf16[2048,3584]{1,0:T(8,128)(2,1)} %param.10), kind=kOutput, calls=%fused_computation.196 | convolution fusion | flops 3758096384 | bytes 19398656 | tf_op jit(solution)/shard_map/dot_general | solution.py:19
  116.8 7.2 %collective-permute-done.12 = f16[64,3712]{1,0:T(8,128)(2,1)} collective-permute-done((f16[64,3712]{1,0:T(8,128)(2,1)}, f16[64,3712]{1,0:T(8,128)(2,1)}, u32[]{:S(2)}, u32[]{:S(2)}) %collective-permute-start.12) | collective-permute-done | bytes 475168 | tf_op jit(solution)/shard_map/ppermute | solution.py:36
  128.6 7.7 %convolution_convert_fusion.1 = bf16[256,2048]{1,0:T(8,128)(2,1)S(1)} fusion(bf16[256,3584]{1,0:T(8,128)(2,1)S(1)} %pad_maximum_fusion, bf16[3584,2048]{1,0:T(8,128)(2,1)} %param.9), kind=kOutput, calls=%fused_computation.1 | convolution fusion | flops 3758620672 | bytes 17563648 | tf_op jit(solution)/shard_map/dot_general | solution.py:19
  138.4 3.9 fusion.91
  143.8 3.6 collective-permute-start.20
  149.5 3.9 fusion.92
  155.2 5.4 %collective-permute-done.15 = bf16[64,3584]{1,0:T(8,128)(2,1)S(1)} collective-permute-done((bf16[64,3584]{1,0:T(8,128)(2,1)S(1)}, bf16[64,3584]{1,0:T(8,128)(2,1)S(1)}, u32[]{:S(2)}, u32[]{:S(2)}) %collective-permute-start.15) | collective-permute-done | bytes 458784 | tf_op jit(solution)/shard_map/ppermute | solution.py:36
  160.7 3.6 multiply_convert_fusion
  164.8 2.4 fusion.37
  168.7 9.0 %collective-permute-done.18 = bf16[64,3584]{1,0:T(8,128)(2,1)S(1)} collective-permute-done((bf16[64,3584]{1,0:T(8,128)(2,1)S(1)}, bf16[64,3584]{1,0:T(8,128)(2,1)S(1)}, u32[]{:S(2)}, u32[]{:S(2)}) %collective-permute-start.18) | collective-permute-done | bytes 458784 | tf_op jit(solution)/shard_map/ppermute | solution.py:36
  178.7 7.6 %collective-permute-done.31 = bf16[64,3584]{1,0:T(8,128)(2,1)S(1)} collective-permute-done((bf16[64,3584]{1,0:T(8,128)(2,1)}, bf16[64,3584]{1,0:T(8,128)(2,1)S(1)}, u32[]{:S(2)}, u32[]{:S(2)}) %collective-permute-start.31) | collective-permute-done | bytes 458784 | tf_op jit(solution)/shard_map/ppermute | solution.py:36
  192.8 7.7 %fusion = f32[256,2048]{1,0:T(8,128)S(1)} fusion(bf16[3584,2048]{1,0:T(8,128)(2,1)} %param.9, bf16[128,3584]{1,0:T(8,128)(2,1)} %collective-permute-done.19, bf16[64,3584]{1,0:T(8,128)(2,1)S(1)} %collective-permute-done.18, bf16[64,3584]{1,0:T(8,128)(2,1)S(1)} %get-tuple-element.81), kind=kOutput, calls=%fused_computation.3 | convolution fusion | flops 3763601408 | bytes 18612224 | tf_op jit(solution)/shard_map/dot_general | solution.py:19
  204.8 5.7 %collective-permute-done.26 = bf16[64,3584]{1,0:T(8,128)(2,1)} collective-permute-done((bf16[64,3584]{1,0:T(8,128)(2,1)S(1)}, bf16[64,3584]{1,0:T(8,128)(2,1)}, u32[]{:S(2)}, u32[]{:S(2)}) %collective-permute-start.26) | collective-permute-done | bytes 458784 | tf_op jit(solution)/shard_map/ppermute | solution.py:36
  213.3 2.5 collective-permute-done.22
  218.0 3.6 collective-permute-start.29
  221.6 9.4 %convolution_convert_fusion = bf16[256,2048]{1,0:T(8,128)(2,1)S(1)} fusion(bf16[3584,2048]{1,0:T(8,128)(2,1)} %param.9, bf16[128,3584]{1,0:T(8,128)(2,1)} %collective-permute-done.33, bf16[64,3584]{1,0:T(8,128)(2,1)S(1)} %copy-done.52, bf16[64,3584]{1,0:T(8,128)(2,1)S(1)} %fusion.40), kind=kOutput, calls=%fused_computation | convolution fusion | flops 3764125696 | bytes 17563648 | tf_op jit(solution)/shard_map/dot_general | solution.py:19
  232.1 2.3 collective-permute-done.34
  235.2 5.2 %collective-permute-done.29 = bf16[4,32,2048]{2,1,0:T(8,128)(2,1)S(1)} collective-permute-done((bf16[4,32,2048]{2,1,0:T(8,128)(2,1)S(1)}, bf16[4,32,2048]{2,1,0:T(8,128)(2,1)S(1)}, u32[]{:S(2)}, u32[]{:S(2)}) %collective-permute-start.29) | collective-permute-done | bytes 524320 | tf_op jit(solution)/shard_map/ppermute | solution.py:41
  240.4 7.3 %fusion.93 = f32[256,3584]{1,0:T(8,128)S(1)} fusion(bf16[256,2048]{1,0:T(8,128)(2,1)S(1)} %bitcast.154, bf16[3584,2048]{1,0:T(8,128)(2,1)} %param.9), kind=kOutput, calls=%fused_computation.199 | convolution fusion | flops 3758096384 | bytes 19398656 | tf_op jit(solution)/shard_map/dot_general | solution.py:23
  248.8 2.3 collective-permute-start.39
  254.2 7.2 %fusion.94 = f32[256,2048]{1,0:T(8,128)S(1)} fusion(bf16[256,3584]{1,0:T(8,128)(2,1)S(1)} %pad_maximum_fusion.1, bf16[3584,2048]{1,0:T(8,128)(2,1)} %param.9), kind=kOutput, calls=%fused_computation.200 | convolution fusion | flops 3758096384 | bytes 18612224 | tf_op jit(solution)/shard_map/dot_general | solution.py:19
  262.0 4.0 collective-permute-done.37
  269.1 6.6 %collective-permute-done.39 = bf16[4,32,2048]{2,1,0:T(8,128)(2,1)S(1)} collective-permute-done((bf16[4,32,2048]{2,1,0:T(8,128)(2,1)S(1)}, bf16[4,32,2048]{2,1,0:T(8,128)(2,1)S(1)}, u32[]{:S(2)}, u32[]{:S(2)}) %collective-permute-start.39) | collective-permute-done | bytes 524320 | tf_op jit(solution)/shard_map/ppermute | solution.py:41
  277.9 10.1 %collective-permute-done.36 = bf16[4,32,2048]{2,1,0:T(8,128)(2,1)S(1)} collective-permute-done((bf16[4,32,2048]{2,1,0:T(8,128)(2,1)S(1)}, bf16[4,32,2048]{2,1,0:T(8,128)(2,1)S(1)}, u32[]{:S(2)}, u32[]{:S(2)}) %collective-permute-start.36) | collective-permute-done | bytes 524320 | tf_op jit(solution)/shard_map/ppermute | solution.py:41
  288.5 9.7 %collective-permute-done.42 = bf16[4,32,2048]{2,1,0:T(8,128)(2,1)S(1)} collective-permute-done((bf16[4,32,2048]{2,1,0:T(8,128)(2,1)S(1)}, bf16[4,32,2048]{2,1,0:T(8,128)(2,1)S(1)}, u32[]{:S(2)}, u32[]{:S(2)}) %collective-permute-start.42) | collective-permute-done | bytes 524320 | tf_op jit(solution)/shard_map/ppermute | solution.py:41
  298.3 7.5 %fusion.95 = f32[256,3584]{1,0:T(8,128)S(1)} fusion(bf16[256,2048]{1,0:T(8,128)(2,1)S(1)} %bitcast.152, bf16[3584,2048]{1,0:T(8,128)(2,1)} %param.9), kind=kOutput, calls=%fused_computation.201 | convolution fusion | flops 3758096384 | bytes 19398656 | tf_op jit(solution)/shard_map/dot_general | solution.py:23
  306.1 10.6 %collective-permute-start.48 = (bf16[4,32,2048]{2,1,0:T(8,128)(2,1)S(1)}, bf16[4,32,2048]{2,1,0:T(8,128)(2,1)S(1)}, u32[]{:S(2)}, u32[]{:S(2)}) collective-permute-start(bf16[4,32,2048]{2,1,0:T(8,128)(2,1)S(1)} %fusion.15), channel_id=1, source_target_pairs={{0,4},{4,8},{8,12},{12,0},{1,5},{5,9},{9,13},{13,1},{2,6},{6,10},{... | collective-permute-start | bytes 1572872 | tf_op jit(solution)/shard_map/ppermute | solution.py:41
  320.1 11.3 %collective-permute-done.48 = bf16[4,32,2048]{2,1,0:T(8,128)(2,1)S(1)} collective-permute-done((bf16[4,32,2048]{2,1,0:T(8,128)(2,1)S(1)}, bf16[4,32,2048]{2,1,0:T(8,128)(2,1)S(1)}, u32[]{:S(2)}, u32[]{:S(2)}) %collective-permute-start.48) | collective-permute-done | bytes 524320 | tf_op jit(solution)/shard_map/ppermute | solution.py:41
  331.4 10.9 %collective-permute-done.47 = bf16[4,32,2048]{2,1,0:T(8,128)(2,1)S(1)} collective-permute-done((bf16[4,32,2048]{2,1,0:T(8,128)(2,1)S(1)}, bf16[4,32,2048]{2,1,0:T(8,128)(2,1)S(1)}, u32[]{:S(2)}, u32[]{:S(2)}) %collective-permute-start.47) | collective-permute-done | bytes 524320 | tf_op jit(solution)/shard_map/ppermute | solution.py:41
  343.1 9.1 %fusion.96 = f32[256,3584]{1,0:T(8,128)} fusion(bf16[256,2048]{1,0:T(8,128)(2,1)S(1)} %bitcast.155, bf16[3584,2048]{1,0:T(8,128)(2,1)} %param.9), kind=kOutput, calls=%fused_computation.202 | convolution fusion | flops 3758096384 | bytes 19398656 | tf_op jit(solution)/shard_map/dot_general | solution.py:23
  362.4 6.0 %collective-permute-done.53 = bf16[4,32,2048]{2,1,0:T(8,128)(2,1)S(1)} collective-permute-done((bf16[4,32,2048]{2,1,0:T(8,128)(2,1)S(1)}, bf16[4,32,2048]{2,1,0:T(8,128)(2,1)S(1)}, u32[]{:S(2)}, u32[]{:S(2)}) %collective-permute-start.53) | collective-permute-done | bytes 524320 | tf_op jit(solution)/shard_map/ppermute | solution.py:41
  370.7 9.0 %collective-permute-done.50 = bf16[64,3584]{1,0:T(8,128)(2,1)S(1)} collective-permute-done((bf16[64,3584]{1,0:T(8,128)(2,1)S(1)}, bf16[64,3584]{1,0:T(8,128)(2,1)S(1)}, u32[]{:S(2)}, u32[]{:S(2)}) %collective-permute-start.50) | collective-permute-done | bytes 458784 | tf_op jit(solution)/shard_map/ppermute | solution.py:36
  380.6 7.3 %fusion.97 = f32[256,3584]{1,0:T(8,128)S(1)} fusion(bf16[256,2048]{1,0:T(8,128)(2,1)S(1)} %bitcast.153, bf16[3584,2048]{1,0:T(8,128)(2,1)} %param.9), kind=kOutput, calls=%fused_computation.203 | convolution fusion | flops 3758096384 | bytes 19398656 | tf_op jit(solution)/shard_map/dot_general | solution.py:23
  403.7 9.7 %collective-permute-done.55 = bf16[64,3584]{1,0:T(8,128)(2,1)S(1)} collective-permute-done((bf16[64,3584]{1,0:T(8,128)(2,1)S(1)}, bf16[64,3584]{1,0:T(8,128)(2,1)S(1)}, u32[]{:S(2)}, u32[]{:S(2)}) %collective-permute-start.55) | collective-permute-done | bytes 458784 | tf_op jit(solution)/shard_map/ppermute | solution.py:36
  416.5 6.8 %collective-permute-done.51 = bf16[64,3584]{1,0:T(8,128)(2,1)S(1)} collective-permute-done((bf16[64,3584]{1,0:T(8,128)(2,1)S(1)}, bf16[64,3584]{1,0:T(8,128)(2,1)S(1)}, u32[]{:S(2)}, u32[]{:S(2)}) %collective-permute-start.51) | collective-permute-done | bytes 458784 | tf_op jit(solution)/shard_map/ppermute | solution.py:36
  423.4 8.8 %collective-permute-done.56 = bf16[64,3584]{1,0:T(8,128)(2,1)S(1)} collective-permute-done((bf16[64,3584]{1,0:T(8,128)(2,1)S(1)}, bf16[64,3584]{1,0:T(8,128)(2,1)S(1)}, u32[]{:S(2)}, u32[]{:S(2)}) %collective-permute-start.56) | collective-permute-done | bytes 458784 | tf_op jit(solution)/shard_map/ppermute | solution.py:36
  434.9 22.5 %shard_map.64 = f32[2048,3584]{1,0:T(8,128)} custom-call(bf16[2048,256]{1,0:T(8,128)(2,1)S(1)} %bitcast.127, bf16[2048,256]{1,0:T(8,128)(2,1)S(1)} %bitcast.126, bf16[2048,256]{1,0:T(8,128)(2,1)S(1)} %bitcast.129, bf16[2048,256]{1,0:T(8,128)(2,1)S(1)} %bitcast.128, bf16[256,3584]{1,0:T(8,128)(2,1)S(1)} %pad_maximum_fusion.2.refs_4_, ...), custom_call_target="tpu_custom_call" | custom-call | flops 15032385536 | bytes 40894464 | tf_op jit(solution)/shard_map/pallas_call | solution.py:91
  (297 shorter events, 114.5 us)
Async XLA Ops:
  6.5 172.1 %all-gather.7.cloned.1.call-start = ((), (), s32[]{:S(2)}) async-start(), calls=%async_computation.1 | async-start | bytes 2752512 | tf_op jit(solution)/shard_map/all_gather | solution.py:210
  8.0 17.0 %collective-permute-start = (bf16[4,32,2048]{2,1,0:T(8,128)(2,1)S(1)}, bf16[4,32,2048]{2,1,0:T(8,128)(2,1)S(1)}, u32[]{:S(2)}, u32[]{:S(2)}) collective-permute-start(bf16[4,32,2048]{2,1,0:T(8,128)(2,1)S(1)} %pad_maximum_fusion.22), channel_id=1, source_target_pairs={{0,4},{4,8},{8,12},{12,0},{1,5},{5,9},{9,13},{13,1},{2,6},{6,10},{... | collective-permute-start | bytes 1572872 | tf_op jit(solution)/shard_map/ppermute | solution.py:41
  36.3 14.0 %collective-permute-start.3 = (f32[128,3584]{1,0:T(8,128)}, f32[128,3584]{1,0:T(8,128)}, u32[]{:S(2)}, u32[]{:S(2)}) collective-permute-start(f32[128,3584]{1,0:T(8,128)} %slice.322), channel_id=1, source_target_pairs={{0,1},{1,0},{2,3},{3,2},{4,5},{5,4},{6,7},{7,6},{8,9},{9,8},{10,11... | collective-permute-start | bytes 5505032 | tf_op jit(solution)/shard_map/ppermute | solution.py:36
  39.3 25.0 %collective-permute-start.5 = (bf16[4,32,2048]{2,1,0:T(8,128)(2,1)S(1)}, bf16[4,32,2048]{2,1,0:T(8,128)(2,1)}, u32[]{:S(2)}, u32[]{:S(2)}) collective-permute-start(bf16[4,32,2048]{2,1,0:T(8,128)(2,1)S(1)} %pad_maximum_fusion.22), channel_id=1, source_target_pairs={{0,12},{4,0},{8,4},{12,8},{1,13},{5,1},{9,5},{13,9},{2,14},{6,2},{... | collective-permute-start | bytes 1572872 | tf_op jit(solution)/shard_map/ppermute | solution.py:41
  41.3 34.3 %collective-permute-start.1 = (bf16[4,32,2048]{2,1,0:T(8,128)(2,1)S(1)}, bf16[4,32,2048]{2,1,0:T(8,128)(2,1)}, u32[]{:S(2)}, u32[]{:S(2)}) collective-permute-start(bf16[4,32,2048]{2,1,0:T(8,128)(2,1)S(1)} %pad_maximum_fusion.22), channel_id=1, source_target_pairs={{0,8},{4,12},{8,0},{12,4},{1,9},{5,13},{9,1},{13,5},{2,10},{6,14},... | collective-permute-start | bytes 1572872 | tf_op jit(solution)/shard_map/ppermute | solution.py:41
  41.3 45.5 %collective-permute-start.6 = (bf16[4,32,2048]{2,1,0:T(8,128)(2,1)S(1)}, bf16[4,32,2048]{2,1,0:T(8,128)(2,1)S(1)}, u32[]{:S(2)}, u32[]{:S(2)}) collective-permute-start(bf16[4,32,2048]{2,1,0:T(8,128)(2,1)S(1)} %copy-done.40), channel_id=1, source_target_pairs={{0,16},{16,0},{1,17},{17,1},{2,18},{18,2},{3,19},{19,3},{4,20},{20... | collective-permute-start | bytes 1572872 | tf_op jit(solution)/shard_map/ppermute | solution.py:36
  50.2 13.9 %collective-permute-start.2 = (f32[128,3584]{1,0:T(8,128)S(1)}, f32[128,3584]{1,0:T(8,128)S(1)}, u32[]{:S(2)}, u32[]{:S(2)}) collective-permute-start(f32[128,3584]{1,0:T(8,128)S(1)} %slice.319), channel_id=1, source_target_pairs={{0,1},{1,0},{2,3},{3,2},{4,5},{5,4},{6,7},{7,6},{8,9},{9,8},{10,11... | collective-permute-start | bytes 5505032 | tf_op jit(solution)/shard_map/ppermute | solution.py:36
  55.2 13.1 %collective-permute-start.4 = (f16[64,3712]{1,0:T(8,128)(2,1)S(1)}, f16[64,3712]{1,0:T(8,128)(2,1)S(1)}, u32[]{:S(2)}, u32[]{:S(2)}) collective-permute-start(f16[64,3712]{1,0:T(8,128)(2,1)S(1)} %pad_maximum_fusion.24), channel_id=1, source_target_pairs={{0,2},{1,3},{2,0},{3,1},{4,6},{5,7},{6,4},{7,5},{8,10},{9,11},{10,... | collective-permute-start | bytes 1425416 | tf_op jit(solution)/shard_map/ppermute | solution.py:36
  64.1 22.0 %collective-permute-start.7 = (f32[128,3584]{1,0:T(8,128)S(1)}, f32[128,3584]{1,0:T(8,128)S(1)}, u32[]{:S(2)}, u32[]{:S(2)}) collective-permute-start(f32[128,3584]{1,0:T(8,128)S(1)} %slice.325), channel_id=1, source_target_pairs={{0,1},{1,0},{2,3},{3,2},{4,5},{5,4},{6,7},{7,6},{8,9},{9,8},{10,11... | collective-permute-start | bytes 5505032 | tf_op jit(solution)/shard_map/ppermute | solution.py:36
  64.3 24.0 %collective-permute-start.8 = (f16[64,3584]{1,0:T(8,128)(2,1)S(1)}, f16[64,3584]{1,0:T(8,128)(2,1)S(1)}, u32[]{:S(2)}, u32[]{:S(2)}) collective-permute-start(f16[64,3584]{1,0:T(8,128)(2,1)S(1)} %fusion.58), channel_id=1, source_target_pairs={{0,2},{1,3},{2,0},{3,1},{4,6},{5,7},{6,4},{7,5},{8,10},{9,11},{10,... | collective-permute-start | bytes 1376264 | tf_op jit(solution)/shard_map/ppermute | solution.py:36
  84.2 19.4 %collective-permute-start.11 = (f32[128,3584]{1,0:T(8,128)S(1)}, f32[128,3584]{1,0:T(8,128)S(1)}, u32[]{:S(2)}, u32[]{:S(2)}) collective-permute-start(f32[128,3584]{1,0:T(8,128)S(1)} %slice.333), channel_id=1, source_target_pairs={{0,1},{1,0},{2,3},{3,2},{4,5},{5,4},{6,7},{7,6},{8,9},{9,8},{10,11... | collective-permute-start | bytes 5505032 | tf_op jit(solution)/shard_map/ppermute | solution.py:36
  84.3 63.2 %collective-permute-start.23 = (bf16[4,32,2048]{2,1,0:T(8,128)(2,1)}, bf16[4,32,2048]{2,1,0:T(8,128)(2,1)}, u32[]{:S(2)}, u32[]{:S(2)}) collective-permute-start(bf16[4,32,2048]{2,1,0:T(8,128)(2,1)} %collective-permute-done.1), channel_id=1, source_target_pairs={{0,16},{16,0},{1,17},{17,1},{2,18},{18,2},{3,19},{19,3},{4,20},{20... | collective-permute-start | bytes 1572872 | tf_op jit(solution)/shard_map/ppermute | solution.py:36
  86.1 61.5 %collective-permute-start.24 = (bf16[4,32,2048]{2,1,0:T(8,128)(2,1)}, bf16[4,32,2048]{2,1,0:T(8,128)(2,1)}, u32[]{:S(2)}, u32[]{:S(2)}) collective-permute-start(bf16[4,32,2048]{2,1,0:T(8,128)(2,1)} %collective-permute-done.5), channel_id=1, source_target_pairs={{0,16},{16,0},{1,17},{17,1},{2,18},{18,2},{3,19},{19,3},{4,20},{20... | collective-permute-start | bytes 1572872 | tf_op jit(solution)/shard_map/ppermute | solution.py:36
  97.1 28.0 %collective-permute-start.9 = (f32[128,3584]{1,0:T(8,128)}, f32[128,3584]{1,0:T(8,128)}, u32[]{:S(2)}, u32[]{:S(2)}) collective-permute-start(f32[128,3584]{1,0:T(8,128)} %slice.328), channel_id=1, source_target_pairs={{0,1},{1,0},{2,3},{3,2},{4,5},{5,4},{6,7},{7,6},{8,9},{9,8},{10,11... | collective-permute-start | bytes 5505032 | tf_op jit(solution)/shard_map/ppermute | solution.py:36
  102.2 14.5 %collective-permute-start.16 = (bf16[64,3584]{1,0:T(8,128)(2,1)S(1)}, bf16[64,3584]{1,0:T(8,128)(2,1)S(1)}, u32[]{:S(2)}, u32[]{:S(2)}) collective-permute-start(bf16[64,3584]{1,0:T(8,128)(2,1)S(1)} %get-tuple-element.83), channel_id=1, source_target_pairs={{0,2},{1,3},{2,0},{3,1},{4,6},{5,7},{6,4},{7,5},{8,10},{9,11},{10,... | collective-permute-start | bytes 1376264 | tf_op jit(solution)/shard_map/ppermute | solution.py:36
  105.1 18.9 %collective-permute-start.12 = (f16[64,3712]{1,0:T(8,128)(2,1)}, f16[64,3712]{1,0:T(8,128)(2,1)}, u32[]{:S(2)}, u32[]{:S(2)}) collective-permute-start(f16[64,3712]{1,0:T(8,128)(2,1)} %pad_maximum_fusion.25), channel_id=1, source_target_pairs={{0,2},{1,3},{2,0},{3,1},{4,6},{5,7},{6,4},{7,5},{8,10},{9,11},{10,... | collective-permute-start | bytes 1425416 | tf_op jit(solution)/shard_map/ppermute | solution.py:36
  116.6 94.0 %all-gather.5.cloned.1.call-start = ((), (), s32[]{:S(2)}) async-start(), calls=%async_computation | async-start | bytes 2752512 | tf_op jit(solution)/shard_map/all_gather | solution.py:210
  116.6 27.2 %collective-permute-start.14 = (f32[128,3584]{1,0:T(8,128)}, f32[128,3584]{1,0:T(8,128)S(1)}, u32[]{:S(2)}, u32[]{:S(2)}) collective-permute-start(f32[128,3584]{1,0:T(8,128)} %slice.343), channel_id=1, source_target_pairs={{0,1},{1,0},{2,3},{3,2},{4,5},{5,4},{6,7},{7,6},{8,9},{9,8},{10,11... | collective-permute-start | bytes 5505032 | tf_op jit(solution)/shard_map/ppermute | solution.py:36
  126.8 21.4 %collective-permute-start.10 = (f16[64,3584]{1,0:T(8,128)(2,1)S(1)}, f16[64,3584]{1,0:T(8,128)(2,1)S(1)}, u32[]{:S(2)}, u32[]{:S(2)}) collective-permute-start(f16[64,3584]{1,0:T(8,128)(2,1)S(1)} %fusion.54), channel_id=1, source_target_pairs={{0,2},{1,3},{2,0},{3,1},{4,6},{5,7},{6,4},{7,5},{8,10},{9,11},{10,... | collective-permute-start | bytes 1376264 | tf_op jit(solution)/shard_map/ppermute | solution.py:36
  137.4 75.9 %collective-permute-start.21 = (bf16[4,32,2048]{2,1,0:T(8,128)(2,1)}, bf16[4,32,2048]{2,1,0:T(8,128)(2,1)}, u32[]{:S(2)}, u32[]{:S(2)}) collective-permute-start(bf16[4,32,2048]{2,1,0:T(8,128)(2,1)} %get-tuple-element.102), channel_id=1, source_target_pairs={{0,8},{4,12},{8,0},{12,4},{1,9},{5,13},{9,1},{13,5},{2,10},{6,14},... | collective-permute-start | bytes 1572872 | tf_op jit(solution)/shard_map/ppermute | solution.py:41
  143.8 69.5 %collective-permute-start.20 = (bf16[4,32,2048]{2,1,0:T(8,128)(2,1)}, bf16[4,32,2048]{2,1,0:T(8,128)(2,1)}, u32[]{:S(2)}, u32[]{:S(2)}) collective-permute-start(bf16[4,32,2048]{2,1,0:T(8,128)(2,1)} %get-tuple-element.101), channel_id=1, source_target_pairs={{0,12},{4,0},{8,4},{12,8},{1,13},{5,1},{9,5},{13,9},{2,14},{6,2},{... | collective-permute-start | bytes 1572872 | tf_op jit(solution)/shard_map/ppermute | solution.py:41
  147.5 17.3 %collective-permute-start.30 = (f32[128,3584]{1,0:T(8,128)}, f32[128,3584]{1,0:T(8,128)}, u32[]{:S(2)}, u32[]{:S(2)}) collective-permute-start(f32[128,3584]{1,0:T(8,128)} %slice.359), channel_id=1, source_target_pairs={{0,1},{1,0},{2,3},{3,2},{4,5},{5,4},{6,7},{7,6},{8,9},{9,8},{10,11... | collective-permute-start | bytes 5505032 | tf_op jit(solution)/shard_map/ppermute | solution.py:36
  147.6 12.9 %collective-permute-start.15 = (bf16[64,3584]{1,0:T(8,128)(2,1)S(1)}, bf16[64,3584]{1,0:T(8,128)(2,1)S(1)}, u32[]{:S(2)}, u32[]{:S(2)}) collective-permute-start(bf16[64,3584]{1,0:T(8,128)(2,1)S(1)} %fusion.49), channel_id=1, source_target_pairs={{0,2},{1,3},{2,0},{3,1},{4,6},{5,7},{6,4},{7,5},{8,10},{9,11},{10,... | collective-permute-start | bytes 1376264 | tf_op jit(solution)/shard_map/ppermute | solution.py:36
  155.0 34.7 %collective-permute-start.25 = (f32[128,3584]{1,0:T(8,128)}, f32[128,3584]{1,0:T(8,128)}, u32[]{:S(2)}, u32[]{:S(2)}) collective-permute-start(f32[128,3584]{1,0:T(8,128)} %slice.363), channel_id=1, source_target_pairs={{0,1},{1,0},{2,3},{3,2},{4,5},{5,4},{6,7},{7,6},{8,9},{9,8},{10,11... | collective-permute-start | bytes 5505032 | tf_op jit(solution)/shard_map/ppermute | solution.py:36
  164.3 13.4 %collective-permute-start.18 = (bf16[64,3584]{1,0:T(8,128)(2,1)S(1)}, bf16[64,3584]{1,0:T(8,128)(2,1)S(1)}, u32[]{:S(2)}, u32[]{:S(2)}) collective-permute-start(bf16[64,3584]{1,0:T(8,128)(2,1)S(1)} %get-tuple-element.81), channel_id=1, source_target_pairs={{0,2},{1,3},{2,0},{3,1},{4,6},{5,7},{6,4},{7,5},{8,10},{9,11},{10,... | collective-permute-start | bytes 1376264 | tf_op jit(solution)/shard_map/ppermute | solution.py:36
  167.2 19.1 %collective-permute-start.31 = (bf16[64,3584]{1,0:T(8,128)(2,1)}, bf16[64,3584]{1,0:T(8,128)(2,1)S(1)}, u32[]{:S(2)}, u32[]{:S(2)}) collective-permute-start(bf16[64,3584]{1,0:T(8,128)(2,1)} %fusion.37), channel_id=1, source_target_pairs={{0,2},{1,3},{2,0},{3,1},{4,6},{5,7},{6,4},{7,5},{8,10},{9,11},{10,... | collective-permute-start | bytes 1376264 | tf_op jit(solution)/shard_map/ppermute | solution.py:36
  178.7 14.1 %collective-permute-start.19 = (bf16[128,3584]{1,0:T(8,128)(2,1)}, bf16[128,3584]{1,0:T(8,128)(2,1)}, u32[]{:S(2)}, u32[]{:S(2)}) collective-permute-start(bf16[128,3584]{1,0:T(8,128)(2,1)} %pad_maximum_fusion.15), channel_id=1, source_target_pairs={{0,1},{1,0},{2,3},{3,2},{4,5},{5,4},{6,7},{7,6},{8,9},{9,8},{10,11... | collective-permute-start | bytes 2752520 | tf_op jit(solution)/shard_map/ppermute | solution.py:36
  189.1 14.6 %collective-permute-start.32 = (bf16[64,3584]{1,0:T(8,128)(2,1)S(1)}, bf16[64,3584]{1,0:T(8,128)(2,1)S(1)}, u32[]{:S(2)}, u32[]{:S(2)}) collective-permute-start(bf16[64,3584]{1,0:T(8,128)(2,1)S(1)} %fusion.40), channel_id=1, source_target_pairs={{0,2},{1,3},{2,0},{3,1},{4,6},{5,7},{6,4},{7,5},{8,10},{9,11},{10,... | collective-permute-start | bytes 1376264 | tf_op jit(solution)/shard_map/ppermute | solution.py:36
  191.3 19.2 %collective-permute-start.26 = (bf16[64,3584]{1,0:T(8,128)(2,1)S(1)}, bf16[64,3584]{1,0:T(8,128)(2,1)}, u32[]{:S(2)}, u32[]{:S(2)}) collective-permute-start(bf16[64,3584]{1,0:T(8,128)(2,1)S(1)} %fusion.41), channel_id=1, source_target_pairs={{0,2},{1,3},{2,0},{3,1},{4,6},{5,7},{6,4},{7,5},{8,10},{9,11},{10,... | collective-permute-start | bytes 1376264 | tf_op jit(solution)/shard_map/ppermute | solution.py:36
  201.5 14.4 %collective-permute-start.22 = (bf16[4,32,2048]{2,1,0:T(8,128)(2,1)}, bf16[4,32,2048]{2,1,0:T(8,128)(2,1)}, u32[]{:S(2)}, u32[]{:S(2)}) collective-permute-start(bf16[4,32,2048]{2,1,0:T(8,128)(2,1)} %fusion.59), channel_id=1, source_target_pairs={{0,4},{4,8},{8,12},{12,0},{1,5},{5,9},{9,13},{13,1},{2,6},{6,10},{... | collective-permute-start | bytes 1572872 | tf_op jit(solution)/shard_map/ppermute | solution.py:41
  204.8 16.8 %collective-permute-start.33 = (bf16[128,3584]{1,0:T(8,128)(2,1)}, bf16[128,3584]{1,0:T(8,128)(2,1)}, u32[]{:S(2)}, u32[]{:S(2)}) collective-permute-start(bf16[128,3584]{1,0:T(8,128)(2,1)} %pad_maximum_fusion.17), channel_id=1, source_target_pairs={{0,1},{1,0},{2,3},{3,2},{4,5},{5,4},{6,7},{7,6},{8,9},{9,8},{10,11... | collective-permute-start | bytes 2752520 | tf_op jit(solution)/shard_map/ppermute | solution.py:36
  212.7 35.3 %collective-permute-start.27 = (bf16[64,3584]{1,0:T(8,128)(2,1)S(1)}, bf16[64,3584]{1,0:T(8,128)(2,1)S(1)}, u32[]{:S(2)}, u32[]{:S(2)}) collective-permute-start(bf16[64,3584]{1,0:T(8,128)(2,1)S(1)} %fusion.44), channel_id=1, source_target_pairs={{0,2},{1,3},{2,0},{3,1},{4,6},{5,7},{6,4},{7,5},{8,10},{9,11},{10,... | collective-permute-start | bytes 1376264 | tf_op jit(solution)/shard_map/ppermute | solution.py:36
  217.7 16.7 %collective-permute-start.34 = (bf16[4,32,2048]{2,1,0:T(8,128)(2,1)S(1)}, bf16[4,32,2048]{2,1,0:T(8,128)(2,1)S(1)}, u32[]{:S(2)}, u32[]{:S(2)}) collective-permute-start(bf16[4,32,2048]{2,1,0:T(8,128)(2,1)S(1)} %fusion.20), channel_id=1, source_target_pairs={{0,4},{4,8},{8,12},{12,0},{1,5},{5,9},{9,13},{13,1},{2,6},{6,10},{... | collective-permute-start | bytes 1572872 | tf_op jit(solution)/shard_map/ppermute | solution.py:41
  218.0 22.3 %collective-permute-start.29 = (bf16[4,32,2048]{2,1,0:T(8,128)(2,1)S(1)}, bf16[4,32,2048]{2,1,0:T(8,128)(2,1)S(1)}, u32[]{:S(2)}, u32[]{:S(2)}) collective-permute-start(bf16[4,32,2048]{2,1,0:T(8,128)(2,1)S(1)} %fusion.20), channel_id=1, source_target_pairs={{0,12},{4,0},{8,4},{12,8},{1,13},{5,1},{9,5},{13,9},{2,14},{6,2},{... | collective-permute-start | bytes 1572872 | tf_op jit(solution)/shard_map/ppermute | solution.py:41
  248.8 26.9 %collective-permute-start.39 = (bf16[4,32,2048]{2,1,0:T(8,128)(2,1)S(1)}, bf16[4,32,2048]{2,1,0:T(8,128)(2,1)S(1)}, u32[]{:S(2)}, u32[]{:S(2)}) collective-permute-start(bf16[4,32,2048]{2,1,0:T(8,128)(2,1)S(1)} %copy-done.46), channel_id=1, source_target_pairs={{0,8},{4,12},{8,0},{12,4},{1,9},{5,13},{9,1},{13,5},{2,10},{6,14},... | collective-permute-start | bytes 1572872 | tf_op jit(solution)/shard_map/ppermute | solution.py:41
  251.2 36.9 %collective-permute-start.36 = (bf16[4,32,2048]{2,1,0:T(8,128)(2,1)S(1)}, bf16[4,32,2048]{2,1,0:T(8,128)(2,1)S(1)}, u32[]{:S(2)}, u32[]{:S(2)}) collective-permute-start(bf16[4,32,2048]{2,1,0:T(8,128)(2,1)S(1)} %copy-done.45), channel_id=1, source_target_pairs={{0,12},{4,0},{8,4},{12,8},{1,13},{5,1},{9,5},{13,9},{2,14},{6,2},{... | collective-permute-start | bytes 1572872 | tf_op jit(solution)/shard_map/ppermute | solution.py:41
  261.6 26.5 %collective-permute-start.40 = (bf16[4,32,2048]{2,1,0:T(8,128)(2,1)S(1)}, bf16[4,32,2048]{2,1,0:T(8,128)(2,1)S(1)}, u32[]{:S(2)}, u32[]{:S(2)}) collective-permute-start(bf16[4,32,2048]{2,1,0:T(8,128)(2,1)S(1)} %fusion.60), channel_id=1, source_target_pairs={{0,4},{4,8},{8,12},{12,0},{1,5},{5,9},{9,13},{13,1},{2,6},{6,10},{... | collective-permute-start | bytes 1572872 | tf_op jit(solution)/shard_map/ppermute | solution.py:41
  267.0 31.2 %collective-permute-start.42 = (bf16[4,32,2048]{2,1,0:T(8,128)(2,1)S(1)}, bf16[4,32,2048]{2,1,0:T(8,128)(2,1)S(1)}, u32[]{:S(2)}, u32[]{:S(2)}) collective-permute-start(bf16[4,32,2048]{2,1,0:T(8,128)(2,1)S(1)} %collective-permute-done.29), channel_id=1, source_target_pairs={{0,12},{4,0},{8,4},{12,8},{1,13},{5,1},{9,5},{13,9},{2,14},{6,2},{... | collective-permute-start | bytes 1572872 | tf_op jit(solution)/shard_map/ppermute | solution.py:41
  306.1 25.3 %collective-permute-start.48 = (bf16[4,32,2048]{2,1,0:T(8,128)(2,1)S(1)}, bf16[4,32,2048]{2,1,0:T(8,128)(2,1)S(1)}, u32[]{:S(2)}, u32[]{:S(2)}) collective-permute-start(bf16[4,32,2048]{2,1,0:T(8,128)(2,1)S(1)} %fusion.15), channel_id=1, source_target_pairs={{0,4},{4,8},{8,12},{12,0},{1,5},{5,9},{9,13},{13,1},{2,6},{6,10},{... | collective-permute-start | bytes 1572872 | tf_op jit(solution)/shard_map/ppermute | solution.py:41
  316.7 25.6 %collective-permute-start.47 = (bf16[4,32,2048]{2,1,0:T(8,128)(2,1)S(1)}, bf16[4,32,2048]{2,1,0:T(8,128)(2,1)S(1)}, u32[]{:S(2)}, u32[]{:S(2)}) collective-permute-start(bf16[4,32,2048]{2,1,0:T(8,128)(2,1)S(1)} %fusion.15), channel_id=1, source_target_pairs={{0,12},{4,0},{8,4},{12,8},{1,13},{5,1},{9,5},{13,9},{2,14},{6,2},{... | collective-permute-start | bytes 1572872 | tf_op jit(solution)/shard_map/ppermute | solution.py:41
  354.2 14.3 %collective-permute-start.53 = (bf16[4,32,2048]{2,1,0:T(8,128)(2,1)S(1)}, bf16[4,32,2048]{2,1,0:T(8,128)(2,1)S(1)}, u32[]{:S(2)}, u32[]{:S(2)}) collective-permute-start(bf16[4,32,2048]{2,1,0:T(8,128)(2,1)S(1)} %copy-done.50), channel_id=1, source_target_pairs={{0,12},{4,0},{8,4},{12,8},{1,13},{5,1},{9,5},{13,9},{2,14},{6,2},{... | collective-permute-start | bytes 1572872 | tf_op jit(solution)/shard_map/ppermute | solution.py:41
  357.3 13.4 %collective-permute-start.45 = (bf16[64,3584]{1,0:T(8,128)(2,1)S(1)}, bf16[64,3584]{1,0:T(8,128)(2,1)S(1)}, u32[]{:S(2)}, u32[]{:S(2)}) collective-permute-start(bf16[64,3584]{1,0:T(8,128)(2,1)S(1)} %fusion.32), channel_id=1, source_target_pairs={{0,2},{1,3},{2,0},{3,1},{4,6},{5,7},{6,4},{7,5},{8,10},{9,11},{10,... | collective-permute-start | bytes 1376264 | tf_op jit(solution)/shard_map/ppermute | solution.py:36
  360.8 18.9 %collective-permute-start.50 = (bf16[64,3584]{1,0:T(8,128)(2,1)S(1)}, bf16[64,3584]{1,0:T(8,128)(2,1)S(1)}, u32[]{:S(2)}, u32[]{:S(2)}) collective-permute-start(bf16[64,3584]{1,0:T(8,128)(2,1)S(1)} %fusion.25), channel_id=1, source_target_pairs={{0,2},{1,3},{2,0},{3,1},{4,6},{5,7},{6,4},{7,5},{8,10},{9,11},{10,... | collective-permute-start | bytes 1376264 | tf_op jit(solution)/shard_map/ppermute | solution.py:36
  362.4 32.7 %collective-permute-start.41 = (bf16[128,3584]{1,0:T(8,128)(2,1)}, bf16[128,3584]{1,0:T(8,128)(2,1)}, u32[]{:S(2)}, u32[]{:S(2)}) collective-permute-start(bf16[128,3584]{1,0:T(8,128)(2,1)} %pad_maximum_fusion.18), channel_id=1, source_target_pairs={{0,1},{1,0},{2,3},{3,2},{4,5},{5,4},{6,7},{7,6},{8,9},{9,8},{10,11... | collective-permute-start | bytes 2752520 | tf_op jit(solution)/shard_map/ppermute | solution.py:36
  398.1 34.2 %collective-permute-start.46 = (bf16[128,3584]{1,0:T(8,128)(2,1)S(1)}, bf16[128,3584]{1,0:T(8,128)(2,1)S(1)}, u32[]{:S(2)}, u32[]{:S(2)}) collective-permute-start(bf16[128,3584]{1,0:T(8,128)(2,1)S(1)} %pad_maximum_fusion.19), channel_id=1, source_target_pairs={{0,1},{1,0},{2,3},{3,2},{4,5},{5,4},{6,7},{7,6},{8,9},{9,8},{10,11... | collective-permute-start | bytes 2752520 | tf_op jit(solution)/shard_map/ppermute | solution.py:36
  400.0 13.4 %collective-permute-start.55 = (bf16[64,3584]{1,0:T(8,128)(2,1)S(1)}, bf16[64,3584]{1,0:T(8,128)(2,1)S(1)}, u32[]{:S(2)}, u32[]{:S(2)}) collective-permute-start(bf16[64,3584]{1,0:T(8,128)(2,1)S(1)} %fusion.21), channel_id=1, source_target_pairs={{0,2},{1,3},{2,0},{3,1},{4,6},{5,7},{6,4},{7,5},{8,10},{9,11},{10,... | collective-permute-start | bytes 1376264 | tf_op jit(solution)/shard_map/ppermute | solution.py:36
  403.1 20.2 %collective-permute-start.51 = (bf16[64,3584]{1,0:T(8,128)(2,1)S(1)}, bf16[64,3584]{1,0:T(8,128)(2,1)S(1)}, u32[]{:S(2)}, u32[]{:S(2)}) collective-permute-start(bf16[64,3584]{1,0:T(8,128)(2,1)S(1)} %fusion.28), channel_id=1, source_target_pairs={{0,2},{1,3},{2,0},{3,1},{4,6},{5,7},{6,4},{7,5},{8,10},{9,11},{10,... | collective-permute-start | bytes 1376264 | tf_op jit(solution)/shard_map/ppermute | solution.py:36
  414.9 17.3 %collective-permute-start.56 = (bf16[64,3584]{1,0:T(8,128)(2,1)S(1)}, bf16[64,3584]{1,0:T(8,128)(2,1)S(1)}, u32[]{:S(2)}, u32[]{:S(2)}) collective-permute-start(bf16[64,3584]{1,0:T(8,128)(2,1)S(1)} %fusion.24), channel_id=1, source_target_pairs={{0,2},{1,3},{2,0},{3,1},{4,6},{5,7},{6,4},{7,5},{8,10},{9,11},{10,... | collective-permute-start | bytes 1376264 | tf_op jit(solution)/shard_map/ppermute | solution.py:36
  (72 other events, 751.1 us)
Sparse Core Ops, SparseCore 0:
  116.7 31.4 all-gather.6
  164.9 30.3 all-gather.4

commit v15 on v14

--- a/solution.py
+++ b/solution.py
@@ -275,7 +275,7 @@
         _, _, after, near = back(0, j, pieces, after)
     after = after + others[:1]
     for j in reversed(range(GROUPS)):
-        _, _, after, _ = back(1, j, others, after)
+        _, after, _, _ = back(1, j, others, after + turned)
         after = after + near
     return last_product(turned, bars, tokens)
 

time: 468 us -> 473 us (1.011)
  other arithmetic: 42.6 us -> 48.4 us
  waiting for transfers between devices: 173 us -> 168 us
  transfers between devices with their start and end apart: 60 -> 60, of which waited for: 27 -> 29; matrix products, arithmetic and copies ran while one was open for 33% -> 33% of each run, Pallas kernels for 0% -> 0%
where the time goes in v15:
time: 473 us; the launch traced here: 469 us
  waiting for transfers between devices  168 us (36%)
  matrix products  113 us (24%)
  starting transfers between devices  64.8 us (14%)
  other arithmetic  48.4 us (10%)
  local copies, waits for them, and re-layouts  37 us (8%)
  Pallas kernels  22.5 us (5%)
  between operations  14.9 us (3%)
    ppermute x15, waiting for transfers between devices, shift(): lax.ppermute(values, axis, [(i, (i + by) % count) for i in range(count)])  84.8 us
    dot_general x12, matrix products, matmul(): return jnp.dot(left, right, preferred_element_type=jnp.float32)  83.8 us
    ppermute x43, waiting for transfers between devices, swap(): return lax.ppermute(values, axis, [(i, i ^ mask) for i in range(count)])  83.6 us
    ppermute x15, starting transfers between devices, shift(): lax.ppermute(values, axis, [(i, (i + by) % count) for i in range(count)])  36.4 us
    dot_general x4, matrix products, times_down(): lax.dot_general(left, w_down, (((1,), (1,)), ((), ())), preferred_element...  29.5 us
    ppermute x43, starting transfers between devices, swap(): return lax.ppermute(values, axis, [(i, i ^ mask) for i in range(count)])  28.3 us
    pallas_call x1, Pallas kernels, last_product(): pl.pallas_call(functools.partial(last_kernel, 1.0 / tokens, len(turned)),...  22.5 us
    unnamed x120, local copies, waits for them, and re-layouts  13.3 us
  transfers between devices with their start and end apart: 60, of which 29 were waited for; matrix products, arithmetic and copies ran while one was open for 33% of the time, Pallas kernels for 0%

profile of v15, /device:TPU:0, one launch (start us, length us, event | category | flops | bytes accessed | tf_op | source)
XLA Modules:
  0.0 469.2 jit_solution(10957426936014696967)
XLA Ops:
  8.7 3.1 collective-permute-start
  11.8 13.9 %collective-permute-done = bf16[4,32,2048]{2,1,0:T(8,128)(2,1)S(1)} collective-permute-done((bf16[4,32,2048]{2,1,0:T(8,128)(2,1)S(1)}, bf16[4,32,2048]{2,1,0:T(8,128)(2,1)S(1)}, u32[]{:S(2)}, u32[]{:S(2)}) %collective-permute-start) | collective-permute-done | bytes 524320 | tf_op jit(solution)/shard_map/ppermute | solution.py:41
  26.6 7.2 %fusion.86 = f32[256,3584]{1,0:T(8,128)S(1)} fusion(bf16[256,2048]{1,0:T(8,128)(2,1)S(1)} %bitcast.130, bf16[2048,3584]{1,0:T(8,128)(2,1)} %param.8), kind=kOutput, calls=%fused_computation.192 | convolution fusion | flops 3758096384 | bytes 19398656 | tf_op jit(solution)/shard_map/dot_general | solution.py:19
  38.2 2.9 dynamic-slice_bitcast_fusion.3
  44.7 7.2 %fusion.85 = f32[256,3584]{1,0:T(8,128)S(1)} fusion(bf16[256,2048]{1,0:T(8,128)(2,1)S(1)} %bitcast.131, bf16[2048,3584]{1,0:T(8,128)(2,1)} %param.7), kind=kOutput, calls=%fused_computation.191 | convolution fusion | flops 3758096384 | bytes 19398656 | tf_op jit(solution)/shard_map/dot_general | solution.py:19
  56.7 7.2 %fusion.87 = f32[256,3584]{1,0:T(8,128)S(1)} fusion(bf16[256,2048]{1,0:T(8,128)(2,1)S(1)} %bitcast.132, bf16[2048,3584]{1,0:T(8,128)(2,1)} %param.10), kind=kOutput, calls=%fused_computation.193 | convolution fusion | flops 3758096384 | bytes 19398656 | tf_op jit(solution)/shard_map/dot_general | solution.py:19
  64.9 3.3 collective-permute-done.4
  68.2 9.2 %collective-permute-done.1 = bf16[4,32,2048]{2,1,0:T(8,128)(2,1)} collective-permute-done((bf16[4,32,2048]{2,1,0:T(8,128)(2,1)S(1)}, bf16[4,32,2048]{2,1,0:T(8,128)(2,1)}, u32[]{:S(2)}, u32[]{:S(2)}) %collective-permute-start.1) | collective-permute-done | bytes 524320 | tf_op jit(solution)/shard_map/ppermute | solution.py:41
  78.7 7.3 %fusion.89 = f32[256,3584]{1,0:T(8,128)S(1)} fusion(bf16[256,2048]{1,0:T(8,128)(2,1)S(1)} %bitcast.134, bf16[2048,3584]{1,0:T(8,128)(2,1)} %param.8), kind=kOutput, calls=%fused_computation.195 | convolution fusion | flops 3758096384 | bytes 19398656 | tf_op jit(solution)/shard_map/dot_general | solution.py:19
  90.2 7.2 %fusion.88 = f32[256,3584]{1,0:T(8,128)S(1)} fusion(bf16[256,2048]{1,0:T(8,128)(2,1)S(1)} %bitcast.135, bf16[2048,3584]{1,0:T(8,128)(2,1)} %param.7), kind=kOutput, calls=%fused_computation.194 | convolution fusion | flops 3758096384 | bytes 19398656 | tf_op jit(solution)/shard_map/dot_general | solution.py:19
  106.3 7.6 %fusion.90 = f32[256,3584]{1,0:T(8,128)S(1)} fusion(bf16[256,2048]{1,0:T(8,128)(2,1)S(1)} %bitcast.136, bf16[2048,3584]{1,0:T(8,128)(2,1)} %param.10), kind=kOutput, calls=%fused_computation.196 | convolution fusion | flops 3758096384 | bytes 19398656 | tf_op jit(solution)/shard_map/dot_general | solution.py:19
  118.4 6.4 %collective-permute-done.12 = f16[64,3712]{1,0:T(8,128)(2,1)} collective-permute-done((f16[64,3712]{1,0:T(8,128)(2,1)}, f16[64,3712]{1,0:T(8,128)(2,1)}, u32[]{:S(2)}, u32[]{:S(2)}) %collective-permute-start.12) | collective-permute-done | bytes 475168 | tf_op jit(solution)/shard_map/ppermute | solution.py:36
  130.4 7.7 %convolution_convert_fusion.1 = bf16[256,2048]{1,0:T(8,128)(2,1)S(1)} fusion(bf16[256,3584]{1,0:T(8,128)(2,1)S(1)} %pad_maximum_fusion, bf16[3584,2048]{1,0:T(8,128)(2,1)} %param.9), kind=kOutput, calls=%fused_computation.1 | convolution fusion | flops 3758620672 | bytes 17563648 | tf_op jit(solution)/shard_map/dot_general | solution.py:19
  139.5 3.9 fusion.91
  144.9 3.6 collective-permute-start.20
  150.7 3.9 fusion.92
  156.3 5.3 %collective-permute-done.15 = bf16[64,3584]{1,0:T(8,128)(2,1)S(1)} collective-permute-done((bf16[64,3584]{1,0:T(8,128)(2,1)S(1)}, bf16[64,3584]{1,0:T(8,128)(2,1)S(1)}, u32[]{:S(2)}, u32[]{:S(2)}) %collective-permute-start.15) | collective-permute-done | bytes 458784 | tf_op jit(solution)/shard_map/ppermute | solution.py:36
  161.8 3.6 multiply_convert_fusion
  166.0 2.4 fusion.37
  169.7 9.0 %collective-permute-done.18 = bf16[64,3584]{1,0:T(8,128)(2,1)S(1)} collective-permute-done((bf16[64,3584]{1,0:T(8,128)(2,1)S(1)}, bf16[64,3584]{1,0:T(8,128)(2,1)S(1)}, u32[]{:S(2)}, u32[]{:S(2)}) %collective-permute-start.18) | collective-permute-done | bytes 458784 | tf_op jit(solution)/shard_map/ppermute | solution.py:36
  179.7 7.6 %collective-permute-done.31 = bf16[64,3584]{1,0:T(8,128)(2,1)S(1)} collective-permute-done((bf16[64,3584]{1,0:T(8,128)(2,1)}, bf16[64,3584]{1,0:T(8,128)(2,1)S(1)}, u32[]{:S(2)}, u32[]{:S(2)}) %collective-permute-start.31) | collective-permute-done | bytes 458784 | tf_op jit(solution)/shard_map/ppermute | solution.py:36
  193.9 7.7 %fusion = f32[256,2048]{1,0:T(8,128)S(1)} fusion(bf16[3584,2048]{1,0:T(8,128)(2,1)} %param.9, bf16[128,3584]{1,0:T(8,128)(2,1)} %collective-permute-done.19, bf16[64,3584]{1,0:T(8,128)(2,1)S(1)} %collective-permute-done.18, bf16[64,3584]{1,0:T(8,128)(2,1)S(1)} %get-tuple-element.81), kind=kOutput, calls=%fused_computation.3 | convolution fusion | flops 3763601408 | bytes 18612224 | tf_op jit(solution)/shard_map/dot_general | solution.py:19
  202.6 3.0 collective-permute-start.22
  206.7 4.9 %collective-permute-done.26 = bf16[64,3584]{1,0:T(8,128)(2,1)} collective-permute-done((bf16[64,3584]{1,0:T(8,128)(2,1)S(1)}, bf16[64,3584]{1,0:T(8,128)(2,1)}, u32[]{:S(2)}, u32[]{:S(2)}) %collective-permute-start.26) | collective-permute-done | bytes 458784 | tf_op jit(solution)/shard_map/ppermute | solution.py:36
  214.5 2.4 collective-permute-done.22
  219.8 2.8 collective-permute-start.29
  222.6 9.4 %convolution_convert_fusion = bf16[256,2048]{1,0:T(8,128)(2,1)S(1)} fusion(bf16[3584,2048]{1,0:T(8,128)(2,1)} %param.9, bf16[128,3584]{1,0:T(8,128)(2,1)} %collective-permute-done.33, bf16[64,3584]{1,0:T(8,128)(2,1)S(1)} %copy-done.53, bf16[64,3584]{1,0:T(8,128)(2,1)S(1)} %fusion.40), kind=kOutput, calls=%fused_computation | convolution fusion | flops 3764125696 | bytes 17563648 | tf_op jit(solution)/shard_map/dot_general | solution.py:19
  233.1 2.4 collective-permute-done.34
  235.4 6.5 %collective-permute-done.29 = bf16[4,32,2048]{2,1,0:T(8,128)(2,1)S(1)} collective-permute-done((bf16[4,32,2048]{2,1,0:T(8,128)(2,1)S(1)}, bf16[4,32,2048]{2,1,0:T(8,128)(2,1)S(1)}, u32[]{:S(2)}, u32[]{:S(2)}) %collective-permute-start.29) | collective-permute-done | bytes 524320 | tf_op jit(solution)/shard_map/ppermute | solution.py:41
  242.8 7.3 %fusion.93 = f32[256,3584]{1,0:T(8,128)S(1)} fusion(bf16[256,2048]{1,0:T(8,128)(2,1)S(1)} %bitcast.154, bf16[3584,2048]{1,0:T(8,128)(2,1)} %param.9), kind=kOutput, calls=%fused_computation.199 | convolution fusion | flops 3758096384 | bytes 19398656 | tf_op jit(solution)/shard_map/dot_general | solution.py:23
  256.8 7.2 %fusion.94 = f32[256,2048]{1,0:T(8,128)S(1)} fusion(bf16[256,3584]{1,0:T(8,128)(2,1)S(1)} %pad_maximum_fusion.1, bf16[3584,2048]{1,0:T(8,128)(2,1)} %param.9), kind=kOutput, calls=%fused_computation.200 | convolution fusion | flops 3758096384 | bytes 18612224 | tf_op jit(solution)/shard_map/dot_general | solution.py:19
  264.5 3.7 collective-permute-done.37
  271.6 6.6 %collective-permute-done.39 = bf16[4,32,2048]{2,1,0:T(8,128)(2,1)S(1)} collective-permute-done((bf16[4,32,2048]{2,1,0:T(8,128)(2,1)S(1)}, bf16[4,32,2048]{2,1,0:T(8,128)(2,1)S(1)}, u32[]{:S(2)}, u32[]{:S(2)}) %collective-permute-start.39) | collective-permute-done | bytes 524320 | tf_op jit(solution)/shard_map/ppermute | solution.py:41
  281.0 7.8 %collective-permute-done.36 = bf16[4,32,2048]{2,1,0:T(8,128)(2,1)S(1)} collective-permute-done((bf16[4,32,2048]{2,1,0:T(8,128)(2,1)S(1)}, bf16[4,32,2048]{2,1,0:T(8,128)(2,1)S(1)}, u32[]{:S(2)}, u32[]{:S(2)}) %collective-permute-start.36) | collective-permute-done | bytes 524320 | tf_op jit(solution)/shard_map/ppermute | solution.py:41
  290.6 9.4 %collective-permute-done.42 = bf16[4,32,2048]{2,1,0:T(8,128)(2,1)S(1)} collective-permute-done((bf16[4,32,2048]{2,1,0:T(8,128)(2,1)S(1)}, bf16[4,32,2048]{2,1,0:T(8,128)(2,1)S(1)}, u32[]{:S(2)}, u32[]{:S(2)}) %collective-permute-start.42) | collective-permute-done | bytes 524320 | tf_op jit(solution)/shard_map/ppermute | solution.py:41
  300.1 7.5 %fusion.95 = f32[256,3584]{1,0:T(8,128)S(1)} fusion(bf16[256,2048]{1,0:T(8,128)(2,1)S(1)} %bitcast.152, bf16[3584,2048]{1,0:T(8,128)(2,1)} %param.9), kind=kOutput, calls=%fused_computation.201 | convolution fusion | flops 3758096384 | bytes 19398656 | tf_op jit(solution)/shard_map/dot_general | solution.py:23
  307.9 11.4 %collective-permute-start.48 = (bf16[4,32,2048]{2,1,0:T(8,128)(2,1)}, bf16[4,32,2048]{2,1,0:T(8,128)(2,1)}, u32[]{:S(2)}, u32[]{:S(2)}) collective-permute-start(bf16[4,32,2048]{2,1,0:T(8,128)(2,1)} %fusion.15), channel_id=1, source_target_pairs={{0,4},{4,8},{8,12},{12,0},{1,5},{5,9},{9,13},{13,1},{2,6},{6,10},{... | collective-permute-start | bytes 1572872 | tf_op jit(solution)/shard_map/ppermute | solution.py:41
  319.2 2.3 collective-permute-start.47
  325.2 9.4 %collective-permute-done.48 = bf16[4,32,2048]{2,1,0:T(8,128)(2,1)} collective-permute-done((bf16[4,32,2048]{2,1,0:T(8,128)(2,1)}, bf16[4,32,2048]{2,1,0:T(8,128)(2,1)}, u32[]{:S(2)}, u32[]{:S(2)}) %collective-permute-start.48) | collective-permute-done | bytes 524320 | tf_op jit(solution)/shard_map/ppermute | solution.py:41
  335.8 9.6 %collective-permute-done.47 = bf16[4,32,2048]{2,1,0:T(8,128)(2,1)} collective-permute-done((bf16[4,32,2048]{2,1,0:T(8,128)(2,1)}, bf16[4,32,2048]{2,1,0:T(8,128)(2,1)}, u32[]{:S(2)}, u32[]{:S(2)}) %collective-permute-start.47) | collective-permute-done | bytes 524320 | tf_op jit(solution)/shard_map/ppermute | solution.py:41
  346.7 7.3 %fusion.96 = f32[256,3584]{1,0:T(8,128)S(1)} fusion(bf16[256,2048]{1,0:T(8,128)(2,1)S(1)} %bitcast.155, bf16[3584,2048]{1,0:T(8,128)(2,1)} %param.9), kind=kOutput, calls=%fused_computation.202 | convolution fusion | flops 3758096384 | bytes 19398656 | tf_op jit(solution)/shard_map/dot_general | solution.py:23
  367.9 6.8 %collective-permute-done.53 = bf16[4,32,2048]{2,1,0:T(8,128)(2,1)S(1)} collective-permute-done((bf16[4,32,2048]{2,1,0:T(8,128)(2,1)}, bf16[4,32,2048]{2,1,0:T(8,128)(2,1)S(1)}, u32[]{:S(2)}, u32[]{:S(2)}) %collective-permute-start.53) | collective-permute-done | bytes 524320 | tf_op jit(solution)/shard_map/ppermute | solution.py:41
  378.5 7.3 %fusion.97 = f32[256,3584]{1,0:T(8,128)S(1)} fusion(bf16[256,2048]{1,0:T(8,128)(2,1)S(1)} %bitcast.153, bf16[3584,2048]{1,0:T(8,128)(2,1)} %param.9), kind=kOutput, calls=%fused_computation.203 | convolution fusion | flops 3758096384 | bytes 19398656 | tf_op jit(solution)/shard_map/dot_general | solution.py:23
  398.3 10.0 %collective-permute-done.50 = bf16[64,3584]{1,0:T(8,128)(2,1)S(1)} collective-permute-done((bf16[64,3584]{1,0:T(8,128)(2,1)S(1)}, bf16[64,3584]{1,0:T(8,128)(2,1)S(1)}, u32[]{:S(2)}, u32[]{:S(2)}) %collective-permute-start.50) | collective-permute-done | bytes 458784 | tf_op jit(solution)/shard_map/ppermute | solution.py:36
  411.2 6.9 %collective-permute-done.55 = bf16[64,3584]{1,0:T(8,128)(2,1)S(1)} collective-permute-done((bf16[64,3584]{1,0:T(8,128)(2,1)S(1)}, bf16[64,3584]{1,0:T(8,128)(2,1)S(1)}, u32[]{:S(2)}, u32[]{:S(2)}) %collective-permute-start.55) | collective-permute-done | bytes 458784 | tf_op jit(solution)/shard_map/ppermute | solution.py:36
  420.8 7.2 %collective-permute-done.51 = bf16[64,3584]{1,0:T(8,128)(2,1)S(1)} collective-permute-done((bf16[64,3584]{1,0:T(8,128)(2,1)S(1)}, bf16[64,3584]{1,0:T(8,128)(2,1)S(1)}, u32[]{:S(2)}, u32[]{:S(2)}) %collective-permute-start.51) | collective-permute-done | bytes 458784 | tf_op jit(solution)/shard_map/ppermute | solution.py:36
  428.1 8.8 %collective-permute-done.56 = bf16[64,3584]{1,0:T(8,128)(2,1)S(1)} collective-permute-done((bf16[64,3584]{1,0:T(8,128)(2,1)S(1)}, bf16[64,3584]{1,0:T(8,128)(2,1)S(1)}, u32[]{:S(2)}, u32[]{:S(2)}) %collective-permute-start.56) | collective-permute-done | bytes 458784 | tf_op jit(solution)/shard_map/ppermute | solution.py:36
  439.7 22.5 %shard_map.64 = f32[2048,3584]{1,0:T(8,128)} custom-call(bf16[2048,256]{1,0:T(8,128)(2,1)S(1)} %bitcast.127, bf16[2048,256]{1,0:T(8,128)(2,1)S(1)} %bitcast.126, bf16[2048,256]{1,0:T(8,128)(2,1)S(1)} %bitcast.128, bf16[2048,256]{1,0:T(8,128)(2,1)S(1)} %bitcast.129, bf16[256,3584]{1,0:T(8,128)(2,1)S(1)} %pad_maximum_fusion.2.refs_4_, ...), custom_call_target="tpu_custom_call" | custom-call | flops 15032385536 | bytes 40894464 | tf_op jit(solution)/shard_map/pallas_call | solution.py:91
  (297 shorter events, 126.4 us)
Async XLA Ops:
  6.5 173.2 %all-gather.7.cloned.1.call-start = ((), (), s32[]{:S(2)}) async-start(), calls=%async_computation.1 | async-start | bytes 2752512 | tf_op jit(solution)/shard_map/all_gather | solution.py:210
  8.7 17.0 %collective-permute-start = (bf16[4,32,2048]{2,1,0:T(8,128)(2,1)S(1)}, bf16[4,32,2048]{2,1,0:T(8,128)(2,1)S(1)}, u32[]{:S(2)}, u32[]{:S(2)}) collective-permute-start(bf16[4,32,2048]{2,1,0:T(8,128)(2,1)S(1)} %pad_maximum_fusion.22), channel_id=1, source_target_pairs={{0,4},{4,8},{8,12},{12,0},{1,5},{5,9},{9,13},{13,1},{2,6},{6,10},{... | collective-permute-start | bytes 1572872 | tf_op jit(solution)/shard_map/ppermute | solution.py:41
  37.0 15.1 %collective-permute-start.3 = (f32[128,3584]{1,0:T(8,128)}, f32[128,3584]{1,0:T(8,128)S(1)}, u32[]{:S(2)}, u32[]{:S(2)}) collective-permute-start(f32[128,3584]{1,0:T(8,128)} %slice.322), channel_id=1, source_target_pairs={{0,1},{1,0},{2,3},{3,2},{4,5},{5,4},{6,7},{7,6},{8,9},{9,8},{10,11... | collective-permute-start | bytes 5505032 | tf_op jit(solution)/shard_map/ppermute | solution.py:36
  41.2 23.1 %collective-permute-start.5 = (bf16[4,32,2048]{2,1,0:T(8,128)(2,1)S(1)}, bf16[4,32,2048]{2,1,0:T(8,128)(2,1)}, u32[]{:S(2)}, u32[]{:S(2)}) collective-permute-start(bf16[4,32,2048]{2,1,0:T(8,128)(2,1)S(1)} %copy-done.41), channel_id=1, source_target_pairs={{0,12},{4,0},{8,4},{12,8},{1,13},{5,1},{9,5},{13,9},{2,14},{6,2},{... | collective-permute-start | bytes 1572872 | tf_op jit(solution)/shard_map/ppermute | solution.py:41
  43.1 34.3 %collective-permute-start.1 = (bf16[4,32,2048]{2,1,0:T(8,128)(2,1)S(1)}, bf16[4,32,2048]{2,1,0:T(8,128)(2,1)}, u32[]{:S(2)}, u32[]{:S(2)}) collective-permute-start(bf16[4,32,2048]{2,1,0:T(8,128)(2,1)S(1)} %copy-done.41), channel_id=1, source_target_pairs={{0,8},{4,12},{8,0},{12,4},{1,9},{5,13},{9,1},{13,5},{2,10},{6,14},... | collective-permute-start | bytes 1572872 | tf_op jit(solution)/shard_map/ppermute | solution.py:41
  43.2 45.5 %collective-permute-start.6 = (bf16[4,32,2048]{2,1,0:T(8,128)(2,1)S(1)}, bf16[4,32,2048]{2,1,0:T(8,128)(2,1)S(1)}, u32[]{:S(2)}, u32[]{:S(2)}) collective-permute-start(bf16[4,32,2048]{2,1,0:T(8,128)(2,1)S(1)} %copy-done.43), channel_id=1, source_target_pairs={{0,16},{16,0},{1,17},{17,1},{2,18},{18,2},{3,19},{19,3},{4,20},{20... | collective-permute-start | bytes 1572872 | tf_op jit(solution)/shard_map/ppermute | solution.py:36
  55.2 13.0 %collective-permute-start.4 = (f16[64,3712]{1,0:T(8,128)(2,1)S(1)}, f16[64,3712]{1,0:T(8,128)(2,1)S(1)}, u32[]{:S(2)}, u32[]{:S(2)}) collective-permute-start(f16[64,3712]{1,0:T(8,128)(2,1)S(1)} %pad_maximum_fusion.24), channel_id=1, source_target_pairs={{0,2},{1,3},{2,0},{3,1},{4,6},{5,7},{6,4},{7,5},{8,10},{9,11},{10,... | collective-permute-start | bytes 1425416 | tf_op jit(solution)/shard_map/ppermute | solution.py:36
  64.1 23.9 %collective-permute-start.7 = (f32[128,3584]{1,0:T(8,128)S(1)}, f32[128,3584]{1,0:T(8,128)S(1)}, u32[]{:S(2)}, u32[]{:S(2)}) collective-permute-start(f32[128,3584]{1,0:T(8,128)S(1)} %slice.325), channel_id=1, source_target_pairs={{0,1},{1,0},{2,3},{3,2},{4,5},{5,4},{6,7},{7,6},{8,9},{9,8},{10,11... | collective-permute-start | bytes 5505032 | tf_op jit(solution)/shard_map/ppermute | solution.py:36
  64.3 25.9 %collective-permute-start.8 = (f16[64,3584]{1,0:T(8,128)(2,1)S(1)}, f16[64,3584]{1,0:T(8,128)(2,1)S(1)}, u32[]{:S(2)}, u32[]{:S(2)}) collective-permute-start(f16[64,3584]{1,0:T(8,128)(2,1)S(1)} %fusion.58), channel_id=1, source_target_pairs={{0,2},{1,3},{2,0},{3,1},{4,6},{5,7},{6,4},{7,5},{8,10},{9,11},{10,... | collective-permute-start | bytes 1376264 | tf_op jit(solution)/shard_map/ppermute | solution.py:36
  86.1 18.2 %collective-permute-start.11 = (f32[128,3584]{1,0:T(8,128)S(1)}, f32[128,3584]{1,0:T(8,128)S(1)}, u32[]{:S(2)}, u32[]{:S(2)}) collective-permute-start(f32[128,3584]{1,0:T(8,128)S(1)} %slice.333), channel_id=1, source_target_pairs={{0,1},{1,0},{2,3},{3,2},{4,5},{5,4},{6,7},{7,6},{8,9},{9,8},{10,11... | collective-permute-start | bytes 5505032 | tf_op jit(solution)/shard_map/ppermute | solution.py:36
  86.2 62.4 %collective-permute-start.23 = (bf16[4,32,2048]{2,1,0:T(8,128)(2,1)}, bf16[4,32,2048]{2,1,0:T(8,128)(2,1)}, u32[]{:S(2)}, u32[]{:S(2)}) collective-permute-start(bf16[4,32,2048]{2,1,0:T(8,128)(2,1)} %collective-permute-done.1), channel_id=1, source_target_pairs={{0,16},{16,0},{1,17},{17,1},{2,18},{18,2},{3,19},{19,3},{4,20},{20... | collective-permute-start | bytes 1572872 | tf_op jit(solution)/shard_map/ppermute | solution.py:36
  88.0 60.7 %collective-permute-start.24 = (bf16[4,32,2048]{2,1,0:T(8,128)(2,1)}, bf16[4,32,2048]{2,1,0:T(8,128)(2,1)}, u32[]{:S(2)}, u32[]{:S(2)}) collective-permute-start(bf16[4,32,2048]{2,1,0:T(8,128)(2,1)} %collective-permute-done.5), channel_id=1, source_target_pairs={{0,16},{16,0},{1,17},{17,1},{2,18},{18,2},{3,19},{19,3},{4,20},{20... | collective-permute-start | bytes 1572872 | tf_op jit(solution)/shard_map/ppermute | solution.py:36
  99.0 26.9 %collective-permute-start.9 = (f32[128,3584]{1,0:T(8,128)}, f32[128,3584]{1,0:T(8,128)}, u32[]{:S(2)}, u32[]{:S(2)}) collective-permute-start(f32[128,3584]{1,0:T(8,128)} %slice.328), channel_id=1, source_target_pairs={{0,1},{1,0},{2,3},{3,2},{4,5},{5,4},{6,7},{7,6},{8,9},{9,8},{10,11... | collective-permute-start | bytes 5505032 | tf_op jit(solution)/shard_map/ppermute | solution.py:36
  102.8 14.5 %collective-permute-start.16 = (bf16[64,3584]{1,0:T(8,128)(2,1)S(1)}, bf16[64,3584]{1,0:T(8,128)(2,1)}, u32[]{:S(2)}, u32[]{:S(2)}) collective-permute-start(bf16[64,3584]{1,0:T(8,128)(2,1)S(1)} %get-tuple-element.83), channel_id=1, source_target_pairs={{0,2},{1,3},{2,0},{3,1},{4,6},{5,7},{6,4},{7,5},{8,10},{9,11},{10,... | collective-permute-start | bytes 1376264 | tf_op jit(solution)/shard_map/ppermute | solution.py:36
  105.8 19.0 %collective-permute-start.12 = (f16[64,3712]{1,0:T(8,128)(2,1)}, f16[64,3712]{1,0:T(8,128)(2,1)}, u32[]{:S(2)}, u32[]{:S(2)}) collective-permute-start(f16[64,3712]{1,0:T(8,128)(2,1)} %pad_maximum_fusion.25), channel_id=1, source_target_pairs={{0,2},{1,3},{2,0},{3,1},{4,6},{5,7},{6,4},{7,5},{8,10},{9,11},{10,... | collective-permute-start | bytes 1425416 | tf_op jit(solution)/shard_map/ppermute | solution.py:36
  117.2 94.4 %all-gather.5.cloned.1.call-start = ((), (), s32[]{:S(2)}) async-start(), calls=%async_computation | async-start | bytes 2752512 | tf_op jit(solution)/shard_map/all_gather | solution.py:210
  117.3 27.6 %collective-permute-start.14 = (f32[128,3584]{1,0:T(8,128)}, f32[128,3584]{1,0:T(8,128)S(1)}, u32[]{:S(2)}, u32[]{:S(2)}) collective-permute-start(f32[128,3584]{1,0:T(8,128)} %slice.343), channel_id=1, source_target_pairs={{0,1},{1,0},{2,3},{3,2},{4,5},{5,4},{6,7},{7,6},{8,9},{9,8},{10,11... | collective-permute-start | bytes 5505032 | tf_op jit(solution)/shard_map/ppermute | solution.py:36
  127.6 21.8 %collective-permute-start.10 = (f16[64,3584]{1,0:T(8,128)(2,1)S(1)}, f16[64,3584]{1,0:T(8,128)(2,1)S(1)}, u32[]{:S(2)}, u32[]{:S(2)}) collective-permute-start(f16[64,3584]{1,0:T(8,128)(2,1)S(1)} %fusion.54), channel_id=1, source_target_pairs={{0,2},{1,3},{2,0},{3,1},{4,6},{5,7},{6,4},{7,5},{8,10},{9,11},{10,... | collective-permute-start | bytes 1376264 | tf_op jit(solution)/shard_map/ppermute | solution.py:36
  139.2 75.2 %collective-permute-start.21 = (bf16[4,32,2048]{2,1,0:T(8,128)(2,1)}, bf16[4,32,2048]{2,1,0:T(8,128)(2,1)}, u32[]{:S(2)}, u32[]{:S(2)}) collective-permute-start(bf16[4,32,2048]{2,1,0:T(8,128)(2,1)} %get-tuple-element.102), channel_id=1, source_target_pairs={{0,8},{4,12},{8,0},{12,4},{1,9},{5,13},{9,1},{13,5},{2,10},{6,14},... | collective-permute-start | bytes 1572872 | tf_op jit(solution)/shard_map/ppermute | solution.py:41
  144.9 69.6 %collective-permute-start.20 = (bf16[4,32,2048]{2,1,0:T(8,128)(2,1)}, bf16[4,32,2048]{2,1,0:T(8,128)(2,1)}, u32[]{:S(2)}, u32[]{:S(2)}) collective-permute-start(bf16[4,32,2048]{2,1,0:T(8,128)(2,1)} %get-tuple-element.101), channel_id=1, source_target_pairs={{0,12},{4,0},{8,4},{12,8},{1,13},{5,1},{9,5},{13,9},{2,14},{6,2},{... | collective-permute-start | bytes 1572872 | tf_op jit(solution)/shard_map/ppermute | solution.py:41
  148.6 17.4 %collective-permute-start.30 = (f32[128,3584]{1,0:T(8,128)}, f32[128,3584]{1,0:T(8,128)}, u32[]{:S(2)}, u32[]{:S(2)}) collective-permute-start(f32[128,3584]{1,0:T(8,128)} %slice.359), channel_id=1, source_target_pairs={{0,1},{1,0},{2,3},{3,2},{4,5},{5,4},{6,7},{7,6},{8,9},{9,8},{10,11... | collective-permute-start | bytes 5505032 | tf_op jit(solution)/shard_map/ppermute | solution.py:36
  148.7 12.9 %collective-permute-start.15 = (bf16[64,3584]{1,0:T(8,128)(2,1)S(1)}, bf16[64,3584]{1,0:T(8,128)(2,1)S(1)}, u32[]{:S(2)}, u32[]{:S(2)}) collective-permute-start(bf16[64,3584]{1,0:T(8,128)(2,1)S(1)} %fusion.49), channel_id=1, source_target_pairs={{0,2},{1,3},{2,0},{3,1},{4,6},{5,7},{6,4},{7,5},{8,10},{9,11},{10,... | collective-permute-start | bytes 1376264 | tf_op jit(solution)/shard_map/ppermute | solution.py:36
  156.2 34.7 %collective-permute-start.25 = (f32[128,3584]{1,0:T(8,128)}, f32[128,3584]{1,0:T(8,128)}, u32[]{:S(2)}, u32[]{:S(2)}) collective-permute-start(f32[128,3584]{1,0:T(8,128)} %slice.363), channel_id=1, source_target_pairs={{0,1},{1,0},{2,3},{3,2},{4,5},{5,4},{6,7},{7,6},{8,9},{9,8},{10,11... | collective-permute-start | bytes 5505032 | tf_op jit(solution)/shard_map/ppermute | solution.py:36
  165.3 13.4 %collective-permute-start.18 = (bf16[64,3584]{1,0:T(8,128)(2,1)S(1)}, bf16[64,3584]{1,0:T(8,128)(2,1)S(1)}, u32[]{:S(2)}, u32[]{:S(2)}) collective-permute-start(bf16[64,3584]{1,0:T(8,128)(2,1)S(1)} %get-tuple-element.81), channel_id=1, source_target_pairs={{0,2},{1,3},{2,0},{3,1},{4,6},{5,7},{6,4},{7,5},{8,10},{9,11},{10,... | collective-permute-start | bytes 1376264 | tf_op jit(solution)/shard_map/ppermute | solution.py:36
  168.4 18.9 %collective-permute-start.31 = (bf16[64,3584]{1,0:T(8,128)(2,1)}, bf16[64,3584]{1,0:T(8,128)(2,1)S(1)}, u32[]{:S(2)}, u32[]{:S(2)}) collective-permute-start(bf16[64,3584]{1,0:T(8,128)(2,1)} %fusion.37), channel_id=1, source_target_pairs={{0,2},{1,3},{2,0},{3,1},{4,6},{5,7},{6,4},{7,5},{8,10},{9,11},{10,... | collective-permute-start | bytes 1376264 | tf_op jit(solution)/shard_map/ppermute | solution.py:36
  179.7 14.1 %collective-permute-start.19 = (bf16[128,3584]{1,0:T(8,128)(2,1)}, bf16[128,3584]{1,0:T(8,128)(2,1)}, u32[]{:S(2)}, u32[]{:S(2)}) collective-permute-start(bf16[128,3584]{1,0:T(8,128)(2,1)} %pad_maximum_fusion.15), channel_id=1, source_target_pairs={{0,1},{1,0},{2,3},{3,2},{4,5},{5,4},{6,7},{7,6},{8,9},{9,8},{10,11... | collective-permute-start | bytes 2752520 | tf_op jit(solution)/shard_map/ppermute | solution.py:36
  190.2 15.4 %collective-permute-start.32 = (bf16[64,3584]{1,0:T(8,128)(2,1)S(1)}, bf16[64,3584]{1,0:T(8,128)(2,1)S(1)}, u32[]{:S(2)}, u32[]{:S(2)}) collective-permute-start(bf16[64,3584]{1,0:T(8,128)(2,1)S(1)} %fusion.40), channel_id=1, source_target_pairs={{0,2},{1,3},{2,0},{3,1},{4,6},{5,7},{6,4},{7,5},{8,10},{9,11},{10,... | collective-permute-start | bytes 1376264 | tf_op jit(solution)/shard_map/ppermute | solution.py:36
  192.4 19.1 %collective-permute-start.26 = (bf16[64,3584]{1,0:T(8,128)(2,1)S(1)}, bf16[64,3584]{1,0:T(8,128)(2,1)}, u32[]{:S(2)}, u32[]{:S(2)}) collective-permute-start(bf16[64,3584]{1,0:T(8,128)(2,1)S(1)} %fusion.41), channel_id=1, source_target_pairs={{0,2},{1,3},{2,0},{3,1},{4,6},{5,7},{6,4},{7,5},{8,10},{9,11},{10,... | collective-permute-start | bytes 1376264 | tf_op jit(solution)/shard_map/ppermute | solution.py:36
  202.6 14.4 %collective-permute-start.22 = (bf16[4,32,2048]{2,1,0:T(8,128)(2,1)}, bf16[4,32,2048]{2,1,0:T(8,128)(2,1)}, u32[]{:S(2)}, u32[]{:S(2)}) collective-permute-start(bf16[4,32,2048]{2,1,0:T(8,128)(2,1)} %fusion.59), channel_id=1, source_target_pairs={{0,4},{4,8},{8,12},{12,0},{1,5},{5,9},{9,13},{13,1},{2,6},{6,10},{... | collective-permute-start | bytes 1572872 | tf_op jit(solution)/shard_map/ppermute | solution.py:41
  206.6 16.0 %collective-permute-start.33 = (bf16[128,3584]{1,0:T(8,128)(2,1)}, bf16[128,3584]{1,0:T(8,128)(2,1)}, u32[]{:S(2)}, u32[]{:S(2)}) collective-permute-start(bf16[128,3584]{1,0:T(8,128)(2,1)} %pad_maximum_fusion.17), channel_id=1, source_target_pairs={{0,1},{1,0},{2,3},{3,2},{4,5},{5,4},{6,7},{7,6},{8,9},{9,8},{10,11... | collective-permute-start | bytes 2752520 | tf_op jit(solution)/shard_map/ppermute | solution.py:36
  213.7 36.6 %collective-permute-start.27 = (bf16[64,3584]{1,0:T(8,128)(2,1)S(1)}, bf16[64,3584]{1,0:T(8,128)(2,1)S(1)}, u32[]{:S(2)}, u32[]{:S(2)}) collective-permute-start(bf16[64,3584]{1,0:T(8,128)(2,1)S(1)} %fusion.44), channel_id=1, source_target_pairs={{0,2},{1,3},{2,0},{3,1},{4,6},{5,7},{6,4},{7,5},{8,10},{9,11},{10,... | collective-permute-start | bytes 1376264 | tf_op jit(solution)/shard_map/ppermute | solution.py:36
  218.7 16.7 %collective-permute-start.34 = (bf16[4,32,2048]{2,1,0:T(8,128)(2,1)S(1)}, bf16[4,32,2048]{2,1,0:T(8,128)(2,1)S(1)}, u32[]{:S(2)}, u32[]{:S(2)}) collective-permute-start(bf16[4,32,2048]{2,1,0:T(8,128)(2,1)S(1)} %fusion.20), channel_id=1, source_target_pairs={{0,4},{4,8},{8,12},{12,0},{1,5},{5,9},{9,13},{13,1},{2,6},{6,10},{... | collective-permute-start | bytes 1572872 | tf_op jit(solution)/shard_map/ppermute | solution.py:41
  219.8 22.2 %collective-permute-start.29 = (bf16[4,32,2048]{2,1,0:T(8,128)(2,1)S(1)}, bf16[4,32,2048]{2,1,0:T(8,128)(2,1)S(1)}, u32[]{:S(2)}, u32[]{:S(2)}) collective-permute-start(bf16[4,32,2048]{2,1,0:T(8,128)(2,1)S(1)} %fusion.20), channel_id=1, source_target_pairs={{0,12},{4,0},{8,4},{12,8},{1,13},{5,1},{9,5},{13,9},{2,14},{6,2},{... | collective-permute-start | bytes 1572872 | tf_op jit(solution)/shard_map/ppermute | solution.py:41
  251.1 27.1 %collective-permute-start.39 = (bf16[4,32,2048]{2,1,0:T(8,128)(2,1)S(1)}, bf16[4,32,2048]{2,1,0:T(8,128)(2,1)S(1)}, u32[]{:S(2)}, u32[]{:S(2)}) collective-permute-start(bf16[4,32,2048]{2,1,0:T(8,128)(2,1)S(1)} %copy-done.51), channel_id=1, source_target_pairs={{0,8},{4,12},{8,0},{12,4},{1,9},{5,13},{9,1},{13,5},{2,10},{6,14},... | collective-permute-start | bytes 1572872 | tf_op jit(solution)/shard_map/ppermute | solution.py:41
  252.9 36.0 %collective-permute-start.36 = (bf16[4,32,2048]{2,1,0:T(8,128)(2,1)S(1)}, bf16[4,32,2048]{2,1,0:T(8,128)(2,1)S(1)}, u32[]{:S(2)}, u32[]{:S(2)}) collective-permute-start(bf16[4,32,2048]{2,1,0:T(8,128)(2,1)S(1)} %copy-done.50), channel_id=1, source_target_pairs={{0,12},{4,0},{8,4},{12,8},{1,13},{5,1},{9,5},{13,9},{2,14},{6,2},{... | collective-permute-start | bytes 1572872 | tf_op jit(solution)/shard_map/ppermute | solution.py:41
  264.1 25.3 %collective-permute-start.40 = (bf16[4,32,2048]{2,1,0:T(8,128)(2,1)S(1)}, bf16[4,32,2048]{2,1,0:T(8,128)(2,1)S(1)}, u32[]{:S(2)}, u32[]{:S(2)}) collective-permute-start(bf16[4,32,2048]{2,1,0:T(8,128)(2,1)S(1)} %fusion.60), channel_id=1, source_target_pairs={{0,4},{4,8},{8,12},{12,0},{1,5},{5,9},{9,13},{13,1},{2,6},{6,10},{... | collective-permute-start | bytes 1572872 | tf_op jit(solution)/shard_map/ppermute | solution.py:41
  269.6 30.4 %collective-permute-start.42 = (bf16[4,32,2048]{2,1,0:T(8,128)(2,1)S(1)}, bf16[4,32,2048]{2,1,0:T(8,128)(2,1)S(1)}, u32[]{:S(2)}, u32[]{:S(2)}) collective-permute-start(bf16[4,32,2048]{2,1,0:T(8,128)(2,1)S(1)} %copy-done.49), channel_id=1, source_target_pairs={{0,12},{4,0},{8,4},{12,8},{1,13},{5,1},{9,5},{13,9},{2,14},{6,2},{... | collective-permute-start | bytes 1572872 | tf_op jit(solution)/shard_map/ppermute | solution.py:41
  307.8 13.8 %collective-permute-start.43 = (f32[128,3584]{1,0:T(8,128)S(1)}, f32[128,3584]{1,0:T(8,128)S(1)}, u32[]{:S(2)}, u32[]{:S(2)}) collective-permute-start(f32[128,3584]{1,0:T(8,128)S(1)} %slice.382), channel_id=1, source_target_pairs={{0,1},{1,0},{2,3},{3,2},{4,5},{5,4},{6,7},{7,6},{8,9},{9,8},{10,11... | collective-permute-start | bytes 5505032 | tf_op jit(solution)/shard_map/ppermute | solution.py:36
  307.9 26.8 %collective-permute-start.48 = (bf16[4,32,2048]{2,1,0:T(8,128)(2,1)}, bf16[4,32,2048]{2,1,0:T(8,128)(2,1)}, u32[]{:S(2)}, u32[]{:S(2)}) collective-permute-start(bf16[4,32,2048]{2,1,0:T(8,128)(2,1)} %fusion.15), channel_id=1, source_target_pairs={{0,4},{4,8},{8,12},{12,0},{1,5},{5,9},{9,13},{13,1},{2,6},{6,10},{... | collective-permute-start | bytes 1572872 | tf_op jit(solution)/shard_map/ppermute | solution.py:41
  319.2 26.2 %collective-permute-start.47 = (bf16[4,32,2048]{2,1,0:T(8,128)(2,1)}, bf16[4,32,2048]{2,1,0:T(8,128)(2,1)}, u32[]{:S(2)}, u32[]{:S(2)}) collective-permute-start(bf16[4,32,2048]{2,1,0:T(8,128)(2,1)} %fusion.15), channel_id=1, source_target_pairs={{0,12},{4,0},{8,4},{12,8},{1,13},{5,1},{9,5},{13,9},{2,14},{6,2},{... | collective-permute-start | bytes 1572872 | tf_op jit(solution)/shard_map/ppermute | solution.py:41
  323.0 12.8 %collective-permute-start.44 = (bf16[64,3584]{1,0:T(8,128)(2,1)}, bf16[64,3584]{1,0:T(8,128)(2,1)}, u32[]{:S(2)}, u32[]{:S(2)}) collective-permute-start(bf16[64,3584]{1,0:T(8,128)(2,1)} %fusion.29), channel_id=1, source_target_pairs={{0,2},{1,3},{2,0},{3,1},{4,6},{5,7},{6,4},{7,5},{8,10},{9,11},{10,... | collective-permute-start | bytes 1376264 | tf_op jit(solution)/shard_map/ppermute | solution.py:36
  360.2 31.2 %collective-permute-start.41 = (bf16[128,3584]{1,0:T(8,128)(2,1)}, bf16[128,3584]{1,0:T(8,128)(2,1)}, u32[]{:S(2)}, u32[]{:S(2)}) collective-permute-start(bf16[128,3584]{1,0:T(8,128)(2,1)} %pad_maximum_fusion.18), channel_id=1, source_target_pairs={{0,1},{1,0},{2,3},{3,2},{4,5},{5,4},{6,7},{7,6},{8,9},{9,8},{10,11... | collective-permute-start | bytes 2752520 | tf_op jit(solution)/shard_map/ppermute | solution.py:36
  360.7 14.0 %collective-permute-start.53 = (bf16[4,32,2048]{2,1,0:T(8,128)(2,1)}, bf16[4,32,2048]{2,1,0:T(8,128)(2,1)S(1)}, u32[]{:S(2)}, u32[]{:S(2)}) collective-permute-start(bf16[4,32,2048]{2,1,0:T(8,128)(2,1)} %collective-permute-done.47), channel_id=1, source_target_pairs={{0,12},{4,0},{8,4},{12,8},{1,13},{5,1},{9,5},{13,9},{2,14},{6,2},{... | collective-permute-start | bytes 1572872 | tf_op jit(solution)/shard_map/ppermute | solution.py:41
  394.3 42.7 %collective-permute-start.46 = (bf16[128,3584]{1,0:T(8,128)(2,1)S(1)}, bf16[128,3584]{1,0:T(8,128)(2,1)S(1)}, u32[]{:S(2)}, u32[]{:S(2)}) collective-permute-start(bf16[128,3584]{1,0:T(8,128)(2,1)S(1)} %pad_maximum_fusion.19), channel_id=1, source_target_pairs={{0,1},{1,0},{2,3},{3,2},{4,5},{5,4},{6,7},{7,6},{8,9},{9,8},{10,11... | collective-permute-start | bytes 2752520 | tf_op jit(solution)/shard_map/ppermute | solution.py:36
  394.9 13.4 %collective-permute-start.50 = (bf16[64,3584]{1,0:T(8,128)(2,1)S(1)}, bf16[64,3584]{1,0:T(8,128)(2,1)S(1)}, u32[]{:S(2)}, u32[]{:S(2)}) collective-permute-start(bf16[64,3584]{1,0:T(8,128)(2,1)S(1)} %copy-done.54), channel_id=1, source_target_pairs={{0,2},{1,3},{2,0},{3,1},{4,6},{5,7},{6,4},{7,5},{8,10},{9,11},{10,... | collective-permute-start | bytes 1376264 | tf_op jit(solution)/shard_map/ppermute | solution.py:36
  397.4 20.7 %collective-permute-start.55 = (bf16[64,3584]{1,0:T(8,128)(2,1)S(1)}, bf16[64,3584]{1,0:T(8,128)(2,1)S(1)}, u32[]{:S(2)}, u32[]{:S(2)}) collective-permute-start(bf16[64,3584]{1,0:T(8,128)(2,1)S(1)} %fusion.21), channel_id=1, source_target_pairs={{0,2},{1,3},{2,0},{3,1},{4,6},{5,7},{6,4},{7,5},{8,10},{9,11},{10,... | collective-permute-start | bytes 1376264 | tf_op jit(solution)/shard_map/ppermute | solution.py:36
  410.0 18.0 %collective-permute-start.51 = (bf16[64,3584]{1,0:T(8,128)(2,1)S(1)}, bf16[64,3584]{1,0:T(8,128)(2,1)S(1)}, u32[]{:S(2)}, u32[]{:S(2)}) collective-permute-start(bf16[64,3584]{1,0:T(8,128)(2,1)S(1)} %fusion.28), channel_id=1, source_target_pairs={{0,2},{1,3},{2,0},{3,1},{4,6},{5,7},{6,4},{7,5},{8,10},{9,11},{10,... | collective-permute-start | bytes 1376264 | tf_op jit(solution)/shard_map/ppermute | solution.py:36
  419.6 17.4 %collective-permute-start.56 = (bf16[64,3584]{1,0:T(8,128)(2,1)S(1)}, bf16[64,3584]{1,0:T(8,128)(2,1)S(1)}, u32[]{:S(2)}, u32[]{:S(2)}) collective-permute-start(bf16[64,3584]{1,0:T(8,128)(2,1)S(1)} %fusion.24), channel_id=1, source_target_pairs={{0,2},{1,3},{2,0},{3,1},{4,6},{5,7},{6,4},{7,5},{8,10},{9,11},{10,... | collective-permute-start | bytes 1376264 | tf_op jit(solution)/shard_map/ppermute | solution.py:36
  (72 other events, 542.7 us)
Sparse Core Ops, SparseCore 0:
  117.3 31.4 all-gather.6
  166.1 30.7 all-gather.4
